TPU v7x, 32 devices: a whole 2x2x4 slice. The times are simulated.
32 devices in a mesh: dom: 8 (over z, x), rows: 4 (over y, core).
Axes of the slice: x: 2, y: 2, z: 4, core: 2. Of those that a mesh axis runs over, the one named last changes fastest.
Arguments:
- features: bfloat16 [8192, 384], P(('dom', 'rows')), may hold values from -7 to 7
- out_grad: bfloat16 [8192, 384], P(('dom', 'rows')), may hold values from -6 to 6
- w_query: bfloat16 [384, 384], replicated, may hold values from -0.3125 to 0.3125
- w_keyval: bfloat16 [384, 768], replicated, may hold values from -0.3125 to 0.3125
- w_out: bfloat16 [384, 384], replicated, may hold values from -0.3125 to 0.3125
- virtual: bfloat16 [4, 384], replicated, may hold values from -6 to 6
- local_nbr: int32 [8192, 16], P(('dom', 'rows')), may hold values from 0 to 255
- expander: int32 [8192, 4], P(('dom', 'rows')), may hold values from 0 to 255
- send_rows: int32 [256, 32], P(('dom', 'rows')), may hold values from 0 to 255
Outputs:
- grad_features: float32 [8192, 384], P(('dom', 'rows'))
- grad_wq: float32 [384, 384], replicated
- grad_wkv: float32 [384, 768], replicated
- grad_wo: float32 [384, 384], replicated
- grad_virtual: float32 [4, 384], replicated
Inputs may be any that keep to these rules, and one draw needn't show every extreme that they name: `local_nbr`: positions 0 to 127 name the previous tile of the partition's block order (cyclic within the partition), 128 to 255 the node's own tile. `expander`: slot s * 32 + k of a device holds the k-th row that the device of dom index s and the same rows index sends to it. `send_rows`: row g * 8 + a lists the 32 local rows that device g sends to dom index a; every device sends exactly 32 rows to every dom index, itself included.
All inputs are finite; a program needn't handle non-finite values.
Results may differ from a plain program's by a relative error of at most 0.008.
The roundings to bfloat16 on the way count: a program that leaves them out, or rounds other values in their place, can miss the bound.
Values may be sent and summed in bfloat16 or wider, within the bound.
No kernel may reach another device: no remote copies, remote signals or barrier semaphores. Data moves between devices by JAX's collectives and lax.ppermute only.
A program may use at most 64 MiB of HBM per device.

v0:
```python
import math

import jax
import jax.numpy as jnp
from jax import lax
from jax.sharding import PartitionSpec as P

HEADS = 8
TILE = 128


NEGATIVE_FILL = -1e30


def shifted(block, axis, distance):
    devices = range(lax.axis_size(axis))
    route = [((i - distance) % len(devices), i) for i in devices]
    return lax.ppermute(block, axis, route)


def einsum_bf(spec, left, right):
    return jnp.einsum(spec, left, right, preferred_element_type=jnp.float32)


def rows_contracted(left, right):
    return lax.dot_general(
        left, right, (((0,), (0,)), ((), ())), preferred_element_type=jnp.float32
    )


def times_transposed(left, right):
    return lax.dot_general(
        left, right, (((1,), (1,)), ((), ())), preferred_element_type=jnp.float32
    )


def attend(queries, key_value, halo_kv, expand_kv, virtual_kv, local_nbr, out_delta):
    row_count, feat_width = queries.shape
    head_count = HEADS
    head_dim = feat_width // head_count
    tile_rows = TILE
    tile_count = row_count // tile_rows
    score_scale = 1.0 / math.sqrt(head_dim)
    extended = jnp.concatenate([halo_kv, key_value], axis=0)
    window = jnp.concatenate(
        [
            extended[:row_count].reshape(tile_count, tile_rows, 2 * feat_width),
            key_value.reshape(tile_count, tile_rows, 2 * feat_width),
        ],
        axis=1,
    )
    win_keys = window[:, :, :feat_width].reshape(tile_count, 2 * tile_rows, head_count, head_dim)
    win_vals = window[:, :, feat_width:].reshape(tile_count, 2 * tile_rows, head_count, head_dim)
    exp_keys = expand_kv[:, :, :feat_width].reshape(row_count, -1, head_count, head_dim)
    exp_vals = expand_kv[:, :, feat_width:].reshape(row_count, -1, head_count, head_dim)
    virt_keys = virtual_kv[:, :feat_width].reshape(-1, head_count, head_dim)
    virt_vals = virtual_kv[:, feat_width:].reshape(-1, head_count, head_dim)
    q_heads = queries.reshape(row_count, head_count, head_dim)
    q_tiles = queries.reshape(tile_count, tile_rows, head_count, head_dim)
    d_heads = out_delta.reshape(row_count, head_count, head_dim)
    d_tiles = out_delta.reshape(tile_count, tile_rows, head_count, head_dim)
    positions = jnp.arange(2 * tile_rows, dtype=jnp.int32)
    local_mask = jnp.any(local_nbr[:, :, None] == positions[None, None, :], axis=1)[:, None, :]
    s_loc = (
        einsum_bf("tqhd,tkhd->tqhk", q_tiles, win_keys).reshape(
            row_count, head_count, 2 * tile_rows
        )
        * score_scale
    )
    s_loc = jnp.where(local_mask, s_loc, NEGATIVE_FILL)
    s_exp = einsum_bf("rhd,rkhd->rhk", q_heads, exp_keys) * score_scale
    s_virt = einsum_bf("rhd,khd->rhk", q_heads, virt_keys) * score_scale
    row_peak = jnp.maximum(jnp.maximum(s_loc.max(-1), s_exp.max(-1)), s_virt.max(-1))[..., None]
    e_loc = jnp.where(local_mask, jnp.exp(s_loc - row_peak), 0.0)
    e_exp = jnp.exp(s_exp - row_peak)
    e_virt = jnp.exp(s_virt - row_peak)
    norm_total = (e_loc.sum(-1) + e_exp.sum(-1) + e_virt.sum(-1))[..., None]
    p_loc = e_loc / norm_total
    p_exp = e_exp / norm_total
    p_virt = e_virt / norm_total
    pb_loc = p_loc.astype(jnp.bfloat16)
    pb_exp = p_exp.astype(jnp.bfloat16)
    pb_virt = p_virt.astype(jnp.bfloat16)
    pb_tiles = pb_loc.reshape(tile_count, tile_rows, head_count, 2 * tile_rows)
    summed = (
        einsum_bf("tqhk,tkhd->tqhd", pb_tiles, win_vals).reshape(row_count, feat_width)
        + einsum_bf("rhk,rkhd->rhd", pb_exp, exp_vals).reshape(row_count, feat_width)
        + einsum_bf("rhk,khd->rhd", pb_virt, virt_vals).reshape(row_count, feat_width)
    )
    attn_out = summed.astype(jnp.bfloat16)
    dp_loc = einsum_bf("tqhd,tkhd->tqhk", d_tiles, win_vals).reshape(
        row_count, head_count, 2 * tile_rows
    )
    dp_exp = einsum_bf("rhd,rkhd->rhk", d_heads, exp_vals)
    dp_virt = einsum_bf("rhd,khd->rhk", d_heads, virt_vals)
    delta = ((p_loc * dp_loc).sum(-1) + (p_exp * dp_exp).sum(-1) + (p_virt * dp_virt).sum(-1))[
        ..., None
    ]
    ds_loc = (p_loc * (dp_loc - delta) * score_scale).astype(jnp.bfloat16)
    ds_exp = (p_exp * (dp_exp - delta) * score_scale).astype(jnp.bfloat16)
    ds_virt = (p_virt * (dp_virt - delta) * score_scale).astype(jnp.bfloat16)
    ds_tiles = ds_loc.reshape(tile_count, tile_rows, head_count, 2 * tile_rows)
    grad_query = (
        einsum_bf("tqhk,tkhd->tqhd", ds_tiles, win_keys).reshape(row_count, feat_width)
        + einsum_bf("rhk,rkhd->rhd", ds_exp, exp_keys).reshape(row_count, feat_width)
        + einsum_bf("rhk,khd->rhd", ds_virt, virt_keys).reshape(row_count, feat_width)
    ).astype(jnp.bfloat16)
    win_kgrad = einsum_bf("tqhk,tqhd->tkhd", ds_tiles, q_tiles).reshape(
        tile_count, 2 * tile_rows, feat_width
    )
    win_vgrad = einsum_bf("tqhk,tqhd->tkhd", pb_tiles, d_tiles).reshape(
        tile_count, 2 * tile_rows, feat_width
    )
    window_grad = jnp.concatenate([win_kgrad, win_vgrad], axis=-1)
    exp_grad = jnp.concatenate(
        [
            einsum_bf("rhk,rhd->rkhd", ds_exp, q_heads).reshape(row_count, -1, feat_width),
            einsum_bf("rhk,rhd->rkhd", pb_exp, d_heads).reshape(row_count, -1, feat_width),
        ],
        axis=-1,
    )
    virt_grad = jnp.concatenate(
        [
            einsum_bf("rhk,rhd->khd", ds_virt, q_heads).reshape(-1, feat_width),
            einsum_bf("rhk,rhd->khd", pb_virt, d_heads).reshape(-1, feat_width),
        ],
        axis=-1,
    )
    return (attn_out, grad_query, window_grad, exp_grad, virt_grad)


def project_slots(slot_grad, w_keyval):
    return lax.optimization_barrier(times_transposed(slot_grad, w_keyval).astype(jnp.bfloat16))


def shards(features, out_grad, w_query, w_keyval, w_out, virtual, local_nbr, expander, send_rows):
    row_count, feat_width = features.shape
    tile_rows = TILE
    queries = jnp.dot(features, w_query, preferred_element_type=jnp.float32).astype(jnp.bfloat16)
    key_value = jnp.dot(features, w_keyval, preferred_element_type=jnp.float32).astype(jnp.bfloat16)
    virtual_kv = jnp.dot(virtual, w_keyval, preferred_element_type=jnp.float32).astype(jnp.bfloat16)
    send_flat = send_rows.reshape(-1)
    sent_features = features[send_flat]
    halo_kv = shifted(key_value[row_count - tile_rows :], "rows", 1)
    arrived = lax.all_to_all(sent_features, "dom", split_axis=0, concat_axis=0, tiled=True)
    slot_kv = jnp.dot(arrived, w_keyval, preferred_element_type=jnp.float32).astype(jnp.bfloat16)
    expand_kv = slot_kv[expander]
    out_delta = times_transposed(out_grad, w_out).astype(jnp.bfloat16)
    attn_out, grad_query, window_grad, exp_grad, virt_grad = attend(
        queries, key_value, halo_kv, expand_kv, virtual_kv, local_nbr, out_delta
    )
    own_grad = window_grad[:, tile_rows:].reshape(row_count, 2 * feat_width)
    prev_grad = window_grad[:, :tile_rows].reshape(row_count, 2 * feat_width)
    returned = shifted(prev_grad[:tile_rows].astype(jnp.bfloat16), "rows", -1).astype(jnp.float32)
    local_grad = (own_grad + jnp.concatenate([prev_grad[tile_rows:], returned], axis=0)).astype(
        jnp.bfloat16
    )
    slot_grad = jax.ops.segment_sum(
        exp_grad.reshape(-1, 2 * feat_width), expander.reshape(-1), num_segments=slot_kv.shape[0]
    ).astype(jnp.bfloat16)
    slot_weight = rows_contracted(arrived, slot_grad)
    returned_feat = lax.all_to_all(
        project_slots(slot_grad, w_keyval), "dom", split_axis=0, concat_axis=0, tiled=True
    )
    grad_features = times_transposed(grad_query, w_query) + times_transposed(local_grad, w_keyval)
    grad_features = grad_features.at[send_flat].add(returned_feat.astype(jnp.float32))
    grad_wq, grad_wkv, grad_wo, virt_total = lax.psum(
        (
            rows_contracted(features, grad_query),
            rows_contracted(features, local_grad) + slot_weight,
            rows_contracted(attn_out, out_grad),
            virt_grad,
        ),
        ("dom", "rows"),
    )
    grad_wkv = grad_wkv + jnp.dot(
        virtual.astype(jnp.float32).T, virt_total, precision=lax.Precision.HIGHEST
    )
    grad_virtual = jnp.dot(
        virt_total, w_keyval.astype(jnp.float32).T, precision=lax.Precision.HIGHEST
    )
    factor = (row_count * lax.axis_size("dom") * lax.axis_size("rows")) ** (-0.5)
    return (
        grad_features,
        grad_wq * factor,
        grad_wkv * factor,
        grad_wo * factor,
        grad_virtual * factor,
    )


def solution(mesh):
    placed = (
        P(("dom", "rows"), None),
        P(("dom", "rows"), None),
        P(),
        P(),
        P(),
        P(),
        P(("dom", "rows"), None),
        P(("dom", "rows"), None),
        P(("dom", "rows"), None),
    )
    return jax.shard_map(
        shards,
        mesh=mesh,
        in_specs=placed,
        out_specs=(P(("dom", "rows"), None), P(), P(), P(), P()),
        check_vma=False,
    )
```

profile of v0, /device:TPU:0, one launch (start us, length us, event | category | flops | bytes accessed | tf_op | source)
XLA Modules:
  0.0 266.5 jit_solution(5672613657944695020)
XLA Ops:
  8.1 2.8 %gather_fusion = bf16[256,384]{1,0:T(8,128)(2,1)} fusion(bf16[256,384]{1,0:T(8,128)(2,1)} %param.9, s32[1024]{0:T(1024)S(1)} %pad_clamp_fusion), kind=kCustom, calls=%fused_computation | custom fusion | bytes 394240 | tf_op jit(solution)/shard_map/gather | solution.py:143
  10.8 7.3 %all-to-all-start = ((bf16[8,32,384]{2,1,0:T(8,128)(2,1)}), bf16[8,32,384]{2,1,0:T(8,128)(2,1)}, u32[]{:S(2)}, u32[]{:S(2)}) async-start(bf16[8,32,384]{2,1,0:T(8,128)(2,1)} %bitcast.11), calls=%async_computation | async-start | bytes 393216 | tf_op jit(solution)/shard_map/all_to_all | solution.py:145
  20.8 1.2 copy.103
  24.0 1.2 copy.105
  26.5 1.8 fusion
  29.2 1.3 fusion.66
  30.9 0.9 copy.88
  31.8 2.1 fusion.9
  33.9 1.3 convolution_convert_fusion
  35.2 5.2 %gather_fusion.1 = bf16[1024,768]{1,0:T(8,128)(2,1)} fusion(bf16[256,768]{1,0:T(8,128)(2,1)S(1)} %convolution_convert_fusion, s32[1024]{0:T(1024)S(1)} %broadcast_clamp_fusion), kind=kCustom, calls=%fused_computation.1 | custom fusion | bytes 3149824 | tf_op jit(solution)/shard_map/gather | solution.py:147
  40.4 3.9 %reshape.235 = bf16[256,4,768]{2,1,0:T(4,128)(2,1)} reshape(bf16[1024,768]{1,0:T(8,128)(2,1)} %gather_fusion.1) | data formatting | bytes 3145728 | tf_op jit(solution)/shard_map/gather | solution.py:147
  44.3 3.1 %fusion.64 = (bf16[256,4,384]{2,1,0:T(4,128)(2,1)}, bf16[256,4,384]{2,1,0:T(4,128)(2,1)}) fusion(bf16[256,4,768]{2,1,0:T(4,128)(2,1)} %reshape.235), kind=kLoop, calls=%fused_computation.128 | loop fusion | bytes 3145728 | tf_op jit(solution)/shard_map/slice | solution.py:55
  47.4 2.2 copy.149
  49.7 1.5 multiply_reduce_fusion.3
  51.9 1.3 convert_convert_fusion
  53.2 1.0 fusion.51
  54.9 1.0 copy.106
  55.9 2.6 convolution_bitcast_fusion.3
  58.5 1.6 fusion.19
  60.2 3.5 %fusion.5 = (f32[2,128,8]{1,2,0:T(8,128)}, f32[2,8,256,128]{3,2,1,0:T(8,128)}) fusion(f32[2,128,8]{1,2,0:T(8,128)} %copy-done.40, f32[2,128,8]{1,2,0:T(8,128)} %copy-done.32, f32[2,8,256,128]{3,2,1,0:T(8,128)S(1)} %get-tuple-element.39, pred[2,128,256]{1,2,0:T(8,128)(4,1)S(1)} %copy.81, bf16[2,256,8,48]{1,3,2,0:T(8,128)(2,1)S(1)} %bitcast.231, ...), kind=kOutput, calls=%fused_computation.14 | convolution fusion | flops 53999616 | bytes 4874240 | tf_op jit(solution)/shard_map/tqhd,tkhd->tqhk/dot_general | solution.py:22
  63.7 2.2 copy.150
  65.9 1.3 multiply_reduce_fusion.2
  69.5 2.5 fusion.8
  72.0 1.1 convolution_bitcast_fusion.4
  75.2 1.0 copy.104
  76.2 1.4 copy.111
  77.9 2.0 fusion.68
  80.3 1.8 collective-permute-start.1
  82.6 1.1 convolution_bitcast_fusion.2
  83.6 3.3 %multiply_bitcast_fusion.1 = f32[256,4,8,48]{3,2,1,0:T(8,128)} fusion(f32[256,8,4]{1,2,0:T(4,128)S(1)} %copy-done.13, f32[256,8,48]{2,1,0:T(8,128)S(1)} %copy-done.5), kind=kLoop, calls=%fused_computation.5 | loop fusion | flops 393216 | bytes 1998848 | tf_op jit(solution)/shard_map/rhk,rhd->rkhd/transpose | solution.py:22
  86.9 4.7 %concatenate.27 = f32[1024,384]{1,0:T(8,128)} reshape(f32[256,4,8,48]{3,2,1,0:T(8,128)} %multiply_bitcast_fusion.1) | data formatting | bytes 3145728 | tf_op jit(solution)/shard_map/concatenate | solution.py:115
  91.6 4.3 %multiply_bitcast_fusion = f32[256,4,8,48]{3,2,1,0:T(8,128)} fusion(f32[256,8,4]{1,2,0:T(4,128)S(1)} %copy-done.12, f32[256,8,48]{2,1,0:T(8,128)} %copy.105), kind=kLoop, calls=%fused_computation.4 | loop fusion | flops 393216 | bytes 1998848 | tf_op jit(solution)/shard_map/rhk,rhd->rkhd/transpose | solution.py:22
  95.9 4.6 %concatenate.28 = f32[1024,384]{1,0:T(8,128)} reshape(f32[256,4,8,48]{3,2,1,0:T(8,128)} %multiply_bitcast_fusion) | data formatting | bytes 3145728 | tf_op jit(solution)/shard_map/concatenate | solution.py:115
  100.5 8.3 %scatter_custom_fusion = f32[256,768]{1,0:T(8,128)S(1)} fusion(s32[1024]{0:T(1024)} %reshape.244, f32[1024,384]{1,0:T(8,128)} %concatenate.28, f32[]{:T(128)} %constant.11.clone.1, f32[1024,384]{1,0:T(8,128)} %concatenate.27, f32[]{:T(128)} %constant.0.clone.1), kind=kCustom, calls=%fused_computation.8 | custom fusion | flops 1572864 | bytes 3933184 | tf_op jit(solution)/shard_map/scatter-add | solution.py:158
  108.8 1.1 convolution_bitcast_fusion.6
  109.9 1.0 convert_element_type.76
  110.9 1.1 fusion.17
  112.7 2.3 convolution_add_fusion
  115.4 1.1 convolution_convert_fusion.4
  116.5 6.0 %all-to-all-start.1 = ((bf16[8,32,384]{2,1,0:T(8,128)(2,1)}), bf16[8,32,384]{2,1,0:T(8,128)(2,1)S(1)}, u32[]{:S(2)}, u32[]{:S(2)}) async-start(bf16[8,32,384]{2,1,0:T(8,128)(2,1)} %bitcast.44), calls=%async_computation.1 | async-start | bytes 393216 | tf_op jit(solution)/shard_map/all_to_all | solution.py:162
  122.4 41.1 %psum.30 = f32[4,768]{1,0:T(4,128)S(1)} all-reduce(f32[4,768]{1,0:T(4,128)S(1)} %pad_maximum_fusion.3), channel_id=1, replica_groups=mesh['dom'=8,'rows'=4] {'dom','rows'}, use_global_device_ids=true, to_apply=%region_14.15 | all-reduce | flops 3072 | bytes 24576 | tf_op jit(solution)/shard_map/psum | solution.py:167
  163.5 1.2 convolution_multiply_fusion.1
  165.5 2.4 scatter_custom_fusion.1
  167.9 86.0 %all-reduce.3.cloned.1.call-done = (f32[384,384]{0,1:T(8,128)}, f32[384,768]{0,1:T(8,128)}, f32[384,384]{0,1:T(8,128)}) async-done(((f32[384,384]{0,1:T(8,128)}, f32[384,768]{0,1:T(8,128)}, f32[384,384]{0,1:T(8,128)}), (f32[384,384]{0,1:T(8,128)}, f32[384,768]{0,1:T(8,128)}, f32[384,384]{0,1:T(8,128)})) %all-reduce.3.cloned.1.call-update) | async-done | bytes 2359312 | tf_op jit(solution)/shard_map/psum | solution.py:167
  253.9 1.4 broadcast_multiply_fusion
  255.4 1.1 copy.116
  256.4 1.0 copy.114
  258.3 1.4 copy.115
  (159 shorter events, 17.2 us)
Async XLA Ops:
  7.2 11.0 %copy-start = (bf16[384,768]{1,0:T(8,128)(2,1)S(1)}, bf16[384,768]{1,0:T(8,128)(2,1)}, u32[]{:S(2)}) copy-start(bf16[384,768]{1,0:T(8,128)(2,1)} %param.12) | copy-start | bytes 1769476
  7.2 11.0 %copy-start.1 = (bf16[256,384]{1,0:T(8,128)(2,1)S(1)}, bf16[256,384]{1,0:T(8,128)(2,1)}, u32[]{:S(2)}) copy-start(bf16[256,384]{1,0:T(8,128)(2,1)} %param.9) | copy-start | bytes 589828
  7.2 11.5 %copy-start.43 = (s32[256,4]{0,1:T(4,128)S(1)}, s32[256,4]{0,1:T(4,128)}, u32[]{:S(2)}) copy-start(s32[256,4]{0,1:T(4,128)} %param.16) | copy-start | bytes 12292
  7.2 11.6 %copy-start.21 = (bf16[384,384]{1,0:T(8,128)(2,1)S(1)}, bf16[384,384]{1,0:T(8,128)(2,1)}, u32[]{:S(2)}) copy-start(bf16[384,384]{1,0:T(8,128)(2,1)} %param.11) | copy-start | bytes 884740
  8.1 10.0 %copy-start.45 = (s32[256,1]{0,1:T(1,128)}, s32[256,1]{0,1:T(1,128)S(1)}, u32[]{:S(2)}) copy-start(s32[256,1]{0,1:T(1,128)S(1)} %compare_select_fusion.1) | copy-start | bytes 3076
  10.8 23.1 %all-to-all-start = ((bf16[8,32,384]{2,1,0:T(8,128)(2,1)}), bf16[8,32,384]{2,1,0:T(8,128)(2,1)}, u32[]{:S(2)}, u32[]{:S(2)}) async-start(bf16[8,32,384]{2,1,0:T(8,128)(2,1)} %bitcast.11), calls=%async_computation | async-start | bytes 393216 | tf_op jit(solution)/shard_map/all_to_all | solution.py:145
  18.1 235.8 %all-reduce.3.cloned.1.call-start = ((), (), s32[]{:S(2)}) async-start(), calls=%async_computation.2 | async-start | bytes 4718592 | tf_op jit(solution)/shard_map/psum | solution.py:167
  18.5 3.5 %copy-start.23 = (bf16[256,384]{1,0:T(8,128)(2,1)S(1)}, bf16[256,384]{1,0:T(8,128)(2,1)}, u32[]{:S(2)}) copy-start(bf16[256,384]{1,0:T(8,128)(2,1)} %param.10) | copy-start | bytes 589828
  18.6 3.5 %copy-start.28 = (bf16[384,384]{1,0:T(8,128)(2,1)S(1)}, bf16[384,384]{1,0:T(8,128)(2,1)}, u32[]{:S(2)}) copy-start(bf16[384,384]{1,0:T(8,128)(2,1)} %param.13) | copy-start | bytes 884740
  18.6 12.0 %collective-permute-start = (bf16[128,768]{1,0:T(8,128)(2,1)S(1)}, bf16[128,768]{1,0:T(8,128)(2,1)S(1)}, u32[]{:S(2)}, u32[]{:S(2)}) collective-permute-start(bf16[128,768]{1,0:T(8,128)(2,1)S(1)} %slice.57), channel_id=1, source_target_pairs={{3,0},{0,1},{1,2},{2,3},{7,4},{4,5},{5,6},{6,7},{11,8},{8,9},{9,10... | collective-permute-start | bytes 589832 | tf_op jit(solution)/shard_map/ppermute | solution.py:18
  20.8 4.4 %copy-start.44 = (bf16[4,384]{1,0:T(4,128)(2,1)S(1)}, bf16[4,384]{1,0:T(4,128)(2,1)}, u32[]{:S(2)}) copy-start(bf16[4,384]{1,0:T(4,128)(2,1)} %param.14) | copy-start | bytes 9220
  22.0 4.4 %copy-start.42 = (s32[256,16]{0,1:T(8,128)S(1)}, s32[256,16]{0,1:T(8,128)}, u32[]{:S(2)}) copy-start(s32[256,16]{0,1:T(8,128)} %param.15) | copy-start | bytes 49156
  22.5 8.1 %copy-start.10 = (bf16[256,384]{0,1:T(8,128)(2,1)}, bf16[256,384]{0,1:T(8,128)(2,1)S(1)}, u32[]{:S(2)}) copy-start(bf16[256,384]{0,1:T(8,128)(2,1)S(1)} %copy.89) | copy-start | bytes 589828
  25.5 5.1 %copy-start.36 = (bf16[4,8,48]{2,1,0:T(8,128)(2,1)}, bf16[4,8,48]{2,1,0:T(8,128)(2,1)S(1)}, u32[]{:S(2)}) copy-start(bf16[4,8,48]{2,1,0:T(8,128)(2,1)S(1)} %reshape.208) | copy-start | bytes 9220
  30.9 3.0 %copy-start.6 = (bf16[2,256,384]{1,2,0:T(8,128)(2,1)}, bf16[2,256,384]{1,2,0:T(8,128)(2,1)S(1)}, u32[]{:S(2)}) copy-start(bf16[2,256,384]{1,2,0:T(8,128)(2,1)S(1)} %copy.79) | copy-start | bytes 1179652
  47.4 3.8 %copy-start.35 = (f32[2,128,8]{1,2,0:T(8,128)S(1)}, f32[2,128,8]{1,2,0:T(8,128)}, u32[]{:S(2)}) copy-start(f32[2,128,8]{1,2,0:T(8,128)} %get-tuple-element.38) | copy-start | bytes 24580
  47.4 3.8 %copy-start.38 = (f32[256,8]{0,1:T(8,128)S(1)}, f32[256,8]{0,1:T(8,128)}, u32[]{:S(2)}) copy-start(f32[256,8]{0,1:T(8,128)} %get-tuple-element.36) | copy-start | bytes 24580
  49.7 2.1 copy-start.24
  49.7 2.2 copy-start.11
  49.7 2.2 copy-start.39
  51.2 7.3 %copy-start.32 = (f32[2,128,8]{1,2,0:T(8,128)}, f32[2,128,8]{1,2,0:T(8,128)S(1)}, u32[]{:S(2)}) copy-start(f32[2,128,8]{1,2,0:T(8,128)S(1)} %bitcast_maximum_fusion.1) | copy-start | bytes 24580
  51.9 6.6 %copy-start.33 = (f32[256,8]{0,1:T(8,128)}, f32[256,8]{0,1:T(8,128)S(1)}, u32[]{:S(2)}) copy-start(f32[256,8]{0,1:T(8,128)S(1)} %fusion.49) | copy-start | bytes 24580
  51.9 6.6 %copy-start.40 = (f32[2,128,8]{1,2,0:T(8,128)}, f32[2,128,8]{1,2,0:T(8,128)S(1)}, u32[]{:S(2)}) copy-start(f32[2,128,8]{1,2,0:T(8,128)S(1)} %bitcast_add_fusion.7) | copy-start | bytes 24580
  55.9 2.6 copy-start.29
  58.5 1.6 copy-start.26
  60.2 5.8 %copy-start.18 = (f32[256,8,48]{0,2,1:T(8,128)S(1)}, f32[256,8,48]{0,2,1:T(8,128)}, u32[]{:S(2)}) copy-start(f32[256,8,48]{0,2,1:T(8,128)} %convert.23) | copy-start | bytes 1179652
  69.5 2.5 copy-start.7
  69.5 3.6 %copy-start.16 = (bf16[2,128,8,48]{1,0,3,2:T(2,128)(2,1)S(1)}, bf16[2,128,8,48]{1,0,3,2:T(2,128)(2,1)}, u32[]{:S(2)}) copy-start(bf16[2,128,8,48]{1,0,3,2:T(2,128)(2,1)} %reshape.204) | copy-start | bytes 589828
  72.0 1.6 copy-start.4
  73.6 1.5 copy-start.25
  73.6 1.5 copy-start.31
  74.3 3.3 %copy-start.3 = (bf16[256,4,384]{0,2,1:T(8,128)(2,1)S(1)}, bf16[256,4,384]{0,2,1:T(8,128)(2,1)}, u32[]{:S(2)}) copy-start(bf16[256,4,384]{0,2,1:T(8,128)(2,1)} %copy.150) | copy-start | bytes 2359300
  74.3 3.3 %copy-start.30 = (f32[256,8,4]{0,1,2:T(8,128)S(1)}, f32[256,8,4]{0,1,2:T(8,128)}, u32[]{:S(2)}) copy-start(f32[256,8,4]{0,1,2:T(8,128)} %copy.154) | copy-start | bytes 98308
  76.2 1.6 copy-start.19
  76.2 3.7 %copy-start.17 = (f32[2,128,8,48]{1,3,2,0:T(8,128)S(1)}, f32[2,128,8,48]{1,3,2,0:T(8,128)}, u32[]{:S(2)}) copy-start(f32[2,128,8,48]{1,3,2,0:T(8,128)} %convolution_bitcast_fusion.4) | copy-start | bytes 1179652
  77.6 4.4 %copy-start.37 = (bf16[4,8,48]{2,1,0:T(8,128)(2,1)S(1)}, bf16[4,8,48]{2,1,0:T(8,128)(2,1)}, u32[]{:S(2)}) copy-start(bf16[4,8,48]{2,1,0:T(8,128)(2,1)} %copy-done.36) | copy-start | bytes 9220
  77.6 4.7 %copy-start.2 = (bf16[256,4,384]{0,2,1:T(8,128)(2,1)S(1)}, bf16[256,4,384]{0,2,1:T(8,128)(2,1)}, u32[]{:S(2)}) copy-start(bf16[256,4,384]{0,2,1:T(8,128)(2,1)} %copy.149) | copy-start | bytes 2359300
  80.2 3.4 %copy-start.5 = (f32[256,8,48]{2,1,0:T(8,128)S(1)}, f32[256,8,48]{2,1,0:T(8,128)}, u32[]{:S(2)}) copy-start(f32[256,8,48]{2,1,0:T(8,128)} %copy.103) | copy-start | bytes 1179652
  80.3 3.4 %copy-start.13 = (f32[256,8,4]{1,2,0:T(4,128)S(1)}, f32[256,8,4]{1,2,0:T(4,128)}, u32[]{:S(2)}) copy-start(f32[256,8,4]{1,2,0:T(4,128)} %copy.104) | copy-start | bytes 98308
  80.3 29.6 %collective-permute-start.1 = (bf16[128,768]{0,1:T(8,128)(2,1)}, bf16[128,768]{0,1:T(8,128)(2,1)}, u32[]{:S(2)}, u32[]{:S(2)}) collective-permute-start(bf16[128,768]{0,1:T(8,128)(2,1)} %fusion.32), channel_id=1, source_target_pairs={{1,0},{2,1},{3,2},{0,3},{5,4},{6,5},{7,6},{4,7},{9,8},{10,9},{11,1... | collective-permute-start | bytes 589832 | tf_op jit(solution)/shard_map/ppermute | solution.py:18
  82.6 4.4 %copy-start.14 = (bf16[256,384]{0,1:T(8,128)(2,1)}, bf16[256,384]{0,1:T(8,128)(2,1)S(1)}, u32[]{:S(2)}) copy-start(bf16[256,384]{0,1:T(8,128)(2,1)S(1)} %fusion.27) | copy-start | bytes 589828
  86.9 4.7 %copy-start.12 = (f32[256,8,4]{1,2,0:T(4,128)S(1)}, f32[256,8,4]{1,2,0:T(4,128)}, u32[]{:S(2)}) copy-start(f32[256,8,4]{1,2,0:T(4,128)} %copy.106) | copy-start | bytes 98308
  115.1 49.7 %copy-start.9 = (bf16[256,768]{0,1:T(8,128)(2,1)S(1)}, bf16[256,768]{0,1:T(8,128)(2,1)}, u32[]{:S(2)}) copy-start(bf16[256,768]{0,1:T(8,128)(2,1)} %copy-done.8) | copy-start | bytes 1179652
  115.2 49.9 %copy-start.15 = (bf16[256,384]{0,1:T(8,128)(2,1)S(1)}, bf16[256,384]{0,1:T(8,128)(2,1)}, u32[]{:S(2)}) copy-start(bf16[256,384]{0,1:T(8,128)(2,1)} %copy-done.14) | copy-start | bytes 589828
  115.2 49.9 %copy-start.22 = (bf16[384,384]{1,0:T(8,128)(2,1)S(1)}, bf16[384,384]{1,0:T(8,128)(2,1)}, u32[]{:S(2)}) copy-start(bf16[384,384]{1,0:T(8,128)(2,1)} %param.11) | copy-start | bytes 884740
  116.5 49.0 %all-to-all-start.1 = ((bf16[8,32,384]{2,1,0:T(8,128)(2,1)}), bf16[8,32,384]{2,1,0:T(8,128)(2,1)S(1)}, u32[]{:S(2)}, u32[]{:S(2)}) async-start(bf16[8,32,384]{2,1,0:T(8,128)(2,1)} %bitcast.44), calls=%async_computation.1 | async-start | bytes 393216 | tf_op jit(solution)/shard_map/all_to_all | solution.py:162
  167.9 89.5 %copy-start.27 = (f32[256,384]{1,0:T(8,128)}, f32[256,384]{1,0:T(8,128)S(1)}, u32[]{:S(2)}) copy-start(f32[256,384]{1,0:T(8,128)S(1)} %scatter_custom_fusion.1) | copy-start | bytes 1179652
  253.9 3.6 %copy-start.20 = (f32[384,768]{0,1:T(8,128)S(1)}, f32[384,768]{0,1:T(8,128)}, u32[]{:S(2)}) copy-start(f32[384,768]{0,1:T(8,128)} %get-tuple-element.23) | copy-start | bytes 3538948
  (3 other events, 3.8 us)
Sparse Core Ops, SparseCore 0:
  115.2 138.6 all-reduce.2
where the time goes:
time: 268 us; the launch traced here: 267 us
  waiting for transfers between devices  86 us (32%)
  local copies, waits for them, and re-layouts  45.6 us (17%)
  blocking collectives  41.1 us (15%)
  other arithmetic  35.5 us (13%)
  matrix products  28.5 us (11%)
  starting transfers between devices  15.1 us (6%)
  between operations  14.8 us (6%)
    psum x1, waiting for transfers between devices, shards(): lax.psum((rows_contracted(features, grad_query), rows_contracted(features...  86 us
    psum x1, blocking collectives, shards(): lax.psum((rows_contracted(features, grad_query), rows_contracted(features...  41.1 us
    dot_general x12, matrix products, einsum_bf(): return jnp.einsum(spec, left, right, preferred_element_type=jnp.float32)  16.5 us
    unnamed x101, local copies, waits for them, and re-layouts  9.38 us
    concatenate x2, local copies, waits for them, and re-layouts, attend(): jnp.concatenate([einsum_bf('rhk,rhd->rkhd', ds_exp, q_heads).reshape(row_...  9.23 us
    gather x2, local copies, waits for them, and re-layouts, shards(): expand_kv = slot_kv[expander]  9.13 us
    scatter-add x1, other arithmetic, shards(): jax.ops.segment_sum(exp_grad.reshape(-1, 2 * feat_width), expander.reshap...  8.33 us
    transpose x2, other arithmetic, einsum_bf(): return jnp.einsum(spec, left, right, preferred_element_type=jnp.float32)  7.58 us
  transfers between devices with their start and end apart: 5, of which 1 were waited for; matrix products, arithmetic and copies ran while one was open for 18% of the time, Pallas kernels for 0%

commit v1 on v0

--- a/solution.py
+++ b/solution.py
@@ -129,6 +129,91 @@
     return (attn_out, grad_query, window_grad, exp_grad, virt_grad)
 
 
+ROW_PACK = 16
+
+
+def exchange_stages(dom_size, rows_size):
+    dom_bits = [1 << i for i in range(dom_size.bit_length() - 1)]
+    rows_bits = [1 << i for i in range(rows_size.bit_length() - 1)]
+    stages = [[("rows", bit)] for bit in rows_bits[:1]]
+    rest = [("rows", bit) for bit in rows_bits[1:2]] + [("dom", bit) for bit in dom_bits[:1]]
+    rest += [("dom", bit) for bit in dom_bits[1:]] + [("rows", bit) for bit in rows_bits[2:]]
+    for at in range(0, len(rest), 2):
+        stages.append(rest[at : at + 2])
+    return stages
+
+
+def partner_masks(stage):
+    masks = []
+    for digit in range(1, 1 << len(stage)):
+        dom_mask = sum(bit for i, (axis, bit) in enumerate(stage) if axis == "dom" and digit >> i & 1)
+        rows_mask = sum(
+            bit for i, (axis, bit) in enumerate(stage) if axis == "rows" and digit >> i & 1
+        )
+        masks.append((digit, dom_mask, rows_mask))
+    return masks
+
+
+def own_digit(stage):
+    digit = jnp.int32(0)
+    for i, (axis, bit) in enumerate(stage):
+        digit += jnp.where(lax.axis_index(axis) & bit, 1 << i, 0)
+    return digit
+
+
+def swapped(block, dom_mask, rows_mask):
+    dom_size, rows_size = lax.axis_size("dom"), lax.axis_size("rows")
+    route = [
+        (a * rows_size + b, (a ^ dom_mask) * rows_size + (b ^ rows_mask))
+        for a in range(dom_size)
+        for b in range(rows_size)
+    ]
+    return lax.ppermute(block, ("dom", "rows"), route)
+
+
+def paired_sum(terms):
+    while len(terms) > 1:
+        terms = [left + right for left, right in zip(terms[::2], terms[1::2])]
+    return terms[0]
+
+
+def summed_everywhere(chunk, rider):
+    stages = exchange_stages(lax.axis_size("dom"), lax.axis_size("rows"))
+    scattered = []
+    for stage in stages:
+        group = 1 << len(stage)
+        own = own_digit(stage)
+        rows = chunk.shape[0]
+        halved = rows % (group * ROW_PACK) == 0
+        part = rows // group if halved else rows
+        scattered.append((stage, own, part, halved))
+        rider_bf = rider.astype(jnp.bfloat16)
+        kept = lax.dynamic_slice_in_dim(chunk, own * part, part) if halved else chunk
+        if not halved:
+            kept = kept.astype(jnp.bfloat16).astype(jnp.float32)
+        terms, rider_terms = [kept], [rider_bf.astype(jnp.float32)]
+        for digit, dom_mask, rows_mask in partner_masks(stage):
+            block = (
+                lax.dynamic_slice_in_dim(chunk, (own ^ digit) * part, part) if halved else chunk
+            )
+            message = jnp.concatenate([block.astype(jnp.bfloat16), rider_bf], axis=0)
+            arrived = swapped(message, dom_mask, rows_mask).astype(jnp.float32)
+            terms.append(arrived[:part])
+            rider_terms.append(arrived[part:])
+        chunk, rider = paired_sum(terms), paired_sum(rider_terms)
+    held = chunk.astype(jnp.bfloat16)
+    for stage, own, part, halved in reversed(scattered):
+        if not halved:
+            continue
+        whole = jnp.zeros((part << len(stage), held.shape[1]), jnp.bfloat16)
+        whole = lax.dynamic_update_slice_in_dim(whole, held, own * part, 0)
+        for digit, dom_mask, rows_mask in partner_masks(stage):
+            arrived = swapped(held, dom_mask, rows_mask)
+            whole = lax.dynamic_update_slice_in_dim(whole, arrived, (own ^ digit) * part, 0)
+        held = whole
+    return held.astype(jnp.float32), rider
+
+
 def project_slots(slot_grad, w_keyval):
     return lax.optimization_barrier(times_transposed(slot_grad, w_keyval).astype(jnp.bfloat16))
 
@@ -164,28 +249,29 @@
     )
     grad_features = times_transposed(grad_query, w_query) + times_transposed(local_grad, w_keyval)
     grad_features = grad_features.at[send_flat].add(returned_feat.astype(jnp.float32))
-    grad_wq, grad_wkv, grad_wo, virt_total = lax.psum(
-        (
+    factor = (row_count * lax.axis_size("dom") * lax.axis_size("rows")) ** (-0.5)
+    virt_wkv = jnp.dot(virtual.astype(jnp.float32).T, virt_grad, precision=lax.Precision.HIGHEST)
+    grad_wkv = rows_contracted(features, local_grad) + slot_weight + virt_wkv
+    partial = jnp.concatenate(
+        [
             rows_contracted(features, grad_query),
-            rows_contracted(features, local_grad) + slot_weight,
+            grad_wkv[:, :feat_width],
+            grad_wkv[:, feat_width:],
             rows_contracted(attn_out, out_grad),
-            virt_grad,
-        ),
-        ("dom", "rows"),
-    )
-    grad_wkv = grad_wkv + jnp.dot(
-        virtual.astype(jnp.float32).T, virt_total, precision=lax.Precision.HIGHEST
-    )
-    grad_virtual = jnp.dot(
-        virt_total, w_keyval.astype(jnp.float32).T, precision=lax.Precision.HIGHEST
-    )
-    factor = (row_count * lax.axis_size("dom") * lax.axis_size("rows")) ** (-0.5)
+        ],
+        axis=0,
+    )
+    virt_part = jnp.dot(virt_grad, w_keyval.astype(jnp.float32).T, precision=lax.Precision.HIGHEST)
+    virt_rows = virt_part.shape[0]
+    virt_part = jnp.pad(virt_part, ((0, -virt_rows % ROW_PACK), (0, 0)))
+    total, virt_total = summed_everywhere(partial * factor, virt_part * factor)
+    grad_wq, grad_wk, grad_wv, grad_wo = jnp.split(total, 4, axis=0)
     return (
         grad_features,
-        grad_wq * factor,
-        grad_wkv * factor,
-        grad_wo * factor,
-        grad_virtual * factor,
+        grad_wq,
+        jnp.concatenate([grad_wk, grad_wv], axis=1),
+        grad_wo,
+        virt_total[:virt_rows],
     )
 
 

time: 268 us -> 168 us (0.63)
  waiting for transfers between devices: 86 us -> 22.8 us
  blocking collectives: 41.1 us -> 0 us
  starting transfers between devices: 15.1 us -> 30.2 us
  between operations: 14.8 us -> 1.74 us
  other arithmetic: 35.5 us -> 39.3 us
  matrix products: 28.5 us -> 25.7 us
    psum x1 -> x0, waiting for transfers between devices: 86 us -> none  [shards(): lax.psum((rows_contracted(features, grad_query), rows_contracted(features...]
    psum x1 -> x0, blocking collectives: 41.1 us -> none  [shards(): lax.psum((rows_contracted(features, grad_query), rows_contracted(features...]
    ppermute x0 -> x14, waiting for transfers between devices: none -> 22.8 us  [swapped(): return lax.ppermute(block, ('dom', 'rows'), route)]
    ppermute x0 -> x14, starting transfers between devices: none -> 16.2 us  [swapped(): return lax.ppermute(block, ('dom', 'rows'), route)]
    dot_general x4, matrix products: 5.83 us -> 3.03 us  [rows_contracted(): lax.dot_general(left, right, (((0,), (0,)), ((), ())), preferred_element_...]
    unnamed x101 -> x135, local copies, waits for them, and re-layouts: 9.38 us -> 10.7 us
  transfers between devices with their start and end apart: 5 -> 18, of which waited for: 1 -> 9; matrix products, arithmetic and copies ran while one was open for 18% -> 31% of each run, Pallas kernels for 0% -> 0%
where the time goes in v1:
time: 168 us; the launch traced here: 167 us
  local copies, waits for them, and re-layouts  46.9 us (28%)
  other arithmetic  39.3 us (23%)
  starting transfers between devices  30.2 us (18%)
  matrix products  25.7 us (15%)
  waiting for transfers between devices  22.8 us (14%)
  between operations  1.74 us (1%)
    ppermute x14, waiting for transfers between devices, swapped(): return lax.ppermute(block, ('dom', 'rows'), route)  22.8 us
    ppermute x14, starting transfers between devices, swapped(): return lax.ppermute(block, ('dom', 'rows'), route)  16.2 us
    dot_general x12, matrix products, einsum_bf(): return jnp.einsum(spec, left, right, preferred_element_type=jnp.float32)  15.3 us
    unnamed x135, local copies, waits for them, and re-layouts  10.7 us
    concatenate x2, local copies, waits for them, and re-layouts, attend(): jnp.concatenate([einsum_bf('rhk,rhd->rkhd', ds_exp, q_heads).reshape(row_...  9.36 us
    gather x2, local copies, waits for them, and re-layouts, shards(): expand_kv = slot_kv[expander]  9.14 us
    scatter-add x1, other arithmetic, shards(): jax.ops.segment_sum(exp_grad.reshape(-1, 2 * feat_width), expander.reshap...  8.68 us
    all_to_all x1, starting transfers between devices, shards(): lax.all_to_all(sent_features, 'dom', split_axis=0, concat_axis=0, tiled=T...  6.95 us
  transfers between devices with their start and end apart: 18, of which 9 were waited for; matrix products, arithmetic and copies ran while one was open for 31% of the time, Pallas kernels for 0%

profile of v1, /device:TPU:0, one launch (start us, length us, event | category | flops | bytes accessed | tf_op | source)
XLA Modules:
  0.0 166.7 jit_solution(16630994454869992244)
XLA Ops:
  1.7 1.3 convolution_convert_fusion.1
  4.8 1.8 %gather_fusion = bf16[256,384]{1,0:T(8,128)(2,1)} fusion(bf16[256,384]{1,0:T(8,128)(2,1)S(1)} %copy-done.1, s32[1024]{0:T(1024)S(1)} %pad_clamp_fusion), kind=kCustom, calls=%fused_computation | custom fusion | bytes 394240 | tf_op jit(solution)/shard_map/gather | solution.py:228
  6.6 6.9 %all-to-all-start = ((bf16[8,32,384]{2,1,0:T(8,128)(2,1)}), bf16[8,32,384]{2,1,0:T(8,128)(2,1)}, u32[]{:S(2)}, u32[]{:S(2)}) async-start(bf16[8,32,384]{2,1,0:T(8,128)(2,1)} %bitcast.11), calls=%async_computation | async-start | bytes 393216 | tf_op jit(solution)/shard_map/all_to_all | solution.py:230
  15.8 1.2 copy.95
  18.9 1.2 copy.93
  20.2 1.6 fusion
  22.6 1.3 fusion.75
  26.6 2.1 %fusion.9 = (f32[2,128,8]{1,2,0:T(8,128)}, f32[2,8,256,128]{3,2,1,0:T(8,128)S(1)}) fusion(pred[2,128,256]{1,2,0:T(8,128)(4,1)S(1)} %copy.71, bf16[2,256,8,48]{1,3,2,0:T(8,128)(2,1)S(1)} %bitcast.216, bf16[2,128,8,48]{1,0,3,2:T(2,128)(2,1)} %reshape.204), kind=kOutput, calls=%fused_computation.25 | convolution fusion | flops 51902464 | bytes 2760704 | tf_op jit(solution)/shard_map/tqhd,tkhd->tqhk/dot_general | solution.py:22
  28.7 1.3 convolution_convert_fusion
  30.0 5.2 %gather_fusion.1 = bf16[1024,768]{1,0:T(8,128)(2,1)} fusion(bf16[256,768]{1,0:T(8,128)(2,1)S(1)} %convolution_convert_fusion, s32[1024]{0:T(1024)S(1)} %broadcast_clamp_fusion), kind=kCustom, calls=%fused_computation.1 | custom fusion | bytes 3149824 | tf_op jit(solution)/shard_map/gather | solution.py:232
  35.2 3.9 %reshape.235 = bf16[256,4,768]{2,1,0:T(4,128)(2,1)} reshape(bf16[1024,768]{1,0:T(8,128)(2,1)} %gather_fusion.1) | data formatting | bytes 3145728 | tf_op jit(solution)/shard_map/gather | solution.py:232
  39.1 3.1 %fusion.71 = (bf16[256,4,384]{2,1,0:T(4,128)(2,1)}, bf16[256,4,384]{2,1,0:T(4,128)(2,1)}) fusion(bf16[256,4,768]{2,1,0:T(4,128)(2,1)} %reshape.235), kind=kLoop, calls=%fused_computation.169 | loop fusion | bytes 3145728 | tf_op jit(solution)/shard_map/slice | solution.py:55
  42.2 2.2 %copy.132 = bf16[256,4,384]{0,2,1:T(8,128)(2,1)} copy(bf16[256,4,384]{2,1,0:T(4,128)(2,1)} %get-tuple-element.12) | data formatting | bytes 1572864
  44.5 1.4 multiply_reduce_fusion.3
  48.8 1.7 %fusion.18 = f32[2,8,48,256]{3,2,1,0:T(8,128)} fusion(bf16[2,128,8,48]{1,0,3,2:T(2,128)(2,1)S(1)} %copy-done.41, f32[2,8,256,128]{3,2,1,0:T(8,128)S(1)} %get-tuple-element.41, f32[2,128,8]{1,2,0:T(8,128)S(1)} %bitcast_add_fusion.7, f32[2,128,8]{1,2,0:T(8,128)S(1)} %bitcast_maximum_fusion.1, pred[2,128,256]{1,2,0:T(8,128)(4,1)S(1)} %copy.71), kind=kOutput, calls=%fused_computation.62 | convolution fusion | flops 53477376 | bytes 3162112 | tf_op jit(solution)/shard_map/tqhk,tqhd->tkhd/dot_general | solution.py:22
  50.5 2.2 %fusion.5 = (f32[2,128,8]{1,2,0:T(8,128)S(1)}, f32[2,8,256,128]{3,2,1,0:T(8,128)}) fusion(f32[2,128,8]{1,2,0:T(8,128)S(1)} %bitcast_add_fusion.7, f32[2,128,8]{1,2,0:T(8,128)S(1)} %bitcast_maximum_fusion.1, f32[2,8,256,128]{3,2,1,0:T(8,128)S(1)} %get-tuple-element.41, pred[2,128,256]{1,2,0:T(8,128)(4,1)S(1)} %copy.71, ...), kind=kOutput, calls=%fused_computation.15 | convolution fusion | flops 53999616 | bytes 4874240 | tf_op jit(solution)/shard_map/tqhd,tkhd->tqhk/dot_general | solution.py:22
  52.7 2.2 %copy.133 = bf16[256,4,384]{0,2,1:T(8,128)(2,1)} copy(bf16[256,4,384]{2,1,0:T(4,128)(2,1)} %get-tuple-element.11) | data formatting | bytes 1572864
  55.6 1.4 multiply_reduce_fusion.2
  57.1 2.5 %fusion.8 = bf16[2,128,8,256]{1,3,2,0:T(8,128)(2,1)S(1)} fusion(f32[2,8,256,128]{3,2,1,0:T(8,128)} %get-tuple-element.44, f32[2,128,8]{1,2,0:T(8,128)S(1)} %bitcast_add_fusion.4, f32[2,128,8]{1,2,0:T(8,128)S(1)} %bitcast_add_fusion.7, f32[2,128,8]{1,2,0:T(8,128)S(1)} %bitcast_maximum_fusion.1, f32[2,8,256,128]{3,2,1,0:T(8,128)S(1)} %get-tuple-element.41, ...), kind=kLoop, calls=%fused_computation.18 | loop fusion | flops 4718592 | bytes 5332992 | tf_op jit(solution)/shard_map/convert_element_type | solution.py:99
  64.4 1.7 %fusion.61 = f32[8,48,256]{2,1,0:T(8,128)} fusion(bf16[256,8,4]{0,2,1:T(4,128)(2,1)S(1)} %get-tuple-element.35, bf16[4,8,48]{2,1,0:T(8,128)(2,1)} %copy-done.53), kind=kOutput, calls=%fused_computation.148 | convolution fusion | flops 786432 | bytes 412672 | tf_op jit(solution)/shard_map/rhk,khd->rhd/dot_general | solution.py:22
  67.4 2.6 %convolution_bitcast_fusion.3 = f32[2,128,8,48]{1,3,2,0:T(8,128)} fusion(bf16[2,256,8,48]{1,3,2,0:T(8,128)(2,1)} %bitcast.226, f32[2,8,256,128]{3,2,1,0:T(8,128)S(1)} %get-tuple-element.41, f32[2,128,8]{1,2,0:T(8,128)} %copy-done.57, f32[2,128,8]{1,2,0:T(8,128)} %copy-done.49, pred[2,128,256]{1,2,0:T(8,128)(4,1)S(1)} %copy.71), kind=kOutput, calls=%fused_computation.39 | convolution fusion | flops 53477376 | bytes 2965504 | tf_op jit(solution)/shard_map/tqhk,tkhd->tqhd/dot_general | solution.py:22
  71.3 1.7 %convolution_bitcast_fusion = f32[384,768]{1,0:T(8,128)} fusion(f32[4,768]{1,0:T(4,128)S(1)} %constant_dynamic-update-slice_fusion.10, bf16[4,384]{1,0:T(4,128)(2,1)S(1)} %copy-done.62), kind=kOutput, calls=%fused_computation.34 | convolution fusion | flops 14155776 | bytes 1195008 | tf_op jit(solution)/shard_map/dot_general | solution.py:253
  73.0 1.4 collective-permute-start.1
  75.6 3.3 %multiply_bitcast_fusion = f32[256,4,8,48]{3,2,1,0:T(8,128)} fusion(f32[256,8,4]{1,2,0:T(4,128)S(1)} %copy.96, f32[256,8,48]{2,1,0:T(8,128)S(1)} %copy-done.11), kind=kLoop, calls=%fused_computation.4 | loop fusion | flops 393216 | bytes 1998848 | tf_op jit(solution)/shard_map/rhk,rhd->rkhd/transpose | solution.py:22
  78.8 4.7 %concatenate.55 = f32[1024,384]{1,0:T(8,128)} reshape(f32[256,4,8,48]{3,2,1,0:T(8,128)} %multiply_bitcast_fusion) | data formatting | bytes 3145728 | tf_op jit(solution)/shard_map/concatenate | solution.py:115
  83.5 3.3 %multiply_bitcast_fusion.1 = f32[256,4,8,48]{3,2,1,0:T(8,128)} fusion(f32[256,8,4]{1,2,0:T(4,128)S(1)} %copy-done.19, f32[256,8,48]{2,1,0:T(8,128)S(1)} %copy-done.12), kind=kLoop, calls=%fused_computation.5 | loop fusion | flops 393216 | bytes 1998848 | tf_op jit(solution)/shard_map/rhk,rhd->rkhd/transpose | solution.py:22
  86.8 4.7 %concatenate.54 = f32[1024,384]{1,0:T(8,128)} reshape(f32[256,4,8,48]{3,2,1,0:T(8,128)} %multiply_bitcast_fusion.1) | data formatting | bytes 3145728 | tf_op jit(solution)/shard_map/concatenate | solution.py:115
  94.1 8.7 %scatter_custom_fusion = f32[256,768]{1,0:T(8,128)S(1)} fusion(s32[1024]{0:T(1024)} %reshape.244, f32[1024,384]{1,0:T(8,128)} %concatenate.55, f32[]{:T(128)} %constant.23.clone.1, f32[1024,384]{1,0:T(8,128)} %concatenate.54, f32[]{:T(128)} %constant.26.clone.1), kind=kCustom, calls=%fused_computation.8 | custom fusion | flops 1572864 | bytes 3933184 | tf_op jit(solution)/shard_map/scatter-add | solution.py:243
  104.1 1.2 fusion.16
  105.7 1.3 fusion.12
  109.6 2.4 %collective-permute-done.2 = bf16[784,384]{1,0:T(8,128)(2,1)} collective-permute-done((bf16[784,384]{1,0:T(8,128)(2,1)}, bf16[784,384]{1,0:T(8,128)(2,1)}, u32[]{:S(2)}, u32[]{:S(2)}) %collective-permute-start.2) | collective-permute-done | bytes 602144 | tf_op jit(solution)/shard_map/ppermute | solution.py:171
  114.5 2.8 %collective-permute-start.5 = (bf16[208,384]{1,0:T(8,128)(2,1)S(1)}, bf16[208,384]{1,0:T(8,128)(2,1)S(1)}, u32[]{:S(2)}, u32[]{:S(2)}) collective-permute-start(bf16[208,384]{1,0:T(8,128)(2,1)S(1)} %get-tuple-element.33), channel_id=1, source_target_pairs={{0,6},{1,7},{2,4},{3,5},{4,2},{5,3},{6,0},{7,1},{8,14},{9,15},{10,... | collective-permute-start | bytes 479240 | tf_op jit(solution)/shard_map/ppermute | solution.py:171
  118.0 4.4 %collective-permute-done.5 = bf16[208,384]{1,0:T(8,128)(2,1)S(1)} collective-permute-done((bf16[208,384]{1,0:T(8,128)(2,1)S(1)}, bf16[208,384]{1,0:T(8,128)(2,1)S(1)}, u32[]{:S(2)}, u32[]{:S(2)}) %collective-permute-start.5) | collective-permute-done | bytes 159776 | tf_op jit(solution)/shard_map/ppermute | solution.py:171
  122.4 2.7 %collective-permute-done.4 = bf16[208,384]{1,0:T(8,128)(2,1)S(1)} collective-permute-done((bf16[208,384]{1,0:T(8,128)(2,1)S(1)}, bf16[208,384]{1,0:T(8,128)(2,1)S(1)}, u32[]{:S(2)}, u32[]{:S(2)}) %collective-permute-start.4) | collective-permute-done | bytes 159776 | tf_op jit(solution)/shard_map/ppermute | solution.py:171
  126.3 3.6 %collective-permute-start.8 = (bf16[64,384]{1,0:T(8,128)(2,1)S(1)}, bf16[64,384]{1,0:T(8,128)(2,1)S(1)}, u32[]{:S(2)}, u32[]{:S(2)}) collective-permute-start(bf16[64,384]{1,0:T(8,128)(2,1)S(1)} %get-tuple-element.30), channel_id=1, source_target_pairs={{0,24},{1,25},{2,26},{3,27},{4,28},{5,29},{6,30},{7,31},{8,16},{9,... | collective-permute-start | bytes 147464 | tf_op jit(solution)/shard_map/ppermute | solution.py:171
  130.8 1.7 %collective-permute-done.8 = bf16[64,384]{1,0:T(8,128)(2,1)S(1)} collective-permute-done((bf16[64,384]{1,0:T(8,128)(2,1)S(1)}, bf16[64,384]{1,0:T(8,128)(2,1)S(1)}, u32[]{:S(2)}, u32[]{:S(2)}) %collective-permute-start.8) | collective-permute-done | bytes 49184 | tf_op jit(solution)/shard_map/ppermute | solution.py:171
  133.1 1.8 %collective-permute-done.7 = bf16[64,384]{1,0:T(8,128)(2,1)S(1)} collective-permute-done((bf16[64,384]{1,0:T(8,128)(2,1)S(1)}, bf16[64,384]{1,0:T(8,128)(2,1)S(1)}, u32[]{:S(2)}, u32[]{:S(2)}) %collective-permute-start.7) | collective-permute-done | bytes 49184 | tf_op jit(solution)/shard_map/ppermute | solution.py:171
  136.8 5.2 %all-to-all-start.1 = ((bf16[8,32,384]{2,1,0:T(8,128)(2,1)}), bf16[8,32,384]{2,1,0:T(8,128)(2,1)S(1)}, u32[]{:S(2)}, u32[]{:S(2)}) async-start(bf16[8,32,384]{2,1,0:T(8,128)(2,1)} %bitcast.44), calls=%async_computation.1 | async-start | bytes 393216 | tf_op jit(solution)/shard_map/all_to_all | solution.py:247
  141.9 2.9 %collective-permute-start.10 = (bf16[48,384]{1,0:T(8,128)(2,1)S(1)}, bf16[48,384]{1,0:T(8,128)(2,1)S(1)}, u32[]{:S(2)}, u32[]{:S(2)}) collective-permute-start(bf16[48,384]{1,0:T(8,128)(2,1)S(1)} %get-tuple-element.8), channel_id=1, source_target_pairs={{0,16},{1,17},{2,18},{3,19},{4,20},{5,21},{6,22},{7,23},{8,24},{9,... | collective-permute-start | bytes 110600 | tf_op jit(solution)/shard_map/ppermute | solution.py:171
  144.8 1.5 collective-permute-start.11
  146.3 4.6 %collective-permute-done.10 = bf16[48,384]{1,0:T(8,128)(2,1)S(1)} collective-permute-done((bf16[48,384]{1,0:T(8,128)(2,1)S(1)}, bf16[48,384]{1,0:T(8,128)(2,1)S(1)}, u32[]{:S(2)}, u32[]{:S(2)}) %collective-permute-start.10) | collective-permute-done | bytes 36896 | tf_op jit(solution)/shard_map/ppermute | solution.py:171
  150.9 1.5 collective-permute-start.12
  152.9 1.5 collective-permute-start.13
  155.1 1.7 %collective-permute-done.12 = bf16[192,384]{1,0:T(8,128)(2,1)S(1)} collective-permute-done((bf16[192,384]{1,0:T(8,128)(2,1)S(1)}, bf16[192,384]{1,0:T(8,128)(2,1)S(1)}, u32[]{:S(2)}, u32[]{:S(2)}) %collective-permute-start.12) | collective-permute-done | bytes 147488 | tf_op jit(solution)/shard_map/ppermute | solution.py:171
  156.8 1.3 collective-permute-done.13
  158.1 2.3 %collective-permute-done.14 = bf16[192,384]{1,0:T(8,128)(2,1)S(1)} collective-permute-done((bf16[192,384]{1,0:T(8,128)(2,1)S(1)}, bf16[192,384]{1,0:T(8,128)(2,1)S(1)}, u32[]{:S(2)}, u32[]{:S(2)}) %collective-permute-start.14) | collective-permute-done | bytes 147488 | tf_op jit(solution)/shard_map/ppermute | solution.py:171
  160.9 2.4 %scatter_custom_fusion.1 = f32[256,384]{1,0:T(8,128)S(1)} fusion(f32[256,384]{1,0:T(8,128)S(1)} %convolution_add_fusion.1, s32[256]{0:T(256)} %bitcast.230, bf16[256,384]{1,0:T(8,128)(2,1)S(1)} %bitcast.225), kind=kCustom, calls=%fused_computation.77 | custom fusion | flops 196608 | bytes 589824 | tf_op jit(solution)/shard_map/scatter-add | solution.py:251
  164.4 1.2 fusion.72
  (255 shorter events, 40.4 us)
Async XLA Ops:
  0.7 12.9 %copy-start.61 = (s32[256,4]{0,1:T(4,128)S(1)}, s32[256,4]{0,1:T(4,128)}, u32[]{:S(2)}) copy-start(s32[256,4]{0,1:T(4,128)} %param.16) | copy-start | bytes 12292
  0.7 13.1 %copy-start.29 = (bf16[256,384]{1,0:T(8,128)(2,1)S(1)}, bf16[256,384]{1,0:T(8,128)(2,1)}, u32[]{:S(2)}) copy-start(bf16[256,384]{1,0:T(8,128)(2,1)} %param.10) | copy-start | bytes 589828
  0.7 13.1 %copy-start.39 = (bf16[384,384]{1,0:T(8,128)(2,1)S(1)}, bf16[384,384]{1,0:T(8,128)(2,1)}, u32[]{:S(2)}) copy-start(bf16[384,384]{1,0:T(8,128)(2,1)} %param.13) | copy-start | bytes 884740
  3.0 22.3 %collective-permute-start = (bf16[128,768]{1,0:T(8,128)(2,1)S(1)}, bf16[128,768]{1,0:T(8,128)(2,1)S(1)}, u32[]{:S(2)}, u32[]{:S(2)}) collective-permute-start(bf16[128,768]{1,0:T(8,128)(2,1)S(1)} %slice.125), channel_id=1, source_target_pairs={{3,0},{0,1},{1,2},{2,3},{7,4},{4,5},{5,6},{6,7},{11,8},{8,9},{9,10... | collective-permute-start | bytes 589832 | tf_op jit(solution)/shard_map/ppermute | solution.py:18
  6.6 10.3 %copy-start.27 = (bf16[384,384]{1,0:T(8,128)(2,1)S(1)}, bf16[384,384]{1,0:T(8,128)(2,1)}, u32[]{:S(2)}) copy-start(bf16[384,384]{1,0:T(8,128)(2,1)} %param.11) | copy-start | bytes 884740
  6.6 22.0 %all-to-all-start = ((bf16[8,32,384]{2,1,0:T(8,128)(2,1)}), bf16[8,32,384]{2,1,0:T(8,128)(2,1)}, u32[]{:S(2)}, u32[]{:S(2)}) async-start(bf16[8,32,384]{2,1,0:T(8,128)(2,1)} %bitcast.11), calls=%async_computation | async-start | bytes 393216 | tf_op jit(solution)/shard_map/all_to_all | solution.py:230
  14.2 4.7 %copy-start.15 = (bf16[256,384]{0,1:T(8,128)(2,1)}, bf16[256,384]{0,1:T(8,128)(2,1)S(1)}, u32[]{:S(2)}) copy-start(bf16[256,384]{0,1:T(8,128)(2,1)S(1)} %copy.79) | copy-start | bytes 589828
  17.0 5.3 %copy-start.62 = (bf16[4,384]{1,0:T(4,128)(2,1)S(1)}, bf16[4,384]{1,0:T(4,128)(2,1)}, u32[]{:S(2)}) copy-start(bf16[4,384]{1,0:T(4,128)(2,1)} %param.14) | copy-start | bytes 9220
  39.1 5.4 %copy-start.24 = (f32[256,8,48]{0,2,1:T(8,128)S(1)}, f32[256,8,48]{0,2,1:T(8,128)}, u32[]{:S(2)}) copy-start(f32[256,8,48]{0,2,1:T(8,128)} %convert.21) | copy-start | bytes 1179652
  47.4 9.7 %copy-start.49 = (f32[2,128,8]{1,2,0:T(8,128)}, f32[2,128,8]{1,2,0:T(8,128)S(1)}, u32[]{:S(2)}) copy-start(f32[2,128,8]{1,2,0:T(8,128)S(1)} %bitcast_maximum_fusion.1) | copy-start | bytes 24580
  48.7 8.4 %copy-start.57 = (f32[2,128,8]{1,2,0:T(8,128)}, f32[2,128,8]{1,2,0:T(8,128)S(1)}, u32[]{:S(2)}) copy-start(f32[2,128,8]{1,2,0:T(8,128)S(1)} %bitcast_add_fusion.7) | copy-start | bytes 24580
  48.8 6.1 %copy-start.50 = (f32[256,8]{0,1:T(8,128)}, f32[256,8]{0,1:T(8,128)S(1)}, u32[]{:S(2)}) copy-start(f32[256,8]{0,1:T(8,128)S(1)} %fusion.54) | copy-start | bytes 24580
  50.5 4.4 %copy-start.31 = (f32[256,8,4]{0,2,1:T(4,128)S(1)}, f32[256,8,4]{0,2,1:T(4,128)}, u32[]{:S(2)}) copy-start(f32[256,8,4]{0,2,1:T(4,128)} %get-tuple-element.39) | copy-start | bytes 98308
  50.5 4.4 %copy-start.38 = (f32[256,8,4]{0,1,2:T(8,128)S(1)}, f32[256,8,4]{0,1,2:T(8,128)}, u32[]{:S(2)}) copy-start(f32[256,8,4]{0,1,2:T(8,128)} %copy-done.37) | copy-start | bytes 98308
  50.5 4.4 %copy-start.55 = (bf16[4,8,48]{2,1,0:T(8,128)(2,1)S(1)}, bf16[4,8,48]{2,1,0:T(8,128)(2,1)}, u32[]{:S(2)}) copy-start(bf16[4,8,48]{2,1,0:T(8,128)(2,1)} %reshape.213) | copy-start | bytes 9220
  52.7 6.9 %copy-start.58 = (f32[2,128,8]{1,2,0:T(8,128)}, f32[2,128,8]{1,2,0:T(8,128)S(1)}, u32[]{:S(2)}) copy-start(f32[2,128,8]{1,2,0:T(8,128)S(1)} %get-tuple-element.43) | copy-start | bytes 24580
  70.0 4.5 %copy-start.23 = (f32[2,128,8,48]{1,3,2,0:T(8,128)S(1)}, f32[2,128,8,48]{1,3,2,0:T(8,128)}, u32[]{:S(2)}) copy-start(f32[2,128,8,48]{1,3,2,0:T(8,128)} %convolution_bitcast_fusion.4) | copy-start | bytes 1179652
  70.0 5.5 %copy-start.11 = (f32[256,8,48]{2,1,0:T(8,128)S(1)}, f32[256,8,48]{2,1,0:T(8,128)}, u32[]{:S(2)}) copy-start(f32[256,8,48]{2,1,0:T(8,128)} %copy.95) | copy-start | bytes 1179652
  73.0 30.1 %collective-permute-start.1 = (bf16[128,768]{0,1:T(8,128)(2,1)S(1)}, bf16[128,768]{0,1:T(8,128)(2,1)}, u32[]{:S(2)}, u32[]{:S(2)}) collective-permute-start(bf16[128,768]{0,1:T(8,128)(2,1)S(1)} %copy-done.40), channel_id=1, source_target_pairs={{1,0},{2,1},{3,2},{0,3},{5,4},{6,5},{7,6},{4,7},{9,8},{10,9},{11,1... | collective-permute-start | bytes 589832 | tf_op jit(solution)/shard_map/ppermute | solution.py:18
  78.8 4.7 %copy-start.12 = (f32[256,8,48]{2,1,0:T(8,128)S(1)}, f32[256,8,48]{2,1,0:T(8,128)}, u32[]{:S(2)}) copy-start(f32[256,8,48]{2,1,0:T(8,128)} %copy.93) | copy-start | bytes 1179652
  78.8 4.7 %copy-start.19 = (f32[256,8,4]{1,2,0:T(4,128)S(1)}, f32[256,8,4]{1,2,0:T(4,128)}, u32[]{:S(2)}) copy-start(f32[256,8,4]{1,2,0:T(4,128)} %copy.94) | copy-start | bytes 98308
  86.8 5.3 %copy-start.35 = (f32[2,128,8,48]{1,3,2,0:T(8,128)S(1)}, f32[2,128,8,48]{1,3,2,0:T(8,128)}, u32[]{:S(2)}) copy-start(f32[2,128,8,48]{1,3,2,0:T(8,128)} %convolution_bitcast_fusion.3) | copy-start | bytes 1179652
  86.8 5.6 %copy-start.5 = (bf16[256,4,384]{0,2,1:T(8,128)(2,1)S(1)}, bf16[256,4,384]{0,2,1:T(8,128)(2,1)}, u32[]{:S(2)}) copy-start(bf16[256,4,384]{0,2,1:T(8,128)(2,1)} %copy.133) | copy-start | bytes 2359300
  94.1 9.0 %copy-start.20 = (bf16[256,384]{0,1:T(8,128)(2,1)}, bf16[256,384]{0,1:T(8,128)(2,1)S(1)}, u32[]{:S(2)}) copy-start(bf16[256,384]{0,1:T(8,128)(2,1)S(1)} %fusion.26) | copy-start | bytes 589828
  94.1 10.0 %copy-start.3 = (f32[2,8,48,256]{3,2,1,0:T(8,128)S(1)}, f32[2,8,48,256]{3,2,1,0:T(8,128)}, u32[]{:S(2)}) copy-start(f32[2,8,48,256]{3,2,1,0:T(8,128)} %copy-done.2) | copy-start | bytes 2359300
  94.1 10.0 %copy-start.7 = (f32[2,8,48,256]{3,2,1,0:T(8,128)S(1)}, f32[2,8,48,256]{3,2,1,0:T(8,128)}, u32[]{:S(2)}) copy-start(f32[2,8,48,256]{3,2,1,0:T(8,128)} %fusion.18) | copy-start | bytes 2359300
  109.6 2.4 %collective-permute-start.2 = (bf16[784,384]{1,0:T(8,128)(2,1)}, bf16[784,384]{1,0:T(8,128)(2,1)}, u32[]{:S(2)}, u32[]{:S(2)}) collective-permute-start(bf16[784,384]{1,0:T(8,128)(2,1)} %pad_maximum_fusion.1), channel_id=1, source_target_pairs={{0,1},{1,0},{2,3},{3,2},{4,5},{5,4},{6,7},{7,6},{8,9},{9,8},{10,11... | collective-permute-start | bytes 1806344 | tf_op jit(solution)/shard_map/ppermute | solution.py:171
  114.5 7.9 %collective-permute-start.5 = (bf16[208,384]{1,0:T(8,128)(2,1)S(1)}, bf16[208,384]{1,0:T(8,128)(2,1)S(1)}, u32[]{:S(2)}, u32[]{:S(2)}) collective-permute-start(bf16[208,384]{1,0:T(8,128)(2,1)S(1)} %get-tuple-element.33), channel_id=1, source_target_pairs={{0,6},{1,7},{2,4},{3,5},{4,2},{5,3},{6,0},{7,1},{8,14},{9,15},{10,... | collective-permute-start | bytes 479240 | tf_op jit(solution)/shard_map/ppermute | solution.py:171
  117.2 7.9 %collective-permute-start.4 = (bf16[208,384]{1,0:T(8,128)(2,1)S(1)}, bf16[208,384]{1,0:T(8,128)(2,1)S(1)}, u32[]{:S(2)}, u32[]{:S(2)}) collective-permute-start(bf16[208,384]{1,0:T(8,128)(2,1)S(1)} %get-tuple-element.32), channel_id=1, source_target_pairs={{0,4},{1,5},{2,6},{3,7},{4,0},{5,1},{6,2},{7,3},{8,12},{9,13},{10,... | collective-permute-start | bytes 479240 | tf_op jit(solution)/shard_map/ppermute | solution.py:171
  117.5 7.6 %collective-permute-start.3 = (bf16[208,384]{1,0:T(8,128)(2,1)S(1)}, bf16[208,384]{1,0:T(8,128)(2,1)S(1)}, u32[]{:S(2)}, u32[]{:S(2)}) collective-permute-start(bf16[208,384]{1,0:T(8,128)(2,1)S(1)} %get-tuple-element.31), channel_id=1, source_target_pairs={{0,2},{1,3},{2,0},{3,1},{4,6},{5,7},{6,4},{7,5},{8,10},{9,11},{10,... | collective-permute-start | bytes 479240 | tf_op jit(solution)/shard_map/ppermute | solution.py:171
  122.4 13.3 %copy-start.9 = (f32[256,768]{1,0:T(8,128)S(1)}, f32[256,768]{1,0:T(8,128)}, u32[]{:S(2)}) copy-start(f32[256,768]{1,0:T(8,128)} %copy-done.8) | copy-start | bytes 2359300
  126.3 6.2 %collective-permute-start.8 = (bf16[64,384]{1,0:T(8,128)(2,1)S(1)}, bf16[64,384]{1,0:T(8,128)(2,1)S(1)}, u32[]{:S(2)}, u32[]{:S(2)}) collective-permute-start(bf16[64,384]{1,0:T(8,128)(2,1)S(1)} %get-tuple-element.30), channel_id=1, source_target_pairs={{0,24},{1,25},{2,26},{3,27},{4,28},{5,29},{6,30},{7,31},{8,16},{9,... | collective-permute-start | bytes 147464 | tf_op jit(solution)/shard_map/ppermute | solution.py:171
  129.9 5.0 %collective-permute-start.7 = (bf16[64,384]{1,0:T(8,128)(2,1)S(1)}, bf16[64,384]{1,0:T(8,128)(2,1)S(1)}, u32[]{:S(2)}, u32[]{:S(2)}) collective-permute-start(bf16[64,384]{1,0:T(8,128)(2,1)S(1)} %get-tuple-element.29), channel_id=1, source_target_pairs={{0,16},{1,17},{2,18},{3,19},{4,20},{5,21},{6,22},{7,23},{8,24},{9,... | collective-permute-start | bytes 147464 | tf_op jit(solution)/shard_map/ppermute | solution.py:171
  129.9 5.6 %collective-permute-start.6 = (bf16[64,384]{1,0:T(8,128)(2,1)S(1)}, bf16[64,384]{1,0:T(8,128)(2,1)S(1)}, u32[]{:S(2)}, u32[]{:S(2)}) collective-permute-start(bf16[64,384]{1,0:T(8,128)(2,1)S(1)} %get-tuple-element.28), channel_id=1, source_target_pairs={{0,8},{1,9},{2,10},{3,11},{4,12},{5,13},{6,14},{7,15},{8,0},{9,1},... | collective-permute-start | bytes 147464 | tf_op jit(solution)/shard_map/ppermute | solution.py:171
  135.5 17.3 %copy-start.47 = (bf16[64,384]{1,0:T(8,128)(2,1)}, bf16[64,384]{1,0:T(8,128)(2,1)S(1)}, u32[]{:S(2)}) copy-start(bf16[64,384]{1,0:T(8,128)(2,1)S(1)} %collective-permute-done.6) | copy-start | bytes 147460
  135.6 10.7 %collective-permute-start.9 = (bf16[48,384]{1,0:T(8,128)(2,1)S(1)}, bf16[48,384]{1,0:T(8,128)(2,1)S(1)}, u32[]{:S(2)}, u32[]{:S(2)}) collective-permute-start(bf16[48,384]{1,0:T(8,128)(2,1)S(1)} %get-tuple-element.8), channel_id=1, source_target_pairs={{0,8},{1,9},{2,10},{3,11},{4,12},{5,13},{6,14},{7,15},{8,0},{9,1},... | collective-permute-start | bytes 110600 | tf_op jit(solution)/shard_map/ppermute | solution.py:171
  136.8 23.8 %copy-start.21 = (bf16[256,384]{0,1:T(8,128)(2,1)S(1)}, bf16[256,384]{0,1:T(8,128)(2,1)}, u32[]{:S(2)}) copy-start(bf16[256,384]{0,1:T(8,128)(2,1)} %copy-done.20) | copy-start | bytes 589828
  136.8 23.8 %copy-start.28 = (bf16[384,384]{1,0:T(8,128)(2,1)S(1)}, bf16[384,384]{1,0:T(8,128)(2,1)}, u32[]{:S(2)}) copy-start(bf16[384,384]{1,0:T(8,128)(2,1)} %param.11) | copy-start | bytes 884740
  136.8 24.1 %all-to-all-start.1 = ((bf16[8,32,384]{2,1,0:T(8,128)(2,1)}), bf16[8,32,384]{2,1,0:T(8,128)(2,1)S(1)}, u32[]{:S(2)}, u32[]{:S(2)}) async-start(bf16[8,32,384]{2,1,0:T(8,128)(2,1)} %bitcast.44), calls=%async_computation.1 | async-start | bytes 393216 | tf_op jit(solution)/shard_map/all_to_all | solution.py:247
  141.9 9.0 %collective-permute-start.10 = (bf16[48,384]{1,0:T(8,128)(2,1)S(1)}, bf16[48,384]{1,0:T(8,128)(2,1)S(1)}, u32[]{:S(2)}, u32[]{:S(2)}) collective-permute-start(bf16[48,384]{1,0:T(8,128)(2,1)S(1)} %get-tuple-element.8), channel_id=1, source_target_pairs={{0,16},{1,17},{2,18},{3,19},{4,20},{5,21},{6,22},{7,23},{8,24},{9,... | collective-permute-start | bytes 110600 | tf_op jit(solution)/shard_map/ppermute | solution.py:171
  144.8 6.0 %collective-permute-start.11 = (bf16[48,384]{1,0:T(8,128)(2,1)S(1)}, bf16[48,384]{1,0:T(8,128)(2,1)S(1)}, u32[]{:S(2)}, u32[]{:S(2)}) collective-permute-start(bf16[48,384]{1,0:T(8,128)(2,1)S(1)} %get-tuple-element.8), channel_id=1, source_target_pairs={{0,24},{1,25},{2,26},{3,27},{4,28},{5,29},{6,30},{7,31},{8,16},{9,... | collective-permute-start | bytes 110600 | tf_op jit(solution)/shard_map/ppermute | solution.py:171
  150.9 5.8 %collective-permute-start.12 = (bf16[192,384]{1,0:T(8,128)(2,1)S(1)}, bf16[192,384]{1,0:T(8,128)(2,1)S(1)}, u32[]{:S(2)}, u32[]{:S(2)}) collective-permute-start(bf16[192,384]{1,0:T(8,128)(2,1)S(1)} %constant_dynamic-update-slice_fusion.6), channel_id=1, source_target_pairs={{0,2},{1,3},{2,0},{3,1},{4,6},{5,7},{6,4},{7,5},{8,10},{9,11},{10,... | collective-permute-start | bytes 442376 | tf_op jit(solution)/shard_map/ppermute | solution.py:171
  152.8 10.5 %copy-start.44 = (bf16[64,384]{1,0:T(8,128)(2,1)S(1)}, bf16[64,384]{1,0:T(8,128)(2,1)}, u32[]{:S(2)}) copy-start(bf16[64,384]{1,0:T(8,128)(2,1)} %copy-done.43) | copy-start | bytes 147460
  152.8 10.5 %copy-start.46 = (bf16[64,384]{1,0:T(8,128)(2,1)S(1)}, bf16[64,384]{1,0:T(8,128)(2,1)}, u32[]{:S(2)}) copy-start(bf16[64,384]{1,0:T(8,128)(2,1)} %copy-done.45) | copy-start | bytes 147460
  152.9 5.2 %collective-permute-start.13 = (bf16[192,384]{1,0:T(8,128)(2,1)S(1)}, bf16[192,384]{1,0:T(8,128)(2,1)S(1)}, u32[]{:S(2)}, u32[]{:S(2)}) collective-permute-start(bf16[192,384]{1,0:T(8,128)(2,1)S(1)} %constant_dynamic-update-slice_fusion.6), channel_id=1, source_target_pairs={{0,4},{1,5},{2,6},{3,7},{4,0},{5,1},{6,2},{7,3},{8,12},{9,13},{10,... | collective-permute-start | bytes 442376 | tf_op jit(solution)/shard_map/ppermute | solution.py:171
  154.4 9.0 %copy-start.48 = (bf16[64,384]{1,0:T(8,128)(2,1)S(1)}, bf16[64,384]{1,0:T(8,128)(2,1)}, u32[]{:S(2)}) copy-start(bf16[64,384]{1,0:T(8,128)(2,1)} %copy-done.47) | copy-start | bytes 147460
  154.4 6.0 %collective-permute-start.14 = (bf16[192,384]{1,0:T(8,128)(2,1)S(1)}, bf16[192,384]{1,0:T(8,128)(2,1)S(1)}, u32[]{:S(2)}, u32[]{:S(2)}) collective-permute-start(bf16[192,384]{1,0:T(8,128)(2,1)S(1)} %constant_dynamic-update-slice_fusion.6), channel_id=1, source_target_pairs={{0,6},{1,7},{2,4},{3,5},{4,2},{5,3},{6,0},{7,1},{8,14},{9,15},{10,... | collective-permute-start | bytes 442376 | tf_op jit(solution)/shard_map/ppermute | solution.py:171
  160.5 3.8 %collective-permute-start.15 = (bf16[768,384]{1,0:T(8,128)(2,1)S(1)}, bf16[768,384]{1,0:T(8,128)(2,1)S(1)}, u32[]{:S(2)}, u32[]{:S(2)}) collective-permute-start(bf16[768,384]{1,0:T(8,128)(2,1)S(1)} %constant_dynamic-update-slice_fusion.2), channel_id=1, source_target_pairs={{0,1},{1,0},{2,3},{3,2},{4,5},{5,4},{6,7},{7,6},{8,9},{9,8},{10,11... | collective-permute-start | bytes 1769480 | tf_op jit(solution)/shard_map/ppermute | solution.py:171
  (34 other events, 72.8 us)

commit v2 on v0

v2 whole, which is shorter than its diff:
```python
import functools
import math

import jax
import jax.numpy as jnp
from jax import lax
from jax.experimental import pallas as pl
from jax.experimental.pallas import tpu as pltpu
from jax.sharding import PartitionSpec as P

HEADS = 8
TILE = 128
ROW_PACK = 16
NEGATIVE_FILL = -1e30
VMEM_BYTES = 48 * 1024 * 1024


def f32_dot(left, right):
    return jnp.dot(left, right, preferred_element_type=jnp.float32)


def rows_contracted(left, right):
    return lax.dot_general(
        left, right, (((0,), (0,)), ((), ())), preferred_element_type=jnp.float32
    )


def times_transposed(left, right):
    return lax.dot_general(
        left, right, (((1,), (1,)), ((), ())), preferred_element_type=jnp.float32
    )


def rounded(value):
    return value.astype(jnp.bfloat16)


def exchange_stages(dom_size, rows_size):
    dom_bits = [1 << i for i in range(dom_size.bit_length() - 1)]
    rows_bits = [1 << i for i in range(rows_size.bit_length() - 1)]
    stages = [[("rows", bit)] for bit in rows_bits[:1]]
    rest = [("rows", bit) for bit in rows_bits[1:2]] + [("dom", bit) for bit in dom_bits]
    rest += [("rows", bit) for bit in rows_bits[2:]]
    for at in range(0, len(rest), 2):
        stages.append(rest[at : at + 2])
    return stages


def scattered_stages(stages, rows):
    taken = []
    for stage in stages:
        if rows % (ROW_PACK << len(stage)):
            break
        rows >>= len(stage)
        taken.append(stage)
    return taken


def partner_masks(stage):
    masks = []
    for digit in range(1, 1 << len(stage)):
        by_axis = {"dom": 0, "rows": 0}
        for i, (axis, bit) in enumerate(stage):
            if digit >> i & 1:
                by_axis[axis] |= bit
        masks.append((by_axis["dom"], by_axis["rows"]))
    return masks


def own_piece(stages):
    index = jnp.int32(0)
    for stage in stages:
        index = index << len(stage)
        for i, (axis, bit) in enumerate(stage):
            index += jnp.where(lax.axis_index(axis) & bit, 1 << i, 0)
    return index


def swapped(block, dom_mask, rows_mask):
    dom_size, rows_size = lax.axis_size("dom"), lax.axis_size("rows")
    route = [
        (a * rows_size + b, (a ^ dom_mask) * rows_size + (b ^ rows_mask))
        for a in range(dom_size)
        for b in range(rows_size)
    ]
    return lax.ppermute(block, ("dom", "rows"), route)


def shifted(block, axis, distance):
    devices = range(lax.axis_size(axis))
    route = [((i - distance) % len(devices), i) for i in devices]
    return lax.ppermute(block, axis, route)


def paired_sum(terms):
    while len(terms) > 1:
        terms = [left + right for left, right in zip(terms[::2], terms[1::2])]
    return terms[0]


def summed_everywhere(keep, message, rider, stages, scattered):
    pieces = []
    first = True
    for stage in stages:
        halved = stage in scattered
        rider_bf = rounded(rider)
        masks = partner_masks(stage)
        if not halved:
            keep = rounded(keep).astype(jnp.float32)
        part = keep.shape[0]
        if halved and not first:
            part //= 1 << len(stage)
        terms, rider_terms = [keep[:part]], [rider_bf.astype(jnp.float32)]
        for at, (dom_mask, rows_mask) in enumerate(masks, 1):
            if not first:
                block = keep[at * part : (at + 1) * part] if halved else keep
                message = jnp.concatenate([rounded(block), rider_bf], axis=0)
            arrived = swapped(message, dom_mask, rows_mask).astype(jnp.float32)
            terms.append(arrived[:part])
            rider_terms.append(arrived[part:])
        keep, rider = paired_sum(terms), paired_sum(rider_terms)
        first = False
    held = rounded(keep)
    for stage in reversed(scattered[1:]):
        held = jnp.concatenate(
            [held] + [swapped(held, *masks) for masks in partner_masks(stage)], axis=0
        )
    return held, swapped(held, *partner_masks(scattered[0])[0]), rider


def listed_rows(dom, send_ref, row_count):
    dom_size, per_peer = send_ref.shape
    slots = dom_size * per_peer
    slot = lax.broadcasted_iota(jnp.int32, (slots, per_peer), 0)
    place = lax.broadcasted_iota(jnp.int32, (slots, per_peer), 1)
    peer = (slot // per_peer) ^ dom
    listed = jnp.zeros((slots, per_peer), jnp.int32)
    for at in range(dom_size):
        listed += jnp.where((peer == at) & (place == slot % per_peer), send_ref[at : at + 1, :], 0)
    column = jnp.sum(listed, axis=1, keepdims=True)
    rows = lax.broadcasted_iota(jnp.int32, (slots, row_count), 1)
    return jnp.where(column == rows, 1.0, 0.0).astype(jnp.bfloat16)


def pick_kernel(place_ref, feat_ref, send_ref, *out_refs):
    chosen = listed_rows(place_ref[0], send_ref, feat_ref.shape[0])
    picked = rounded(f32_dot(chosen, feat_ref[...]))
    per_peer = send_ref.shape[1]
    for at, out_ref in enumerate(out_refs):
        out_ref[...] = picked[at * per_peer : (at + 1) * per_peer]


def attend_kernel(
    dom_size,
    rows_per_piece,
    factor,
    place_ref,
    feat_ref,
    halo_ref,
    *refs,
):
    piece_refs, refs = refs[:dom_size], refs[dom_size:]
    og_ref, wq_ref, wkv_ref, wo_ref, virt_ref, nbr_ref, exp_ref = refs[:7]
    refs = refs[7:]
    gf_ref, halo_feat_ref = refs[:2]
    slot_feat_refs, refs = refs[2 : 2 + dom_size], refs[2 + dom_size :]
    keep_ref, send_ref, rider_ref = refs[:3]
    ext_ref, kv_ref, kvt_ref, extt_ref, qt_ref, odt_ref, gqt_ref, gkvt_ref, ot_ref = refs[3:12]

    row_count, width = feat_ref.shape
    tile = halo_ref.shape[0]
    tile_count = row_count // tile
    per_peer = piece_refs[0].shape[0]
    slots = dom_size * per_peer
    near = tile + row_count
    virt_at = near + slots
    ext_rows = ext_ref.shape[0]
    far = ext_rows - near
    virt_rows = virt_ref.shape[0]
    head_dim = width // HEADS
    scale = 1.0 / math.sqrt(head_dim)

    ext_ref[:tile] = halo_ref[...]
    ext_ref[tile:near] = feat_ref[...]
    for at, piece_ref in enumerate(piece_refs):
        ext_ref[near + at * per_peer : near + (at + 1) * per_peer] = piece_ref[...]
    ext_ref[virt_at:] = jnp.concatenate(
        [virt_ref[...], jnp.zeros((ext_rows - virt_at - virt_rows, width), jnp.bfloat16)], axis=0
    )
    kv_ref[...] = rounded(f32_dot(ext_ref[...], wkv_ref[...]))
    extt_ref[...] = ext_ref[...].T
    kvt_ref[...] = kv_ref[...].T
    qt_ref[...] = rounded(rows_contracted(wq_ref[...], extt_ref[:, tile:near]))
    odt_ref[...] = rounded(times_transposed(wo_ref[...], og_ref[...]))

    def multiplicity(key_rows, named, first, last):
        position = lax.broadcasted_iota(jnp.int32, (key_rows, row_count), 0)
        count = jnp.zeros((key_rows, row_count), jnp.float32)
        for at in range(first, last):
            count += jnp.where(named[at : at + 1, :] == position, 1.0, 0.0)
        return count

    local_bias = jnp.where(
        multiplicity(2 * tile, nbr_ref[...], 0, nbr_ref.shape[0]) > 0.0, 0.0, NEGATIVE_FILL
    )
    expander = exp_ref[...]
    expander = ((expander // per_peer) ^ place_ref[0]) * per_peer + expander % per_peer
    named_times = multiplicity(slots, expander, 0, expander.shape[0])
    slot_bias = jnp.full((slots, row_count), NEGATIVE_FILL, jnp.float32)
    for times in range(1, expander.shape[0] + 1):
        slot_bias = jnp.where(named_times == float(times), math.log(times) / scale, slot_bias)
    virt_row = lax.broadcasted_iota(jnp.int32, (ext_rows - virt_at, row_count), 0)
    virt_bias = jnp.where(virt_row < virt_rows, 0.0, NEGATIVE_FILL)
    far_bias = jnp.concatenate([slot_bias, virt_bias], axis=0)

    def tiles(of):
        return jnp.concatenate([of(t, slice(t * tile, (t + 1) * tile)) for t in range(tile_count)], 1)

    for head in range(HEADS):
        low, high = head * head_dim, (head + 1) * head_dim
        first = low // 128 * 128
        last = min(-(-high // 128) * 128, width)
        column = lax.broadcasted_iota(jnp.int32, (last - first, row_count), 0) + first
        of_head = (column >= low) & (column < high)
        q_rows = jnp.where(of_head, qt_ref[first:last, :], 0)
        d_rows = jnp.where(of_head, odt_ref[first:last, :], 0)

        def products(operand, start, stop):
            local = tiles(
                lambda t, lanes: f32_dot(
                    kv_ref[t * tile : (t + 2) * tile, start:stop], operand[:, lanes]
                )
            )
            return local, f32_dot(kv_ref[near:, start:stop], operand)

        s_local, s_far = products(q_rows, first, last)
        s_local += local_bias
        s_far += far_bias
        peak = jnp.maximum(
            jnp.max(s_local, axis=0, keepdims=True), jnp.max(s_far, axis=0, keepdims=True)
        )
        exponent_scale = scale * math.log2(math.e)
        e_local = jnp.exp2((s_local - peak) * exponent_scale)
        e_far = jnp.exp2((s_far - peak) * exponent_scale)
        total = jnp.sum(e_local, axis=0, keepdims=True) + jnp.sum(e_far, axis=0, keepdims=True)
        inverse = 1.0 / total
        p_local = e_local * inverse
        p_far = e_far * inverse
        dp_local, dp_far = products(d_rows, width + first, width + last)
        delta = jnp.sum(p_local * dp_local, axis=0, keepdims=True) + jnp.sum(
            p_far * dp_far, axis=0, keepdims=True
        )
        pb_local, pb_far = rounded(p_local), rounded(p_far)
        ds_local = rounded(p_local * (dp_local - delta))
        ds_far = rounded(p_far * (dp_far - delta))

        def to_queries(start, local, beyond):
            rows = slice(start + low, start + high)
            near_part = tiles(
                lambda t, lanes: f32_dot(kvt_ref[rows, t * tile : (t + 2) * tile], local[:, lanes])
            )
            return near_part + f32_dot(kvt_ref[rows, near:], beyond)

        ot_ref[low:high] = rounded(to_queries(width, pb_local, pb_far))
        gqt_ref[low:high] = rounded(to_queries(0, ds_local, ds_far) * scale)

        def to_keys(start, operand, local, beyond, factor):
            rows = slice(start + low, start + high)
            parts = []
            carried = None
            for t in range(tile_count):
                lanes = slice(t * tile, (t + 1) * tile)
                window = times_transposed(operand[:, lanes], local[:, lanes])
                previous = window[:, :tile]
                parts.append(previous if carried is None else previous + carried)
                carried = window[:, tile:]
            parts.append(carried)
            parts.append(times_transposed(operand, beyond))
            gathered = jnp.concatenate(parts, axis=1)
            gkvt_ref[rows] = rounded(gathered if factor is None else gathered * factor)

        to_keys(0, qt_ref[low:high], ds_local, ds_far, scale)
        to_keys(width, odt_ref[low:high], pb_local, pb_far, None)

    by_feature = f32_dot(wkv_ref[...], gkvt_ref[...])
    own = by_feature[:, tile:near] + f32_dot(wq_ref[...], gqt_ref[...])
    gf_ref[...] = own.T
    halo_feat_ref[...] = rounded(by_feature[:, :tile].T)
    slot_feat = rounded(by_feature[:, near:virt_at].T)
    for at, out_ref in enumerate(slot_feat_refs):
        out_ref[...] = slot_feat[at * per_peer : (at + 1) * per_peer]
    rider_ref[...] = by_feature[:, virt_at:].T * factor

    held = place_ref[1]
    blocks = keep_ref.shape[0] // rows_per_piece
    sums = (
        times_transposed(extt_ref[:, tile:near], gqt_ref[...]),
        times_transposed(extt_ref[...], gkvt_ref[:width]),
        times_transposed(extt_ref[...], gkvt_ref[width:]),
        f32_dot(ot_ref[...], og_ref[...]),
    )
    for at in range(2 * blocks):
        start = at * rows_per_piece
        value = sums[start // width][start % width : start % width + rows_per_piece] * factor
        distance = held ^ at
        kept = distance < blocks
        offset = pl.multiple_of((distance % blocks) * rows_per_piece, ROW_PACK)

        @pl.when(kept)
        def _():
            keep_ref[pl.ds(offset, rows_per_piece), :] = value

        @pl.when(jnp.logical_not(kept))
        def _():
            send_ref[pl.ds(offset, rows_per_piece), :] = rounded(value)

    send_ref[keep_ref.shape[0] :] = rounded(rider_ref[...])


def place_kernel(rows_per_piece, place_ref, near_ref, far_ref, gq_ref, gkv_ref, go_ref, all_ref):
    width = gq_ref.shape[0]
    half = near_ref.shape[0]
    all_ref[:half] = near_ref[...]
    all_ref[half:] = far_ref[...]
    for at in range(2 * half // rows_per_piece):
        offset = pl.multiple_of((place_ref[1] ^ at) * rows_per_piece, ROW_PACK)
        value = all_ref[pl.ds(offset, rows_per_piece), :].astype(jnp.float32)
        start = at * rows_per_piece
        rows = slice(start % width, start % width + rows_per_piece)
        which = start // width
        if which == 0:
            gq_ref[rows] = value
        elif which == 3:
            go_ref[rows] = value
        else:
            gkv_ref[rows, (which - 1) * width : which * width] = value


def return_kernel(place_ref, gf_ref, halo_ref, send_ref, *refs):
    piece_refs, out_ref = refs[:-1], refs[-1]
    row_count = gf_ref.shape[0]
    tile = halo_ref.shape[0]
    chosen = listed_rows(place_ref[0], send_ref, row_count)
    returned = jnp.concatenate([ref[...] for ref in piece_refs], axis=0)
    total = gf_ref[...] + rows_contracted(chosen, returned)
    out_ref[: row_count - tile] = total[: row_count - tile]
    out_ref[row_count - tile :] = total[row_count - tile :] + halo_ref[...].astype(jnp.float32)


def call(kernel, outs, args, name, scratch=(), flops=0):
    in_specs = [pl.BlockSpec(memory_space=pltpu.SMEM)]
    in_specs += [pl.BlockSpec(memory_space=pltpu.VMEM)] * (len(args) - 1)
    moved = sum(x.size * x.dtype.itemsize for x in list(args) + list(outs))
    return pl.pallas_call(
        kernel,
        out_shape=outs,
        in_specs=in_specs,
        out_specs=[pl.BlockSpec(memory_space=pltpu.VMEM)] * len(outs),
        scratch_shapes=scratch,
        compiler_params=pltpu.CompilerParams(vmem_limit_bytes=VMEM_BYTES),
        cost_estimate=pl.CostEstimate(flops=flops, bytes_accessed=moved, transcendentals=0),
        name=name,
    )(*args)


def shards(features, out_grad, w_query, w_keyval, w_out, virtual, local_nbr, expander, send_rows):
    row_count, width = features.shape
    dom_size, per_peer = send_rows.shape
    devices = lax.axis_size("dom") * lax.axis_size("rows")
    stages = exchange_stages(lax.axis_size("dom"), lax.axis_size("rows"))
    scattered = scattered_stages(stages, 4 * width)
    pieces = 1 << sum(len(stage) for stage in scattered)
    rows_per_piece = 4 * width // pieces
    place = jnp.stack([lax.axis_index("dom").astype(jnp.int32), own_piece(scattered)])
    bf16, f32 = jnp.bfloat16, jnp.float32
    shape = jax.ShapeDtypeStruct

    sent = call(
        pick_kernel,
        [shape((per_peer, width), bf16)] * dom_size,
        [place, features, send_rows],
        "pick_rows",
    )
    halo = shifted(features[row_count - TILE :], "rows", 1)
    arrived = [sent[0]] + [swapped(sent[at], at, 0) for at in range(1, dom_size)]

    ext_rows = TILE + row_count + dom_size * per_peer + ROW_PACK * -(-virtual.shape[0] // ROW_PACK)
    half = 2 * width
    rider_rows = ext_rows - TILE - row_count - dom_size * per_peer
    outs = [
        shape((row_count, width), f32),
        shape((TILE, width), bf16),
        *[shape((per_peer, width), bf16)] * dom_size,
        shape((half, width), f32),
        shape((half + rider_rows, width), bf16),
        shape((rider_rows, width), f32),
    ]
    scratch = [
        pltpu.VMEM((ext_rows, width), bf16),
        pltpu.VMEM((ext_rows, 2 * width), bf16),
        pltpu.VMEM((2 * width, ext_rows), bf16),
        pltpu.VMEM((width, ext_rows), bf16),
        pltpu.VMEM((width, row_count), bf16),
        pltpu.VMEM((width, row_count), bf16),
        pltpu.VMEM((width, row_count), bf16),
        pltpu.VMEM((2 * width, ext_rows), bf16),
        pltpu.VMEM((width, row_count), bf16),
    ]
    results = call(
        functools.partial(attend_kernel, dom_size, rows_per_piece, (row_count * devices) ** -0.5),
        outs,
        [place, features, halo, *arrived, out_grad, w_query, w_keyval, w_out, virtual]
        + [local_nbr.T, expander.T],
        "attend",
        scratch,
        flops=8 * ext_rows * width * width * 4,
    )
    own_feat, halo_feat = results[:2]
    slot_feat = results[2 : 2 + dom_size]
    keep, message, rider = results[2 + dom_size :]

    halo_back = shifted(halo_feat, "rows", -1)
    slots_back = [slot_feat[0]] + [swapped(slot_feat[at], at, 0) for at in range(1, dom_size)]
    near, far, rider = summed_everywhere(keep, message, rider, stages, scattered)
    (grad_features,) = call(
        return_kernel,
        [shape((row_count, width), f32)],
        [place, own_feat, halo_back, send_rows, *slots_back],
        "return_rows",
    )
    grad_wq, grad_wkv, grad_wo = call(
        functools.partial(place_kernel, rows_per_piece),
        [shape((width, width), f32), shape((width, 2 * width), f32), shape((width, width), f32)],
        [place, near, far],
        "place_sums",
        [pltpu.VMEM((4 * width, width), bf16)],
    )
    return grad_features, grad_wq, grad_wkv, grad_wo, rider[: virtual.shape[0]]


def solution(mesh):
    placed = (
        P(("dom", "rows"), None),
        P(("dom", "rows"), None),
        P(),
        P(),
        P(),
        P(),
        P(("dom", "rows"), None),
        P(("dom", "rows"), None),
        P(("dom", "rows"), None),
    )
    return jax.shard_map(
        shards,
        mesh=mesh,
        in_specs=placed,
        out_specs=(P(("dom", "rows"), None), P(), P(), P(), P()),
        check_vma=False,
    )
```

time: 268 us -> 97.3 us (0.36)
  waiting for transfers between devices: 86 us -> 30.6 us
  blocking collectives: 41.1 us -> 0 us
  local copies, waits for them, and re-layouts: 45.6 us -> 8.71 us
  other arithmetic: 35.5 us -> 1.23 us
  matrix products: 28.5 us -> 0 us
  starting transfers between devices: 15.1 us -> 41.1 us
  Pallas kernels: 0 us -> 14.3 us
  between operations: 14.8 us -> 0.85 us
    psum x1 -> x0, waiting for transfers between devices: 86 us -> none  [shards(): lax.psum((rows_contracted(features, grad_query), rows_contracted(features...]
    psum x1 -> x0, blocking collectives: 41.1 us -> none  [shards(): lax.psum((rows_contracted(features, grad_query), rows_contracted(features...]
    ppermute x0 -> x28, starting transfers between devices: none -> 39.5 us  [swapped(): return lax.ppermute(block, ('dom', 'rows'), route)]
    ppermute x0 -> x28, waiting for transfers between devices: none -> 30.6 us  [swapped(): return lax.ppermute(block, ('dom', 'rows'), route)]
    dot_general x26 -> x0, matrix products: 28.5 us -> none  [the longest x12 16.5 us: einsum_bf(): return jnp.einsum(spec, left, right, preferred_element_type=jnp.float32)]
    pallas_call x0 -> x4, Pallas kernels: none -> 14.3 us  [call(): pl.pallas_call(kernel, out_shape=outs, in_specs=in_specs, out_specs=[pl.B...]
    all_to_all x2 -> x0, starting transfers between devices: 13.2 us -> none  [the longest x1 7.25 us: shards(): lax.all_to_all(sent_features, 'dom', split_axis=0, concat_axis=0, tiled=T...]
    gather x3 -> x0, local copies, waits for them, and re-layouts: 11.9 us -> none  [the longest x2 9.13 us: shards(): expand_kv = slot_kv[expander]]
  transfers between devices with their start and end apart: 5 -> 30, of which waited for: 1 -> 15; matrix products, arithmetic and copies ran while one was open for 18% -> 1% of each run, Pallas kernels for 0% -> 3%
where the time goes in v2:
time: 97.3 us; the launch traced here: 96.9 us
  starting transfers between devices  41.1 us (42%)
  waiting for transfers between devices  30.6 us (31%)
  Pallas kernels  14.3 us (15%)
  local copies, waits for them, and re-layouts  8.71 us (9%)
  other arithmetic  1.23 us (1%)
    ppermute x28, starting transfers between devices, swapped(): return lax.ppermute(block, ('dom', 'rows'), route)  39.5 us
    ppermute x28, waiting for transfers between devices, swapped(): return lax.ppermute(block, ('dom', 'rows'), route)  30.6 us
    pallas_call x4, Pallas kernels, call(): pl.pallas_call(kernel, out_shape=outs, in_specs=in_specs, out_specs=[pl.B...  14.3 us
    unnamed x25, local copies, waits for them, and re-layouts  7.7 us
  transfers between devices with their start and end apart: 30, of which 15 were waited for; matrix products, arithmetic and copies ran while one was open for 1% of the time, Pallas kernels for 3%

profile of v2, /device:TPU:0, one launch (start us, length us, event | category | flops | bytes accessed | tf_op | source)
XLA Modules:
  0.0 96.9 jit_solution(1809572796583150266)
XLA Ops:
  0.6 0.9 slice.78
  2.1 0.9 copy-done
  3.0 0.7 copy-done.1
  3.7 0.9 pick_rows.1
  4.7 2.6 %collective-permute-start.1 = (bf16[32,384]{1,0:T(8,128)(2,1)S(1)}, bf16[32,384]{1,0:T(8,128)(2,1)S(1)}, u32[]{:S(2)}, u32[]{:S(2)}) collective-permute-start(bf16[32,384]{1,0:T(8,128)(2,1)S(1)} %get-tuple-element.30), channel_id=1, source_target_pairs={{0,4},{1,5},{2,6},{3,7},{4,0},{5,1},{6,2},{7,3},{8,12},{9,13},{10,... | collective-permute-start | bytes 73736 | tf_op jit(solution)/shard_map/ppermute | solution.py:86
  7.3 1.6 %collective-permute-start.2 = (bf16[32,384]{1,0:T(8,128)(2,1)S(1)}, bf16[32,384]{1,0:T(8,128)(2,1)S(1)}, u32[]{:S(2)}, u32[]{:S(2)}) collective-permute-start(bf16[32,384]{1,0:T(8,128)(2,1)S(1)} %get-tuple-element.31), channel_id=1, source_target_pairs={{0,8},{1,9},{2,10},{3,11},{4,12},{5,13},{6,14},{7,15},{8,0},{9,1},... | collective-permute-start | bytes 73736 | tf_op jit(solution)/shard_map/ppermute | solution.py:86
  8.8 3.0 %collective-permute-start.4 = (bf16[32,384]{1,0:T(8,128)(2,1)S(1)}, bf16[32,384]{1,0:T(8,128)(2,1)S(1)}, u32[]{:S(2)}, u32[]{:S(2)}) collective-permute-start(bf16[32,384]{1,0:T(8,128)(2,1)S(1)} %get-tuple-element.33), channel_id=1, source_target_pairs={{0,16},{1,17},{2,18},{3,19},{4,20},{5,21},{6,22},{7,23},{8,24},{9,... | collective-permute-start | bytes 73736 | tf_op jit(solution)/shard_map/ppermute | solution.py:86
  11.8 1.3 %collective-permute-start.5 = (bf16[32,384]{1,0:T(8,128)(2,1)S(1)}, bf16[32,384]{1,0:T(8,128)(2,1)S(1)}, u32[]{:S(2)}, u32[]{:S(2)}) collective-permute-start(bf16[32,384]{1,0:T(8,128)(2,1)S(1)} %get-tuple-element.34), channel_id=1, source_target_pairs={{0,20},{1,21},{2,22},{3,23},{4,16},{5,17},{6,18},{7,19},{8,28},{9,... | collective-permute-start | bytes 73736 | tf_op jit(solution)/shard_map/ppermute | solution.py:86
  13.1 3.6 %collective-permute-start.6 = (bf16[32,384]{1,0:T(8,128)(2,1)S(1)}, bf16[32,384]{1,0:T(8,128)(2,1)S(1)}, u32[]{:S(2)}, u32[]{:S(2)}) collective-permute-start(bf16[32,384]{1,0:T(8,128)(2,1)S(1)} %get-tuple-element.35), channel_id=1, source_target_pairs={{0,24},{1,25},{2,26},{3,27},{4,28},{5,29},{6,30},{7,31},{8,16},{9,... | collective-permute-start | bytes 73736 | tf_op jit(solution)/shard_map/ppermute | solution.py:86
  16.9 0.6 collective-permute-done.5.refs_5_
  17.5 1.4 %collective-permute-done.6.refs_6_ = bf16[32,384]{1,0:T(8,128)(2,1)S(1)} collective-permute-done((bf16[32,384]{1,0:T(8,128)(2,1)S(1)}, bf16[32,384]{1,0:T(8,128)(2,1)S(1)}, u32[]{:S(2)}, u32[]{:S(2)}) %collective-permute-start.6) | collective-permute-done | bytes 24608 | tf_op jit(solution)/shard_map/ppermute | solution.py:86
  18.9 4.3 %collective-permute-done.7.refs_7_ = bf16[32,384]{1,0:T(8,128)(2,1)S(1)} collective-permute-done((bf16[32,384]{1,0:T(8,128)(2,1)S(1)}, bf16[32,384]{1,0:T(8,128)(2,1)S(1)}, u32[]{:S(2)}, u32[]{:S(2)}) %collective-permute-start.7) | collective-permute-done | bytes 24608 | tf_op jit(solution)/shard_map/ppermute | solution.py:86
  23.3 1.1 %copy-done.3 = bf16[384,768]{1,0:T(8,128)(2,1)S(1)} copy-done((bf16[384,768]{1,0:T(8,128)(2,1)S(1)}, bf16[384,768]{1,0:T(8,128)(2,1)}, u32[]{:S(2)}) %copy-start.3) | copy-done | bytes 589848
  24.3 1.0 copy-done.4
  25.3 1.0 copy-done.5
  26.2 0.9 copy-done.6
  27.2 0.7 copy-done.7
  27.9 0.7 copy-done.8
  28.6 0.7 copy-done.9
  29.3 9.5 %attend.1 = (f32[256,384]{1,0:T(8,128)S(1)}, bf16[128,384]{1,0:T(8,128)(2,1)S(1)}, bf16[32,384]{1,0:T(8,128)(2,1)S(1)}, bf16[32,384]{1,0:T(8,128)(2,1)S(1)}, bf1...) custom-call(s32[2]{0:T(128)S(1)} %pad_add_fusion.place_ref, ...), custom_call_target="tpu_custom_call" | custom-call | flops 3095396352 | bytes 4385800 | tf_op jit(solution)/shard_map/attend/pallas_call | solution.py:354
  38.8 2.0 %collective-permute-done.16 = bf16[784,384]{1,0:T(8,128)(2,1)S(1)} collective-permute-done((bf16[784,384]{1,0:T(8,128)(2,1)S(1)}, bf16[784,384]{1,0:T(8,128)(2,1)S(1)}, u32[]{:S(2)}, u32[]{:S(2)}) %collective-permute-start.16) | collective-permute-done | bytes 602144 | tf_op jit(solution)/shard_map/ppermute | solution.py:86
  41.2 1.6 %collective-permute-start.17 = (bf16[208,384]{1,0:T(8,128)(2,1)S(1)}, bf16[208,384]{1,0:T(8,128)(2,1)S(1)}, u32[]{:S(2)}, u32[]{:S(2)}) collective-permute-start(bf16[208,384]{1,0:T(8,128)(2,1)S(1)} %get-tuple-element.68), channel_id=1, source_target_pairs={{0,2},{1,3},{2,0},{3,1},{4,6},{5,7},{6,4},{7,5},{8,10},{9,11},{10,... | collective-permute-start | bytes 479240 | tf_op jit(solution)/shard_map/ppermute | solution.py:86
  43.3 1.4 %collective-permute-start.19 = (bf16[208,384]{1,0:T(8,128)(2,1)S(1)}, bf16[208,384]{1,0:T(8,128)(2,1)S(1)}, u32[]{:S(2)}, u32[]{:S(2)}) collective-permute-start(bf16[208,384]{1,0:T(8,128)(2,1)S(1)} %get-tuple-element.70), channel_id=1, source_target_pairs={{0,6},{1,7},{2,4},{3,5},{4,2},{5,3},{6,0},{7,1},{8,14},{9,15},{10,... | collective-permute-start | bytes 479240 | tf_op jit(solution)/shard_map/ppermute | solution.py:86
  44.8 2.7 %collective-permute-done.17 = bf16[208,384]{1,0:T(8,128)(2,1)S(1)} collective-permute-done((bf16[208,384]{1,0:T(8,128)(2,1)S(1)}, bf16[208,384]{1,0:T(8,128)(2,1)S(1)}, u32[]{:S(2)}, u32[]{:S(2)}) %collective-permute-start.17) | collective-permute-done | bytes 159776 | tf_op jit(solution)/shard_map/ppermute | solution.py:86
  47.5 2.3 %collective-permute-done.18 = bf16[208,384]{1,0:T(8,128)(2,1)S(1)} collective-permute-done((bf16[208,384]{1,0:T(8,128)(2,1)S(1)}, bf16[208,384]{1,0:T(8,128)(2,1)S(1)}, u32[]{:S(2)}, u32[]{:S(2)}) %collective-permute-start.18) | collective-permute-done | bytes 159776 | tf_op jit(solution)/shard_map/ppermute | solution.py:86
  49.8 2.2 %collective-permute-done.19 = bf16[208,384]{1,0:T(8,128)(2,1)S(1)} collective-permute-done((bf16[208,384]{1,0:T(8,128)(2,1)S(1)}, bf16[208,384]{1,0:T(8,128)(2,1)S(1)}, u32[]{:S(2)}, u32[]{:S(2)}) %collective-permute-start.19) | collective-permute-done | bytes 159776 | tf_op jit(solution)/shard_map/ppermute | solution.py:86
  52.3 0.8 collective-permute-start.21
  53.1 3.6 %collective-permute-start.22 = (bf16[64,384]{1,0:T(8,128)(2,1)S(1)}, bf16[64,384]{1,0:T(8,128)(2,1)S(1)}, u32[]{:S(2)}, u32[]{:S(2)}) collective-permute-start(bf16[64,384]{1,0:T(8,128)(2,1)S(1)} %get-tuple-element.67), channel_id=1, source_target_pairs={{0,24},{1,25},{2,26},{3,27},{4,28},{5,29},{6,30},{7,31},{8,16},{9,... | collective-permute-start | bytes 147464 | tf_op jit(solution)/shard_map/ppermute | solution.py:86
  56.7 0.8 collective-permute-done.21
  57.5 1.7 %collective-permute-done.22 = bf16[64,384]{1,0:T(8,128)(2,1)S(1)} collective-permute-done((bf16[64,384]{1,0:T(8,128)(2,1)S(1)}, bf16[64,384]{1,0:T(8,128)(2,1)S(1)}, u32[]{:S(2)}, u32[]{:S(2)}) %collective-permute-start.22) | collective-permute-done | bytes 49184 | tf_op jit(solution)/shard_map/ppermute | solution.py:86
  59.3 3.3 %collective-permute-start.25 = (bf16[48,384]{1,0:T(8,128)(2,1)S(1)}, bf16[48,384]{1,0:T(8,128)(2,1)S(1)}, u32[]{:S(2)}, u32[]{:S(2)}) collective-permute-start(bf16[48,384]{1,0:T(8,128)(2,1)S(1)} %get-tuple-element.54), channel_id=1, source_target_pairs={{0,24},{1,25},{2,26},{3,27},{4,28},{5,29},{6,30},{7,31},{8,16},{9,... | collective-permute-start | bytes 110600 | tf_op jit(solution)/shard_map/ppermute | solution.py:86
  62.7 1.1 %collective-permute-start.23 = (bf16[48,384]{1,0:T(8,128)(2,1)S(1)}, bf16[48,384]{1,0:T(8,128)(2,1)S(1)}, u32[]{:S(2)}, u32[]{:S(2)}) collective-permute-start(bf16[48,384]{1,0:T(8,128)(2,1)S(1)} %get-tuple-element.54), channel_id=1, source_target_pairs={{0,8},{1,9},{2,10},{3,11},{4,12},{5,13},{6,14},{7,15},{8,0},{9,1},... | collective-permute-start | bytes 110600 | tf_op jit(solution)/shard_map/ppermute | solution.py:86
  63.8 1.4 %collective-permute-done.25 = bf16[48,384]{1,0:T(8,128)(2,1)S(1)} collective-permute-done((bf16[48,384]{1,0:T(8,128)(2,1)S(1)}, bf16[48,384]{1,0:T(8,128)(2,1)S(1)}, u32[]{:S(2)}, u32[]{:S(2)}) %collective-permute-start.25) | collective-permute-done | bytes 36896 | tf_op jit(solution)/shard_map/ppermute | solution.py:86
  65.2 2.4 %collective-permute-done.24 = bf16[48,384]{1,0:T(8,128)(2,1)S(1)} collective-permute-done((bf16[48,384]{1,0:T(8,128)(2,1)S(1)}, bf16[48,384]{1,0:T(8,128)(2,1)S(1)}, u32[]{:S(2)}, u32[]{:S(2)}) %collective-permute-start.24) | collective-permute-done | bytes 36896 | tf_op jit(solution)/shard_map/ppermute | solution.py:86
  67.6 1.5 %collective-permute-start.28 = (bf16[192,384]{1,0:T(8,128)(2,1)S(1)}, bf16[192,384]{1,0:T(8,128)(2,1)S(1)}, u32[]{:S(2)}, u32[]{:S(2)}) collective-permute-start(bf16[192,384]{1,0:T(8,128)(2,1)S(1)} %pad_maximum_fusion.3), channel_id=1, source_target_pairs={{0,6},{1,7},{2,4},{3,5},{4,2},{5,3},{6,0},{7,1},{8,14},{9,15},{10,... | collective-permute-start | bytes 442376 | tf_op jit(solution)/shard_map/ppermute | solution.py:86
  69.1 1.5 %collective-permute-start.27 = (bf16[192,384]{1,0:T(8,128)(2,1)S(1)}, bf16[192,384]{1,0:T(8,128)(2,1)S(1)}, u32[]{:S(2)}, u32[]{:S(2)}) collective-permute-start(bf16[192,384]{1,0:T(8,128)(2,1)S(1)} %pad_maximum_fusion.3), channel_id=1, source_target_pairs={{0,4},{1,5},{2,6},{3,7},{4,0},{5,1},{6,2},{7,3},{8,12},{9,13},{10,... | collective-permute-start | bytes 442376 | tf_op jit(solution)/shard_map/ppermute | solution.py:86
  71.2 4.6 %collective-permute-done.26 = bf16[192,384]{1,0:T(8,128)(2,1)S(1)} collective-permute-done((bf16[192,384]{1,0:T(8,128)(2,1)S(1)}, bf16[192,384]{1,0:T(8,128)(2,1)S(1)}, u32[]{:S(2)}, u32[]{:S(2)}) %collective-permute-start.26) | collective-permute-done | bytes 147488 | tf_op jit(solution)/shard_map/ppermute | solution.py:86
  75.9 1.1 %collective-permute-start.8 = (bf16[128,384]{1,0:T(8,128)(2,1)S(1)}, bf16[128,384]{1,0:T(8,128)(2,1)S(1)}, u32[]{:S(2)}, u32[]{:S(2)}) collective-permute-start(bf16[128,384]{1,0:T(8,128)(2,1)S(1)} %get-tuple-element.38), channel_id=1, source_target_pairs={{1,0},{2,1},{3,2},{0,3},{5,4},{6,5},{7,6},{4,7},{9,8},{10,9},{11,1... | collective-permute-start | bytes 294920 | tf_op jit(solution)/shard_map/ppermute | solution.py:92
  77.8 2.7 %collective-permute-start.11 = (bf16[32,384]{1,0:T(8,128)(2,1)S(1)}, bf16[32,384]{1,0:T(8,128)(2,1)S(1)}, u32[]{:S(2)}, u32[]{:S(2)}) collective-permute-start(bf16[32,384]{1,0:T(8,128)(2,1)S(1)} %get-tuple-element.42), channel_id=1, source_target_pairs={{0,12},{1,13},{2,14},{3,15},{4,8},{5,9},{6,10},{7,11},{8,4},{9,5},... | collective-permute-start | bytes 73736 | tf_op jit(solution)/shard_map/ppermute | solution.py:86
  81.1 2.0 %collective-permute-start.12 = (bf16[32,384]{1,0:T(8,128)(2,1)S(1)}, bf16[32,384]{1,0:T(8,128)(2,1)S(1)}, u32[]{:S(2)}, u32[]{:S(2)}) collective-permute-start(bf16[32,384]{1,0:T(8,128)(2,1)S(1)} %get-tuple-element.43), channel_id=1, source_target_pairs={{0,16},{1,17},{2,18},{3,19},{4,20},{5,21},{6,22},{7,23},{8,24},{9,... | collective-permute-start | bytes 73736 | tf_op jit(solution)/shard_map/ppermute | solution.py:86
  83.1 1.3 %collective-permute-start.13 = (bf16[32,384]{1,0:T(8,128)(2,1)S(1)}, bf16[32,384]{1,0:T(8,128)(2,1)S(1)}, u32[]{:S(2)}, u32[]{:S(2)}) collective-permute-start(bf16[32,384]{1,0:T(8,128)(2,1)S(1)} %get-tuple-element.44), channel_id=1, source_target_pairs={{0,20},{1,21},{2,22},{3,23},{4,16},{5,17},{6,18},{7,19},{8,28},{9,... | collective-permute-start | bytes 73736 | tf_op jit(solution)/shard_map/ppermute | solution.py:86
  84.4 1.4 %collective-permute-start.14 = (bf16[32,384]{1,0:T(8,128)(2,1)S(1)}, bf16[32,384]{1,0:T(8,128)(2,1)S(1)}, u32[]{:S(2)}, u32[]{:S(2)}) collective-permute-start(bf16[32,384]{1,0:T(8,128)(2,1)S(1)} %get-tuple-element.45), channel_id=1, source_target_pairs={{0,24},{1,25},{2,26},{3,27},{4,28},{5,29},{6,30},{7,31},{8,16},{9,... | collective-permute-start | bytes 73736 | tf_op jit(solution)/shard_map/ppermute | solution.py:86
  85.8 2.9 %collective-permute-start.15 = (bf16[32,384]{1,0:T(8,128)(2,1)S(1)}, bf16[32,384]{1,0:T(8,128)(2,1)S(1)}, u32[]{:S(2)}, u32[]{:S(2)}) collective-permute-start(bf16[32,384]{1,0:T(8,128)(2,1)S(1)} %get-tuple-element.46), channel_id=1, source_target_pairs={{0,28},{1,29},{2,30},{3,31},{4,24},{5,25},{6,26},{7,27},{8,20},{9,... | collective-permute-start | bytes 73736 | tf_op jit(solution)/shard_map/ppermute | solution.py:86
  88.7 1.3 %collective-permute-done.14.refs_6_ = bf16[32,384]{1,0:T(8,128)(2,1)S(1)} collective-permute-done((bf16[32,384]{1,0:T(8,128)(2,1)S(1)}, bf16[32,384]{1,0:T(8,128)(2,1)S(1)}, u32[]{:S(2)}, u32[]{:S(2)}) %collective-permute-start.14) | collective-permute-done | bytes 24608 | tf_op jit(solution)/shard_map/ppermute | solution.py:86
  90.0 2.3 %collective-permute-done.15.refs_7_ = bf16[32,384]{1,0:T(8,128)(2,1)S(1)} collective-permute-done((bf16[32,384]{1,0:T(8,128)(2,1)S(1)}, bf16[32,384]{1,0:T(8,128)(2,1)S(1)}, u32[]{:S(2)}, u32[]{:S(2)}) %collective-permute-start.15) | collective-permute-done | bytes 24608 | tf_op jit(solution)/shard_map/ppermute | solution.py:86
  92.3 1.8 %return_rows.1 = f32[256,384]{1,0:T(8,128)} custom-call(s32[2]{0:T(128)S(1)} %pad_add_fusion.place_ref, f32[256,384]{1,0:T(8,128)S(1)} %get-tuple-element.37.gf_ref, bf16[128,384]{1,0:T(8,128)(2,1)S(1)} %collective-permute-done.8.halo_ref, s32[8,32]{1,0:T(8,128)S(1)} %copy-done.2, bf16[32,384]{1,0:T(8,128)(2,1)S(1)} %get-tuple-element.39.refs_0_, ...), custom_call_target="tpu_custom_call" | custom-call | bytes 1082376 | tf_op jit(solution)/shard_map/return_rows/pallas_call | solution.py:354
  94.2 0.6 fusion.6
  94.8 2.1 %place_sums.1 = (f32[384,384]{1,0:T(8,128)}, f32[384,768]{1,0:T(8,128)}, f32[384,384]{1,0:T(8,128)}) custom-call(s32[2]{0:T(128)S(1)} %pad_add_fusion.place_ref, bf16[768,384]{1,0:T(8,128)(2,1)S(1)} %constant_dynamic-update-slice_fusion.near_ref, bf16[768,384]{1,0:T(8,128)(2,1)S(1)} %collective-permute-done.29.far_ref), custom_call_target="tpu_custom_call" | custom-call | bytes 3538952 | tf_op jit(solution)/shard_map/place_sums/pallas_call | solution.py:354
  (65 shorter events, 4.1 us)
Async XLA Ops:
  1.5 21.7 %collective-permute-start = (bf16[128,384]{1,0:T(8,128)(2,1)S(1)}, bf16[128,384]{1,0:T(8,128)(2,1)S(1)}, u32[]{:S(2)}, u32[]{:S(2)}) collective-permute-start(bf16[128,384]{1,0:T(8,128)(2,1)S(1)} %slice.78), channel_id=1, source_target_pairs={{3,0},{0,1},{1,2},{2,3},{7,4},{4,5},{5,6},{6,7},{11,8},{8,9},{9,10... | collective-permute-start | bytes 294920 | tf_op jit(solution)/shard_map/ppermute | solution.py:92
  2.1 0.9 copy-start
  3.0 0.7 copy-start.1
  4.7 7.2 %collective-permute-start.1 = (bf16[32,384]{1,0:T(8,128)(2,1)S(1)}, bf16[32,384]{1,0:T(8,128)(2,1)S(1)}, u32[]{:S(2)}, u32[]{:S(2)}) collective-permute-start(bf16[32,384]{1,0:T(8,128)(2,1)S(1)} %get-tuple-element.30), channel_id=1, source_target_pairs={{0,4},{1,5},{2,6},{3,7},{4,0},{5,1},{6,2},{7,3},{8,12},{9,13},{10,... | collective-permute-start | bytes 73736 | tf_op jit(solution)/shard_map/ppermute | solution.py:86
  7.3 5.9 %collective-permute-start.2 = (bf16[32,384]{1,0:T(8,128)(2,1)S(1)}, bf16[32,384]{1,0:T(8,128)(2,1)S(1)}, u32[]{:S(2)}, u32[]{:S(2)}) collective-permute-start(bf16[32,384]{1,0:T(8,128)(2,1)S(1)} %get-tuple-element.31), channel_id=1, source_target_pairs={{0,8},{1,9},{2,10},{3,11},{4,12},{5,13},{6,14},{7,15},{8,0},{9,1},... | collective-permute-start | bytes 73736 | tf_op jit(solution)/shard_map/ppermute | solution.py:86
  8.8 7.9 %collective-permute-start.3 = (bf16[32,384]{1,0:T(8,128)(2,1)S(1)}, bf16[32,384]{1,0:T(8,128)(2,1)S(1)}, u32[]{:S(2)}, u32[]{:S(2)}) collective-permute-start(bf16[32,384]{1,0:T(8,128)(2,1)S(1)} %get-tuple-element.32), channel_id=1, source_target_pairs={{0,12},{1,13},{2,14},{3,15},{4,8},{5,9},{6,10},{7,11},{8,4},{9,5},... | collective-permute-start | bytes 73736 | tf_op jit(solution)/shard_map/ppermute | solution.py:86
  8.8 8.1 %collective-permute-start.4 = (bf16[32,384]{1,0:T(8,128)(2,1)S(1)}, bf16[32,384]{1,0:T(8,128)(2,1)S(1)}, u32[]{:S(2)}, u32[]{:S(2)}) collective-permute-start(bf16[32,384]{1,0:T(8,128)(2,1)S(1)} %get-tuple-element.33), channel_id=1, source_target_pairs={{0,16},{1,17},{2,18},{3,19},{4,20},{5,21},{6,22},{7,23},{8,24},{9,... | collective-permute-start | bytes 73736 | tf_op jit(solution)/shard_map/ppermute | solution.py:86
  11.8 5.7 %collective-permute-start.5 = (bf16[32,384]{1,0:T(8,128)(2,1)S(1)}, bf16[32,384]{1,0:T(8,128)(2,1)S(1)}, u32[]{:S(2)}, u32[]{:S(2)}) collective-permute-start(bf16[32,384]{1,0:T(8,128)(2,1)S(1)} %get-tuple-element.34), channel_id=1, source_target_pairs={{0,20},{1,21},{2,22},{3,23},{4,16},{5,17},{6,18},{7,19},{8,28},{9,... | collective-permute-start | bytes 73736 | tf_op jit(solution)/shard_map/ppermute | solution.py:86
  13.1 5.8 %collective-permute-start.6 = (bf16[32,384]{1,0:T(8,128)(2,1)S(1)}, bf16[32,384]{1,0:T(8,128)(2,1)S(1)}, u32[]{:S(2)}, u32[]{:S(2)}) collective-permute-start(bf16[32,384]{1,0:T(8,128)(2,1)S(1)} %get-tuple-element.35), channel_id=1, source_target_pairs={{0,24},{1,25},{2,26},{3,27},{4,28},{5,29},{6,30},{7,31},{8,16},{9,... | collective-permute-start | bytes 73736 | tf_op jit(solution)/shard_map/ppermute | solution.py:86
  16.7 6.5 %collective-permute-start.7 = (bf16[32,384]{1,0:T(8,128)(2,1)S(1)}, bf16[32,384]{1,0:T(8,128)(2,1)S(1)}, u32[]{:S(2)}, u32[]{:S(2)}) collective-permute-start(bf16[32,384]{1,0:T(8,128)(2,1)S(1)} %get-tuple-element.36), channel_id=1, source_target_pairs={{0,28},{1,29},{2,30},{3,31},{4,24},{5,25},{6,26},{7,27},{8,20},{9,... | collective-permute-start | bytes 73736 | tf_op jit(solution)/shard_map/ppermute | solution.py:86
  23.3 1.1 %copy-start.3 = (bf16[384,768]{1,0:T(8,128)(2,1)S(1)}, bf16[384,768]{1,0:T(8,128)(2,1)}, u32[]{:S(2)}) copy-start(bf16[384,768]{1,0:T(8,128)(2,1)} %refs_10_.1) | copy-start | bytes 1769476
  24.3 1.0 copy-start.4
  25.3 1.0 copy-start.5
  26.2 0.9 copy-start.6
  27.2 0.7 copy-start.7
  27.9 0.7 copy-start.8
  28.6 0.7 copy-start.9
  38.7 2.1 %collective-permute-start.16 = (bf16[784,384]{1,0:T(8,128)(2,1)S(1)}, bf16[784,384]{1,0:T(8,128)(2,1)S(1)}, u32[]{:S(2)}, u32[]{:S(2)}) collective-permute-start(bf16[784,384]{1,0:T(8,128)(2,1)S(1)} %get-tuple-element.48), channel_id=1, source_target_pairs={{0,1},{1,0},{2,3},{3,2},{4,5},{5,4},{6,7},{7,6},{8,9},{9,8},{10,11... | collective-permute-start | bytes 1806344 | tf_op jit(solution)/shard_map/ppermute | solution.py:86
  41.2 6.2 %collective-permute-start.17 = (bf16[208,384]{1,0:T(8,128)(2,1)S(1)}, bf16[208,384]{1,0:T(8,128)(2,1)S(1)}, u32[]{:S(2)}, u32[]{:S(2)}) collective-permute-start(bf16[208,384]{1,0:T(8,128)(2,1)S(1)} %get-tuple-element.68), channel_id=1, source_target_pairs={{0,2},{1,3},{2,0},{3,1},{4,6},{5,7},{6,4},{7,5},{8,10},{9,11},{10,... | collective-permute-start | bytes 479240 | tf_op jit(solution)/shard_map/ppermute | solution.py:86
  42.8 7.0 %collective-permute-start.18 = (bf16[208,384]{1,0:T(8,128)(2,1)S(1)}, bf16[208,384]{1,0:T(8,128)(2,1)S(1)}, u32[]{:S(2)}, u32[]{:S(2)}) collective-permute-start(bf16[208,384]{1,0:T(8,128)(2,1)S(1)} %get-tuple-element.69), channel_id=1, source_target_pairs={{0,4},{1,5},{2,6},{3,7},{4,0},{5,1},{6,2},{7,3},{8,12},{9,13},{10,... | collective-permute-start | bytes 479240 | tf_op jit(solution)/shard_map/ppermute | solution.py:86
  43.3 8.7 %collective-permute-start.19 = (bf16[208,384]{1,0:T(8,128)(2,1)S(1)}, bf16[208,384]{1,0:T(8,128)(2,1)S(1)}, u32[]{:S(2)}, u32[]{:S(2)}) collective-permute-start(bf16[208,384]{1,0:T(8,128)(2,1)S(1)} %get-tuple-element.70), channel_id=1, source_target_pairs={{0,6},{1,7},{2,4},{3,5},{4,2},{5,3},{6,0},{7,1},{8,14},{9,15},{10,... | collective-permute-start | bytes 479240 | tf_op jit(solution)/shard_map/ppermute | solution.py:86
  52.2 40.1 %copy-start.2 = (s32[8,32]{1,0:T(8,128)S(1)}, s32[8,32]{1,0:T(8,128)}, u32[]{:S(2)}) copy-start(s32[8,32]{1,0:T(8,128)} %send_ref.3) | copy-start | bytes 3076
  52.2 4.5 %collective-permute-start.20 = (bf16[64,384]{1,0:T(8,128)(2,1)S(1)}, bf16[64,384]{1,0:T(8,128)(2,1)S(1)}, u32[]{:S(2)}, u32[]{:S(2)}) collective-permute-start(bf16[64,384]{1,0:T(8,128)(2,1)S(1)} %get-tuple-element.65), channel_id=1, source_target_pairs={{0,8},{1,9},{2,10},{3,11},{4,12},{5,13},{6,14},{7,15},{8,0},{9,1},... | collective-permute-start | bytes 147464 | tf_op jit(solution)/shard_map/ppermute | solution.py:86
  52.3 5.2 %collective-permute-start.21 = (bf16[64,384]{1,0:T(8,128)(2,1)S(1)}, bf16[64,384]{1,0:T(8,128)(2,1)S(1)}, u32[]{:S(2)}, u32[]{:S(2)}) collective-permute-start(bf16[64,384]{1,0:T(8,128)(2,1)S(1)} %get-tuple-element.66), channel_id=1, source_target_pairs={{0,16},{1,17},{2,18},{3,19},{4,20},{5,21},{6,22},{7,23},{8,24},{9,... | collective-permute-start | bytes 147464 | tf_op jit(solution)/shard_map/ppermute | solution.py:86
  53.1 6.2 %collective-permute-start.22 = (bf16[64,384]{1,0:T(8,128)(2,1)S(1)}, bf16[64,384]{1,0:T(8,128)(2,1)S(1)}, u32[]{:S(2)}, u32[]{:S(2)}) collective-permute-start(bf16[64,384]{1,0:T(8,128)(2,1)S(1)} %get-tuple-element.67), channel_id=1, source_target_pairs={{0,24},{1,25},{2,26},{3,27},{4,28},{5,29},{6,30},{7,31},{8,16},{9,... | collective-permute-start | bytes 147464 | tf_op jit(solution)/shard_map/ppermute | solution.py:86
  59.3 5.8 %collective-permute-start.25 = (bf16[48,384]{1,0:T(8,128)(2,1)S(1)}, bf16[48,384]{1,0:T(8,128)(2,1)S(1)}, u32[]{:S(2)}, u32[]{:S(2)}) collective-permute-start(bf16[48,384]{1,0:T(8,128)(2,1)S(1)} %get-tuple-element.54), channel_id=1, source_target_pairs={{0,24},{1,25},{2,26},{3,27},{4,28},{5,29},{6,30},{7,31},{8,16},{9,... | collective-permute-start | bytes 110600 | tf_op jit(solution)/shard_map/ppermute | solution.py:86
  62.7 4.9 %collective-permute-start.24 = (bf16[48,384]{1,0:T(8,128)(2,1)S(1)}, bf16[48,384]{1,0:T(8,128)(2,1)S(1)}, u32[]{:S(2)}, u32[]{:S(2)}) collective-permute-start(bf16[48,384]{1,0:T(8,128)(2,1)S(1)} %get-tuple-element.54), channel_id=1, source_target_pairs={{0,16},{1,17},{2,18},{3,19},{4,20},{5,21},{6,22},{7,23},{8,24},{9,... | collective-permute-start | bytes 110600 | tf_op jit(solution)/shard_map/ppermute | solution.py:86
  62.7 4.9 %collective-permute-start.23 = (bf16[48,384]{1,0:T(8,128)(2,1)S(1)}, bf16[48,384]{1,0:T(8,128)(2,1)S(1)}, u32[]{:S(2)}, u32[]{:S(2)}) collective-permute-start(bf16[48,384]{1,0:T(8,128)(2,1)S(1)} %get-tuple-element.54), channel_id=1, source_target_pairs={{0,8},{1,9},{2,10},{3,11},{4,12},{5,13},{6,14},{7,15},{8,0},{9,1},... | collective-permute-start | bytes 110600 | tf_op jit(solution)/shard_map/ppermute | solution.py:86
  67.6 8.3 %collective-permute-start.28 = (bf16[192,384]{1,0:T(8,128)(2,1)S(1)}, bf16[192,384]{1,0:T(8,128)(2,1)S(1)}, u32[]{:S(2)}, u32[]{:S(2)}) collective-permute-start(bf16[192,384]{1,0:T(8,128)(2,1)S(1)} %pad_maximum_fusion.3), channel_id=1, source_target_pairs={{0,6},{1,7},{2,4},{3,5},{4,2},{5,3},{6,0},{7,1},{8,14},{9,15},{10,... | collective-permute-start | bytes 442376 | tf_op jit(solution)/shard_map/ppermute | solution.py:86
  69.1 6.7 %collective-permute-start.27 = (bf16[192,384]{1,0:T(8,128)(2,1)S(1)}, bf16[192,384]{1,0:T(8,128)(2,1)S(1)}, u32[]{:S(2)}, u32[]{:S(2)}) collective-permute-start(bf16[192,384]{1,0:T(8,128)(2,1)S(1)} %pad_maximum_fusion.3), channel_id=1, source_target_pairs={{0,4},{1,5},{2,6},{3,7},{4,0},{5,1},{6,2},{7,3},{8,12},{9,13},{10,... | collective-permute-start | bytes 442376 | tf_op jit(solution)/shard_map/ppermute | solution.py:86
  70.6 5.1 %collective-permute-start.26 = (bf16[192,384]{1,0:T(8,128)(2,1)S(1)}, bf16[192,384]{1,0:T(8,128)(2,1)S(1)}, u32[]{:S(2)}, u32[]{:S(2)}) collective-permute-start(bf16[192,384]{1,0:T(8,128)(2,1)S(1)} %pad_maximum_fusion.3), channel_id=1, source_target_pairs={{0,2},{1,3},{2,0},{3,1},{4,6},{5,7},{6,4},{7,5},{8,10},{9,11},{10,... | collective-permute-start | bytes 442376 | tf_op jit(solution)/shard_map/ppermute | solution.py:86
  75.9 18.9 %collective-permute-start.29 = (bf16[768,384]{1,0:T(8,128)(2,1)S(1)}, bf16[768,384]{1,0:T(8,128)(2,1)S(1)}, u32[]{:S(2)}, u32[]{:S(2)}) collective-permute-start(bf16[768,384]{1,0:T(8,128)(2,1)S(1)} %constant_dynamic-update-slice_fusion.near_ref), channel_id=1, source_target_pairs={{0,1},{1,0},{2,3},{3,2},{4,5},{5,4},{6,7},{7,6},{8,9},{9,8},{10,11... | collective-permute-start | bytes 1769480 | tf_op jit(solution)/shard_map/ppermute | solution.py:86
  75.9 16.4 %collective-permute-start.8 = (bf16[128,384]{1,0:T(8,128)(2,1)S(1)}, bf16[128,384]{1,0:T(8,128)(2,1)S(1)}, u32[]{:S(2)}, u32[]{:S(2)}) collective-permute-start(bf16[128,384]{1,0:T(8,128)(2,1)S(1)} %get-tuple-element.38), channel_id=1, source_target_pairs={{1,0},{2,1},{3,2},{0,3},{5,4},{6,5},{7,6},{4,7},{9,8},{10,9},{11,1... | collective-permute-start | bytes 294920 | tf_op jit(solution)/shard_map/ppermute | solution.py:92
  77.1 4.0 %collective-permute-start.9 = (bf16[32,384]{1,0:T(8,128)(2,1)S(1)}, bf16[32,384]{1,0:T(8,128)(2,1)S(1)}, u32[]{:S(2)}, u32[]{:S(2)}) collective-permute-start(bf16[32,384]{1,0:T(8,128)(2,1)S(1)} %get-tuple-element.40), channel_id=1, source_target_pairs={{0,4},{1,5},{2,6},{3,7},{4,0},{5,1},{6,2},{7,3},{8,12},{9,13},{10,... | collective-permute-start | bytes 73736 | tf_op jit(solution)/shard_map/ppermute | solution.py:86
  77.6 5.5 %collective-permute-start.10 = (bf16[32,384]{1,0:T(8,128)(2,1)S(1)}, bf16[32,384]{1,0:T(8,128)(2,1)S(1)}, u32[]{:S(2)}, u32[]{:S(2)}) collective-permute-start(bf16[32,384]{1,0:T(8,128)(2,1)S(1)} %get-tuple-element.41), channel_id=1, source_target_pairs={{0,8},{1,9},{2,10},{3,11},{4,12},{5,13},{6,14},{7,15},{8,0},{9,1},... | collective-permute-start | bytes 73736 | tf_op jit(solution)/shard_map/ppermute | solution.py:86
  77.8 6.6 %collective-permute-start.11 = (bf16[32,384]{1,0:T(8,128)(2,1)S(1)}, bf16[32,384]{1,0:T(8,128)(2,1)S(1)}, u32[]{:S(2)}, u32[]{:S(2)}) collective-permute-start(bf16[32,384]{1,0:T(8,128)(2,1)S(1)} %get-tuple-element.42), channel_id=1, source_target_pairs={{0,12},{1,13},{2,14},{3,15},{4,8},{5,9},{6,10},{7,11},{8,4},{9,5},... | collective-permute-start | bytes 73736 | tf_op jit(solution)/shard_map/ppermute | solution.py:86
  81.1 4.7 %collective-permute-start.12 = (bf16[32,384]{1,0:T(8,128)(2,1)S(1)}, bf16[32,384]{1,0:T(8,128)(2,1)S(1)}, u32[]{:S(2)}, u32[]{:S(2)}) collective-permute-start(bf16[32,384]{1,0:T(8,128)(2,1)S(1)} %get-tuple-element.43), channel_id=1, source_target_pairs={{0,16},{1,17},{2,18},{3,19},{4,20},{5,21},{6,22},{7,23},{8,24},{9,... | collective-permute-start | bytes 73736 | tf_op jit(solution)/shard_map/ppermute | solution.py:86
  83.1 5.6 %collective-permute-start.13 = (bf16[32,384]{1,0:T(8,128)(2,1)S(1)}, bf16[32,384]{1,0:T(8,128)(2,1)S(1)}, u32[]{:S(2)}, u32[]{:S(2)}) collective-permute-start(bf16[32,384]{1,0:T(8,128)(2,1)S(1)} %get-tuple-element.44), channel_id=1, source_target_pairs={{0,20},{1,21},{2,22},{3,23},{4,16},{5,17},{6,18},{7,19},{8,28},{9,... | collective-permute-start | bytes 73736 | tf_op jit(solution)/shard_map/ppermute | solution.py:86
  84.4 5.6 %collective-permute-start.14 = (bf16[32,384]{1,0:T(8,128)(2,1)S(1)}, bf16[32,384]{1,0:T(8,128)(2,1)S(1)}, u32[]{:S(2)}, u32[]{:S(2)}) collective-permute-start(bf16[32,384]{1,0:T(8,128)(2,1)S(1)} %get-tuple-element.45), channel_id=1, source_target_pairs={{0,24},{1,25},{2,26},{3,27},{4,28},{5,29},{6,30},{7,31},{8,16},{9,... | collective-permute-start | bytes 73736 | tf_op jit(solution)/shard_map/ppermute | solution.py:86
  85.8 6.5 %collective-permute-start.15 = (bf16[32,384]{1,0:T(8,128)(2,1)S(1)}, bf16[32,384]{1,0:T(8,128)(2,1)S(1)}, u32[]{:S(2)}, u32[]{:S(2)}) collective-permute-start(bf16[32,384]{1,0:T(8,128)(2,1)S(1)} %get-tuple-element.46), channel_id=1, source_target_pairs={{0,28},{1,29},{2,30},{3,31},{4,24},{5,25},{6,26},{7,27},{8,20},{9,... | collective-permute-start | bytes 73736 | tf_op jit(solution)/shard_map/ppermute | solution.py:86

commit v3 on v2

v3 whole, which is shorter than its diff:
```python
import functools
import math

import jax
import jax.numpy as jnp
from jax import lax
from jax.experimental import pallas as pl
from jax.experimental.pallas import tpu as pltpu
from jax.sharding import PartitionSpec as P

HEADS = 8
TILE = 128
ROW_PACK = 16
NEGATIVE_FILL = -1e30
VMEM_BYTES = 24 * 1024 * 1024
LANES = 128
CORE = "core"
ROWS = ("row_chip", CORE)
DOM = ("dom",)
CHIPS = ("dom", "row_chip")


def f32_dot(left, right):
    return jnp.dot(left, right, preferred_element_type=jnp.float32)


def rows_contracted(left, right):
    return lax.dot_general(
        left, right, (((0,), (0,)), ((), ())), preferred_element_type=jnp.float32
    )


def times_transposed(left, right):
    return lax.dot_general(
        left, right, (((1,), (1,)), ((), ())), preferred_element_type=jnp.float32
    )


def rounded(value):
    return value.astype(jnp.bfloat16)


def swapped(block, axis):
    return lax.ppermute(block, axis, [(i, i ^ 1) for i in range(lax.axis_size(axis))])


def shifted(block, axes, distance):
    count = math.prod(lax.axis_size(axis) for axis in axes)
    return lax.ppermute(block, axes, [((i - distance) % count, i) for i in range(count)])


def exchanged(blocks, axes):
    return lax.all_to_all(blocks, axes, split_axis=0, concat_axis=0, tiled=True)


def listed_rows(send_ref, row_count):
    dom_size, per_peer = send_ref.shape
    slots = dom_size * per_peer
    slot = lax.broadcasted_iota(jnp.int32, (slots, per_peer), 0)
    place = lax.broadcasted_iota(jnp.int32, (slots, per_peer), 1)
    listed = jnp.zeros((slots, per_peer), jnp.int32)
    for at in range(dom_size):
        here = slot == place + at * per_peer
        listed += jnp.where(here, send_ref[at : at + 1, :], 0)
    column = jnp.sum(listed, axis=1, keepdims=True)
    rows = lax.broadcasted_iota(jnp.int32, (slots, row_count), 1)
    return jnp.where(column == rows, 1.0, 0.0).astype(jnp.bfloat16)


def fetch(pairs, sems):
    copies = [
        pltpu.make_async_copy(source, target, sems.at[at])
        for at, (source, target) in enumerate(pairs)
    ]
    for copy in copies:
        copy.start()
    return copies


def pick_kernel(feat_hbm, send_hbm, out_ref, halo_ref, feat_ref, send_ref, sems):
    copies = fetch([(send_hbm, send_ref), (feat_hbm, feat_ref)], sems)
    copies[0].wait()
    chosen = listed_rows(send_ref, feat_ref.shape[0])
    copies[1].wait()
    halo_ref[...] = feat_ref[feat_ref.shape[0] - halo_ref.shape[0] :]
    out_ref[...] = rounded(f32_dot(chosen, feat_ref[...]))


def prepare_kernel(
    feat_hbm,
    og_hbm,
    wq_hbm,
    wkv_hbm,
    wo_hbm,
    virt_hbm,
    nbr_hbm,
    exp_hbm,
    og_ref,
    wq_ref,
    wkv_ref,
    featt_ref,
    qt_ref,
    odt_ref,
    kv_ref,
    kvt_ref,
    local_bias_ref,
    far_bias_ref,
    feat_ref,
    wo_ref,
    virt_ref,
    nbr_ref,
    exp_ref,
    sems,
):
    nbr_copy, exp_copy, feat_copy, virt_copy, wq_copy, wkv_copy, og_copy, wo_copy = fetch(
        [
            (nbr_hbm, nbr_ref),
            (exp_hbm, exp_ref),
            (feat_hbm, feat_ref),
            (virt_hbm, virt_ref),
            (wq_hbm, wq_ref),
            (wkv_hbm, wkv_ref),
            (og_hbm, og_ref),
            (wo_hbm, wo_ref),
        ],
        sems,
    )
    row_count, width = feat_ref.shape
    window = local_bias_ref.shape[0]
    far = far_bias_ref.shape[0]
    virt_rows = virt_ref.shape[0]
    padded = kv_ref.shape[0] - row_count
    slots = far - padded
    scale = 1.0 / math.sqrt(width // HEADS)

    def multiplicity(key_rows, named):
        position = lax.broadcasted_iota(jnp.int32, (key_rows, row_count), 0)
        count = jnp.zeros((key_rows, row_count), jnp.float32)
        for at in range(named.shape[0]):
            count += jnp.where(named[at : at + 1, :] == position, 1.0, 0.0)
        return count

    nbr_copy.wait()
    local_bias_ref[...] = jnp.where(multiplicity(window, nbr_ref) > 0.0, 0.0, NEGATIVE_FILL)
    exp_copy.wait()
    named_times = multiplicity(slots, exp_ref)
    slot_bias = jnp.full((slots, row_count), NEGATIVE_FILL, jnp.float32)
    for times in range(1, exp_ref.shape[0] + 1):
        slot_bias = jnp.where(named_times == float(times), math.log(times) / scale, slot_bias)
    far_bias_ref[:slots] = slot_bias
    virt_row = lax.broadcasted_iota(jnp.int32, (padded, row_count), 0)
    far_bias_ref[slots:] = jnp.where(virt_row < virt_rows, 0.0, NEGATIVE_FILL)

    feat_copy.wait()
    featt_ref[:, :row_count] = feat_ref[...].T
    virt_copy.wait()
    virt = jnp.concatenate(
        [virt_ref[...], jnp.zeros((padded - virt_rows, width), jnp.bfloat16)], axis=0
    )
    featt_ref[:, row_count:] = virt.T
    wq_copy.wait()
    qt_ref[...] = rounded(rows_contracted(wq_ref[...], featt_ref[:, :row_count]))
    wkv_copy.wait()
    kv_ref[:row_count] = rounded(f32_dot(feat_ref[...], wkv_ref[...]))
    kv_ref[row_count:] = rounded(f32_dot(virt, wkv_ref[...]))
    kvt_ref[...] = kv_ref[...].T
    og_copy.wait()
    wo_copy.wait()
    odt_ref[...] = rounded(times_transposed(wo_ref[...], og_ref[...]))


def attend_kernel(
    rows_per_piece,
    factor,
    virt_rows,
    core_ref,
    halo_ref,
    arrived_ref,
    og_ref,
    wq_ref,
    wkv_ref,
    featt_ref,
    qt_ref,
    odt_ref,
    own_kv_ref,
    own_kvt_ref,
    local_bias_ref,
    far_bias_ref,
    gf_ref,
    halo_feat_ref,
    slot_feat_ref,
    keep_ref,
    send_ref,
    kv_ref,
    kvt_ref,
    extt_ref,
    gqt_ref,
    gkvt_ref,
    ot_ref,
):
    width, row_count = qt_ref.shape
    tile = halo_ref.shape[0]
    tile_count = row_count // tile
    slots = arrived_ref.shape[0]
    near = tile + row_count
    virt_at = near + slots
    head_dim = width // HEADS
    scale = 1.0 / math.sqrt(head_dim)

    kv_ref[tile:near] = own_kv_ref[:row_count]
    kv_ref[virt_at:] = own_kv_ref[row_count:]
    kvt_ref[:, tile:near] = own_kvt_ref[:, :row_count]
    kvt_ref[:, virt_at:] = own_kvt_ref[:, row_count:]
    extt_ref[:, tile:near] = featt_ref[:, :row_count]
    extt_ref[:, virt_at:] = featt_ref[:, row_count:]
    for rows, source_ref in ((slice(0, tile), halo_ref), (slice(near, virt_at), arrived_ref)):
        extt_ref[:, rows] = source_ref[...].T
        kv_ref[rows] = rounded(f32_dot(source_ref[...], wkv_ref[...]))
        kvt_ref[:, rows] = kv_ref[rows].T

    def tiles(of):
        return jnp.concatenate([of(t, slice(t * tile, (t + 1) * tile)) for t in range(tile_count)], 1)

    for head in range(HEADS):
        low, high = head * head_dim, (head + 1) * head_dim
        first = low // 128 * 128
        last = min(-(-high // 128) * 128, width)
        column = lax.broadcasted_iota(jnp.int32, (last - first, row_count), 0) + first
        of_head = (column >= low) & (column < high)
        q_rows = jnp.where(of_head, qt_ref[first:last, :], 0)
        d_rows = jnp.where(of_head, odt_ref[first:last, :], 0)

        def products(operand, start, stop):
            local = tiles(
                lambda t, lanes: f32_dot(
                    kv_ref[t * tile : (t + 2) * tile, start:stop], operand[:, lanes]
                )
            )
            return local, f32_dot(kv_ref[near:, start:stop], operand)

        s_local, s_far = products(q_rows, first, last)
        s_local += local_bias_ref[...]
        s_far += far_bias_ref[...]
        peak = jnp.maximum(
            jnp.max(s_local, axis=0, keepdims=True), jnp.max(s_far, axis=0, keepdims=True)
        )
        exponent_scale = scale * math.log2(math.e)
        e_local = jnp.exp2((s_local - peak) * exponent_scale)
        e_far = jnp.exp2((s_far - peak) * exponent_scale)
        total = jnp.sum(e_local, axis=0, keepdims=True) + jnp.sum(e_far, axis=0, keepdims=True)
        inverse = 1.0 / total
        p_local = e_local * inverse
        p_far = e_far * inverse
        dp_local, dp_far = products(d_rows, width + first, width + last)
        delta = jnp.sum(p_local * dp_local, axis=0, keepdims=True) + jnp.sum(
            p_far * dp_far, axis=0, keepdims=True
        )
        pb_local, pb_far = rounded(p_local), rounded(p_far)
        ds_local = rounded(p_local * (dp_local - delta))
        ds_far = rounded(p_far * (dp_far - delta))

        def to_queries(start, local, beyond):
            rows = slice(start + low, start + high)
            near_part = tiles(
                lambda t, lanes: f32_dot(kvt_ref[rows, t * tile : (t + 2) * tile], local[:, lanes])
            )
            return near_part + f32_dot(kvt_ref[rows, near:], beyond)

        ot_ref[low:high] = rounded(to_queries(width, pb_local, pb_far))
        gqt_ref[low:high] = rounded(to_queries(0, ds_local, ds_far) * scale)

        def to_keys(start, operand, local, beyond, factor):
            rows = slice(start + low, start + high)
            parts = []
            carried = None
            for t in range(tile_count):
                lanes = slice(t * tile, (t + 1) * tile)
                window = times_transposed(operand[:, lanes], local[:, lanes])
                previous = window[:, :tile]
                parts.append(previous if carried is None else previous + carried)
                carried = window[:, tile:]
            parts.append(carried)
            parts.append(times_transposed(operand, beyond))
            gathered = jnp.concatenate(parts, axis=1)
            gkvt_ref[rows] = rounded(gathered if factor is None else gathered * factor)

        to_keys(0, qt_ref[low:high], ds_local, ds_far, scale)
        to_keys(width, odt_ref[low:high], pb_local, pb_far, None)

    by_feature = f32_dot(wkv_ref[...], gkvt_ref[...])
    own = by_feature[:, tile:near] + f32_dot(wq_ref[...], gqt_ref[...])
    gf_ref[...] = own.T
    halo_feat_ref[...] = rounded(by_feature[:, :tile].T)
    slot_feat_ref[...] = rounded(by_feature[:, near:virt_at].T)
    virt_feat = by_feature[:, virt_at:].T * factor

    sums = (
        times_transposed(extt_ref[:, tile:near], gqt_ref[...]),
        times_transposed(extt_ref[...], gkvt_ref[:width]),
        times_transposed(extt_ref[...], gkvt_ref[width:]),
        f32_dot(ot_ref[...], og_ref[...]),
    )
    pieces = keep_ref.shape[0]
    columns = width // LANES

    def write(half, piece_ref, cast):
        rest = piece_ref.shape[1] - columns * rows_per_piece
        for piece in range(pieces):
            start = (half * pieces + piece) * rows_per_piece
            value = sums[start // width][start % width : start % width + rows_per_piece] * factor
            for at in range(columns):
                rows = slice(at * rows_per_piece, (at + 1) * rows_per_piece)
                piece_ref[piece, rows] = cast(value[:, at * LANES : (at + 1) * LANES])
            rider = half * pieces + piece
            padding = jnp.zeros((rest, LANES), jnp.float32)
            if rider < virt_rows * columns:
                row, at = rider // columns, rider % columns
                padding = jnp.broadcast_to(
                    virt_feat[row : row + 1, at * LANES : (at + 1) * LANES], (rest, LANES)
                )
            piece_ref[piece, columns * rows_per_piece :] = cast(padding)

    for core in range(2):

        @pl.when(core_ref[0] == core)
        def _():
            write(core, keep_ref, lambda value: value)
            write(1 - core, send_ref, rounded)


def place_kernel(rows_per_piece, core_ref, near_ref, far_ref, gq_ref, gkv_ref, go_ref, gvirt_ref):
    width = gq_ref.shape[0]
    pieces = near_ref.shape[0]
    columns = width // LANES

    def write(half, piece_ref):
        for piece in range(pieces):
            start = (half * pieces + piece) * rows_per_piece
            which, row = start // width, start % width
            rows = slice(row, row + rows_per_piece)
            for at in range(columns):
                lanes = slice(at * LANES, (at + 1) * LANES)
                value = piece_ref[piece, at * rows_per_piece : (at + 1) * rows_per_piece]
                value = value.astype(jnp.float32)
                if which == 0:
                    gq_ref[rows, lanes] = value
                elif which == 3:
                    go_ref[rows, lanes] = value
                else:
                    shift = (which - 1) * width
                    gkv_ref[rows, slice(lanes.start + shift, lanes.stop + shift)] = value
            rider = half * pieces + piece
            if rider < gvirt_ref.shape[0] * columns:
                row, at = rider // columns, rider % columns
                rest = piece_ref[piece, columns * rows_per_piece :].astype(jnp.float32)
                gvirt_ref[row : row + 1, at * LANES : (at + 1) * LANES] = rest[:1]

    for core in range(2):

        @pl.when(core_ref[0] == core)
        def _():
            write(core, near_ref)
            write(1 - core, far_ref)


def return_kernel(gf_ref, halo_ref, send_ref, returned_ref, out_ref):
    row_count = gf_ref.shape[0]
    tile = halo_ref.shape[0]
    chosen = listed_rows(send_ref, row_count)
    total = gf_ref[...] + rows_contracted(chosen, returned_ref[...])
    out_ref[: row_count - tile] = total[: row_count - tile]
    out_ref[row_count - tile :] = total[row_count - tile :] + halo_ref[...].astype(jnp.float32)


def call(kernel, name, outs, args, scratch=(), fetched=0, scalars=0, flops=0):
    spaces = [pltpu.SMEM] * scalars + [pl.ANY] * fetched
    spaces += [pltpu.VMEM] * (len(args) - len(spaces))
    moved = sum(x.size * x.dtype.itemsize for x in list(args) + list(outs))
    scratch = list(scratch)
    if fetched:
        scratch.append(pltpu.SemaphoreType.DMA((fetched,)))
    return pl.pallas_call(
        kernel,
        out_shape=outs,
        in_specs=[pl.BlockSpec(memory_space=space) for space in spaces],
        out_specs=[pl.BlockSpec(memory_space=pltpu.VMEM)] * len(outs),
        scratch_shapes=scratch,
        compiler_params=pltpu.CompilerParams(vmem_limit_bytes=VMEM_BYTES),
        cost_estimate=pl.CostEstimate(flops=flops, bytes_accessed=moved, transcendentals=0),
        name=name,
    )(*args)


def shards(features, out_grad, w_query, w_keyval, w_out, virtual, local_nbr, expander, send_rows):
    row_count, width = features.shape
    dom_size, per_peer = send_rows.shape
    slots = dom_size * per_peer
    virt_rows = virtual.shape[0]
    padded = ROW_PACK * -(-virt_rows // ROW_PACK)
    ext_rows = TILE + row_count + slots + padded
    chips = math.prod(lax.axis_size(axis) for axis in CHIPS)
    rows_per_piece = 2 * width // chips
    piece_rows = width // LANES * rows_per_piece + 1
    piece_rows = ROW_PACK * -(-piece_rows // ROW_PACK)
    bf16, f32 = jnp.bfloat16, jnp.float32
    shape = jax.ShapeDtypeStruct
    core = lax.axis_index(CORE).astype(jnp.int32).reshape(1)

    sent, halo = call(
        pick_kernel,
        "pick_rows",
        [shape((slots, width), bf16), shape((TILE, width), bf16)],
        [features, send_rows],
        [pltpu.VMEM(features.shape, bf16), pltpu.VMEM(send_rows.shape, jnp.int32)],
        fetched=2,
    )
    arrived = exchanged(sent, DOM)
    halo = shifted(halo, ROWS, 1)
    prepared = call(
        prepare_kernel,
        "prepare",
        [
            shape(out_grad.shape, bf16),
            shape(w_query.shape, bf16),
            shape(w_keyval.shape, bf16),
            shape((width, row_count + padded), bf16),
            shape((width, row_count), bf16),
            shape((width, row_count), bf16),
            shape((row_count + padded, 2 * width), bf16),
            shape((2 * width, row_count + padded), bf16),
            shape((2 * TILE, row_count), f32),
            shape((slots + padded, row_count), f32),
        ],
        [features, out_grad, w_query, w_keyval, w_out, virtual, local_nbr.T, expander.T],
        [
            pltpu.VMEM(features.shape, bf16),
            pltpu.VMEM(w_out.shape, bf16),
            pltpu.VMEM(virtual.shape, bf16),
            pltpu.VMEM(local_nbr.shape[::-1], jnp.int32),
            pltpu.VMEM(expander.shape[::-1], jnp.int32),
        ],
        fetched=8,
        flops=10 * row_count * width * width,
    )
    own_feat, halo_feat, slot_feat, keep, message = call(
        functools.partial(
            attend_kernel, rows_per_piece, (row_count * dom_size * lax.axis_size(CORE) * lax.axis_size(ROWS[0])) ** -0.5, virt_rows
        ),
        "attend",
        [
            shape((row_count, width), f32),
            shape((TILE, width), bf16),
            shape((slots, width), bf16),
            shape((chips, piece_rows, LANES), f32),
            shape((chips, piece_rows, LANES), bf16),
        ],
        [core, halo, arrived, *prepared],
        [
            pltpu.VMEM((ext_rows, 2 * width), bf16),
            pltpu.VMEM((2 * width, ext_rows), bf16),
            pltpu.VMEM((width, ext_rows), bf16),
            pltpu.VMEM((width, row_count), bf16),
            pltpu.VMEM((2 * width, ext_rows), bf16),
            pltpu.VMEM((width, row_count), bf16),
        ],
        scalars=1,
        flops=32 * ext_rows * width * width,
    )

    both = rounded(keep + swapped(message, CORE).astype(f32))
    parts = exchanged(both, CHIPS)
    slots_back = exchanged(slot_feat, DOM)
    halo_back = shifted(halo_feat, ROWS, -1)
    (grad_features,) = call(
        return_kernel,
        "return_rows",
        [shape((row_count, width), f32)],
        [own_feat, halo_back, send_rows, slots_back],
    )
    summed = rounded(jnp.sum(parts.astype(f32), axis=0))
    near = exchanged(jnp.broadcast_to(summed, parts.shape), CHIPS)
    grad_wq, grad_wkv, grad_wo, grad_virtual = call(
        functools.partial(place_kernel, rows_per_piece),
        "place_sums",
        [
            shape((width, width), f32),
            shape((width, 2 * width), f32),
            shape((width, width), f32),
            shape((virt_rows, width), f32),
        ],
        [core, near, swapped(near, CORE)],
        scalars=1,
    )
    return grad_features, grad_wq, grad_wkv, grad_wo, grad_virtual


def solution(mesh):
    dom_size, rows_size = mesh.shape["dom"], mesh.shape["rows"]
    split = jax.sharding.Mesh(
        mesh.devices.reshape(dom_size, rows_size // 2, 2), (*DOM, *ROWS)
    )
    nodes = P((*DOM, *ROWS), None)
    placed = (nodes, nodes, P(), P(), P(), P(), nodes, nodes, nodes)
    return jax.shard_map(
        shards,
        mesh=split,
        in_specs=placed,
        out_specs=(nodes, P(), P(), P(), P()),
        check_vma=False,
    )
```

time: 97.3 us -> 105 us (1.079)
  blocking collectives: 0 us -> 46.4 us
  starting transfers between devices: 41.1 us -> 13 us
  waiting for transfers between devices: 30.6 us -> 9.83 us
  local copies, waits for them, and re-layouts: 8.71 us -> 18.3 us
    all_to_all x0 -> x2, blocking collectives: none -> 46.4 us  [exchanged(): return lax.all_to_all(blocks, axes, split_axis=0, concat_axis=0, tiled=True)]
    ppermute x30 -> x4, starting transfers between devices: 41.1 us -> 2.35 us  [the longest x2 1.62 us: swapped(): lax.ppermute(block, axis, [(i, i ^ 1) for i in range(lax.axis_size(axis))])]
    ppermute x30 -> x4, waiting for transfers between devices: 30.6 us -> 3.94 us  [the longest x2 2.22 us: shifted(): lax.ppermute(block, axes, [((i - distance) % count, i) for i in range(cou...]
    all_to_all x0 -> x2, starting transfers between devices: none -> 10.7 us  [exchanged(): return lax.all_to_all(blocks, axes, split_axis=0, concat_axis=0, tiled=True)]
    unnamed x25 -> x50, local copies, waits for them, and re-layouts: 7.7 us -> 18.2 us
    all_to_all x0 -> x2, waiting for transfers between devices: none -> 5.89 us  [exchanged(): return lax.all_to_all(blocks, axes, split_axis=0, concat_axis=0, tiled=True)]
    pallas_call x4 -> x5, Pallas kernels: 14.3 us -> 15.2 us  [call(): pl.pallas_call(kernel, out_shape=outs, in_specs=[pl.BlockSpec(memory_spac...]
  transfers between devices with their start and end apart: 30 -> 6, of which waited for: 15 -> 3; matrix products, arithmetic and copies ran while one was open for 1% -> 0% of each run, Pallas kernels for 3% -> 4%
where the time goes in v3:
time: 105 us; the launch traced here: 104 us
  blocking collectives  46.4 us (44%)
  local copies, waits for them, and re-layouts  18.3 us (17%)
  Pallas kernels  15.2 us (14%)
  starting transfers between devices  13 us (12%)
  waiting for transfers between devices  9.83 us (9%)
    all_to_all x2, blocking collectives, exchanged(): return lax.all_to_all(blocks, axes, split_axis=0, concat_axis=0, tiled=True)  46.4 us
    unnamed x50, local copies, waits for them, and re-layouts  18.2 us
    pallas_call x5, Pallas kernels, call(): pl.pallas_call(kernel, out_shape=outs, in_specs=[pl.BlockSpec(memory_spac...  15.2 us
    all_to_all x2, starting transfers between devices, exchanged(): return lax.all_to_all(blocks, axes, split_axis=0, concat_axis=0, tiled=True)  10.7 us
    all_to_all x2, waiting for transfers between devices, exchanged(): return lax.all_to_all(blocks, axes, split_axis=0, concat_axis=0, tiled=True)  5.89 us
    ppermute x2, waiting for transfers between devices, shifted(): lax.ppermute(block, axes, [((i - distance) % count, i) for i in range(cou...  2.22 us
  transfers between devices with their start and end apart: 6, of which 3 were waited for; matrix products, arithmetic and copies ran while one was open for 0% of the time, Pallas kernels for 4%

profile of v3, /device:TPU:0, one launch (start us, length us, event | category | flops | bytes accessed | tf_op | source)
XLA Modules:
  0.0 103.7 jit_solution(16601063023894195461)
XLA Ops:
  0.6 0.0 copy-start
  0.6 0.9 copy-done
  1.6 0.7 copy-done.7
  2.2 1.3 %pick_rows.1 = (bf16[256,384]{1,0:T(8,128)(2,1)}, bf16[128,384]{1,0:T(8,128)(2,1)}) custom-call(bf16[256,384]{1,0:T(8,128)(2,1)S(1)} %copy-done, s32[8,32]{1,0:T(8,128)S(1)} %copy-done.7), custom_call_target="tpu_custom_call" | custom-call | bytes 492544 | tf_op jit(solution)/shard_map/pick_rows/pallas_call | solution.py:382
  3.6 7.3 %all-to-all-start = ((bf16[8,32,384]{2,1,0:T(8,128)(2,1)}), bf16[8,32,384]{2,1,0:T(8,128)(2,1)S(1)}, u32[]{:S(2)}, u32[]{:S(2)}) async-start(bf16[8,32,384]{2,1,0:T(8,128)(2,1)} %bitcast.1), calls=%async_computation | async-start | bytes 393216 | tf_op jit(solution)/shard_map/all_to_all | solution.py:53
  10.8 0.0 collective-permute-start
  10.8 0.0 copy-start.1
  10.9 0.9 copy-done.1
  11.8 1.1 %copy-done.2 = bf16[384,768]{1,0:T(8,128)(2,1)S(1)} copy-done((bf16[384,768]{1,0:T(8,128)(2,1)S(1)}, bf16[384,768]{1,0:T(8,128)(2,1)}, u32[]{:S(2)}) %copy-start.2) | copy-done | bytes 589848
  12.8 1.0 copy-done.3
  13.8 1.0 copy-done.4
  14.8 0.9 copy-done.5
  15.7 0.7 copy-done.6
  16.4 0.7 copy-done.9
  17.1 0.7 copy-done.10
  17.8 3.0 %prepare.1 = (bf16[256,384]{1,0:T(8,128)(2,1)S(1)}, bf16[384,384]{1,0:T(8,128)(2,1)S(1)}, bf16[384,768]{1,0:T(8,128)(2,1)S(1)}, bf16[384,272]{1,0:T(8,128)(2,1)S...) custom-call(bf16[256,384]{1,0:T(8,128)(2,1)S(1)} %copy-done.1, ...), custom_call_target="tpu_custom_call" | custom-call | flops 377487360 | bytes 4656128 | tf_op jit(solution)/shard_map/prepare/pallas_call | solution.py:382
  20.8 0.0 copy-start.11
  20.8 0.7 copy-done.11
  21.5 0.7 copy-done.13
  22.2 0.7 copy-done.15
  22.9 0.7 copy-done.17
  23.6 0.7 copy-done.19
  24.2 0.0 collective-permute-done.halo_ref
  24.2 0.6 copy-done.23
  24.9 0.0 all-to-all-done
  24.9 1.0 copy-done.12
  25.9 0.9 copy-done.14
  26.8 0.9 copy-done.16
  27.7 0.9 copy-done.18
  28.7 0.9 copy-done.20
  29.6 0.9 copy-done.24
  30.5 8.2 %attend.1 = (f32[256,384]{1,0:T(8,128)S(1)}, bf16[128,384]{1,0:T(8,128)(2,1)S(1)}, bf16[256,384]{1,0:T(8,128)(2,1)}, f32[16,160,128]{2,1,0:T(8,128)S(1)}, bf16[16,160,128]{2,1,0:T(8,128)(2,1)S(1)}) custom-call(s32[1]{0:T(128)} %bitcast.core_ref, bf16[128,384]{1,0:T(8,128)(2,1)S(1)} %copy-done.24, bf16[256,384]{1,0:T(8,128)(2,1)S(1)} %bitcast.8, ...), custom_call_target="tpu_custom_call" | custom-call | flops 3095396352 | bytes 6008836 | tf_op jit(solution)/shard_map/attend/pallas_call | solution.py:382
  38.7 1.6 %collective-permute-start.2 = (bf16[16,160,128]{2,1,0:T(8,128)(2,1)S(1)}, bf16[16,160,128]{2,1,0:T(8,128)(2,1)S(1)}, u32[]{:S(2)}, u32[]{:S(2)}) collective-permute-start(bf16[16,160,128]{2,1,0:T(8,128)(2,1)S(1)} %get-tuple-element.42), channel_id=1, source_target_pairs={{0,1},{1,0},{2,3},{3,2},{4,5},{5,4},{6,7},{7,6},{8,9},{9,8},{10,11... | collective-permute-start | bytes 1966088 | tf_op jit(solution)/shard_map/ppermute | solution.py:44
  40.3 1.7 %collective-permute-done.2 = bf16[16,160,128]{2,1,0:T(8,128)(2,1)S(1)} collective-permute-done((bf16[16,160,128]{2,1,0:T(8,128)(2,1)S(1)}, bf16[16,160,128]{2,1,0:T(8,128)(2,1)S(1)}, u32[]{:S(2)}, u32[]{:S(2)}) %collective-permute-start.2) | collective-permute-done | bytes 655392 | tf_op jit(solution)/shard_map/ppermute | solution.py:44
  42.0 0.2 add_convert_fusion
  42.2 25.2 %all_to_all.32 = bf16[16,160,128]{2,1,0:T(8,128)(2,1)S(1)} all-to-all(bf16[16,160,128]{2,1,0:T(8,128)(2,1)S(1)} %add_convert_fusion), channel_id=1, replica_groups=mesh['dom'=8,'row_chip'=2,'core'=2] {'dom','row_chip'}, dimensions={0} | all-to-all | bytes 1310720 | tf_op jit(solution)/shard_map/all_to_all | solution.py:53
  67.4 0.1 reduce_sum.12
  67.5 0.0 copy-start.22
  67.5 0.0 copy-start.8
  67.5 0.1 broadcast_in_dim.3
  67.6 21.2 %all_to_all.33.near_ref = bf16[16,160,128]{2,1,0:T(8,128)(2,1)S(1)} all-to-all(bf16[16,160,128]{2,1,0:T(8,128)(2,1)S(1)} %broadcast_in_dim.3), channel_id=1, replica_groups=mesh['dom'=8,'row_chip'=2,'core'=2] {'dom','row_chip'}, dimensions={0} | all-to-all | bytes 1310720 | tf_op jit(solution)/shard_map/all_to_all | solution.py:53
  88.8 3.4 %all-to-all-start.1 = ((bf16[8,32,384]{2,1,0:T(8,128)(2,1)}), bf16[8,32,384]{2,1,0:T(8,128)(2,1)S(1)}, u32[]{:S(2)}, u32[]{:S(2)}) async-start(bf16[8,32,384]{2,1,0:T(8,128)(2,1)} %bitcast.5), calls=%async_computation.1 | async-start | bytes 393216 | tf_op jit(solution)/shard_map/all_to_all | solution.py:53
  92.2 0.7 collective-permute-start.1
  92.9 2.2 %collective-permute-done.1.halo_ref = bf16[128,384]{1,0:T(8,128)(2,1)S(1)} collective-permute-done((bf16[128,384]{1,0:T(8,128)(2,1)S(1)}, bf16[128,384]{1,0:T(8,128)(2,1)S(1)}, u32[]{:S(2)}, u32[]{:S(2)}) %collective-permute-start.1) | collective-permute-done | bytes 98336 | tf_op jit(solution)/shard_map/ppermute | solution.py:49
  95.2 5.9 %all-to-all-done.1 = bf16[8,32,384]{2,1,0:T(8,128)(2,1)S(1)} async-done(((bf16[8,32,384]{2,1,0:T(8,128)(2,1)}), bf16[8,32,384]{2,1,0:T(8,128)(2,1)S(1)}, u32[]{:S(2)}, u32[]{:S(2)}) %all-to-all-start.1) | async-done | bytes 196640 | tf_op jit(solution)/shard_map/all_to_all | solution.py:53
  101.1 1.1 %return_rows.1 = f32[256,384]{1,0:T(8,128)} custom-call(f32[256,384]{1,0:T(8,128)S(1)} %get-tuple-element.38.gf_ref, bf16[128,384]{1,0:T(8,128)(2,1)S(1)} %collective-permute-done.1.halo_ref, s32[8,32]{1,0:T(8,128)S(1)} %copy-done.8, bf16[256,384]{1,0:T(8,128)(2,1)S(1)} %bitcast.7), custom_call_target="tpu_custom_call" | custom-call | bytes 1082368 | tf_op jit(solution)/shard_map/return_rows/pallas_call | solution.py:382
  102.2 0.0 collective-permute-done.3.far_ref
  102.2 1.6 %place_sums.1 = (f32[384,384]{1,0:T(8,128)}, f32[384,768]{1,0:T(8,128)}, f32[384,384]{1,0:T(8,128)}, f32[4,384]{1,0:T(4,128)}) custom-call(s32[1]{0:T(128)} %bitcast.core_ref, bf16[16,160,128]{2,1,0:T(8,128)(2,1)S(1)} %all_to_all.33.near_ref, bf16[16,160,128]{2,1,0:T(8,128)(2,1)S(1)} %collective-permute-done.3.far_ref), custom_call_target="tpu_custom_call" | custom-call | bytes 3676164 | tf_op jit(solution)/shard_map/place_sums/pallas_call | solution.py:382
  (24 shorter events, 0.0 us)
Async XLA Ops:
  0.6 0.9 copy-start
  1.6 0.7 copy-start.7
  3.6 21.3 %all-to-all-start = ((bf16[8,32,384]{2,1,0:T(8,128)(2,1)}), bf16[8,32,384]{2,1,0:T(8,128)(2,1)S(1)}, u32[]{:S(2)}, u32[]{:S(2)}) async-start(bf16[8,32,384]{2,1,0:T(8,128)(2,1)} %bitcast.1), calls=%async_computation | async-start | bytes 393216 | tf_op jit(solution)/shard_map/all_to_all | solution.py:53
  10.8 13.4 %collective-permute-start = (bf16[128,384]{1,0:T(8,128)(2,1)}, bf16[128,384]{1,0:T(8,128)(2,1)S(1)}, u32[]{:S(2)}, u32[]{:S(2)}) collective-permute-start(bf16[128,384]{1,0:T(8,128)(2,1)} %get-tuple-element.26), channel_id=1, source_target_pairs={{3,0},{0,1},{1,2},{2,3},{7,4},{4,5},{5,6},{6,7},{11,8},{8,9},{9,10... | collective-permute-start | bytes 294920 | tf_op jit(solution)/shard_map/ppermute | solution.py:49
  10.8 0.9 copy-start.1
  11.8 1.1 %copy-start.2 = (bf16[384,768]{1,0:T(8,128)(2,1)S(1)}, bf16[384,768]{1,0:T(8,128)(2,1)}, u32[]{:S(2)}) copy-start(bf16[384,768]{1,0:T(8,128)(2,1)} %wkv_hbm.1) | copy-start | bytes 1769476
  12.8 1.0 copy-start.3
  13.8 1.0 copy-start.4
  14.8 0.9 copy-start.5
  15.7 0.7 copy-start.6
  16.4 0.7 copy-start.9
  17.1 0.7 copy-start.10
  20.8 0.7 copy-start.11
  21.5 0.7 copy-start.13
  22.2 0.7 copy-start.15
  22.9 0.7 copy-start.17
  23.6 0.7 copy-start.19
  24.2 0.7 copy-start.23
  24.9 1.0 copy-start.12
  25.9 0.9 copy-start.14
  26.8 0.9 copy-start.16
  27.7 0.9 copy-start.18
  28.7 0.9 copy-start.20
  29.6 0.9 copy-start.24
  38.7 3.5 %copy-start.21 = (bf16[128,384]{1,0:T(8,128)(2,1)}, bf16[128,384]{1,0:T(8,128)(2,1)S(1)}, u32[]{:S(2)}) copy-start(bf16[128,384]{1,0:T(8,128)(2,1)S(1)} %get-tuple-element.39) | copy-start | bytes 294916
  38.7 3.3 %collective-permute-start.2 = (bf16[16,160,128]{2,1,0:T(8,128)(2,1)S(1)}, bf16[16,160,128]{2,1,0:T(8,128)(2,1)S(1)}, u32[]{:S(2)}, u32[]{:S(2)}) collective-permute-start(bf16[16,160,128]{2,1,0:T(8,128)(2,1)S(1)} %get-tuple-element.42), channel_id=1, source_target_pairs={{0,1},{1,0},{2,3},{3,2},{4,5},{5,4},{6,7},{7,6},{8,9},{9,8},{10,11... | collective-permute-start | bytes 1966088 | tf_op jit(solution)/shard_map/ppermute | solution.py:44
  67.5 24.7 %copy-start.22 = (bf16[128,384]{1,0:T(8,128)(2,1)S(1)}, bf16[128,384]{1,0:T(8,128)(2,1)}, u32[]{:S(2)}) copy-start(bf16[128,384]{1,0:T(8,128)(2,1)} %copy-done.21) | copy-start | bytes 294916
  67.5 33.6 %copy-start.8 = (s32[8,32]{1,0:T(8,128)S(1)}, s32[8,32]{1,0:T(8,128)}, u32[]{:S(2)}) copy-start(s32[8,32]{1,0:T(8,128)} %send_ref.1) | copy-start | bytes 3076
  88.8 13.4 %collective-permute-start.3 = (bf16[16,160,128]{2,1,0:T(8,128)(2,1)S(1)}, bf16[16,160,128]{2,1,0:T(8,128)(2,1)S(1)}, u32[]{:S(2)}, u32[]{:S(2)}) collective-permute-start(bf16[16,160,128]{2,1,0:T(8,128)(2,1)S(1)} %all_to_all.33.near_ref), channel_id=1, source_target_pairs={{0,1},{1,0},{2,3},{3,2},{4,5},{5,4},{6,7},{7,6},{8,9},{9,8},{10,11... | collective-permute-start | bytes 1966088 | tf_op jit(solution)/shard_map/ppermute | solution.py:44
  88.8 12.2 %all-to-all-start.1 = ((bf16[8,32,384]{2,1,0:T(8,128)(2,1)}), bf16[8,32,384]{2,1,0:T(8,128)(2,1)S(1)}, u32[]{:S(2)}, u32[]{:S(2)}) async-start(bf16[8,32,384]{2,1,0:T(8,128)(2,1)} %bitcast.5), calls=%async_computation.1 | async-start | bytes 393216 | tf_op jit(solution)/shard_map/all_to_all | solution.py:53
  92.2 2.9 %collective-permute-start.1 = (bf16[128,384]{1,0:T(8,128)(2,1)S(1)}, bf16[128,384]{1,0:T(8,128)(2,1)S(1)}, u32[]{:S(2)}, u32[]{:S(2)}) collective-permute-start(bf16[128,384]{1,0:T(8,128)(2,1)S(1)} %copy-done.22), channel_id=1, source_target_pairs={{1,0},{2,1},{3,2},{0,3},{5,4},{6,5},{7,6},{4,7},{9,8},{10,9},{11,1... | collective-permute-start | bytes 294920 | tf_op jit(solution)/shard_map/ppermute | solution.py:49

commit v4 on v3

--- a/solution.py
+++ b/solution.py
@@ -14,10 +14,6 @@
 NEGATIVE_FILL = -1e30
 VMEM_BYTES = 24 * 1024 * 1024
 LANES = 128
-CORE = "core"
-ROWS = ("row_chip", CORE)
-DOM = ("dom",)
-CHIPS = ("dom", "row_chip")
 
 
 def f32_dot(left, right):
@@ -40,28 +36,151 @@
     return value.astype(jnp.bfloat16)
 
 
-def swapped(block, axis):
-    return lax.ppermute(block, axis, [(i, i ^ 1) for i in range(lax.axis_size(axis))])
-
-
-def shifted(block, axes, distance):
-    count = math.prod(lax.axis_size(axis) for axis in axes)
-    return lax.ppermute(block, axes, [((i - distance) % count, i) for i in range(count)])
-
-
-def exchanged(blocks, axes):
-    return lax.all_to_all(blocks, axes, split_axis=0, concat_axis=0, tiled=True)
-
-
-def listed_rows(send_ref, row_count):
+def exchange_stages(dom_size, rows_size):
+    dom_bits = [1 << i for i in range(dom_size.bit_length() - 1)]
+    rows_bits = [1 << i for i in range(rows_size.bit_length() - 1)]
+    stages = [[("rows", bit)] for bit in rows_bits[:1]]
+    rest = [("rows", bit) for bit in rows_bits[1:2]] + [("dom", bit) for bit in dom_bits]
+    rest += [("rows", bit) for bit in rows_bits[2:]]
+    for at in range(0, len(rest), 2):
+        stages.append(rest[at : at + 2])
+    return stages
+
+
+def scattered_stages(stages, rows):
+    taken = []
+    for stage in stages:
+        if rows % (ROW_PACK << len(stage)):
+            break
+        rows >>= len(stage)
+        taken.append(stage)
+    return taken
+
+
+def partner_masks(stage):
+    masks = []
+    for digit in range(1, 1 << len(stage)):
+        by_axis = {"dom": 0, "rows": 0}
+        for i, (axis, bit) in enumerate(stage):
+            if digit >> i & 1:
+                by_axis[axis] |= bit
+        masks.append((by_axis["dom"], by_axis["rows"]))
+    return masks
+
+
+def own_piece(stages):
+    index = jnp.int32(0)
+    for stage in stages:
+        index = index << len(stage)
+        for i, (axis, bit) in enumerate(stage):
+            index += jnp.where(lax.axis_index(axis) & bit, 1 << i, 0)
+    return index
+
+
+def swapped(block, dom_mask, rows_mask):
+    dom_size, rows_size = lax.axis_size("dom"), lax.axis_size("rows")
+    route = [
+        (a * rows_size + b, (a ^ dom_mask) * rows_size + (b ^ rows_mask))
+        for a in range(dom_size)
+        for b in range(rows_size)
+    ]
+    return lax.ppermute(block, ("dom", "rows"), route)
+
+
+def shifted(block, axis, distance):
+    devices = range(lax.axis_size(axis))
+    route = [((i - distance) % len(devices), i) for i in devices]
+    return lax.ppermute(block, axis, route)
+
+
+def paired_sum(terms):
+    while len(terms) > 1:
+        terms = [left + right for left, right in zip(terms[::2], terms[1::2])]
+    return terms[0]
+
+
+def summed_everywhere(keep, message, rider, stages, scattered, slots):
+    per_peer = slots[0].shape[0]
+    returned = [slots[0]]
+    handed_on = {}
+    dom_masks = set(range(2, len(slots), 2))
+
+    def riding(dom_mask, rows_mask):
+        if rows_mask or not dom_mask:
+            return []
+        if dom_mask == 1:
+            return slots[1::2]
+        dom_masks.discard(dom_mask)
+        return [slots[dom_mask], handed_on[dom_mask]]
+
+    def unloaded(dom_mask, rows_mask, load):
+        if rows_mask or not dom_mask:
+            return
+        if dom_mask == 1:
+            returned.append(load[:per_peer])
+            for at in range(1, len(slots) // 2):
+                handed_on[2 * at] = load[at * per_peer : (at + 1) * per_peer]
+        else:
+            returned.append((dom_mask, load))
+
+    first = True
+    for stage in stages:
+        halved = stage in scattered
+        rider_bf = rounded(rider)
+        masks = partner_masks(stage)
+        if not halved:
+            keep = rounded(keep).astype(jnp.float32)
+        part = keep.shape[0]
+        if halved and not first:
+            part //= 1 << len(stage)
+        base = part + rider.shape[0]
+        messages = {}
+        for at, (dom_mask, rows_mask) in enumerate(masks, 1):
+            if not first:
+                block = keep[at * part : (at + 1) * part] if halved else keep
+                message = jnp.concatenate(
+                    [rounded(block), rider_bf, *riding(dom_mask, rows_mask)], axis=0
+                )
+            messages[at] = message
+        order = reversed(messages) if ("rows", 2) in stage else messages
+        sent = {at: swapped(messages[at], *masks[at - 1]) for at in order}
+        terms, rider_terms = [keep[:part]], [rider_bf.astype(jnp.float32)]
+        for at, (dom_mask, rows_mask) in enumerate(masks, 1):
+            arrived = sent[at]
+            terms.append(arrived[:part].astype(jnp.float32))
+            rider_terms.append(arrived[part:base].astype(jnp.float32))
+            if not first:
+                unloaded(dom_mask, rows_mask, arrived[base:])
+        keep, rider = paired_sum(terms), paired_sum(rider_terms)
+        first = False
+    for mask in sorted(dom_masks):
+        load = jnp.concatenate([slots[mask], handed_on[mask]], axis=0)
+        returned.append((mask, swapped(load, mask, 0)))
+    loads = dict(returned[2:])
+    returned = returned[:2] + [loads[mask] for mask in sorted(loads)]
+
+    held = rounded(keep)
+    for stage in reversed(scattered[2:]):
+        held = jnp.concatenate(
+            [held] + [swapped(held, *masks) for masks in partner_masks(stage)], axis=0
+        )
+    near = [held]
+    if len(scattered) > 1:
+        arrived = [swapped(held, *masks) for masks in reversed(partner_masks(scattered[1]))]
+        near += arrived[::-1]
+    far = [swapped(block, *partner_masks(scattered[0])[0]) for block in near]
+    return near, far, rider, returned
+
+
+def listed_rows(dom, send_ref, row_count):
     dom_size, per_peer = send_ref.shape
     slots = dom_size * per_peer
     slot = lax.broadcasted_iota(jnp.int32, (slots, per_peer), 0)
     place = lax.broadcasted_iota(jnp.int32, (slots, per_peer), 1)
+    peer = (slot // per_peer) ^ dom
     listed = jnp.zeros((slots, per_peer), jnp.int32)
     for at in range(dom_size):
-        here = slot == place + at * per_peer
-        listed += jnp.where(here, send_ref[at : at + 1, :], 0)
+        listed += jnp.where((peer == at) & (place == slot % per_peer), send_ref[at : at + 1, :], 0)
     column = jnp.sum(listed, axis=1, keepdims=True)
     rows = lax.broadcasted_iota(jnp.int32, (slots, row_count), 1)
     return jnp.where(column == rows, 1.0, 0.0).astype(jnp.bfloat16)
@@ -77,16 +196,25 @@
     return copies
 
 
-def pick_kernel(feat_hbm, send_hbm, out_ref, halo_ref, feat_ref, send_ref, sems):
+def pick_kernel(place_ref, feat_hbm, send_hbm, halo_ref, through_ref, *refs):
+    direct_refs, (feat_ref, send_ref, sems) = refs[:-3], refs[-3:]
     copies = fetch([(send_hbm, send_ref), (feat_hbm, feat_ref)], sems)
     copies[0].wait()
-    chosen = listed_rows(send_ref, feat_ref.shape[0])
+    per_peer = send_ref.shape[1]
+    chosen = listed_rows(place_ref[0], send_ref, feat_ref.shape[0])
     copies[1].wait()
     halo_ref[...] = feat_ref[feat_ref.shape[0] - halo_ref.shape[0] :]
-    out_ref[...] = rounded(f32_dot(chosen, feat_ref[...]))
+    picked = rounded(f32_dot(chosen, feat_ref[...]))
+    for at, out_ref in enumerate(direct_refs):
+        out_ref[...] = picked[2 * at * per_peer : (2 * at + 1) * per_peer]
+        through_ref[at * per_peer : (at + 1) * per_peer] = picked[
+            (2 * at + 1) * per_peer : (2 * at + 2) * per_peer
+        ]
 
 
 def prepare_kernel(
+    per_peer,
+    place_ref,
     feat_hbm,
     og_hbm,
     wq_hbm,
@@ -143,7 +271,9 @@
     nbr_copy.wait()
     local_bias_ref[...] = jnp.where(multiplicity(window, nbr_ref) > 0.0, 0.0, NEGATIVE_FILL)
     exp_copy.wait()
-    named_times = multiplicity(slots, exp_ref)
+    expander = exp_ref[...]
+    expander = ((expander // per_peer) ^ place_ref[0]) * per_peer + expander % per_peer
+    named_times = multiplicity(slots, expander)
     slot_bias = jnp.full((slots, row_count), NEGATIVE_FILL, jnp.float32)
     for times in range(1, exp_ref.shape[0] + 1):
         slot_bias = jnp.where(named_times == float(times), math.log(times) / scale, slot_bias)
@@ -172,36 +302,22 @@
 def attend_kernel(
     rows_per_piece,
     factor,
-    virt_rows,
-    core_ref,
+    per_peer,
+    dom_size,
+    place_ref,
     halo_ref,
-    arrived_ref,
-    og_ref,
-    wq_ref,
-    wkv_ref,
-    featt_ref,
-    qt_ref,
-    odt_ref,
-    own_kv_ref,
-    own_kvt_ref,
-    local_bias_ref,
-    far_bias_ref,
-    gf_ref,
-    halo_feat_ref,
-    slot_feat_ref,
-    keep_ref,
-    send_ref,
-    kv_ref,
-    kvt_ref,
-    extt_ref,
-    gqt_ref,
-    gkvt_ref,
-    ot_ref,
+    *refs,
 ):
+    piece_refs, refs = refs[: 1 + dom_size // 2], refs[1 + dom_size // 2 :]
+    og_ref, wq_ref, wkv_ref, featt_ref, qt_ref, odt_ref, own_kv_ref, own_kvt_ref = refs[:8]
+    local_bias_ref, far_bias_ref, gf_ref, halo_feat_ref = refs[8:12]
+    slot_feat_refs, refs = refs[12 : 12 + dom_size], refs[12 + dom_size :]
+    keep_ref, send_ref, rider_ref = refs[:3]
+    slot_ref, kv_ref, kvt_ref, extt_ref, gqt_ref, gkvt_ref, ot_ref = refs[3:]
     width, row_count = qt_ref.shape
     tile = halo_ref.shape[0]
     tile_count = row_count // tile
-    slots = arrived_ref.shape[0]
+    slots = dom_size * per_peer
     near = tile + row_count
     virt_at = near + slots
     head_dim = width // HEADS
@@ -213,7 +329,11 @@
     kvt_ref[:, virt_at:] = own_kvt_ref[:, row_count:]
     extt_ref[:, tile:near] = featt_ref[:, :row_count]
     extt_ref[:, virt_at:] = featt_ref[:, row_count:]
-    for rows, source_ref in ((slice(0, tile), halo_ref), (slice(near, virt_at), arrived_ref)):
+    slot_ref[:per_peer] = piece_refs[0][...]
+    slot_ref[per_peer : 2 * per_peer] = piece_refs[1][:per_peer]
+    for at, piece_ref in enumerate(piece_refs[2:], 1):
+        slot_ref[2 * at * per_peer : (2 * at + 2) * per_peer] = piece_ref[...]
+    for rows, source_ref in ((slice(0, tile), halo_ref), (slice(near, virt_at), slot_ref)):
         extt_ref[:, rows] = source_ref[...].T
         kv_ref[rows] = rounded(f32_dot(source_ref[...], wkv_ref[...]))
         kvt_ref[:, rows] = kv_ref[rows].T
@@ -291,8 +411,10 @@
     own = by_feature[:, tile:near] + f32_dot(wq_ref[...], gqt_ref[...])
     gf_ref[...] = own.T
     halo_feat_ref[...] = rounded(by_feature[:, :tile].T)
-    slot_feat_ref[...] = rounded(by_feature[:, near:virt_at].T)
-    virt_feat = by_feature[:, virt_at:].T * factor
+    slot_feat = rounded(by_feature[:, near:virt_at].T)
+    for at, out_ref in enumerate(slot_feat_refs):
+        out_ref[...] = slot_feat[at * per_peer : (at + 1) * per_peer]
+    rider_ref[...] = by_feature[:, virt_at:].T * factor
 
     sums = (
         times_transposed(extt_ref[:, tile:near], gqt_ref[...]),
@@ -300,80 +422,59 @@
         times_transposed(extt_ref[...], gkvt_ref[width:]),
         f32_dot(ot_ref[...], og_ref[...]),
     )
-    pieces = keep_ref.shape[0]
-    columns = width // LANES
-
-    def write(half, piece_ref, cast):
-        rest = piece_ref.shape[1] - columns * rows_per_piece
+    pieces = keep_ref.shape[0] // rows_per_piece
+    held = place_ref[1] % pieces
+
+    def write(half, out_ref, cast):
         for piece in range(pieces):
             start = (half * pieces + piece) * rows_per_piece
             value = sums[start // width][start % width : start % width + rows_per_piece] * factor
-            for at in range(columns):
-                rows = slice(at * rows_per_piece, (at + 1) * rows_per_piece)
-                piece_ref[piece, rows] = cast(value[:, at * LANES : (at + 1) * LANES])
-            rider = half * pieces + piece
-            padding = jnp.zeros((rest, LANES), jnp.float32)
-            if rider < virt_rows * columns:
-                row, at = rider // columns, rider % columns
-                padding = jnp.broadcast_to(
-                    virt_feat[row : row + 1, at * LANES : (at + 1) * LANES], (rest, LANES)
-                )
-            piece_ref[piece, columns * rows_per_piece :] = cast(padding)
-
-    for core in range(2):
-
-        @pl.when(core_ref[0] == core)
+            offset = pl.multiple_of((piece ^ held) * rows_per_piece, ROW_PACK)
+            out_ref[pl.ds(offset, rows_per_piece), :] = cast(value)
+
+    for half in range(2):
+
+        @pl.when(place_ref[1] // pieces == half)
         def _():
-            write(core, keep_ref, lambda value: value)
-            write(1 - core, send_ref, rounded)
-
-
-def place_kernel(rows_per_piece, core_ref, near_ref, far_ref, gq_ref, gkv_ref, go_ref, gvirt_ref):
+            write(half, keep_ref, lambda value: value)
+            write(1 - half, send_ref, rounded)
+
+    send_ref[keep_ref.shape[0] :] = rounded(rider_ref[...])
+
+
+def place_kernel(rows_per_piece, place_ref, *refs):
+    part_refs, (gq_ref, gkv_ref, go_ref, all_ref) = refs[:-4], refs[-4:]
     width = gq_ref.shape[0]
-    pieces = near_ref.shape[0]
-    columns = width // LANES
-
-    def write(half, piece_ref):
-        for piece in range(pieces):
-            start = (half * pieces + piece) * rows_per_piece
-            which, row = start // width, start % width
-            rows = slice(row, row + rows_per_piece)
-            for at in range(columns):
-                lanes = slice(at * LANES, (at + 1) * LANES)
-                value = piece_ref[piece, at * rows_per_piece : (at + 1) * rows_per_piece]
-                value = value.astype(jnp.float32)
-                if which == 0:
-                    gq_ref[rows, lanes] = value
-                elif which == 3:
-                    go_ref[rows, lanes] = value
-                else:
-                    shift = (which - 1) * width
-                    gkv_ref[rows, slice(lanes.start + shift, lanes.stop + shift)] = value
-            rider = half * pieces + piece
-            if rider < gvirt_ref.shape[0] * columns:
-                row, at = rider // columns, rider % columns
-                rest = piece_ref[piece, columns * rows_per_piece :].astype(jnp.float32)
-                gvirt_ref[row : row + 1, at * LANES : (at + 1) * LANES] = rest[:1]
-
-    for core in range(2):
-
-        @pl.when(core_ref[0] == core)
-        def _():
-            write(core, near_ref)
-            write(1 - core, far_ref)
-
-
-def return_kernel(gf_ref, halo_ref, send_ref, returned_ref, out_ref):
+    rows = part_refs[0].shape[0]
+    for at, part_ref in enumerate(part_refs):
+        all_ref[at * rows : (at + 1) * rows] = part_ref[...]
+    for at in range(all_ref.shape[0] // rows_per_piece):
+        offset = pl.multiple_of((place_ref[1] ^ at) * rows_per_piece, ROW_PACK)
+        value = all_ref[pl.ds(offset, rows_per_piece), :].astype(jnp.float32)
+        start = at * rows_per_piece
+        rows = slice(start % width, start % width + rows_per_piece)
+        which = start // width
+        if which == 0:
+            gq_ref[rows] = value
+        elif which == 3:
+            go_ref[rows] = value
+        else:
+            gkv_ref[rows, (which - 1) * width : which * width] = value
+
+
+def return_kernel(place_ref, gf_ref, halo_ref, send_ref, *refs):
+    piece_refs, out_ref = refs[:-1], refs[-1]
     row_count = gf_ref.shape[0]
     tile = halo_ref.shape[0]
-    chosen = listed_rows(send_ref, row_count)
-    total = gf_ref[...] + rows_contracted(chosen, returned_ref[...])
+    chosen = listed_rows(place_ref[0], send_ref, row_count)
+    returned = jnp.concatenate([ref[...] for ref in piece_refs], axis=0)
+    total = gf_ref[...] + rows_contracted(chosen, returned)
     out_ref[: row_count - tile] = total[: row_count - tile]
     out_ref[row_count - tile :] = total[row_count - tile :] + halo_ref[...].astype(jnp.float32)
 
 
-def call(kernel, name, outs, args, scratch=(), fetched=0, scalars=0, flops=0):
-    spaces = [pltpu.SMEM] * scalars + [pl.ANY] * fetched
+def call(kernel, name, outs, args, scratch=(), fetched=0, flops=0):
+    spaces = [pltpu.SMEM] + [pltpu.HBM] * fetched
     spaces += [pltpu.VMEM] * (len(args) - len(spaces))
     moved = sum(x.size * x.dtype.itemsize for x in list(args) + list(outs))
     scratch = list(scratch)
@@ -398,26 +499,31 @@
     virt_rows = virtual.shape[0]
     padded = ROW_PACK * -(-virt_rows // ROW_PACK)
     ext_rows = TILE + row_count + slots + padded
-    chips = math.prod(lax.axis_size(axis) for axis in CHIPS)
-    rows_per_piece = 2 * width // chips
-    piece_rows = width // LANES * rows_per_piece + 1
-    piece_rows = ROW_PACK * -(-piece_rows // ROW_PACK)
+    nodes = row_count * lax.axis_size("dom") * lax.axis_size("rows")
+    stages = exchange_stages(lax.axis_size("dom"), lax.axis_size("rows"))
+    scattered = scattered_stages(stages, 4 * width)
+    rows_per_piece = 4 * width >> sum(len(stage) for stage in scattered)
+    place = jnp.stack([lax.axis_index("dom").astype(jnp.int32), own_piece(scattered)])
     bf16, f32 = jnp.bfloat16, jnp.float32
     shape = jax.ShapeDtypeStruct
-    core = lax.axis_index(CORE).astype(jnp.int32).reshape(1)
-
-    sent, halo = call(
+
+    halo, through, *direct = call(
         pick_kernel,
         "pick_rows",
-        [shape((slots, width), bf16), shape((TILE, width), bf16)],
-        [features, send_rows],
+        [shape((TILE, width), bf16), shape((slots // 2, width), bf16)]
+        + [shape((per_peer, width), bf16)] * (dom_size // 2),
+        [place, features, send_rows],
         [pltpu.VMEM(features.shape, bf16), pltpu.VMEM(send_rows.shape, jnp.int32)],
         fetched=2,
     )
-    arrived = exchanged(sent, DOM)
-    halo = shifted(halo, ROWS, 1)
+    through = swapped(through, 1, 0)
+    halo = shifted(halo, "rows", 1)
+    arrived = [direct[0], through]
+    for at in range(1, dom_size // 2):
+        handed_on = through[at * per_peer : (at + 1) * per_peer]
+        arrived.append(swapped(jnp.concatenate([direct[at], handed_on], axis=0), 2 * at, 0))
     prepared = call(
-        prepare_kernel,
+        functools.partial(prepare_kernel, per_peer),
         "prepare",
         [
             shape(out_grad.shape, bf16),
@@ -431,7 +537,7 @@
             shape((2 * TILE, row_count), f32),
             shape((slots + padded, row_count), f32),
         ],
-        [features, out_grad, w_query, w_keyval, w_out, virtual, local_nbr.T, expander.T],
+        [place, features, out_grad, w_query, w_keyval, w_out, virtual, local_nbr.T, expander.T],
         [
             pltpu.VMEM(features.shape, bf16),
             pltpu.VMEM(w_out.shape, bf16),
@@ -442,20 +548,20 @@
         fetched=8,
         flops=10 * row_count * width * width,
     )
-    own_feat, halo_feat, slot_feat, keep, message = call(
-        functools.partial(
-            attend_kernel, rows_per_piece, (row_count * dom_size * lax.axis_size(CORE) * lax.axis_size(ROWS[0])) ** -0.5, virt_rows
-        ),
+    own_feat, halo_feat, *results = call(
+        functools.partial(attend_kernel, rows_per_piece, nodes**-0.5, per_peer, dom_size),
         "attend",
         [
             shape((row_count, width), f32),
             shape((TILE, width), bf16),
-            shape((slots, width), bf16),
-            shape((chips, piece_rows, LANES), f32),
-            shape((chips, piece_rows, LANES), bf16),
+            *[shape((per_peer, width), bf16)] * dom_size,
+            shape((2 * width, width), f32),
+            shape((2 * width + padded, width), bf16),
+            shape((padded, width), f32),
         ],
-        [core, halo, arrived, *prepared],
+        [place, halo, *arrived, *prepared],
         [
+            pltpu.VMEM((slots, width), bf16),
             pltpu.VMEM((ext_rows, 2 * width), bf16),
             pltpu.VMEM((2 * width, ext_rows), bf16),
             pltpu.VMEM((width, ext_rows), bf16),
@@ -463,48 +569,46 @@
             pltpu.VMEM((2 * width, ext_rows), bf16),
             pltpu.VMEM((width, row_count), bf16),
         ],
-        scalars=1,
         flops=32 * ext_rows * width * width,
     )
-
-    both = rounded(keep + swapped(message, CORE).astype(f32))
-    parts = exchanged(both, CHIPS)
-    slots_back = exchanged(slot_feat, DOM)
-    halo_back = shifted(halo_feat, ROWS, -1)
+    slot_feat, (keep, message, rider) = results[:dom_size], results[dom_size:]
+
+    near, far, rider, returned = summed_everywhere(
+        keep, message, rider, stages, scattered, slot_feat
+    )
+    halo_back = shifted(halo_feat, "rows", -1)
     (grad_features,) = call(
         return_kernel,
         "return_rows",
         [shape((row_count, width), f32)],
-        [own_feat, halo_back, send_rows, slots_back],
-    )
-    summed = rounded(jnp.sum(parts.astype(f32), axis=0))
-    near = exchanged(jnp.broadcast_to(summed, parts.shape), CHIPS)
-    grad_wq, grad_wkv, grad_wo, grad_virtual = call(
+        [place, own_feat, halo_back, send_rows, *returned],
+    )
+    grad_wq, grad_wkv, grad_wo = call(
         functools.partial(place_kernel, rows_per_piece),
         "place_sums",
-        [
-            shape((width, width), f32),
-            shape((width, 2 * width), f32),
-            shape((width, width), f32),
-            shape((virt_rows, width), f32),
-        ],
-        [core, near, swapped(near, CORE)],
-        scalars=1,
-    )
-    return grad_features, grad_wq, grad_wkv, grad_wo, grad_virtual
+        [shape((width, width), f32), shape((width, 2 * width), f32), shape((width, width), f32)],
+        [place, *near, *far],
+        [pltpu.VMEM((4 * width, width), bf16)],
+    )
+    return grad_features, grad_wq, grad_wkv, grad_wo, rider[:virt_rows]
 
 
 def solution(mesh):
-    dom_size, rows_size = mesh.shape["dom"], mesh.shape["rows"]
-    split = jax.sharding.Mesh(
-        mesh.devices.reshape(dom_size, rows_size // 2, 2), (*DOM, *ROWS)
-    )
-    nodes = P((*DOM, *ROWS), None)
-    placed = (nodes, nodes, P(), P(), P(), P(), nodes, nodes, nodes)
+    placed = (
+        P(("dom", "rows"), None),
+        P(("dom", "rows"), None),
+        P(),
+        P(),
+        P(),
+        P(),
+        P(("dom", "rows"), None),
+        P(("dom", "rows"), None),
+        P(("dom", "rows"), None),
+    )
     return jax.shard_map(
         shards,
-        mesh=split,
+        mesh=mesh,
         in_specs=placed,
-        out_specs=(nodes, P(), P(), P(), P()),
+        out_specs=(P(("dom", "rows"), None), P(), P(), P(), P()),
         check_vma=False,
     )

time: 105 us -> 81.8 us (0.78)
  blocking collectives: 46.4 us -> 0 us
  waiting for transfers between devices: 9.83 us -> 28.5 us
  starting transfers between devices: 13 us -> 26.2 us
  local copies, waits for them, and re-layouts: 18.3 us -> 7.77 us
  Pallas kernels: 15.2 us -> 17 us
    all_to_all x2 -> x0, blocking collectives: 46.4 us -> none  [exchanged(): return lax.all_to_all(blocks, axes, split_axis=0, concat_axis=0, tiled=True)]
    ppermute x4 -> x23, waiting for transfers between devices: 3.94 us -> 28.5 us  [the longest x21 24.4 us: swapped(): return lax.ppermute(block, ('dom', 'rows'), route)]
    ppermute x4 -> x23, starting transfers between devices: 2.35 us -> 26.2 us  [the longest x21 26.1 us: swapped(): return lax.ppermute(block, ('dom', 'rows'), route)]
    all_to_all x2 -> x0, starting transfers between devices: 10.7 us -> none  [exchanged(): return lax.all_to_all(blocks, axes, split_axis=0, concat_axis=0, tiled=True)]
    unnamed x50 -> x23, local copies, waits for them, and re-layouts: 18.2 us -> 7.65 us
    all_to_all x2 -> x0, waiting for transfers between devices: 5.89 us -> none  [exchanged(): return lax.all_to_all(blocks, axes, split_axis=0, concat_axis=0, tiled=True)]
    pallas_call x5, Pallas kernels: 15.2 us -> 17 us  [call(): pl.pallas_call(kernel, out_shape=outs, in_specs=[pl.BlockSpec(memory_spac...]
  transfers between devices with their start and end apart: 6 -> 23, of which waited for: 3 -> 12; matrix products, arithmetic and copies ran while one was open for 0% -> 1% of each run, Pallas kernels for 4% -> 7%
where the time goes in v4:
time: 81.8 us; the launch traced here: 81.4 us
  waiting for transfers between devices  28.5 us (35%)
  starting transfers between devices  26.2 us (32%)
  Pallas kernels  17 us (21%)
  local copies, waits for them, and re-layouts  7.77 us (9%)
  other arithmetic  1.07 us (1%)
  between operations  0.9 us (1%)
    ppermute x21, starting transfers between devices, swapped(): return lax.ppermute(block, ('dom', 'rows'), route)  26.1 us
    ppermute x21, waiting for transfers between devices, swapped(): return lax.ppermute(block, ('dom', 'rows'), route)  24.4 us
    pallas_call x5, Pallas kernels, call(): pl.pallas_call(kernel, out_shape=outs, in_specs=[pl.BlockSpec(memory_spac...  17 us
    unnamed x23, local copies, waits for them, and re-layouts  7.65 us
    ppermute x2, waiting for transfers between devices, shifted(): return lax.ppermute(block, axis, route)  4.13 us
  transfers between devices with their start and end apart: 23, of which 12 were waited for; matrix products, arithmetic and copies ran while one was open for 1% of the time, Pallas kernels for 7%

profile of v4, /device:TPU:0, one launch (start us, length us, event | category | flops | bytes accessed | tf_op | source)
XLA Modules:
  0.0 81.4 jit_solution(18435568584749533170)
XLA Ops:
  0.7 0.1 pad_add_fusion.place_ref
  0.7 0.9 %copy-done = bf16[256,384]{1,0:T(8,128)(2,1)S(1)} copy-done((bf16[256,384]{1,0:T(8,128)(2,1)S(1)}, bf16[256,384]{1,0:T(8,128)(2,1)}, u32[]{:S(2)}) %copy-start) | copy-done | bytes 196632
  1.7 0.7 copy-done.6
  2.3 1.3 %pick_rows.1 = (bf16[128,384]{1,0:T(8,128)(2,1)S(1)}, bf16[128,384]{1,0:T(8,128)(2,1)S(1)}, bf16[32,384]{1,0:T(8,128)(2,1)S(1)}, bf16[32,384]{1,0:T(8,128)(2,1)S...) custom-call(s32[2]{0:T(128)S(1)} %pad_add_fusion.place_ref, bf16[256,384]{1,0:T(8,128)(2,1)S(1)} %copy-done, ...), custom_call_target="tpu_custom_call" | custom-call | bytes 492552 | tf_op jit(solution)/shard_map/pick_rows/pallas_call | solution.py:483
  3.7 3.0 %collective-permute-start.1 = (bf16[128,384]{1,0:T(8,128)(2,1)S(1)}, bf16[128,384]{1,0:T(8,128)(2,1)S(1)}, u32[]{:S(2)}, u32[]{:S(2)}) collective-permute-start(bf16[128,384]{1,0:T(8,128)(2,1)S(1)} %get-tuple-element.39), channel_id=1, source_target_pairs={{0,4},{1,5},{2,6},{3,7},{4,0},{5,1},{6,2},{7,3},{8,12},{9,13},{10,... | collective-permute-start | bytes 294920 | tf_op jit(solution)/shard_map/ppermute | solution.py:87
  6.7 2.8 %collective-permute-done.1.refs_1_ = bf16[128,384]{1,0:T(8,128)(2,1)S(1)} collective-permute-done((bf16[128,384]{1,0:T(8,128)(2,1)S(1)}, bf16[128,384]{1,0:T(8,128)(2,1)S(1)}, u32[]{:S(2)}, u32[]{:S(2)}) %collective-permute-start.1) | collective-permute-done | bytes 98336 | tf_op jit(solution)/shard_map/ppermute | solution.py:87
  9.5 2.0 %collective-permute-start.2 = (bf16[64,384]{1,0:T(8,128)(2,1)S(1)}, bf16[64,384]{1,0:T(8,128)(2,1)S(1)}, u32[]{:S(2)}, u32[]{:S(2)}) collective-permute-start(bf16[64,384]{1,0:T(8,128)(2,1)S(1)} %pad_maximum_fusion.6), channel_id=1, source_target_pairs={{0,8},{1,9},{2,10},{3,11},{4,12},{5,13},{6,14},{7,15},{8,0},{9,1},... | collective-permute-start | bytes 147464 | tf_op jit(solution)/shard_map/ppermute | solution.py:87
  11.5 2.6 %collective-permute-start.3 = (bf16[64,384]{1,0:T(8,128)(2,1)S(1)}, bf16[64,384]{1,0:T(8,128)(2,1)S(1)}, u32[]{:S(2)}, u32[]{:S(2)}) collective-permute-start(bf16[64,384]{1,0:T(8,128)(2,1)S(1)} %pad_maximum_fusion.7), channel_id=1, source_target_pairs={{0,16},{1,17},{2,18},{3,19},{4,20},{5,21},{6,22},{7,23},{8,24},{9,... | collective-permute-start | bytes 147464 | tf_op jit(solution)/shard_map/ppermute | solution.py:87
  14.1 0.0 copy-start.1
  14.1 1.1 %copy-done.1 = bf16[384,768]{1,0:T(8,128)(2,1)S(1)} copy-done((bf16[384,768]{1,0:T(8,128)(2,1)S(1)}, bf16[384,768]{1,0:T(8,128)(2,1)}, u32[]{:S(2)}) %copy-start.1) | copy-done | bytes 589848
  15.2 1.0 %copy-done.2 = bf16[384,384]{1,0:T(8,128)(2,1)S(1)} copy-done((bf16[384,384]{1,0:T(8,128)(2,1)S(1)}, bf16[384,384]{1,0:T(8,128)(2,1)}, u32[]{:S(2)}) %copy-start.2) | copy-done | bytes 294936
  16.1 1.0 %copy-done.3 = bf16[384,384]{1,0:T(8,128)(2,1)S(1)} copy-done((bf16[384,384]{1,0:T(8,128)(2,1)S(1)}, bf16[384,384]{1,0:T(8,128)(2,1)}, u32[]{:S(2)}) %copy-start.3) | copy-done | bytes 294936
  17.1 0.9 %copy-done.4 = bf16[256,384]{1,0:T(8,128)(2,1)S(1)} copy-done((bf16[256,384]{1,0:T(8,128)(2,1)S(1)}, bf16[256,384]{1,0:T(8,128)(2,1)}, u32[]{:S(2)}) %copy-start.4) | copy-done | bytes 196632
  18.0 0.7 copy-done.5
  18.7 0.7 copy-done.8
  19.4 0.7 copy-done.9
  20.1 3.6 %prepare.1 = (bf16[256,384]{1,0:T(8,128)(2,1)S(1)}, bf16[384,384]{1,0:T(8,128)(2,1)S(1)}, bf16[384,768]{1,0:T(8,128)(2,1)S(1)}, bf16[384,272]{1,0:T(8,128)(2,1)S...) custom-call(s32[2]{0:T(128)S(1)} %pad_add_fusion.place_ref, ...), custom_call_target="tpu_custom_call" | custom-call | flops 377487360 | bytes 4656136 | tf_op jit(solution)/shard_map/prepare/pallas_call | solution.py:483
  23.7 8.1 %attend.1 = (f32[256,384]{1,0:T(8,128)S(1)}, bf16[128,384]{1,0:T(8,128)(2,1)S(1)}, bf16[32,384]{1,0:T(8,128)(2,1)S(1)}, bf16[32,384]{1,0:T(8,128)(2,1)S(1)}, bf1...) custom-call(s32[2]{0:T(128)S(1)} %pad_add_fusion.place_ref, ...), custom_call_target="tpu_custom_call" | custom-call | flops 3095396352 | bytes 5922824 | tf_op jit(solution)/shard_map/attend/pallas_call | solution.py:483
  31.9 0.1 collective-permute-start.6
  32.0 2.0 %collective-permute-done.6 = bf16[784,384]{1,0:T(8,128)(2,1)S(1)} collective-permute-done((bf16[784,384]{1,0:T(8,128)(2,1)S(1)}, bf16[784,384]{1,0:T(8,128)(2,1)S(1)}, u32[]{:S(2)}, u32[]{:S(2)}) %collective-permute-start.6) | collective-permute-done | bytes 602144 | tf_op jit(solution)/shard_map/ppermute | solution.py:87
  34.0 0.2 fusion.11
  34.3 1.8 %collective-permute-start.7 = (bf16[336,384]{1,0:T(8,128)(2,1)S(1)}, bf16[336,384]{1,0:T(8,128)(2,1)S(1)}, u32[]{:S(2)}, u32[]{:S(2)}) collective-permute-start(bf16[336,384]{1,0:T(8,128)(2,1)S(1)} %constant_dynamic-update-slice_fusion), channel_id=1, source_target_pairs={{0,4},{1,5},{2,6},{3,7},{4,0},{5,1},{6,2},{7,3},{8,12},{9,13},{10,... | collective-permute-start | bytes 774152 | tf_op jit(solution)/shard_map/ppermute | solution.py:87
  36.1 1.6 %collective-permute-start.8 = (bf16[208,384]{1,0:T(8,128)(2,1)S(1)}, bf16[208,384]{1,0:T(8,128)(2,1)S(1)}, u32[]{:S(2)}, u32[]{:S(2)}) collective-permute-start(bf16[208,384]{1,0:T(8,128)(2,1)S(1)} %get-tuple-element.91), channel_id=1, source_target_pairs={{0,2},{1,3},{2,0},{3,1},{4,6},{5,7},{6,4},{7,5},{8,10},{9,11},{10,... | collective-permute-start | bytes 479240 | tf_op jit(solution)/shard_map/ppermute | solution.py:87
  37.7 0.3 collective-permute-start.9
  37.9 4.1 %collective-permute-done.8 = bf16[208,384]{1,0:T(8,128)(2,1)S(1)} collective-permute-done((bf16[208,384]{1,0:T(8,128)(2,1)S(1)}, bf16[208,384]{1,0:T(8,128)(2,1)S(1)}, u32[]{:S(2)}, u32[]{:S(2)}) %collective-permute-start.8) | collective-permute-done | bytes 159776 | tf_op jit(solution)/shard_map/ppermute | solution.py:87
  42.0 5.2 %collective-permute-done.9 = bf16[208,384]{1,0:T(8,128)(2,1)S(1)} collective-permute-done((bf16[208,384]{1,0:T(8,128)(2,1)S(1)}, bf16[208,384]{1,0:T(8,128)(2,1)S(1)}, u32[]{:S(2)}, u32[]{:S(2)}) %collective-permute-start.9) | collective-permute-done | bytes 159776 | tf_op jit(solution)/shard_map/ppermute | solution.py:87
  47.2 0.1 fusion.9
  47.4 3.7 %collective-permute-start.12 = (bf16[128,384]{1,0:T(8,128)(2,1)S(1)}, bf16[128,384]{1,0:T(8,128)(2,1)S(1)}, u32[]{:S(2)}, u32[]{:S(2)}) collective-permute-start(bf16[128,384]{1,0:T(8,128)(2,1)S(1)} %get-tuple-element.88), channel_id=1, source_target_pairs={{0,24},{1,25},{2,26},{3,27},{4,28},{5,29},{6,30},{7,31},{8,16},{9,... | collective-permute-start | bytes 294920 | tf_op jit(solution)/shard_map/ppermute | solution.py:87
  51.1 0.8 collective-permute-start.10
  51.9 2.7 %collective-permute-done.12 = bf16[128,384]{1,0:T(8,128)(2,1)S(1)} collective-permute-done((bf16[128,384]{1,0:T(8,128)(2,1)S(1)}, bf16[128,384]{1,0:T(8,128)(2,1)S(1)}, u32[]{:S(2)}, u32[]{:S(2)}) %collective-permute-start.12) | collective-permute-done | bytes 98336 | tf_op jit(solution)/shard_map/ppermute | solution.py:87
  54.6 3.9 %collective-permute-done.11 = bf16[128,384]{1,0:T(8,128)(2,1)S(1)} collective-permute-done((bf16[128,384]{1,0:T(8,128)(2,1)S(1)}, bf16[128,384]{1,0:T(8,128)(2,1)S(1)}, u32[]{:S(2)}, u32[]{:S(2)}) %collective-permute-start.11) | collective-permute-done | bytes 98336 | tf_op jit(solution)/shard_map/ppermute | solution.py:87
  58.5 2.5 %collective-permute-start.15 = (bf16[48,384]{1,0:T(8,128)(2,1)S(1)}, bf16[48,384]{1,0:T(8,128)(2,1)S(1)}, u32[]{:S(2)}, u32[]{:S(2)}) collective-permute-start(bf16[48,384]{1,0:T(8,128)(2,1)S(1)} %fusion.8), channel_id=1, source_target_pairs={{0,24},{1,25},{2,26},{3,27},{4,28},{5,29},{6,30},{7,31},{8,16},{9,... | collective-permute-start | bytes 110600 | tf_op jit(solution)/shard_map/ppermute | solution.py:87
  61.1 1.9 %collective-permute-start.13 = (bf16[48,384]{1,0:T(8,128)(2,1)S(1)}, bf16[48,384]{1,0:T(8,128)(2,1)S(1)}, u32[]{:S(2)}, u32[]{:S(2)}) collective-permute-start(bf16[48,384]{1,0:T(8,128)(2,1)S(1)} %fusion.8), channel_id=1, source_target_pairs={{0,8},{1,9},{2,10},{3,11},{4,12},{5,13},{6,14},{7,15},{8,0},{9,1},... | collective-permute-start | bytes 110600 | tf_op jit(solution)/shard_map/ppermute | solution.py:87
  63.0 1.5 %collective-permute-done.15 = bf16[48,384]{1,0:T(8,128)(2,1)S(1)} collective-permute-done((bf16[48,384]{1,0:T(8,128)(2,1)S(1)}, bf16[48,384]{1,0:T(8,128)(2,1)S(1)}, u32[]{:S(2)}, u32[]{:S(2)}) %collective-permute-start.15) | collective-permute-done | bytes 36896 | tf_op jit(solution)/shard_map/ppermute | solution.py:87
  64.5 1.5 %collective-permute-done.14 = bf16[48,384]{1,0:T(8,128)(2,1)S(1)} collective-permute-done((bf16[48,384]{1,0:T(8,128)(2,1)S(1)}, bf16[48,384]{1,0:T(8,128)(2,1)S(1)}, u32[]{:S(2)}, u32[]{:S(2)}) %collective-permute-start.14) | collective-permute-done | bytes 36896 | tf_op jit(solution)/shard_map/ppermute | solution.py:87
  66.0 1.5 %collective-permute-start.18 = (bf16[192,384]{1,0:T(8,128)(2,1)S(1)}, bf16[192,384]{1,0:T(8,128)(2,1)S(1)}, u32[]{:S(2)}, u32[]{:S(2)}) collective-permute-start(bf16[192,384]{1,0:T(8,128)(2,1)S(1)} %pad_maximum_fusion.5.refs_0_), channel_id=1, source_target_pairs={{0,6},{1,7},{2,4},{3,5},{4,2},{5,3},{6,0},{7,1},{8,14},{9,15},{10,... | collective-permute-start | bytes 442376 | tf_op jit(solution)/shard_map/ppermute | solution.py:87
  67.5 0.5 collective-permute-start.17
  68.0 1.5 %collective-permute-start.16 = (bf16[192,384]{1,0:T(8,128)(2,1)S(1)}, bf16[192,384]{1,0:T(8,128)(2,1)S(1)}, u32[]{:S(2)}, u32[]{:S(2)}) collective-permute-start(bf16[192,384]{1,0:T(8,128)(2,1)S(1)} %pad_maximum_fusion.5.refs_0_), channel_id=1, source_target_pairs={{0,2},{1,3},{2,0},{3,1},{4,6},{5,7},{6,4},{7,5},{8,10},{9,11},{10,... | collective-permute-start | bytes 442376 | tf_op jit(solution)/shard_map/ppermute | solution.py:87
  69.6 4.1 %collective-permute-done.5.halo_ref = bf16[128,384]{1,0:T(8,128)(2,1)S(1)} collective-permute-done((bf16[128,384]{1,0:T(8,128)(2,1)S(1)}, bf16[128,384]{1,0:T(8,128)(2,1)S(1)}, u32[]{:S(2)}, u32[]{:S(2)}) %collective-permute-start.5) | collective-permute-done | bytes 98336 | tf_op jit(solution)/shard_map/ppermute | solution.py:93
  73.7 1.8 %return_rows.1 = f32[256,384]{1,0:T(8,128)} custom-call(s32[2]{0:T(128)S(1)} %pad_add_fusion.place_ref, f32[256,384]{1,0:T(8,128)S(1)} %get-tuple-element.53.gf_ref, bf16[128,384]{1,0:T(8,128)(2,1)S(1)} %collective-permute-done.5.halo_ref, s32[8,32]{1,0:T(8,128)S(1)} %copy-done.7, bf16[32,384]{1,0:T(8,128)(2,1)S(1)} %get-tuple-element.55.refs_0_, ...), custom_call_target="tpu_custom_call" | custom-call | bytes 1082376 | tf_op jit(solution)/shard_map/return_rows/pallas_call | solution.py:483
  75.5 1.8 %collective-permute-start.19 = (bf16[192,384]{1,0:T(8,128)(2,1)S(1)}, bf16[192,384]{1,0:T(8,128)(2,1)S(1)}, u32[]{:S(2)}, u32[]{:S(2)}) collective-permute-start(bf16[192,384]{1,0:T(8,128)(2,1)S(1)} %pad_maximum_fusion.5.refs_0_), channel_id=1, source_target_pairs={{0,1},{1,0},{2,3},{3,2},{4,5},{5,4},{6,7},{7,6},{8,9},{9,8},{10,11... | collective-permute-start | bytes 442376 | tf_op jit(solution)/shard_map/ppermute | solution.py:87
  77.4 0.5 collective-permute-start.21
  77.9 0.1 collective-permute-start.20
  78.0 0.6 add_add_fusion
  78.6 0.2 collective-permute-done.22.refs_7_
  78.7 0.2 collective-permute-done.21.refs_6_
  79.0 0.3 collective-permute-done.20.refs_5_
  79.3 2.1 %place_sums.1 = (f32[384,384]{1,0:T(8,128)}, f32[384,768]{1,0:T(8,128)}, f32[384,384]{1,0:T(8,128)}) custom-call(s32[2]{0:T(128)S(1)} %pad_add_fusion.place_ref, bf16[192,384]{1,0:T(8,128)(2,1)S(1)} %pad_maximum_fusion.5.refs_0_, bf16[192,384]{1,0:T(8,128)(2,1)S(1)} %collective-permute-done.16.refs_1_, bf16[192,384]{1,0:T(8,128)(2,1)S(1)} %collective-permute-done.17.refs_2_, ...), custom_call_target="tpu_custom_call" | custom-call | bytes 3538952 | tf_op jit(solution)/shard_map/place_sums/pallas_call | solution.py:483
  (50 shorter events, 0.4 us)
Async XLA Ops:
  0.7 0.9 %copy-start = (bf16[256,384]{1,0:T(8,128)(2,1)S(1)}, bf16[256,384]{1,0:T(8,128)(2,1)}, u32[]{:S(2)}) copy-start(bf16[256,384]{1,0:T(8,128)(2,1)} %feat_hbm.3) | copy-start | bytes 589828
  1.7 0.7 copy-start.6
  3.7 5.8 %collective-permute-start.1 = (bf16[128,384]{1,0:T(8,128)(2,1)S(1)}, bf16[128,384]{1,0:T(8,128)(2,1)S(1)}, u32[]{:S(2)}, u32[]{:S(2)}) collective-permute-start(bf16[128,384]{1,0:T(8,128)(2,1)S(1)} %get-tuple-element.39), channel_id=1, source_target_pairs={{0,4},{1,5},{2,6},{3,7},{4,0},{5,1},{6,2},{7,3},{8,12},{9,13},{10,... | collective-permute-start | bytes 294920 | tf_op jit(solution)/shard_map/ppermute | solution.py:87
  6.7 17.0 %collective-permute-start = (bf16[128,384]{1,0:T(8,128)(2,1)S(1)}, bf16[128,384]{1,0:T(8,128)(2,1)S(1)}, u32[]{:S(2)}, u32[]{:S(2)}) collective-permute-start(bf16[128,384]{1,0:T(8,128)(2,1)S(1)} %get-tuple-element.37), channel_id=1, source_target_pairs={{3,0},{0,1},{1,2},{2,3},{7,4},{4,5},{5,6},{6,7},{11,8},{8,9},{9,10... | collective-permute-start | bytes 294920 | tf_op jit(solution)/shard_map/ppermute | solution.py:93
  9.5 14.2 %collective-permute-start.2 = (bf16[64,384]{1,0:T(8,128)(2,1)S(1)}, bf16[64,384]{1,0:T(8,128)(2,1)S(1)}, u32[]{:S(2)}, u32[]{:S(2)}) collective-permute-start(bf16[64,384]{1,0:T(8,128)(2,1)S(1)} %pad_maximum_fusion.6), channel_id=1, source_target_pairs={{0,8},{1,9},{2,10},{3,11},{4,12},{5,13},{6,14},{7,15},{8,0},{9,1},... | collective-permute-start | bytes 147464 | tf_op jit(solution)/shard_map/ppermute | solution.py:87
  11.5 12.2 %collective-permute-start.3 = (bf16[64,384]{1,0:T(8,128)(2,1)S(1)}, bf16[64,384]{1,0:T(8,128)(2,1)S(1)}, u32[]{:S(2)}, u32[]{:S(2)}) collective-permute-start(bf16[64,384]{1,0:T(8,128)(2,1)S(1)} %pad_maximum_fusion.7), channel_id=1, source_target_pairs={{0,16},{1,17},{2,18},{3,19},{4,20},{5,21},{6,22},{7,23},{8,24},{9,... | collective-permute-start | bytes 147464 | tf_op jit(solution)/shard_map/ppermute | solution.py:87
  14.1 9.7 %collective-permute-start.4 = (bf16[64,384]{1,0:T(8,128)(2,1)S(1)}, bf16[64,384]{1,0:T(8,128)(2,1)S(1)}, u32[]{:S(2)}, u32[]{:S(2)}) collective-permute-start(bf16[64,384]{1,0:T(8,128)(2,1)S(1)} %pad_maximum_fusion.8), channel_id=1, source_target_pairs={{0,24},{1,25},{2,26},{3,27},{4,28},{5,29},{6,30},{7,31},{8,16},{9,... | collective-permute-start | bytes 147464 | tf_op jit(solution)/shard_map/ppermute | solution.py:87
  14.1 1.1 %copy-start.1 = (bf16[384,768]{1,0:T(8,128)(2,1)S(1)}, bf16[384,768]{1,0:T(8,128)(2,1)}, u32[]{:S(2)}) copy-start(bf16[384,768]{1,0:T(8,128)(2,1)} %wkv_hbm.1) | copy-start | bytes 1769476
  15.2 1.0 %copy-start.2 = (bf16[384,384]{1,0:T(8,128)(2,1)S(1)}, bf16[384,384]{1,0:T(8,128)(2,1)}, u32[]{:S(2)}) copy-start(bf16[384,384]{1,0:T(8,128)(2,1)} %wq_hbm.1) | copy-start | bytes 884740
  16.1 1.0 %copy-start.3 = (bf16[384,384]{1,0:T(8,128)(2,1)S(1)}, bf16[384,384]{1,0:T(8,128)(2,1)}, u32[]{:S(2)}) copy-start(bf16[384,384]{1,0:T(8,128)(2,1)} %wo_hbm.1) | copy-start | bytes 884740
  17.1 0.9 %copy-start.4 = (bf16[256,384]{1,0:T(8,128)(2,1)S(1)}, bf16[256,384]{1,0:T(8,128)(2,1)}, u32[]{:S(2)}) copy-start(bf16[256,384]{1,0:T(8,128)(2,1)} %og_hbm.1) | copy-start | bytes 589828
  18.0 0.7 copy-start.5
  18.7 0.7 copy-start.8
  19.4 0.7 copy-start.9
  31.9 2.1 %collective-permute-start.6 = (bf16[784,384]{1,0:T(8,128)(2,1)S(1)}, bf16[784,384]{1,0:T(8,128)(2,1)S(1)}, u32[]{:S(2)}, u32[]{:S(2)}) collective-permute-start(bf16[784,384]{1,0:T(8,128)(2,1)S(1)} %get-tuple-element.57), channel_id=1, source_target_pairs={{0,1},{1,0},{2,3},{3,2},{4,5},{5,4},{6,7},{7,6},{8,9},{9,8},{10,11... | collective-permute-start | bytes 1806344 | tf_op jit(solution)/shard_map/ppermute | solution.py:87
  34.3 12.9 %collective-permute-start.7 = (bf16[336,384]{1,0:T(8,128)(2,1)S(1)}, bf16[336,384]{1,0:T(8,128)(2,1)S(1)}, u32[]{:S(2)}, u32[]{:S(2)}) collective-permute-start(bf16[336,384]{1,0:T(8,128)(2,1)S(1)} %constant_dynamic-update-slice_fusion), channel_id=1, source_target_pairs={{0,4},{1,5},{2,6},{3,7},{4,0},{5,1},{6,2},{7,3},{8,12},{9,13},{10,... | collective-permute-start | bytes 774152 | tf_op jit(solution)/shard_map/ppermute | solution.py:87
  36.1 5.9 %collective-permute-start.8 = (bf16[208,384]{1,0:T(8,128)(2,1)S(1)}, bf16[208,384]{1,0:T(8,128)(2,1)S(1)}, u32[]{:S(2)}, u32[]{:S(2)}) collective-permute-start(bf16[208,384]{1,0:T(8,128)(2,1)S(1)} %get-tuple-element.91), channel_id=1, source_target_pairs={{0,2},{1,3},{2,0},{3,1},{4,6},{5,7},{6,4},{7,5},{8,10},{9,11},{10,... | collective-permute-start | bytes 479240 | tf_op jit(solution)/shard_map/ppermute | solution.py:87
  37.7 9.5 %collective-permute-start.9 = (bf16[208,384]{1,0:T(8,128)(2,1)S(1)}, bf16[208,384]{1,0:T(8,128)(2,1)S(1)}, u32[]{:S(2)}, u32[]{:S(2)}) collective-permute-start(bf16[208,384]{1,0:T(8,128)(2,1)S(1)} %get-tuple-element.92), channel_id=1, source_target_pairs={{0,6},{1,7},{2,4},{3,5},{4,2},{5,3},{6,0},{7,1},{8,14},{9,15},{10,... | collective-permute-start | bytes 479240 | tf_op jit(solution)/shard_map/ppermute | solution.py:87
  47.3 26.4 %copy-start.7 = (s32[8,32]{1,0:T(8,128)S(1)}, s32[8,32]{1,0:T(8,128)}, u32[]{:S(2)}) copy-start(s32[8,32]{1,0:T(8,128)} %send_ref.1) | copy-start | bytes 3076
  47.4 7.2 %collective-permute-start.12 = (bf16[128,384]{1,0:T(8,128)(2,1)S(1)}, bf16[128,384]{1,0:T(8,128)(2,1)S(1)}, u32[]{:S(2)}, u32[]{:S(2)}) collective-permute-start(bf16[128,384]{1,0:T(8,128)(2,1)S(1)} %get-tuple-element.88), channel_id=1, source_target_pairs={{0,24},{1,25},{2,26},{3,27},{4,28},{5,29},{6,30},{7,31},{8,16},{9,... | collective-permute-start | bytes 294920 | tf_op jit(solution)/shard_map/ppermute | solution.py:87
  51.1 7.4 %collective-permute-start.11 = (bf16[128,384]{1,0:T(8,128)(2,1)S(1)}, bf16[128,384]{1,0:T(8,128)(2,1)S(1)}, u32[]{:S(2)}, u32[]{:S(2)}) collective-permute-start(bf16[128,384]{1,0:T(8,128)(2,1)S(1)} %get-tuple-element.89), channel_id=1, source_target_pairs={{0,16},{1,17},{2,18},{3,19},{4,20},{5,21},{6,22},{7,23},{8,24},{9,... | collective-permute-start | bytes 294920 | tf_op jit(solution)/shard_map/ppermute | solution.py:87
  51.1 7.4 %collective-permute-start.10 = (bf16[128,384]{1,0:T(8,128)(2,1)S(1)}, bf16[128,384]{1,0:T(8,128)(2,1)S(1)}, u32[]{:S(2)}, u32[]{:S(2)}) collective-permute-start(bf16[128,384]{1,0:T(8,128)(2,1)S(1)} %get-tuple-element.90), channel_id=1, source_target_pairs={{0,8},{1,9},{2,10},{3,11},{4,12},{5,13},{6,14},{7,15},{8,0},{9,1},... | collective-permute-start | bytes 294920 | tf_op jit(solution)/shard_map/ppermute | solution.py:87
  58.5 5.9 %collective-permute-start.15 = (bf16[48,384]{1,0:T(8,128)(2,1)S(1)}, bf16[48,384]{1,0:T(8,128)(2,1)S(1)}, u32[]{:S(2)}, u32[]{:S(2)}) collective-permute-start(bf16[48,384]{1,0:T(8,128)(2,1)S(1)} %fusion.8), channel_id=1, source_target_pairs={{0,24},{1,25},{2,26},{3,27},{4,28},{5,29},{6,30},{7,31},{8,16},{9,... | collective-permute-start | bytes 110600 | tf_op jit(solution)/shard_map/ppermute | solution.py:87
  61.1 4.9 %collective-permute-start.14 = (bf16[48,384]{1,0:T(8,128)(2,1)S(1)}, bf16[48,384]{1,0:T(8,128)(2,1)S(1)}, u32[]{:S(2)}, u32[]{:S(2)}) collective-permute-start(bf16[48,384]{1,0:T(8,128)(2,1)S(1)} %fusion.8), channel_id=1, source_target_pairs={{0,16},{1,17},{2,18},{3,19},{4,20},{5,21},{6,22},{7,23},{8,24},{9,... | collective-permute-start | bytes 110600 | tf_op jit(solution)/shard_map/ppermute | solution.py:87
  61.1 4.9 %collective-permute-start.13 = (bf16[48,384]{1,0:T(8,128)(2,1)S(1)}, bf16[48,384]{1,0:T(8,128)(2,1)S(1)}, u32[]{:S(2)}, u32[]{:S(2)}) collective-permute-start(bf16[48,384]{1,0:T(8,128)(2,1)S(1)} %fusion.8), channel_id=1, source_target_pairs={{0,8},{1,9},{2,10},{3,11},{4,12},{5,13},{6,14},{7,15},{8,0},{9,1},... | collective-permute-start | bytes 110600 | tf_op jit(solution)/shard_map/ppermute | solution.py:87
  66.0 11.4 %collective-permute-start.18 = (bf16[192,384]{1,0:T(8,128)(2,1)S(1)}, bf16[192,384]{1,0:T(8,128)(2,1)S(1)}, u32[]{:S(2)}, u32[]{:S(2)}) collective-permute-start(bf16[192,384]{1,0:T(8,128)(2,1)S(1)} %pad_maximum_fusion.5.refs_0_), channel_id=1, source_target_pairs={{0,6},{1,7},{2,4},{3,5},{4,2},{5,3},{6,0},{7,1},{8,14},{9,15},{10,... | collective-permute-start | bytes 442376 | tf_op jit(solution)/shard_map/ppermute | solution.py:87
  67.5 9.9 %collective-permute-start.17 = (bf16[192,384]{1,0:T(8,128)(2,1)S(1)}, bf16[192,384]{1,0:T(8,128)(2,1)S(1)}, u32[]{:S(2)}, u32[]{:S(2)}) collective-permute-start(bf16[192,384]{1,0:T(8,128)(2,1)S(1)} %pad_maximum_fusion.5.refs_0_), channel_id=1, source_target_pairs={{0,4},{1,5},{2,6},{3,7},{4,0},{5,1},{6,2},{7,3},{8,12},{9,13},{10,... | collective-permute-start | bytes 442376 | tf_op jit(solution)/shard_map/ppermute | solution.py:87
  68.0 9.9 %collective-permute-start.16 = (bf16[192,384]{1,0:T(8,128)(2,1)S(1)}, bf16[192,384]{1,0:T(8,128)(2,1)S(1)}, u32[]{:S(2)}, u32[]{:S(2)}) collective-permute-start(bf16[192,384]{1,0:T(8,128)(2,1)S(1)} %pad_maximum_fusion.5.refs_0_), channel_id=1, source_target_pairs={{0,2},{1,3},{2,0},{3,1},{4,6},{5,7},{6,4},{7,5},{8,10},{9,11},{10,... | collective-permute-start | bytes 442376 | tf_op jit(solution)/shard_map/ppermute | solution.py:87
  69.5 4.2 %collective-permute-start.5 = (bf16[128,384]{1,0:T(8,128)(2,1)S(1)}, bf16[128,384]{1,0:T(8,128)(2,1)S(1)}, u32[]{:S(2)}, u32[]{:S(2)}) collective-permute-start(bf16[128,384]{1,0:T(8,128)(2,1)S(1)} %get-tuple-element.54), channel_id=1, source_target_pairs={{1,0},{2,1},{3,2},{0,3},{5,4},{6,5},{7,6},{4,7},{9,8},{10,9},{11,1... | collective-permute-start | bytes 294920 | tf_op jit(solution)/shard_map/ppermute | solution.py:93
  75.5 3.0 %collective-permute-start.19 = (bf16[192,384]{1,0:T(8,128)(2,1)S(1)}, bf16[192,384]{1,0:T(8,128)(2,1)S(1)}, u32[]{:S(2)}, u32[]{:S(2)}) collective-permute-start(bf16[192,384]{1,0:T(8,128)(2,1)S(1)} %pad_maximum_fusion.5.refs_0_), channel_id=1, source_target_pairs={{0,1},{1,0},{2,3},{3,2},{4,5},{5,4},{6,7},{7,6},{8,9},{9,8},{10,11... | collective-permute-start | bytes 442376 | tf_op jit(solution)/shard_map/ppermute | solution.py:87
  77.4 1.4 %collective-permute-start.22 = (bf16[192,384]{1,0:T(8,128)(2,1)S(1)}, bf16[192,384]{1,0:T(8,128)(2,1)S(1)}, u32[]{:S(2)}, u32[]{:S(2)}) collective-permute-start(bf16[192,384]{1,0:T(8,128)(2,1)S(1)} %collective-permute-done.18.refs_3_), channel_id=1, source_target_pairs={{0,1},{1,0},{2,3},{3,2},{4,5},{5,4},{6,7},{7,6},{8,9},{9,8},{10,11... | collective-permute-start | bytes 442376 | tf_op jit(solution)/shard_map/ppermute | solution.py:87
  77.4 1.6 %collective-permute-start.21 = (bf16[192,384]{1,0:T(8,128)(2,1)S(1)}, bf16[192,384]{1,0:T(8,128)(2,1)S(1)}, u32[]{:S(2)}, u32[]{:S(2)}) collective-permute-start(bf16[192,384]{1,0:T(8,128)(2,1)S(1)} %collective-permute-done.17.refs_2_), channel_id=1, source_target_pairs={{0,1},{1,0},{2,3},{3,2},{4,5},{5,4},{6,7},{7,6},{8,9},{9,8},{10,11... | collective-permute-start | bytes 442376 | tf_op jit(solution)/shard_map/ppermute | solution.py:87
  77.9 1.4 %collective-permute-start.20 = (bf16[192,384]{1,0:T(8,128)(2,1)S(1)}, bf16[192,384]{1,0:T(8,128)(2,1)S(1)}, u32[]{:S(2)}, u32[]{:S(2)}) collective-permute-start(bf16[192,384]{1,0:T(8,128)(2,1)S(1)} %collective-permute-done.16.refs_1_), channel_id=1, source_target_pairs={{0,1},{1,0},{2,3},{3,2},{4,5},{5,4},{6,7},{7,6},{8,9},{9,8},{10,11... | collective-permute-start | bytes 442376 | tf_op jit(solution)/shard_map/ppermute | solution.py:87

commit v5 on v4

--- a/solution.py
+++ b/solution.py
@@ -99,77 +99,47 @@
     return terms[0]
 
 
-def summed_everywhere(keep, message, rider, stages, scattered, slots):
-    per_peer = slots[0].shape[0]
-    returned = [slots[0]]
-    handed_on = {}
-    dom_masks = set(range(2, len(slots), 2))
-
-    def riding(dom_mask, rows_mask):
-        if rows_mask or not dom_mask:
-            return []
-        if dom_mask == 1:
-            return slots[1::2]
-        dom_masks.discard(dom_mask)
-        return [slots[dom_mask], handed_on[dom_mask]]
-
-    def unloaded(dom_mask, rows_mask, load):
-        if rows_mask or not dom_mask:
-            return
-        if dom_mask == 1:
-            returned.append(load[:per_peer])
-            for at in range(1, len(slots) // 2):
-                handed_on[2 * at] = load[at * per_peer : (at + 1) * per_peer]
-        else:
-            returned.append((dom_mask, load))
-
-    first = True
-    for stage in stages:
-        halved = stage in scattered
-        rider_bf = rounded(rider)
-        masks = partner_masks(stage)
-        if not halved:
-            keep = rounded(keep).astype(jnp.float32)
-        part = keep.shape[0]
-        if halved and not first:
-            part //= 1 << len(stage)
-        base = part + rider.shape[0]
-        messages = {}
-        for at, (dom_mask, rows_mask) in enumerate(masks, 1):
-            if not first:
-                block = keep[at * part : (at + 1) * part] if halved else keep
-                message = jnp.concatenate(
-                    [rounded(block), rider_bf, *riding(dom_mask, rows_mask)], axis=0
-                )
-            messages[at] = message
-        order = reversed(messages) if ("rows", 2) in stage else messages
-        sent = {at: swapped(messages[at], *masks[at - 1]) for at in order}
-        terms, rider_terms = [keep[:part]], [rider_bf.astype(jnp.float32)]
-        for at, (dom_mask, rows_mask) in enumerate(masks, 1):
-            arrived = sent[at]
-            terms.append(arrived[:part].astype(jnp.float32))
-            rider_terms.append(arrived[part:base].astype(jnp.float32))
-            if not first:
-                unloaded(dom_mask, rows_mask, arrived[base:])
-        keep, rider = paired_sum(terms), paired_sum(rider_terms)
-        first = False
-    for mask in sorted(dom_masks):
-        load = jnp.concatenate([slots[mask], handed_on[mask]], axis=0)
-        returned.append((mask, swapped(load, mask, 0)))
-    loads = dict(returned[2:])
-    returned = returned[:2] + [loads[mask] for mask in sorted(loads)]
-
-    held = rounded(keep)
-    for stage in reversed(scattered[2:]):
-        held = jnp.concatenate(
-            [held] + [swapped(held, *masks) for masks in partner_masks(stage)], axis=0
-        )
-    near = [held]
-    if len(scattered) > 1:
-        arrived = [swapped(held, *masks) for masks in reversed(partner_masks(scattered[1]))]
-        near += arrived[::-1]
-    far = [swapped(block, *partner_masks(scattered[0])[0]) for block in near]
-    return near, far, rider, returned
+def routed(direct, through):
+    return handed_on(direct, swapped(through, 1, 0))
+
+
+def handed_on(direct, through):
+    rows = direct[0].shape[0]
+    arrived = [direct[0], through]
+    for at in range(1, len(direct)):
+        message = jnp.concatenate([direct[at], through[at * rows : (at + 1) * rows]], axis=0)
+        arrived.append(swapped(message, 2 * at, 0))
+    return arrived
+
+
+def scatter_stage(keep, rider, stage, halved):
+    part = keep.shape[0] >> len(stage) if halved else keep.shape[0]
+    rider_bf = rounded(rider)
+    if not halved:
+        keep = rounded(keep).astype(jnp.float32)
+    messages = []
+    for at in range(1, 1 << len(stage)):
+        block = keep[at * part : (at + 1) * part] if halved else keep
+        messages.append(jnp.concatenate([rounded(block), rider_bf], axis=0))
+    return keep[:part], rider_bf.astype(jnp.float32), messages
+
+
+def exchange(messages, stage, last_first):
+    routes = list(zip(messages, partner_masks(stage)))
+    if last_first:
+        return [swapped(message, *masks) for message, masks in routes[::-1]][::-1]
+    return [swapped(message, *masks) for message, masks in routes]
+
+
+def added(keep, rider, arrived):
+    part = keep.shape[0]
+    terms = [keep] + [block[:part].astype(jnp.float32) for block in arrived]
+    riders = [rider] + [block[part:].astype(jnp.float32) for block in arrived]
+    return paired_sum(terms), paired_sum(riders)
+
+
+def gathered(held, stage):
+    return jnp.concatenate([held] + exchange([held] * ((1 << len(stage)) - 1), stage, True), axis=0)
 
 
 def listed_rows(dom, send_ref, row_count):
@@ -311,7 +281,8 @@
     piece_refs, refs = refs[: 1 + dom_size // 2], refs[1 + dom_size // 2 :]
     og_ref, wq_ref, wkv_ref, featt_ref, qt_ref, odt_ref, own_kv_ref, own_kvt_ref = refs[:8]
     local_bias_ref, far_bias_ref, gf_ref, halo_feat_ref = refs[8:12]
-    slot_feat_refs, refs = refs[12 : 12 + dom_size], refs[12 + dom_size :]
+    direct_refs, refs = refs[12 : 12 + dom_size // 2], refs[12 + dom_size // 2 :]
+    through_ref, refs = refs[0], refs[1:]
     keep_ref, send_ref, rider_ref = refs[:3]
     slot_ref, kv_ref, kvt_ref, extt_ref, gqt_ref, gkvt_ref, ot_ref = refs[3:]
     width, row_count = qt_ref.shape
@@ -412,8 +383,11 @@
     gf_ref[...] = own.T
     halo_feat_ref[...] = rounded(by_feature[:, :tile].T)
     slot_feat = rounded(by_feature[:, near:virt_at].T)
-    for at, out_ref in enumerate(slot_feat_refs):
-        out_ref[...] = slot_feat[at * per_peer : (at + 1) * per_peer]
+    for at, out_ref in enumerate(direct_refs):
+        out_ref[...] = slot_feat[2 * at * per_peer : (2 * at + 1) * per_peer]
+        through_ref[at * per_peer : (at + 1) * per_peer] = slot_feat[
+            (2 * at + 1) * per_peer : (2 * at + 2) * per_peer
+        ]
     rider_ref[...] = by_feature[:, virt_at:].T * factor
 
     sums = (
@@ -462,12 +436,17 @@
             gkv_ref[rows, (which - 1) * width : which * width] = value
 
 
-def return_kernel(place_ref, gf_ref, halo_ref, send_ref, *refs):
-    piece_refs, out_ref = refs[:-1], refs[-1]
+def return_kernel(place_ref, send_hbm, gf_ref, halo_ref, *refs):
+    piece_refs, (out_ref, send_ref, sems) = refs[:-3], refs[-3:]
+    fetch([(send_hbm, send_ref)], sems)[0].wait()
     row_count = gf_ref.shape[0]
     tile = halo_ref.shape[0]
+    per_peer = send_ref.shape[1]
     chosen = listed_rows(place_ref[0], send_ref, row_count)
-    returned = jnp.concatenate([ref[...] for ref in piece_refs], axis=0)
+    returned = jnp.concatenate(
+        [piece_refs[0][...], piece_refs[1][:per_peer]] + [ref[...] for ref in piece_refs[2:]],
+        axis=0,
+    )
     total = gf_ref[...] + rows_contracted(chosen, returned)
     out_ref[: row_count - tile] = total[: row_count - tile]
     out_ref[row_count - tile :] = total[row_count - tile :] + halo_ref[...].astype(jnp.float32)
@@ -480,6 +459,10 @@
     scratch = list(scratch)
     if fetched:
         scratch.append(pltpu.SemaphoreType.DMA((fetched,)))
+    constrained = [
+        pltpu.with_memory_space_constraint(x, pltpu.HBM) if space is pltpu.HBM else x
+        for x, space in zip(args, spaces)
+    ]
     return pl.pallas_call(
         kernel,
         out_shape=outs,
@@ -489,7 +472,7 @@
         compiler_params=pltpu.CompilerParams(vmem_limit_bytes=VMEM_BYTES),
         cost_estimate=pl.CostEstimate(flops=flops, bytes_accessed=moved, transcendentals=0),
         name=name,
-    )(*args)
+    )(*constrained)
 
 
 def shards(features, out_grad, w_query, w_keyval, w_out, virtual, local_nbr, expander, send_rows):
@@ -516,12 +499,8 @@
         [pltpu.VMEM(features.shape, bf16), pltpu.VMEM(send_rows.shape, jnp.int32)],
         fetched=2,
     )
-    through = swapped(through, 1, 0)
+    arrived = routed(direct, through)
     halo = shifted(halo, "rows", 1)
-    arrived = [direct[0], through]
-    for at in range(1, dom_size // 2):
-        handed_on = through[at * per_peer : (at + 1) * per_peer]
-        arrived.append(swapped(jnp.concatenate([direct[at], handed_on], axis=0), 2 * at, 0))
     prepared = call(
         functools.partial(prepare_kernel, per_peer),
         "prepare",
@@ -554,7 +533,8 @@
         [
             shape((row_count, width), f32),
             shape((TILE, width), bf16),
-            *[shape((per_peer, width), bf16)] * dom_size,
+            *[shape((per_peer, width), bf16)] * (dom_size // 2),
+            shape((slots // 2, width), bf16),
             shape((2 * width, width), f32),
             shape((2 * width + padded, width), bf16),
             shape((padded, width), f32),
@@ -571,18 +551,34 @@
         ],
         flops=32 * ext_rows * width * width,
     )
-    slot_feat, (keep, message, rider) = results[:dom_size], results[dom_size:]
-
-    near, far, rider, returned = summed_everywhere(
-        keep, message, rider, stages, scattered, slot_feat
-    )
+    *direct, through, keep, message, rider = results
+
+    rider = rounded(rider).astype(f32)
+    keep, rider = added(keep, rider, exchange([message], stages[0], False))
+    through = swapped(through, 1, 0)
     halo_back = shifted(halo_feat, "rows", -1)
+    for at, stage in enumerate(stages[1:], 1):
+        keep, rider, messages = scatter_stage(keep, rider, stage, stage in scattered)
+        if at == 1:
+            through, _ = lax.optimization_barrier((through, messages))
+            returned = handed_on(direct, through)
+        if at == 2:
+            messages, returned = lax.optimization_barrier((messages, returned))
+        keep, rider = added(keep, rider, exchange(messages, stage, False))
     (grad_features,) = call(
         return_kernel,
         "return_rows",
         [shape((row_count, width), f32)],
-        [place, own_feat, halo_back, send_rows, *returned],
-    )
+        [place, send_rows, own_feat, halo_back, *returned],
+        [pltpu.VMEM(send_rows.shape, jnp.int32)],
+        fetched=1,
+    )
+    held = rounded(keep)
+    for stage in reversed(scattered[2:]):
+        held = gathered(held, stage)
+    held, grad_features = lax.optimization_barrier((held, grad_features))
+    near = [held] + exchange([held] * ((1 << len(scattered[1])) - 1), scattered[1], True)
+    far = [swapped(block, *partner_masks(scattered[0])[0]) for block in near]
     grad_wq, grad_wkv, grad_wo = call(
         functools.partial(place_kernel, rows_per_piece),
         "place_sums",

time: 81.8 us -> 68.8 us (0.84)
  waiting for transfers between devices: 28.5 us -> 19.2 us
  local copies, waits for them, and re-layouts: 7.77 us -> 0.08 us
  starting transfers between devices: 26.2 us -> 29.2 us
  Pallas kernels: 17 us -> 17.9 us
    unnamed x23 -> x0, local copies, waits for them, and re-layouts: 7.65 us -> none
    ppermute x21 -> x25, waiting for transfers between devices: 24.4 us -> 19.2 us  [swapped(): return lax.ppermute(block, ('dom', 'rows'), route)]
    ppermute x2, waiting for transfers between devices: 4.13 us -> 0.01 us  [shifted(): return lax.ppermute(block, axis, route)]
    ppermute x21 -> x25, starting transfers between devices: 26.1 us -> 29.2 us  [swapped(): return lax.ppermute(block, ('dom', 'rows'), route)]
    pallas_call x5, Pallas kernels: 17 us -> 17.9 us  [call(): pl.pallas_call(kernel, out_shape=outs, in_specs=[pl.BlockSpec(memory_spac...]
  transfers between devices with their start and end apart: 23 -> 27, of which waited for: 12 -> 14; matrix products, arithmetic and copies ran while one was open for 1% -> 2% of each run, Pallas kernels for 7% -> 9%
where the time goes in v5:
time: 68.8 us; the launch traced here: 68.5 us
  starting transfers between devices  29.2 us (42%)
  waiting for transfers between devices  19.2 us (28%)
  Pallas kernels  17.9 us (26%)
  other arithmetic  1.08 us (2%)
  between operations  0.9 us (1%)
    ppermute x25, starting transfers between devices, swapped(): return lax.ppermute(block, ('dom', 'rows'), route)  29.2 us
    ppermute x25, waiting for transfers between devices, swapped(): return lax.ppermute(block, ('dom', 'rows'), route)  19.2 us
    pallas_call x5, Pallas kernels, call(): pl.pallas_call(kernel, out_shape=outs, in_specs=[pl.BlockSpec(memory_spac...  17.9 us
  transfers between devices with their start and end apart: 27, of which 14 were waited for; matrix products, arithmetic and copies ran while one was open for 2% of the time, Pallas kernels for 9%

profile of v5, /device:TPU:0, one launch (start us, length us, event | category | flops | bytes accessed | tf_op | source)
XLA Modules:
  0.0 68.5 jit_solution(2498672784872356495)
XLA Ops:
  0.7 0.1 pad_add_fusion.place_ref
  0.7 1.8 %pick_rows.1 = (bf16[128,384]{1,0:T(8,128)(2,1)S(1)}, bf16[128,384]{1,0:T(8,128)(2,1)S(1)}, bf16[32,384]{1,0:T(8,128)(2,1)S(1)}, bf16[32,384]{1,0:T(8,128)(2,1)S...) custom-call(s32[2]{0:T(128)S(1)} %pad_add_fusion.place_ref, bf16[256,384]{1,0:T(8,128)(2,1)} %feat_hbm.3, ...), custom_call_target="tpu_custom_call" | custom-call | bytes 492552 | tf_op jit(solution)/shard_map/pick_rows/pallas_call | solution.py:466
  2.5 3.0 %collective-permute-start.1 = (bf16[128,384]{1,0:T(8,128)(2,1)S(1)}, bf16[128,384]{1,0:T(8,128)(2,1)S(1)}, u32[]{:S(2)}, u32[]{:S(2)}) collective-permute-start(bf16[128,384]{1,0:T(8,128)(2,1)S(1)} %get-tuple-element.47), channel_id=1, source_target_pairs={{0,4},{1,5},{2,6},{3,7},{4,0},{5,1},{6,2},{7,3},{8,12},{9,13},{10,... | collective-permute-start | bytes 294920 | tf_op jit(solution)/shard_map/ppermute | solution.py:87
  5.5 2.8 %collective-permute-done.1.refs_1_ = bf16[128,384]{1,0:T(8,128)(2,1)S(1)} collective-permute-done((bf16[128,384]{1,0:T(8,128)(2,1)S(1)}, bf16[128,384]{1,0:T(8,128)(2,1)S(1)}, u32[]{:S(2)}, u32[]{:S(2)}) %collective-permute-start.1) | collective-permute-done | bytes 98336 | tf_op jit(solution)/shard_map/ppermute | solution.py:87
  8.3 2.0 %collective-permute-start.2 = (bf16[64,384]{1,0:T(8,128)(2,1)S(1)}, bf16[64,384]{1,0:T(8,128)(2,1)S(1)}, u32[]{:S(2)}, u32[]{:S(2)}) collective-permute-start(bf16[64,384]{1,0:T(8,128)(2,1)S(1)} %pad_maximum_fusion.7), channel_id=1, source_target_pairs={{0,8},{1,9},{2,10},{3,11},{4,12},{5,13},{6,14},{7,15},{8,0},{9,1},... | collective-permute-start | bytes 147464 | tf_op jit(solution)/shard_map/ppermute | solution.py:87
  10.3 2.6 %collective-permute-start.3 = (bf16[64,384]{1,0:T(8,128)(2,1)S(1)}, bf16[64,384]{1,0:T(8,128)(2,1)S(1)}, u32[]{:S(2)}, u32[]{:S(2)}) collective-permute-start(bf16[64,384]{1,0:T(8,128)(2,1)S(1)} %pad_maximum_fusion.8), channel_id=1, source_target_pairs={{0,16},{1,17},{2,18},{3,19},{4,20},{5,21},{6,22},{7,23},{8,24},{9,... | collective-permute-start | bytes 147464 | tf_op jit(solution)/shard_map/ppermute | solution.py:87
  12.9 0.0 collective-permute-start.4
  12.9 3.5 %prepare.1 = (bf16[256,384]{1,0:T(8,128)(2,1)S(1)}, bf16[384,384]{1,0:T(8,128)(2,1)S(1)}, bf16[384,768]{1,0:T(8,128)(2,1)S(1)}, bf16[384,272]{1,0:T(8,128)(2,1)S...) custom-call(s32[2]{0:T(128)S(1)} %pad_add_fusion.place_ref, ...), custom_call_target="tpu_custom_call" | custom-call | flops 377487360 | bytes 4656136 | tf_op jit(solution)/shard_map/prepare/pallas_call | solution.py:466
  16.4 0.0 collective-permute-done.halo_ref
  16.4 2.4 %collective-permute-done.4.refs_4_ = bf16[64,384]{1,0:T(8,128)(2,1)S(1)} collective-permute-done((bf16[64,384]{1,0:T(8,128)(2,1)S(1)}, bf16[64,384]{1,0:T(8,128)(2,1)S(1)}, u32[]{:S(2)}, u32[]{:S(2)}) %collective-permute-start.4) | collective-permute-done | bytes 49184 | tf_op jit(solution)/shard_map/ppermute | solution.py:87
  18.8 8.1 %attend.1 = (f32[256,384]{1,0:T(8,128)S(1)}, bf16[128,384]{1,0:T(8,128)(2,1)S(1)}, bf16[32,384]{1,0:T(8,128)(2,1)S(1)}, bf16[32,384]{1,0:T(8,128)(2,1)S(1)}, bf1...) custom-call(s32[2]{0:T(128)S(1)} %pad_add_fusion.place_ref, ...), custom_call_target="tpu_custom_call" | custom-call | flops 3095396352 | bytes 5922824 | tf_op jit(solution)/shard_map/attend/pallas_call | solution.py:466
  26.9 0.1 collective-permute-start.5
  27.0 1.6 %collective-permute-start.9 = (bf16[128,384]{1,0:T(8,128)(2,1)S(1)}, bf16[128,384]{1,0:T(8,128)(2,1)S(1)}, u32[]{:S(2)}, u32[]{:S(2)}) collective-permute-start(bf16[128,384]{1,0:T(8,128)(2,1)S(1)} %get-tuple-element.65), channel_id=1, source_target_pairs={{0,4},{1,5},{2,6},{3,7},{4,0},{5,1},{6,2},{7,3},{8,12},{9,13},{10,... | collective-permute-start | bytes 294920 | tf_op jit(solution)/shard_map/ppermute | solution.py:87
  28.5 0.5 collective-permute-done.5
  29.0 0.2 fusion.5
  29.2 0.1 pad_maximum_fusion.2
  29.3 1.6 %collective-permute-start.6 = (bf16[208,384]{1,0:T(8,128)(2,1)S(1)}, bf16[208,384]{1,0:T(8,128)(2,1)S(1)}, u32[]{:S(2)}, u32[]{:S(2)}) collective-permute-start(bf16[208,384]{1,0:T(8,128)(2,1)S(1)} %get-tuple-element.104), channel_id=1, source_target_pairs={{0,2},{1,3},{2,0},{3,1},{4,6},{5,7},{6,4},{7,5},{8,10},{9,11},{10,... | collective-permute-start | bytes 479240 | tf_op jit(solution)/shard_map/ppermute | solution.py:87
  30.9 1.5 %collective-permute-start.7 = (bf16[208,384]{1,0:T(8,128)(2,1)S(1)}, bf16[208,384]{1,0:T(8,128)(2,1)S(1)}, u32[]{:S(2)}, u32[]{:S(2)}) collective-permute-start(bf16[208,384]{1,0:T(8,128)(2,1)S(1)} %get-tuple-element.105), channel_id=1, source_target_pairs={{0,4},{1,5},{2,6},{3,7},{4,0},{5,1},{6,2},{7,3},{8,12},{9,13},{10,... | collective-permute-start | bytes 479240 | tf_op jit(solution)/shard_map/ppermute | solution.py:87
  32.4 0.5 collective-permute-start.8
  32.8 0.0 collective-permute-done.9.refs_1_
  32.9 0.1 collective-permute-start.10
  33.0 2.0 %collective-permute-start.11 = (bf16[64,384]{1,0:T(8,128)(2,1)S(1)}, bf16[64,384]{1,0:T(8,128)(2,1)S(1)}, u32[]{:S(2)}, u32[]{:S(2)}) collective-permute-start(bf16[64,384]{1,0:T(8,128)(2,1)S(1)} %pad_maximum_fusion.11), channel_id=1, source_target_pairs={{0,16},{1,17},{2,18},{3,19},{4,20},{5,21},{6,22},{7,23},{8,24},{9,... | collective-permute-start | bytes 147464 | tf_op jit(solution)/shard_map/ppermute | solution.py:87
  35.0 0.5 collective-permute-done.6
  35.5 1.9 %collective-permute-start.12 = (bf16[64,384]{1,0:T(8,128)(2,1)S(1)}, bf16[64,384]{1,0:T(8,128)(2,1)S(1)}, u32[]{:S(2)}, u32[]{:S(2)}) collective-permute-start(bf16[64,384]{1,0:T(8,128)(2,1)S(1)} %pad_maximum_fusion.12), channel_id=1, source_target_pairs={{0,24},{1,25},{2,26},{3,27},{4,28},{5,29},{6,30},{7,31},{8,16},{9,... | collective-permute-start | bytes 147464 | tf_op jit(solution)/shard_map/ppermute | solution.py:87
  37.4 0.5 collective-permute-done.7
  37.9 2.2 %collective-permute-done.8 = bf16[208,384]{1,0:T(8,128)(2,1)S(1)} collective-permute-done((bf16[208,384]{1,0:T(8,128)(2,1)S(1)}, bf16[208,384]{1,0:T(8,128)(2,1)S(1)}, u32[]{:S(2)}, u32[]{:S(2)}) %collective-permute-start.8) | collective-permute-done | bytes 159776 | tf_op jit(solution)/shard_map/ppermute | solution.py:87
  40.1 0.1 fusion.3
  40.3 0.0 collective-permute-done.10.refs_2_
  40.3 1.1 %collective-permute-done.12.refs_4_ = bf16[64,384]{1,0:T(8,128)(2,1)S(1)} collective-permute-done((bf16[64,384]{1,0:T(8,128)(2,1)S(1)}, bf16[64,384]{1,0:T(8,128)(2,1)S(1)}, u32[]{:S(2)}, u32[]{:S(2)}) %collective-permute-start.12) | collective-permute-done | bytes 49184 | tf_op jit(solution)/shard_map/ppermute | solution.py:87
  41.4 2.5 %collective-permute-start.14 = (bf16[64,384]{1,0:T(8,128)(2,1)S(1)}, bf16[64,384]{1,0:T(8,128)(2,1)S(1)}, u32[]{:S(2)}, u32[]{:S(2)}) collective-permute-start(bf16[64,384]{1,0:T(8,128)(2,1)S(1)} %get-tuple-element.71), channel_id=1, source_target_pairs={{0,16},{1,17},{2,18},{3,19},{4,20},{5,21},{6,22},{7,23},{8,24},{9,... | collective-permute-start | bytes 147464 | tf_op jit(solution)/shard_map/ppermute | solution.py:87
  43.9 1.9 %collective-permute-start.15 = (bf16[64,384]{1,0:T(8,128)(2,1)S(1)}, bf16[64,384]{1,0:T(8,128)(2,1)S(1)}, u32[]{:S(2)}, u32[]{:S(2)}) collective-permute-start(bf16[64,384]{1,0:T(8,128)(2,1)S(1)} %get-tuple-element.72), channel_id=1, source_target_pairs={{0,24},{1,25},{2,26},{3,27},{4,28},{5,29},{6,30},{7,31},{8,16},{9,... | collective-permute-start | bytes 147464 | tf_op jit(solution)/shard_map/ppermute | solution.py:87
  45.8 0.9 %collective-permute-done.14 = bf16[64,384]{1,0:T(8,128)(2,1)S(1)} collective-permute-done((bf16[64,384]{1,0:T(8,128)(2,1)S(1)}, bf16[64,384]{1,0:T(8,128)(2,1)S(1)}, u32[]{:S(2)}, u32[]{:S(2)}) %collective-permute-start.14) | collective-permute-done | bytes 49184 | tf_op jit(solution)/shard_map/ppermute | solution.py:87
  46.7 3.0 %collective-permute-done.15 = bf16[64,384]{1,0:T(8,128)(2,1)S(1)} collective-permute-done((bf16[64,384]{1,0:T(8,128)(2,1)S(1)}, bf16[64,384]{1,0:T(8,128)(2,1)S(1)}, u32[]{:S(2)}, u32[]{:S(2)}) %collective-permute-start.15) | collective-permute-done | bytes 49184 | tf_op jit(solution)/shard_map/ppermute | solution.py:87
  49.8 2.0 %collective-permute-start.18 = (bf16[48,384]{1,0:T(8,128)(2,1)S(1)}, bf16[48,384]{1,0:T(8,128)(2,1)S(1)}, u32[]{:S(2)}, u32[]{:S(2)}) collective-permute-start(bf16[48,384]{1,0:T(8,128)(2,1)S(1)} %fusion.2), channel_id=1, source_target_pairs={{0,24},{1,25},{2,26},{3,27},{4,28},{5,29},{6,30},{7,31},{8,16},{9,... | collective-permute-start | bytes 110600 | tf_op jit(solution)/shard_map/ppermute | solution.py:87
  51.8 2.5 %collective-permute-start.16 = (bf16[48,384]{1,0:T(8,128)(2,1)S(1)}, bf16[48,384]{1,0:T(8,128)(2,1)S(1)}, u32[]{:S(2)}, u32[]{:S(2)}) collective-permute-start(bf16[48,384]{1,0:T(8,128)(2,1)S(1)} %fusion.2), channel_id=1, source_target_pairs={{0,8},{1,9},{2,10},{3,11},{4,12},{5,13},{6,14},{7,15},{8,0},{9,1},... | collective-permute-start | bytes 110600 | tf_op jit(solution)/shard_map/ppermute | solution.py:87
  54.2 2.5 %return_rows.1 = f32[256,384]{1,0:T(8,128)} custom-call(s32[2]{0:T(128)S(1)} %pad_add_fusion.place_ref, s32[8,32]{1,0:T(8,128)} %send_hbm.3, f32[256,384]{1,0:T(8,128)S(1)} %get-tuple-element.73.gf_ref, bf16[128,384]{1,0:T(8,128)(2,1)S(1)} %collective-permute-done.19.halo_ref, bf16[32,384]{1,0:T(8,128)(2,1)S(1)} %get-tuple-element.75.refs_0_, ...), custom_call_target="tpu_custom_call" | custom-call | bytes 1156104 | tf_op jit(solution)/shard_map/return_rows/pallas_call | solution.py:466
  56.8 2.5 %collective-permute-start.22 = (bf16[192,384]{1,0:T(8,128)(2,1)S(1)}, bf16[192,384]{1,0:T(8,128)(2,1)S(1)}, u32[]{:S(2)}, u32[]{:S(2)}) collective-permute-start(bf16[192,384]{1,0:T(8,128)(2,1)S(1)} %pad_maximum_fusion.3.refs_0_), channel_id=1, source_target_pairs={{0,6},{1,7},{2,4},{3,5},{4,2},{5,3},{6,0},{7,1},{8,14},{9,15},{10,... | collective-permute-start | bytes 442376 | tf_op jit(solution)/shard_map/ppermute | solution.py:87
  59.3 0.5 collective-permute-start.21
  59.8 0.5 collective-permute-start.20
  60.3 0.1 collective-permute-start.23
  60.4 2.5 %collective-permute-done.22.refs_3_ = bf16[192,384]{1,0:T(8,128)(2,1)S(1)} collective-permute-done((bf16[192,384]{1,0:T(8,128)(2,1)S(1)}, bf16[192,384]{1,0:T(8,128)(2,1)S(1)}, u32[]{:S(2)}, u32[]{:S(2)}) %collective-permute-start.22) | collective-permute-done | bytes 147488 | tf_op jit(solution)/shard_map/ppermute | solution.py:87
  62.9 1.6 %collective-permute-done.21.refs_2_ = bf16[192,384]{1,0:T(8,128)(2,1)S(1)} collective-permute-done((bf16[192,384]{1,0:T(8,128)(2,1)S(1)}, bf16[192,384]{1,0:T(8,128)(2,1)S(1)}, u32[]{:S(2)}, u32[]{:S(2)}) %collective-permute-start.21) | collective-permute-done | bytes 147488 | tf_op jit(solution)/shard_map/ppermute | solution.py:87
  64.5 0.4 collective-permute-done.20.refs_1_
  65.0 0.1 collective-permute-start.24
  65.0 0.6 add_add_fusion
  65.7 0.3 collective-permute-done.25.refs_6_
  65.9 0.4 collective-permute-done.24.refs_5_
  66.3 2.1 %place_sums.1 = (f32[384,384]{1,0:T(8,128)}, f32[384,768]{1,0:T(8,128)}, f32[384,384]{1,0:T(8,128)}) custom-call(s32[2]{0:T(128)S(1)} %pad_add_fusion.place_ref, bf16[192,384]{1,0:T(8,128)(2,1)S(1)} %pad_maximum_fusion.3.refs_0_, bf16[192,384]{1,0:T(8,128)(2,1)S(1)} %collective-permute-done.20.refs_1_, bf16[192,384]{1,0:T(8,128)(2,1)S(1)} %collective-permute-done.21.refs_2_, ...), custom_call_target="tpu_custom_call" | custom-call | bytes 3538952 | tf_op jit(solution)/shard_map/place_sums/pallas_call | solution.py:466
  (34 shorter events, 0.2 us)
Async XLA Ops:
  2.5 5.8 %collective-permute-start.1 = (bf16[128,384]{1,0:T(8,128)(2,1)S(1)}, bf16[128,384]{1,0:T(8,128)(2,1)S(1)}, u32[]{:S(2)}, u32[]{:S(2)}) collective-permute-start(bf16[128,384]{1,0:T(8,128)(2,1)S(1)} %get-tuple-element.47), channel_id=1, source_target_pairs={{0,4},{1,5},{2,6},{3,7},{4,0},{5,1},{6,2},{7,3},{8,12},{9,13},{10,... | collective-permute-start | bytes 294920 | tf_op jit(solution)/shard_map/ppermute | solution.py:87
  5.5 10.9 %collective-permute-start = (bf16[128,384]{1,0:T(8,128)(2,1)S(1)}, bf16[128,384]{1,0:T(8,128)(2,1)S(1)}, u32[]{:S(2)}, u32[]{:S(2)}) collective-permute-start(bf16[128,384]{1,0:T(8,128)(2,1)S(1)} %get-tuple-element.45), channel_id=1, source_target_pairs={{3,0},{0,1},{1,2},{2,3},{7,4},{4,5},{5,6},{6,7},{11,8},{8,9},{9,10... | collective-permute-start | bytes 294920 | tf_op jit(solution)/shard_map/ppermute | solution.py:93
  8.3 8.1 %collective-permute-start.2 = (bf16[64,384]{1,0:T(8,128)(2,1)S(1)}, bf16[64,384]{1,0:T(8,128)(2,1)S(1)}, u32[]{:S(2)}, u32[]{:S(2)}) collective-permute-start(bf16[64,384]{1,0:T(8,128)(2,1)S(1)} %pad_maximum_fusion.7), channel_id=1, source_target_pairs={{0,8},{1,9},{2,10},{3,11},{4,12},{5,13},{6,14},{7,15},{8,0},{9,1},... | collective-permute-start | bytes 147464 | tf_op jit(solution)/shard_map/ppermute | solution.py:87
  10.3 6.1 %collective-permute-start.3 = (bf16[64,384]{1,0:T(8,128)(2,1)S(1)}, bf16[64,384]{1,0:T(8,128)(2,1)S(1)}, u32[]{:S(2)}, u32[]{:S(2)}) collective-permute-start(bf16[64,384]{1,0:T(8,128)(2,1)S(1)} %pad_maximum_fusion.8), channel_id=1, source_target_pairs={{0,16},{1,17},{2,18},{3,19},{4,20},{5,21},{6,22},{7,23},{8,24},{9,... | collective-permute-start | bytes 147464 | tf_op jit(solution)/shard_map/ppermute | solution.py:87
  12.9 5.9 %collective-permute-start.4 = (bf16[64,384]{1,0:T(8,128)(2,1)S(1)}, bf16[64,384]{1,0:T(8,128)(2,1)S(1)}, u32[]{:S(2)}, u32[]{:S(2)}) collective-permute-start(bf16[64,384]{1,0:T(8,128)(2,1)S(1)} %pad_maximum_fusion.9), channel_id=1, source_target_pairs={{0,24},{1,25},{2,26},{3,27},{4,28},{5,29},{6,30},{7,31},{8,16},{9,... | collective-permute-start | bytes 147464 | tf_op jit(solution)/shard_map/ppermute | solution.py:87
  26.9 2.1 %collective-permute-start.5 = (bf16[784,384]{1,0:T(8,128)(2,1)S(1)}, bf16[784,384]{1,0:T(8,128)(2,1)S(1)}, u32[]{:S(2)}, u32[]{:S(2)}) collective-permute-start(bf16[784,384]{1,0:T(8,128)(2,1)S(1)} %get-tuple-element.62), channel_id=1, source_target_pairs={{0,1},{1,0},{2,3},{3,2},{4,5},{5,4},{6,7},{7,6},{8,9},{9,8},{10,11... | collective-permute-start | bytes 1806344 | tf_op jit(solution)/shard_map/ppermute | solution.py:87
  27.0 5.9 %collective-permute-start.9 = (bf16[128,384]{1,0:T(8,128)(2,1)S(1)}, bf16[128,384]{1,0:T(8,128)(2,1)S(1)}, u32[]{:S(2)}, u32[]{:S(2)}) collective-permute-start(bf16[128,384]{1,0:T(8,128)(2,1)S(1)} %get-tuple-element.65), channel_id=1, source_target_pairs={{0,4},{1,5},{2,6},{3,7},{4,0},{5,1},{6,2},{7,3},{8,12},{9,13},{10,... | collective-permute-start | bytes 294920 | tf_op jit(solution)/shard_map/ppermute | solution.py:87
  29.3 6.2 %collective-permute-start.6 = (bf16[208,384]{1,0:T(8,128)(2,1)S(1)}, bf16[208,384]{1,0:T(8,128)(2,1)S(1)}, u32[]{:S(2)}, u32[]{:S(2)}) collective-permute-start(bf16[208,384]{1,0:T(8,128)(2,1)S(1)} %get-tuple-element.104), channel_id=1, source_target_pairs={{0,2},{1,3},{2,0},{3,1},{4,6},{5,7},{6,4},{7,5},{8,10},{9,11},{10,... | collective-permute-start | bytes 479240 | tf_op jit(solution)/shard_map/ppermute | solution.py:87
  30.9 7.0 %collective-permute-start.7 = (bf16[208,384]{1,0:T(8,128)(2,1)S(1)}, bf16[208,384]{1,0:T(8,128)(2,1)S(1)}, u32[]{:S(2)}, u32[]{:S(2)}) collective-permute-start(bf16[208,384]{1,0:T(8,128)(2,1)S(1)} %get-tuple-element.105), channel_id=1, source_target_pairs={{0,4},{1,5},{2,6},{3,7},{4,0},{5,1},{6,2},{7,3},{8,12},{9,13},{10,... | collective-permute-start | bytes 479240 | tf_op jit(solution)/shard_map/ppermute | solution.py:87
  32.4 7.8 %collective-permute-start.8 = (bf16[208,384]{1,0:T(8,128)(2,1)S(1)}, bf16[208,384]{1,0:T(8,128)(2,1)S(1)}, u32[]{:S(2)}, u32[]{:S(2)}) collective-permute-start(bf16[208,384]{1,0:T(8,128)(2,1)S(1)} %get-tuple-element.106), channel_id=1, source_target_pairs={{0,6},{1,7},{2,4},{3,5},{4,2},{5,3},{6,0},{7,1},{8,14},{9,15},{10,... | collective-permute-start | bytes 479240 | tf_op jit(solution)/shard_map/ppermute | solution.py:87
  32.9 7.4 %collective-permute-start.10 = (bf16[64,384]{1,0:T(8,128)(2,1)S(1)}, bf16[64,384]{1,0:T(8,128)(2,1)S(1)}, u32[]{:S(2)}, u32[]{:S(2)}) collective-permute-start(bf16[64,384]{1,0:T(8,128)(2,1)S(1)} %pad_maximum_fusion.10), channel_id=1, source_target_pairs={{0,8},{1,9},{2,10},{3,11},{4,12},{5,13},{6,14},{7,15},{8,0},{9,1},... | collective-permute-start | bytes 147464 | tf_op jit(solution)/shard_map/ppermute | solution.py:87
  33.0 7.3 %collective-permute-start.11 = (bf16[64,384]{1,0:T(8,128)(2,1)S(1)}, bf16[64,384]{1,0:T(8,128)(2,1)S(1)}, u32[]{:S(2)}, u32[]{:S(2)}) collective-permute-start(bf16[64,384]{1,0:T(8,128)(2,1)S(1)} %pad_maximum_fusion.11), channel_id=1, source_target_pairs={{0,16},{1,17},{2,18},{3,19},{4,20},{5,21},{6,22},{7,23},{8,24},{9,... | collective-permute-start | bytes 147464 | tf_op jit(solution)/shard_map/ppermute | solution.py:87
  35.5 5.9 %collective-permute-start.12 = (bf16[64,384]{1,0:T(8,128)(2,1)S(1)}, bf16[64,384]{1,0:T(8,128)(2,1)S(1)}, u32[]{:S(2)}, u32[]{:S(2)}) collective-permute-start(bf16[64,384]{1,0:T(8,128)(2,1)S(1)} %pad_maximum_fusion.12), channel_id=1, source_target_pairs={{0,24},{1,25},{2,26},{3,27},{4,28},{5,29},{6,30},{7,31},{8,16},{9,... | collective-permute-start | bytes 147464 | tf_op jit(solution)/shard_map/ppermute | solution.py:87
  41.4 4.4 %collective-permute-start.13 = (bf16[64,384]{1,0:T(8,128)(2,1)S(1)}, bf16[64,384]{1,0:T(8,128)(2,1)S(1)}, u32[]{:S(2)}, u32[]{:S(2)}) collective-permute-start(bf16[64,384]{1,0:T(8,128)(2,1)S(1)} %get-tuple-element.70), channel_id=1, source_target_pairs={{0,8},{1,9},{2,10},{3,11},{4,12},{5,13},{6,14},{7,15},{8,0},{9,1},... | collective-permute-start | bytes 147464 | tf_op jit(solution)/shard_map/ppermute | solution.py:87
  41.4 5.3 %collective-permute-start.14 = (bf16[64,384]{1,0:T(8,128)(2,1)S(1)}, bf16[64,384]{1,0:T(8,128)(2,1)S(1)}, u32[]{:S(2)}, u32[]{:S(2)}) collective-permute-start(bf16[64,384]{1,0:T(8,128)(2,1)S(1)} %get-tuple-element.71), channel_id=1, source_target_pairs={{0,16},{1,17},{2,18},{3,19},{4,20},{5,21},{6,22},{7,23},{8,24},{9,... | collective-permute-start | bytes 147464 | tf_op jit(solution)/shard_map/ppermute | solution.py:87
  43.9 5.9 %collective-permute-start.15 = (bf16[64,384]{1,0:T(8,128)(2,1)S(1)}, bf16[64,384]{1,0:T(8,128)(2,1)S(1)}, u32[]{:S(2)}, u32[]{:S(2)}) collective-permute-start(bf16[64,384]{1,0:T(8,128)(2,1)S(1)} %get-tuple-element.72), channel_id=1, source_target_pairs={{0,24},{1,25},{2,26},{3,27},{4,28},{5,29},{6,30},{7,31},{8,16},{9,... | collective-permute-start | bytes 147464 | tf_op jit(solution)/shard_map/ppermute | solution.py:87
  45.8 8.4 %collective-permute-start.19 = (bf16[128,384]{1,0:T(8,128)(2,1)S(1)}, bf16[128,384]{1,0:T(8,128)(2,1)S(1)}, u32[]{:S(2)}, u32[]{:S(2)}) collective-permute-start(bf16[128,384]{1,0:T(8,128)(2,1)S(1)} %get-tuple-element.74), channel_id=1, source_target_pairs={{1,0},{2,1},{3,2},{0,3},{5,4},{6,5},{7,6},{4,7},{9,8},{10,9},{11,1... | collective-permute-start | bytes 294920 | tf_op jit(solution)/shard_map/ppermute | solution.py:93
  49.8 7.0 %collective-permute-start.18 = (bf16[48,384]{1,0:T(8,128)(2,1)S(1)}, bf16[48,384]{1,0:T(8,128)(2,1)S(1)}, u32[]{:S(2)}, u32[]{:S(2)}) collective-permute-start(bf16[48,384]{1,0:T(8,128)(2,1)S(1)} %fusion.2), channel_id=1, source_target_pairs={{0,24},{1,25},{2,26},{3,27},{4,28},{5,29},{6,30},{7,31},{8,16},{9,... | collective-permute-start | bytes 110600 | tf_op jit(solution)/shard_map/ppermute | solution.py:87
  51.8 5.0 %collective-permute-start.17 = (bf16[48,384]{1,0:T(8,128)(2,1)S(1)}, bf16[48,384]{1,0:T(8,128)(2,1)S(1)}, u32[]{:S(2)}, u32[]{:S(2)}) collective-permute-start(bf16[48,384]{1,0:T(8,128)(2,1)S(1)} %fusion.2), channel_id=1, source_target_pairs={{0,16},{1,17},{2,18},{3,19},{4,20},{5,21},{6,22},{7,23},{8,24},{9,... | collective-permute-start | bytes 110600 | tf_op jit(solution)/shard_map/ppermute | solution.py:87
  51.8 5.0 %collective-permute-start.16 = (bf16[48,384]{1,0:T(8,128)(2,1)S(1)}, bf16[48,384]{1,0:T(8,128)(2,1)S(1)}, u32[]{:S(2)}, u32[]{:S(2)}) collective-permute-start(bf16[48,384]{1,0:T(8,128)(2,1)S(1)} %fusion.2), channel_id=1, source_target_pairs={{0,8},{1,9},{2,10},{3,11},{4,12},{5,13},{6,14},{7,15},{8,0},{9,1},... | collective-permute-start | bytes 110600 | tf_op jit(solution)/shard_map/ppermute | solution.py:87
  56.8 6.1 %collective-permute-start.22 = (bf16[192,384]{1,0:T(8,128)(2,1)S(1)}, bf16[192,384]{1,0:T(8,128)(2,1)S(1)}, u32[]{:S(2)}, u32[]{:S(2)}) collective-permute-start(bf16[192,384]{1,0:T(8,128)(2,1)S(1)} %pad_maximum_fusion.3.refs_0_), channel_id=1, source_target_pairs={{0,6},{1,7},{2,4},{3,5},{4,2},{5,3},{6,0},{7,1},{8,14},{9,15},{10,... | collective-permute-start | bytes 442376 | tf_op jit(solution)/shard_map/ppermute | solution.py:87
  59.3 5.2 %collective-permute-start.21 = (bf16[192,384]{1,0:T(8,128)(2,1)S(1)}, bf16[192,384]{1,0:T(8,128)(2,1)S(1)}, u32[]{:S(2)}, u32[]{:S(2)}) collective-permute-start(bf16[192,384]{1,0:T(8,128)(2,1)S(1)} %pad_maximum_fusion.3.refs_0_), channel_id=1, source_target_pairs={{0,4},{1,5},{2,6},{3,7},{4,0},{5,1},{6,2},{7,3},{8,12},{9,13},{10,... | collective-permute-start | bytes 442376 | tf_op jit(solution)/shard_map/ppermute | solution.py:87
  59.8 5.1 %collective-permute-start.20 = (bf16[192,384]{1,0:T(8,128)(2,1)S(1)}, bf16[192,384]{1,0:T(8,128)(2,1)S(1)}, u32[]{:S(2)}, u32[]{:S(2)}) collective-permute-start(bf16[192,384]{1,0:T(8,128)(2,1)S(1)} %pad_maximum_fusion.3.refs_0_), channel_id=1, source_target_pairs={{0,2},{1,3},{2,0},{3,1},{4,6},{5,7},{6,4},{7,5},{8,10},{9,11},{10,... | collective-permute-start | bytes 442376 | tf_op jit(solution)/shard_map/ppermute | solution.py:87
  60.3 5.3 %collective-permute-start.23 = (bf16[192,384]{1,0:T(8,128)(2,1)S(1)}, bf16[192,384]{1,0:T(8,128)(2,1)S(1)}, u32[]{:S(2)}, u32[]{:S(2)}) collective-permute-start(bf16[192,384]{1,0:T(8,128)(2,1)S(1)} %pad_maximum_fusion.3.refs_0_), channel_id=1, source_target_pairs={{0,1},{1,0},{2,3},{3,2},{4,5},{5,4},{6,7},{7,6},{8,9},{9,8},{10,11... | collective-permute-start | bytes 442376 | tf_op jit(solution)/shard_map/ppermute | solution.py:87
  62.9 2.8 %collective-permute-start.26 = (bf16[192,384]{1,0:T(8,128)(2,1)S(1)}, bf16[192,384]{1,0:T(8,128)(2,1)S(1)}, u32[]{:S(2)}, u32[]{:S(2)}) collective-permute-start(bf16[192,384]{1,0:T(8,128)(2,1)S(1)} %collective-permute-done.22.refs_3_), channel_id=1, source_target_pairs={{0,1},{1,0},{2,3},{3,2},{4,5},{5,4},{6,7},{7,6},{8,9},{9,8},{10,11... | collective-permute-start | bytes 442376 | tf_op jit(solution)/shard_map/ppermute | solution.py:87
  64.5 1.4 %collective-permute-start.25 = (bf16[192,384]{1,0:T(8,128)(2,1)S(1)}, bf16[192,384]{1,0:T(8,128)(2,1)S(1)}, u32[]{:S(2)}, u32[]{:S(2)}) collective-permute-start(bf16[192,384]{1,0:T(8,128)(2,1)S(1)} %collective-permute-done.21.refs_2_), channel_id=1, source_target_pairs={{0,1},{1,0},{2,3},{3,2},{4,5},{5,4},{6,7},{7,6},{8,9},{9,8},{10,11... | collective-permute-start | bytes 442376 | tf_op jit(solution)/shard_map/ppermute | solution.py:87
  65.0 1.4 %collective-permute-start.24 = (bf16[192,384]{1,0:T(8,128)(2,1)S(1)}, bf16[192,384]{1,0:T(8,128)(2,1)S(1)}, u32[]{:S(2)}, u32[]{:S(2)}) collective-permute-start(bf16[192,384]{1,0:T(8,128)(2,1)S(1)} %collective-permute-done.20.refs_1_), channel_id=1, source_target_pairs={{0,1},{1,0},{2,3},{3,2},{4,5},{5,4},{6,7},{7,6},{8,9},{9,8},{10,11... | collective-permute-start | bytes 442376 | tf_op jit(solution)/shard_map/ppermute | solution.py:87

commit v6 on v5

--- a/solution.py
+++ b/solution.py
@@ -37,34 +37,25 @@
 
 
 def exchange_stages(dom_size, rows_size):
-    dom_bits = [1 << i for i in range(dom_size.bit_length() - 1)]
-    rows_bits = [1 << i for i in range(rows_size.bit_length() - 1)]
-    stages = [[("rows", bit)] for bit in rows_bits[:1]]
-    rest = [("rows", bit) for bit in rows_bits[1:2]] + [("dom", bit) for bit in dom_bits]
-    rest += [("rows", bit) for bit in rows_bits[2:]]
-    for at in range(0, len(rest), 2):
-        stages.append(rest[at : at + 2])
+    stages = [[((0, 1), (0, 1))], [((1, 2), (0, 2)), ((1, 0), (1, 2))]]
+    stages += [[((bit, 0), (bit, 0))] for bit in powers_of_two(2, dom_size)]
+    stages += [[((0, bit), (0, bit))] for bit in powers_of_two(4, rows_size)]
     return stages
 
 
-def scattered_stages(stages, rows):
-    taken = []
-    for stage in stages:
-        if rows % (ROW_PACK << len(stage)):
-            break
-        rows >>= len(stage)
-        taken.append(stage)
-    return taken
+def powers_of_two(first, size):
+    return [1 << i for i in range(size.bit_length() - 1) if 1 << i >= first]
 
 
 def partner_masks(stage):
     masks = []
     for digit in range(1, 1 << len(stage)):
-        by_axis = {"dom": 0, "rows": 0}
-        for i, (axis, bit) in enumerate(stage):
+        dom_mask = rows_mask = 0
+        for i, (mask, _) in enumerate(stage):
             if digit >> i & 1:
-                by_axis[axis] |= bit
-        masks.append((by_axis["dom"], by_axis["rows"]))
+                dom_mask ^= mask[0]
+                rows_mask ^= mask[1]
+        masks.append((dom_mask, rows_mask))
     return masks
 
 
@@ -72,8 +63,12 @@
     index = jnp.int32(0)
     for stage in stages:
         index = index << len(stage)
-        for i, (axis, bit) in enumerate(stage):
-            index += jnp.where(lax.axis_index(axis) & bit, 1 << i, 0)
+        for i, (_, parity) in enumerate(stage):
+            odd = jnp.int32(0)
+            for axis, mask in zip(("dom", "rows"), parity):
+                for bit in powers_of_two(1, 2 * mask) if mask else []:
+                    odd ^= jnp.where(lax.axis_index(axis) & bit & mask, 1, 0)
+            index += odd << i
     return index
 
 
@@ -124,11 +119,8 @@
     return keep[:part], rider_bf.astype(jnp.float32), messages
 
 
-def exchange(messages, stage, last_first):
-    routes = list(zip(messages, partner_masks(stage)))
-    if last_first:
-        return [swapped(message, *masks) for message, masks in routes[::-1]][::-1]
-    return [swapped(message, *masks) for message, masks in routes]
+def exchange(messages, stage):
+    return [swapped(message, *masks) for message, masks in zip(messages, partner_masks(stage))]
 
 
 def added(keep, rider, arrived):
@@ -139,7 +131,7 @@
 
 
 def gathered(held, stage):
-    return jnp.concatenate([held] + exchange([held] * ((1 << len(stage)) - 1), stage, True), axis=0)
+    return jnp.concatenate([held] + exchange([held] * ((1 << len(stage)) - 1), stage), axis=0)
 
 
 def listed_rows(dom, send_ref, row_count):
@@ -484,7 +476,7 @@
     ext_rows = TILE + row_count + slots + padded
     nodes = row_count * lax.axis_size("dom") * lax.axis_size("rows")
     stages = exchange_stages(lax.axis_size("dom"), lax.axis_size("rows"))
-    scattered = scattered_stages(stages, 4 * width)
+    scattered = stages[:3]
     rows_per_piece = 4 * width >> sum(len(stage) for stage in scattered)
     place = jnp.stack([lax.axis_index("dom").astype(jnp.int32), own_piece(scattered)])
     bf16, f32 = jnp.bfloat16, jnp.float32
@@ -554,7 +546,7 @@
     *direct, through, keep, message, rider = results
 
     rider = rounded(rider).astype(f32)
-    keep, rider = added(keep, rider, exchange([message], stages[0], False))
+    keep, rider = added(keep, rider, exchange([message], stages[0]))
     through = swapped(through, 1, 0)
     halo_back = shifted(halo_feat, "rows", -1)
     for at, stage in enumerate(stages[1:], 1):
@@ -562,9 +554,9 @@
         if at == 1:
             through, _ = lax.optimization_barrier((through, messages))
             returned = handed_on(direct, through)
-        if at == 2:
+        if at == 3:
             messages, returned = lax.optimization_barrier((messages, returned))
-        keep, rider = added(keep, rider, exchange(messages, stage, False))
+        keep, rider = added(keep, rider, exchange(messages, stage))
     (grad_features,) = call(
         return_kernel,
         "return_rows",
@@ -573,11 +565,10 @@
         [pltpu.VMEM(send_rows.shape, jnp.int32)],
         fetched=1,
     )
-    held = rounded(keep)
-    for stage in reversed(scattered[2:]):
-        held = gathered(held, stage)
-    held, grad_features = lax.optimization_barrier((held, grad_features))
-    near = [held] + exchange([held] * ((1 << len(scattered[1])) - 1), scattered[1], True)
+    held, grad_features = lax.optimization_barrier((rounded(keep), grad_features))
+    held = gathered(held, scattered[2])
+    square = partner_masks(scattered[1])
+    near = [held] + [swapped(held, *masks) for masks in square[::-1]][::-1]
     far = [swapped(block, *partner_masks(scattered[0])[0]) for block in near]
     grad_wq, grad_wkv, grad_wo = call(
         functools.partial(place_kernel, rows_per_piece),

time: 68.8 us -> 69.3 us (level)
  waiting for transfers between devices: 19.2 us -> 28.5 us
  starting transfers between devices: 29.2 us -> 20.5 us
    ppermute x25 -> x22, starting transfers between devices: 29.2 us -> 19.2 us  [swapped(): return lax.ppermute(block, ('dom', 'rows'), route)]
    ppermute x25 -> x22, waiting for transfers between devices: 19.2 us -> 28.5 us  [swapped(): return lax.ppermute(block, ('dom', 'rows'), route)]
    ppermute x2, starting transfers between devices: 0.01 us -> 1.3 us  [shifted(): return lax.ppermute(block, axis, route)]
  transfers between devices with their start and end apart: 27 -> 24, of which waited for: 14 -> 13; matrix products, arithmetic and copies ran while one was open for 2% -> 2% of each run, Pallas kernels for 9% -> 9%
where the time goes in v6:
time: 69.3 us; the launch traced here: 69 us
  waiting for transfers between devices  28.5 us (41%)
  starting transfers between devices  20.5 us (30%)
  Pallas kernels  17.9 us (26%)
  other arithmetic  1.09 us (2%)
  between operations  0.9 us (1%)
    ppermute x22, waiting for transfers between devices, swapped(): return lax.ppermute(block, ('dom', 'rows'), route)  28.5 us
    ppermute x22, starting transfers between devices, swapped(): return lax.ppermute(block, ('dom', 'rows'), route)  19.2 us
    pallas_call x5, Pallas kernels, call(): pl.pallas_call(kernel, out_shape=outs, in_specs=[pl.BlockSpec(memory_spac...  17.9 us
  transfers between devices with their start and end apart: 24, of which 13 were waited for; matrix products, arithmetic and copies ran while one was open for 2% of the time, Pallas kernels for 9%

profile of v6, /device:TPU:0, one launch (start us, length us, event | category | flops | bytes accessed | tf_op | source)
XLA Modules:
  0.0 69.0 jit_solution(7957787278727956358)
XLA Ops:
  0.7 0.1 pad_add_fusion.place_ref
  0.7 1.8 %pick_rows.1 = (bf16[128,384]{1,0:T(8,128)(2,1)S(1)}, bf16[128,384]{1,0:T(8,128)(2,1)S(1)}, bf16[32,384]{1,0:T(8,128)(2,1)S(1)}, bf16[32,384]{1,0:T(8,128)(2,1)S...) custom-call(s32[2]{0:T(128)S(1)} %pad_add_fusion.place_ref, bf16[256,384]{1,0:T(8,128)(2,1)} %feat_hbm.3, ...), custom_call_target="tpu_custom_call" | custom-call | bytes 492552 | tf_op jit(solution)/shard_map/pick_rows/pallas_call | solution.py:458
  2.5 3.0 %collective-permute-start.1 = (bf16[128,384]{1,0:T(8,128)(2,1)S(1)}, bf16[128,384]{1,0:T(8,128)(2,1)S(1)}, u32[]{:S(2)}, u32[]{:S(2)}) collective-permute-start(bf16[128,384]{1,0:T(8,128)(2,1)S(1)} %get-tuple-element.45), channel_id=1, source_target_pairs={{0,4},{1,5},{2,6},{3,7},{4,0},{5,1},{6,2},{7,3},{8,12},{9,13},{10,... | collective-permute-start | bytes 294920 | tf_op jit(solution)/shard_map/ppermute | solution.py:82
  5.5 2.8 %collective-permute-done.1.refs_1_ = bf16[128,384]{1,0:T(8,128)(2,1)S(1)} collective-permute-done((bf16[128,384]{1,0:T(8,128)(2,1)S(1)}, bf16[128,384]{1,0:T(8,128)(2,1)S(1)}, u32[]{:S(2)}, u32[]{:S(2)}) %collective-permute-start.1) | collective-permute-done | bytes 98336 | tf_op jit(solution)/shard_map/ppermute | solution.py:82
  8.3 2.0 %collective-permute-start.2 = (bf16[64,384]{1,0:T(8,128)(2,1)S(1)}, bf16[64,384]{1,0:T(8,128)(2,1)S(1)}, u32[]{:S(2)}, u32[]{:S(2)}) collective-permute-start(bf16[64,384]{1,0:T(8,128)(2,1)S(1)} %pad_maximum_fusion.5), channel_id=1, source_target_pairs={{0,8},{1,9},{2,10},{3,11},{4,12},{5,13},{6,14},{7,15},{8,0},{9,1},... | collective-permute-start | bytes 147464 | tf_op jit(solution)/shard_map/ppermute | solution.py:82
  10.3 2.6 %collective-permute-start.3 = (bf16[64,384]{1,0:T(8,128)(2,1)S(1)}, bf16[64,384]{1,0:T(8,128)(2,1)S(1)}, u32[]{:S(2)}, u32[]{:S(2)}) collective-permute-start(bf16[64,384]{1,0:T(8,128)(2,1)S(1)} %pad_maximum_fusion.6), channel_id=1, source_target_pairs={{0,16},{1,17},{2,18},{3,19},{4,20},{5,21},{6,22},{7,23},{8,24},{9,... | collective-permute-start | bytes 147464 | tf_op jit(solution)/shard_map/ppermute | solution.py:82
  12.9 3.5 %prepare.1 = (bf16[256,384]{1,0:T(8,128)(2,1)S(1)}, bf16[384,384]{1,0:T(8,128)(2,1)S(1)}, bf16[384,768]{1,0:T(8,128)(2,1)S(1)}, bf16[384,272]{1,0:T(8,128)(2,1)S...) custom-call(s32[2]{0:T(128)S(1)} %pad_add_fusion.place_ref, ...), custom_call_target="tpu_custom_call" | custom-call | flops 377487360 | bytes 4656136 | tf_op jit(solution)/shard_map/prepare/pallas_call | solution.py:458
  16.4 0.0 collective-permute-done.2.refs_2_
  16.4 0.0 collective-permute-done.3.refs_3_
  16.4 2.4 %collective-permute-done.4.refs_4_ = bf16[64,384]{1,0:T(8,128)(2,1)S(1)} collective-permute-done((bf16[64,384]{1,0:T(8,128)(2,1)S(1)}, bf16[64,384]{1,0:T(8,128)(2,1)S(1)}, u32[]{:S(2)}, u32[]{:S(2)}) %collective-permute-start.4) | collective-permute-done | bytes 49184 | tf_op jit(solution)/shard_map/ppermute | solution.py:82
  18.8 8.1 %attend.1 = (f32[256,384]{1,0:T(8,128)S(1)}, bf16[128,384]{1,0:T(8,128)(2,1)S(1)}, bf16[32,384]{1,0:T(8,128)(2,1)S(1)}, bf16[32,384]{1,0:T(8,128)(2,1)S(1)}, bf1...) custom-call(s32[2]{0:T(128)S(1)} %pad_add_fusion.place_ref, ...), custom_call_target="tpu_custom_call" | custom-call | flops 3095396352 | bytes 5922824 | tf_op jit(solution)/shard_map/attend/pallas_call | solution.py:458
  26.9 0.1 collective-permute-start.5
  27.0 1.6 %collective-permute-start.10 = (bf16[128,384]{1,0:T(8,128)(2,1)S(1)}, bf16[128,384]{1,0:T(8,128)(2,1)S(1)}, u32[]{:S(2)}, u32[]{:S(2)}) collective-permute-start(bf16[128,384]{1,0:T(8,128)(2,1)S(1)} %get-tuple-element.63), channel_id=1, source_target_pairs={{0,4},{1,5},{2,6},{3,7},{4,0},{5,1},{6,2},{7,3},{8,12},{9,13},{10,... | collective-permute-start | bytes 294920 | tf_op jit(solution)/shard_map/ppermute | solution.py:82
  28.6 1.3 %collective-permute-start.15 = (bf16[128,384]{1,0:T(8,128)(2,1)S(1)}, bf16[128,384]{1,0:T(8,128)(2,1)S(1)}, u32[]{:S(2)}, u32[]{:S(2)}) collective-permute-start(bf16[128,384]{1,0:T(8,128)(2,1)S(1)} %get-tuple-element.70), channel_id=1, source_target_pairs={{1,0},{2,1},{3,2},{0,3},{5,4},{6,5},{7,6},{4,7},{9,8},{10,9},{11,1... | collective-permute-start | bytes 294920 | tf_op jit(solution)/shard_map/ppermute | solution.py:88
  29.9 0.2 fusion.2
  30.1 0.1 pad_maximum_fusion.2
  30.1 1.7 %collective-permute-start.6 = (bf16[208,384]{1,0:T(8,128)(2,1)S(1)}, bf16[208,384]{1,0:T(8,128)(2,1)S(1)}, u32[]{:S(2)}, u32[]{:S(2)}) collective-permute-start(bf16[208,384]{1,0:T(8,128)(2,1)S(1)} %get-tuple-element.92), channel_id=1, source_target_pairs={{0,6},{1,7},{2,4},{3,5},{4,2},{5,3},{6,0},{7,1},{8,14},{9,15},{10,... | collective-permute-start | bytes 479240 | tf_op jit(solution)/shard_map/ppermute | solution.py:82
  31.8 0.5 collective-permute-start.7
  32.3 1.4 %collective-permute-start.8 = (bf16[208,384]{1,0:T(8,128)(2,1)S(1)}, bf16[208,384]{1,0:T(8,128)(2,1)S(1)}, u32[]{:S(2)}, u32[]{:S(2)}) collective-permute-start(bf16[208,384]{1,0:T(8,128)(2,1)S(1)} %get-tuple-element.94), channel_id=1, source_target_pairs={{0,2},{1,3},{2,0},{3,1},{4,6},{5,7},{6,4},{7,5},{8,10},{9,11},{10,... | collective-permute-start | bytes 479240 | tf_op jit(solution)/shard_map/ppermute | solution.py:82
  33.7 0.1 collective-permute-start.11
  33.8 4.3 %collective-permute-done.6 = bf16[208,384]{1,0:T(8,128)(2,1)S(1)} collective-permute-done((bf16[208,384]{1,0:T(8,128)(2,1)S(1)}, bf16[208,384]{1,0:T(8,128)(2,1)S(1)}, u32[]{:S(2)}, u32[]{:S(2)}) %collective-permute-start.6) | collective-permute-done | bytes 159776 | tf_op jit(solution)/shard_map/ppermute | solution.py:82
  38.2 1.8 %collective-permute-done.7 = bf16[208,384]{1,0:T(8,128)(2,1)S(1)} collective-permute-done((bf16[208,384]{1,0:T(8,128)(2,1)S(1)}, bf16[208,384]{1,0:T(8,128)(2,1)S(1)}, u32[]{:S(2)}, u32[]{:S(2)}) %collective-permute-start.7) | collective-permute-done | bytes 159776 | tf_op jit(solution)/shard_map/ppermute | solution.py:82
  39.9 0.1 collective-permute-done.8
  40.0 0.1 fusion
  40.1 0.2 collective-permute-start.9
  40.4 2.4 %collective-permute-start.13 = (bf16[64,384]{1,0:T(8,128)(2,1)S(1)}, bf16[64,384]{1,0:T(8,128)(2,1)S(1)}, u32[]{:S(2)}, u32[]{:S(2)}) collective-permute-start(bf16[64,384]{1,0:T(8,128)(2,1)S(1)} %pad_maximum_fusion.10), channel_id=1, source_target_pairs={{0,24},{1,25},{2,26},{3,27},{4,28},{5,29},{6,30},{7,31},{8,16},{9,... | collective-permute-start | bytes 147464 | tf_op jit(solution)/shard_map/ppermute | solution.py:82
  42.8 2.5 %collective-permute-done.9 = bf16[112,384]{1,0:T(8,128)(2,1)S(1)} collective-permute-done((bf16[112,384]{1,0:T(8,128)(2,1)S(1)}, bf16[112,384]{1,0:T(8,128)(2,1)S(1)}, u32[]{:S(2)}, u32[]{:S(2)}) %collective-permute-start.9) | collective-permute-done | bytes 86048 | tf_op jit(solution)/shard_map/ppermute | solution.py:82
  45.3 0.0 collective-permute-done.12.refs_3_
  45.3 1.0 %collective-permute-done.13.refs_4_ = bf16[64,384]{1,0:T(8,128)(2,1)S(1)} collective-permute-done((bf16[64,384]{1,0:T(8,128)(2,1)S(1)}, bf16[64,384]{1,0:T(8,128)(2,1)S(1)}, u32[]{:S(2)}, u32[]{:S(2)}) %collective-permute-start.13) | collective-permute-done | bytes 49184 | tf_op jit(solution)/shard_map/ppermute | solution.py:82
  46.4 0.1 collective-permute-start.14
  46.5 2.5 %return_rows.1 = f32[256,384]{1,0:T(8,128)} custom-call(s32[2]{0:T(128)S(1)} %pad_add_fusion.place_ref, s32[8,32]{1,0:T(8,128)} %send_hbm.3, f32[256,384]{1,0:T(8,128)S(1)} %get-tuple-element.69.gf_ref, bf16[128,384]{1,0:T(8,128)(2,1)S(1)} %collective-permute-done.15.halo_ref, bf16[32,384]{1,0:T(8,128)(2,1)S(1)} %get-tuple-element.71.refs_0_, ...), custom_call_target="tpu_custom_call" | custom-call | bytes 1156104 | tf_op jit(solution)/shard_map/return_rows/pallas_call | solution.py:458
  48.9 3.2 %collective-permute-done.14 = bf16[112,384]{1,0:T(8,128)(2,1)S(1)} collective-permute-done((bf16[112,384]{1,0:T(8,128)(2,1)S(1)}, bf16[112,384]{1,0:T(8,128)(2,1)S(1)}, u32[]{:S(2)}, u32[]{:S(2)}) %collective-permute-start.14) | collective-permute-done | bytes 86048 | tf_op jit(solution)/shard_map/ppermute | solution.py:82
  52.2 0.1 collective-permute-start.16
  52.3 4.3 %collective-permute-done.16 = bf16[96,384]{1,0:T(8,128)(2,1)S(1)} collective-permute-done((bf16[96,384]{1,0:T(8,128)(2,1)S(1)}, bf16[96,384]{1,0:T(8,128)(2,1)S(1)}, u32[]{:S(2)}, u32[]{:S(2)}) %collective-permute-start.16) | collective-permute-done | bytes 73760 | tf_op jit(solution)/shard_map/ppermute | solution.py:82
  56.6 1.4 %collective-permute-start.19 = (bf16[192,384]{1,0:T(8,128)(2,1)S(1)}, bf16[192,384]{1,0:T(8,128)(2,1)S(1)}, u32[]{:S(2)}, u32[]{:S(2)}) collective-permute-start(bf16[192,384]{1,0:T(8,128)(2,1)S(1)} %constant_dynamic-update-slice_fusion.refs_0_), channel_id=1, source_target_pairs={{0,2},{1,3},{2,0},{3,1},{4,6},{5,7},{6,4},{7,5},{8,10},{9,11},{10,... | collective-permute-start | bytes 442376 | tf_op jit(solution)/shard_map/ppermute | solution.py:82
  58.0 1.5 %collective-permute-start.18 = (bf16[192,384]{1,0:T(8,128)(2,1)S(1)}, bf16[192,384]{1,0:T(8,128)(2,1)S(1)}, u32[]{:S(2)}, u32[]{:S(2)}) collective-permute-start(bf16[192,384]{1,0:T(8,128)(2,1)S(1)} %constant_dynamic-update-slice_fusion.refs_0_), channel_id=1, source_target_pairs={{0,4},{1,5},{2,6},{3,7},{4,0},{5,1},{6,2},{7,3},{8,12},{9,13},{10,... | collective-permute-start | bytes 442376 | tf_op jit(solution)/shard_map/ppermute | solution.py:82
  59.5 0.7 %collective-permute-start.17 = (bf16[192,384]{1,0:T(8,128)(2,1)S(1)}, bf16[192,384]{1,0:T(8,128)(2,1)S(1)}, u32[]{:S(2)}, u32[]{:S(2)}) collective-permute-start(bf16[192,384]{1,0:T(8,128)(2,1)S(1)} %constant_dynamic-update-slice_fusion.refs_0_), channel_id=1, source_target_pairs={{0,6},{1,7},{2,4},{3,5},{4,2},{5,3},{6,0},{7,1},{8,14},{9,15},{10,... | collective-permute-start | bytes 442376 | tf_op jit(solution)/shard_map/ppermute | solution.py:82
  60.2 0.0 collective-permute-start.20
  60.2 2.0 %collective-permute-done.19.refs_3_ = bf16[192,384]{1,0:T(8,128)(2,1)S(1)} collective-permute-done((bf16[192,384]{1,0:T(8,128)(2,1)S(1)}, bf16[192,384]{1,0:T(8,128)(2,1)S(1)}, u32[]{:S(2)}, u32[]{:S(2)}) %collective-permute-start.19) | collective-permute-done | bytes 147488 | tf_op jit(solution)/shard_map/ppermute | solution.py:82
  62.1 0.0 collective-permute-start.23
  62.1 1.0 %collective-permute-done.18.refs_2_ = bf16[192,384]{1,0:T(8,128)(2,1)S(1)} collective-permute-done((bf16[192,384]{1,0:T(8,128)(2,1)S(1)}, bf16[192,384]{1,0:T(8,128)(2,1)S(1)}, u32[]{:S(2)}, u32[]{:S(2)}) %collective-permute-start.18) | collective-permute-done | bytes 147488 | tf_op jit(solution)/shard_map/ppermute | solution.py:82
  63.1 0.0 collective-permute-start.22
  63.1 2.4 %collective-permute-done.17.refs_1_ = bf16[192,384]{1,0:T(8,128)(2,1)S(1)} collective-permute-done((bf16[192,384]{1,0:T(8,128)(2,1)S(1)}, bf16[192,384]{1,0:T(8,128)(2,1)S(1)}, u32[]{:S(2)}, u32[]{:S(2)}) %collective-permute-start.17) | collective-permute-done | bytes 147488 | tf_op jit(solution)/shard_map/ppermute | solution.py:82
  65.5 0.0 collective-permute-start.21
  65.5 0.6 convert_add_fusion.1
  66.1 0.0 collective-permute-done.20.refs_4_
  66.1 0.8 %collective-permute-done.21.refs_5_ = bf16[192,384]{1,0:T(8,128)(2,1)S(1)} collective-permute-done((bf16[192,384]{1,0:T(8,128)(2,1)S(1)}, bf16[192,384]{1,0:T(8,128)(2,1)S(1)}, u32[]{:S(2)}, u32[]{:S(2)}) %collective-permute-start.21) | collective-permute-done | bytes 147488 | tf_op jit(solution)/shard_map/ppermute | solution.py:82
  66.9 2.1 %place_sums.1 = (f32[384,384]{1,0:T(8,128)}, f32[384,768]{1,0:T(8,128)}, f32[384,384]{1,0:T(8,128)}) custom-call(s32[2]{0:T(128)S(1)} %pad_add_fusion.place_ref, bf16[192,384]{1,0:T(8,128)(2,1)S(1)} %constant_dynamic-update-slice_fusion.refs_0_, bf16[192,384]{1,0:T(8,128)(2,1)S(1)} %collective-permute-done.17.refs_1_, ...), custom_call_target="tpu_custom_call" | custom-call | bytes 3538952 | tf_op jit(solution)/shard_map/place_sums/pallas_call | solution.py:458
  (30 shorter events, 0.3 us)
Async XLA Ops:
  2.5 5.8 %collective-permute-start.1 = (bf16[128,384]{1,0:T(8,128)(2,1)S(1)}, bf16[128,384]{1,0:T(8,128)(2,1)S(1)}, u32[]{:S(2)}, u32[]{:S(2)}) collective-permute-start(bf16[128,384]{1,0:T(8,128)(2,1)S(1)} %get-tuple-element.45), channel_id=1, source_target_pairs={{0,4},{1,5},{2,6},{3,7},{4,0},{5,1},{6,2},{7,3},{8,12},{9,13},{10,... | collective-permute-start | bytes 294920 | tf_op jit(solution)/shard_map/ppermute | solution.py:82
  5.5 10.9 %collective-permute-start = (bf16[128,384]{1,0:T(8,128)(2,1)S(1)}, bf16[128,384]{1,0:T(8,128)(2,1)S(1)}, u32[]{:S(2)}, u32[]{:S(2)}) collective-permute-start(bf16[128,384]{1,0:T(8,128)(2,1)S(1)} %get-tuple-element.43), channel_id=1, source_target_pairs={{3,0},{0,1},{1,2},{2,3},{7,4},{4,5},{5,6},{6,7},{11,8},{8,9},{9,10... | collective-permute-start | bytes 294920 | tf_op jit(solution)/shard_map/ppermute | solution.py:88
  8.3 8.1 %collective-permute-start.2 = (bf16[64,384]{1,0:T(8,128)(2,1)S(1)}, bf16[64,384]{1,0:T(8,128)(2,1)S(1)}, u32[]{:S(2)}, u32[]{:S(2)}) collective-permute-start(bf16[64,384]{1,0:T(8,128)(2,1)S(1)} %pad_maximum_fusion.5), channel_id=1, source_target_pairs={{0,8},{1,9},{2,10},{3,11},{4,12},{5,13},{6,14},{7,15},{8,0},{9,1},... | collective-permute-start | bytes 147464 | tf_op jit(solution)/shard_map/ppermute | solution.py:82
  10.3 6.1 %collective-permute-start.3 = (bf16[64,384]{1,0:T(8,128)(2,1)S(1)}, bf16[64,384]{1,0:T(8,128)(2,1)S(1)}, u32[]{:S(2)}, u32[]{:S(2)}) collective-permute-start(bf16[64,384]{1,0:T(8,128)(2,1)S(1)} %pad_maximum_fusion.6), channel_id=1, source_target_pairs={{0,16},{1,17},{2,18},{3,19},{4,20},{5,21},{6,22},{7,23},{8,24},{9,... | collective-permute-start | bytes 147464 | tf_op jit(solution)/shard_map/ppermute | solution.py:82
  12.9 5.9 %collective-permute-start.4 = (bf16[64,384]{1,0:T(8,128)(2,1)S(1)}, bf16[64,384]{1,0:T(8,128)(2,1)S(1)}, u32[]{:S(2)}, u32[]{:S(2)}) collective-permute-start(bf16[64,384]{1,0:T(8,128)(2,1)S(1)} %pad_maximum_fusion.7), channel_id=1, source_target_pairs={{0,24},{1,25},{2,26},{3,27},{4,28},{5,29},{6,30},{7,31},{8,16},{9,... | collective-permute-start | bytes 147464 | tf_op jit(solution)/shard_map/ppermute | solution.py:82
  26.9 2.9 %collective-permute-start.5 = (bf16[784,384]{1,0:T(8,128)(2,1)S(1)}, bf16[784,384]{1,0:T(8,128)(2,1)S(1)}, u32[]{:S(2)}, u32[]{:S(2)}) collective-permute-start(bf16[784,384]{1,0:T(8,128)(2,1)S(1)} %get-tuple-element.60), channel_id=1, source_target_pairs={{0,1},{1,0},{2,3},{3,2},{4,5},{5,4},{6,7},{7,6},{8,9},{9,8},{10,11... | collective-permute-start | bytes 1806344 | tf_op jit(solution)/shard_map/ppermute | solution.py:82
  27.0 6.7 %collective-permute-start.10 = (bf16[128,384]{1,0:T(8,128)(2,1)S(1)}, bf16[128,384]{1,0:T(8,128)(2,1)S(1)}, u32[]{:S(2)}, u32[]{:S(2)}) collective-permute-start(bf16[128,384]{1,0:T(8,128)(2,1)S(1)} %get-tuple-element.63), channel_id=1, source_target_pairs={{0,4},{1,5},{2,6},{3,7},{4,0},{5,1},{6,2},{7,3},{8,12},{9,13},{10,... | collective-permute-start | bytes 294920 | tf_op jit(solution)/shard_map/ppermute | solution.py:82
  28.6 17.9 %collective-permute-start.15 = (bf16[128,384]{1,0:T(8,128)(2,1)S(1)}, bf16[128,384]{1,0:T(8,128)(2,1)S(1)}, u32[]{:S(2)}, u32[]{:S(2)}) collective-permute-start(bf16[128,384]{1,0:T(8,128)(2,1)S(1)} %get-tuple-element.70), channel_id=1, source_target_pairs={{1,0},{2,1},{3,2},{0,3},{5,4},{6,5},{7,6},{4,7},{9,8},{10,9},{11,1... | collective-permute-start | bytes 294920 | tf_op jit(solution)/shard_map/ppermute | solution.py:88
  30.1 8.0 %collective-permute-start.6 = (bf16[208,384]{1,0:T(8,128)(2,1)S(1)}, bf16[208,384]{1,0:T(8,128)(2,1)S(1)}, u32[]{:S(2)}, u32[]{:S(2)}) collective-permute-start(bf16[208,384]{1,0:T(8,128)(2,1)S(1)} %get-tuple-element.92), channel_id=1, source_target_pairs={{0,6},{1,7},{2,4},{3,5},{4,2},{5,3},{6,0},{7,1},{8,14},{9,15},{10,... | collective-permute-start | bytes 479240 | tf_op jit(solution)/shard_map/ppermute | solution.py:82
  31.8 8.1 %collective-permute-start.7 = (bf16[208,384]{1,0:T(8,128)(2,1)S(1)}, bf16[208,384]{1,0:T(8,128)(2,1)S(1)}, u32[]{:S(2)}, u32[]{:S(2)}) collective-permute-start(bf16[208,384]{1,0:T(8,128)(2,1)S(1)} %get-tuple-element.93), channel_id=1, source_target_pairs={{0,4},{1,5},{2,6},{3,7},{4,0},{5,1},{6,2},{7,3},{8,12},{9,13},{10,... | collective-permute-start | bytes 479240 | tf_op jit(solution)/shard_map/ppermute | solution.py:82
  32.3 7.7 %collective-permute-start.8 = (bf16[208,384]{1,0:T(8,128)(2,1)S(1)}, bf16[208,384]{1,0:T(8,128)(2,1)S(1)}, u32[]{:S(2)}, u32[]{:S(2)}) collective-permute-start(bf16[208,384]{1,0:T(8,128)(2,1)S(1)} %get-tuple-element.94), channel_id=1, source_target_pairs={{0,2},{1,3},{2,0},{3,1},{4,6},{5,7},{6,4},{7,5},{8,10},{9,11},{10,... | collective-permute-start | bytes 479240 | tf_op jit(solution)/shard_map/ppermute | solution.py:82
  33.7 11.6 %collective-permute-start.11 = (bf16[64,384]{1,0:T(8,128)(2,1)S(1)}, bf16[64,384]{1,0:T(8,128)(2,1)S(1)}, u32[]{:S(2)}, u32[]{:S(2)}) collective-permute-start(bf16[64,384]{1,0:T(8,128)(2,1)S(1)} %pad_maximum_fusion.8), channel_id=1, source_target_pairs={{0,8},{1,9},{2,10},{3,11},{4,12},{5,13},{6,14},{7,15},{8,0},{9,1},... | collective-permute-start | bytes 147464 | tf_op jit(solution)/shard_map/ppermute | solution.py:82
  38.2 7.2 %collective-permute-start.12 = (bf16[64,384]{1,0:T(8,128)(2,1)S(1)}, bf16[64,384]{1,0:T(8,128)(2,1)S(1)}, u32[]{:S(2)}, u32[]{:S(2)}) collective-permute-start(bf16[64,384]{1,0:T(8,128)(2,1)S(1)} %pad_maximum_fusion.9), channel_id=1, source_target_pairs={{0,16},{1,17},{2,18},{3,19},{4,20},{5,21},{6,22},{7,23},{8,24},{9,... | collective-permute-start | bytes 147464 | tf_op jit(solution)/shard_map/ppermute | solution.py:82
  40.1 5.1 %collective-permute-start.9 = (bf16[112,384]{1,0:T(8,128)(2,1)S(1)}, bf16[112,384]{1,0:T(8,128)(2,1)S(1)}, u32[]{:S(2)}, u32[]{:S(2)}) collective-permute-start(bf16[112,384]{1,0:T(8,128)(2,1)S(1)} %pad_maximum_fusion.3), channel_id=1, source_target_pairs={{0,8},{1,9},{2,10},{3,11},{4,12},{5,13},{6,14},{7,15},{8,0},{9,1},... | collective-permute-start | bytes 258056 | tf_op jit(solution)/shard_map/ppermute | solution.py:82
  40.4 6.0 %collective-permute-start.13 = (bf16[64,384]{1,0:T(8,128)(2,1)S(1)}, bf16[64,384]{1,0:T(8,128)(2,1)S(1)}, u32[]{:S(2)}, u32[]{:S(2)}) collective-permute-start(bf16[64,384]{1,0:T(8,128)(2,1)S(1)} %pad_maximum_fusion.10), channel_id=1, source_target_pairs={{0,24},{1,25},{2,26},{3,27},{4,28},{5,29},{6,30},{7,31},{8,16},{9,... | collective-permute-start | bytes 147464 | tf_op jit(solution)/shard_map/ppermute | solution.py:82
  46.4 5.8 %collective-permute-start.14 = (bf16[112,384]{1,0:T(8,128)(2,1)S(1)}, bf16[112,384]{1,0:T(8,128)(2,1)S(1)}, u32[]{:S(2)}, u32[]{:S(2)}) collective-permute-start(bf16[112,384]{1,0:T(8,128)(2,1)S(1)} %pad_maximum_fusion.4), channel_id=1, source_target_pairs={{0,16},{1,17},{2,18},{3,19},{4,20},{5,21},{6,22},{7,23},{8,24},{9,... | collective-permute-start | bytes 258056 | tf_op jit(solution)/shard_map/ppermute | solution.py:82
  52.2 4.4 %collective-permute-start.16 = (bf16[96,384]{1,0:T(8,128)(2,1)S(1)}, bf16[96,384]{1,0:T(8,128)(2,1)S(1)}, u32[]{:S(2)}, u32[]{:S(2)}) collective-permute-start(bf16[96,384]{1,0:T(8,128)(2,1)S(1)} %add_convert_fusion), channel_id=1, source_target_pairs={{0,8},{1,9},{2,10},{3,11},{4,12},{5,13},{6,14},{7,15},{8,0},{9,1},... | collective-permute-start | bytes 221192 | tf_op jit(solution)/shard_map/ppermute | solution.py:82
  56.6 5.5 %collective-permute-start.19 = (bf16[192,384]{1,0:T(8,128)(2,1)S(1)}, bf16[192,384]{1,0:T(8,128)(2,1)S(1)}, u32[]{:S(2)}, u32[]{:S(2)}) collective-permute-start(bf16[192,384]{1,0:T(8,128)(2,1)S(1)} %constant_dynamic-update-slice_fusion.refs_0_), channel_id=1, source_target_pairs={{0,2},{1,3},{2,0},{3,1},{4,6},{5,7},{6,4},{7,5},{8,10},{9,11},{10,... | collective-permute-start | bytes 442376 | tf_op jit(solution)/shard_map/ppermute | solution.py:82
  58.0 5.1 %collective-permute-start.18 = (bf16[192,384]{1,0:T(8,128)(2,1)S(1)}, bf16[192,384]{1,0:T(8,128)(2,1)S(1)}, u32[]{:S(2)}, u32[]{:S(2)}) collective-permute-start(bf16[192,384]{1,0:T(8,128)(2,1)S(1)} %constant_dynamic-update-slice_fusion.refs_0_), channel_id=1, source_target_pairs={{0,4},{1,5},{2,6},{3,7},{4,0},{5,1},{6,2},{7,3},{8,12},{9,13},{10,... | collective-permute-start | bytes 442376 | tf_op jit(solution)/shard_map/ppermute | solution.py:82
  59.5 6.0 %collective-permute-start.17 = (bf16[192,384]{1,0:T(8,128)(2,1)S(1)}, bf16[192,384]{1,0:T(8,128)(2,1)S(1)}, u32[]{:S(2)}, u32[]{:S(2)}) collective-permute-start(bf16[192,384]{1,0:T(8,128)(2,1)S(1)} %constant_dynamic-update-slice_fusion.refs_0_), channel_id=1, source_target_pairs={{0,6},{1,7},{2,4},{3,5},{4,2},{5,3},{6,0},{7,1},{8,14},{9,15},{10,... | collective-permute-start | bytes 442376 | tf_op jit(solution)/shard_map/ppermute | solution.py:82
  60.2 5.9 %collective-permute-start.20 = (bf16[192,384]{1,0:T(8,128)(2,1)S(1)}, bf16[192,384]{1,0:T(8,128)(2,1)S(1)}, u32[]{:S(2)}, u32[]{:S(2)}) collective-permute-start(bf16[192,384]{1,0:T(8,128)(2,1)S(1)} %constant_dynamic-update-slice_fusion.refs_0_), channel_id=1, source_target_pairs={{0,1},{1,0},{2,3},{3,2},{4,5},{5,4},{6,7},{7,6},{8,9},{9,8},{10,11... | collective-permute-start | bytes 442376 | tf_op jit(solution)/shard_map/ppermute | solution.py:82
  62.1 4.0 %collective-permute-start.23 = (bf16[192,384]{1,0:T(8,128)(2,1)S(1)}, bf16[192,384]{1,0:T(8,128)(2,1)S(1)}, u32[]{:S(2)}, u32[]{:S(2)}) collective-permute-start(bf16[192,384]{1,0:T(8,128)(2,1)S(1)} %collective-permute-done.19.refs_3_), channel_id=1, source_target_pairs={{0,1},{1,0},{2,3},{3,2},{4,5},{5,4},{6,7},{7,6},{8,9},{9,8},{10,11... | collective-permute-start | bytes 442376 | tf_op jit(solution)/shard_map/ppermute | solution.py:82
  63.1 3.0 %collective-permute-start.22 = (bf16[192,384]{1,0:T(8,128)(2,1)S(1)}, bf16[192,384]{1,0:T(8,128)(2,1)S(1)}, u32[]{:S(2)}, u32[]{:S(2)}) collective-permute-start(bf16[192,384]{1,0:T(8,128)(2,1)S(1)} %collective-permute-done.18.refs_2_), channel_id=1, source_target_pairs={{0,1},{1,0},{2,3},{3,2},{4,5},{5,4},{6,7},{7,6},{8,9},{9,8},{10,11... | collective-permute-start | bytes 442376 | tf_op jit(solution)/shard_map/ppermute | solution.py:82
  65.5 1.4 %collective-permute-start.21 = (bf16[192,384]{1,0:T(8,128)(2,1)S(1)}, bf16[192,384]{1,0:T(8,128)(2,1)S(1)}, u32[]{:S(2)}, u32[]{:S(2)}) collective-permute-start(bf16[192,384]{1,0:T(8,128)(2,1)S(1)} %collective-permute-done.17.refs_1_), channel_id=1, source_target_pairs={{0,1},{1,0},{2,3},{3,2},{4,5},{5,4},{6,7},{7,6},{8,9},{9,8},{10,11... | collective-permute-start | bytes 442376 | tf_op jit(solution)/shard_map/ppermute | solution.py:82

commit v7 on v6

--- a/solution.py
+++ b/solution.py
@@ -100,11 +100,11 @@
 
 def handed_on(direct, through):
     rows = direct[0].shape[0]
-    arrived = [direct[0], through]
-    for at in range(1, len(direct)):
+    arrived = []
+    for at in reversed(range(1, len(direct))):
         message = jnp.concatenate([direct[at], through[at * rows : (at + 1) * rows]], axis=0)
         arrived.append(swapped(message, 2 * at, 0))
-    return arrived
+    return [direct[0], through] + arrived
 
 
 def scatter_stage(keep, rider, stage, halved):
@@ -294,7 +294,7 @@
     extt_ref[:, virt_at:] = featt_ref[:, row_count:]
     slot_ref[:per_peer] = piece_refs[0][...]
     slot_ref[per_peer : 2 * per_peer] = piece_refs[1][:per_peer]
-    for at, piece_ref in enumerate(piece_refs[2:], 1):
+    for at, piece_ref in enumerate(piece_refs[:1:-1], 1):
         slot_ref[2 * at * per_peer : (2 * at + 2) * per_peer] = piece_ref[...]
     for rows, source_ref in ((slice(0, tile), halo_ref), (slice(near, virt_at), slot_ref)):
         extt_ref[:, rows] = source_ref[...].T
@@ -409,23 +409,31 @@
 
 
 def place_kernel(rows_per_piece, place_ref, *refs):
-    part_refs, (gq_ref, gkv_ref, go_ref, all_ref) = refs[:-4], refs[-4:]
-    width = gq_ref.shape[0]
+    part_refs, (gq_hbm, gkv_hbm, go_hbm, all_ref, out_ref, sems) = refs[:-6], refs[-6:]
+    width = gq_hbm.shape[0]
     rows = part_refs[0].shape[0]
+    half = len(part_refs) // 2
     for at, part_ref in enumerate(part_refs):
-        all_ref[at * rows : (at + 1) * rows] = part_ref[...]
+        digit = at // half * half + -at % half
+        all_ref[digit * rows : (digit + 1) * rows] = part_ref[...]
+    copies = []
     for at in range(all_ref.shape[0] // rows_per_piece):
         offset = pl.multiple_of((place_ref[1] ^ at) * rows_per_piece, ROW_PACK)
-        value = all_ref[pl.ds(offset, rows_per_piece), :].astype(jnp.float32)
         start = at * rows_per_piece
-        rows = slice(start % width, start % width + rows_per_piece)
+        piece = slice(start, start + rows_per_piece)
+        out_ref[piece] = all_ref[pl.ds(offset, rows_per_piece), :].astype(jnp.float32)
+        rows_out = pl.ds(start % width, rows_per_piece)
         which = start // width
         if which == 0:
-            gq_ref[rows] = value
+            target = gq_hbm.at[rows_out]
         elif which == 3:
-            go_ref[rows] = value
+            target = go_hbm.at[rows_out]
         else:
-            gkv_ref[rows, (which - 1) * width : which * width] = value
+            target = gkv_hbm.at[rows_out, pl.ds((which - 1) * width, width)]
+        copies.append(pltpu.make_async_copy(out_ref.at[piece], target, sems.at[at]))
+        copies[-1].start()
+    for copy in copies:
+        copy.wait()
 
 
 def return_kernel(place_ref, send_hbm, gf_ref, halo_ref, *refs):
@@ -436,7 +444,7 @@
     per_peer = send_ref.shape[1]
     chosen = listed_rows(place_ref[0], send_ref, row_count)
     returned = jnp.concatenate(
-        [piece_refs[0][...], piece_refs[1][:per_peer]] + [ref[...] for ref in piece_refs[2:]],
+        [piece_refs[0][...], piece_refs[1][:per_peer]] + [ref[...] for ref in piece_refs[:1:-1]],
         axis=0,
     )
     total = gf_ref[...] + rows_contracted(chosen, returned)
@@ -444,7 +452,7 @@
     out_ref[row_count - tile :] = total[row_count - tile :] + halo_ref[...].astype(jnp.float32)
 
 
-def call(kernel, name, outs, args, scratch=(), fetched=0, flops=0):
+def call(kernel, name, outs, args, scratch=(), fetched=0, flops=0, stored=False):
     spaces = [pltpu.SMEM] + [pltpu.HBM] * fetched
     spaces += [pltpu.VMEM] * (len(args) - len(spaces))
     moved = sum(x.size * x.dtype.itemsize for x in list(args) + list(outs))
@@ -459,7 +467,7 @@
         kernel,
         out_shape=outs,
         in_specs=[pl.BlockSpec(memory_space=space) for space in spaces],
-        out_specs=[pl.BlockSpec(memory_space=pltpu.VMEM)] * len(outs),
+        out_specs=[pl.BlockSpec(memory_space=pl.ANY if stored else pltpu.VMEM)] * len(outs),
         scratch_shapes=scratch,
         compiler_params=pltpu.CompilerParams(vmem_limit_bytes=VMEM_BYTES),
         cost_estimate=pl.CostEstimate(flops=flops, bytes_accessed=moved, transcendentals=0),
@@ -548,14 +556,16 @@
     rider = rounded(rider).astype(f32)
     keep, rider = added(keep, rider, exchange([message], stages[0]))
     through = swapped(through, 1, 0)
-    halo_back = shifted(halo_feat, "rows", -1)
     for at, stage in enumerate(stages[1:], 1):
         keep, rider, messages = scatter_stage(keep, rider, stage, stage in scattered)
         if at == 1:
             through, _ = lax.optimization_barrier((through, messages))
             returned = handed_on(direct, through)
-        if at == 3:
-            messages, returned = lax.optimization_barrier((messages, returned))
+        if at == 2:
+            messages, returned, halo_feat = lax.optimization_barrier(
+                (messages, returned, halo_feat)
+            )
+            halo_back = shifted(halo_feat, "rows", -1)
         keep, rider = added(keep, rider, exchange(messages, stage))
     (grad_features,) = call(
         return_kernel,
@@ -568,14 +578,19 @@
     held, grad_features = lax.optimization_barrier((rounded(keep), grad_features))
     held = gathered(held, scattered[2])
     square = partner_masks(scattered[1])
-    near = [held] + [swapped(held, *masks) for masks in square[::-1]][::-1]
+    near = [held] + [swapped(held, *masks) for masks in square[::-1]]
     far = [swapped(block, *partner_masks(scattered[0])[0]) for block in near]
     grad_wq, grad_wkv, grad_wo = call(
         functools.partial(place_kernel, rows_per_piece),
         "place_sums",
         [shape((width, width), f32), shape((width, 2 * width), f32), shape((width, width), f32)],
         [place, *near, *far],
-        [pltpu.VMEM((4 * width, width), bf16)],
+        [
+            pltpu.VMEM((4 * width, width), bf16),
+            pltpu.VMEM((4 * width, width), f32),
+            pltpu.SemaphoreType.DMA((4 * width // rows_per_piece,)),
+        ],
+        stored=True,
     )
     return grad_features, grad_wq, grad_wkv, grad_wo, rider[:virt_rows]
 

time: 69.3 us -> 67.4 us (0.973)
  waiting for transfers between devices: 28.5 us -> 24.4 us
  starting transfers between devices: 20.5 us -> 22.7 us
    ppermute x22, waiting for transfers between devices: 28.5 us -> 24.4 us  [swapped(): return lax.ppermute(block, ('dom', 'rows'), route)]
    ppermute x22, starting transfers between devices: 19.2 us -> 22.7 us  [swapped(): return lax.ppermute(block, ('dom', 'rows'), route)]
    ppermute x2, starting transfers between devices: 1.3 us -> 0.01 us  [shifted(): return lax.ppermute(block, axis, route)]
  transfers between devices with their start and end apart: 24 -> 24, of which waited for: 13 -> 16; matrix products, arithmetic and copies ran while one was open for 2% -> 2% of each run, Pallas kernels for 9% -> 9%
where the time goes in v7:
time: 67.4 us; the launch traced here: 67.1 us
  waiting for transfers between devices  24.4 us (36%)
  starting transfers between devices  22.7 us (34%)
  Pallas kernels  18 us (27%)
  other arithmetic  1.09 us (2%)
  between operations  0.89 us (1%)
    ppermute x22, waiting for transfers between devices, swapped(): return lax.ppermute(block, ('dom', 'rows'), route)  24.4 us
    ppermute x22, starting transfers between devices, swapped(): return lax.ppermute(block, ('dom', 'rows'), route)  22.7 us
    pallas_call x5, Pallas kernels, call(): pl.pallas_call(kernel, out_shape=outs, in_specs=[pl.BlockSpec(memory_spac...  18 us
  transfers between devices with their start and end apart: 24, of which 16 were waited for; matrix products, arithmetic and copies ran while one was open for 2% of the time, Pallas kernels for 9%

profile of v7, /device:TPU:0, one launch (start us, length us, event | category | flops | bytes accessed | tf_op | source)
XLA Modules:
  0.0 67.1 jit_solution(12347060455764659467)
XLA Ops:
  0.7 0.1 pad_add_fusion.place_ref
  0.7 1.8 %pick_rows.1 = (bf16[128,384]{1,0:T(8,128)(2,1)S(1)}, bf16[128,384]{1,0:T(8,128)(2,1)S(1)}, bf16[32,384]{1,0:T(8,128)(2,1)S(1)}, bf16[32,384]{1,0:T(8,128)(2,1)S...) custom-call(s32[2]{0:T(128)S(1)} %pad_add_fusion.place_ref, bf16[256,384]{1,0:T(8,128)(2,1)} %feat_hbm.3, ...), custom_call_target="tpu_custom_call" | custom-call | bytes 492552 | tf_op jit(solution)/shard_map/pick_rows/pallas_call | solution.py:466
  2.5 3.0 %collective-permute-start.1 = (bf16[128,384]{1,0:T(8,128)(2,1)S(1)}, bf16[128,384]{1,0:T(8,128)(2,1)S(1)}, u32[]{:S(2)}, u32[]{:S(2)}) collective-permute-start(bf16[128,384]{1,0:T(8,128)(2,1)S(1)} %get-tuple-element.46), channel_id=1, source_target_pairs={{0,4},{1,5},{2,6},{3,7},{4,0},{5,1},{6,2},{7,3},{8,12},{9,13},{10,... | collective-permute-start | bytes 294920 | tf_op jit(solution)/shard_map/ppermute | solution.py:82
  5.5 0.0 collective-permute-start
  5.5 2.8 %collective-permute-done.1.refs_1_ = bf16[128,384]{1,0:T(8,128)(2,1)S(1)} collective-permute-done((bf16[128,384]{1,0:T(8,128)(2,1)S(1)}, bf16[128,384]{1,0:T(8,128)(2,1)S(1)}, u32[]{:S(2)}, u32[]{:S(2)}) %collective-permute-start.1) | collective-permute-done | bytes 98336 | tf_op jit(solution)/shard_map/ppermute | solution.py:82
  8.3 4.0 %collective-permute-start.2 = (bf16[64,384]{1,0:T(8,128)(2,1)S(1)}, bf16[64,384]{1,0:T(8,128)(2,1)S(1)}, u32[]{:S(2)}, u32[]{:S(2)}) collective-permute-start(bf16[64,384]{1,0:T(8,128)(2,1)S(1)} %pad_maximum_fusion.5), channel_id=1, source_target_pairs={{0,24},{1,25},{2,26},{3,27},{4,28},{5,29},{6,30},{7,31},{8,16},{9,... | collective-permute-start | bytes 147464 | tf_op jit(solution)/shard_map/ppermute | solution.py:82
  12.3 0.0 collective-permute-start.3
  12.4 0.6 collective-permute-start.4
  13.0 3.4 %prepare.1 = (bf16[256,384]{1,0:T(8,128)(2,1)S(1)}, bf16[384,384]{1,0:T(8,128)(2,1)S(1)}, bf16[384,768]{1,0:T(8,128)(2,1)S(1)}, bf16[384,272]{1,0:T(8,128)(2,1)S...) custom-call(s32[2]{0:T(128)S(1)} %pad_add_fusion.place_ref, ...), custom_call_target="tpu_custom_call" | custom-call | flops 377487360 | bytes 4656136 | tf_op jit(solution)/shard_map/prepare/pallas_call | solution.py:466
  16.4 0.0 collective-permute-done.2.refs_2_
  16.5 0.9 %collective-permute-done.3.refs_3_ = bf16[64,384]{1,0:T(8,128)(2,1)S(1)} collective-permute-done((bf16[64,384]{1,0:T(8,128)(2,1)S(1)}, bf16[64,384]{1,0:T(8,128)(2,1)S(1)}, u32[]{:S(2)}, u32[]{:S(2)}) %collective-permute-start.3) | collective-permute-done | bytes 49184 | tf_op jit(solution)/shard_map/ppermute | solution.py:82
  17.3 8.1 %attend.1 = (f32[256,384]{1,0:T(8,128)S(1)}, bf16[128,384]{1,0:T(8,128)(2,1)S(1)}, bf16[32,384]{1,0:T(8,128)(2,1)S(1)}, bf16[32,384]{1,0:T(8,128)(2,1)S(1)}, bf1...) custom-call(s32[2]{0:T(128)S(1)} %pad_add_fusion.place_ref, ...), custom_call_target="tpu_custom_call" | custom-call | flops 3095396352 | bytes 5922824 | tf_op jit(solution)/shard_map/attend/pallas_call | solution.py:466
  25.5 0.1 collective-permute-start.5
  25.5 1.6 %collective-permute-start.9 = (bf16[128,384]{1,0:T(8,128)(2,1)S(1)}, bf16[128,384]{1,0:T(8,128)(2,1)S(1)}, u32[]{:S(2)}, u32[]{:S(2)}) collective-permute-start(bf16[128,384]{1,0:T(8,128)(2,1)S(1)} %get-tuple-element.64), channel_id=1, source_target_pairs={{0,4},{1,5},{2,6},{3,7},{4,0},{5,1},{6,2},{7,3},{8,12},{9,13},{10,... | collective-permute-start | bytes 294920 | tf_op jit(solution)/shard_map/ppermute | solution.py:82
  27.1 0.5 collective-permute-done.5
  27.5 0.2 fusion.2
  27.8 0.1 pad_maximum_fusion.2
  27.8 2.5 %collective-permute-start.6 = (bf16[208,384]{1,0:T(8,128)(2,1)S(1)}, bf16[208,384]{1,0:T(8,128)(2,1)S(1)}, u32[]{:S(2)}, u32[]{:S(2)}) collective-permute-start(bf16[208,384]{1,0:T(8,128)(2,1)S(1)} %get-tuple-element.94), channel_id=1, source_target_pairs={{0,6},{1,7},{2,4},{3,5},{4,2},{5,3},{6,0},{7,1},{8,14},{9,15},{10,... | collective-permute-start | bytes 479240 | tf_op jit(solution)/shard_map/ppermute | solution.py:82
  30.3 0.5 collective-permute-start.7
  30.9 0.5 collective-permute-start.8
  31.4 0.0 collective-permute-done.9.refs_1_
  31.4 3.0 %collective-permute-start.10 = (bf16[64,384]{1,0:T(8,128)(2,1)S(1)}, bf16[64,384]{1,0:T(8,128)(2,1)S(1)}, u32[]{:S(2)}, u32[]{:S(2)}) collective-permute-start(bf16[64,384]{1,0:T(8,128)(2,1)S(1)} %pad_maximum_fusion.8), channel_id=1, source_target_pairs={{0,24},{1,25},{2,26},{3,27},{4,28},{5,29},{6,30},{7,31},{8,16},{9,... | collective-permute-start | bytes 147464 | tf_op jit(solution)/shard_map/ppermute | solution.py:82
  34.4 0.0 collective-permute-start.11
  34.4 1.3 %collective-permute-done.6 = bf16[208,384]{1,0:T(8,128)(2,1)S(1)} collective-permute-done((bf16[208,384]{1,0:T(8,128)(2,1)S(1)}, bf16[208,384]{1,0:T(8,128)(2,1)S(1)}, u32[]{:S(2)}, u32[]{:S(2)}) %collective-permute-start.6) | collective-permute-done | bytes 159776 | tf_op jit(solution)/shard_map/ppermute | solution.py:82
  35.8 0.6 collective-permute-start.12
  36.4 2.1 %collective-permute-done.7 = bf16[208,384]{1,0:T(8,128)(2,1)S(1)} collective-permute-done((bf16[208,384]{1,0:T(8,128)(2,1)S(1)}, bf16[208,384]{1,0:T(8,128)(2,1)S(1)}, u32[]{:S(2)}, u32[]{:S(2)}) %collective-permute-start.7) | collective-permute-done | bytes 159776 | tf_op jit(solution)/shard_map/ppermute | solution.py:82
  38.5 0.1 collective-permute-done.8
  38.5 0.1 fusion
  38.7 0.7 %collective-permute-done.11.refs_3_ = bf16[64,384]{1,0:T(8,128)(2,1)S(1)} collective-permute-done((bf16[64,384]{1,0:T(8,128)(2,1)S(1)}, bf16[64,384]{1,0:T(8,128)(2,1)S(1)}, u32[]{:S(2)}, u32[]{:S(2)}) %collective-permute-start.11) | collective-permute-done | bytes 49184 | tf_op jit(solution)/shard_map/ppermute | solution.py:82
  39.4 0.5 collective-permute-done.12.refs_4_
  39.9 0.6 collective-permute-start.13
  40.5 3.9 %collective-permute-done.13 = bf16[112,384]{1,0:T(8,128)(2,1)S(1)} collective-permute-done((bf16[112,384]{1,0:T(8,128)(2,1)S(1)}, bf16[112,384]{1,0:T(8,128)(2,1)S(1)}, u32[]{:S(2)}, u32[]{:S(2)}) %collective-permute-start.13) | collective-permute-done | bytes 86048 | tf_op jit(solution)/shard_map/ppermute | solution.py:82
  44.5 2.0 %collective-permute-start.14 = (bf16[112,384]{1,0:T(8,128)(2,1)S(1)}, bf16[112,384]{1,0:T(8,128)(2,1)S(1)}, u32[]{:S(2)}, u32[]{:S(2)}) collective-permute-start(bf16[112,384]{1,0:T(8,128)(2,1)S(1)} %pad_maximum_fusion.4), channel_id=1, source_target_pairs={{0,16},{1,17},{2,18},{3,19},{4,20},{5,21},{6,22},{7,23},{8,24},{9,... | collective-permute-start | bytes 258056 | tf_op jit(solution)/shard_map/ppermute | solution.py:82
  46.5 2.5 %return_rows.1 = f32[256,384]{1,0:T(8,128)} custom-call(s32[2]{0:T(128)S(1)} %pad_add_fusion.place_ref, s32[8,32]{1,0:T(8,128)} %send_hbm.3, f32[256,384]{1,0:T(8,128)S(1)} %get-tuple-element.71.gf_ref, bf16[128,384]{1,0:T(8,128)(2,1)S(1)} %collective-permute-done.15.halo_ref, bf16[32,384]{1,0:T(8,128)(2,1)S(1)} %get-tuple-element.73.refs_0_, ...), custom_call_target="tpu_custom_call" | custom-call | bytes 1156104 | tf_op jit(solution)/shard_map/return_rows/pallas_call | solution.py:466
  49.0 1.9 %collective-permute-done.14 = bf16[112,384]{1,0:T(8,128)(2,1)S(1)} collective-permute-done((bf16[112,384]{1,0:T(8,128)(2,1)S(1)}, bf16[112,384]{1,0:T(8,128)(2,1)S(1)}, u32[]{:S(2)}, u32[]{:S(2)}) %collective-permute-start.14) | collective-permute-done | bytes 86048 | tf_op jit(solution)/shard_map/ppermute | solution.py:82
  50.9 0.1 collective-permute-start.16
  51.0 4.3 %collective-permute-done.16 = bf16[96,384]{1,0:T(8,128)(2,1)S(1)} collective-permute-done((bf16[96,384]{1,0:T(8,128)(2,1)S(1)}, bf16[96,384]{1,0:T(8,128)(2,1)S(1)}, u32[]{:S(2)}, u32[]{:S(2)}) %collective-permute-start.16) | collective-permute-done | bytes 73760 | tf_op jit(solution)/shard_map/ppermute | solution.py:82
  55.4 2.5 %collective-permute-start.19 = (bf16[192,384]{1,0:T(8,128)(2,1)S(1)}, bf16[192,384]{1,0:T(8,128)(2,1)S(1)}, u32[]{:S(2)}, u32[]{:S(2)}) collective-permute-start(bf16[192,384]{1,0:T(8,128)(2,1)S(1)} %constant_dynamic-update-slice_fusion.refs_0_), channel_id=1, source_target_pairs={{0,6},{1,7},{2,4},{3,5},{4,2},{5,3},{6,0},{7,1},{8,14},{9,15},{10,... | collective-permute-start | bytes 442376 | tf_op jit(solution)/shard_map/ppermute | solution.py:82
  57.9 0.5 collective-permute-start.18
  58.4 0.5 collective-permute-start.17
  58.9 2.5 %collective-permute-done.19.refs_3_ = bf16[192,384]{1,0:T(8,128)(2,1)S(1)} collective-permute-done((bf16[192,384]{1,0:T(8,128)(2,1)S(1)}, bf16[192,384]{1,0:T(8,128)(2,1)S(1)}, u32[]{:S(2)}, u32[]{:S(2)}) %collective-permute-start.19) | collective-permute-done | bytes 147488 | tf_op jit(solution)/shard_map/ppermute | solution.py:82
  61.5 1.7 %collective-permute-done.18.refs_2_ = bf16[192,384]{1,0:T(8,128)(2,1)S(1)} collective-permute-done((bf16[192,384]{1,0:T(8,128)(2,1)S(1)}, bf16[192,384]{1,0:T(8,128)(2,1)S(1)}, u32[]{:S(2)}, u32[]{:S(2)}) %collective-permute-start.18) | collective-permute-done | bytes 147488 | tf_op jit(solution)/shard_map/ppermute | solution.py:82
  63.1 0.4 collective-permute-done.17.refs_1_
  63.6 0.1 collective-permute-start.21
  63.6 0.6 convert_add_fusion.1
  64.3 0.3 collective-permute-done.22.refs_6_
  64.5 0.4 collective-permute-done.21.refs_5_
  65.0 2.2 %place_sums.1 = (f32[384,384]{1,0:T(8,128)}, f32[384,768]{1,0:T(8,128)}, f32[384,384]{1,0:T(8,128)}) custom-call(s32[2]{0:T(128)S(1)} %pad_add_fusion.place_ref, bf16[192,384]{1,0:T(8,128)(2,1)S(1)} %constant_dynamic-update-slice_fusion.refs_0_, bf16[192,384]{1,0:T(8,128)(2,1)S(1)} %collective-permute-done.17.refs_1_, ...), custom_call_target="tpu_custom_call" | custom-call | bytes 3538952 | tf_op jit(solution)/shard_map/place_sums/pallas_call | solution.py:466
  (30 shorter events, 0.3 us)
Async XLA Ops:
  2.5 5.8 %collective-permute-start.1 = (bf16[128,384]{1,0:T(8,128)(2,1)S(1)}, bf16[128,384]{1,0:T(8,128)(2,1)S(1)}, u32[]{:S(2)}, u32[]{:S(2)}) collective-permute-start(bf16[128,384]{1,0:T(8,128)(2,1)S(1)} %get-tuple-element.46), channel_id=1, source_target_pairs={{0,4},{1,5},{2,6},{3,7},{4,0},{5,1},{6,2},{7,3},{8,12},{9,13},{10,... | collective-permute-start | bytes 294920 | tf_op jit(solution)/shard_map/ppermute | solution.py:82
  5.5 10.9 %collective-permute-start = (bf16[128,384]{1,0:T(8,128)(2,1)S(1)}, bf16[128,384]{1,0:T(8,128)(2,1)S(1)}, u32[]{:S(2)}, u32[]{:S(2)}) collective-permute-start(bf16[128,384]{1,0:T(8,128)(2,1)S(1)} %get-tuple-element.44), channel_id=1, source_target_pairs={{3,0},{0,1},{1,2},{2,3},{7,4},{4,5},{5,6},{6,7},{11,8},{8,9},{9,10... | collective-permute-start | bytes 294920 | tf_op jit(solution)/shard_map/ppermute | solution.py:88
  8.3 8.1 %collective-permute-start.2 = (bf16[64,384]{1,0:T(8,128)(2,1)S(1)}, bf16[64,384]{1,0:T(8,128)(2,1)S(1)}, u32[]{:S(2)}, u32[]{:S(2)}) collective-permute-start(bf16[64,384]{1,0:T(8,128)(2,1)S(1)} %pad_maximum_fusion.5), channel_id=1, source_target_pairs={{0,24},{1,25},{2,26},{3,27},{4,28},{5,29},{6,30},{7,31},{8,16},{9,... | collective-permute-start | bytes 147464 | tf_op jit(solution)/shard_map/ppermute | solution.py:82
  12.3 5.0 %collective-permute-start.3 = (bf16[64,384]{1,0:T(8,128)(2,1)S(1)}, bf16[64,384]{1,0:T(8,128)(2,1)S(1)}, u32[]{:S(2)}, u32[]{:S(2)}) collective-permute-start(bf16[64,384]{1,0:T(8,128)(2,1)S(1)} %pad_maximum_fusion.6), channel_id=1, source_target_pairs={{0,16},{1,17},{2,18},{3,19},{4,20},{5,21},{6,22},{7,23},{8,24},{9,... | collective-permute-start | bytes 147464 | tf_op jit(solution)/shard_map/ppermute | solution.py:82
  12.4 5.0 %collective-permute-start.4 = (bf16[64,384]{1,0:T(8,128)(2,1)S(1)}, bf16[64,384]{1,0:T(8,128)(2,1)S(1)}, u32[]{:S(2)}, u32[]{:S(2)}) collective-permute-start(bf16[64,384]{1,0:T(8,128)(2,1)S(1)} %pad_maximum_fusion.7), channel_id=1, source_target_pairs={{0,8},{1,9},{2,10},{3,11},{4,12},{5,13},{6,14},{7,15},{8,0},{9,1},... | collective-permute-start | bytes 147464 | tf_op jit(solution)/shard_map/ppermute | solution.py:82
  25.5 2.1 %collective-permute-start.5 = (bf16[784,384]{1,0:T(8,128)(2,1)S(1)}, bf16[784,384]{1,0:T(8,128)(2,1)S(1)}, u32[]{:S(2)}, u32[]{:S(2)}) collective-permute-start(bf16[784,384]{1,0:T(8,128)(2,1)S(1)} %get-tuple-element.61), channel_id=1, source_target_pairs={{0,1},{1,0},{2,3},{3,2},{4,5},{5,4},{6,7},{7,6},{8,9},{9,8},{10,11... | collective-permute-start | bytes 1806344 | tf_op jit(solution)/shard_map/ppermute | solution.py:82
  25.5 5.9 %collective-permute-start.9 = (bf16[128,384]{1,0:T(8,128)(2,1)S(1)}, bf16[128,384]{1,0:T(8,128)(2,1)S(1)}, u32[]{:S(2)}, u32[]{:S(2)}) collective-permute-start(bf16[128,384]{1,0:T(8,128)(2,1)S(1)} %get-tuple-element.64), channel_id=1, source_target_pairs={{0,4},{1,5},{2,6},{3,7},{4,0},{5,1},{6,2},{7,3},{8,12},{9,13},{10,... | collective-permute-start | bytes 294920 | tf_op jit(solution)/shard_map/ppermute | solution.py:82
  27.8 7.9 %collective-permute-start.6 = (bf16[208,384]{1,0:T(8,128)(2,1)S(1)}, bf16[208,384]{1,0:T(8,128)(2,1)S(1)}, u32[]{:S(2)}, u32[]{:S(2)}) collective-permute-start(bf16[208,384]{1,0:T(8,128)(2,1)S(1)} %get-tuple-element.94), channel_id=1, source_target_pairs={{0,6},{1,7},{2,4},{3,5},{4,2},{5,3},{6,0},{7,1},{8,14},{9,15},{10,... | collective-permute-start | bytes 479240 | tf_op jit(solution)/shard_map/ppermute | solution.py:82
  30.3 8.1 %collective-permute-start.7 = (bf16[208,384]{1,0:T(8,128)(2,1)S(1)}, bf16[208,384]{1,0:T(8,128)(2,1)S(1)}, u32[]{:S(2)}, u32[]{:S(2)}) collective-permute-start(bf16[208,384]{1,0:T(8,128)(2,1)S(1)} %get-tuple-element.95), channel_id=1, source_target_pairs={{0,4},{1,5},{2,6},{3,7},{4,0},{5,1},{6,2},{7,3},{8,12},{9,13},{10,... | collective-permute-start | bytes 479240 | tf_op jit(solution)/shard_map/ppermute | solution.py:82
  30.9 7.7 %collective-permute-start.8 = (bf16[208,384]{1,0:T(8,128)(2,1)S(1)}, bf16[208,384]{1,0:T(8,128)(2,1)S(1)}, u32[]{:S(2)}, u32[]{:S(2)}) collective-permute-start(bf16[208,384]{1,0:T(8,128)(2,1)S(1)} %get-tuple-element.96), channel_id=1, source_target_pairs={{0,2},{1,3},{2,0},{3,1},{4,6},{5,7},{6,4},{7,5},{8,10},{9,11},{10,... | collective-permute-start | bytes 479240 | tf_op jit(solution)/shard_map/ppermute | solution.py:82
  31.4 7.3 %collective-permute-start.10 = (bf16[64,384]{1,0:T(8,128)(2,1)S(1)}, bf16[64,384]{1,0:T(8,128)(2,1)S(1)}, u32[]{:S(2)}, u32[]{:S(2)}) collective-permute-start(bf16[64,384]{1,0:T(8,128)(2,1)S(1)} %pad_maximum_fusion.8), channel_id=1, source_target_pairs={{0,24},{1,25},{2,26},{3,27},{4,28},{5,29},{6,30},{7,31},{8,16},{9,... | collective-permute-start | bytes 147464 | tf_op jit(solution)/shard_map/ppermute | solution.py:82
  34.4 5.0 %collective-permute-start.11 = (bf16[64,384]{1,0:T(8,128)(2,1)S(1)}, bf16[64,384]{1,0:T(8,128)(2,1)S(1)}, u32[]{:S(2)}, u32[]{:S(2)}) collective-permute-start(bf16[64,384]{1,0:T(8,128)(2,1)S(1)} %pad_maximum_fusion.9), channel_id=1, source_target_pairs={{0,16},{1,17},{2,18},{3,19},{4,20},{5,21},{6,22},{7,23},{8,24},{9,... | collective-permute-start | bytes 147464 | tf_op jit(solution)/shard_map/ppermute | solution.py:82
  35.8 4.2 %collective-permute-start.12 = (bf16[64,384]{1,0:T(8,128)(2,1)S(1)}, bf16[64,384]{1,0:T(8,128)(2,1)S(1)}, u32[]{:S(2)}, u32[]{:S(2)}) collective-permute-start(bf16[64,384]{1,0:T(8,128)(2,1)S(1)} %pad_maximum_fusion.10), channel_id=1, source_target_pairs={{0,8},{1,9},{2,10},{3,11},{4,12},{5,13},{6,14},{7,15},{8,0},{9,1},... | collective-permute-start | bytes 147464 | tf_op jit(solution)/shard_map/ppermute | solution.py:82
  39.9 4.5 %collective-permute-start.13 = (bf16[112,384]{1,0:T(8,128)(2,1)S(1)}, bf16[112,384]{1,0:T(8,128)(2,1)S(1)}, u32[]{:S(2)}, u32[]{:S(2)}) collective-permute-start(bf16[112,384]{1,0:T(8,128)(2,1)S(1)} %pad_maximum_fusion.3), channel_id=1, source_target_pairs={{0,8},{1,9},{2,10},{3,11},{4,12},{5,13},{6,14},{7,15},{8,0},{9,1},... | collective-permute-start | bytes 258056 | tf_op jit(solution)/shard_map/ppermute | solution.py:82
  40.5 6.0 %collective-permute-start.15 = (bf16[128,384]{1,0:T(8,128)(2,1)S(1)}, bf16[128,384]{1,0:T(8,128)(2,1)S(1)}, u32[]{:S(2)}, u32[]{:S(2)}) collective-permute-start(bf16[128,384]{1,0:T(8,128)(2,1)S(1)} %get-tuple-element.72), channel_id=1, source_target_pairs={{1,0},{2,1},{3,2},{0,3},{5,4},{6,5},{7,6},{4,7},{9,8},{10,9},{11,1... | collective-permute-start | bytes 294920 | tf_op jit(solution)/shard_map/ppermute | solution.py:88
  44.5 6.4 %collective-permute-start.14 = (bf16[112,384]{1,0:T(8,128)(2,1)S(1)}, bf16[112,384]{1,0:T(8,128)(2,1)S(1)}, u32[]{:S(2)}, u32[]{:S(2)}) collective-permute-start(bf16[112,384]{1,0:T(8,128)(2,1)S(1)} %pad_maximum_fusion.4), channel_id=1, source_target_pairs={{0,16},{1,17},{2,18},{3,19},{4,20},{5,21},{6,22},{7,23},{8,24},{9,... | collective-permute-start | bytes 258056 | tf_op jit(solution)/shard_map/ppermute | solution.py:82
  50.9 4.4 %collective-permute-start.16 = (bf16[96,384]{1,0:T(8,128)(2,1)S(1)}, bf16[96,384]{1,0:T(8,128)(2,1)S(1)}, u32[]{:S(2)}, u32[]{:S(2)}) collective-permute-start(bf16[96,384]{1,0:T(8,128)(2,1)S(1)} %add_convert_fusion), channel_id=1, source_target_pairs={{0,8},{1,9},{2,10},{3,11},{4,12},{5,13},{6,14},{7,15},{8,0},{9,1},... | collective-permute-start | bytes 221192 | tf_op jit(solution)/shard_map/ppermute | solution.py:82
  55.4 6.1 %collective-permute-start.19 = (bf16[192,384]{1,0:T(8,128)(2,1)S(1)}, bf16[192,384]{1,0:T(8,128)(2,1)S(1)}, u32[]{:S(2)}, u32[]{:S(2)}) collective-permute-start(bf16[192,384]{1,0:T(8,128)(2,1)S(1)} %constant_dynamic-update-slice_fusion.refs_0_), channel_id=1, source_target_pairs={{0,6},{1,7},{2,4},{3,5},{4,2},{5,3},{6,0},{7,1},{8,14},{9,15},{10,... | collective-permute-start | bytes 442376 | tf_op jit(solution)/shard_map/ppermute | solution.py:82
  57.9 5.2 %collective-permute-start.18 = (bf16[192,384]{1,0:T(8,128)(2,1)S(1)}, bf16[192,384]{1,0:T(8,128)(2,1)S(1)}, u32[]{:S(2)}, u32[]{:S(2)}) collective-permute-start(bf16[192,384]{1,0:T(8,128)(2,1)S(1)} %constant_dynamic-update-slice_fusion.refs_0_), channel_id=1, source_target_pairs={{0,4},{1,5},{2,6},{3,7},{4,0},{5,1},{6,2},{7,3},{8,12},{9,13},{10,... | collective-permute-start | bytes 442376 | tf_op jit(solution)/shard_map/ppermute | solution.py:82
  58.4 5.1 %collective-permute-start.17 = (bf16[192,384]{1,0:T(8,128)(2,1)S(1)}, bf16[192,384]{1,0:T(8,128)(2,1)S(1)}, u32[]{:S(2)}, u32[]{:S(2)}) collective-permute-start(bf16[192,384]{1,0:T(8,128)(2,1)S(1)} %constant_dynamic-update-slice_fusion.refs_0_), channel_id=1, source_target_pairs={{0,2},{1,3},{2,0},{3,1},{4,6},{5,7},{6,4},{7,5},{8,10},{9,11},{10,... | collective-permute-start | bytes 442376 | tf_op jit(solution)/shard_map/ppermute | solution.py:82
  58.9 5.3 %collective-permute-start.20 = (bf16[192,384]{1,0:T(8,128)(2,1)S(1)}, bf16[192,384]{1,0:T(8,128)(2,1)S(1)}, u32[]{:S(2)}, u32[]{:S(2)}) collective-permute-start(bf16[192,384]{1,0:T(8,128)(2,1)S(1)} %constant_dynamic-update-slice_fusion.refs_0_), channel_id=1, source_target_pairs={{0,1},{1,0},{2,3},{3,2},{4,5},{5,4},{6,7},{7,6},{8,9},{9,8},{10,11... | collective-permute-start | bytes 442376 | tf_op jit(solution)/shard_map/ppermute | solution.py:82
  61.5 2.8 %collective-permute-start.23 = (bf16[192,384]{1,0:T(8,128)(2,1)S(1)}, bf16[192,384]{1,0:T(8,128)(2,1)S(1)}, u32[]{:S(2)}, u32[]{:S(2)}) collective-permute-start(bf16[192,384]{1,0:T(8,128)(2,1)S(1)} %collective-permute-done.19.refs_3_), channel_id=1, source_target_pairs={{0,1},{1,0},{2,3},{3,2},{4,5},{5,4},{6,7},{7,6},{8,9},{9,8},{10,11... | collective-permute-start | bytes 442376 | tf_op jit(solution)/shard_map/ppermute | solution.py:82
  63.1 1.4 %collective-permute-start.22 = (bf16[192,384]{1,0:T(8,128)(2,1)S(1)}, bf16[192,384]{1,0:T(8,128)(2,1)S(1)}, u32[]{:S(2)}, u32[]{:S(2)}) collective-permute-start(bf16[192,384]{1,0:T(8,128)(2,1)S(1)} %collective-permute-done.18.refs_2_), channel_id=1, source_target_pairs={{0,1},{1,0},{2,3},{3,2},{4,5},{5,4},{6,7},{7,6},{8,9},{9,8},{10,11... | collective-permute-start | bytes 442376 | tf_op jit(solution)/shard_map/ppermute | solution.py:82
  63.6 1.4 %collective-permute-start.21 = (bf16[192,384]{1,0:T(8,128)(2,1)S(1)}, bf16[192,384]{1,0:T(8,128)(2,1)S(1)}, u32[]{:S(2)}, u32[]{:S(2)}) collective-permute-start(bf16[192,384]{1,0:T(8,128)(2,1)S(1)} %collective-permute-done.17.refs_1_), channel_id=1, source_target_pairs={{0,1},{1,0},{2,3},{3,2},{4,5},{5,4},{6,7},{7,6},{8,9},{9,8},{10,11... | collective-permute-start | bytes 442376 | tf_op jit(solution)/shard_map/ppermute | solution.py:82

commit v8 on v7

--- a/solution.py
+++ b/solution.py
@@ -36,39 +36,25 @@
     return value.astype(jnp.bfloat16)
 
 
-def exchange_stages(dom_size, rows_size):
-    stages = [[((0, 1), (0, 1))], [((1, 2), (0, 2)), ((1, 0), (1, 2))]]
-    stages += [[((bit, 0), (bit, 0))] for bit in powers_of_two(2, dom_size)]
-    stages += [[((0, bit), (0, bit))] for bit in powers_of_two(4, rows_size)]
-    return stages
+HALVINGS = 3
+
+
+def exchange_steps(dom_size, rows_size):
+    near = [(0, 2), (1, 0)]
+    rest = [(bit, 0) for bit in powers_of_two(2, dom_size)]
+    rest += [(0, bit) for bit in powers_of_two(4, rows_size)]
+    return near + rest, near[::-1] + rest
 
 
 def powers_of_two(first, size):
     return [1 << i for i in range(size.bit_length() - 1) if 1 << i >= first]
 
 
-def partner_masks(stage):
-    masks = []
-    for digit in range(1, 1 << len(stage)):
-        dom_mask = rows_mask = 0
-        for i, (mask, _) in enumerate(stage):
-            if digit >> i & 1:
-                dom_mask ^= mask[0]
-                rows_mask ^= mask[1]
-        masks.append((dom_mask, rows_mask))
-    return masks
-
-
-def own_piece(stages):
+def own_piece(steps):
     index = jnp.int32(0)
-    for stage in stages:
-        index = index << len(stage)
-        for i, (_, parity) in enumerate(stage):
-            odd = jnp.int32(0)
-            for axis, mask in zip(("dom", "rows"), parity):
-                for bit in powers_of_two(1, 2 * mask) if mask else []:
-                    odd ^= jnp.where(lax.axis_index(axis) & bit & mask, 1, 0)
-            index += odd << i
+    for dom_mask, rows_mask in steps[:HALVINGS]:
+        own = (lax.axis_index("dom") & dom_mask) | (lax.axis_index("rows") & rows_mask)
+        index = index * 2 + jnp.where(own != 0, 1, 0)
     return index
 
 
@@ -88,16 +74,6 @@
     return lax.ppermute(block, axis, route)
 
 
-def paired_sum(terms):
-    while len(terms) > 1:
-        terms = [left + right for left, right in zip(terms[::2], terms[1::2])]
-    return terms[0]
-
-
-def routed(direct, through):
-    return handed_on(direct, swapped(through, 1, 0))
-
-
 def handed_on(direct, through):
     rows = direct[0].shape[0]
     arrived = []
@@ -107,31 +83,33 @@
     return [direct[0], through] + arrived
 
 
-def scatter_stage(keep, rider, stage, halved):
-    part = keep.shape[0] >> len(stage) if halved else keep.shape[0]
-    rider_bf = rounded(rider)
-    if not halved:
-        keep = rounded(keep).astype(jnp.float32)
-    messages = []
-    for at in range(1, 1 << len(stage)):
-        block = keep[at * part : (at + 1) * part] if halved else keep
-        messages.append(jnp.concatenate([rounded(block), rider_bf], axis=0))
-    return keep[:part], rider_bf.astype(jnp.float32), messages
-
-
-def exchange(messages, stage):
-    return [swapped(message, *masks) for message, masks in zip(messages, partner_masks(stage))]
-
-
-def added(keep, rider, arrived):
-    part = keep.shape[0]
-    terms = [keep] + [block[:part].astype(jnp.float32) for block in arrived]
-    riders = [rider] + [block[part:].astype(jnp.float32) for block in arrived]
-    return paired_sum(terms), paired_sum(riders)
-
-
-def gathered(held, stage):
-    return jnp.concatenate([held] + exchange([held] * ((1 << len(stage)) - 1), stage), axis=0)
+class Chain:
+    def __init__(self, keep, message, rider):
+        self.keep, self.message = keep, message
+        self.rider = None if rider is None else rounded(rider).astype(jnp.float32)
+
+    def form(self, halved):
+        rows = self.keep.shape[0]
+        if halved:
+            block = rounded(self.keep[rows // 2 :])
+            self.keep = self.keep[: rows // 2]
+        else:
+            block = rounded(self.keep)
+            self.keep = block.astype(jnp.float32)
+        if self.rider is not None:
+            rider = rounded(self.rider)
+            self.rider = rider.astype(jnp.float32)
+            block = jnp.concatenate([block, rider], axis=0)
+        self.message = block
+
+    def send(self, masks):
+        self.message = swapped(self.message, *masks)
+
+    def add(self):
+        rows = self.keep.shape[0]
+        self.keep += self.message[:rows].astype(jnp.float32)
+        if self.rider is not None:
+            self.rider += self.message[rows:].astype(jnp.float32)
 
 
 def listed_rows(dom, send_ref, row_count):
@@ -275,8 +253,8 @@
     local_bias_ref, far_bias_ref, gf_ref, halo_feat_ref = refs[8:12]
     direct_refs, refs = refs[12 : 12 + dom_size // 2], refs[12 + dom_size // 2 :]
     through_ref, refs = refs[0], refs[1:]
-    keep_ref, send_ref, rider_ref = refs[:3]
-    slot_ref, kv_ref, kvt_ref, extt_ref, gqt_ref, gkvt_ref, ot_ref = refs[3:]
+    keep_refs, send_refs, rider_ref = refs[:2], refs[2:4], refs[4]
+    slot_ref, kv_ref, kvt_ref, extt_ref, gqt_ref, gkvt_ref, ot_ref = refs[5:]
     width, row_count = qt_ref.shape
     tile = halo_ref.shape[0]
     tile_count = row_count // tile
@@ -382,54 +360,57 @@
         ]
     rider_ref[...] = by_feature[:, virt_at:].T * factor
 
+    features, queries = extt_ref[:, tile:near], gqt_ref[...]
     sums = (
-        times_transposed(extt_ref[:, tile:near], gqt_ref[...]),
-        times_transposed(extt_ref[...], gkvt_ref[:width]),
-        times_transposed(extt_ref[...], gkvt_ref[width:]),
-        f32_dot(ot_ref[...], og_ref[...]),
-    )
-    pieces = keep_ref.shape[0] // rows_per_piece
-    held = place_ref[1] % pieces
-
-    def write(half, out_ref, cast):
-        for piece in range(pieces):
-            start = (half * pieces + piece) * rows_per_piece
-            value = sums[start // width][start % width : start % width + rows_per_piece] * factor
-            offset = pl.multiple_of((piece ^ held) * rows_per_piece, ROW_PACK)
+        (
+            lambda: times_transposed(features, queries),
+            lambda: times_transposed(extt_ref[...], gkvt_ref[:width]),
+        ),
+        (
+            lambda: f32_dot(ot_ref[...], og_ref[...]),
+            lambda: times_transposed(extt_ref[...], gkvt_ref[width:]),
+        ),
+    )
+    sums = [[make() * factor for make in of_core] for of_core in sums]
+
+    def write(total, chain, out_ref, cast):
+        for piece in range(width // rows_per_piece):
+            value = total[piece * rows_per_piece : (piece + 1) * rows_per_piece]
+            offset = pl.multiple_of((piece ^ place_ref[2 + chain]) * rows_per_piece, ROW_PACK)
             out_ref[pl.ds(offset, rows_per_piece), :] = cast(value)
 
-    for half in range(2):
-
-        @pl.when(place_ref[1] // pieces == half)
+    for core in range(2):
+
+        @pl.when(place_ref[1] == core)
         def _():
-            write(half, keep_ref, lambda value: value)
-            write(1 - half, send_ref, rounded)
-
-    send_ref[keep_ref.shape[0] :] = rounded(rider_ref[...])
-
-
-def place_kernel(rows_per_piece, place_ref, *refs):
-    part_refs, (gq_hbm, gkv_hbm, go_hbm, all_ref, out_ref, sems) = refs[:-6], refs[-6:]
-    width = gq_hbm.shape[0]
+            for chain in range(2):
+                write(sums[1 - core][chain], chain, send_refs[chain], rounded)
+                write(sums[core][chain], chain, keep_refs[chain], lambda value: value)
+
+    send_refs[0][width:] = rounded(rider_ref[...])
+
+
+def place_kernel(rows_per_piece, chain, place_ref, *refs):
+    outs = 2 if chain == 0 else 1
+    part_refs, out_hbms = refs[: -3 - outs], refs[-3 - outs : -3]
+    all_ref, out_ref, sems = refs[-3:]
     rows = part_refs[0].shape[0]
-    half = len(part_refs) // 2
+    width = all_ref.shape[1]
     for at, part_ref in enumerate(part_refs):
-        digit = at // half * half + -at % half
-        all_ref[digit * rows : (digit + 1) * rows] = part_ref[...]
+        all_ref[at * rows : (at + 1) * rows] = part_ref[...]
     copies = []
-    for at in range(all_ref.shape[0] // rows_per_piece):
-        offset = pl.multiple_of((place_ref[1] ^ at) * rows_per_piece, ROW_PACK)
-        start = at * rows_per_piece
-        piece = slice(start, start + rows_per_piece)
+    for at in range(2 * width // rows_per_piece):
+        core, start = at * rows_per_piece // width, at * rows_per_piece % width
+        distance = (start // rows_per_piece) ^ place_ref[2 + chain]
+        offset = (core ^ place_ref[1]) * width + distance * rows_per_piece
+        offset = pl.multiple_of(offset, ROW_PACK)
+        piece = slice(at * rows_per_piece, (at + 1) * rows_per_piece)
         out_ref[piece] = all_ref[pl.ds(offset, rows_per_piece), :].astype(jnp.float32)
-        rows_out = pl.ds(start % width, rows_per_piece)
-        which = start // width
-        if which == 0:
-            target = gq_hbm.at[rows_out]
-        elif which == 3:
-            target = go_hbm.at[rows_out]
+        target = pl.ds(start, rows_per_piece)
+        if chain == 0:
+            target = out_hbms[core].at[target]
         else:
-            target = gkv_hbm.at[rows_out, pl.ds((which - 1) * width, width)]
+            target = out_hbms[0].at[target, pl.ds(core * width, width)]
         copies.append(pltpu.make_async_copy(out_ref.at[piece], target, sems.at[at]))
         copies[-1].start()
     for copy in copies:
@@ -483,10 +464,12 @@
     padded = ROW_PACK * -(-virt_rows // ROW_PACK)
     ext_rows = TILE + row_count + slots + padded
     nodes = row_count * lax.axis_size("dom") * lax.axis_size("rows")
-    stages = exchange_stages(lax.axis_size("dom"), lax.axis_size("rows"))
-    scattered = stages[:3]
-    rows_per_piece = 4 * width >> sum(len(stage) for stage in scattered)
-    place = jnp.stack([lax.axis_index("dom").astype(jnp.int32), own_piece(scattered)])
+    chain_steps = exchange_steps(lax.axis_size("dom"), lax.axis_size("rows"))
+    rows_per_piece = width >> HALVINGS
+    place = jnp.stack(
+        [lax.axis_index("dom").astype(jnp.int32), lax.axis_index("rows").astype(jnp.int32) & 1]
+        + [own_piece(steps) for steps in chain_steps]
+    )
     bf16, f32 = jnp.bfloat16, jnp.float32
     shape = jax.ShapeDtypeStruct
 
@@ -499,7 +482,9 @@
         [pltpu.VMEM(features.shape, bf16), pltpu.VMEM(send_rows.shape, jnp.int32)],
         fetched=2,
     )
-    arrived = routed(direct, through)
+    through = swapped(through, 1, 0)
+    arrived = handed_on(direct, through)
+    halo, _ = lax.optimization_barrier((halo, through))
     halo = shifted(halo, "rows", 1)
     prepared = call(
         functools.partial(prepare_kernel, per_peer),
@@ -535,8 +520,9 @@
             shape((TILE, width), bf16),
             *[shape((per_peer, width), bf16)] * (dom_size // 2),
             shape((slots // 2, width), bf16),
-            shape((2 * width, width), f32),
-            shape((2 * width + padded, width), bf16),
+            *[shape((width, width), f32)] * 2,
+            shape((width + padded, width), bf16),
+            shape((width, width), bf16),
             shape((padded, width), f32),
         ],
         [place, halo, *arrived, *prepared],
@@ -551,22 +537,29 @@
         ],
         flops=32 * ext_rows * width * width,
     )
-    *direct, through, keep, message, rider = results
-
-    rider = rounded(rider).astype(f32)
-    keep, rider = added(keep, rider, exchange([message], stages[0]))
+    *direct, through, keep, other_keep, message, other_message, rider = results
+
+    chains = [Chain(keep, message, rider), Chain(other_keep, other_message, None)]
     through = swapped(through, 1, 0)
-    for at, stage in enumerate(stages[1:], 1):
-        keep, rider, messages = scatter_stage(keep, rider, stage, stage in scattered)
-        if at == 1:
-            through, _ = lax.optimization_barrier((through, messages))
+    for chain in chains:
+        chain.send((0, 1))
+    for chain in chains:
+        chain.add()
+    for at, masks in enumerate(zip(*chain_steps)):
+        for chain in chains:
+            chain.form(at < HALVINGS)
+        if at == 0:
+            through, _ = lax.optimization_barrier((through, [chain.message for chain in chains]))
             returned = handed_on(direct, through)
         if at == 2:
             messages, returned, halo_feat = lax.optimization_barrier(
-                (messages, returned, halo_feat)
+                ([chain.message for chain in chains], returned, halo_feat)
             )
+            chains[0].message, chains[1].message = messages
             halo_back = shifted(halo_feat, "rows", -1)
-        keep, rider = added(keep, rider, exchange(messages, stage))
+        for chain, mask in zip(chains, masks):
+            chain.send(mask)
+            chain.add()
     (grad_features,) = call(
         return_kernel,
         "return_rows",
@@ -575,23 +568,27 @@
         [pltpu.VMEM(send_rows.shape, jnp.int32)],
         fetched=1,
     )
-    held, grad_features = lax.optimization_barrier((rounded(keep), grad_features))
-    held = gathered(held, scattered[2])
-    square = partner_masks(scattered[1])
-    near = [held] + [swapped(held, *masks) for masks in square[::-1]]
-    far = [swapped(block, *partner_masks(scattered[0])[0]) for block in near]
-    grad_wq, grad_wkv, grad_wo = call(
-        functools.partial(place_kernel, rows_per_piece),
-        "place_sums",
-        [shape((width, width), f32), shape((width, 2 * width), f32), shape((width, width), f32)],
-        [place, *near, *far],
-        [
-            pltpu.VMEM((4 * width, width), bf16),
-            pltpu.VMEM((4 * width, width), f32),
-            pltpu.SemaphoreType.DMA((4 * width // rows_per_piece,)),
-        ],
-        stored=True,
-    )
+    placed = []
+    for at, (chain, steps) in enumerate(zip(chains, chain_steps)):
+        held = rounded(chain.keep)
+        for masks in steps[HALVINGS - 1 : 0 : -1]:
+            held = jnp.concatenate([held, swapped(held, *masks)], axis=0)
+        near = [held, swapped(held, *steps[0])]
+        far = [swapped(block, 0, 1) for block in near]
+        placed += call(
+            functools.partial(place_kernel, rows_per_piece, at),
+            ("place_wq_wo", "place_wkv")[at],
+            [shape((width, width), f32)] * 2 if at == 0 else [shape((width, 2 * width), f32)],
+            [place, *near, *far],
+            [
+                pltpu.VMEM((2 * width, width), bf16),
+                pltpu.VMEM((2 * width, width), f32),
+                pltpu.SemaphoreType.DMA((2 * width // rows_per_piece,)),
+            ],
+            stored=True,
+        )
+    grad_wq, grad_wo, grad_wkv = placed
+    rider = chains[0].rider
     return grad_features, grad_wq, grad_wkv, grad_wo, rider[:virt_rows]
 
 

time: 67.4 us -> 76.6 us (1.14)
  starting transfers between devices: 22.7 us -> 37.9 us
  waiting for transfers between devices: 24.4 us -> 17 us
  Pallas kernels: 18 us -> 19.3 us
    ppermute x22 -> x28, starting transfers between devices: 22.7 us -> 37.8 us  [swapped(): return lax.ppermute(block, ('dom', 'rows'), route)]
    ppermute x22 -> x28, waiting for transfers between devices: 24.4 us -> 13.3 us  [swapped(): return lax.ppermute(block, ('dom', 'rows'), route)]
    ppermute x2, waiting for transfers between devices: 0.01 us -> 3.71 us  [shifted(): return lax.ppermute(block, axis, route)]
    pallas_call x5 -> x6, Pallas kernels: 18 us -> 19.3 us  [call(): pl.pallas_call(kernel, out_shape=outs, in_specs=[pl.BlockSpec(memory_spac...]
  transfers between devices with their start and end apart: 24 -> 30, of which waited for: 16 -> 13; matrix products, arithmetic and copies ran while one was open for 2% -> 1% of each run, Pallas kernels for 9% -> 10%
where the time goes in v8:
time: 76.6 us; the launch traced here: 76.3 us
  starting transfers between devices  37.9 us (49%)
  Pallas kernels  19.3 us (25%)
  waiting for transfers between devices  17 us (22%)
  other arithmetic  1.11 us (1%)
  between operations  0.97 us (1%)
    ppermute x28, starting transfers between devices, swapped(): return lax.ppermute(block, ('dom', 'rows'), route)  37.8 us
    pallas_call x6, Pallas kernels, call(): pl.pallas_call(kernel, out_shape=outs, in_specs=[pl.BlockSpec(memory_spac...  19.3 us
    ppermute x28, waiting for transfers between devices, swapped(): return lax.ppermute(block, ('dom', 'rows'), route)  13.3 us
    ppermute x2, waiting for transfers between devices, shifted(): return lax.ppermute(block, axis, route)  3.71 us
  transfers between devices with their start and end apart: 30, of which 13 were waited for; matrix products, arithmetic and copies ran while one was open for 1% of the time, Pallas kernels for 10%

profile of v8, /device:TPU:0, one launch (start us, length us, event | category | flops | bytes accessed | tf_op | source)
XLA Modules:
  0.0 76.3 jit_solution(5186809537526053686)
XLA Ops:
  0.7 0.1 pad_add_fusion.place_ref
  0.7 1.8 %pick_rows.1 = (bf16[128,384]{1,0:T(8,128)(2,1)S(1)}, bf16[128,384]{1,0:T(8,128)(2,1)S(1)}, bf16[32,384]{1,0:T(8,128)(2,1)S(1)}, bf16[32,384]{1,0:T(8,128)(2,1)S...) custom-call(s32[4]{0:T(128)S(1)} %pad_add_fusion.place_ref, bf16[256,384]{1,0:T(8,128)(2,1)} %feat_hbm.3, ...), custom_call_target="tpu_custom_call" | custom-call | bytes 492560 | tf_op jit(solution)/shard_map/pick_rows/pallas_call | solution.py:447
  2.5 3.0 %collective-permute-start = (bf16[128,384]{1,0:T(8,128)(2,1)S(1)}, bf16[128,384]{1,0:T(8,128)(2,1)S(1)}, u32[]{:S(2)}, u32[]{:S(2)}) collective-permute-start(bf16[128,384]{1,0:T(8,128)(2,1)S(1)} %get-tuple-element.46), channel_id=1, source_target_pairs={{0,4},{1,5},{2,6},{3,7},{4,0},{5,1},{6,2},{7,3},{8,12},{9,13},{10,... | collective-permute-start | bytes 294920 | tf_op jit(solution)/shard_map/ppermute | solution.py:68
  5.5 2.8 %collective-permute-done.refs_1_ = bf16[128,384]{1,0:T(8,128)(2,1)S(1)} collective-permute-done((bf16[128,384]{1,0:T(8,128)(2,1)S(1)}, bf16[128,384]{1,0:T(8,128)(2,1)S(1)}, u32[]{:S(2)}, u32[]{:S(2)}) %collective-permute-start) | collective-permute-done | bytes 98336 | tf_op jit(solution)/shard_map/ppermute | solution.py:68
  8.3 4.0 %collective-permute-start.2 = (bf16[64,384]{1,0:T(8,128)(2,1)S(1)}, bf16[64,384]{1,0:T(8,128)(2,1)S(1)}, u32[]{:S(2)}, u32[]{:S(2)}) collective-permute-start(bf16[64,384]{1,0:T(8,128)(2,1)S(1)} %pad_maximum_fusion.6), channel_id=1, source_target_pairs={{0,24},{1,25},{2,26},{3,27},{4,28},{5,29},{6,30},{7,31},{8,16},{9,... | collective-permute-start | bytes 147464 | tf_op jit(solution)/shard_map/ppermute | solution.py:68
  12.4 0.6 collective-permute-start.4
  13.1 3.4 %prepare.1 = (bf16[256,384]{1,0:T(8,128)(2,1)S(1)}, bf16[384,384]{1,0:T(8,128)(2,1)S(1)}, bf16[384,768]{1,0:T(8,128)(2,1)S(1)}, bf16[384,272]{1,0:T(8,128)(2,1)S...) custom-call(s32[4]{0:T(128)S(1)} %pad_add_fusion.place_ref, ...), custom_call_target="tpu_custom_call" | custom-call | flops 377487360 | bytes 4656144 | tf_op jit(solution)/shard_map/prepare/pallas_call | solution.py:447
  16.5 0.9 %collective-permute-done.3.refs_3_ = bf16[64,384]{1,0:T(8,128)(2,1)S(1)} collective-permute-done((bf16[64,384]{1,0:T(8,128)(2,1)S(1)}, bf16[64,384]{1,0:T(8,128)(2,1)S(1)}, u32[]{:S(2)}, u32[]{:S(2)}) %collective-permute-start.3) | collective-permute-done | bytes 49184 | tf_op jit(solution)/shard_map/ppermute | solution.py:68
  17.4 8.1 %attend.1 = (f32[256,384]{1,0:T(8,128)S(1)}, bf16[128,384]{1,0:T(8,128)(2,1)S(1)}, bf16[32,384]{1,0:T(8,128)(2,1)S(1)}, bf16[32,384]{1,0:T(8,128)(2,1)S(1)}, bf1...) custom-call(s32[4]{0:T(128)S(1)} %pad_add_fusion.place_ref, ...), custom_call_target="tpu_custom_call" | custom-call | flops 3095396352 | bytes 5922832 | tf_op jit(solution)/shard_map/attend/pallas_call | solution.py:447
  25.6 0.6 collective-permute-start.8
  26.2 0.1 collective-permute-start.5
  26.2 1.5 %collective-permute-start.11 = (bf16[128,384]{1,0:T(8,128)(2,1)S(1)}, bf16[128,384]{1,0:T(8,128)(2,1)S(1)}, u32[]{:S(2)}, u32[]{:S(2)}) collective-permute-start(bf16[128,384]{1,0:T(8,128)(2,1)S(1)} %get-tuple-element.69), channel_id=1, source_target_pairs={{0,4},{1,5},{2,6},{3,7},{4,0},{5,1},{6,2},{7,3},{8,12},{9,13},{10,... | collective-permute-start | bytes 294920 | tf_op jit(solution)/shard_map/ppermute | solution.py:68
  27.8 1.2 %collective-permute-start.9 = (bf16[192,384]{1,0:T(8,128)(2,1)S(1)}, bf16[192,384]{1,0:T(8,128)(2,1)S(1)}, u32[]{:S(2)}, u32[]{:S(2)}) collective-permute-start(bf16[192,384]{1,0:T(8,128)(2,1)S(1)} %slice.176), channel_id=1, source_target_pairs={{0,4},{1,5},{2,6},{3,7},{4,0},{5,1},{6,2},{7,3},{8,12},{9,13},{10,... | collective-permute-start | bytes 442376 | tf_op jit(solution)/shard_map/ppermute | solution.py:68
  29.0 0.1 convert_add_fusion.1
  29.2 1.3 %collective-permute-start.6 = (bf16[208,384]{1,0:T(8,128)(2,1)S(1)}, bf16[208,384]{1,0:T(8,128)(2,1)S(1)}, u32[]{:S(2)}, u32[]{:S(2)}) collective-permute-start(bf16[208,384]{1,0:T(8,128)(2,1)S(1)} %pad_maximum_fusion), channel_id=1, source_target_pairs={{0,2},{1,3},{2,0},{3,1},{4,6},{5,7},{6,4},{7,5},{8,10},{9,11},{10,... | collective-permute-start | bytes 479240 | tf_op jit(solution)/shard_map/ppermute | solution.py:68
  30.5 1.4 %collective-permute-done.11.refs_1_ = bf16[128,384]{1,0:T(8,128)(2,1)S(1)} collective-permute-done((bf16[128,384]{1,0:T(8,128)(2,1)S(1)}, bf16[128,384]{1,0:T(8,128)(2,1)S(1)}, u32[]{:S(2)}, u32[]{:S(2)}) %collective-permute-start.11) | collective-permute-done | bytes 98336 | tf_op jit(solution)/shard_map/ppermute | solution.py:68
  31.9 3.7 %collective-permute-start.12 = (bf16[64,384]{1,0:T(8,128)(2,1)S(1)}, bf16[64,384]{1,0:T(8,128)(2,1)S(1)}, u32[]{:S(2)}, u32[]{:S(2)}) collective-permute-start(bf16[64,384]{1,0:T(8,128)(2,1)S(1)} %pad_maximum_fusion.10), channel_id=1, source_target_pairs={{0,24},{1,25},{2,26},{3,27},{4,28},{5,29},{6,30},{7,31},{8,16},{9,... | collective-permute-start | bytes 147464 | tf_op jit(solution)/shard_map/ppermute | solution.py:68
  35.6 0.8 %collective-permute-start.14 = (bf16[64,384]{1,0:T(8,128)(2,1)S(1)}, bf16[64,384]{1,0:T(8,128)(2,1)S(1)}, u32[]{:S(2)}, u32[]{:S(2)}) collective-permute-start(bf16[64,384]{1,0:T(8,128)(2,1)S(1)} %pad_maximum_fusion.12), channel_id=1, source_target_pairs={{0,8},{1,9},{2,10},{3,11},{4,12},{5,13},{6,14},{7,15},{8,0},{9,1},... | collective-permute-start | bytes 147464 | tf_op jit(solution)/shard_map/ppermute | solution.py:68
  36.4 1.3 %collective-permute-start.10 = (bf16[96,384]{1,0:T(8,128)(2,1)S(1)}, bf16[96,384]{1,0:T(8,128)(2,1)S(1)}, u32[]{:S(2)}, u32[]{:S(2)}) collective-permute-start(bf16[96,384]{1,0:T(8,128)(2,1)S(1)} %slice.178), channel_id=1, source_target_pairs={{0,2},{1,3},{2,0},{3,1},{4,6},{5,7},{6,4},{7,5},{8,10},{9,11},{10,... | collective-permute-start | bytes 221192 | tf_op jit(solution)/shard_map/ppermute | solution.py:68
  37.8 1.6 %collective-permute-start.7 = (bf16[112,384]{1,0:T(8,128)(2,1)S(1)}, bf16[112,384]{1,0:T(8,128)(2,1)S(1)}, u32[]{:S(2)}, u32[]{:S(2)}) collective-permute-start(bf16[112,384]{1,0:T(8,128)(2,1)S(1)} %pad_maximum_fusion.3), channel_id=1, source_target_pairs={{0,4},{1,5},{2,6},{3,7},{4,0},{5,1},{6,2},{7,3},{8,12},{9,13},{10,... | collective-permute-start | bytes 258056 | tf_op jit(solution)/shard_map/ppermute | solution.py:68
  39.4 1.4 %collective-permute-done.10 = bf16[96,384]{1,0:T(8,128)(2,1)S(1)} collective-permute-done((bf16[96,384]{1,0:T(8,128)(2,1)S(1)}, bf16[96,384]{1,0:T(8,128)(2,1)S(1)}, u32[]{:S(2)}, u32[]{:S(2)}) %collective-permute-start.10) | collective-permute-done | bytes 73760 | tf_op jit(solution)/shard_map/ppermute | solution.py:68
  40.8 1.5 %collective-permute-done.7 = bf16[112,384]{1,0:T(8,128)(2,1)S(1)} collective-permute-done((bf16[112,384]{1,0:T(8,128)(2,1)S(1)}, bf16[112,384]{1,0:T(8,128)(2,1)S(1)}, u32[]{:S(2)}, u32[]{:S(2)}) %collective-permute-start.7) | collective-permute-done | bytes 86048 | tf_op jit(solution)/shard_map/ppermute | solution.py:68
  42.4 0.8 %collective-permute-start.23 = (bf16[48,384]{1,0:T(8,128)(2,1)S(1)}, bf16[48,384]{1,0:T(8,128)(2,1)S(1)}, u32[]{:S(2)}, u32[]{:S(2)}) collective-permute-start(bf16[48,384]{1,0:T(8,128)(2,1)S(1)} %slice.180), channel_id=1, source_target_pairs={{0,8},{1,9},{2,10},{3,11},{4,12},{5,13},{6,14},{7,15},{8,0},{9,1},... | collective-permute-start | bytes 110600 | tf_op jit(solution)/shard_map/ppermute | solution.py:68
  43.3 1.2 %collective-permute-start.16 = (bf16[64,384]{1,0:T(8,128)(2,1)S(1)}, bf16[64,384]{1,0:T(8,128)(2,1)S(1)}, u32[]{:S(2)}, u32[]{:S(2)}) collective-permute-start(bf16[64,384]{1,0:T(8,128)(2,1)S(1)} %pad_maximum_fusion.9), channel_id=1, source_target_pairs={{0,8},{1,9},{2,10},{3,11},{4,12},{5,13},{6,14},{7,15},{8,0},{9,1},... | collective-permute-start | bytes 147464 | tf_op jit(solution)/shard_map/ppermute | solution.py:68
  44.5 1.9 %collective-permute-done.23 = bf16[48,384]{1,0:T(8,128)(2,1)S(1)} collective-permute-done((bf16[48,384]{1,0:T(8,128)(2,1)S(1)}, bf16[48,384]{1,0:T(8,128)(2,1)S(1)}, u32[]{:S(2)}, u32[]{:S(2)}) %collective-permute-start.23) | collective-permute-done | bytes 36896 | tf_op jit(solution)/shard_map/ppermute | solution.py:68
  46.5 2.1 %collective-permute-start.24 = (bf16[48,384]{1,0:T(8,128)(2,1)S(1)}, bf16[48,384]{1,0:T(8,128)(2,1)S(1)}, u32[]{:S(2)}, u32[]{:S(2)}) collective-permute-start(bf16[48,384]{1,0:T(8,128)(2,1)S(1)} %fusion), channel_id=1, source_target_pairs={{0,16},{1,17},{2,18},{3,19},{4,20},{5,21},{6,22},{7,23},{8,24},{9,... | collective-permute-start | bytes 110600 | tf_op jit(solution)/shard_map/ppermute | solution.py:68
  48.6 1.9 %collective-permute-start.17 = (bf16[64,384]{1,0:T(8,128)(2,1)S(1)}, bf16[64,384]{1,0:T(8,128)(2,1)S(1)}, u32[]{:S(2)}, u32[]{:S(2)}) collective-permute-start(bf16[64,384]{1,0:T(8,128)(2,1)S(1)} %pad_maximum_fusion.13), channel_id=1, source_target_pairs={{0,16},{1,17},{2,18},{3,19},{4,20},{5,21},{6,22},{7,23},{8,24},{9,... | collective-permute-start | bytes 147464 | tf_op jit(solution)/shard_map/ppermute | solution.py:68
  50.5 1.0 %collective-permute-done.24 = bf16[48,384]{1,0:T(8,128)(2,1)S(1)} collective-permute-done((bf16[48,384]{1,0:T(8,128)(2,1)S(1)}, bf16[48,384]{1,0:T(8,128)(2,1)S(1)}, u32[]{:S(2)}, u32[]{:S(2)}) %collective-permute-start.24) | collective-permute-done | bytes 36896 | tf_op jit(solution)/shard_map/ppermute | solution.py:68
  51.5 1.9 %collective-permute-start.25 = (bf16[48,384]{1,0:T(8,128)(2,1)S(1)}, bf16[48,384]{1,0:T(8,128)(2,1)S(1)}, u32[]{:S(2)}, u32[]{:S(2)}) collective-permute-start(bf16[48,384]{1,0:T(8,128)(2,1)S(1)} %add_convert_fusion), channel_id=1, source_target_pairs={{0,8},{1,9},{2,10},{3,11},{4,12},{5,13},{6,14},{7,15},{8,0},{9,1},... | collective-permute-start | bytes 110600 | tf_op jit(solution)/shard_map/ppermute | solution.py:68
  53.4 0.3 collective-permute-done.17
  53.7 2.5 %collective-permute-start.18 = (bf16[48,384]{1,0:T(8,128)(2,1)S(1)}, bf16[48,384]{1,0:T(8,128)(2,1)S(1)}, u32[]{:S(2)}, u32[]{:S(2)}) collective-permute-start(bf16[48,384]{1,0:T(8,128)(2,1)S(1)} %add_convert_fusion.1), channel_id=1, source_target_pairs={{0,8},{1,9},{2,10},{3,11},{4,12},{5,13},{6,14},{7,15},{8,0},{9,1},... | collective-permute-start | bytes 110600 | tf_op jit(solution)/shard_map/ppermute | solution.py:68
  56.2 1.4 %collective-permute-start.26 = (bf16[96,384]{1,0:T(8,128)(2,1)S(1)}, bf16[96,384]{1,0:T(8,128)(2,1)S(1)}, u32[]{:S(2)}, u32[]{:S(2)}) collective-permute-start(bf16[96,384]{1,0:T(8,128)(2,1)S(1)} %pad_maximum_fusion.5), channel_id=1, source_target_pairs={{0,2},{1,3},{2,0},{3,1},{4,6},{5,7},{6,4},{7,5},{8,10},{9,11},{10,... | collective-permute-start | bytes 221192 | tf_op jit(solution)/shard_map/ppermute | solution.py:68
  57.7 0.5 collective-permute-done.18
  58.1 1.6 %collective-permute-start.19 = (bf16[96,384]{1,0:T(8,128)(2,1)S(1)}, bf16[96,384]{1,0:T(8,128)(2,1)S(1)}, u32[]{:S(2)}, u32[]{:S(2)}) collective-permute-start(bf16[96,384]{1,0:T(8,128)(2,1)S(1)} %pad_maximum_fusion.4), channel_id=1, source_target_pairs={{0,4},{1,5},{2,6},{3,7},{4,0},{5,1},{6,2},{7,3},{8,12},{9,13},{10,... | collective-permute-start | bytes 221192 | tf_op jit(solution)/shard_map/ppermute | solution.py:68
  59.7 0.9 %collective-permute-done.26 = bf16[96,384]{1,0:T(8,128)(2,1)S(1)} collective-permute-done((bf16[96,384]{1,0:T(8,128)(2,1)S(1)}, bf16[96,384]{1,0:T(8,128)(2,1)S(1)}, u32[]{:S(2)}, u32[]{:S(2)}) %collective-permute-start.26) | collective-permute-done | bytes 73760 | tf_op jit(solution)/shard_map/ppermute | solution.py:68
  60.6 1.6 %collective-permute-start.27 = (bf16[192,384]{1,0:T(8,128)(2,1)S(1)}, bf16[192,384]{1,0:T(8,128)(2,1)S(1)}, u32[]{:S(2)}, u32[]{:S(2)}) collective-permute-start(bf16[192,384]{1,0:T(8,128)(2,1)S(1)} %pad_maximum_fusion.2.refs_0_), channel_id=1, source_target_pairs={{0,4},{1,5},{2,6},{3,7},{4,0},{5,1},{6,2},{7,3},{8,12},{9,13},{10,... | collective-permute-start | bytes 442376 | tf_op jit(solution)/shard_map/ppermute | solution.py:68
  62.2 0.4 collective-permute-done.19
  62.6 1.4 %collective-permute-start.20 = (bf16[192,384]{1,0:T(8,128)(2,1)S(1)}, bf16[192,384]{1,0:T(8,128)(2,1)S(1)}, u32[]{:S(2)}, u32[]{:S(2)}) collective-permute-start(bf16[192,384]{1,0:T(8,128)(2,1)S(1)} %pad_maximum_fusion.1.refs_0_), channel_id=1, source_target_pairs={{0,2},{1,3},{2,0},{3,1},{4,6},{5,7},{6,4},{7,5},{8,10},{9,11},{10,... | collective-permute-start | bytes 442376 | tf_op jit(solution)/shard_map/ppermute | solution.py:68
  64.0 3.7 %collective-permute-done.15.halo_ref = bf16[128,384]{1,0:T(8,128)(2,1)S(1)} collective-permute-done((bf16[128,384]{1,0:T(8,128)(2,1)S(1)}, bf16[128,384]{1,0:T(8,128)(2,1)S(1)}, u32[]{:S(2)}, u32[]{:S(2)}) %collective-permute-start.15) | collective-permute-done | bytes 98336 | tf_op jit(solution)/shard_map/ppermute | solution.py:74
  67.7 2.5 %return_rows.1 = f32[256,384]{1,0:T(8,128)} custom-call(s32[4]{0:T(128)S(1)} %pad_add_fusion.place_ref, s32[8,32]{1,0:T(8,128)} %send_hbm.3, f32[256,384]{1,0:T(8,128)S(1)} %get-tuple-element.62.gf_ref, bf16[128,384]{1,0:T(8,128)(2,1)S(1)} %collective-permute-done.15.halo_ref, bf16[32,384]{1,0:T(8,128)(2,1)S(1)} %get-tuple-element.76.refs_0_, ...), custom_call_target="tpu_custom_call" | custom-call | bytes 1156112 | tf_op jit(solution)/shard_map/return_rows/pallas_call | solution.py:447
  70.2 1.0 %collective-permute-start.28 = (bf16[192,384]{1,0:T(8,128)(2,1)S(1)}, bf16[192,384]{1,0:T(8,128)(2,1)S(1)}, u32[]{:S(2)}, u32[]{:S(2)}) collective-permute-start(bf16[192,384]{1,0:T(8,128)(2,1)S(1)} %pad_maximum_fusion.2.refs_0_), channel_id=1, source_target_pairs={{0,1},{1,0},{2,3},{3,2},{4,5},{5,4},{6,7},{7,6},{8,9},{9,8},{10,11... | collective-permute-start | bytes 442376 | tf_op jit(solution)/shard_map/ppermute | solution.py:68
  71.2 0.1 collective-permute-start.21
  71.3 0.4 collective-permute-start.29
  71.7 0.1 collective-permute-start.22
  71.8 0.6 convert_add_fusion.2
  72.4 0.4 collective-permute-done.29.refs_3_
  72.8 1.7 %place_wkv.1 = f32[384,768]{1,0:T(8,128)} custom-call(s32[4]{0:T(128)S(1)} %pad_add_fusion.place_ref, bf16[192,384]{1,0:T(8,128)(2,1)S(1)} %pad_maximum_fusion.2.refs_0_, bf16[192,384]{1,0:T(8,128)(2,1)S(1)} %collective-permute-done.27.refs_1_, bf16[192,384]{1,0:T(8,128)(2,1)S(1)} %collective-permute-done.28.refs_2_, ...), custom_call_target="tpu_custom_call" | custom-call | bytes 1769488 | tf_op jit(solution)/shard_map/place_wkv/pallas_call | solution.py:447
  74.6 1.7 %place_wq_wo.1 = (f32[384,384]{1,0:T(8,128)}, f32[384,384]{1,0:T(8,128)}) custom-call(s32[4]{0:T(128)S(1)} %pad_add_fusion.place_ref, bf16[192,384]{1,0:T(8,128)(2,1)S(1)} %pad_maximum_fusion.1.refs_0_, bf16[192,384]{1,0:T(8,128)(2,1)S(1)} %collective-permute-done.20.refs_1_, bf16[192,384]{1,0:T(8,128)(2,1)S(1)} %collective-permute-done.21.refs_2_, ...), custom_call_target="tpu_custom_call" | custom-call | bytes 1769488 | tf_op jit(solution)/shard_map/place_wq_wo/pallas_call | solution.py:447
  (57 shorter events, 0.6 us)
Async XLA Ops:
  2.5 5.8 %collective-permute-start = (bf16[128,384]{1,0:T(8,128)(2,1)S(1)}, bf16[128,384]{1,0:T(8,128)(2,1)S(1)}, u32[]{:S(2)}, u32[]{:S(2)}) collective-permute-start(bf16[128,384]{1,0:T(8,128)(2,1)S(1)} %get-tuple-element.46), channel_id=1, source_target_pairs={{0,4},{1,5},{2,6},{3,7},{4,0},{5,1},{6,2},{7,3},{8,12},{9,13},{10,... | collective-permute-start | bytes 294920 | tf_op jit(solution)/shard_map/ppermute | solution.py:68
  8.3 8.2 %collective-permute-start.2 = (bf16[64,384]{1,0:T(8,128)(2,1)S(1)}, bf16[64,384]{1,0:T(8,128)(2,1)S(1)}, u32[]{:S(2)}, u32[]{:S(2)}) collective-permute-start(bf16[64,384]{1,0:T(8,128)(2,1)S(1)} %pad_maximum_fusion.6), channel_id=1, source_target_pairs={{0,24},{1,25},{2,26},{3,27},{4,28},{5,29},{6,30},{7,31},{8,16},{9,... | collective-permute-start | bytes 147464 | tf_op jit(solution)/shard_map/ppermute | solution.py:68
  12.3 5.1 %collective-permute-start.3 = (bf16[64,384]{1,0:T(8,128)(2,1)S(1)}, bf16[64,384]{1,0:T(8,128)(2,1)S(1)}, u32[]{:S(2)}, u32[]{:S(2)}) collective-permute-start(bf16[64,384]{1,0:T(8,128)(2,1)S(1)} %pad_maximum_fusion.7), channel_id=1, source_target_pairs={{0,16},{1,17},{2,18},{3,19},{4,20},{5,21},{6,22},{7,23},{8,24},{9,... | collective-permute-start | bytes 147464 | tf_op jit(solution)/shard_map/ppermute | solution.py:68
  12.3 5.1 %collective-permute-start.1 = (bf16[128,384]{1,0:T(8,128)(2,1)S(1)}, bf16[128,384]{1,0:T(8,128)(2,1)S(1)}, u32[]{:S(2)}, u32[]{:S(2)}) collective-permute-start(bf16[128,384]{1,0:T(8,128)(2,1)S(1)} %get-tuple-element.47), channel_id=1, source_target_pairs={{3,0},{0,1},{1,2},{2,3},{7,4},{4,5},{5,6},{6,7},{11,8},{8,9},{9,10... | collective-permute-start | bytes 294920 | tf_op jit(solution)/shard_map/ppermute | solution.py:74
  12.4 5.0 %collective-permute-start.4 = (bf16[64,384]{1,0:T(8,128)(2,1)S(1)}, bf16[64,384]{1,0:T(8,128)(2,1)S(1)}, u32[]{:S(2)}, u32[]{:S(2)}) collective-permute-start(bf16[64,384]{1,0:T(8,128)(2,1)S(1)} %pad_maximum_fusion.8), channel_id=1, source_target_pairs={{0,8},{1,9},{2,10},{3,11},{4,12},{5,13},{6,14},{7,15},{8,0},{9,1},... | collective-permute-start | bytes 147464 | tf_op jit(solution)/shard_map/ppermute | solution.py:68
  25.6 2.2 %collective-permute-start.8 = (bf16[384,384]{1,0:T(8,128)(2,1)S(1)}, bf16[384,384]{1,0:T(8,128)(2,1)S(1)}, u32[]{:S(2)}, u32[]{:S(2)}) collective-permute-start(bf16[384,384]{1,0:T(8,128)(2,1)S(1)} %get-tuple-element.67), channel_id=1, source_target_pairs={{0,1},{1,0},{2,3},{3,2},{4,5},{5,4},{6,7},{7,6},{8,9},{9,8},{10,11... | collective-permute-start | bytes 884744 | tf_op jit(solution)/shard_map/ppermute | solution.py:68
  26.2 2.9 %collective-permute-start.5 = (bf16[400,384]{1,0:T(8,128)(2,1)S(1)}, bf16[400,384]{1,0:T(8,128)(2,1)S(1)}, u32[]{:S(2)}, u32[]{:S(2)}) collective-permute-start(bf16[400,384]{1,0:T(8,128)(2,1)S(1)} %get-tuple-element.64), channel_id=1, source_target_pairs={{0,1},{1,0},{2,3},{3,2},{4,5},{5,4},{6,7},{7,6},{8,9},{9,8},{10,11... | collective-permute-start | bytes 921608 | tf_op jit(solution)/shard_map/ppermute | solution.py:68
  26.2 5.6 %collective-permute-start.11 = (bf16[128,384]{1,0:T(8,128)(2,1)S(1)}, bf16[128,384]{1,0:T(8,128)(2,1)S(1)}, u32[]{:S(2)}, u32[]{:S(2)}) collective-permute-start(bf16[128,384]{1,0:T(8,128)(2,1)S(1)} %get-tuple-element.69), channel_id=1, source_target_pairs={{0,4},{1,5},{2,6},{3,7},{4,0},{5,1},{6,2},{7,3},{8,12},{9,13},{10,... | collective-permute-start | bytes 294920 | tf_op jit(solution)/shard_map/ppermute | solution.py:68
  27.8 8.5 %collective-permute-start.9 = (bf16[192,384]{1,0:T(8,128)(2,1)S(1)}, bf16[192,384]{1,0:T(8,128)(2,1)S(1)}, u32[]{:S(2)}, u32[]{:S(2)}) collective-permute-start(bf16[192,384]{1,0:T(8,128)(2,1)S(1)} %slice.176), channel_id=1, source_target_pairs={{0,4},{1,5},{2,6},{3,7},{4,0},{5,1},{6,2},{7,3},{8,12},{9,13},{10,... | collective-permute-start | bytes 442376 | tf_op jit(solution)/shard_map/ppermute | solution.py:68
  29.2 8.5 %collective-permute-start.6 = (bf16[208,384]{1,0:T(8,128)(2,1)S(1)}, bf16[208,384]{1,0:T(8,128)(2,1)S(1)}, u32[]{:S(2)}, u32[]{:S(2)}) collective-permute-start(bf16[208,384]{1,0:T(8,128)(2,1)S(1)} %pad_maximum_fusion), channel_id=1, source_target_pairs={{0,2},{1,3},{2,0},{3,1},{4,6},{5,7},{6,4},{7,5},{8,10},{9,11},{10,... | collective-permute-start | bytes 479240 | tf_op jit(solution)/shard_map/ppermute | solution.py:68
  31.9 10.5 %collective-permute-start.12 = (bf16[64,384]{1,0:T(8,128)(2,1)S(1)}, bf16[64,384]{1,0:T(8,128)(2,1)S(1)}, u32[]{:S(2)}, u32[]{:S(2)}) collective-permute-start(bf16[64,384]{1,0:T(8,128)(2,1)S(1)} %pad_maximum_fusion.10), channel_id=1, source_target_pairs={{0,24},{1,25},{2,26},{3,27},{4,28},{5,29},{6,30},{7,31},{8,16},{9,... | collective-permute-start | bytes 147464 | tf_op jit(solution)/shard_map/ppermute | solution.py:68
  35.5 6.9 %collective-permute-start.13 = (bf16[64,384]{1,0:T(8,128)(2,1)S(1)}, bf16[64,384]{1,0:T(8,128)(2,1)S(1)}, u32[]{:S(2)}, u32[]{:S(2)}) collective-permute-start(bf16[64,384]{1,0:T(8,128)(2,1)S(1)} %pad_maximum_fusion.11), channel_id=1, source_target_pairs={{0,16},{1,17},{2,18},{3,19},{4,20},{5,21},{6,22},{7,23},{8,24},{9,... | collective-permute-start | bytes 147464 | tf_op jit(solution)/shard_map/ppermute | solution.py:68
  35.6 6.9 %collective-permute-start.14 = (bf16[64,384]{1,0:T(8,128)(2,1)S(1)}, bf16[64,384]{1,0:T(8,128)(2,1)S(1)}, u32[]{:S(2)}, u32[]{:S(2)}) collective-permute-start(bf16[64,384]{1,0:T(8,128)(2,1)S(1)} %pad_maximum_fusion.12), channel_id=1, source_target_pairs={{0,8},{1,9},{2,10},{3,11},{4,12},{5,13},{6,14},{7,15},{8,0},{9,1},... | collective-permute-start | bytes 147464 | tf_op jit(solution)/shard_map/ppermute | solution.py:68
  36.4 4.4 %collective-permute-start.10 = (bf16[96,384]{1,0:T(8,128)(2,1)S(1)}, bf16[96,384]{1,0:T(8,128)(2,1)S(1)}, u32[]{:S(2)}, u32[]{:S(2)}) collective-permute-start(bf16[96,384]{1,0:T(8,128)(2,1)S(1)} %slice.178), channel_id=1, source_target_pairs={{0,2},{1,3},{2,0},{3,1},{4,6},{5,7},{6,4},{7,5},{8,10},{9,11},{10,... | collective-permute-start | bytes 221192 | tf_op jit(solution)/shard_map/ppermute | solution.py:68
  37.8 4.6 %collective-permute-start.7 = (bf16[112,384]{1,0:T(8,128)(2,1)S(1)}, bf16[112,384]{1,0:T(8,128)(2,1)S(1)}, u32[]{:S(2)}, u32[]{:S(2)}) collective-permute-start(bf16[112,384]{1,0:T(8,128)(2,1)S(1)} %pad_maximum_fusion.3), channel_id=1, source_target_pairs={{0,4},{1,5},{2,6},{3,7},{4,0},{5,1},{6,2},{7,3},{8,12},{9,13},{10,... | collective-permute-start | bytes 258056 | tf_op jit(solution)/shard_map/ppermute | solution.py:68
  42.4 4.0 %collective-permute-start.23 = (bf16[48,384]{1,0:T(8,128)(2,1)S(1)}, bf16[48,384]{1,0:T(8,128)(2,1)S(1)}, u32[]{:S(2)}, u32[]{:S(2)}) collective-permute-start(bf16[48,384]{1,0:T(8,128)(2,1)S(1)} %slice.180), channel_id=1, source_target_pairs={{0,8},{1,9},{2,10},{3,11},{4,12},{5,13},{6,14},{7,15},{8,0},{9,1},... | collective-permute-start | bytes 110600 | tf_op jit(solution)/shard_map/ppermute | solution.py:68
  43.3 5.3 %collective-permute-start.16 = (bf16[64,384]{1,0:T(8,128)(2,1)S(1)}, bf16[64,384]{1,0:T(8,128)(2,1)S(1)}, u32[]{:S(2)}, u32[]{:S(2)}) collective-permute-start(bf16[64,384]{1,0:T(8,128)(2,1)S(1)} %pad_maximum_fusion.9), channel_id=1, source_target_pairs={{0,8},{1,9},{2,10},{3,11},{4,12},{5,13},{6,14},{7,15},{8,0},{9,1},... | collective-permute-start | bytes 147464 | tf_op jit(solution)/shard_map/ppermute | solution.py:68
  46.5 5.0 %collective-permute-start.24 = (bf16[48,384]{1,0:T(8,128)(2,1)S(1)}, bf16[48,384]{1,0:T(8,128)(2,1)S(1)}, u32[]{:S(2)}, u32[]{:S(2)}) collective-permute-start(bf16[48,384]{1,0:T(8,128)(2,1)S(1)} %fusion), channel_id=1, source_target_pairs={{0,16},{1,17},{2,18},{3,19},{4,20},{5,21},{6,22},{7,23},{8,24},{9,... | collective-permute-start | bytes 110600 | tf_op jit(solution)/shard_map/ppermute | solution.py:68
  48.6 5.1 %collective-permute-start.17 = (bf16[64,384]{1,0:T(8,128)(2,1)S(1)}, bf16[64,384]{1,0:T(8,128)(2,1)S(1)}, u32[]{:S(2)}, u32[]{:S(2)}) collective-permute-start(bf16[64,384]{1,0:T(8,128)(2,1)S(1)} %pad_maximum_fusion.13), channel_id=1, source_target_pairs={{0,16},{1,17},{2,18},{3,19},{4,20},{5,21},{6,22},{7,23},{8,24},{9,... | collective-permute-start | bytes 147464 | tf_op jit(solution)/shard_map/ppermute | solution.py:68
  51.5 4.7 %collective-permute-start.25 = (bf16[48,384]{1,0:T(8,128)(2,1)S(1)}, bf16[48,384]{1,0:T(8,128)(2,1)S(1)}, u32[]{:S(2)}, u32[]{:S(2)}) collective-permute-start(bf16[48,384]{1,0:T(8,128)(2,1)S(1)} %add_convert_fusion), channel_id=1, source_target_pairs={{0,8},{1,9},{2,10},{3,11},{4,12},{5,13},{6,14},{7,15},{8,0},{9,1},... | collective-permute-start | bytes 110600 | tf_op jit(solution)/shard_map/ppermute | solution.py:68
  53.7 4.5 %collective-permute-start.18 = (bf16[48,384]{1,0:T(8,128)(2,1)S(1)}, bf16[48,384]{1,0:T(8,128)(2,1)S(1)}, u32[]{:S(2)}, u32[]{:S(2)}) collective-permute-start(bf16[48,384]{1,0:T(8,128)(2,1)S(1)} %add_convert_fusion.1), channel_id=1, source_target_pairs={{0,8},{1,9},{2,10},{3,11},{4,12},{5,13},{6,14},{7,15},{8,0},{9,1},... | collective-permute-start | bytes 110600 | tf_op jit(solution)/shard_map/ppermute | solution.py:68
  56.2 4.4 %collective-permute-start.26 = (bf16[96,384]{1,0:T(8,128)(2,1)S(1)}, bf16[96,384]{1,0:T(8,128)(2,1)S(1)}, u32[]{:S(2)}, u32[]{:S(2)}) collective-permute-start(bf16[96,384]{1,0:T(8,128)(2,1)S(1)} %pad_maximum_fusion.5), channel_id=1, source_target_pairs={{0,2},{1,3},{2,0},{3,1},{4,6},{5,7},{6,4},{7,5},{8,10},{9,11},{10,... | collective-permute-start | bytes 221192 | tf_op jit(solution)/shard_map/ppermute | solution.py:68
  58.1 4.4 %collective-permute-start.19 = (bf16[96,384]{1,0:T(8,128)(2,1)S(1)}, bf16[96,384]{1,0:T(8,128)(2,1)S(1)}, u32[]{:S(2)}, u32[]{:S(2)}) collective-permute-start(bf16[96,384]{1,0:T(8,128)(2,1)S(1)} %pad_maximum_fusion.4), channel_id=1, source_target_pairs={{0,4},{1,5},{2,6},{3,7},{4,0},{5,1},{6,2},{7,3},{8,12},{9,13},{10,... | collective-permute-start | bytes 221192 | tf_op jit(solution)/shard_map/ppermute | solution.py:68
  60.6 10.7 %collective-permute-start.27 = (bf16[192,384]{1,0:T(8,128)(2,1)S(1)}, bf16[192,384]{1,0:T(8,128)(2,1)S(1)}, u32[]{:S(2)}, u32[]{:S(2)}) collective-permute-start(bf16[192,384]{1,0:T(8,128)(2,1)S(1)} %pad_maximum_fusion.2.refs_0_), channel_id=1, source_target_pairs={{0,4},{1,5},{2,6},{3,7},{4,0},{5,1},{6,2},{7,3},{8,12},{9,13},{10,... | collective-permute-start | bytes 442376 | tf_op jit(solution)/shard_map/ppermute | solution.py:68
  62.6 9.2 %collective-permute-start.20 = (bf16[192,384]{1,0:T(8,128)(2,1)S(1)}, bf16[192,384]{1,0:T(8,128)(2,1)S(1)}, u32[]{:S(2)}, u32[]{:S(2)}) collective-permute-start(bf16[192,384]{1,0:T(8,128)(2,1)S(1)} %pad_maximum_fusion.1.refs_0_), channel_id=1, source_target_pairs={{0,2},{1,3},{2,0},{3,1},{4,6},{5,7},{6,4},{7,5},{8,10},{9,11},{10,... | collective-permute-start | bytes 442376 | tf_op jit(solution)/shard_map/ppermute | solution.py:68
  64.0 3.7 %collective-permute-start.15 = (bf16[128,384]{1,0:T(8,128)(2,1)S(1)}, bf16[128,384]{1,0:T(8,128)(2,1)S(1)}, u32[]{:S(2)}, u32[]{:S(2)}) collective-permute-start(bf16[128,384]{1,0:T(8,128)(2,1)S(1)} %get-tuple-element.75), channel_id=1, source_target_pairs={{1,0},{2,1},{3,2},{0,3},{5,4},{6,5},{7,6},{4,7},{9,8},{10,9},{11,1... | collective-permute-start | bytes 294920 | tf_op jit(solution)/shard_map/ppermute | solution.py:74
  70.2 2.2 %collective-permute-start.28 = (bf16[192,384]{1,0:T(8,128)(2,1)S(1)}, bf16[192,384]{1,0:T(8,128)(2,1)S(1)}, u32[]{:S(2)}, u32[]{:S(2)}) collective-permute-start(bf16[192,384]{1,0:T(8,128)(2,1)S(1)} %pad_maximum_fusion.2.refs_0_), channel_id=1, source_target_pairs={{0,1},{1,0},{2,3},{3,2},{4,5},{5,4},{6,7},{7,6},{8,9},{9,8},{10,11... | collective-permute-start | bytes 442376 | tf_op jit(solution)/shard_map/ppermute | solution.py:68
  71.2 3.3 %collective-permute-start.21 = (bf16[192,384]{1,0:T(8,128)(2,1)S(1)}, bf16[192,384]{1,0:T(8,128)(2,1)S(1)}, u32[]{:S(2)}, u32[]{:S(2)}) collective-permute-start(bf16[192,384]{1,0:T(8,128)(2,1)S(1)} %pad_maximum_fusion.1.refs_0_), channel_id=1, source_target_pairs={{0,1},{1,0},{2,3},{3,2},{4,5},{5,4},{6,7},{7,6},{8,9},{9,8},{10,11... | collective-permute-start | bytes 442376 | tf_op jit(solution)/shard_map/ppermute | solution.py:68
  71.3 1.5 %collective-permute-start.29 = (bf16[192,384]{1,0:T(8,128)(2,1)S(1)}, bf16[192,384]{1,0:T(8,128)(2,1)S(1)}, u32[]{:S(2)}, u32[]{:S(2)}) collective-permute-start(bf16[192,384]{1,0:T(8,128)(2,1)S(1)} %collective-permute-done.27.refs_1_), channel_id=1, source_target_pairs={{0,1},{1,0},{2,3},{3,2},{4,5},{5,4},{6,7},{7,6},{8,9},{9,8},{10,11... | collective-permute-start | bytes 442376 | tf_op jit(solution)/shard_map/ppermute | solution.py:68
  71.7 2.8 %collective-permute-start.22 = (bf16[192,384]{1,0:T(8,128)(2,1)S(1)}, bf16[192,384]{1,0:T(8,128)(2,1)S(1)}, u32[]{:S(2)}, u32[]{:S(2)}) collective-permute-start(bf16[192,384]{1,0:T(8,128)(2,1)S(1)} %collective-permute-done.20.refs_1_), channel_id=1, source_target_pairs={{0,1},{1,0},{2,3},{3,2},{4,5},{5,4},{6,7},{7,6},{8,9},{9,8},{10,11... | collective-permute-start | bytes 442376 | tf_op jit(solution)/shard_map/ppermute | solution.py:68

commit v9 on v7

--- a/solution.py
+++ b/solution.py
@@ -36,40 +36,38 @@
     return value.astype(jnp.bfloat16)
 
 
-def exchange_stages(dom_size, rows_size):
-    stages = [[((0, 1), (0, 1))], [((1, 2), (0, 2)), ((1, 0), (1, 2))]]
-    stages += [[((bit, 0), (bit, 0))] for bit in powers_of_two(2, dom_size)]
-    stages += [[((0, bit), (0, bit))] for bit in powers_of_two(4, rows_size)]
-    return stages
-
-
-def powers_of_two(first, size):
+CORES = (0, 1)
+
+
+def bits_of(size, first=1):
     return [1 << i for i in range(size.bit_length() - 1) if 1 << i >= first]
 
 
-def partner_masks(stage):
+def exchange_plan():
+    dom_size, rows_size = lax.axis_size("dom"), lax.axis_size("rows")
+    block = [(1, 0), (0, 2), (2, 0)]
+    rest = [(bit, 0) for bit in bits_of(dom_size, 4)] + [(0, bit) for bit in bits_of(rows_size, 4)]
+    return block, rest
+
+
+def partner_masks(block):
     masks = []
-    for digit in range(1, 1 << len(stage)):
-        dom_mask = rows_mask = 0
-        for i, (mask, _) in enumerate(stage):
-            if digit >> i & 1:
-                dom_mask ^= mask[0]
-                rows_mask ^= mask[1]
-        masks.append((dom_mask, rows_mask))
+    for digit in range(1 << len(block)):
+        chosen = [mask for i, mask in enumerate(block) if digit >> i & 1]
+        masks.append((sum(mask[0] for mask in chosen), sum(mask[1] for mask in chosen)))
     return masks
 
 
-def own_piece(stages):
-    index = jnp.int32(0)
-    for stage in stages:
-        index = index << len(stage)
-        for i, (_, parity) in enumerate(stage):
-            odd = jnp.int32(0)
-            for axis, mask in zip(("dom", "rows"), parity):
-                for bit in powers_of_two(1, 2 * mask) if mask else []:
-                    odd ^= jnp.where(lax.axis_index(axis) & bit & mask, 1, 0)
-            index += odd << i
-    return index
+def farthest_first(count):
+    return sorted(range(1, count), key=lambda digit: (-digit.bit_count(), -digit))
+
+
+def own_digit(block):
+    digit = 0
+    for i, (dom_mask, rows_mask) in enumerate(block):
+        own = (lax.axis_index("dom") & dom_mask) | (lax.axis_index("rows") & rows_mask)
+        digit += jnp.where(own != 0, 1 << i, 0)
+    return digit
 
 
 def swapped(block, dom_mask, rows_mask):
@@ -94,52 +92,31 @@
     return terms[0]
 
 
-def routed(direct, through):
-    return handed_on(direct, swapped(through, 1, 0))
-
-
-def handed_on(direct, through):
-    rows = direct[0].shape[0]
-    arrived = []
-    for at in reversed(range(1, len(direct))):
-        message = jnp.concatenate([direct[at], through[at * rows : (at + 1) * rows]], axis=0)
-        arrived.append(swapped(message, 2 * at, 0))
-    return [direct[0], through] + arrived
-
-
-def scatter_stage(keep, rider, stage, halved):
-    part = keep.shape[0] >> len(stage) if halved else keep.shape[0]
-    rider_bf = rounded(rider)
-    if not halved:
-        keep = rounded(keep).astype(jnp.float32)
-    messages = []
-    for at in range(1, 1 << len(stage)):
-        block = keep[at * part : (at + 1) * part] if halved else keep
-        messages.append(jnp.concatenate([rounded(block), rider_bf], axis=0))
-    return keep[:part], rider_bf.astype(jnp.float32), messages
-
-
-def exchange(messages, stage):
-    return [swapped(message, *masks) for message, masks in zip(messages, partner_masks(stage))]
+def with_rider(block, rider):
+    return jnp.concatenate([rounded(block), rounded(rider)], axis=0)
 
 
 def added(keep, rider, arrived):
-    part = keep.shape[0]
-    terms = [keep] + [block[:part].astype(jnp.float32) for block in arrived]
-    riders = [rider] + [block[part:].astype(jnp.float32) for block in arrived]
-    return paired_sum(terms), paired_sum(riders)
-
-
-def gathered(held, stage):
-    return jnp.concatenate([held] + exchange([held] * ((1 << len(stage)) - 1), stage), axis=0)
-
-
-def listed_rows(dom, send_ref, row_count):
+    rows = keep.shape[0]
+    riders = [rider] + [arrived[at][rows:].astype(jnp.float32) for at in sorted(arrived)]
+    for block in arrived.values():
+        keep = keep + block[:rows].astype(jnp.float32)
+    return keep, paired_sum(riders)
+
+
+def hop(blocks, bit):
+    moving = [at for at in range(len(blocks)) if at & bit]
+    rows = blocks[0].shape[0]
+    arrived = swapped(jnp.concatenate([blocks[at] for at in moving], axis=0), bit, 0)
+    return {at: arrived[i * rows : (i + 1) * rows] for i, at in enumerate(moving)}
+
+
+def listed_rows(send_ref, row_count):
     dom_size, per_peer = send_ref.shape
     slots = dom_size * per_peer
     slot = lax.broadcasted_iota(jnp.int32, (slots, per_peer), 0)
     place = lax.broadcasted_iota(jnp.int32, (slots, per_peer), 1)
-    peer = (slot // per_peer) ^ dom
+    peer = (slot // per_peer) ^ lax.axis_index("dom")
     listed = jnp.zeros((slots, per_peer), jnp.int32)
     for at in range(dom_size):
         listed += jnp.where((peer == at) & (place == slot % per_peer), send_ref[at : at + 1, :], 0)
@@ -158,25 +135,21 @@
     return copies
 
 
-def pick_kernel(place_ref, feat_hbm, send_hbm, halo_ref, through_ref, *refs):
-    direct_refs, (feat_ref, send_ref, sems) = refs[:-3], refs[-3:]
+def pick_kernel(feat_hbm, send_hbm, halo_ref, chosen_ref, *refs):
+    out_refs, (feat_ref, send_ref, sems) = refs[:-3], refs[-3:]
     copies = fetch([(send_hbm, send_ref), (feat_hbm, feat_ref)], sems)
     copies[0].wait()
     per_peer = send_ref.shape[1]
-    chosen = listed_rows(place_ref[0], send_ref, feat_ref.shape[0])
+    chosen_ref[...] = listed_rows(send_ref, feat_ref.shape[0])
     copies[1].wait()
     halo_ref[...] = feat_ref[feat_ref.shape[0] - halo_ref.shape[0] :]
-    picked = rounded(f32_dot(chosen, feat_ref[...]))
-    for at, out_ref in enumerate(direct_refs):
-        out_ref[...] = picked[2 * at * per_peer : (2 * at + 1) * per_peer]
-        through_ref[at * per_peer : (at + 1) * per_peer] = picked[
-            (2 * at + 1) * per_peer : (2 * at + 2) * per_peer
-        ]
+    picked = rounded(f32_dot(chosen_ref[...], feat_ref[...]))
+    for at, out_ref in enumerate(out_refs):
+        out_ref[...] = picked[at * per_peer : (at + 1) * per_peer]
 
 
 def prepare_kernel(
     per_peer,
-    place_ref,
     feat_hbm,
     og_hbm,
     wq_hbm,
@@ -234,7 +207,7 @@
     local_bias_ref[...] = jnp.where(multiplicity(window, nbr_ref) > 0.0, 0.0, NEGATIVE_FILL)
     exp_copy.wait()
     expander = exp_ref[...]
-    expander = ((expander // per_peer) ^ place_ref[0]) * per_peer + expander % per_peer
+    expander = ((expander // per_peer) ^ lax.axis_index("dom")) * per_peer + expander % per_peer
     named_times = multiplicity(slots, expander)
     slot_bias = jnp.full((slots, row_count), NEGATIVE_FILL, jnp.float32)
     for times in range(1, exp_ref.shape[0] + 1):
@@ -266,15 +239,12 @@
     factor,
     per_peer,
     dom_size,
-    place_ref,
-    halo_ref,
     *refs,
 ):
-    piece_refs, refs = refs[: 1 + dom_size // 2], refs[1 + dom_size // 2 :]
+    piece_refs, halo_ref, refs = refs[:dom_size], refs[dom_size], refs[dom_size + 1 :]
     og_ref, wq_ref, wkv_ref, featt_ref, qt_ref, odt_ref, own_kv_ref, own_kvt_ref = refs[:8]
     local_bias_ref, far_bias_ref, gf_ref, halo_feat_ref = refs[8:12]
-    direct_refs, refs = refs[12 : 12 + dom_size // 2], refs[12 + dom_size // 2 :]
-    through_ref, refs = refs[0], refs[1:]
+    slot_feat_refs, refs = refs[12 : 12 + dom_size], refs[12 + dom_size :]
     keep_ref, send_ref, rider_ref = refs[:3]
     slot_ref, kv_ref, kvt_ref, extt_ref, gqt_ref, gkvt_ref, ot_ref = refs[3:]
     width, row_count = qt_ref.shape
@@ -292,10 +262,8 @@
     kvt_ref[:, virt_at:] = own_kvt_ref[:, row_count:]
     extt_ref[:, tile:near] = featt_ref[:, :row_count]
     extt_ref[:, virt_at:] = featt_ref[:, row_count:]
-    slot_ref[:per_peer] = piece_refs[0][...]
-    slot_ref[per_peer : 2 * per_peer] = piece_refs[1][:per_peer]
-    for at, piece_ref in enumerate(piece_refs[:1:-1], 1):
-        slot_ref[2 * at * per_peer : (2 * at + 2) * per_peer] = piece_ref[...]
+    for at, piece_ref in zip([0] + farthest_first(dom_size), piece_refs):
+        slot_ref[at * per_peer : (at + 1) * per_peer] = piece_ref[...]
     for rows, source_ref in ((slice(0, tile), halo_ref), (slice(near, virt_at), slot_ref)):
         extt_ref[:, rows] = source_ref[...].T
         kv_ref[rows] = rounded(f32_dot(source_ref[...], wkv_ref[...]))
@@ -375,11 +343,8 @@
     gf_ref[...] = own.T
     halo_feat_ref[...] = rounded(by_feature[:, :tile].T)
     slot_feat = rounded(by_feature[:, near:virt_at].T)
-    for at, out_ref in enumerate(direct_refs):
-        out_ref[...] = slot_feat[2 * at * per_peer : (2 * at + 1) * per_peer]
-        through_ref[at * per_peer : (at + 1) * per_peer] = slot_feat[
-            (2 * at + 1) * per_peer : (2 * at + 2) * per_peer
-        ]
+    for at, out_ref in enumerate(slot_feat_refs):
+        out_ref[...] = slot_feat[at * per_peer : (at + 1) * per_peer]
     rider_ref[...] = by_feature[:, virt_at:].T * factor
 
     sums = (
@@ -389,7 +354,7 @@
         f32_dot(ot_ref[...], og_ref[...]),
     )
     pieces = keep_ref.shape[0] // rows_per_piece
-    held = place_ref[1] % pieces
+    held = own_digit(exchange_plan()[0])
 
     def write(half, out_ref, cast):
         for piece in range(pieces):
@@ -400,7 +365,7 @@
 
     for half in range(2):
 
-        @pl.when(place_ref[1] // pieces == half)
+        @pl.when(lax.axis_index("rows") % 2 == half)
         def _():
             write(half, keep_ref, lambda value: value)
             write(1 - half, send_ref, rounded)
@@ -408,21 +373,23 @@
     send_ref[keep_ref.shape[0] :] = rounded(rider_ref[...])
 
 
-def place_kernel(rows_per_piece, place_ref, *refs):
+def place_kernel(*refs):
     part_refs, (gq_hbm, gkv_hbm, go_hbm, all_ref, out_ref, sems) = refs[:-6], refs[-6:]
     width = gq_hbm.shape[0]
     rows = part_refs[0].shape[0]
     half = len(part_refs) // 2
-    for at, part_ref in enumerate(part_refs):
-        digit = at // half * half + -at % half
-        all_ref[digit * rows : (digit + 1) * rows] = part_ref[...]
+    for at, digit in enumerate([0] + farthest_first(half)[::-1]):
+        for core in range(2):
+            place = (core * half + digit) * rows
+            all_ref[place : place + rows] = part_refs[core * half + at][...]
+    held = own_digit(exchange_plan()[0]) + (lax.axis_index("rows") % 2) * half
     copies = []
-    for at in range(all_ref.shape[0] // rows_per_piece):
-        offset = pl.multiple_of((place_ref[1] ^ at) * rows_per_piece, ROW_PACK)
-        start = at * rows_per_piece
-        piece = slice(start, start + rows_per_piece)
-        out_ref[piece] = all_ref[pl.ds(offset, rows_per_piece), :].astype(jnp.float32)
-        rows_out = pl.ds(start % width, rows_per_piece)
+    for at in range(2 * half):
+        start = at * rows
+        piece = slice(start, start + rows)
+        offset = pl.multiple_of((held ^ at) * rows, ROW_PACK)
+        out_ref[piece] = all_ref[pl.ds(offset, rows), :].astype(jnp.float32)
+        rows_out = pl.ds(start % width, rows)
         which = start // width
         if which == 0:
             target = gq_hbm.at[rows_out]
@@ -436,24 +403,18 @@
         copy.wait()
 
 
-def return_kernel(place_ref, send_hbm, gf_ref, halo_ref, *refs):
-    piece_refs, (out_ref, send_ref, sems) = refs[:-3], refs[-3:]
-    fetch([(send_hbm, send_ref)], sems)[0].wait()
+def return_kernel(gf_ref, chosen_ref, halo_ref, *refs):
+    piece_refs, out_ref = refs[:-1], refs[-1]
     row_count = gf_ref.shape[0]
     tile = halo_ref.shape[0]
-    per_peer = send_ref.shape[1]
-    chosen = listed_rows(place_ref[0], send_ref, row_count)
-    returned = jnp.concatenate(
-        [piece_refs[0][...], piece_refs[1][:per_peer]] + [ref[...] for ref in piece_refs[:1:-1]],
-        axis=0,
-    )
-    total = gf_ref[...] + rows_contracted(chosen, returned)
+    returned = jnp.concatenate([ref[...] for ref in piece_refs], axis=0)
+    total = gf_ref[...] + rows_contracted(chosen_ref[...], returned)
     out_ref[: row_count - tile] = total[: row_count - tile]
     out_ref[row_count - tile :] = total[row_count - tile :] + halo_ref[...].astype(jnp.float32)
 
 
 def call(kernel, name, outs, args, scratch=(), fetched=0, flops=0, stored=False):
-    spaces = [pltpu.SMEM] + [pltpu.HBM] * fetched
+    spaces = [pltpu.HBM] * fetched
     spaces += [pltpu.VMEM] * (len(args) - len(spaces))
     moved = sum(x.size * x.dtype.itemsize for x in list(args) + list(outs))
     scratch = list(scratch)
@@ -483,23 +444,24 @@
     padded = ROW_PACK * -(-virt_rows // ROW_PACK)
     ext_rows = TILE + row_count + slots + padded
     nodes = row_count * lax.axis_size("dom") * lax.axis_size("rows")
-    stages = exchange_stages(lax.axis_size("dom"), lax.axis_size("rows"))
-    scattered = stages[:3]
-    rows_per_piece = 4 * width >> sum(len(stage) for stage in scattered)
-    place = jnp.stack([lax.axis_index("dom").astype(jnp.int32), own_piece(scattered)])
+    block, rest = exchange_plan()
+    masks = partner_masks(block)
+    order = farthest_first(len(masks))
+    rows_per_piece = 2 * width // len(masks)
     bf16, f32 = jnp.bfloat16, jnp.float32
     shape = jax.ShapeDtypeStruct
 
-    halo, through, *direct = call(
+    halo, chosen, *sent = call(
         pick_kernel,
         "pick_rows",
-        [shape((TILE, width), bf16), shape((slots // 2, width), bf16)]
-        + [shape((per_peer, width), bf16)] * (dom_size // 2),
-        [place, features, send_rows],
+        [shape((TILE, width), bf16), shape((slots, row_count), bf16)]
+        + [shape((per_peer, width), bf16)] * dom_size,
+        [features, send_rows],
         [pltpu.VMEM(features.shape, bf16), pltpu.VMEM(send_rows.shape, jnp.int32)],
         fetched=2,
     )
-    arrived = routed(direct, through)
+    arrived = [sent[0]] + [swapped(sent[at], at, 0) for at in farthest_first(dom_size)]
+    halo, _ = lax.optimization_barrier((halo, arrived[1]))
     halo = shifted(halo, "rows", 1)
     prepared = call(
         functools.partial(prepare_kernel, per_peer),
@@ -516,7 +478,7 @@
             shape((2 * TILE, row_count), f32),
             shape((slots + padded, row_count), f32),
         ],
-        [place, features, out_grad, w_query, w_keyval, w_out, virtual, local_nbr.T, expander.T],
+        [features, out_grad, w_query, w_keyval, w_out, virtual, local_nbr.T, expander.T],
         [
             pltpu.VMEM(features.shape, bf16),
             pltpu.VMEM(w_out.shape, bf16),
@@ -533,13 +495,12 @@
         [
             shape((row_count, width), f32),
             shape((TILE, width), bf16),
-            *[shape((per_peer, width), bf16)] * (dom_size // 2),
-            shape((slots // 2, width), bf16),
+            *[shape((per_peer, width), bf16)] * dom_size,
             shape((2 * width, width), f32),
             shape((2 * width + padded, width), bf16),
             shape((padded, width), f32),
         ],
-        [place, halo, *arrived, *prepared],
+        [*arrived, halo, *prepared],
         [
             pltpu.VMEM((slots, width), bf16),
             pltpu.VMEM((ext_rows, 2 * width), bf16),
@@ -551,44 +512,51 @@
         ],
         flops=32 * ext_rows * width * width,
     )
-    *direct, through, keep, message, rider = results
+    *slot_feat, keep, message, rider = results
 
     rider = rounded(rider).astype(f32)
-    keep, rider = added(keep, rider, exchange([message], stages[0]))
-    through = swapped(through, 1, 0)
-    for at, stage in enumerate(stages[1:], 1):
-        keep, rider, messages = scatter_stage(keep, rider, stage, stage in scattered)
-        if at == 1:
-            through, _ = lax.optimization_barrier((through, messages))
-            returned = handed_on(direct, through)
-        if at == 2:
-            messages, returned, halo_feat = lax.optimization_barrier(
-                (messages, returned, halo_feat)
+    keep, rider = added(keep, rider, {1: swapped(message, *CORES)})
+    rider = rider[: -(-virt_rows // 8) * 8]
+    dom_bits = bits_of(dom_size)
+    slot_feat = [hop(slot_feat, dom_bits[0]).get(at, own) for at, own in enumerate(slot_feat)]
+
+    parts = [keep[at * rows_per_piece : (at + 1) * rows_per_piece] for at in range(len(masks))]
+    messages = {at: swapped(with_rider(parts[at], rider), *masks[at]) for at in order}
+    rider = rounded(rider).astype(f32)
+    keep, rider = added(parts[0], rider, messages)
+
+    for at, mask in enumerate(rest):
+        message = with_rider(keep, rider)
+        if at == 0:
+            (slot_feat, halo_feat), _ = lax.optimization_barrier(
+                ((slot_feat, halo_feat), message)
             )
+            for bit in dom_bits[1:-1]:
+                slot_feat = [hop(slot_feat, bit).get(i, own) for i, own in enumerate(slot_feat)]
             halo_back = shifted(halo_feat, "rows", -1)
-        keep, rider = added(keep, rider, exchange(messages, stage))
+        keep, rider = rounded(keep).astype(f32), rounded(rider).astype(f32)
+        keep, rider = added(keep, rider, {1: swapped(message, *mask)})
+
+    held = rounded(keep)
+    held, slot_feat, halo_back = lax.optimization_barrier((held, slot_feat, halo_back))
+    slot_feat = [hop(slot_feat, dom_bits[-1]).get(at, own) for at, own in enumerate(slot_feat)]
+    near = [held] + [swapped(held, *masks[at]) for at in order[::-1]]
+    far = [swapped(part, *CORES) for part in near]
     (grad_features,) = call(
         return_kernel,
         "return_rows",
         [shape((row_count, width), f32)],
-        [place, send_rows, own_feat, halo_back, *returned],
-        [pltpu.VMEM(send_rows.shape, jnp.int32)],
-        fetched=1,
-    )
-    held, grad_features = lax.optimization_barrier((rounded(keep), grad_features))
-    held = gathered(held, scattered[2])
-    square = partner_masks(scattered[1])
-    near = [held] + [swapped(held, *masks) for masks in square[::-1]]
-    far = [swapped(block, *partner_masks(scattered[0])[0]) for block in near]
+        [own_feat, chosen, halo_back, *slot_feat],
+    )
     grad_wq, grad_wkv, grad_wo = call(
-        functools.partial(place_kernel, rows_per_piece),
+        place_kernel,
         "place_sums",
         [shape((width, width), f32), shape((width, 2 * width), f32), shape((width, width), f32)],
-        [place, *near, *far],
+        [*near, *far],
         [
             pltpu.VMEM((4 * width, width), bf16),
             pltpu.VMEM((4 * width, width), f32),
-            pltpu.SemaphoreType.DMA((4 * width // rows_per_piece,)),
+            pltpu.SemaphoreType.DMA((2 * len(masks),)),
         ],
         stored=True,
     )

time: 67.4 us -> 73.5 us (1.091)
  starting transfers between devices: 22.7 us -> 41.7 us
  waiting for transfers between devices: 24.4 us -> 15.2 us
  Pallas kernels: 18 us -> 14.4 us
    ppermute x22 -> x34, starting transfers between devices: 22.7 us -> 41.7 us  [swapped(): return lax.ppermute(block, ('dom', 'rows'), route)]
    ppermute x22 -> x34, waiting for transfers between devices: 24.4 us -> 15.2 us  [swapped(): return lax.ppermute(block, ('dom', 'rows'), route)]
    pallas_call x5, Pallas kernels: 18 us -> 14.4 us  [call(): pl.pallas_call(kernel, out_shape=outs, in_specs=[pl.BlockSpec(memory_spac...]
  transfers between devices with their start and end apart: 24 -> 36, of which waited for: 16 -> 12; matrix products, arithmetic and copies ran while one was open for 2% -> 1% of each run, Pallas kernels for 9% -> 5%
where the time goes in v9:
time: 73.5 us; the launch traced here: 73.2 us
  starting transfers between devices  41.7 us (57%)
  waiting for transfers between devices  15.2 us (21%)
  Pallas kernels  14.4 us (20%)
  other arithmetic  1 us (1%)
  between operations  0.86 us (1%)
    ppermute x34, starting transfers between devices, swapped(): return lax.ppermute(block, ('dom', 'rows'), route)  41.7 us
    ppermute x34, waiting for transfers between devices, swapped(): return lax.ppermute(block, ('dom', 'rows'), route)  15.2 us
    pallas_call x5, Pallas kernels, call(): pl.pallas_call(kernel, out_shape=outs, in_specs=[pl.BlockSpec(memory_spac...  14.4 us
  transfers between devices with their start and end apart: 36, of which 12 were waited for; matrix products, arithmetic and copies ran while one was open for 1% of the time, Pallas kernels for 5%

profile of v9, /device:TPU:0, one launch (start us, length us, event | category | flops | bytes accessed | tf_op | source)
XLA Modules:
  0.0 73.2 jit_solution(7065235033760544264)
XLA Ops:
  0.6 1.2 %pick_rows.1 = (bf16[128,384]{1,0:T(8,128)(2,1)S(1)}, bf16[256,256]{1,0:T(8,128)(2,1)S(1)}, bf16[32,384]{1,0:T(8,128)(2,1)S(1)}, bf16[32,384]{1,0:T(8,128)(2,1)S...) custom-call(bf16[256,384]{1,0:T(8,128)(2,1)} %feat_hbm.3, ...), custom_call_target="tpu_custom_call" | custom-call | bytes 623616 | tf_op jit(solution)/shard_map/pick_rows/pallas_call | solution.py:427
  1.9 6.0 %collective-permute-start = (bf16[32,384]{1,0:T(8,128)(2,1)S(1)}, bf16[32,384]{1,0:T(8,128)(2,1)S(1)}, u32[]{:S(2)}, u32[]{:S(2)}) collective-permute-start(bf16[32,384]{1,0:T(8,128)(2,1)S(1)} %get-tuple-element.62), channel_id=1, source_target_pairs={{0,28},{1,29},{2,30},{3,31},{4,24},{5,25},{6,26},{7,27},{8,20},{9,... | collective-permute-start | bytes 73736 | tf_op jit(solution)/shard_map/ppermute | solution.py:80
  7.9 1.8 %collective-permute-done.refs_1_ = bf16[32,384]{1,0:T(8,128)(2,1)S(1)} collective-permute-done((bf16[32,384]{1,0:T(8,128)(2,1)S(1)}, bf16[32,384]{1,0:T(8,128)(2,1)S(1)}, u32[]{:S(2)}, u32[]{:S(2)}) %collective-permute-start) | collective-permute-done | bytes 24608 | tf_op jit(solution)/shard_map/ppermute | solution.py:80
  9.7 3.8 %collective-permute-start.1 = (bf16[32,384]{1,0:T(8,128)(2,1)S(1)}, bf16[32,384]{1,0:T(8,128)(2,1)S(1)}, u32[]{:S(2)}, u32[]{:S(2)}) collective-permute-start(bf16[32,384]{1,0:T(8,128)(2,1)S(1)} %get-tuple-element.63), channel_id=1, source_target_pairs={{0,24},{1,25},{2,26},{3,27},{4,28},{5,29},{6,30},{7,31},{8,16},{9,... | collective-permute-start | bytes 73736 | tf_op jit(solution)/shard_map/ppermute | solution.py:80
  13.5 1.5 %collective-permute-start.3 = (bf16[32,384]{1,0:T(8,128)(2,1)S(1)}, bf16[32,384]{1,0:T(8,128)(2,1)S(1)}, u32[]{:S(2)}, u32[]{:S(2)}) collective-permute-start(bf16[32,384]{1,0:T(8,128)(2,1)S(1)} %get-tuple-element.65), channel_id=1, source_target_pairs={{0,12},{1,13},{2,14},{3,15},{4,8},{5,9},{6,10},{7,11},{8,4},{9,5},... | collective-permute-start | bytes 73736 | tf_op jit(solution)/shard_map/ppermute | solution.py:80
  15.0 2.4 %collective-permute-start.4 = (bf16[32,384]{1,0:T(8,128)(2,1)S(1)}, bf16[32,384]{1,0:T(8,128)(2,1)S(1)}, u32[]{:S(2)}, u32[]{:S(2)}) collective-permute-start(bf16[32,384]{1,0:T(8,128)(2,1)S(1)} %get-tuple-element.66), channel_id=1, source_target_pairs={{0,16},{1,17},{2,18},{3,19},{4,20},{5,21},{6,22},{7,23},{8,24},{9,... | collective-permute-start | bytes 73736 | tf_op jit(solution)/shard_map/ppermute | solution.py:80
  17.4 2.0 %collective-permute-start.5 = (bf16[32,384]{1,0:T(8,128)(2,1)S(1)}, bf16[32,384]{1,0:T(8,128)(2,1)S(1)}, u32[]{:S(2)}, u32[]{:S(2)}) collective-permute-start(bf16[32,384]{1,0:T(8,128)(2,1)S(1)} %get-tuple-element.67), channel_id=1, source_target_pairs={{0,8},{1,9},{2,10},{3,11},{4,12},{5,13},{6,14},{7,15},{8,0},{9,1},... | collective-permute-start | bytes 73736 | tf_op jit(solution)/shard_map/ppermute | solution.py:80
  19.4 1.5 %collective-permute-start.6 = (bf16[32,384]{1,0:T(8,128)(2,1)S(1)}, bf16[32,384]{1,0:T(8,128)(2,1)S(1)}, u32[]{:S(2)}, u32[]{:S(2)}) collective-permute-start(bf16[32,384]{1,0:T(8,128)(2,1)S(1)} %get-tuple-element.68), channel_id=1, source_target_pairs={{0,4},{1,5},{2,6},{3,7},{4,0},{5,1},{6,2},{7,3},{8,12},{9,13},{10,... | collective-permute-start | bytes 73736 | tf_op jit(solution)/shard_map/ppermute | solution.py:80
  20.9 2.9 %prepare.1 = (bf16[256,384]{1,0:T(8,128)(2,1)S(1)}, bf16[384,384]{1,0:T(8,128)(2,1)S(1)}, bf16[384,768]{1,0:T(8,128)(2,1)S(1)}, bf16[384,272]{1,0:T(8,128)(2,1)S...) custom-call(bf16[256,384]{1,0:T(8,128)(2,1)} %feat_hbm.3, ...), custom_call_target="tpu_custom_call" | custom-call | flops 377487360 | bytes 4656128 | tf_op jit(solution)/shard_map/prepare/pallas_call | solution.py:427
  23.8 7.6 %attend.1 = (f32[256,384]{1,0:T(8,128)S(1)}, bf16[128,384]{1,0:T(8,128)(2,1)S(1)}, bf16[32,384]{1,0:T(8,128)(2,1)S(1)}, bf16[32,384]{1,0:T(8,128)(2,1)S(1)}, bf1...) custom-call(bf16[32,384]{1,0:T(8,128)(2,1)S(1)} %get-tuple-element.6, ...), custom_call_target="tpu_custom_call" | custom-call | flops 3095396352 | bytes 5849088 | tf_op jit(solution)/shard_map/attend/pallas_call | solution.py:427
  31.4 0.1 collective-permute-start.8
  31.5 0.9 %collective-permute-start.17 = (bf16[128,384]{1,0:T(8,128)(2,1)S(1)}, bf16[128,384]{1,0:T(8,128)(2,1)S(1)}, u32[]{:S(2)}, u32[]{:S(2)}) collective-permute-start(bf16[128,384]{1,0:T(8,128)(2,1)S(1)} %pad_maximum_fusion.7), channel_id=1, source_target_pairs={{0,4},{1,5},{2,6},{3,7},{4,0},{5,1},{6,2},{7,3},{8,12},{9,13},{10,... | collective-permute-start | bytes 294920 | tf_op jit(solution)/shard_map/ppermute | solution.py:80
  32.4 1.1 %collective-permute-done.8 = bf16[784,384]{1,0:T(8,128)(2,1)S(1)} collective-permute-done((bf16[784,384]{1,0:T(8,128)(2,1)S(1)}, bf16[784,384]{1,0:T(8,128)(2,1)S(1)}, u32[]{:S(2)}, u32[]{:S(2)}) %collective-permute-start.8) | collective-permute-done | bytes 602144 | tf_op jit(solution)/shard_map/ppermute | solution.py:80
  33.5 0.2 fusion.7
  33.7 0.1 pad_maximum_fusion.6
  33.8 1.4 %collective-permute-start.9 = (bf16[104,384]{1,0:T(8,128)(2,1)S(1)}, bf16[104,384]{1,0:T(8,128)(2,1)S(1)}, u32[]{:S(2)}, u32[]{:S(2)}) collective-permute-start(bf16[104,384]{1,0:T(8,128)(2,1)S(1)} %get-tuple-element.138), channel_id=1, source_target_pairs={{0,14},{1,15},{2,12},{3,13},{4,10},{5,11},{6,8},{7,9},{8,6},{9,7},... | collective-permute-start | bytes 239624 | tf_op jit(solution)/shard_map/ppermute | solution.py:80
  35.2 1.9 %collective-permute-start.10 = (bf16[104,384]{1,0:T(8,128)(2,1)S(1)}, bf16[104,384]{1,0:T(8,128)(2,1)S(1)}, u32[]{:S(2)}, u32[]{:S(2)}) collective-permute-start(bf16[104,384]{1,0:T(8,128)(2,1)S(1)} %get-tuple-element.139), channel_id=1, source_target_pairs={{0,10},{1,11},{2,8},{3,9},{4,14},{5,15},{6,12},{7,13},{8,2},{9,3},... | collective-permute-start | bytes 239624 | tf_op jit(solution)/shard_map/ppermute | solution.py:80
  37.1 0.7 collective-permute-start.11
  37.8 1.8 %collective-permute-start.12 = (bf16[104,384]{1,0:T(8,128)(2,1)S(1)}, bf16[104,384]{1,0:T(8,128)(2,1)S(1)}, u32[]{:S(2)}, u32[]{:S(2)}) collective-permute-start(bf16[104,384]{1,0:T(8,128)(2,1)S(1)} %get-tuple-element.141), channel_id=1, source_target_pairs={{0,6},{1,7},{2,4},{3,5},{4,2},{5,3},{6,0},{7,1},{8,14},{9,15},{10,... | collective-permute-start | bytes 239624 | tf_op jit(solution)/shard_map/ppermute | solution.py:80
  39.6 2.0 %collective-permute-start.13 = (bf16[104,384]{1,0:T(8,128)(2,1)S(1)}, bf16[104,384]{1,0:T(8,128)(2,1)S(1)}, u32[]{:S(2)}, u32[]{:S(2)}) collective-permute-start(bf16[104,384]{1,0:T(8,128)(2,1)S(1)} %get-tuple-element.142), channel_id=1, source_target_pairs={{0,8},{1,9},{2,10},{3,11},{4,12},{5,13},{6,14},{7,15},{8,0},{9,1},... | collective-permute-start | bytes 239624 | tf_op jit(solution)/shard_map/ppermute | solution.py:80
  41.6 1.4 %collective-permute-start.14 = (bf16[104,384]{1,0:T(8,128)(2,1)S(1)}, bf16[104,384]{1,0:T(8,128)(2,1)S(1)}, u32[]{:S(2)}, u32[]{:S(2)}) collective-permute-start(bf16[104,384]{1,0:T(8,128)(2,1)S(1)} %get-tuple-element.143), channel_id=1, source_target_pairs={{0,2},{1,3},{2,0},{3,1},{4,6},{5,7},{6,4},{7,5},{8,10},{9,11},{10,... | collective-permute-start | bytes 239624 | tf_op jit(solution)/shard_map/ppermute | solution.py:80
  43.0 0.7 collective-permute-start.15
  43.7 0.7 collective-permute-done.11
  44.4 0.3 collective-permute-done.13
  44.7 1.3 %collective-permute-done.14 = bf16[104,384]{1,0:T(8,128)(2,1)S(1)} collective-permute-done((bf16[104,384]{1,0:T(8,128)(2,1)S(1)}, bf16[104,384]{1,0:T(8,128)(2,1)S(1)}, u32[]{:S(2)}, u32[]{:S(2)}) %collective-permute-start.14) | collective-permute-done | bytes 79904 | tf_op jit(solution)/shard_map/ppermute | solution.py:80
  46.0 1.4 %collective-permute-done.15 = bf16[104,384]{1,0:T(8,128)(2,1)S(1)} collective-permute-done((bf16[104,384]{1,0:T(8,128)(2,1)S(1)}, bf16[104,384]{1,0:T(8,128)(2,1)S(1)}, u32[]{:S(2)}, u32[]{:S(2)}) %collective-permute-start.15) | collective-permute-done | bytes 79904 | tf_op jit(solution)/shard_map/ppermute | solution.py:80
  47.4 0.1 fusion.6
  47.5 0.4 collective-permute-start.16
  47.9 0.9 %collective-permute-start.18 = (bf16[128,384]{1,0:T(8,128)(2,1)S(1)}, bf16[128,384]{1,0:T(8,128)(2,1)S(1)}, u32[]{:S(2)}, u32[]{:S(2)}) collective-permute-start(bf16[128,384]{1,0:T(8,128)(2,1)S(1)} %pad_maximum_fusion.8), channel_id=1, source_target_pairs={{0,8},{1,9},{2,10},{3,11},{4,12},{5,13},{6,14},{7,15},{8,0},{9,1},... | collective-permute-start | bytes 294920 | tf_op jit(solution)/shard_map/ppermute | solution.py:80
  48.8 4.7 %collective-permute-done.16 = bf16[104,384]{1,0:T(8,128)(2,1)S(1)} collective-permute-done((bf16[104,384]{1,0:T(8,128)(2,1)S(1)}, bf16[104,384]{1,0:T(8,128)(2,1)S(1)}, u32[]{:S(2)}, u32[]{:S(2)}) %collective-permute-start.16) | collective-permute-done | bytes 79904 | tf_op jit(solution)/shard_map/ppermute | solution.py:80
  53.6 0.8 %collective-permute-start.27 = (bf16[96,384]{1,0:T(8,128)(2,1)S(1)}, bf16[96,384]{1,0:T(8,128)(2,1)S(1)}, u32[]{:S(2)}, u32[]{:S(2)}) collective-permute-start(bf16[96,384]{1,0:T(8,128)(2,1)S(1)} %add_convert_fusion.refs_0_), channel_id=1, source_target_pairs={{0,14},{1,15},{2,12},{3,13},{4,10},{5,11},{6,8},{7,9},{8,6},{9,7},... | collective-permute-start | bytes 221192 | tf_op jit(solution)/shard_map/ppermute | solution.py:80
  54.4 2.7 %collective-permute-start.26 = (bf16[96,384]{1,0:T(8,128)(2,1)S(1)}, bf16[96,384]{1,0:T(8,128)(2,1)S(1)}, u32[]{:S(2)}, u32[]{:S(2)}) collective-permute-start(bf16[96,384]{1,0:T(8,128)(2,1)S(1)} %add_convert_fusion.refs_0_), channel_id=1, source_target_pairs={{0,10},{1,11},{2,8},{3,9},{4,14},{5,15},{6,12},{7,13},{8,2},{9,3},... | collective-permute-start | bytes 221192 | tf_op jit(solution)/shard_map/ppermute | solution.py:80
  57.1 0.3 collective-permute-start.25
  57.4 1.4 %collective-permute-start.24 = (bf16[96,384]{1,0:T(8,128)(2,1)S(1)}, bf16[96,384]{1,0:T(8,128)(2,1)S(1)}, u32[]{:S(2)}, u32[]{:S(2)}) collective-permute-start(bf16[96,384]{1,0:T(8,128)(2,1)S(1)} %add_convert_fusion.refs_0_), channel_id=1, source_target_pairs={{0,6},{1,7},{2,4},{3,5},{4,2},{5,3},{6,0},{7,1},{8,14},{9,15},{10,... | collective-permute-start | bytes 221192 | tf_op jit(solution)/shard_map/ppermute | solution.py:80
  58.8 2.1 %collective-permute-start.23 = (bf16[96,384]{1,0:T(8,128)(2,1)S(1)}, bf16[96,384]{1,0:T(8,128)(2,1)S(1)}, u32[]{:S(2)}, u32[]{:S(2)}) collective-permute-start(bf16[96,384]{1,0:T(8,128)(2,1)S(1)} %add_convert_fusion.refs_0_), channel_id=1, source_target_pairs={{0,8},{1,9},{2,10},{3,11},{4,12},{5,13},{6,14},{7,15},{8,0},{9,1},... | collective-permute-start | bytes 221192 | tf_op jit(solution)/shard_map/ppermute | solution.py:80
  60.9 0.1 collective-permute-done.27.refs_7_
  61.0 1.1 %collective-permute-start.22 = (bf16[96,384]{1,0:T(8,128)(2,1)S(1)}, bf16[96,384]{1,0:T(8,128)(2,1)S(1)}, u32[]{:S(2)}, u32[]{:S(2)}) collective-permute-start(bf16[96,384]{1,0:T(8,128)(2,1)S(1)} %add_convert_fusion.refs_0_), channel_id=1, source_target_pairs={{0,2},{1,3},{2,0},{3,1},{4,6},{5,7},{6,4},{7,5},{8,10},{9,11},{10,... | collective-permute-start | bytes 221192 | tf_op jit(solution)/shard_map/ppermute | solution.py:80
  62.1 0.3 collective-permute-done.26.refs_6_
  62.5 1.0 %collective-permute-start.21 = (bf16[96,384]{1,0:T(8,128)(2,1)S(1)}, bf16[96,384]{1,0:T(8,128)(2,1)S(1)}, u32[]{:S(2)}, u32[]{:S(2)}) collective-permute-start(bf16[96,384]{1,0:T(8,128)(2,1)S(1)} %add_convert_fusion.refs_0_), channel_id=1, source_target_pairs={{0,4},{1,5},{2,6},{3,7},{4,0},{5,1},{6,2},{7,3},{8,12},{9,13},{10,... | collective-permute-start | bytes 221192 | tf_op jit(solution)/shard_map/ppermute | solution.py:80
  63.5 1.7 %collective-permute-start.20 = (bf16[128,384]{1,0:T(8,128)(2,1)S(1)}, bf16[128,384]{1,0:T(8,128)(2,1)S(1)}, u32[]{:S(2)}, u32[]{:S(2)}) collective-permute-start(bf16[128,384]{1,0:T(8,128)(2,1)S(1)} %pad_maximum_fusion.9), channel_id=1, source_target_pairs={{0,16},{1,17},{2,18},{3,19},{4,20},{5,21},{6,22},{7,23},{8,24},{9,... | collective-permute-start | bytes 294920 | tf_op jit(solution)/shard_map/ppermute | solution.py:80
  65.2 0.5 collective-permute-start.34
  65.7 0.6 convert_add_fusion.1
  66.4 0.4 collective-permute-done.21.refs_1_
  66.8 3.0 %collective-permute-done.20 = bf16[128,384]{1,0:T(8,128)(2,1)S(1)} collective-permute-done((bf16[128,384]{1,0:T(8,128)(2,1)S(1)}, bf16[128,384]{1,0:T(8,128)(2,1)S(1)}, u32[]{:S(2)}, u32[]{:S(2)}) %collective-permute-start.20) | collective-permute-done | bytes 98336 | tf_op jit(solution)/shard_map/ppermute | solution.py:80
  69.8 0.5 collective-permute-start.30
  70.4 1.0 %return_rows.1 = f32[256,384]{1,0:T(8,128)} custom-call(f32[256,384]{1,0:T(8,128)S(1)} %get-tuple-element.81.gf_ref, bf16[256,256]{1,0:T(8,128)(2,1)S(1)} %get-tuple-element.82.chosen_ref, bf16[128,384]{1,0:T(8,128)(2,1)S(1)} %collective-permute-done.19.halo_ref, bf16[32,384]{1,0:T(8,128)(2,1)S(1)} %get-tuple-element.105.refs_0_, ...), custom_call_target="tpu_custom_call" | custom-call | bytes 1212416 | tf_op jit(solution)/shard_map/return_rows/pallas_call | solution.py:427
  71.4 0.2 collective-permute-done.29.refs_9_
  71.6 1.6 %place_sums.1 = (f32[384,384]{1,0:T(8,128)}, f32[384,768]{1,0:T(8,128)}, f32[384,384]{1,0:T(8,128)}) custom-call(bf16[96,384]{1,0:T(8,128)(2,1)S(1)} %add_convert_fusion.refs_0_, bf16[96,384]{1,0:T(8,128)(2,1)S(1)} %collective-permute-done.21.refs_1_, bf16[96,384]{1,0:T(8,128)(2,1)S(1)} %collective-permute-done.22.refs_2_, ...), custom_call_target="tpu_custom_call" | custom-call | bytes 3538944 | tf_op jit(solution)/shard_map/place_sums/pallas_call | solution.py:427
  (46 shorter events, 0.5 us)
Async XLA Ops:
  1.9 7.8 %collective-permute-start = (bf16[32,384]{1,0:T(8,128)(2,1)S(1)}, bf16[32,384]{1,0:T(8,128)(2,1)S(1)}, u32[]{:S(2)}, u32[]{:S(2)}) collective-permute-start(bf16[32,384]{1,0:T(8,128)(2,1)S(1)} %get-tuple-element.62), channel_id=1, source_target_pairs={{0,28},{1,29},{2,30},{3,31},{4,24},{5,25},{6,26},{7,27},{8,20},{9,... | collective-permute-start | bytes 73736 | tf_op jit(solution)/shard_map/ppermute | solution.py:80
  9.7 14.1 %collective-permute-start.7 = (bf16[128,384]{1,0:T(8,128)(2,1)S(1)}, bf16[128,384]{1,0:T(8,128)(2,1)S(1)}, u32[]{:S(2)}, u32[]{:S(2)}) collective-permute-start(bf16[128,384]{1,0:T(8,128)(2,1)S(1)} %get-tuple-element.70), channel_id=1, source_target_pairs={{3,0},{0,1},{1,2},{2,3},{7,4},{4,5},{5,6},{6,7},{11,8},{8,9},{9,10... | collective-permute-start | bytes 294920 | tf_op jit(solution)/shard_map/ppermute | solution.py:86
  9.7 7.6 %collective-permute-start.1 = (bf16[32,384]{1,0:T(8,128)(2,1)S(1)}, bf16[32,384]{1,0:T(8,128)(2,1)S(1)}, u32[]{:S(2)}, u32[]{:S(2)}) collective-permute-start(bf16[32,384]{1,0:T(8,128)(2,1)S(1)} %get-tuple-element.63), channel_id=1, source_target_pairs={{0,24},{1,25},{2,26},{3,27},{4,28},{5,29},{6,30},{7,31},{8,16},{9,... | collective-permute-start | bytes 73736 | tf_op jit(solution)/shard_map/ppermute | solution.py:80
  13.5 5.9 %collective-permute-start.2 = (bf16[32,384]{1,0:T(8,128)(2,1)S(1)}, bf16[32,384]{1,0:T(8,128)(2,1)S(1)}, u32[]{:S(2)}, u32[]{:S(2)}) collective-permute-start(bf16[32,384]{1,0:T(8,128)(2,1)S(1)} %get-tuple-element.64), channel_id=1, source_target_pairs={{0,20},{1,21},{2,22},{3,23},{4,16},{5,17},{6,18},{7,19},{8,28},{9,... | collective-permute-start | bytes 73736 | tf_op jit(solution)/shard_map/ppermute | solution.py:80
  13.5 10.3 %collective-permute-start.3 = (bf16[32,384]{1,0:T(8,128)(2,1)S(1)}, bf16[32,384]{1,0:T(8,128)(2,1)S(1)}, u32[]{:S(2)}, u32[]{:S(2)}) collective-permute-start(bf16[32,384]{1,0:T(8,128)(2,1)S(1)} %get-tuple-element.65), channel_id=1, source_target_pairs={{0,12},{1,13},{2,14},{3,15},{4,8},{5,9},{6,10},{7,11},{8,4},{9,5},... | collective-permute-start | bytes 73736 | tf_op jit(solution)/shard_map/ppermute | solution.py:80
  15.0 8.8 %collective-permute-start.4 = (bf16[32,384]{1,0:T(8,128)(2,1)S(1)}, bf16[32,384]{1,0:T(8,128)(2,1)S(1)}, u32[]{:S(2)}, u32[]{:S(2)}) collective-permute-start(bf16[32,384]{1,0:T(8,128)(2,1)S(1)} %get-tuple-element.66), channel_id=1, source_target_pairs={{0,16},{1,17},{2,18},{3,19},{4,20},{5,21},{6,22},{7,23},{8,24},{9,... | collective-permute-start | bytes 73736 | tf_op jit(solution)/shard_map/ppermute | solution.py:80
  17.4 6.4 %collective-permute-start.5 = (bf16[32,384]{1,0:T(8,128)(2,1)S(1)}, bf16[32,384]{1,0:T(8,128)(2,1)S(1)}, u32[]{:S(2)}, u32[]{:S(2)}) collective-permute-start(bf16[32,384]{1,0:T(8,128)(2,1)S(1)} %get-tuple-element.67), channel_id=1, source_target_pairs={{0,8},{1,9},{2,10},{3,11},{4,12},{5,13},{6,14},{7,15},{8,0},{9,1},... | collective-permute-start | bytes 73736 | tf_op jit(solution)/shard_map/ppermute | solution.py:80
  19.4 4.4 %collective-permute-start.6 = (bf16[32,384]{1,0:T(8,128)(2,1)S(1)}, bf16[32,384]{1,0:T(8,128)(2,1)S(1)}, u32[]{:S(2)}, u32[]{:S(2)}) collective-permute-start(bf16[32,384]{1,0:T(8,128)(2,1)S(1)} %get-tuple-element.68), channel_id=1, source_target_pairs={{0,4},{1,5},{2,6},{3,7},{4,0},{5,1},{6,2},{7,3},{8,12},{9,13},{10,... | collective-permute-start | bytes 73736 | tf_op jit(solution)/shard_map/ppermute | solution.py:80
  31.4 2.1 %collective-permute-start.8 = (bf16[784,384]{1,0:T(8,128)(2,1)S(1)}, bf16[784,384]{1,0:T(8,128)(2,1)S(1)}, u32[]{:S(2)}, u32[]{:S(2)}) collective-permute-start(bf16[784,384]{1,0:T(8,128)(2,1)S(1)} %get-tuple-element.84), channel_id=1, source_target_pairs={{0,1},{1,0},{2,3},{3,2},{4,5},{5,4},{6,7},{7,6},{8,9},{9,8},{10,11... | collective-permute-start | bytes 1806344 | tf_op jit(solution)/shard_map/ppermute | solution.py:80
  31.5 8.1 %collective-permute-start.17 = (bf16[128,384]{1,0:T(8,128)(2,1)S(1)}, bf16[128,384]{1,0:T(8,128)(2,1)S(1)}, u32[]{:S(2)}, u32[]{:S(2)}) collective-permute-start(bf16[128,384]{1,0:T(8,128)(2,1)S(1)} %pad_maximum_fusion.7), channel_id=1, source_target_pairs={{0,4},{1,5},{2,6},{3,7},{4,0},{5,1},{6,2},{7,3},{8,12},{9,13},{10,... | collective-permute-start | bytes 294920 | tf_op jit(solution)/shard_map/ppermute | solution.py:80
  33.8 7.7 %collective-permute-start.9 = (bf16[104,384]{1,0:T(8,128)(2,1)S(1)}, bf16[104,384]{1,0:T(8,128)(2,1)S(1)}, u32[]{:S(2)}, u32[]{:S(2)}) collective-permute-start(bf16[104,384]{1,0:T(8,128)(2,1)S(1)} %get-tuple-element.138), channel_id=1, source_target_pairs={{0,14},{1,15},{2,12},{3,13},{4,10},{5,11},{6,8},{7,9},{8,6},{9,7},... | collective-permute-start | bytes 239624 | tf_op jit(solution)/shard_map/ppermute | solution.py:80
  35.2 7.8 %collective-permute-start.10 = (bf16[104,384]{1,0:T(8,128)(2,1)S(1)}, bf16[104,384]{1,0:T(8,128)(2,1)S(1)}, u32[]{:S(2)}, u32[]{:S(2)}) collective-permute-start(bf16[104,384]{1,0:T(8,128)(2,1)S(1)} %get-tuple-element.139), channel_id=1, source_target_pairs={{0,10},{1,11},{2,8},{3,9},{4,14},{5,15},{6,12},{7,13},{8,2},{9,3},... | collective-permute-start | bytes 239624 | tf_op jit(solution)/shard_map/ppermute | solution.py:80
  37.1 7.3 %collective-permute-start.11 = (bf16[104,384]{1,0:T(8,128)(2,1)S(1)}, bf16[104,384]{1,0:T(8,128)(2,1)S(1)}, u32[]{:S(2)}, u32[]{:S(2)}) collective-permute-start(bf16[104,384]{1,0:T(8,128)(2,1)S(1)} %get-tuple-element.140), channel_id=1, source_target_pairs={{0,12},{1,13},{2,14},{3,15},{4,8},{5,9},{6,10},{7,11},{8,4},{9,5},... | collective-permute-start | bytes 239624 | tf_op jit(solution)/shard_map/ppermute | solution.py:80
  37.8 6.6 %collective-permute-start.12 = (bf16[104,384]{1,0:T(8,128)(2,1)S(1)}, bf16[104,384]{1,0:T(8,128)(2,1)S(1)}, u32[]{:S(2)}, u32[]{:S(2)}) collective-permute-start(bf16[104,384]{1,0:T(8,128)(2,1)S(1)} %get-tuple-element.141), channel_id=1, source_target_pairs={{0,6},{1,7},{2,4},{3,5},{4,2},{5,3},{6,0},{7,1},{8,14},{9,15},{10,... | collective-permute-start | bytes 239624 | tf_op jit(solution)/shard_map/ppermute | solution.py:80
  39.6 5.1 %collective-permute-start.13 = (bf16[104,384]{1,0:T(8,128)(2,1)S(1)}, bf16[104,384]{1,0:T(8,128)(2,1)S(1)}, u32[]{:S(2)}, u32[]{:S(2)}) collective-permute-start(bf16[104,384]{1,0:T(8,128)(2,1)S(1)} %get-tuple-element.142), channel_id=1, source_target_pairs={{0,8},{1,9},{2,10},{3,11},{4,12},{5,13},{6,14},{7,15},{8,0},{9,1},... | collective-permute-start | bytes 239624 | tf_op jit(solution)/shard_map/ppermute | solution.py:80
  41.6 4.4 %collective-permute-start.14 = (bf16[104,384]{1,0:T(8,128)(2,1)S(1)}, bf16[104,384]{1,0:T(8,128)(2,1)S(1)}, u32[]{:S(2)}, u32[]{:S(2)}) collective-permute-start(bf16[104,384]{1,0:T(8,128)(2,1)S(1)} %get-tuple-element.143), channel_id=1, source_target_pairs={{0,2},{1,3},{2,0},{3,1},{4,6},{5,7},{6,4},{7,5},{8,10},{9,11},{10,... | collective-permute-start | bytes 239624 | tf_op jit(solution)/shard_map/ppermute | solution.py:80
  43.0 4.4 %collective-permute-start.15 = (bf16[104,384]{1,0:T(8,128)(2,1)S(1)}, bf16[104,384]{1,0:T(8,128)(2,1)S(1)}, u32[]{:S(2)}, u32[]{:S(2)}) collective-permute-start(bf16[104,384]{1,0:T(8,128)(2,1)S(1)} %get-tuple-element.144), channel_id=1, source_target_pairs={{0,4},{1,5},{2,6},{3,7},{4,0},{5,1},{6,2},{7,3},{8,12},{9,13},{10,... | collective-permute-start | bytes 239624 | tf_op jit(solution)/shard_map/ppermute | solution.py:80
  47.5 5.9 %collective-permute-start.16 = (bf16[104,384]{1,0:T(8,128)(2,1)S(1)}, bf16[104,384]{1,0:T(8,128)(2,1)S(1)}, u32[]{:S(2)}, u32[]{:S(2)}) collective-permute-start(bf16[104,384]{1,0:T(8,128)(2,1)S(1)} %pad_maximum_fusion.10), channel_id=1, source_target_pairs={{0,16},{1,17},{2,18},{3,19},{4,20},{5,21},{6,22},{7,23},{8,24},{9,... | collective-permute-start | bytes 239624 | tf_op jit(solution)/shard_map/ppermute | solution.py:80
  47.9 5.6 %collective-permute-start.18 = (bf16[128,384]{1,0:T(8,128)(2,1)S(1)}, bf16[128,384]{1,0:T(8,128)(2,1)S(1)}, u32[]{:S(2)}, u32[]{:S(2)}) collective-permute-start(bf16[128,384]{1,0:T(8,128)(2,1)S(1)} %pad_maximum_fusion.8), channel_id=1, source_target_pairs={{0,8},{1,9},{2,10},{3,11},{4,12},{5,13},{6,14},{7,15},{8,0},{9,1},... | collective-permute-start | bytes 294920 | tf_op jit(solution)/shard_map/ppermute | solution.py:80
  48.8 4.7 %collective-permute-start.19 = (bf16[128,384]{1,0:T(8,128)(2,1)S(1)}, bf16[128,384]{1,0:T(8,128)(2,1)S(1)}, u32[]{:S(2)}, u32[]{:S(2)}) collective-permute-start(bf16[128,384]{1,0:T(8,128)(2,1)S(1)} %get-tuple-element.103), channel_id=1, source_target_pairs={{1,0},{2,1},{3,2},{0,3},{5,4},{6,5},{7,6},{4,7},{9,8},{10,9},{11,1... | collective-permute-start | bytes 294920 | tf_op jit(solution)/shard_map/ppermute | solution.py:86
  53.5 5.3 %collective-permute-start.28 = (bf16[96,384]{1,0:T(8,128)(2,1)S(1)}, bf16[96,384]{1,0:T(8,128)(2,1)S(1)}, u32[]{:S(2)}, u32[]{:S(2)}) collective-permute-start(bf16[96,384]{1,0:T(8,128)(2,1)S(1)} %add_convert_fusion.refs_0_), channel_id=1, source_target_pairs={{0,1},{1,0},{2,3},{3,2},{4,5},{5,4},{6,7},{7,6},{8,9},{9,8},{10,11... | collective-permute-start | bytes 221192 | tf_op jit(solution)/shard_map/ppermute | solution.py:80
  53.6 7.4 %collective-permute-start.27 = (bf16[96,384]{1,0:T(8,128)(2,1)S(1)}, bf16[96,384]{1,0:T(8,128)(2,1)S(1)}, u32[]{:S(2)}, u32[]{:S(2)}) collective-permute-start(bf16[96,384]{1,0:T(8,128)(2,1)S(1)} %add_convert_fusion.refs_0_), channel_id=1, source_target_pairs={{0,14},{1,15},{2,12},{3,13},{4,10},{5,11},{6,8},{7,9},{8,6},{9,7},... | collective-permute-start | bytes 221192 | tf_op jit(solution)/shard_map/ppermute | solution.py:80
  54.4 8.0 %collective-permute-start.26 = (bf16[96,384]{1,0:T(8,128)(2,1)S(1)}, bf16[96,384]{1,0:T(8,128)(2,1)S(1)}, u32[]{:S(2)}, u32[]{:S(2)}) collective-permute-start(bf16[96,384]{1,0:T(8,128)(2,1)S(1)} %add_convert_fusion.refs_0_), channel_id=1, source_target_pairs={{0,10},{1,11},{2,8},{3,9},{4,14},{5,15},{6,12},{7,13},{8,2},{9,3},... | collective-permute-start | bytes 221192 | tf_op jit(solution)/shard_map/ppermute | solution.py:80
  57.1 6.4 %collective-permute-start.25 = (bf16[96,384]{1,0:T(8,128)(2,1)S(1)}, bf16[96,384]{1,0:T(8,128)(2,1)S(1)}, u32[]{:S(2)}, u32[]{:S(2)}) collective-permute-start(bf16[96,384]{1,0:T(8,128)(2,1)S(1)} %add_convert_fusion.refs_0_), channel_id=1, source_target_pairs={{0,12},{1,13},{2,14},{3,15},{4,8},{5,9},{6,10},{7,11},{8,4},{9,5},... | collective-permute-start | bytes 221192 | tf_op jit(solution)/shard_map/ppermute | solution.py:80
  57.4 7.8 %collective-permute-start.24 = (bf16[96,384]{1,0:T(8,128)(2,1)S(1)}, bf16[96,384]{1,0:T(8,128)(2,1)S(1)}, u32[]{:S(2)}, u32[]{:S(2)}) collective-permute-start(bf16[96,384]{1,0:T(8,128)(2,1)S(1)} %add_convert_fusion.refs_0_), channel_id=1, source_target_pairs={{0,6},{1,7},{2,4},{3,5},{4,2},{5,3},{6,0},{7,1},{8,14},{9,15},{10,... | collective-permute-start | bytes 221192 | tf_op jit(solution)/shard_map/ppermute | solution.py:80
  58.8 6.4 %collective-permute-start.23 = (bf16[96,384]{1,0:T(8,128)(2,1)S(1)}, bf16[96,384]{1,0:T(8,128)(2,1)S(1)}, u32[]{:S(2)}, u32[]{:S(2)}) collective-permute-start(bf16[96,384]{1,0:T(8,128)(2,1)S(1)} %add_convert_fusion.refs_0_), channel_id=1, source_target_pairs={{0,8},{1,9},{2,10},{3,11},{4,12},{5,13},{6,14},{7,15},{8,0},{9,1},... | collective-permute-start | bytes 221192 | tf_op jit(solution)/shard_map/ppermute | solution.py:80
  61.0 5.3 %collective-permute-start.22 = (bf16[96,384]{1,0:T(8,128)(2,1)S(1)}, bf16[96,384]{1,0:T(8,128)(2,1)S(1)}, u32[]{:S(2)}, u32[]{:S(2)}) collective-permute-start(bf16[96,384]{1,0:T(8,128)(2,1)S(1)} %add_convert_fusion.refs_0_), channel_id=1, source_target_pairs={{0,2},{1,3},{2,0},{3,1},{4,6},{5,7},{6,4},{7,5},{8,10},{9,11},{10,... | collective-permute-start | bytes 221192 | tf_op jit(solution)/shard_map/ppermute | solution.py:80
  62.5 4.4 %collective-permute-start.21 = (bf16[96,384]{1,0:T(8,128)(2,1)S(1)}, bf16[96,384]{1,0:T(8,128)(2,1)S(1)}, u32[]{:S(2)}, u32[]{:S(2)}) collective-permute-start(bf16[96,384]{1,0:T(8,128)(2,1)S(1)} %add_convert_fusion.refs_0_), channel_id=1, source_target_pairs={{0,4},{1,5},{2,6},{3,7},{4,0},{5,1},{6,2},{7,3},{8,12},{9,13},{10,... | collective-permute-start | bytes 221192 | tf_op jit(solution)/shard_map/ppermute | solution.py:80
  63.5 6.3 %collective-permute-start.20 = (bf16[128,384]{1,0:T(8,128)(2,1)S(1)}, bf16[128,384]{1,0:T(8,128)(2,1)S(1)}, u32[]{:S(2)}, u32[]{:S(2)}) collective-permute-start(bf16[128,384]{1,0:T(8,128)(2,1)S(1)} %pad_maximum_fusion.9), channel_id=1, source_target_pairs={{0,16},{1,17},{2,18},{3,19},{4,20},{5,21},{6,22},{7,23},{8,24},{9,... | collective-permute-start | bytes 294920 | tf_op jit(solution)/shard_map/ppermute | solution.py:80
  65.2 4.6 %collective-permute-start.35 = (bf16[96,384]{1,0:T(8,128)(2,1)S(1)}, bf16[96,384]{1,0:T(8,128)(2,1)S(1)}, u32[]{:S(2)}, u32[]{:S(2)}) collective-permute-start(bf16[96,384]{1,0:T(8,128)(2,1)S(1)} %collective-permute-done.27.refs_7_), channel_id=1, source_target_pairs={{0,1},{1,0},{2,3},{3,2},{4,5},{5,4},{6,7},{7,6},{8,9},{9,8},{10,11... | collective-permute-start | bytes 221192 | tf_op jit(solution)/shard_map/ppermute | solution.py:80
  65.2 5.1 %collective-permute-start.34 = (bf16[96,384]{1,0:T(8,128)(2,1)S(1)}, bf16[96,384]{1,0:T(8,128)(2,1)S(1)}, u32[]{:S(2)}, u32[]{:S(2)}) collective-permute-start(bf16[96,384]{1,0:T(8,128)(2,1)S(1)} %collective-permute-done.26.refs_6_), channel_id=1, source_target_pairs={{0,1},{1,0},{2,3},{3,2},{4,5},{5,4},{6,7},{7,6},{8,9},{9,8},{10,11... | collective-permute-start | bytes 221192 | tf_op jit(solution)/shard_map/ppermute | solution.py:80
  66.3 5.1 %collective-permute-start.33 = (bf16[96,384]{1,0:T(8,128)(2,1)S(1)}, bf16[96,384]{1,0:T(8,128)(2,1)S(1)}, u32[]{:S(2)}, u32[]{:S(2)}) collective-permute-start(bf16[96,384]{1,0:T(8,128)(2,1)S(1)} %collective-permute-done.25.refs_5_), channel_id=1, source_target_pairs={{0,1},{1,0},{2,3},{3,2},{4,5},{5,4},{6,7},{7,6},{8,9},{9,8},{10,11... | collective-permute-start | bytes 221192 | tf_op jit(solution)/shard_map/ppermute | solution.py:80
  66.8 4.6 %collective-permute-start.32 = (bf16[96,384]{1,0:T(8,128)(2,1)S(1)}, bf16[96,384]{1,0:T(8,128)(2,1)S(1)}, u32[]{:S(2)}, u32[]{:S(2)}) collective-permute-start(bf16[96,384]{1,0:T(8,128)(2,1)S(1)} %collective-permute-done.24.refs_4_), channel_id=1, source_target_pairs={{0,1},{1,0},{2,3},{3,2},{4,5},{5,4},{6,7},{7,6},{8,9},{9,8},{10,11... | collective-permute-start | bytes 221192 | tf_op jit(solution)/shard_map/ppermute | solution.py:80
  69.8 1.6 %collective-permute-start.31 = (bf16[96,384]{1,0:T(8,128)(2,1)S(1)}, bf16[96,384]{1,0:T(8,128)(2,1)S(1)}, u32[]{:S(2)}, u32[]{:S(2)}) collective-permute-start(bf16[96,384]{1,0:T(8,128)(2,1)S(1)} %collective-permute-done.23.refs_3_), channel_id=1, source_target_pairs={{0,1},{1,0},{2,3},{3,2},{4,5},{5,4},{6,7},{7,6},{8,9},{9,8},{10,11... | collective-permute-start | bytes 221192 | tf_op jit(solution)/shard_map/ppermute | solution.py:80
  69.8 1.6 %collective-permute-start.30 = (bf16[96,384]{1,0:T(8,128)(2,1)S(1)}, bf16[96,384]{1,0:T(8,128)(2,1)S(1)}, u32[]{:S(2)}, u32[]{:S(2)}) collective-permute-start(bf16[96,384]{1,0:T(8,128)(2,1)S(1)} %collective-permute-done.22.refs_2_), channel_id=1, source_target_pairs={{0,1},{1,0},{2,3},{3,2},{4,5},{5,4},{6,7},{7,6},{8,9},{9,8},{10,11... | collective-permute-start | bytes 221192 | tf_op jit(solution)/shard_map/ppermute | solution.py:80
  70.3 1.3 %collective-permute-start.29 = (bf16[96,384]{1,0:T(8,128)(2,1)S(1)}, bf16[96,384]{1,0:T(8,128)(2,1)S(1)}, u32[]{:S(2)}, u32[]{:S(2)}) collective-permute-start(bf16[96,384]{1,0:T(8,128)(2,1)S(1)} %collective-permute-done.21.refs_1_), channel_id=1, source_target_pairs={{0,1},{1,0},{2,3},{3,2},{4,5},{5,4},{6,7},{7,6},{8,9},{9,8},{10,11... | collective-permute-start | bytes 221192 | tf_op jit(solution)/shard_map/ppermute | solution.py:80

commit v10 on v9

--- a/solution.py
+++ b/solution.py
@@ -135,17 +135,21 @@
     return copies
 
 
-def pick_kernel(feat_hbm, send_hbm, halo_ref, chosen_ref, *refs):
-    out_refs, (feat_ref, send_ref, sems) = refs[:-3], refs[-3:]
+def store_blocks(rows, through_ref, direct_refs):
+    size = direct_refs[0].shape[0]
+    for at, out_ref in enumerate(direct_refs):
+        out_ref[...] = rows[2 * at * size : (2 * at + 1) * size]
+        through_ref[at * size : (at + 1) * size] = rows[(2 * at + 1) * size : (2 * at + 2) * size]
+
+
+def pick_kernel(feat_hbm, send_hbm, halo_ref, chosen_ref, through_ref, *refs):
+    direct_refs, (feat_ref, send_ref, sems) = refs[:-3], refs[-3:]
     copies = fetch([(send_hbm, send_ref), (feat_hbm, feat_ref)], sems)
     copies[0].wait()
-    per_peer = send_ref.shape[1]
     chosen_ref[...] = listed_rows(send_ref, feat_ref.shape[0])
     copies[1].wait()
     halo_ref[...] = feat_ref[feat_ref.shape[0] - halo_ref.shape[0] :]
-    picked = rounded(f32_dot(chosen_ref[...], feat_ref[...]))
-    for at, out_ref in enumerate(out_refs):
-        out_ref[...] = picked[at * per_peer : (at + 1) * per_peer]
+    store_blocks(rounded(f32_dot(chosen_ref[...], feat_ref[...])), through_ref, direct_refs)
 
 
 def prepare_kernel(
@@ -241,10 +245,11 @@
     dom_size,
     *refs,
 ):
-    piece_refs, halo_ref, refs = refs[:dom_size], refs[dom_size], refs[dom_size + 1 :]
+    count = dom_size // 2 + 1
+    piece_refs, halo_ref, refs = refs[:count], refs[count], refs[count + 1 :]
     og_ref, wq_ref, wkv_ref, featt_ref, qt_ref, odt_ref, own_kv_ref, own_kvt_ref = refs[:8]
     local_bias_ref, far_bias_ref, gf_ref, halo_feat_ref = refs[8:12]
-    slot_feat_refs, refs = refs[12 : 12 + dom_size], refs[12 + dom_size :]
+    through_ref, direct_refs, refs = refs[12], refs[13 : 12 + count], refs[12 + count :]
     keep_ref, send_ref, rider_ref = refs[:3]
     slot_ref, kv_ref, kvt_ref, extt_ref, gqt_ref, gkvt_ref, ot_ref = refs[3:]
     width, row_count = qt_ref.shape
@@ -262,8 +267,10 @@
     kvt_ref[:, virt_at:] = own_kvt_ref[:, row_count:]
     extt_ref[:, tile:near] = featt_ref[:, :row_count]
     extt_ref[:, virt_at:] = featt_ref[:, row_count:]
-    for at, piece_ref in zip([0] + farthest_first(dom_size), piece_refs):
-        slot_ref[at * per_peer : (at + 1) * per_peer] = piece_ref[...]
+    slot_ref[:per_peer] = piece_refs[0][...]
+    slot_ref[per_peer : 2 * per_peer] = piece_refs[1][:per_peer]
+    for at, piece_ref in enumerate(piece_refs[:1:-1], 1):
+        slot_ref[2 * at * per_peer : (2 * at + 2) * per_peer] = piece_ref[...]
     for rows, source_ref in ((slice(0, tile), halo_ref), (slice(near, virt_at), slot_ref)):
         extt_ref[:, rows] = source_ref[...].T
         kv_ref[rows] = rounded(f32_dot(source_ref[...], wkv_ref[...]))
@@ -342,9 +349,7 @@
     own = by_feature[:, tile:near] + f32_dot(wq_ref[...], gqt_ref[...])
     gf_ref[...] = own.T
     halo_feat_ref[...] = rounded(by_feature[:, :tile].T)
-    slot_feat = rounded(by_feature[:, near:virt_at].T)
-    for at, out_ref in enumerate(slot_feat_refs):
-        out_ref[...] = slot_feat[at * per_peer : (at + 1) * per_peer]
+    store_blocks(rounded(by_feature[:, near:virt_at].T), through_ref, direct_refs)
     rider_ref[...] = by_feature[:, virt_at:].T * factor
 
     sums = (
@@ -376,12 +381,15 @@
 def place_kernel(*refs):
     part_refs, (gq_hbm, gkv_hbm, go_hbm, all_ref, out_ref, sems) = refs[:-6], refs[-6:]
     width = gq_hbm.shape[0]
-    rows = part_refs[0].shape[0]
-    half = len(part_refs) // 2
-    for at, digit in enumerate([0] + farthest_first(half)[::-1]):
+    square = len(part_refs) // 2
+    rows = part_refs[0].shape[0] // 2
+    half = 2 * square
+    for at, digit in enumerate(range(square)):
         for core in range(2):
-            place = (core * half + digit) * rows
-            all_ref[place : place + rows] = part_refs[core * half + at][...]
+            for near_z in range(2):
+                place = (core * half + near_z * square + digit) * rows
+                part = part_refs[core * square + at][near_z * rows : (near_z + 1) * rows]
+                all_ref[place : place + rows] = part
     held = own_digit(exchange_plan()[0]) + (lax.axis_index("rows") % 2) * half
     copies = []
     for at in range(2 * half):
@@ -445,24 +453,24 @@
     ext_rows = TILE + row_count + slots + padded
     nodes = row_count * lax.axis_size("dom") * lax.axis_size("rows")
     block, rest = exchange_plan()
+    square = block[:2]
     masks = partner_masks(block)
     order = farthest_first(len(masks))
     rows_per_piece = 2 * width // len(masks)
     bf16, f32 = jnp.bfloat16, jnp.float32
     shape = jax.ShapeDtypeStruct
 
-    halo, chosen, *sent = call(
+    halo, chosen, through, *direct = call(
         pick_kernel,
         "pick_rows",
         [shape((TILE, width), bf16), shape((slots, row_count), bf16)]
-        + [shape((per_peer, width), bf16)] * dom_size,
+        + [shape((slots // 2, width), bf16)]
+        + [shape((per_peer, width), bf16)] * (dom_size // 2),
         [features, send_rows],
         [pltpu.VMEM(features.shape, bf16), pltpu.VMEM(send_rows.shape, jnp.int32)],
         fetched=2,
     )
-    arrived = [sent[0]] + [swapped(sent[at], at, 0) for at in farthest_first(dom_size)]
-    halo, _ = lax.optimization_barrier((halo, arrived[1]))
-    halo = shifted(halo, "rows", 1)
+    through = swapped(through, 1, 0)
     prepared = call(
         functools.partial(prepare_kernel, per_peer),
         "prepare",
@@ -489,13 +497,20 @@
         fetched=8,
         flops=10 * row_count * width * width,
     )
+    (through, halo), _ = lax.optimization_barrier(((through, halo), prepared[0]))
+    arrived = [direct[0], through]
+    for at in reversed(range(1, dom_size // 2)):
+        handed_on = through[at * per_peer : (at + 1) * per_peer]
+        arrived.append(swapped(jnp.concatenate([direct[at], handed_on], axis=0), 2 * at, 0))
+    halo = shifted(halo, "rows", 1)
     own_feat, halo_feat, *results = call(
         functools.partial(attend_kernel, rows_per_piece, nodes**-0.5, per_peer, dom_size),
         "attend",
         [
             shape((row_count, width), f32),
             shape((TILE, width), bf16),
-            *[shape((per_peer, width), bf16)] * dom_size,
+            shape((slots // 2, width), bf16),
+            *[shape((per_peer, width), bf16)] * (dom_size // 2),
             shape((2 * width, width), f32),
             shape((2 * width + padded, width), bf16),
             shape((padded, width), f32),
@@ -512,13 +527,16 @@
         ],
         flops=32 * ext_rows * width * width,
     )
-    *slot_feat, keep, message, rider = results
+    through, *direct, keep, message, rider = results
 
     rider = rounded(rider).astype(f32)
     keep, rider = added(keep, rider, {1: swapped(message, *CORES)})
     rider = rider[: -(-virt_rows // 8) * 8]
     dom_bits = bits_of(dom_size)
-    slot_feat = [hop(slot_feat, dom_bits[0]).get(at, own) for at, own in enumerate(slot_feat)]
+    through = swapped(through, 1, 0)
+    slot_feat = []
+    for at, block_rows in enumerate(direct):
+        slot_feat += [block_rows, through[at * per_peer : (at + 1) * per_peer]]
 
     parts = [keep[at * rows_per_piece : (at + 1) * rows_per_piece] for at in range(len(masks))]
     messages = {at: swapped(with_rider(parts[at], rider), *masks[at]) for at in order}
@@ -540,14 +558,17 @@
     held = rounded(keep)
     held, slot_feat, halo_back = lax.optimization_barrier((held, slot_feat, halo_back))
     slot_feat = [hop(slot_feat, dom_bits[-1]).get(at, own) for at, own in enumerate(slot_feat)]
-    near = [held] + [swapped(held, *masks[at]) for at in order[::-1]]
-    far = [swapped(part, *CORES) for part in near]
+    held = jnp.concatenate([held, swapped(held, *block[2])], axis=0)
+    arrived = [swapped(held, *masks[at]) for at in (1, 2, 3)]
     (grad_features,) = call(
         return_kernel,
         "return_rows",
         [shape((row_count, width), f32)],
         [own_feat, chosen, halo_back, *slot_feat],
     )
+    arrived, _ = lax.optimization_barrier((arrived, grad_features))
+    near = [held, *arrived]
+    far = [swapped(part, *CORES) for part in near]
     grad_wq, grad_wkv, grad_wo = call(
         place_kernel,
         "place_sums",

time: 73.5 us -> 66.6 us (0.906)
  starting transfers between devices: 41.7 us -> 29.5 us
  waiting for transfers between devices: 15.2 us -> 20.5 us
    ppermute x34 -> x24, starting transfers between devices: 41.7 us -> 29.4 us  [swapped(): return lax.ppermute(block, ('dom', 'rows'), route)]
    ppermute x34 -> x24, waiting for transfers between devices: 15.2 us -> 20.5 us  [swapped(): return lax.ppermute(block, ('dom', 'rows'), route)]
  transfers between devices with their start and end apart: 36 -> 26, of which waited for: 12 -> 15; matrix products, arithmetic and copies ran while one was open for 1% -> 2% of each run, Pallas kernels for 5% -> 6%
where the time goes in v10:
time: 66.6 us; the launch traced here: 66.3 us
  starting transfers between devices  29.5 us (44%)
  waiting for transfers between devices  20.5 us (31%)
  Pallas kernels  14.4 us (22%)
  other arithmetic  1.01 us (2%)
  between operations  0.83 us (1%)
    ppermute x24, starting transfers between devices, swapped(): return lax.ppermute(block, ('dom', 'rows'), route)  29.4 us
    ppermute x24, waiting for transfers between devices, swapped(): return lax.ppermute(block, ('dom', 'rows'), route)  20.5 us
    pallas_call x5, Pallas kernels, call(): pl.pallas_call(kernel, out_shape=outs, in_specs=[pl.BlockSpec(memory_spac...  14.4 us
  transfers between devices with their start and end apart: 26, of which 15 were waited for; matrix products, arithmetic and copies ran while one was open for 2% of the time, Pallas kernels for 6%

profile of v10, /device:TPU:0, one launch (start us, length us, event | category | flops | bytes accessed | tf_op | source)
XLA Modules:
  0.0 66.3 jit_solution(17624360998452795489)
XLA Ops:
  0.6 1.2 %pick_rows.1 = (bf16[128,384]{1,0:T(8,128)(2,1)S(1)}, bf16[256,256]{1,0:T(8,128)(2,1)S(1)}, bf16[128,384]{1,0:T(8,128)(2,1)S(1)}, bf16[32,384]{1,0:T(8,128)(2,1)...) custom-call(bf16[256,384]{1,0:T(8,128)(2,1)} %feat_hbm.3, ...), custom_call_target="tpu_custom_call" | custom-call | bytes 623616 | tf_op jit(solution)/shard_map/pick_rows/pallas_call | solution.py:435
  1.9 3.0 %collective-permute-start = (bf16[128,384]{1,0:T(8,128)(2,1)S(1)}, bf16[128,384]{1,0:T(8,128)(2,1)S(1)}, u32[]{:S(2)}, u32[]{:S(2)}) collective-permute-start(bf16[128,384]{1,0:T(8,128)(2,1)S(1)} %get-tuple-element.60), channel_id=1, source_target_pairs={{0,4},{1,5},{2,6},{3,7},{4,0},{5,1},{6,2},{7,3},{8,12},{9,13},{10,... | collective-permute-start | bytes 294920 | tf_op jit(solution)/shard_map/ppermute | solution.py:80
  4.9 2.9 %prepare.1 = (bf16[256,384]{1,0:T(8,128)(2,1)S(1)}, bf16[384,384]{1,0:T(8,128)(2,1)S(1)}, bf16[384,768]{1,0:T(8,128)(2,1)S(1)}, bf16[384,272]{1,0:T(8,128)(2,1)S...) custom-call(bf16[256,384]{1,0:T(8,128)(2,1)} %feat_hbm.3, ...), custom_call_target="tpu_custom_call" | custom-call | flops 377487360 | bytes 4656128 | tf_op jit(solution)/shard_map/prepare/pallas_call | solution.py:435
  7.8 3.9 %collective-permute-start.1 = (bf16[64,384]{1,0:T(8,128)(2,1)S(1)}, bf16[64,384]{1,0:T(8,128)(2,1)S(1)}, u32[]{:S(2)}, u32[]{:S(2)}) collective-permute-start(bf16[64,384]{1,0:T(8,128)(2,1)S(1)} %pad_maximum_fusion.10), channel_id=1, source_target_pairs={{0,24},{1,25},{2,26},{3,27},{4,28},{5,29},{6,30},{7,31},{8,16},{9,... | collective-permute-start | bytes 147464 | tf_op jit(solution)/shard_map/ppermute | solution.py:80
  11.7 0.1 collective-permute-start.4
  11.8 0.6 collective-permute-start.3
  12.4 1.9 %collective-permute-done.1.refs_2_ = bf16[64,384]{1,0:T(8,128)(2,1)S(1)} collective-permute-done((bf16[64,384]{1,0:T(8,128)(2,1)S(1)}, bf16[64,384]{1,0:T(8,128)(2,1)S(1)}, u32[]{:S(2)}, u32[]{:S(2)}) %collective-permute-start.1) | collective-permute-done | bytes 49184 | tf_op jit(solution)/shard_map/ppermute | solution.py:80
  14.3 2.5 %collective-permute-done.2.refs_3_ = bf16[64,384]{1,0:T(8,128)(2,1)S(1)} collective-permute-done((bf16[64,384]{1,0:T(8,128)(2,1)S(1)}, bf16[64,384]{1,0:T(8,128)(2,1)S(1)}, u32[]{:S(2)}, u32[]{:S(2)}) %collective-permute-start.2) | collective-permute-done | bytes 49184 | tf_op jit(solution)/shard_map/ppermute | solution.py:80
  16.8 7.6 %attend.1 = (f32[256,384]{1,0:T(8,128)S(1)}, bf16[128,384]{1,0:T(8,128)(2,1)S(1)}, bf16[128,384]{1,0:T(8,128)(2,1)S(1)}, bf16[32,384]{1,0:T(8,128)(2,1)S(1)}, bf...) custom-call(bf16[32,384]{1,0:T(8,128)(2,1)S(1)} %get-tuple-element.5, ...), custom_call_target="tpu_custom_call" | custom-call | flops 3095396352 | bytes 5922816 | tf_op jit(solution)/shard_map/attend/pallas_call | solution.py:435
  24.4 0.1 collective-permute-start.5
  24.5 1.5 %collective-permute-start.14 = (bf16[128,384]{1,0:T(8,128)(2,1)S(1)}, bf16[128,384]{1,0:T(8,128)(2,1)S(1)}, u32[]{:S(2)}, u32[]{:S(2)}) collective-permute-start(bf16[128,384]{1,0:T(8,128)(2,1)S(1)} %get-tuple-element.83), channel_id=1, source_target_pairs={{0,4},{1,5},{2,6},{3,7},{4,0},{5,1},{6,2},{7,3},{8,12},{9,13},{10,... | collective-permute-start | bytes 294920 | tf_op jit(solution)/shard_map/ppermute | solution.py:80
  26.0 0.5 collective-permute-done.5
  26.5 0.2 fusion.7
  26.6 0.1 fusion.8
  26.7 0.1 pad_maximum_fusion.6
  26.8 2.5 %collective-permute-start.6 = (bf16[104,384]{1,0:T(8,128)(2,1)S(1)}, bf16[104,384]{1,0:T(8,128)(2,1)S(1)}, u32[]{:S(2)}, u32[]{:S(2)}) collective-permute-start(bf16[104,384]{1,0:T(8,128)(2,1)S(1)} %get-tuple-element.137), channel_id=1, source_target_pairs={{0,14},{1,15},{2,12},{3,13},{4,10},{5,11},{6,8},{7,9},{8,6},{9,7},... | collective-permute-start | bytes 239624 | tf_op jit(solution)/shard_map/ppermute | solution.py:80
  29.3 1.4 %collective-permute-start.7 = (bf16[104,384]{1,0:T(8,128)(2,1)S(1)}, bf16[104,384]{1,0:T(8,128)(2,1)S(1)}, u32[]{:S(2)}, u32[]{:S(2)}) collective-permute-start(bf16[104,384]{1,0:T(8,128)(2,1)S(1)} %get-tuple-element.138), channel_id=1, source_target_pairs={{0,10},{1,11},{2,8},{3,9},{4,14},{5,15},{6,12},{7,13},{8,2},{9,3},... | collective-permute-start | bytes 239624 | tf_op jit(solution)/shard_map/ppermute | solution.py:80
  30.7 0.2 collective-permute-start.8
  30.9 2.8 %collective-permute-start.9 = (bf16[104,384]{1,0:T(8,128)(2,1)S(1)}, bf16[104,384]{1,0:T(8,128)(2,1)S(1)}, u32[]{:S(2)}, u32[]{:S(2)}) collective-permute-start(bf16[104,384]{1,0:T(8,128)(2,1)S(1)} %get-tuple-element.140), channel_id=1, source_target_pairs={{0,6},{1,7},{2,4},{3,5},{4,2},{5,3},{6,0},{7,1},{8,14},{9,15},{10,... | collective-permute-start | bytes 239624 | tf_op jit(solution)/shard_map/ppermute | solution.py:80
  33.7 1.4 %collective-permute-start.10 = (bf16[104,384]{1,0:T(8,128)(2,1)S(1)}, bf16[104,384]{1,0:T(8,128)(2,1)S(1)}, u32[]{:S(2)}, u32[]{:S(2)}) collective-permute-start(bf16[104,384]{1,0:T(8,128)(2,1)S(1)} %get-tuple-element.141), channel_id=1, source_target_pairs={{0,8},{1,9},{2,10},{3,11},{4,12},{5,13},{6,14},{7,15},{8,0},{9,1},... | collective-permute-start | bytes 239624 | tf_op jit(solution)/shard_map/ppermute | solution.py:80
  35.1 0.6 collective-permute-start.11
  35.7 0.1 collective-permute-done.7
  35.8 1.6 %collective-permute-start.12 = (bf16[104,384]{1,0:T(8,128)(2,1)S(1)}, bf16[104,384]{1,0:T(8,128)(2,1)S(1)}, u32[]{:S(2)}, u32[]{:S(2)}) collective-permute-start(bf16[104,384]{1,0:T(8,128)(2,1)S(1)} %get-tuple-element.143), channel_id=1, source_target_pairs={{0,4},{1,5},{2,6},{3,7},{4,0},{5,1},{6,2},{7,3},{8,12},{9,13},{10,... | collective-permute-start | bytes 239624 | tf_op jit(solution)/shard_map/ppermute | solution.py:80
  37.4 0.8 %collective-permute-done.10 = bf16[104,384]{1,0:T(8,128)(2,1)S(1)} collective-permute-done((bf16[104,384]{1,0:T(8,128)(2,1)S(1)}, bf16[104,384]{1,0:T(8,128)(2,1)S(1)}, u32[]{:S(2)}, u32[]{:S(2)}) %collective-permute-start.10) | collective-permute-done | bytes 79904 | tf_op jit(solution)/shard_map/ppermute | solution.py:80
  38.2 1.3 %collective-permute-done.11 = bf16[104,384]{1,0:T(8,128)(2,1)S(1)} collective-permute-done((bf16[104,384]{1,0:T(8,128)(2,1)S(1)}, bf16[104,384]{1,0:T(8,128)(2,1)S(1)}, u32[]{:S(2)}, u32[]{:S(2)}) %collective-permute-start.11) | collective-permute-done | bytes 79904 | tf_op jit(solution)/shard_map/ppermute | solution.py:80
  39.5 0.7 %collective-permute-done.12 = bf16[104,384]{1,0:T(8,128)(2,1)S(1)} collective-permute-done((bf16[104,384]{1,0:T(8,128)(2,1)S(1)}, bf16[104,384]{1,0:T(8,128)(2,1)S(1)}, u32[]{:S(2)}, u32[]{:S(2)}) %collective-permute-start.12) | collective-permute-done | bytes 79904 | tf_op jit(solution)/shard_map/ppermute | solution.py:80
  40.2 0.1 fusion.6
  40.3 2.4 %collective-permute-start.13 = (bf16[104,384]{1,0:T(8,128)(2,1)S(1)}, bf16[104,384]{1,0:T(8,128)(2,1)S(1)}, u32[]{:S(2)}, u32[]{:S(2)}) collective-permute-start(bf16[104,384]{1,0:T(8,128)(2,1)S(1)} %pad_maximum_fusion.9), channel_id=1, source_target_pairs={{0,16},{1,17},{2,18},{3,19},{4,20},{5,21},{6,22},{7,23},{8,24},{9,... | collective-permute-start | bytes 239624 | tf_op jit(solution)/shard_map/ppermute | solution.py:80
  42.7 0.9 %collective-permute-start.15 = (bf16[128,384]{1,0:T(8,128)(2,1)S(1)}, bf16[128,384]{1,0:T(8,128)(2,1)S(1)}, u32[]{:S(2)}, u32[]{:S(2)}) collective-permute-start(bf16[128,384]{1,0:T(8,128)(2,1)S(1)} %pad_maximum_fusion.7), channel_id=1, source_target_pairs={{0,8},{1,9},{2,10},{3,11},{4,12},{5,13},{6,14},{7,15},{8,0},{9,1},... | collective-permute-start | bytes 294920 | tf_op jit(solution)/shard_map/ppermute | solution.py:80
  43.6 3.0 %collective-permute-done.13 = bf16[104,384]{1,0:T(8,128)(2,1)S(1)} collective-permute-done((bf16[104,384]{1,0:T(8,128)(2,1)S(1)}, bf16[104,384]{1,0:T(8,128)(2,1)S(1)}, u32[]{:S(2)}, u32[]{:S(2)}) %collective-permute-start.13) | collective-permute-done | bytes 79904 | tf_op jit(solution)/shard_map/ppermute | solution.py:80
  46.6 1.0 %collective-permute-done.15 = bf16[128,384]{1,0:T(8,128)(2,1)S(1)} collective-permute-done((bf16[128,384]{1,0:T(8,128)(2,1)S(1)}, bf16[128,384]{1,0:T(8,128)(2,1)S(1)}, u32[]{:S(2)}, u32[]{:S(2)}) %collective-permute-start.15) | collective-permute-done | bytes 98336 | tf_op jit(solution)/shard_map/ppermute | solution.py:80
  47.6 0.7 %collective-permute-start.18 = (bf16[96,384]{1,0:T(8,128)(2,1)S(1)}, bf16[96,384]{1,0:T(8,128)(2,1)S(1)}, u32[]{:S(2)}, u32[]{:S(2)}) collective-permute-start(bf16[96,384]{1,0:T(8,128)(2,1)S(1)} %add_convert_fusion), channel_id=1, source_target_pairs={{0,8},{1,9},{2,10},{3,11},{4,12},{5,13},{6,14},{7,15},{8,0},{9,1},... | collective-permute-start | bytes 221192 | tf_op jit(solution)/shard_map/ppermute | solution.py:80
  48.3 1.7 %collective-permute-start.17 = (bf16[128,384]{1,0:T(8,128)(2,1)S(1)}, bf16[128,384]{1,0:T(8,128)(2,1)S(1)}, u32[]{:S(2)}, u32[]{:S(2)}) collective-permute-start(bf16[128,384]{1,0:T(8,128)(2,1)S(1)} %pad_maximum_fusion.8), channel_id=1, source_target_pairs={{0,16},{1,17},{2,18},{3,19},{4,20},{5,21},{6,22},{7,23},{8,24},{9,... | collective-permute-start | bytes 294920 | tf_op jit(solution)/shard_map/ppermute | solution.py:80
  50.0 2.3 %collective-permute-done.18 = bf16[96,384]{1,0:T(8,128)(2,1)S(1)} collective-permute-done((bf16[96,384]{1,0:T(8,128)(2,1)S(1)}, bf16[96,384]{1,0:T(8,128)(2,1)S(1)}, u32[]{:S(2)}, u32[]{:S(2)}) %collective-permute-start.18) | collective-permute-done | bytes 73760 | tf_op jit(solution)/shard_map/ppermute | solution.py:80
  52.4 0.1 collective-permute-start.22
  52.4 1.5 %collective-permute-start.21 = (bf16[192,384]{1,0:T(8,128)(2,1)S(1)}, bf16[192,384]{1,0:T(8,128)(2,1)S(1)}, u32[]{:S(2)}, u32[]{:S(2)}) collective-permute-start(bf16[192,384]{1,0:T(8,128)(2,1)S(1)} %constant_dynamic-update-slice_fusion.refs_0_), channel_id=1, source_target_pairs={{0,6},{1,7},{2,4},{3,5},{4,2},{5,3},{6,0},{7,1},{8,14},{9,15},{10,... | collective-permute-start | bytes 442376 | tf_op jit(solution)/shard_map/ppermute | solution.py:80
  53.9 1.9 %collective-permute-start.20 = (bf16[192,384]{1,0:T(8,128)(2,1)S(1)}, bf16[192,384]{1,0:T(8,128)(2,1)S(1)}, u32[]{:S(2)}, u32[]{:S(2)}) collective-permute-start(bf16[192,384]{1,0:T(8,128)(2,1)S(1)} %constant_dynamic-update-slice_fusion.refs_0_), channel_id=1, source_target_pairs={{0,2},{1,3},{2,0},{3,1},{4,6},{5,7},{6,4},{7,5},{8,10},{9,11},{10,... | collective-permute-start | bytes 442376 | tf_op jit(solution)/shard_map/ppermute | solution.py:80
  55.8 0.2 collective-permute-start.19
  56.0 1.0 %return_rows.1 = f32[256,384]{1,0:T(8,128)} custom-call(f32[256,384]{1,0:T(8,128)S(1)} %get-tuple-element.77.gf_ref, bf16[256,256]{1,0:T(8,128)(2,1)S(1)} %get-tuple-element.78.chosen_ref, bf16[128,384]{1,0:T(8,128)(2,1)S(1)} %collective-permute-done.16.halo_ref, bf16[32,384]{1,0:T(8,128)(2,1)S(1)} %get-tuple-element.98.refs_0_, ...), custom_call_target="tpu_custom_call" | custom-call | bytes 1212416 | tf_op jit(solution)/shard_map/return_rows/pallas_call | solution.py:435
  57.0 3.1 %collective-permute-done.21.refs_3_ = bf16[192,384]{1,0:T(8,128)(2,1)S(1)} collective-permute-done((bf16[192,384]{1,0:T(8,128)(2,1)S(1)}, bf16[192,384]{1,0:T(8,128)(2,1)S(1)}, u32[]{:S(2)}, u32[]{:S(2)}) %collective-permute-start.21) | collective-permute-done | bytes 147488 | tf_op jit(solution)/shard_map/ppermute | solution.py:80
  60.1 2.7 %collective-permute-done.20.refs_2_ = bf16[192,384]{1,0:T(8,128)(2,1)S(1)} collective-permute-done((bf16[192,384]{1,0:T(8,128)(2,1)S(1)}, bf16[192,384]{1,0:T(8,128)(2,1)S(1)}, u32[]{:S(2)}, u32[]{:S(2)}) %collective-permute-start.20) | collective-permute-done | bytes 147488 | tf_op jit(solution)/shard_map/ppermute | solution.py:80
  62.8 0.0 collective-permute-start.23
  62.8 0.5 collective-permute-start.24
  63.3 0.6 convert_add_fusion.1
  63.9 0.2 collective-permute-done.23.refs_5_
  64.1 0.2 collective-permute-done.24.refs_6_
  64.4 0.3 collective-permute-done.25.refs_7_
  64.7 1.6 %place_sums.1 = (f32[384,384]{1,0:T(8,128)}, f32[384,768]{1,0:T(8,128)}, f32[384,384]{1,0:T(8,128)}) custom-call(bf16[192,384]{1,0:T(8,128)(2,1)S(1)} %constant_dynamic-update-slice_fusion.refs_0_, bf16[192,384]{1,0:T(8,128)(2,1)S(1)} %collective-permute-done.19.refs_1_, bf16[192,384]{1,0:T(8,128)(2,1)S(1)} %collective-permute-done.20.refs_2_, ...), custom_call_target="tpu_custom_call" | custom-call | bytes 3538944 | tf_op jit(solution)/shard_map/place_sums/pallas_call | solution.py:435
  (31 shorter events, 0.3 us)
Async XLA Ops:
  1.9 5.9 %collective-permute-start = (bf16[128,384]{1,0:T(8,128)(2,1)S(1)}, bf16[128,384]{1,0:T(8,128)(2,1)S(1)}, u32[]{:S(2)}, u32[]{:S(2)}) collective-permute-start(bf16[128,384]{1,0:T(8,128)(2,1)S(1)} %get-tuple-element.60), channel_id=1, source_target_pairs={{0,4},{1,5},{2,6},{3,7},{4,0},{5,1},{6,2},{7,3},{8,12},{9,13},{10,... | collective-permute-start | bytes 294920 | tf_op jit(solution)/shard_map/ppermute | solution.py:80
  7.8 6.5 %collective-permute-start.1 = (bf16[64,384]{1,0:T(8,128)(2,1)S(1)}, bf16[64,384]{1,0:T(8,128)(2,1)S(1)}, u32[]{:S(2)}, u32[]{:S(2)}) collective-permute-start(bf16[64,384]{1,0:T(8,128)(2,1)S(1)} %pad_maximum_fusion.10), channel_id=1, source_target_pairs={{0,24},{1,25},{2,26},{3,27},{4,28},{5,29},{6,30},{7,31},{8,16},{9,... | collective-permute-start | bytes 147464 | tf_op jit(solution)/shard_map/ppermute | solution.py:80
  11.7 5.1 %collective-permute-start.2 = (bf16[64,384]{1,0:T(8,128)(2,1)S(1)}, bf16[64,384]{1,0:T(8,128)(2,1)S(1)}, u32[]{:S(2)}, u32[]{:S(2)}) collective-permute-start(bf16[64,384]{1,0:T(8,128)(2,1)S(1)} %pad_maximum_fusion.11), channel_id=1, source_target_pairs={{0,16},{1,17},{2,18},{3,19},{4,20},{5,21},{6,22},{7,23},{8,24},{9,... | collective-permute-start | bytes 147464 | tf_op jit(solution)/shard_map/ppermute | solution.py:80
  11.7 5.1 %collective-permute-start.4 = (bf16[128,384]{1,0:T(8,128)(2,1)S(1)}, bf16[128,384]{1,0:T(8,128)(2,1)S(1)}, u32[]{:S(2)}, u32[]{:S(2)}) collective-permute-start(bf16[128,384]{1,0:T(8,128)(2,1)S(1)} %get-tuple-element.67), channel_id=1, source_target_pairs={{3,0},{0,1},{1,2},{2,3},{7,4},{4,5},{5,6},{6,7},{11,8},{8,9},{9,10... | collective-permute-start | bytes 294920 | tf_op jit(solution)/shard_map/ppermute | solution.py:86
  11.8 5.0 %collective-permute-start.3 = (bf16[64,384]{1,0:T(8,128)(2,1)S(1)}, bf16[64,384]{1,0:T(8,128)(2,1)S(1)}, u32[]{:S(2)}, u32[]{:S(2)}) collective-permute-start(bf16[64,384]{1,0:T(8,128)(2,1)S(1)} %pad_maximum_fusion.12), channel_id=1, source_target_pairs={{0,8},{1,9},{2,10},{3,11},{4,12},{5,13},{6,14},{7,15},{8,0},{9,1},... | collective-permute-start | bytes 147464 | tf_op jit(solution)/shard_map/ppermute | solution.py:80
  24.4 2.1 %collective-permute-start.5 = (bf16[784,384]{1,0:T(8,128)(2,1)S(1)}, bf16[784,384]{1,0:T(8,128)(2,1)S(1)}, u32[]{:S(2)}, u32[]{:S(2)}) collective-permute-start(bf16[784,384]{1,0:T(8,128)(2,1)S(1)} %get-tuple-element.80), channel_id=1, source_target_pairs={{0,1},{1,0},{2,3},{3,2},{4,5},{5,4},{6,7},{7,6},{8,9},{9,8},{10,11... | collective-permute-start | bytes 1806344 | tf_op jit(solution)/shard_map/ppermute | solution.py:80
  24.5 9.2 %collective-permute-start.14 = (bf16[128,384]{1,0:T(8,128)(2,1)S(1)}, bf16[128,384]{1,0:T(8,128)(2,1)S(1)}, u32[]{:S(2)}, u32[]{:S(2)}) collective-permute-start(bf16[128,384]{1,0:T(8,128)(2,1)S(1)} %get-tuple-element.83), channel_id=1, source_target_pairs={{0,4},{1,5},{2,6},{3,7},{4,0},{5,1},{6,2},{7,3},{8,12},{9,13},{10,... | collective-permute-start | bytes 294920 | tf_op jit(solution)/shard_map/ppermute | solution.py:80
  26.8 8.3 %collective-permute-start.6 = (bf16[104,384]{1,0:T(8,128)(2,1)S(1)}, bf16[104,384]{1,0:T(8,128)(2,1)S(1)}, u32[]{:S(2)}, u32[]{:S(2)}) collective-permute-start(bf16[104,384]{1,0:T(8,128)(2,1)S(1)} %get-tuple-element.137), channel_id=1, source_target_pairs={{0,14},{1,15},{2,12},{3,13},{4,10},{5,11},{6,8},{7,9},{8,6},{9,7},... | collective-permute-start | bytes 239624 | tf_op jit(solution)/shard_map/ppermute | solution.py:80
  29.3 6.5 %collective-permute-start.7 = (bf16[104,384]{1,0:T(8,128)(2,1)S(1)}, bf16[104,384]{1,0:T(8,128)(2,1)S(1)}, u32[]{:S(2)}, u32[]{:S(2)}) collective-permute-start(bf16[104,384]{1,0:T(8,128)(2,1)S(1)} %get-tuple-element.138), channel_id=1, source_target_pairs={{0,10},{1,11},{2,8},{3,9},{4,14},{5,15},{6,12},{7,13},{8,2},{9,3},... | collective-permute-start | bytes 239624 | tf_op jit(solution)/shard_map/ppermute | solution.py:80
  30.7 6.6 %collective-permute-start.8 = (bf16[104,384]{1,0:T(8,128)(2,1)S(1)}, bf16[104,384]{1,0:T(8,128)(2,1)S(1)}, u32[]{:S(2)}, u32[]{:S(2)}) collective-permute-start(bf16[104,384]{1,0:T(8,128)(2,1)S(1)} %get-tuple-element.139), channel_id=1, source_target_pairs={{0,12},{1,13},{2,14},{3,15},{4,8},{5,9},{6,10},{7,11},{8,4},{9,5},... | collective-permute-start | bytes 239624 | tf_op jit(solution)/shard_map/ppermute | solution.py:80
  30.9 6.5 %collective-permute-start.9 = (bf16[104,384]{1,0:T(8,128)(2,1)S(1)}, bf16[104,384]{1,0:T(8,128)(2,1)S(1)}, u32[]{:S(2)}, u32[]{:S(2)}) collective-permute-start(bf16[104,384]{1,0:T(8,128)(2,1)S(1)} %get-tuple-element.140), channel_id=1, source_target_pairs={{0,6},{1,7},{2,4},{3,5},{4,2},{5,3},{6,0},{7,1},{8,14},{9,15},{10,... | collective-permute-start | bytes 239624 | tf_op jit(solution)/shard_map/ppermute | solution.py:80
  33.7 4.5 %collective-permute-start.10 = (bf16[104,384]{1,0:T(8,128)(2,1)S(1)}, bf16[104,384]{1,0:T(8,128)(2,1)S(1)}, u32[]{:S(2)}, u32[]{:S(2)}) collective-permute-start(bf16[104,384]{1,0:T(8,128)(2,1)S(1)} %get-tuple-element.141), channel_id=1, source_target_pairs={{0,8},{1,9},{2,10},{3,11},{4,12},{5,13},{6,14},{7,15},{8,0},{9,1},... | collective-permute-start | bytes 239624 | tf_op jit(solution)/shard_map/ppermute | solution.py:80
  35.1 4.4 %collective-permute-start.11 = (bf16[104,384]{1,0:T(8,128)(2,1)S(1)}, bf16[104,384]{1,0:T(8,128)(2,1)S(1)}, u32[]{:S(2)}, u32[]{:S(2)}) collective-permute-start(bf16[104,384]{1,0:T(8,128)(2,1)S(1)} %get-tuple-element.142), channel_id=1, source_target_pairs={{0,2},{1,3},{2,0},{3,1},{4,6},{5,7},{6,4},{7,5},{8,10},{9,11},{10,... | collective-permute-start | bytes 239624 | tf_op jit(solution)/shard_map/ppermute | solution.py:80
  35.8 4.4 %collective-permute-start.12 = (bf16[104,384]{1,0:T(8,128)(2,1)S(1)}, bf16[104,384]{1,0:T(8,128)(2,1)S(1)}, u32[]{:S(2)}, u32[]{:S(2)}) collective-permute-start(bf16[104,384]{1,0:T(8,128)(2,1)S(1)} %get-tuple-element.143), channel_id=1, source_target_pairs={{0,4},{1,5},{2,6},{3,7},{4,0},{5,1},{6,2},{7,3},{8,12},{9,13},{10,... | collective-permute-start | bytes 239624 | tf_op jit(solution)/shard_map/ppermute | solution.py:80
  40.3 6.3 %collective-permute-start.13 = (bf16[104,384]{1,0:T(8,128)(2,1)S(1)}, bf16[104,384]{1,0:T(8,128)(2,1)S(1)}, u32[]{:S(2)}, u32[]{:S(2)}) collective-permute-start(bf16[104,384]{1,0:T(8,128)(2,1)S(1)} %pad_maximum_fusion.9), channel_id=1, source_target_pairs={{0,16},{1,17},{2,18},{3,19},{4,20},{5,21},{6,22},{7,23},{8,24},{9,... | collective-permute-start | bytes 239624 | tf_op jit(solution)/shard_map/ppermute | solution.py:80
  42.7 4.9 %collective-permute-start.15 = (bf16[128,384]{1,0:T(8,128)(2,1)S(1)}, bf16[128,384]{1,0:T(8,128)(2,1)S(1)}, u32[]{:S(2)}, u32[]{:S(2)}) collective-permute-start(bf16[128,384]{1,0:T(8,128)(2,1)S(1)} %pad_maximum_fusion.7), channel_id=1, source_target_pairs={{0,8},{1,9},{2,10},{3,11},{4,12},{5,13},{6,14},{7,15},{8,0},{9,1},... | collective-permute-start | bytes 294920 | tf_op jit(solution)/shard_map/ppermute | solution.py:80
  43.6 4.0 %collective-permute-start.16 = (bf16[128,384]{1,0:T(8,128)(2,1)S(1)}, bf16[128,384]{1,0:T(8,128)(2,1)S(1)}, u32[]{:S(2)}, u32[]{:S(2)}) collective-permute-start(bf16[128,384]{1,0:T(8,128)(2,1)S(1)} %get-tuple-element.96), channel_id=1, source_target_pairs={{1,0},{2,1},{3,2},{0,3},{5,4},{6,5},{7,6},{4,7},{9,8},{10,9},{11,1... | collective-permute-start | bytes 294920 | tf_op jit(solution)/shard_map/ppermute | solution.py:86
  47.6 4.7 %collective-permute-start.18 = (bf16[96,384]{1,0:T(8,128)(2,1)S(1)}, bf16[96,384]{1,0:T(8,128)(2,1)S(1)}, u32[]{:S(2)}, u32[]{:S(2)}) collective-permute-start(bf16[96,384]{1,0:T(8,128)(2,1)S(1)} %add_convert_fusion), channel_id=1, source_target_pairs={{0,8},{1,9},{2,10},{3,11},{4,12},{5,13},{6,14},{7,15},{8,0},{9,1},... | collective-permute-start | bytes 221192 | tf_op jit(solution)/shard_map/ppermute | solution.py:80
  48.3 7.7 %collective-permute-start.17 = (bf16[128,384]{1,0:T(8,128)(2,1)S(1)}, bf16[128,384]{1,0:T(8,128)(2,1)S(1)}, u32[]{:S(2)}, u32[]{:S(2)}) collective-permute-start(bf16[128,384]{1,0:T(8,128)(2,1)S(1)} %pad_maximum_fusion.8), channel_id=1, source_target_pairs={{0,16},{1,17},{2,18},{3,19},{4,20},{5,21},{6,22},{7,23},{8,24},{9,... | collective-permute-start | bytes 294920 | tf_op jit(solution)/shard_map/ppermute | solution.py:80
  52.4 11.6 %collective-permute-start.22 = (bf16[192,384]{1,0:T(8,128)(2,1)S(1)}, bf16[192,384]{1,0:T(8,128)(2,1)S(1)}, u32[]{:S(2)}, u32[]{:S(2)}) collective-permute-start(bf16[192,384]{1,0:T(8,128)(2,1)S(1)} %constant_dynamic-update-slice_fusion.refs_0_), channel_id=1, source_target_pairs={{0,1},{1,0},{2,3},{3,2},{4,5},{5,4},{6,7},{7,6},{8,9},{9,8},{10,11... | collective-permute-start | bytes 442376 | tf_op jit(solution)/shard_map/ppermute | solution.py:80
  52.4 7.7 %collective-permute-start.21 = (bf16[192,384]{1,0:T(8,128)(2,1)S(1)}, bf16[192,384]{1,0:T(8,128)(2,1)S(1)}, u32[]{:S(2)}, u32[]{:S(2)}) collective-permute-start(bf16[192,384]{1,0:T(8,128)(2,1)S(1)} %constant_dynamic-update-slice_fusion.refs_0_), channel_id=1, source_target_pairs={{0,6},{1,7},{2,4},{3,5},{4,2},{5,3},{6,0},{7,1},{8,14},{9,15},{10,... | collective-permute-start | bytes 442376 | tf_op jit(solution)/shard_map/ppermute | solution.py:80
  53.9 8.9 %collective-permute-start.20 = (bf16[192,384]{1,0:T(8,128)(2,1)S(1)}, bf16[192,384]{1,0:T(8,128)(2,1)S(1)}, u32[]{:S(2)}, u32[]{:S(2)}) collective-permute-start(bf16[192,384]{1,0:T(8,128)(2,1)S(1)} %constant_dynamic-update-slice_fusion.refs_0_), channel_id=1, source_target_pairs={{0,2},{1,3},{2,0},{3,1},{4,6},{5,7},{6,4},{7,5},{8,10},{9,11},{10,... | collective-permute-start | bytes 442376 | tf_op jit(solution)/shard_map/ppermute | solution.py:80
  55.8 7.0 %collective-permute-start.19 = (bf16[192,384]{1,0:T(8,128)(2,1)S(1)}, bf16[192,384]{1,0:T(8,128)(2,1)S(1)}, u32[]{:S(2)}, u32[]{:S(2)}) collective-permute-start(bf16[192,384]{1,0:T(8,128)(2,1)S(1)} %constant_dynamic-update-slice_fusion.refs_0_), channel_id=1, source_target_pairs={{0,4},{1,5},{2,6},{3,7},{4,0},{5,1},{6,2},{7,3},{8,12},{9,13},{10,... | collective-permute-start | bytes 442376 | tf_op jit(solution)/shard_map/ppermute | solution.py:80
  62.8 1.4 %collective-permute-start.23 = (bf16[192,384]{1,0:T(8,128)(2,1)S(1)}, bf16[192,384]{1,0:T(8,128)(2,1)S(1)}, u32[]{:S(2)}, u32[]{:S(2)}) collective-permute-start(bf16[192,384]{1,0:T(8,128)(2,1)S(1)} %collective-permute-done.19.refs_1_), channel_id=1, source_target_pairs={{0,1},{1,0},{2,3},{3,2},{4,5},{5,4},{6,7},{7,6},{8,9},{9,8},{10,11... | collective-permute-start | bytes 442376 | tf_op jit(solution)/shard_map/ppermute | solution.py:80
  62.8 1.6 %collective-permute-start.24 = (bf16[192,384]{1,0:T(8,128)(2,1)S(1)}, bf16[192,384]{1,0:T(8,128)(2,1)S(1)}, u32[]{:S(2)}, u32[]{:S(2)}) collective-permute-start(bf16[192,384]{1,0:T(8,128)(2,1)S(1)} %collective-permute-done.20.refs_2_), channel_id=1, source_target_pairs={{0,1},{1,0},{2,3},{3,2},{4,5},{5,4},{6,7},{7,6},{8,9},{9,8},{10,11... | collective-permute-start | bytes 442376 | tf_op jit(solution)/shard_map/ppermute | solution.py:80
  63.3 1.4 %collective-permute-start.25 = (bf16[192,384]{1,0:T(8,128)(2,1)S(1)}, bf16[192,384]{1,0:T(8,128)(2,1)S(1)}, u32[]{:S(2)}, u32[]{:S(2)}) collective-permute-start(bf16[192,384]{1,0:T(8,128)(2,1)S(1)} %collective-permute-done.21.refs_3_), channel_id=1, source_target_pairs={{0,1},{1,0},{2,3},{3,2},{4,5},{5,4},{6,7},{7,6},{8,9},{9,8},{10,11... | collective-permute-start | bytes 442376 | tf_op jit(solution)/shard_map/ppermute | solution.py:80

commit v11 on v10

--- a/solution.py
+++ b/solution.py
@@ -45,9 +45,9 @@
 
 def exchange_plan():
     dom_size, rows_size = lax.axis_size("dom"), lax.axis_size("rows")
-    block = [(1, 0), (0, 2), (2, 0)]
-    rest = [(bit, 0) for bit in bits_of(dom_size, 4)] + [(0, bit) for bit in bits_of(rows_size, 4)]
-    return block, rest
+    line, square = [(2, 0), (4, 0)], [(1, 0), (0, 2)]
+    rest = [(bit, 0) for bit in bits_of(dom_size, 8)] + [(0, bit) for bit in bits_of(rows_size, 4)]
+    return line, square, rest
 
 
 def partner_masks(block):
@@ -62,9 +62,10 @@
     return sorted(range(1, count), key=lambda digit: (-digit.bit_count(), -digit))
 
 
-def own_digit(block):
+def own_digit():
+    line, square, _ = exchange_plan()
     digit = 0
-    for i, (dom_mask, rows_mask) in enumerate(block):
+    for i, (dom_mask, rows_mask) in enumerate(line + square):
         own = (lax.axis_index("dom") & dom_mask) | (lax.axis_index("rows") & rows_mask)
         digit += jnp.where(own != 0, 1 << i, 0)
     return digit
@@ -104,11 +105,22 @@
     return keep, paired_sum(riders)
 
 
-def hop(blocks, bit):
-    moving = [at for at in range(len(blocks)) if at & bit]
-    rows = blocks[0].shape[0]
-    arrived = swapped(jnp.concatenate([blocks[at] for at in moving], axis=0), bit, 0)
-    return {at: arrived[i * rows : (i + 1) * rows] for i, at in enumerate(moving)}
+def scattered(keep, rider, bits):
+    masks = partner_masks(bits)
+    rows = keep.shape[0] // len(masks)
+    parts = [keep[at * rows : (at + 1) * rows] for at in range(len(masks))]
+    messages = {at: with_rider(parts[at], rider) for at in farthest_first(len(masks))}
+    arrived = {at: swapped(message, *masks[at]) for at, message in messages.items()}
+    return added(parts[0], rounded(rider).astype(jnp.float32), arrived)
+
+
+def handed_on(direct, through):
+    rows = direct[0].shape[0]
+    arrived = [direct[0], through]
+    for at in reversed(range(1, len(direct))):
+        message = jnp.concatenate([direct[at], through[at * rows : (at + 1) * rows]], axis=0)
+        arrived.append(swapped(message, 2 * at, 0))
+    return arrived
 
 
 def listed_rows(send_ref, row_count):
@@ -239,7 +251,6 @@
 
 
 def attend_kernel(
-    rows_per_piece,
     factor,
     per_peer,
     dom_size,
@@ -248,10 +259,8 @@
     count = dom_size // 2 + 1
     piece_refs, halo_ref, refs = refs[:count], refs[count], refs[count + 1 :]
     og_ref, wq_ref, wkv_ref, featt_ref, qt_ref, odt_ref, own_kv_ref, own_kvt_ref = refs[:8]
-    local_bias_ref, far_bias_ref, gf_ref, halo_feat_ref = refs[8:12]
-    through_ref, direct_refs, refs = refs[12], refs[13 : 12 + count], refs[12 + count :]
-    keep_ref, send_ref, rider_ref = refs[:3]
-    slot_ref, kv_ref, kvt_ref, extt_ref, gqt_ref, gkvt_ref, ot_ref = refs[3:]
+    local_bias_ref, far_bias_ref, send_ref, rider_ref = refs[8:12]
+    extt_ref, gqt_ref, gkvt_ref, ot_ref, slot_ref, kv_ref, kvt_ref = refs[12:]
     width, row_count = qt_ref.shape
     tile = halo_ref.shape[0]
     tile_count = row_count // tile
@@ -345,52 +354,64 @@
         to_keys(0, qt_ref[low:high], ds_local, ds_far, scale)
         to_keys(width, odt_ref[low:high], pb_local, pb_far, None)
 
-    by_feature = f32_dot(wkv_ref[...], gkvt_ref[...])
-    own = by_feature[:, tile:near] + f32_dot(wq_ref[...], gqt_ref[...])
+    rider_ref[...] = f32_dot(wkv_ref[...], gkvt_ref[:, virt_at:]).T * factor
+    weight_sums(
+        1 - lax.axis_index("rows") % 2, send_ref, extt_ref, gqt_ref, gkvt_ref, ot_ref, og_ref, factor
+    )
+    send_ref[2 * width :] = rounded(rider_ref[...])
+
+
+def weight_sums(core, out_ref, extt_ref, gqt_ref, gkvt_ref, ot_ref, og_ref, factor):
+    width, row_count = gqt_ref.shape
+    held = own_digit()
+    line, square, _ = exchange_plan()
+    rows = 2 * width >> len(line + square)
+
+    def write(at, total):
+        total = (total * factor).astype(out_ref.dtype)
+        for start in range(0, width, rows):
+            piece = (at * width + start) // rows
+            offset = pl.multiple_of((piece ^ held) * rows, ROW_PACK)
+            out_ref[pl.ds(offset, rows), :] = total[start : start + rows]
+
+    @pl.when(core == 0)
+    def _():
+        own = slice(TILE, TILE + row_count)
+        write(0, times_transposed(extt_ref[:, own], gqt_ref[...]))
+        write(1, times_transposed(extt_ref[...], gkvt_ref[:width]))
+
+    @pl.when(core == 1)
+    def _():
+        write(0, times_transposed(extt_ref[...], gkvt_ref[width:]))
+        write(1, f32_dot(ot_ref[...], og_ref[...]))
+
+
+def finish_kernel(factor, og_ref, wq_ref, wkv_ref, extt_ref, gqt_ref, gkvt_ref, ot_ref, *refs):
+    gf_ref, halo_feat_ref, keep_ref, through_ref = refs[:4]
+    direct_refs = refs[4:]
+    width, row_count = gqt_ref.shape
+    near = TILE + row_count
+    slots = 2 * through_ref.shape[0]
+    weight_sums(
+        lax.axis_index("rows") % 2, keep_ref, extt_ref, gqt_ref, gkvt_ref, ot_ref, og_ref, factor
+    )
+    by_feature = f32_dot(wkv_ref[...], gkvt_ref[:, : near + slots])
+    own = by_feature[:, TILE:near] + f32_dot(wq_ref[...], gqt_ref[...])
     gf_ref[...] = own.T
-    halo_feat_ref[...] = rounded(by_feature[:, :tile].T)
-    store_blocks(rounded(by_feature[:, near:virt_at].T), through_ref, direct_refs)
-    rider_ref[...] = by_feature[:, virt_at:].T * factor
-
-    sums = (
-        times_transposed(extt_ref[:, tile:near], gqt_ref[...]),
-        times_transposed(extt_ref[...], gkvt_ref[:width]),
-        times_transposed(extt_ref[...], gkvt_ref[width:]),
-        f32_dot(ot_ref[...], og_ref[...]),
-    )
-    pieces = keep_ref.shape[0] // rows_per_piece
-    held = own_digit(exchange_plan()[0])
-
-    def write(half, out_ref, cast):
-        for piece in range(pieces):
-            start = (half * pieces + piece) * rows_per_piece
-            value = sums[start // width][start % width : start % width + rows_per_piece] * factor
-            offset = pl.multiple_of((piece ^ held) * rows_per_piece, ROW_PACK)
-            out_ref[pl.ds(offset, rows_per_piece), :] = cast(value)
-
-    for half in range(2):
-
-        @pl.when(lax.axis_index("rows") % 2 == half)
-        def _():
-            write(half, keep_ref, lambda value: value)
-            write(1 - half, send_ref, rounded)
-
-    send_ref[keep_ref.shape[0] :] = rounded(rider_ref[...])
+    halo_feat_ref[...] = rounded(by_feature[:, :TILE].T)
+    store_blocks(rounded(by_feature[:, near:].T), through_ref, direct_refs)
 
 
 def place_kernel(*refs):
     part_refs, (gq_hbm, gkv_hbm, go_hbm, all_ref, out_ref, sems) = refs[:-6], refs[-6:]
     width = gq_hbm.shape[0]
-    square = len(part_refs) // 2
-    rows = part_refs[0].shape[0] // 2
-    half = 2 * square
-    for at, digit in enumerate(range(square)):
-        for core in range(2):
-            for near_z in range(2):
-                place = (core * half + near_z * square + digit) * rows
-                part = part_refs[core * square + at][near_z * rows : (near_z + 1) * rows]
-                all_ref[place : place + rows] = part
-    held = own_digit(exchange_plan()[0]) + (lax.axis_index("rows") % 2) * half
+    line, square, _ = exchange_plan()
+    half = 1 << len(line + square)
+    rows = 2 * width // half
+    step = part_refs[0].shape[0]
+    for at, part_ref in enumerate(part_refs):
+        all_ref[at * step : (at + 1) * step] = part_ref[...]
+    held = own_digit() + (lax.axis_index("rows") % 2) * half
     copies = []
     for at in range(2 * half):
         start = at * rows
@@ -415,7 +436,11 @@
     piece_refs, out_ref = refs[:-1], refs[-1]
     row_count = gf_ref.shape[0]
     tile = halo_ref.shape[0]
-    returned = jnp.concatenate([ref[...] for ref in piece_refs], axis=0)
+    per_peer = piece_refs[0].shape[0]
+    returned = jnp.concatenate(
+        [piece_refs[0][...], piece_refs[1][:per_peer]] + [ref[...] for ref in piece_refs[:1:-1]],
+        axis=0,
+    )
     total = gf_ref[...] + rows_contracted(chosen_ref[...], returned)
     out_ref[: row_count - tile] = total[: row_count - tile]
     out_ref[row_count - tile :] = total[row_count - tile :] + halo_ref[...].astype(jnp.float32)
@@ -452,11 +477,7 @@
     padded = ROW_PACK * -(-virt_rows // ROW_PACK)
     ext_rows = TILE + row_count + slots + padded
     nodes = row_count * lax.axis_size("dom") * lax.axis_size("rows")
-    block, rest = exchange_plan()
-    square = block[:2]
-    masks = partner_masks(block)
-    order = farthest_first(len(masks))
-    rows_per_piece = 2 * width // len(masks)
+    line, square, rest = exchange_plan()
     bf16, f32 = jnp.bfloat16, jnp.float32
     shape = jax.ShapeDtypeStruct
 
@@ -498,75 +519,67 @@
         flops=10 * row_count * width * width,
     )
     (through, halo), _ = lax.optimization_barrier(((through, halo), prepared[0]))
-    arrived = [direct[0], through]
-    for at in reversed(range(1, dom_size // 2)):
-        handed_on = through[at * per_peer : (at + 1) * per_peer]
-        arrived.append(swapped(jnp.concatenate([direct[at], handed_on], axis=0), 2 * at, 0))
+    arrived = handed_on(direct, through)
     halo = shifted(halo, "rows", 1)
-    own_feat, halo_feat, *results = call(
-        functools.partial(attend_kernel, rows_per_piece, nodes**-0.5, per_peer, dom_size),
+    message, rider, *gradients = call(
+        functools.partial(attend_kernel, nodes**-0.5, per_peer, dom_size),
         "attend",
         [
-            shape((row_count, width), f32),
-            shape((TILE, width), bf16),
-            shape((slots // 2, width), bf16),
-            *[shape((per_peer, width), bf16)] * (dom_size // 2),
-            shape((2 * width, width), f32),
             shape((2 * width + padded, width), bf16),
             shape((padded, width), f32),
+            shape((width, ext_rows), bf16),
+            shape((width, row_count), bf16),
+            shape((2 * width, ext_rows), bf16),
+            shape((width, row_count), bf16),
         ],
         [*arrived, halo, *prepared],
         [
             pltpu.VMEM((slots, width), bf16),
             pltpu.VMEM((ext_rows, 2 * width), bf16),
             pltpu.VMEM((2 * width, ext_rows), bf16),
-            pltpu.VMEM((width, ext_rows), bf16),
-            pltpu.VMEM((width, row_count), bf16),
-            pltpu.VMEM((2 * width, ext_rows), bf16),
-            pltpu.VMEM((width, row_count), bf16),
         ],
-        flops=32 * ext_rows * width * width,
-    )
-    through, *direct, keep, message, rider = results
-
-    rider = rounded(rider).astype(f32)
-    keep, rider = added(keep, rider, {1: swapped(message, *CORES)})
+        flops=28 * ext_rows * width * width,
+    )
+    message = swapped(message, *CORES)
+    own_feat, halo_feat, keep, through, *direct = call(
+        functools.partial(finish_kernel, nodes**-0.5),
+        "finish",
+        [
+            shape((row_count, width), f32),
+            shape((TILE, width), bf16),
+            shape((2 * width, width), f32),
+            shape((slots // 2, width), bf16),
+        ]
+        + [shape((per_peer, width), bf16)] * (dom_size // 2),
+        [*prepared[:3], *gradients],
+        flops=6 * ext_rows * width * width,
+    )
+
+    keep, rider = added(keep, rounded(rider).astype(f32), {1: message})
     rider = rider[: -(-virt_rows // 8) * 8]
-    dom_bits = bits_of(dom_size)
+    through, halo_feat, _ = lax.optimization_barrier((through, halo_feat, keep))
     through = swapped(through, 1, 0)
-    slot_feat = []
-    for at, block_rows in enumerate(direct):
-        slot_feat += [block_rows, through[at * per_peer : (at + 1) * per_peer]]
-
-    parts = [keep[at * rows_per_piece : (at + 1) * rows_per_piece] for at in range(len(masks))]
-    messages = {at: swapped(with_rider(parts[at], rider), *masks[at]) for at in order}
-    rider = rounded(rider).astype(f32)
-    keep, rider = added(parts[0], rider, messages)
-
-    for at, mask in enumerate(rest):
-        message = with_rider(keep, rider)
-        if at == 0:
-            (slot_feat, halo_feat), _ = lax.optimization_barrier(
-                ((slot_feat, halo_feat), message)
-            )
-            for bit in dom_bits[1:-1]:
-                slot_feat = [hop(slot_feat, bit).get(i, own) for i, own in enumerate(slot_feat)]
-            halo_back = shifted(halo_feat, "rows", -1)
+    halo_back = shifted(halo_feat, "rows", -1)
+    keep, rider = scattered(keep, rider, square)
+    keep, through, halo_back = lax.optimization_barrier((keep, through, halo_back))
+    keep, rider = scattered(keep, rider, line)
+    for mask in rest:
+        message = swapped(with_rider(keep, rider), *mask)
         keep, rider = rounded(keep).astype(f32), rounded(rider).astype(f32)
-        keep, rider = added(keep, rider, {1: swapped(message, *mask)})
+        keep, rider = added(keep, rider, {1: message})
 
     held = rounded(keep)
-    held, slot_feat, halo_back = lax.optimization_barrier((held, slot_feat, halo_back))
-    slot_feat = [hop(slot_feat, dom_bits[-1]).get(at, own) for at, own in enumerate(slot_feat)]
-    held = jnp.concatenate([held, swapped(held, *block[2])], axis=0)
-    arrived = [swapped(held, *masks[at]) for at in (1, 2, 3)]
+    back = {at: swapped(held, *partner_masks(line)[at]) for at in (3, 2, 1)}
+    held = jnp.concatenate([held] + [back[at] for at in sorted(back)], axis=0)
+    through, _ = lax.optimization_barrier((through, held))
+    returned = handed_on(direct, through)
+    arrived = [swapped(held, *masks) for masks in partner_masks(square)[1:]]
     (grad_features,) = call(
         return_kernel,
         "return_rows",
         [shape((row_count, width), f32)],
-        [own_feat, chosen, halo_back, *slot_feat],
-    )
-    arrived, _ = lax.optimization_barrier((arrived, grad_features))
+        [own_feat, chosen, halo_back, *returned],
+    )
     near = [held, *arrived]
     far = [swapped(part, *CORES) for part in near]
     grad_wq, grad_wkv, grad_wo = call(
@@ -577,7 +590,7 @@
         [
             pltpu.VMEM((4 * width, width), bf16),
             pltpu.VMEM((4 * width, width), f32),
-            pltpu.SemaphoreType.DMA((2 * len(masks),)),
+            pltpu.SemaphoreType.DMA((2 << len(line + square),)),
         ],
         stored=True,
     )

time: 66.6 us -> 71.4 us (1.072)
  waiting for transfers between devices: 20.5 us -> 25 us
  Pallas kernels: 14.4 us -> 15.2 us
    ppermute x24 -> x25, waiting for transfers between devices: 20.5 us -> 25 us  [swapped(): return lax.ppermute(block, ('dom', 'rows'), route)]
    pallas_call x5 -> x6, Pallas kernels: 14.4 us -> 15.2 us  [call(): pl.pallas_call(kernel, out_shape=outs, in_specs=[pl.BlockSpec(memory_spac...]
    ppermute x24 -> x25, starting transfers between devices: 29.4 us -> 28.9 us  [swapped(): return lax.ppermute(block, ('dom', 'rows'), route)]
  transfers between devices with their start and end apart: 26 -> 27, of which waited for: 15 -> 14; matrix products, arithmetic and copies ran while one was open for 2% -> 1% of each run, Pallas kernels for 6% -> 8%
where the time goes in v11:
time: 71.4 us; the launch traced here: 71.1 us
  starting transfers between devices  29 us (41%)
  waiting for transfers between devices  25 us (35%)
  Pallas kernels  15.2 us (21%)
  other arithmetic  1.01 us (1%)
  between operations  0.84 us (1%)
    ppermute x25, starting transfers between devices, swapped(): return lax.ppermute(block, ('dom', 'rows'), route)  28.9 us
    ppermute x25, waiting for transfers between devices, swapped(): return lax.ppermute(block, ('dom', 'rows'), route)  25 us
    pallas_call x6, Pallas kernels, call(): pl.pallas_call(kernel, out_shape=outs, in_specs=[pl.BlockSpec(memory_spac...  15.2 us
  transfers between devices with their start and end apart: 27, of which 14 were waited for; matrix products, arithmetic and copies ran while one was open for 1% of the time, Pallas kernels for 8%

profile of v11, /device:TPU:0, one launch (start us, length us, event | category | flops | bytes accessed | tf_op | source)
XLA Modules:
  0.0 71.1 jit_solution(2953505524717462128)
XLA Ops:
  0.6 1.2 %pick_rows.1 = (bf16[128,384]{1,0:T(8,128)(2,1)S(1)}, bf16[256,256]{1,0:T(8,128)(2,1)S(1)}, bf16[128,384]{1,0:T(8,128)(2,1)S(1)}, bf16[32,384]{1,0:T(8,128)(2,1)...) custom-call(bf16[256,384]{1,0:T(8,128)(2,1)} %feat_hbm.3, ...), custom_call_target="tpu_custom_call" | custom-call | bytes 623616 | tf_op jit(solution)/shard_map/pick_rows/pallas_call | solution.py:460
  1.9 3.0 %collective-permute-start = (bf16[128,384]{1,0:T(8,128)(2,1)S(1)}, bf16[128,384]{1,0:T(8,128)(2,1)S(1)}, u32[]{:S(2)}, u32[]{:S(2)}) collective-permute-start(bf16[128,384]{1,0:T(8,128)(2,1)S(1)} %get-tuple-element.51), channel_id=1, source_target_pairs={{0,4},{1,5},{2,6},{3,7},{4,0},{5,1},{6,2},{7,3},{8,12},{9,13},{10,... | collective-permute-start | bytes 294920 | tf_op jit(solution)/shard_map/ppermute | solution.py:81
  4.9 2.9 %prepare.1 = (bf16[256,384]{1,0:T(8,128)(2,1)S(1)}, bf16[384,384]{1,0:T(8,128)(2,1)S(1)}, bf16[384,768]{1,0:T(8,128)(2,1)S(1)}, bf16[384,272]{1,0:T(8,128)(2,1)S...) custom-call(bf16[256,384]{1,0:T(8,128)(2,1)} %feat_hbm.3, ...), custom_call_target="tpu_custom_call" | custom-call | flops 377487360 | bytes 4656128 | tf_op jit(solution)/shard_map/prepare/pallas_call | solution.py:460
  7.8 3.9 %collective-permute-start.1 = (bf16[64,384]{1,0:T(8,128)(2,1)S(1)}, bf16[64,384]{1,0:T(8,128)(2,1)S(1)}, u32[]{:S(2)}, u32[]{:S(2)}) collective-permute-start(bf16[64,384]{1,0:T(8,128)(2,1)S(1)} %pad_maximum_fusion.7), channel_id=1, source_target_pairs={{0,24},{1,25},{2,26},{3,27},{4,28},{5,29},{6,30},{7,31},{8,16},{9,... | collective-permute-start | bytes 147464 | tf_op jit(solution)/shard_map/ppermute | solution.py:81
  11.7 0.0 collective-permute-start.2
  11.7 0.1 collective-permute-start.4
  11.8 0.6 collective-permute-start.3
  12.4 1.9 %collective-permute-done.1.refs_2_ = bf16[64,384]{1,0:T(8,128)(2,1)S(1)} collective-permute-done((bf16[64,384]{1,0:T(8,128)(2,1)S(1)}, bf16[64,384]{1,0:T(8,128)(2,1)S(1)}, u32[]{:S(2)}, u32[]{:S(2)}) %collective-permute-start.1) | collective-permute-done | bytes 49184 | tf_op jit(solution)/shard_map/ppermute | solution.py:81
  14.3 2.5 %collective-permute-done.2.refs_3_ = bf16[64,384]{1,0:T(8,128)(2,1)S(1)} collective-permute-done((bf16[64,384]{1,0:T(8,128)(2,1)S(1)}, bf16[64,384]{1,0:T(8,128)(2,1)S(1)}, u32[]{:S(2)}, u32[]{:S(2)}) %collective-permute-start.2) | collective-permute-done | bytes 49184 | tf_op jit(solution)/shard_map/ppermute | solution.py:81
  16.8 6.9 %attend.1 = (bf16[784,384]{1,0:T(8,128)(2,1)S(1)}, f32[16,384]{1,0:T(8,128)S(1)}, bf16[384,656]{1,0:T(8,128)(2,1)S(1)}, bf16[384,256]{1,0:T(8,128)(2,1)S(1)}, bf...) custom-call(bf16[32,384]{1,0:T(8,128)(2,1)S(1)} %get-tuple-element.50.refs_0_, ...), custom_call_target="tpu_custom_call" | custom-call | flops 2708471808 | bytes 5959680 | tf_op jit(solution)/shard_map/attend/pallas_call | solution.py:460
  23.7 0.1 collective-permute-start.5
  23.7 1.5 %finish.1 = (f32[256,384]{1,0:T(8,128)S(1)}, bf16[128,384]{1,0:T(8,128)(2,1)S(1)}, f32[768,384]{1,0:T(8,128)S(1)}, bf16[128,384]{1,0:T(8,128)(2,1)S(1)}, bf16[32...) custom-call(bf16[256,384]{1,0:T(8,128)(2,1)S(1)} %get-tuple-element., ...), custom_call_target="tpu_custom_call" | custom-call | flops 580386816 | bytes 4853760 | tf_op jit(solution)/shard_map/finish/pallas_call | solution.py:460
  25.2 0.5 collective-permute-done.5
  25.7 0.2 fusion.2
  26.0 2.4 %collective-permute-start.6 = (bf16[200,384]{1,0:T(8,128)(2,1)S(1)}, bf16[200,384]{1,0:T(8,128)(2,1)S(1)}, u32[]{:S(2)}, u32[]{:S(2)}) collective-permute-start(bf16[200,384]{1,0:T(8,128)(2,1)S(1)} %get-tuple-element.106), channel_id=1, source_target_pairs={{0,6},{1,7},{2,4},{3,5},{4,2},{5,3},{6,0},{7,1},{8,14},{9,15},{10,... | collective-permute-start | bytes 460808 | tf_op jit(solution)/shard_map/ppermute | solution.py:81
  28.4 0.6 collective-permute-start.7
  29.1 0.5 collective-permute-start.8
  29.6 1.5 %collective-permute-start.9 = (bf16[128,384]{1,0:T(8,128)(2,1)S(1)}, bf16[128,384]{1,0:T(8,128)(2,1)S(1)}, u32[]{:S(2)}, u32[]{:S(2)}) collective-permute-start(bf16[128,384]{1,0:T(8,128)(2,1)S(1)} %get-tuple-element.76), channel_id=1, source_target_pairs={{0,4},{1,5},{2,6},{3,7},{4,0},{5,1},{6,2},{7,3},{8,12},{9,13},{10,... | collective-permute-start | bytes 294920 | tf_op jit(solution)/shard_map/ppermute | solution.py:81
  31.1 0.0 collective-permute-start.10
  31.1 2.7 %collective-permute-done.6 = bf16[200,384]{1,0:T(8,128)(2,1)S(1)} collective-permute-done((bf16[200,384]{1,0:T(8,128)(2,1)S(1)}, bf16[200,384]{1,0:T(8,128)(2,1)S(1)}, u32[]{:S(2)}, u32[]{:S(2)}) %collective-permute-start.6) | collective-permute-done | bytes 153632 | tf_op jit(solution)/shard_map/ppermute | solution.py:81
  33.8 2.5 %collective-permute-done.7 = bf16[200,384]{1,0:T(8,128)(2,1)S(1)} collective-permute-done((bf16[200,384]{1,0:T(8,128)(2,1)S(1)}, bf16[200,384]{1,0:T(8,128)(2,1)S(1)}, u32[]{:S(2)}, u32[]{:S(2)}) %collective-permute-start.7) | collective-permute-done | bytes 153632 | tf_op jit(solution)/shard_map/ppermute | solution.py:81
  36.3 0.8 %collective-permute-done.8 = bf16[200,384]{1,0:T(8,128)(2,1)S(1)} collective-permute-done((bf16[200,384]{1,0:T(8,128)(2,1)S(1)}, bf16[200,384]{1,0:T(8,128)(2,1)S(1)}, u32[]{:S(2)}, u32[]{:S(2)}) %collective-permute-start.8) | collective-permute-done | bytes 153632 | tf_op jit(solution)/shard_map/ppermute | solution.py:81
  37.1 0.1 fusion.1
  37.2 1.2 %collective-permute-done.9.refs_1_ = bf16[128,384]{1,0:T(8,128)(2,1)S(1)} collective-permute-done((bf16[128,384]{1,0:T(8,128)(2,1)S(1)}, bf16[128,384]{1,0:T(8,128)(2,1)S(1)}, u32[]{:S(2)}, u32[]{:S(2)}) %collective-permute-start.9) | collective-permute-done | bytes 98336 | tf_op jit(solution)/shard_map/ppermute | solution.py:81
  38.5 2.2 %collective-permute-start.11 = (bf16[56,384]{1,0:T(8,128)(2,1)S(1)}, bf16[56,384]{1,0:T(8,128)(2,1)S(1)}, u32[]{:S(2)}, u32[]{:S(2)}) collective-permute-start(bf16[56,384]{1,0:T(8,128)(2,1)S(1)} %get-tuple-element.103), channel_id=1, source_target_pairs={{0,24},{1,25},{2,26},{3,27},{4,28},{5,29},{6,30},{7,31},{8,16},{9,... | collective-permute-start | bytes 129032 | tf_op jit(solution)/shard_map/ppermute | solution.py:81
  40.7 0.1 collective-permute-start.12
  40.8 2.1 %collective-permute-start.13 = (bf16[56,384]{1,0:T(8,128)(2,1)S(1)}, bf16[56,384]{1,0:T(8,128)(2,1)S(1)}, u32[]{:S(2)}, u32[]{:S(2)}) collective-permute-start(bf16[56,384]{1,0:T(8,128)(2,1)S(1)} %get-tuple-element.105), channel_id=1, source_target_pairs={{0,8},{1,9},{2,10},{3,11},{4,12},{5,13},{6,14},{7,15},{8,0},{9,1},... | collective-permute-start | bytes 129032 | tf_op jit(solution)/shard_map/ppermute | solution.py:81
  43.0 1.4 %collective-permute-done.11 = bf16[56,384]{1,0:T(8,128)(2,1)S(1)} collective-permute-done((bf16[56,384]{1,0:T(8,128)(2,1)S(1)}, bf16[56,384]{1,0:T(8,128)(2,1)S(1)}, u32[]{:S(2)}, u32[]{:S(2)}) %collective-permute-start.11) | collective-permute-done | bytes 43040 | tf_op jit(solution)/shard_map/ppermute | solution.py:81
  44.4 1.7 %collective-permute-done.12 = bf16[56,384]{1,0:T(8,128)(2,1)S(1)} collective-permute-done((bf16[56,384]{1,0:T(8,128)(2,1)S(1)}, bf16[56,384]{1,0:T(8,128)(2,1)S(1)}, u32[]{:S(2)}, u32[]{:S(2)}) %collective-permute-start.12) | collective-permute-done | bytes 43040 | tf_op jit(solution)/shard_map/ppermute | solution.py:81
  46.1 2.1 %collective-permute-start.16 = (bf16[48,384]{1,0:T(8,128)(2,1)S(1)}, bf16[48,384]{1,0:T(8,128)(2,1)S(1)}, u32[]{:S(2)}, u32[]{:S(2)}) collective-permute-start(bf16[48,384]{1,0:T(8,128)(2,1)S(1)} %add_convert_fusion), channel_id=1, source_target_pairs={{0,24},{1,25},{2,26},{3,27},{4,28},{5,29},{6,30},{7,31},{8,16},{9,... | collective-permute-start | bytes 110600 | tf_op jit(solution)/shard_map/ppermute | solution.py:81
  48.2 0.3 collective-permute-start.15
  48.5 2.0 %collective-permute-start.14 = (bf16[48,384]{1,0:T(8,128)(2,1)S(1)}, bf16[48,384]{1,0:T(8,128)(2,1)S(1)}, u32[]{:S(2)}, u32[]{:S(2)}) collective-permute-start(bf16[48,384]{1,0:T(8,128)(2,1)S(1)} %add_convert_fusion), channel_id=1, source_target_pairs={{0,8},{1,9},{2,10},{3,11},{4,12},{5,13},{6,14},{7,15},{8,0},{9,1},... | collective-permute-start | bytes 110600 | tf_op jit(solution)/shard_map/ppermute | solution.py:81
  50.6 1.4 %collective-permute-done.16 = bf16[48,384]{1,0:T(8,128)(2,1)S(1)} collective-permute-done((bf16[48,384]{1,0:T(8,128)(2,1)S(1)}, bf16[48,384]{1,0:T(8,128)(2,1)S(1)}, u32[]{:S(2)}, u32[]{:S(2)}) %collective-permute-start.16) | collective-permute-done | bytes 36896 | tf_op jit(solution)/shard_map/ppermute | solution.py:81
  51.9 1.1 %collective-permute-done.15 = bf16[48,384]{1,0:T(8,128)(2,1)S(1)} collective-permute-done((bf16[48,384]{1,0:T(8,128)(2,1)S(1)}, bf16[48,384]{1,0:T(8,128)(2,1)S(1)}, u32[]{:S(2)}, u32[]{:S(2)}) %collective-permute-start.15) | collective-permute-done | bytes 36896 | tf_op jit(solution)/shard_map/ppermute | solution.py:81
  53.1 1.6 %collective-permute-start.22 = (bf16[192,384]{1,0:T(8,128)(2,1)S(1)}, bf16[192,384]{1,0:T(8,128)(2,1)S(1)}, u32[]{:S(2)}, u32[]{:S(2)}) collective-permute-start(bf16[192,384]{1,0:T(8,128)(2,1)S(1)} %pad_maximum_fusion.3.refs_0_), channel_id=1, source_target_pairs={{0,6},{1,7},{2,4},{3,5},{4,2},{5,3},{6,0},{7,1},{8,14},{9,15},{10,... | collective-permute-start | bytes 442376 | tf_op jit(solution)/shard_map/ppermute | solution.py:81
  54.7 1.4 %collective-permute-start.21 = (bf16[192,384]{1,0:T(8,128)(2,1)S(1)}, bf16[192,384]{1,0:T(8,128)(2,1)S(1)}, u32[]{:S(2)}, u32[]{:S(2)}) collective-permute-start(bf16[192,384]{1,0:T(8,128)(2,1)S(1)} %pad_maximum_fusion.3.refs_0_), channel_id=1, source_target_pairs={{0,2},{1,3},{2,0},{3,1},{4,6},{5,7},{6,4},{7,5},{8,10},{9,11},{10,... | collective-permute-start | bytes 442376 | tf_op jit(solution)/shard_map/ppermute | solution.py:81
  56.1 0.5 collective-permute-start.20
  56.7 2.0 %collective-permute-start.17 = (bf16[64,384]{1,0:T(8,128)(2,1)S(1)}, bf16[64,384]{1,0:T(8,128)(2,1)S(1)}, u32[]{:S(2)}, u32[]{:S(2)}) collective-permute-start(bf16[64,384]{1,0:T(8,128)(2,1)S(1)} %pad_maximum_fusion.10), channel_id=1, source_target_pairs={{0,24},{1,25},{2,26},{3,27},{4,28},{5,29},{6,30},{7,31},{8,16},{9,... | collective-permute-start | bytes 147464 | tf_op jit(solution)/shard_map/ppermute | solution.py:81
  58.7 1.0 %collective-permute-start.18 = (bf16[64,384]{1,0:T(8,128)(2,1)S(1)}, bf16[64,384]{1,0:T(8,128)(2,1)S(1)}, u32[]{:S(2)}, u32[]{:S(2)}) collective-permute-start(bf16[64,384]{1,0:T(8,128)(2,1)S(1)} %pad_maximum_fusion.11), channel_id=1, source_target_pairs={{0,16},{1,17},{2,18},{3,19},{4,20},{5,21},{6,22},{7,23},{8,24},{9,... | collective-permute-start | bytes 147464 | tf_op jit(solution)/shard_map/ppermute | solution.py:81
  59.7 2.9 %collective-permute-done.17.refs_2_ = bf16[64,384]{1,0:T(8,128)(2,1)S(1)} collective-permute-done((bf16[64,384]{1,0:T(8,128)(2,1)S(1)}, bf16[64,384]{1,0:T(8,128)(2,1)S(1)}, u32[]{:S(2)}, u32[]{:S(2)}) %collective-permute-start.17) | collective-permute-done | bytes 49184 | tf_op jit(solution)/shard_map/ppermute | solution.py:81
  62.6 1.6 %collective-permute-done.18.refs_3_ = bf16[64,384]{1,0:T(8,128)(2,1)S(1)} collective-permute-done((bf16[64,384]{1,0:T(8,128)(2,1)S(1)}, bf16[64,384]{1,0:T(8,128)(2,1)S(1)}, u32[]{:S(2)}, u32[]{:S(2)}) %collective-permute-start.18) | collective-permute-done | bytes 49184 | tf_op jit(solution)/shard_map/ppermute | solution.py:81
  64.2 0.2 collective-permute-start.19
  64.4 0.5 collective-permute-start.25
  64.9 0.1 collective-permute-start.24
  65.0 0.6 add_add_fusion
  65.6 2.7 %collective-permute-done.19.refs_4_ = bf16[64,384]{1,0:T(8,128)(2,1)S(1)} collective-permute-done((bf16[64,384]{1,0:T(8,128)(2,1)S(1)}, bf16[64,384]{1,0:T(8,128)(2,1)S(1)}, u32[]{:S(2)}, u32[]{:S(2)}) %collective-permute-start.19) | collective-permute-done | bytes 49184 | tf_op jit(solution)/shard_map/ppermute | solution.py:81
  68.3 1.0 %return_rows.1 = f32[256,384]{1,0:T(8,128)} custom-call(f32[256,384]{1,0:T(8,128)S(1)} %get-tuple-element.69.gf_ref, bf16[256,256]{1,0:T(8,128)(2,1)S(1)} %get-tuple-element.70.chosen_ref, bf16[128,384]{1,0:T(8,128)(2,1)S(1)} %collective-permute-done.10.halo_ref, bf16[32,384]{1,0:T(8,128)(2,1)S(1)} %get-tuple-element.79.refs_0_, ...), custom_call_target="tpu_custom_call" | custom-call | bytes 1286144 | tf_op jit(solution)/shard_map/return_rows/pallas_call | solution.py:460
  69.3 1.8 %place_sums.1 = (f32[384,384]{1,0:T(8,128)}, f32[384,768]{1,0:T(8,128)}, f32[384,384]{1,0:T(8,128)}) custom-call(bf16[192,384]{1,0:T(8,128)(2,1)S(1)} %pad_maximum_fusion.3.refs_0_, bf16[192,384]{1,0:T(8,128)(2,1)S(1)} %collective-permute-done.20.refs_1_, bf16[192,384]{1,0:T(8,128)(2,1)S(1)} %collective-permute-done.21.refs_2_, ...), custom_call_target="tpu_custom_call" | custom-call | bytes 3538944 | tf_op jit(solution)/shard_map/place_sums/pallas_call | solution.py:460
  (36 shorter events, 0.3 us)
Async XLA Ops:
  1.9 5.9 %collective-permute-start = (bf16[128,384]{1,0:T(8,128)(2,1)S(1)}, bf16[128,384]{1,0:T(8,128)(2,1)S(1)}, u32[]{:S(2)}, u32[]{:S(2)}) collective-permute-start(bf16[128,384]{1,0:T(8,128)(2,1)S(1)} %get-tuple-element.51), channel_id=1, source_target_pairs={{0,4},{1,5},{2,6},{3,7},{4,0},{5,1},{6,2},{7,3},{8,12},{9,13},{10,... | collective-permute-start | bytes 294920 | tf_op jit(solution)/shard_map/ppermute | solution.py:81
  7.8 6.5 %collective-permute-start.1 = (bf16[64,384]{1,0:T(8,128)(2,1)S(1)}, bf16[64,384]{1,0:T(8,128)(2,1)S(1)}, u32[]{:S(2)}, u32[]{:S(2)}) collective-permute-start(bf16[64,384]{1,0:T(8,128)(2,1)S(1)} %pad_maximum_fusion.7), channel_id=1, source_target_pairs={{0,24},{1,25},{2,26},{3,27},{4,28},{5,29},{6,30},{7,31},{8,16},{9,... | collective-permute-start | bytes 147464 | tf_op jit(solution)/shard_map/ppermute | solution.py:81
  11.7 5.1 %collective-permute-start.2 = (bf16[64,384]{1,0:T(8,128)(2,1)S(1)}, bf16[64,384]{1,0:T(8,128)(2,1)S(1)}, u32[]{:S(2)}, u32[]{:S(2)}) collective-permute-start(bf16[64,384]{1,0:T(8,128)(2,1)S(1)} %pad_maximum_fusion.8), channel_id=1, source_target_pairs={{0,16},{1,17},{2,18},{3,19},{4,20},{5,21},{6,22},{7,23},{8,24},{9,... | collective-permute-start | bytes 147464 | tf_op jit(solution)/shard_map/ppermute | solution.py:81
  11.7 5.1 %collective-permute-start.4 = (bf16[128,384]{1,0:T(8,128)(2,1)S(1)}, bf16[128,384]{1,0:T(8,128)(2,1)S(1)}, u32[]{:S(2)}, u32[]{:S(2)}) collective-permute-start(bf16[128,384]{1,0:T(8,128)(2,1)S(1)} %get-tuple-element.57), channel_id=1, source_target_pairs={{3,0},{0,1},{1,2},{2,3},{7,4},{4,5},{5,6},{6,7},{11,8},{8,9},{9,10... | collective-permute-start | bytes 294920 | tf_op jit(solution)/shard_map/ppermute | solution.py:87
  11.8 5.0 %collective-permute-start.3 = (bf16[64,384]{1,0:T(8,128)(2,1)S(1)}, bf16[64,384]{1,0:T(8,128)(2,1)S(1)}, u32[]{:S(2)}, u32[]{:S(2)}) collective-permute-start(bf16[64,384]{1,0:T(8,128)(2,1)S(1)} %pad_maximum_fusion.9), channel_id=1, source_target_pairs={{0,8},{1,9},{2,10},{3,11},{4,12},{5,13},{6,14},{7,15},{8,0},{9,1},... | collective-permute-start | bytes 147464 | tf_op jit(solution)/shard_map/ppermute | solution.py:81
  23.7 2.1 %collective-permute-start.5 = (bf16[784,384]{1,0:T(8,128)(2,1)S(1)}, bf16[784,384]{1,0:T(8,128)(2,1)S(1)}, u32[]{:S(2)}, u32[]{:S(2)}) collective-permute-start(bf16[784,384]{1,0:T(8,128)(2,1)S(1)} %get-tuple-element.72), channel_id=1, source_target_pairs={{0,1},{1,0},{2,3},{3,2},{4,5},{5,4},{6,7},{7,6},{8,9},{9,8},{10,11... | collective-permute-start | bytes 1806344 | tf_op jit(solution)/shard_map/ppermute | solution.py:81
  26.0 7.8 %collective-permute-start.6 = (bf16[200,384]{1,0:T(8,128)(2,1)S(1)}, bf16[200,384]{1,0:T(8,128)(2,1)S(1)}, u32[]{:S(2)}, u32[]{:S(2)}) collective-permute-start(bf16[200,384]{1,0:T(8,128)(2,1)S(1)} %get-tuple-element.106), channel_id=1, source_target_pairs={{0,6},{1,7},{2,4},{3,5},{4,2},{5,3},{6,0},{7,1},{8,14},{9,15},{10,... | collective-permute-start | bytes 460808 | tf_op jit(solution)/shard_map/ppermute | solution.py:81
  28.4 7.9 %collective-permute-start.7 = (bf16[200,384]{1,0:T(8,128)(2,1)S(1)}, bf16[200,384]{1,0:T(8,128)(2,1)S(1)}, u32[]{:S(2)}, u32[]{:S(2)}) collective-permute-start(bf16[200,384]{1,0:T(8,128)(2,1)S(1)} %get-tuple-element.107), channel_id=1, source_target_pairs={{0,2},{1,3},{2,0},{3,1},{4,6},{5,7},{6,4},{7,5},{8,10},{9,11},{10,... | collective-permute-start | bytes 460808 | tf_op jit(solution)/shard_map/ppermute | solution.py:81
  29.1 8.1 %collective-permute-start.8 = (bf16[200,384]{1,0:T(8,128)(2,1)S(1)}, bf16[200,384]{1,0:T(8,128)(2,1)S(1)}, u32[]{:S(2)}, u32[]{:S(2)}) collective-permute-start(bf16[200,384]{1,0:T(8,128)(2,1)S(1)} %get-tuple-element.108), channel_id=1, source_target_pairs={{0,4},{1,5},{2,6},{3,7},{4,0},{5,1},{6,2},{7,3},{8,12},{9,13},{10,... | collective-permute-start | bytes 460808 | tf_op jit(solution)/shard_map/ppermute | solution.py:81
  29.6 8.8 %collective-permute-start.9 = (bf16[128,384]{1,0:T(8,128)(2,1)S(1)}, bf16[128,384]{1,0:T(8,128)(2,1)S(1)}, u32[]{:S(2)}, u32[]{:S(2)}) collective-permute-start(bf16[128,384]{1,0:T(8,128)(2,1)S(1)} %get-tuple-element.76), channel_id=1, source_target_pairs={{0,4},{1,5},{2,6},{3,7},{4,0},{5,1},{6,2},{7,3},{8,12},{9,13},{10,... | collective-permute-start | bytes 294920 | tf_op jit(solution)/shard_map/ppermute | solution.py:81
  31.1 7.3 %collective-permute-start.10 = (bf16[128,384]{1,0:T(8,128)(2,1)S(1)}, bf16[128,384]{1,0:T(8,128)(2,1)S(1)}, u32[]{:S(2)}, u32[]{:S(2)}) collective-permute-start(bf16[128,384]{1,0:T(8,128)(2,1)S(1)} %get-tuple-element.77), channel_id=1, source_target_pairs={{1,0},{2,1},{3,2},{0,3},{5,4},{6,5},{7,6},{4,7},{9,8},{10,9},{11,1... | collective-permute-start | bytes 294920 | tf_op jit(solution)/shard_map/ppermute | solution.py:87
  38.5 5.9 %collective-permute-start.11 = (bf16[56,384]{1,0:T(8,128)(2,1)S(1)}, bf16[56,384]{1,0:T(8,128)(2,1)S(1)}, u32[]{:S(2)}, u32[]{:S(2)}) collective-permute-start(bf16[56,384]{1,0:T(8,128)(2,1)S(1)} %get-tuple-element.103), channel_id=1, source_target_pairs={{0,24},{1,25},{2,26},{3,27},{4,28},{5,29},{6,30},{7,31},{8,16},{9,... | collective-permute-start | bytes 129032 | tf_op jit(solution)/shard_map/ppermute | solution.py:81
  40.7 5.4 %collective-permute-start.12 = (bf16[56,384]{1,0:T(8,128)(2,1)S(1)}, bf16[56,384]{1,0:T(8,128)(2,1)S(1)}, u32[]{:S(2)}, u32[]{:S(2)}) collective-permute-start(bf16[56,384]{1,0:T(8,128)(2,1)S(1)} %get-tuple-element.104), channel_id=1, source_target_pairs={{0,16},{1,17},{2,18},{3,19},{4,20},{5,21},{6,22},{7,23},{8,24},{9,... | collective-permute-start | bytes 129032 | tf_op jit(solution)/shard_map/ppermute | solution.py:81
  40.8 5.2 %collective-permute-start.13 = (bf16[56,384]{1,0:T(8,128)(2,1)S(1)}, bf16[56,384]{1,0:T(8,128)(2,1)S(1)}, u32[]{:S(2)}, u32[]{:S(2)}) collective-permute-start(bf16[56,384]{1,0:T(8,128)(2,1)S(1)} %get-tuple-element.105), channel_id=1, source_target_pairs={{0,8},{1,9},{2,10},{3,11},{4,12},{5,13},{6,14},{7,15},{8,0},{9,1},... | collective-permute-start | bytes 129032 | tf_op jit(solution)/shard_map/ppermute | solution.py:81
  46.1 5.8 %collective-permute-start.16 = (bf16[48,384]{1,0:T(8,128)(2,1)S(1)}, bf16[48,384]{1,0:T(8,128)(2,1)S(1)}, u32[]{:S(2)}, u32[]{:S(2)}) collective-permute-start(bf16[48,384]{1,0:T(8,128)(2,1)S(1)} %add_convert_fusion), channel_id=1, source_target_pairs={{0,24},{1,25},{2,26},{3,27},{4,28},{5,29},{6,30},{7,31},{8,16},{9,... | collective-permute-start | bytes 110600 | tf_op jit(solution)/shard_map/ppermute | solution.py:81
  48.2 4.9 %collective-permute-start.15 = (bf16[48,384]{1,0:T(8,128)(2,1)S(1)}, bf16[48,384]{1,0:T(8,128)(2,1)S(1)}, u32[]{:S(2)}, u32[]{:S(2)}) collective-permute-start(bf16[48,384]{1,0:T(8,128)(2,1)S(1)} %add_convert_fusion), channel_id=1, source_target_pairs={{0,16},{1,17},{2,18},{3,19},{4,20},{5,21},{6,22},{7,23},{8,24},{9,... | collective-permute-start | bytes 110600 | tf_op jit(solution)/shard_map/ppermute | solution.py:81
  48.5 4.5 %collective-permute-start.14 = (bf16[48,384]{1,0:T(8,128)(2,1)S(1)}, bf16[48,384]{1,0:T(8,128)(2,1)S(1)}, u32[]{:S(2)}, u32[]{:S(2)}) collective-permute-start(bf16[48,384]{1,0:T(8,128)(2,1)S(1)} %add_convert_fusion), channel_id=1, source_target_pairs={{0,8},{1,9},{2,10},{3,11},{4,12},{5,13},{6,14},{7,15},{8,0},{9,1},... | collective-permute-start | bytes 110600 | tf_op jit(solution)/shard_map/ppermute | solution.py:81
  53.1 11.3 %collective-permute-start.22 = (bf16[192,384]{1,0:T(8,128)(2,1)S(1)}, bf16[192,384]{1,0:T(8,128)(2,1)S(1)}, u32[]{:S(2)}, u32[]{:S(2)}) collective-permute-start(bf16[192,384]{1,0:T(8,128)(2,1)S(1)} %pad_maximum_fusion.3.refs_0_), channel_id=1, source_target_pairs={{0,6},{1,7},{2,4},{3,5},{4,2},{5,3},{6,0},{7,1},{8,14},{9,15},{10,... | collective-permute-start | bytes 442376 | tf_op jit(solution)/shard_map/ppermute | solution.py:81
  54.7 9.7 %collective-permute-start.21 = (bf16[192,384]{1,0:T(8,128)(2,1)S(1)}, bf16[192,384]{1,0:T(8,128)(2,1)S(1)}, u32[]{:S(2)}, u32[]{:S(2)}) collective-permute-start(bf16[192,384]{1,0:T(8,128)(2,1)S(1)} %pad_maximum_fusion.3.refs_0_), channel_id=1, source_target_pairs={{0,2},{1,3},{2,0},{3,1},{4,6},{5,7},{6,4},{7,5},{8,10},{9,11},{10,... | collective-permute-start | bytes 442376 | tf_op jit(solution)/shard_map/ppermute | solution.py:81
  56.1 8.8 %collective-permute-start.20 = (bf16[192,384]{1,0:T(8,128)(2,1)S(1)}, bf16[192,384]{1,0:T(8,128)(2,1)S(1)}, u32[]{:S(2)}, u32[]{:S(2)}) collective-permute-start(bf16[192,384]{1,0:T(8,128)(2,1)S(1)} %pad_maximum_fusion.3.refs_0_), channel_id=1, source_target_pairs={{0,4},{1,5},{2,6},{3,7},{4,0},{5,1},{6,2},{7,3},{8,12},{9,13},{10,... | collective-permute-start | bytes 442376 | tf_op jit(solution)/shard_map/ppermute | solution.py:81
  56.7 6.0 %collective-permute-start.17 = (bf16[64,384]{1,0:T(8,128)(2,1)S(1)}, bf16[64,384]{1,0:T(8,128)(2,1)S(1)}, u32[]{:S(2)}, u32[]{:S(2)}) collective-permute-start(bf16[64,384]{1,0:T(8,128)(2,1)S(1)} %pad_maximum_fusion.10), channel_id=1, source_target_pairs={{0,24},{1,25},{2,26},{3,27},{4,28},{5,29},{6,30},{7,31},{8,16},{9,... | collective-permute-start | bytes 147464 | tf_op jit(solution)/shard_map/ppermute | solution.py:81
  58.7 5.5 %collective-permute-start.18 = (bf16[64,384]{1,0:T(8,128)(2,1)S(1)}, bf16[64,384]{1,0:T(8,128)(2,1)S(1)}, u32[]{:S(2)}, u32[]{:S(2)}) collective-permute-start(bf16[64,384]{1,0:T(8,128)(2,1)S(1)} %pad_maximum_fusion.11), channel_id=1, source_target_pairs={{0,16},{1,17},{2,18},{3,19},{4,20},{5,21},{6,22},{7,23},{8,24},{9,... | collective-permute-start | bytes 147464 | tf_op jit(solution)/shard_map/ppermute | solution.py:81
  62.6 6.7 %collective-permute-start.23 = (bf16[192,384]{1,0:T(8,128)(2,1)S(1)}, bf16[192,384]{1,0:T(8,128)(2,1)S(1)}, u32[]{:S(2)}, u32[]{:S(2)}) collective-permute-start(bf16[192,384]{1,0:T(8,128)(2,1)S(1)} %pad_maximum_fusion.3.refs_0_), channel_id=1, source_target_pairs={{0,1},{1,0},{2,3},{3,2},{4,5},{5,4},{6,7},{7,6},{8,9},{9,8},{10,11... | collective-permute-start | bytes 442376 | tf_op jit(solution)/shard_map/ppermute | solution.py:81
  64.2 4.1 %collective-permute-start.19 = (bf16[64,384]{1,0:T(8,128)(2,1)S(1)}, bf16[64,384]{1,0:T(8,128)(2,1)S(1)}, u32[]{:S(2)}, u32[]{:S(2)}) collective-permute-start(bf16[64,384]{1,0:T(8,128)(2,1)S(1)} %pad_maximum_fusion.12), channel_id=1, source_target_pairs={{0,8},{1,9},{2,10},{3,11},{4,12},{5,13},{6,14},{7,15},{8,0},{9,1},... | collective-permute-start | bytes 147464 | tf_op jit(solution)/shard_map/ppermute | solution.py:81
  64.4 4.9 %collective-permute-start.26 = (bf16[192,384]{1,0:T(8,128)(2,1)S(1)}, bf16[192,384]{1,0:T(8,128)(2,1)S(1)}, u32[]{:S(2)}, u32[]{:S(2)}) collective-permute-start(bf16[192,384]{1,0:T(8,128)(2,1)S(1)} %collective-permute-done.22.refs_3_), channel_id=1, source_target_pairs={{0,1},{1,0},{2,3},{3,2},{4,5},{5,4},{6,7},{7,6},{8,9},{9,8},{10,11... | collective-permute-start | bytes 442376 | tf_op jit(solution)/shard_map/ppermute | solution.py:81
  64.4 4.9 %collective-permute-start.25 = (bf16[192,384]{1,0:T(8,128)(2,1)S(1)}, bf16[192,384]{1,0:T(8,128)(2,1)S(1)}, u32[]{:S(2)}, u32[]{:S(2)}) collective-permute-start(bf16[192,384]{1,0:T(8,128)(2,1)S(1)} %collective-permute-done.21.refs_2_), channel_id=1, source_target_pairs={{0,1},{1,0},{2,3},{3,2},{4,5},{5,4},{6,7},{7,6},{8,9},{9,8},{10,11... | collective-permute-start | bytes 442376 | tf_op jit(solution)/shard_map/ppermute | solution.py:81
  64.9 4.4 %collective-permute-start.24 = (bf16[192,384]{1,0:T(8,128)(2,1)S(1)}, bf16[192,384]{1,0:T(8,128)(2,1)S(1)}, u32[]{:S(2)}, u32[]{:S(2)}) collective-permute-start(bf16[192,384]{1,0:T(8,128)(2,1)S(1)} %collective-permute-done.20.refs_1_), channel_id=1, source_target_pairs={{0,1},{1,0},{2,3},{3,2},{4,5},{5,4},{6,7},{7,6},{8,9},{9,8},{10,11... | collective-permute-start | bytes 442376 | tf_op jit(solution)/shard_map/ppermute | solution.py:81

commit v12 on v11

--- a/solution.py
+++ b/solution.py
@@ -45,9 +45,9 @@
 
 def exchange_plan():
     dom_size, rows_size = lax.axis_size("dom"), lax.axis_size("rows")
-    line, square = [(2, 0), (4, 0)], [(1, 0), (0, 2)]
-    rest = [(bit, 0) for bit in bits_of(dom_size, 8)] + [(0, bit) for bit in bits_of(rows_size, 4)]
-    return line, square, rest
+    pair, square = [(2, 0)], [(1, 0), (0, 2)]
+    rest = [(bit, 0) for bit in bits_of(dom_size, 4)] + [(0, bit) for bit in bits_of(rows_size, 4)]
+    return pair, square, rest
 
 
 def partner_masks(block):
@@ -63,9 +63,9 @@
 
 
 def own_digit():
-    line, square, _ = exchange_plan()
+    pair, square, _ = exchange_plan()
     digit = 0
-    for i, (dom_mask, rows_mask) in enumerate(line + square):
+    for i, (dom_mask, rows_mask) in enumerate(pair + square):
         own = (lax.axis_index("dom") & dom_mask) | (lax.axis_index("rows") & rows_mask)
         digit += jnp.where(own != 0, 1 << i, 0)
     return digit
@@ -364,8 +364,8 @@
 def weight_sums(core, out_ref, extt_ref, gqt_ref, gkvt_ref, ot_ref, og_ref, factor):
     width, row_count = gqt_ref.shape
     held = own_digit()
-    line, square, _ = exchange_plan()
-    rows = 2 * width >> len(line + square)
+    pair, square, _ = exchange_plan()
+    rows = 2 * width >> len(pair + square)
 
     def write(at, total):
         total = (total * factor).astype(out_ref.dtype)
@@ -387,11 +387,12 @@
 
 
 def finish_kernel(factor, og_ref, wq_ref, wkv_ref, extt_ref, gqt_ref, gkvt_ref, ot_ref, *refs):
-    gf_ref, halo_feat_ref, keep_ref, through_ref = refs[:4]
-    direct_refs = refs[4:]
+    gf_ref, halo_feat_ref, keep_ref = refs[:3]
+    pair_refs = refs[3:]
     width, row_count = gqt_ref.shape
     near = TILE + row_count
-    slots = 2 * through_ref.shape[0]
+    step = pair_refs[0].shape[0]
+    slots = step * len(pair_refs)
     weight_sums(
         lax.axis_index("rows") % 2, keep_ref, extt_ref, gqt_ref, gkvt_ref, ot_ref, og_ref, factor
     )
@@ -399,14 +400,16 @@
     own = by_feature[:, TILE:near] + f32_dot(wq_ref[...], gqt_ref[...])
     gf_ref[...] = own.T
     halo_feat_ref[...] = rounded(by_feature[:, :TILE].T)
-    store_blocks(rounded(by_feature[:, near:].T), through_ref, direct_refs)
+    slot_feat = rounded(by_feature[:, near:].T)
+    for at, out_ref in enumerate(pair_refs):
+        out_ref[...] = slot_feat[at * step : (at + 1) * step]
 
 
 def place_kernel(*refs):
     part_refs, (gq_hbm, gkv_hbm, go_hbm, all_ref, out_ref, sems) = refs[:-6], refs[-6:]
     width = gq_hbm.shape[0]
-    line, square, _ = exchange_plan()
-    half = 1 << len(line + square)
+    pair, square, _ = exchange_plan()
+    half = 1 << len(pair + square)
     rows = 2 * width // half
     step = part_refs[0].shape[0]
     for at, part_ref in enumerate(part_refs):
@@ -432,16 +435,15 @@
         copy.wait()
 
 
-def return_kernel(gf_ref, chosen_ref, halo_ref, *refs):
-    piece_refs, out_ref = refs[:-1], refs[-1]
+def return_kernel(gf_ref, chosen_ref, halo_ref, own_ref, through_ref, *refs):
+    far_refs, out_ref = refs[:-1], refs[-1]
     row_count = gf_ref.shape[0]
     tile = halo_ref.shape[0]
-    per_peer = piece_refs[0].shape[0]
-    returned = jnp.concatenate(
-        [piece_refs[0][...], piece_refs[1][:per_peer]] + [ref[...] for ref in piece_refs[:1:-1]],
-        axis=0,
-    )
-    total = gf_ref[...] + rows_contracted(chosen_ref[...], returned)
+    per_peer = own_ref.shape[0] // 2
+    returned = []
+    for at, even_ref in enumerate([own_ref, *far_refs[::-1]]):
+        returned += [even_ref[:per_peer], through_ref[at * per_peer : (at + 1) * per_peer]]
+    total = gf_ref[...] + rows_contracted(chosen_ref[...], jnp.concatenate(returned, axis=0))
     out_ref[: row_count - tile] = total[: row_count - tile]
     out_ref[row_count - tile :] = total[row_count - tile :] + halo_ref[...].astype(jnp.float32)
 
@@ -477,7 +479,7 @@
     padded = ROW_PACK * -(-virt_rows // ROW_PACK)
     ext_rows = TILE + row_count + slots + padded
     nodes = row_count * lax.axis_size("dom") * lax.axis_size("rows")
-    line, square, rest = exchange_plan()
+    pair, square, rest = exchange_plan()
     bf16, f32 = jnp.bfloat16, jnp.float32
     shape = jax.ShapeDtypeStruct
 
@@ -541,45 +543,38 @@
         flops=28 * ext_rows * width * width,
     )
     message = swapped(message, *CORES)
-    own_feat, halo_feat, keep, through, *direct = call(
+    own_feat, halo_feat, keep, *pairs = call(
         functools.partial(finish_kernel, nodes**-0.5),
         "finish",
-        [
-            shape((row_count, width), f32),
-            shape((TILE, width), bf16),
-            shape((2 * width, width), f32),
-            shape((slots // 2, width), bf16),
-        ]
-        + [shape((per_peer, width), bf16)] * (dom_size // 2),
+        [shape((row_count, width), f32), shape((TILE, width), bf16), shape((2 * width, width), f32)]
+        + [shape((2 * per_peer, width), bf16)] * (dom_size // 2),
         [*prepared[:3], *gradients],
         flops=6 * ext_rows * width * width,
     )
 
     keep, rider = added(keep, rounded(rider).astype(f32), {1: message})
     rider = rider[: -(-virt_rows // 8) * 8]
-    through, halo_feat, _ = lax.optimization_barrier((through, halo_feat, keep))
-    through = swapped(through, 1, 0)
+    pairs, _ = lax.optimization_barrier((pairs, keep))
+    returned = [swapped(pairs[at], 2 * at, 0) for at in reversed(range(1, dom_size // 2))]
+    keep, rider = scattered(keep, rider, square)
+    (returned, halo_feat), _ = lax.optimization_barrier(((returned, halo_feat), keep))
+    through = swapped(jnp.concatenate([x[per_peer:] for x in [pairs[0]] + returned[::-1]]), 1, 0)
     halo_back = shifted(halo_feat, "rows", -1)
-    keep, rider = scattered(keep, rider, square)
-    keep, through, halo_back = lax.optimization_barrier((keep, through, halo_back))
-    keep, rider = scattered(keep, rider, line)
+    keep, rider = scattered(keep, rider, pair)
     for mask in rest:
         message = swapped(with_rider(keep, rider), *mask)
         keep, rider = rounded(keep).astype(f32), rounded(rider).astype(f32)
         keep, rider = added(keep, rider, {1: message})
-
-    held = rounded(keep)
-    back = {at: swapped(held, *partner_masks(line)[at]) for at in (3, 2, 1)}
-    held = jnp.concatenate([held] + [back[at] for at in sorted(back)], axis=0)
-    through, _ = lax.optimization_barrier((through, held))
-    returned = handed_on(direct, through)
-    arrived = [swapped(held, *masks) for masks in partner_masks(square)[1:]]
     (grad_features,) = call(
         return_kernel,
         "return_rows",
         [shape((row_count, width), f32)],
-        [own_feat, chosen, halo_back, *returned],
-    )
+        [own_feat, chosen, halo_back, pairs[0], through, *returned],
+    )
+
+    held, grad_features = lax.optimization_barrier((rounded(keep), grad_features))
+    held = jnp.concatenate([held, swapped(held, *pair[0])], axis=0)
+    arrived = [swapped(held, *masks) for masks in partner_masks(square)[1:]]
     near = [held, *arrived]
     far = [swapped(part, *CORES) for part in near]
     grad_wq, grad_wkv, grad_wo = call(
@@ -590,7 +585,7 @@
         [
             pltpu.VMEM((4 * width, width), bf16),
             pltpu.VMEM((4 * width, width), f32),
-            pltpu.SemaphoreType.DMA((2 << len(line + square),)),
+            pltpu.SemaphoreType.DMA((2 << len(pair + square),)),
         ],
         stored=True,
     )

time: 71.4 us -> 64.4 us (0.902)
  starting transfers between devices: 29 us -> 21.3 us
  waiting for transfers between devices: 25 us -> 25.8 us
    ppermute x25 -> x22, starting transfers between devices: 28.9 us -> 21.2 us  [swapped(): return lax.ppermute(block, ('dom', 'rows'), route)]
    ppermute x25 -> x22, waiting for transfers between devices: 25 us -> 25.8 us  [swapped(): return lax.ppermute(block, ('dom', 'rows'), route)]
  transfers between devices with their start and end apart: 27 -> 24, of which waited for: 14 -> 15; matrix products, arithmetic and copies ran while one was open for 1% -> 1% of each run, Pallas kernels for 8% -> 8%
where the time goes in v12:
time: 64.4 us; the launch traced here: 64.1 us
  waiting for transfers between devices  25.8 us (40%)
  starting transfers between devices  21.3 us (33%)
  Pallas kernels  15.1 us (23%)
  other arithmetic  0.98 us (2%)
  between operations  0.85 us (1%)
    ppermute x22, waiting for transfers between devices, swapped(): return lax.ppermute(block, ('dom', 'rows'), route)  25.8 us
    ppermute x22, starting transfers between devices, swapped(): return lax.ppermute(block, ('dom', 'rows'), route)  21.2 us
    pallas_call x6, Pallas kernels, call(): pl.pallas_call(kernel, out_shape=outs, in_specs=[pl.BlockSpec(memory_spac...  15.1 us
  transfers between devices with their start and end apart: 24, of which 15 were waited for; matrix products, arithmetic and copies ran while one was open for 1% of the time, Pallas kernels for 8%

profile of v12, /device:TPU:0, one launch (start us, length us, event | category | flops | bytes accessed | tf_op | source)
XLA Modules:
  0.0 64.1 jit_solution(4250865488395583853)
XLA Ops:
  0.6 1.2 %pick_rows.1 = (bf16[128,384]{1,0:T(8,128)(2,1)S(1)}, bf16[256,256]{1,0:T(8,128)(2,1)S(1)}, bf16[128,384]{1,0:T(8,128)(2,1)S(1)}, bf16[32,384]{1,0:T(8,128)(2,1)...) custom-call(bf16[256,384]{1,0:T(8,128)(2,1)} %feat_hbm.3, ...), custom_call_target="tpu_custom_call" | custom-call | bytes 623616 | tf_op jit(solution)/shard_map/pick_rows/pallas_call | solution.py:462
  1.9 3.0 %collective-permute-start = (bf16[128,384]{1,0:T(8,128)(2,1)S(1)}, bf16[128,384]{1,0:T(8,128)(2,1)S(1)}, u32[]{:S(2)}, u32[]{:S(2)}) collective-permute-start(bf16[128,384]{1,0:T(8,128)(2,1)S(1)} %get-tuple-element.54), channel_id=1, source_target_pairs={{0,4},{1,5},{2,6},{3,7},{4,0},{5,1},{6,2},{7,3},{8,12},{9,13},{10,... | collective-permute-start | bytes 294920 | tf_op jit(solution)/shard_map/ppermute | solution.py:81
  4.9 2.9 %prepare.1 = (bf16[256,384]{1,0:T(8,128)(2,1)S(1)}, bf16[384,384]{1,0:T(8,128)(2,1)S(1)}, bf16[384,768]{1,0:T(8,128)(2,1)S(1)}, bf16[384,272]{1,0:T(8,128)(2,1)S...) custom-call(bf16[256,384]{1,0:T(8,128)(2,1)} %feat_hbm.3, ...), custom_call_target="tpu_custom_call" | custom-call | flops 377487360 | bytes 4656128 | tf_op jit(solution)/shard_map/prepare/pallas_call | solution.py:462
  7.8 3.9 %collective-permute-start.1 = (bf16[64,384]{1,0:T(8,128)(2,1)S(1)}, bf16[64,384]{1,0:T(8,128)(2,1)S(1)}, u32[]{:S(2)}, u32[]{:S(2)}) collective-permute-start(bf16[64,384]{1,0:T(8,128)(2,1)S(1)} %pad_maximum_fusion.6), channel_id=1, source_target_pairs={{0,24},{1,25},{2,26},{3,27},{4,28},{5,29},{6,30},{7,31},{8,16},{9,... | collective-permute-start | bytes 147464 | tf_op jit(solution)/shard_map/ppermute | solution.py:81
  11.7 0.1 collective-permute-start.4
  11.8 0.6 collective-permute-start.3
  12.4 1.9 %collective-permute-done.1.refs_2_ = bf16[64,384]{1,0:T(8,128)(2,1)S(1)} collective-permute-done((bf16[64,384]{1,0:T(8,128)(2,1)S(1)}, bf16[64,384]{1,0:T(8,128)(2,1)S(1)}, u32[]{:S(2)}, u32[]{:S(2)}) %collective-permute-start.1) | collective-permute-done | bytes 49184 | tf_op jit(solution)/shard_map/ppermute | solution.py:81
  14.3 2.5 %collective-permute-done.2.refs_3_ = bf16[64,384]{1,0:T(8,128)(2,1)S(1)} collective-permute-done((bf16[64,384]{1,0:T(8,128)(2,1)S(1)}, bf16[64,384]{1,0:T(8,128)(2,1)S(1)}, u32[]{:S(2)}, u32[]{:S(2)}) %collective-permute-start.2) | collective-permute-done | bytes 49184 | tf_op jit(solution)/shard_map/ppermute | solution.py:81
  16.8 0.0 collective-permute-done.3.refs_4_
  16.8 0.0 collective-permute-done.4.refs_5_
  16.8 6.9 %attend.1 = (bf16[784,384]{1,0:T(8,128)(2,1)S(1)}, f32[16,384]{1,0:T(8,128)S(1)}, bf16[384,656]{1,0:T(8,128)(2,1)S(1)}, bf16[384,256]{1,0:T(8,128)(2,1)S(1)}, bf...) custom-call(bf16[32,384]{1,0:T(8,128)(2,1)S(1)} %get-tuple-element.53.refs_0_, ...), custom_call_target="tpu_custom_call" | custom-call | flops 2708471808 | bytes 5959680 | tf_op jit(solution)/shard_map/attend/pallas_call | solution.py:462
  23.7 0.1 collective-permute-start.5
  23.7 1.5 %finish.1 = (f32[256,384]{1,0:T(8,128)S(1)}, bf16[128,384]{1,0:T(8,128)(2,1)S(1)}, f32[768,384]{1,0:T(8,128)S(1)}, bf16[64,384]{1,0:T(8,128)(2,1)S(1)}, bf16[64,...) custom-call(bf16[256,384]{1,0:T(8,128)(2,1)S(1)} %get-tuple-element.50.refs_6_.og_ref, ...), custom_call_target="tpu_custom_call" | custom-call | flops 580386816 | bytes 4853760 | tf_op jit(solution)/shard_map/finish/pallas_call | solution.py:462
  25.2 0.5 collective-permute-done.5
  25.7 0.1 fusion.3
  26.0 2.4 %collective-permute-start.6 = (bf16[200,384]{1,0:T(8,128)(2,1)S(1)}, bf16[200,384]{1,0:T(8,128)(2,1)S(1)}, u32[]{:S(2)}, u32[]{:S(2)}) collective-permute-start(bf16[200,384]{1,0:T(8,128)(2,1)S(1)} %get-tuple-element.103), channel_id=1, source_target_pairs={{0,6},{1,7},{2,4},{3,5},{4,2},{5,3},{6,0},{7,1},{8,14},{9,15},{10,... | collective-permute-start | bytes 460808 | tf_op jit(solution)/shard_map/ppermute | solution.py:81
  28.4 0.6 collective-permute-start.7
  29.0 0.5 collective-permute-start.8
  29.6 1.7 %collective-permute-start.11 = (bf16[64,384]{1,0:T(8,128)(2,1)S(1)}, bf16[64,384]{1,0:T(8,128)(2,1)S(1)}, u32[]{:S(2)}, u32[]{:S(2)}) collective-permute-start(bf16[64,384]{1,0:T(8,128)(2,1)S(1)} %get-tuple-element.81), channel_id=1, source_target_pairs={{0,24},{1,25},{2,26},{3,27},{4,28},{5,29},{6,30},{7,31},{8,16},{9,... | collective-permute-start | bytes 147464 | tf_op jit(solution)/shard_map/ppermute | solution.py:81
  31.3 0.3 collective-permute-start.12
  31.6 2.2 %collective-permute-done.6 = bf16[200,384]{1,0:T(8,128)(2,1)S(1)} collective-permute-done((bf16[200,384]{1,0:T(8,128)(2,1)S(1)}, bf16[200,384]{1,0:T(8,128)(2,1)S(1)}, u32[]{:S(2)}, u32[]{:S(2)}) %collective-permute-start.6) | collective-permute-done | bytes 153632 | tf_op jit(solution)/shard_map/ppermute | solution.py:81
  33.8 0.2 collective-permute-start.13
  34.0 2.3 %collective-permute-done.7 = bf16[200,384]{1,0:T(8,128)(2,1)S(1)} collective-permute-done((bf16[200,384]{1,0:T(8,128)(2,1)S(1)}, bf16[200,384]{1,0:T(8,128)(2,1)S(1)}, u32[]{:S(2)}, u32[]{:S(2)}) %collective-permute-start.7) | collective-permute-done | bytes 153632 | tf_op jit(solution)/shard_map/ppermute | solution.py:81
  36.3 0.1 fusion.1
  36.4 0.4 collective-permute-done.12.refs_1_
  36.8 1.1 %collective-permute-done.13.refs_2_ = bf16[64,384]{1,0:T(8,128)(2,1)S(1)} collective-permute-done((bf16[64,384]{1,0:T(8,128)(2,1)S(1)}, bf16[64,384]{1,0:T(8,128)(2,1)S(1)}, u32[]{:S(2)}, u32[]{:S(2)}) %collective-permute-start.13) | collective-permute-done | bytes 49184 | tf_op jit(solution)/shard_map/ppermute | solution.py:81
  38.0 0.2 collective-permute-start.9
  38.2 1.6 %collective-permute-start.15 = (bf16[128,384]{1,0:T(8,128)(2,1)S(1)}, bf16[128,384]{1,0:T(8,128)(2,1)S(1)}, u32[]{:S(2)}, u32[]{:S(2)}) collective-permute-start(bf16[128,384]{1,0:T(8,128)(2,1)S(1)} %pad_maximum_fusion.3), channel_id=1, source_target_pairs={{0,4},{1,5},{2,6},{3,7},{4,0},{5,1},{6,2},{7,3},{8,12},{9,13},{10,... | collective-permute-start | bytes 294920 | tf_op jit(solution)/shard_map/ppermute | solution.py:81
  39.8 2.7 %collective-permute-done.9 = bf16[104,384]{1,0:T(8,128)(2,1)S(1)} collective-permute-done((bf16[104,384]{1,0:T(8,128)(2,1)S(1)}, bf16[104,384]{1,0:T(8,128)(2,1)S(1)}, u32[]{:S(2)}, u32[]{:S(2)}) %collective-permute-start.9) | collective-permute-done | bytes 79904 | tf_op jit(solution)/shard_map/ppermute | solution.py:81
  42.5 2.0 %collective-permute-start.10 = (bf16[104,384]{1,0:T(8,128)(2,1)S(1)}, bf16[104,384]{1,0:T(8,128)(2,1)S(1)}, u32[]{:S(2)}, u32[]{:S(2)}) collective-permute-start(bf16[104,384]{1,0:T(8,128)(2,1)S(1)} %pad_maximum_fusion.5), channel_id=1, source_target_pairs={{0,16},{1,17},{2,18},{3,19},{4,20},{5,21},{6,22},{7,23},{8,24},{9,... | collective-permute-start | bytes 239624 | tf_op jit(solution)/shard_map/ppermute | solution.py:81
  44.5 0.0 collective-permute-done.15.through_ref
  44.5 0.0 collective-permute-done.14.halo_ref
  44.5 1.0 %return_rows.1 = f32[256,384]{1,0:T(8,128)} custom-call(f32[256,384]{1,0:T(8,128)S(1)} %get-tuple-element.75.gf_ref, bf16[256,256]{1,0:T(8,128)(2,1)S(1)} %get-tuple-element.76.chosen_ref, bf16[128,384]{1,0:T(8,128)(2,1)S(1)} %collective-permute-done.14.halo_ref, bf16[64,384]{1,0:T(8,128)(2,1)S(1)} %get-tuple-element.86.own_ref, ...), custom_call_target="tpu_custom_call" | custom-call | bytes 1310720 | tf_op jit(solution)/shard_map/return_rows/pallas_call | solution.py:462
  45.6 2.8 %collective-permute-done.10 = bf16[104,384]{1,0:T(8,128)(2,1)S(1)} collective-permute-done((bf16[104,384]{1,0:T(8,128)(2,1)S(1)}, bf16[104,384]{1,0:T(8,128)(2,1)S(1)}, u32[]{:S(2)}, u32[]{:S(2)}) %collective-permute-start.10) | collective-permute-done | bytes 79904 | tf_op jit(solution)/shard_map/ppermute | solution.py:81
  48.4 0.1 collective-permute-start.16
  48.5 4.3 %collective-permute-done.16 = bf16[96,384]{1,0:T(8,128)(2,1)S(1)} collective-permute-done((bf16[96,384]{1,0:T(8,128)(2,1)S(1)}, bf16[96,384]{1,0:T(8,128)(2,1)S(1)}, u32[]{:S(2)}, u32[]{:S(2)}) %collective-permute-start.16) | collective-permute-done | bytes 73760 | tf_op jit(solution)/shard_map/ppermute | solution.py:81
  52.8 2.9 %collective-permute-start.19 = (bf16[192,384]{1,0:T(8,128)(2,1)S(1)}, bf16[192,384]{1,0:T(8,128)(2,1)S(1)}, u32[]{:S(2)}, u32[]{:S(2)}) collective-permute-start(bf16[192,384]{1,0:T(8,128)(2,1)S(1)} %constant_dynamic-update-slice_fusion.refs_0_), channel_id=1, source_target_pairs={{0,6},{1,7},{2,4},{3,5},{4,2},{5,3},{6,0},{7,1},{8,14},{9,15},{10,... | collective-permute-start | bytes 442376 | tf_op jit(solution)/shard_map/ppermute | solution.py:81
  55.7 0.1 collective-permute-start.18
  55.8 0.6 collective-permute-start.17
  56.4 0.0 collective-permute-start.20
  56.4 2.5 %collective-permute-done.19.refs_3_ = bf16[192,384]{1,0:T(8,128)(2,1)S(1)} collective-permute-done((bf16[192,384]{1,0:T(8,128)(2,1)S(1)}, bf16[192,384]{1,0:T(8,128)(2,1)S(1)}, u32[]{:S(2)}, u32[]{:S(2)}) %collective-permute-start.19) | collective-permute-done | bytes 147488 | tf_op jit(solution)/shard_map/ppermute | solution.py:81
  59.0 1.9 %collective-permute-done.18.refs_2_ = bf16[192,384]{1,0:T(8,128)(2,1)S(1)} collective-permute-done((bf16[192,384]{1,0:T(8,128)(2,1)S(1)}, bf16[192,384]{1,0:T(8,128)(2,1)S(1)}, u32[]{:S(2)}, u32[]{:S(2)}) %collective-permute-start.18) | collective-permute-done | bytes 147488 | tf_op jit(solution)/shard_map/ppermute | solution.py:81
  60.9 0.1 collective-permute-done.17.refs_1_
  61.0 0.4 collective-permute-start.21
  61.4 0.6 convert_add_fusion.1
  62.0 0.3 collective-permute-done.22.refs_6_
  62.3 0.2 collective-permute-done.21.refs_5_
  62.5 1.6 %place_sums.1 = (f32[384,384]{1,0:T(8,128)}, f32[384,768]{1,0:T(8,128)}, f32[384,384]{1,0:T(8,128)}) custom-call(bf16[192,384]{1,0:T(8,128)(2,1)S(1)} %constant_dynamic-update-slice_fusion.refs_0_, bf16[192,384]{1,0:T(8,128)(2,1)S(1)} %collective-permute-done.17.refs_1_, bf16[192,384]{1,0:T(8,128)(2,1)S(1)} %collective-permute-done.18.refs_2_, ...), custom_call_target="tpu_custom_call" | custom-call | bytes 3538944 | tf_op jit(solution)/shard_map/place_sums/pallas_call | solution.py:462
  (32 shorter events, 0.3 us)
Async XLA Ops:
  1.9 5.9 %collective-permute-start = (bf16[128,384]{1,0:T(8,128)(2,1)S(1)}, bf16[128,384]{1,0:T(8,128)(2,1)S(1)}, u32[]{:S(2)}, u32[]{:S(2)}) collective-permute-start(bf16[128,384]{1,0:T(8,128)(2,1)S(1)} %get-tuple-element.54), channel_id=1, source_target_pairs={{0,4},{1,5},{2,6},{3,7},{4,0},{5,1},{6,2},{7,3},{8,12},{9,13},{10,... | collective-permute-start | bytes 294920 | tf_op jit(solution)/shard_map/ppermute | solution.py:81
  7.8 6.5 %collective-permute-start.1 = (bf16[64,384]{1,0:T(8,128)(2,1)S(1)}, bf16[64,384]{1,0:T(8,128)(2,1)S(1)}, u32[]{:S(2)}, u32[]{:S(2)}) collective-permute-start(bf16[64,384]{1,0:T(8,128)(2,1)S(1)} %pad_maximum_fusion.6), channel_id=1, source_target_pairs={{0,24},{1,25},{2,26},{3,27},{4,28},{5,29},{6,30},{7,31},{8,16},{9,... | collective-permute-start | bytes 147464 | tf_op jit(solution)/shard_map/ppermute | solution.py:81
  11.7 5.1 %collective-permute-start.2 = (bf16[64,384]{1,0:T(8,128)(2,1)S(1)}, bf16[64,384]{1,0:T(8,128)(2,1)S(1)}, u32[]{:S(2)}, u32[]{:S(2)}) collective-permute-start(bf16[64,384]{1,0:T(8,128)(2,1)S(1)} %pad_maximum_fusion.7), channel_id=1, source_target_pairs={{0,16},{1,17},{2,18},{3,19},{4,20},{5,21},{6,22},{7,23},{8,24},{9,... | collective-permute-start | bytes 147464 | tf_op jit(solution)/shard_map/ppermute | solution.py:81
  11.7 5.1 %collective-permute-start.4 = (bf16[128,384]{1,0:T(8,128)(2,1)S(1)}, bf16[128,384]{1,0:T(8,128)(2,1)S(1)}, u32[]{:S(2)}, u32[]{:S(2)}) collective-permute-start(bf16[128,384]{1,0:T(8,128)(2,1)S(1)} %get-tuple-element.60), channel_id=1, source_target_pairs={{3,0},{0,1},{1,2},{2,3},{7,4},{4,5},{5,6},{6,7},{11,8},{8,9},{9,10... | collective-permute-start | bytes 294920 | tf_op jit(solution)/shard_map/ppermute | solution.py:87
  11.8 5.0 %collective-permute-start.3 = (bf16[64,384]{1,0:T(8,128)(2,1)S(1)}, bf16[64,384]{1,0:T(8,128)(2,1)S(1)}, u32[]{:S(2)}, u32[]{:S(2)}) collective-permute-start(bf16[64,384]{1,0:T(8,128)(2,1)S(1)} %pad_maximum_fusion.8), channel_id=1, source_target_pairs={{0,8},{1,9},{2,10},{3,11},{4,12},{5,13},{6,14},{7,15},{8,0},{9,1},... | collective-permute-start | bytes 147464 | tf_op jit(solution)/shard_map/ppermute | solution.py:81
  23.7 2.1 %collective-permute-start.5 = (bf16[784,384]{1,0:T(8,128)(2,1)S(1)}, bf16[784,384]{1,0:T(8,128)(2,1)S(1)}, u32[]{:S(2)}, u32[]{:S(2)}) collective-permute-start(bf16[784,384]{1,0:T(8,128)(2,1)S(1)} %get-tuple-element.73), channel_id=1, source_target_pairs={{0,1},{1,0},{2,3},{3,2},{4,5},{5,4},{6,7},{7,6},{8,9},{9,8},{10,11... | collective-permute-start | bytes 1806344 | tf_op jit(solution)/shard_map/ppermute | solution.py:81
  26.0 7.8 %collective-permute-start.6 = (bf16[200,384]{1,0:T(8,128)(2,1)S(1)}, bf16[200,384]{1,0:T(8,128)(2,1)S(1)}, u32[]{:S(2)}, u32[]{:S(2)}) collective-permute-start(bf16[200,384]{1,0:T(8,128)(2,1)S(1)} %get-tuple-element.103), channel_id=1, source_target_pairs={{0,6},{1,7},{2,4},{3,5},{4,2},{5,3},{6,0},{7,1},{8,14},{9,15},{10,... | collective-permute-start | bytes 460808 | tf_op jit(solution)/shard_map/ppermute | solution.py:81
  28.4 7.9 %collective-permute-start.7 = (bf16[200,384]{1,0:T(8,128)(2,1)S(1)}, bf16[200,384]{1,0:T(8,128)(2,1)S(1)}, u32[]{:S(2)}, u32[]{:S(2)}) collective-permute-start(bf16[200,384]{1,0:T(8,128)(2,1)S(1)} %get-tuple-element.104), channel_id=1, source_target_pairs={{0,2},{1,3},{2,0},{3,1},{4,6},{5,7},{6,4},{7,5},{8,10},{9,11},{10,... | collective-permute-start | bytes 460808 | tf_op jit(solution)/shard_map/ppermute | solution.py:81
  29.0 7.3 %collective-permute-start.8 = (bf16[200,384]{1,0:T(8,128)(2,1)S(1)}, bf16[200,384]{1,0:T(8,128)(2,1)S(1)}, u32[]{:S(2)}, u32[]{:S(2)}) collective-permute-start(bf16[200,384]{1,0:T(8,128)(2,1)S(1)} %get-tuple-element.105), channel_id=1, source_target_pairs={{0,4},{1,5},{2,6},{3,7},{4,0},{5,1},{6,2},{7,3},{8,12},{9,13},{10,... | collective-permute-start | bytes 460808 | tf_op jit(solution)/shard_map/ppermute | solution.py:81
  29.6 6.8 %collective-permute-start.11 = (bf16[64,384]{1,0:T(8,128)(2,1)S(1)}, bf16[64,384]{1,0:T(8,128)(2,1)S(1)}, u32[]{:S(2)}, u32[]{:S(2)}) collective-permute-start(bf16[64,384]{1,0:T(8,128)(2,1)S(1)} %get-tuple-element.81), channel_id=1, source_target_pairs={{0,24},{1,25},{2,26},{3,27},{4,28},{5,29},{6,30},{7,31},{8,16},{9,... | collective-permute-start | bytes 147464 | tf_op jit(solution)/shard_map/ppermute | solution.py:81
  31.3 5.5 %collective-permute-start.12 = (bf16[64,384]{1,0:T(8,128)(2,1)S(1)}, bf16[64,384]{1,0:T(8,128)(2,1)S(1)}, u32[]{:S(2)}, u32[]{:S(2)}) collective-permute-start(bf16[64,384]{1,0:T(8,128)(2,1)S(1)} %get-tuple-element.82), channel_id=1, source_target_pairs={{0,16},{1,17},{2,18},{3,19},{4,20},{5,21},{6,22},{7,23},{8,24},{9,... | collective-permute-start | bytes 147464 | tf_op jit(solution)/shard_map/ppermute | solution.py:81
  33.8 4.1 %collective-permute-start.13 = (bf16[64,384]{1,0:T(8,128)(2,1)S(1)}, bf16[64,384]{1,0:T(8,128)(2,1)S(1)}, u32[]{:S(2)}, u32[]{:S(2)}) collective-permute-start(bf16[64,384]{1,0:T(8,128)(2,1)S(1)} %get-tuple-element.83), channel_id=1, source_target_pairs={{0,8},{1,9},{2,10},{3,11},{4,12},{5,13},{6,14},{7,15},{8,0},{9,1},... | collective-permute-start | bytes 147464 | tf_op jit(solution)/shard_map/ppermute | solution.py:81
  38.0 4.5 %collective-permute-start.9 = (bf16[104,384]{1,0:T(8,128)(2,1)S(1)}, bf16[104,384]{1,0:T(8,128)(2,1)S(1)}, u32[]{:S(2)}, u32[]{:S(2)}) collective-permute-start(bf16[104,384]{1,0:T(8,128)(2,1)S(1)} %pad_maximum_fusion.4), channel_id=1, source_target_pairs={{0,8},{1,9},{2,10},{3,11},{4,12},{5,13},{6,14},{7,15},{8,0},{9,1},... | collective-permute-start | bytes 239624 | tf_op jit(solution)/shard_map/ppermute | solution.py:81
  38.2 6.3 %collective-permute-start.15 = (bf16[128,384]{1,0:T(8,128)(2,1)S(1)}, bf16[128,384]{1,0:T(8,128)(2,1)S(1)}, u32[]{:S(2)}, u32[]{:S(2)}) collective-permute-start(bf16[128,384]{1,0:T(8,128)(2,1)S(1)} %pad_maximum_fusion.3), channel_id=1, source_target_pairs={{0,4},{1,5},{2,6},{3,7},{4,0},{5,1},{6,2},{7,3},{8,12},{9,13},{10,... | collective-permute-start | bytes 294920 | tf_op jit(solution)/shard_map/ppermute | solution.py:81
  39.8 4.8 %collective-permute-start.14 = (bf16[128,384]{1,0:T(8,128)(2,1)S(1)}, bf16[128,384]{1,0:T(8,128)(2,1)S(1)}, u32[]{:S(2)}, u32[]{:S(2)}) collective-permute-start(bf16[128,384]{1,0:T(8,128)(2,1)S(1)} %get-tuple-element.85), channel_id=1, source_target_pairs={{1,0},{2,1},{3,2},{0,3},{5,4},{6,5},{7,6},{4,7},{9,8},{10,9},{11,1... | collective-permute-start | bytes 294920 | tf_op jit(solution)/shard_map/ppermute | solution.py:87
  42.5 5.9 %collective-permute-start.10 = (bf16[104,384]{1,0:T(8,128)(2,1)S(1)}, bf16[104,384]{1,0:T(8,128)(2,1)S(1)}, u32[]{:S(2)}, u32[]{:S(2)}) collective-permute-start(bf16[104,384]{1,0:T(8,128)(2,1)S(1)} %pad_maximum_fusion.5), channel_id=1, source_target_pairs={{0,16},{1,17},{2,18},{3,19},{4,20},{5,21},{6,22},{7,23},{8,24},{9,... | collective-permute-start | bytes 239624 | tf_op jit(solution)/shard_map/ppermute | solution.py:81
  48.4 4.4 %collective-permute-start.16 = (bf16[96,384]{1,0:T(8,128)(2,1)S(1)}, bf16[96,384]{1,0:T(8,128)(2,1)S(1)}, u32[]{:S(2)}, u32[]{:S(2)}) collective-permute-start(bf16[96,384]{1,0:T(8,128)(2,1)S(1)} %add_convert_fusion), channel_id=1, source_target_pairs={{0,8},{1,9},{2,10},{3,11},{4,12},{5,13},{6,14},{7,15},{8,0},{9,1},... | collective-permute-start | bytes 221192 | tf_op jit(solution)/shard_map/ppermute | solution.py:81
  52.8 6.1 %collective-permute-start.19 = (bf16[192,384]{1,0:T(8,128)(2,1)S(1)}, bf16[192,384]{1,0:T(8,128)(2,1)S(1)}, u32[]{:S(2)}, u32[]{:S(2)}) collective-permute-start(bf16[192,384]{1,0:T(8,128)(2,1)S(1)} %constant_dynamic-update-slice_fusion.refs_0_), channel_id=1, source_target_pairs={{0,6},{1,7},{2,4},{3,5},{4,2},{5,3},{6,0},{7,1},{8,14},{9,15},{10,... | collective-permute-start | bytes 442376 | tf_op jit(solution)/shard_map/ppermute | solution.py:81
  55.7 5.1 %collective-permute-start.18 = (bf16[192,384]{1,0:T(8,128)(2,1)S(1)}, bf16[192,384]{1,0:T(8,128)(2,1)S(1)}, u32[]{:S(2)}, u32[]{:S(2)}) collective-permute-start(bf16[192,384]{1,0:T(8,128)(2,1)S(1)} %constant_dynamic-update-slice_fusion.refs_0_), channel_id=1, source_target_pairs={{0,2},{1,3},{2,0},{3,1},{4,6},{5,7},{6,4},{7,5},{8,10},{9,11},{10,... | collective-permute-start | bytes 442376 | tf_op jit(solution)/shard_map/ppermute | solution.py:81
  55.8 5.1 %collective-permute-start.17 = (bf16[192,384]{1,0:T(8,128)(2,1)S(1)}, bf16[192,384]{1,0:T(8,128)(2,1)S(1)}, u32[]{:S(2)}, u32[]{:S(2)}) collective-permute-start(bf16[192,384]{1,0:T(8,128)(2,1)S(1)} %constant_dynamic-update-slice_fusion.refs_0_), channel_id=1, source_target_pairs={{0,4},{1,5},{2,6},{3,7},{4,0},{5,1},{6,2},{7,3},{8,12},{9,13},{10,... | collective-permute-start | bytes 442376 | tf_op jit(solution)/shard_map/ppermute | solution.py:81
  56.4 5.6 %collective-permute-start.20 = (bf16[192,384]{1,0:T(8,128)(2,1)S(1)}, bf16[192,384]{1,0:T(8,128)(2,1)S(1)}, u32[]{:S(2)}, u32[]{:S(2)}) collective-permute-start(bf16[192,384]{1,0:T(8,128)(2,1)S(1)} %constant_dynamic-update-slice_fusion.refs_0_), channel_id=1, source_target_pairs={{0,1},{1,0},{2,3},{3,2},{4,5},{5,4},{6,7},{7,6},{8,9},{9,8},{10,11... | collective-permute-start | bytes 442376 | tf_op jit(solution)/shard_map/ppermute | solution.py:81
  59.0 3.1 %collective-permute-start.23 = (bf16[192,384]{1,0:T(8,128)(2,1)S(1)}, bf16[192,384]{1,0:T(8,128)(2,1)S(1)}, u32[]{:S(2)}, u32[]{:S(2)}) collective-permute-start(bf16[192,384]{1,0:T(8,128)(2,1)S(1)} %collective-permute-done.19.refs_3_), channel_id=1, source_target_pairs={{0,1},{1,0},{2,3},{3,2},{4,5},{5,4},{6,7},{7,6},{8,9},{9,8},{10,11... | collective-permute-start | bytes 442376 | tf_op jit(solution)/shard_map/ppermute | solution.py:81
  60.9 1.4 %collective-permute-start.22 = (bf16[192,384]{1,0:T(8,128)(2,1)S(1)}, bf16[192,384]{1,0:T(8,128)(2,1)S(1)}, u32[]{:S(2)}, u32[]{:S(2)}) collective-permute-start(bf16[192,384]{1,0:T(8,128)(2,1)S(1)} %collective-permute-done.18.refs_2_), channel_id=1, source_target_pairs={{0,1},{1,0},{2,3},{3,2},{4,5},{5,4},{6,7},{7,6},{8,9},{9,8},{10,11... | collective-permute-start | bytes 442376 | tf_op jit(solution)/shard_map/ppermute | solution.py:81
  61.0 1.5 %collective-permute-start.21 = (bf16[192,384]{1,0:T(8,128)(2,1)S(1)}, bf16[192,384]{1,0:T(8,128)(2,1)S(1)}, u32[]{:S(2)}, u32[]{:S(2)}) collective-permute-start(bf16[192,384]{1,0:T(8,128)(2,1)S(1)} %collective-permute-done.17.refs_1_), channel_id=1, source_target_pairs={{0,1},{1,0},{2,3},{3,2},{4,5},{5,4},{6,7},{7,6},{8,9},{9,8},{10,11... | collective-permute-start | bytes 442376 | tf_op jit(solution)/shard_map/ppermute | solution.py:81

commit v13 on v12

--- a/solution.py
+++ b/solution.py
@@ -250,6 +250,36 @@
     odt_ref[...] = rounded(times_transposed(wo_ref[...], og_ref[...]))
 
 
+def head_rows(rows_ref, head):
+    width, row_count = rows_ref.shape
+    head_dim = width // HEADS
+    low, high = head * head_dim, (head + 1) * head_dim
+    first = low // LANES * LANES
+    last = min(-(-high // LANES) * LANES, width)
+    row = lax.broadcasted_iota(jnp.int32, (last - first, row_count), 0) + first
+    return first, last, jnp.where((row >= low) & (row < high), rows_ref[first:last, :], 0)
+
+
+def window_kernel(
+    halo_ref, wkv_ref, qt_ref, odt_ref, own_kv_ref, bias_ref, halo_kv_ref, scores_ref, dprobs_ref, kv_ref
+):
+    width, row_count = qt_ref.shape
+    tile = halo_ref.shape[0]
+    halo_kv_ref[...] = rounded(f32_dot(halo_ref[...], wkv_ref[...]))
+    kv_ref[:tile] = halo_kv_ref[...]
+    kv_ref[tile:] = own_kv_ref[:row_count]
+    for head in range(HEADS):
+        for rows_ref, start, out_ref in ((qt_ref, 0, scores_ref), (odt_ref, width, dprobs_ref)):
+            first, last, rows = head_rows(rows_ref, head)
+            every = f32_dot(kv_ref[:, start + first : start + last], rows)
+            for at in range(0, row_count, tile):
+                lanes = slice(at, at + tile)
+                value = every[at : at + 2 * tile, lanes]
+                if start == 0:
+                    value = value + bias_ref[:, lanes]
+                out_ref[head, :, lanes] = value
+
+
 def attend_kernel(
     factor,
     per_peer,
@@ -259,8 +289,8 @@
     count = dom_size // 2 + 1
     piece_refs, halo_ref, refs = refs[:count], refs[count], refs[count + 1 :]
     og_ref, wq_ref, wkv_ref, featt_ref, qt_ref, odt_ref, own_kv_ref, own_kvt_ref = refs[:8]
-    local_bias_ref, far_bias_ref, send_ref, rider_ref = refs[8:12]
-    extt_ref, gqt_ref, gkvt_ref, ot_ref, slot_ref, kv_ref, kvt_ref = refs[12:]
+    far_bias_ref, halo_kv_ref, scores_ref, dprobs_ref, send_ref, rider_ref = refs[8:14]
+    extt_ref, gqt_ref, gkvt_ref, ot_ref, slot_ref, kv_ref, kvt_ref = refs[14:]
     width, row_count = qt_ref.shape
     tile = halo_ref.shape[0]
     tile_count = row_count // tile
@@ -270,44 +300,30 @@
     head_dim = width // HEADS
     scale = 1.0 / math.sqrt(head_dim)
 
-    kv_ref[tile:near] = own_kv_ref[:row_count]
-    kv_ref[virt_at:] = own_kv_ref[row_count:]
+    kv_ref[virt_at - near :] = own_kv_ref[row_count:]
     kvt_ref[:, tile:near] = own_kvt_ref[:, :row_count]
     kvt_ref[:, virt_at:] = own_kvt_ref[:, row_count:]
     extt_ref[:, tile:near] = featt_ref[:, :row_count]
     extt_ref[:, virt_at:] = featt_ref[:, row_count:]
+    extt_ref[:, :tile] = halo_ref[...].T
+    kvt_ref[:, :tile] = halo_kv_ref[...].T
     slot_ref[:per_peer] = piece_refs[0][...]
     slot_ref[per_peer : 2 * per_peer] = piece_refs[1][:per_peer]
     for at, piece_ref in enumerate(piece_refs[:1:-1], 1):
         slot_ref[2 * at * per_peer : (2 * at + 2) * per_peer] = piece_ref[...]
-    for rows, source_ref in ((slice(0, tile), halo_ref), (slice(near, virt_at), slot_ref)):
-        extt_ref[:, rows] = source_ref[...].T
-        kv_ref[rows] = rounded(f32_dot(source_ref[...], wkv_ref[...]))
-        kvt_ref[:, rows] = kv_ref[rows].T
+    extt_ref[:, near:virt_at] = slot_ref[...].T
+    kv_ref[:slots] = rounded(f32_dot(slot_ref[...], wkv_ref[...]))
+    kvt_ref[:, near:virt_at] = kv_ref[:slots].T
 
     def tiles(of):
         return jnp.concatenate([of(t, slice(t * tile, (t + 1) * tile)) for t in range(tile_count)], 1)
 
     for head in range(HEADS):
         low, high = head * head_dim, (head + 1) * head_dim
-        first = low // 128 * 128
-        last = min(-(-high // 128) * 128, width)
-        column = lax.broadcasted_iota(jnp.int32, (last - first, row_count), 0) + first
-        of_head = (column >= low) & (column < high)
-        q_rows = jnp.where(of_head, qt_ref[first:last, :], 0)
-        d_rows = jnp.where(of_head, odt_ref[first:last, :], 0)
-
-        def products(operand, start, stop):
-            local = tiles(
-                lambda t, lanes: f32_dot(
-                    kv_ref[t * tile : (t + 2) * tile, start:stop], operand[:, lanes]
-                )
-            )
-            return local, f32_dot(kv_ref[near:, start:stop], operand)
-
-        s_local, s_far = products(q_rows, first, last)
-        s_local += local_bias_ref[...]
-        s_far += far_bias_ref[...]
+        first, last, q_rows = head_rows(qt_ref, head)
+        d_rows = head_rows(odt_ref, head)[2]
+        s_local = scores_ref[head]
+        s_far = f32_dot(kv_ref[:, first:last], q_rows) + far_bias_ref[...]
         peak = jnp.maximum(
             jnp.max(s_local, axis=0, keepdims=True), jnp.max(s_far, axis=0, keepdims=True)
         )
@@ -318,7 +334,8 @@
         inverse = 1.0 / total
         p_local = e_local * inverse
         p_far = e_far * inverse
-        dp_local, dp_far = products(d_rows, width + first, width + last)
+        dp_local = dprobs_ref[head]
+        dp_far = f32_dot(kv_ref[:, width + first : width + last], d_rows)
         delta = jnp.sum(p_local * dp_local, axis=0, keepdims=True) + jnp.sum(
             p_far * dp_far, axis=0, keepdims=True
         )
@@ -520,9 +537,22 @@
         fetched=8,
         flops=10 * row_count * width * width,
     )
-    (through, halo), _ = lax.optimization_barrier(((through, halo), prepared[0]))
+    halo = shifted(halo, "rows", 1)
+    through, _ = lax.optimization_barrier((through, prepared[0]))
     arrived = handed_on(direct, through)
-    halo = shifted(halo, "rows", 1)
+    *prepared, local_bias, far_bias = prepared
+    window = call(
+        window_kernel,
+        "window",
+        [
+            shape((TILE, 2 * width), bf16),
+            shape((HEADS, 2 * TILE, row_count), f32),
+            shape((HEADS, 2 * TILE, row_count), f32),
+        ],
+        [halo, prepared[2], *prepared[4:7], local_bias],
+        [pltpu.VMEM((TILE + row_count, 2 * width), bf16)],
+        flops=8 * HEADS * TILE * row_count * LANES,
+    )
     message, rider, *gradients = call(
         functools.partial(attend_kernel, nodes**-0.5, per_peer, dom_size),
         "attend",
@@ -534,10 +564,10 @@
             shape((2 * width, ext_rows), bf16),
             shape((width, row_count), bf16),
         ],
-        [*arrived, halo, *prepared],
+        [*arrived, halo, *prepared, far_bias, *window],
         [
             pltpu.VMEM((slots, width), bf16),
-            pltpu.VMEM((ext_rows, 2 * width), bf16),
+            pltpu.VMEM((slots + padded, 2 * width), bf16),
             pltpu.VMEM((2 * width, ext_rows), bf16),
         ],
         flops=28 * ext_rows * width * width,

time: 64.4 us -> 64.6 us (level)
  waiting for transfers between devices: 25.8 us -> 23.6 us
  starting transfers between devices: 21.3 us -> 22.7 us
  Pallas kernels: 15.1 us -> 16 us
    ppermute x22, waiting for transfers between devices: 25.8 us -> 23.6 us  [swapped(): return lax.ppermute(block, ('dom', 'rows'), route)]
    ppermute x22, starting transfers between devices: 21.2 us -> 22.7 us  [swapped(): return lax.ppermute(block, ('dom', 'rows'), route)]
    pallas_call x6 -> x7, Pallas kernels: 15.1 us -> 16 us  [call(): pl.pallas_call(kernel, out_shape=outs, in_specs=[pl.BlockSpec(memory_spac...]
  transfers between devices with their start and end apart: 24 -> 24, of which waited for: 15 -> 15; matrix products, arithmetic and copies ran while one was open for 1% -> 1% of each run, Pallas kernels for 8% -> 10%
where the time goes in v13:
time: 64.6 us; the launch traced here: 64.3 us
  waiting for transfers between devices  23.6 us (37%)
  starting transfers between devices  22.7 us (35%)
  Pallas kernels  16 us (25%)
  between operations  1 us (2%)
  other arithmetic  0.97 us (2%)
    ppermute x22, waiting for transfers between devices, swapped(): return lax.ppermute(block, ('dom', 'rows'), route)  23.6 us
    ppermute x22, starting transfers between devices, swapped(): return lax.ppermute(block, ('dom', 'rows'), route)  22.7 us
    pallas_call x7, Pallas kernels, call(): pl.pallas_call(kernel, out_shape=outs, in_specs=[pl.BlockSpec(memory_spac...  16 us
  transfers between devices with their start and end apart: 24, of which 15 were waited for; matrix products, arithmetic and copies ran while one was open for 1% of the time, Pallas kernels for 10%

profile of v13, /device:TPU:0, one launch (start us, length us, event | category | flops | bytes accessed | tf_op | source)
XLA Modules:
  0.0 64.3 jit_solution(7754585617685993338)
XLA Ops:
  0.6 1.2 %pick_rows.1 = (bf16[128,384]{1,0:T(8,128)(2,1)S(1)}, bf16[256,256]{1,0:T(8,128)(2,1)S(1)}, bf16[128,384]{1,0:T(8,128)(2,1)S(1)}, bf16[32,384]{1,0:T(8,128)(2,1)...) custom-call(bf16[256,384]{1,0:T(8,128)(2,1)} %feat_hbm.3, ...), custom_call_target="tpu_custom_call" | custom-call | bytes 623616 | tf_op jit(solution)/shard_map/pick_rows/pallas_call | solution.py:479
  1.9 3.0 %collective-permute-start = (bf16[128,384]{1,0:T(8,128)(2,1)S(1)}, bf16[128,384]{1,0:T(8,128)(2,1)S(1)}, u32[]{:S(2)}, u32[]{:S(2)}) collective-permute-start(bf16[128,384]{1,0:T(8,128)(2,1)S(1)} %get-tuple-element.56), channel_id=1, source_target_pairs={{0,4},{1,5},{2,6},{3,7},{4,0},{5,1},{6,2},{7,3},{8,12},{9,13},{10,... | collective-permute-start | bytes 294920 | tf_op jit(solution)/shard_map/ppermute | solution.py:81
  4.9 0.0 collective-permute-start.4
  4.9 2.9 %prepare.1 = (bf16[256,384]{1,0:T(8,128)(2,1)S(1)}, bf16[384,384]{1,0:T(8,128)(2,1)S(1)}, bf16[384,768]{1,0:T(8,128)(2,1)S(1)}, bf16[384,272]{1,0:T(8,128)(2,1)S...) custom-call(bf16[256,384]{1,0:T(8,128)(2,1)} %feat_hbm.3, ...), custom_call_target="tpu_custom_call" | custom-call | flops 377487360 | bytes 4656128 | tf_op jit(solution)/shard_map/prepare/pallas_call | solution.py:479
  7.8 0.0 collective-permute-done.refs_1_
  7.8 3.9 %collective-permute-start.1 = (bf16[64,384]{1,0:T(8,128)(2,1)S(1)}, bf16[64,384]{1,0:T(8,128)(2,1)S(1)}, u32[]{:S(2)}, u32[]{:S(2)}) collective-permute-start(bf16[64,384]{1,0:T(8,128)(2,1)S(1)} %pad_maximum_fusion.6), channel_id=1, source_target_pairs={{0,24},{1,25},{2,26},{3,27},{4,28},{5,29},{6,30},{7,31},{8,16},{9,... | collective-permute-start | bytes 147464 | tf_op jit(solution)/shard_map/ppermute | solution.py:81
  11.7 0.0 collective-permute-start.2
  11.7 0.6 collective-permute-start.3
  12.3 0.0 collective-permute-done.4.halo_ref.refs_5_
  12.4 1.2 %window.1 = (bf16[128,768]{1,0:T(8,128)(2,1)S(1)}, f32[8,256,256]{2,1,0:T(8,128)S(1)}, f32[8,256,256]{2,1,0:T(8,128)S(1)}) custom-call(bf16[128,384]{1,0:T(8,128)(2,1)S(1)} %collective-permute-done.4.halo_ref.refs_5_, bf16[384,768]{1,0:T(8,128)(2,1)S(1)} %get-tuple-element.54.wkv_ref.refs_8_, bf16[384,256]{1,0:T(8,128)(2,1)S(1)} %get-tuple-element.63.qt_ref.refs_10_, ...), custom_call_target="tpu_custom_call" | custom-call | flops 268435456 | bytes 6152192 | tf_op jit(solution)/shard_map/window/pallas_call | solution.py:479
  13.6 0.3 collective-permute-done.1.refs_2_
  13.9 3.3 %collective-permute-done.2.refs_3_ = bf16[64,384]{1,0:T(8,128)(2,1)S(1)} collective-permute-done((bf16[64,384]{1,0:T(8,128)(2,1)S(1)}, bf16[64,384]{1,0:T(8,128)(2,1)S(1)}, u32[]{:S(2)}, u32[]{:S(2)}) %collective-permute-start.2) | collective-permute-done | bytes 49184 | tf_op jit(solution)/shard_map/ppermute | solution.py:81
  17.2 6.4 %attend.1 = (bf16[784,384]{1,0:T(8,128)(2,1)S(1)}, f32[16,384]{1,0:T(8,128)S(1)}, bf16[384,656]{1,0:T(8,128)(2,1)S(1)}, bf16[384,256]{1,0:T(8,128)(2,1)S(1)}, bf...) custom-call(bf16[32,384]{1,0:T(8,128)(2,1)S(1)} %get-tuple-element.55.refs_0_, ...), custom_call_target="tpu_custom_call" | custom-call | flops 2708471808 | bytes 10088448 | tf_op jit(solution)/shard_map/attend/pallas_call | solution.py:479
  23.6 0.1 collective-permute-start.5
  23.7 1.6 %finish.1 = (f32[256,384]{1,0:T(8,128)S(1)}, bf16[128,384]{1,0:T(8,128)(2,1)S(1)}, f32[768,384]{1,0:T(8,128)S(1)}, bf16[64,384]{1,0:T(8,128)(2,1)S(1)}, bf16[64,...) custom-call(bf16[256,384]{1,0:T(8,128)(2,1)S(1)} %get-tuple-element.52.refs_6_.og_ref, ...), custom_call_target="tpu_custom_call" | custom-call | flops 580386816 | bytes 4853760 | tf_op jit(solution)/shard_map/finish/pallas_call | solution.py:479
  25.3 0.4 collective-permute-done.5
  25.7 0.1 fusion.3
  25.9 0.1 pad_maximum_fusion.2
  26.0 2.0 %collective-permute-start.6 = (bf16[200,384]{1,0:T(8,128)(2,1)S(1)}, bf16[200,384]{1,0:T(8,128)(2,1)S(1)}, u32[]{:S(2)}, u32[]{:S(2)}) collective-permute-start(bf16[200,384]{1,0:T(8,128)(2,1)S(1)} %get-tuple-element.107), channel_id=1, source_target_pairs={{0,6},{1,7},{2,4},{3,5},{4,2},{5,3},{6,0},{7,1},{8,14},{9,15},{10,... | collective-permute-start | bytes 460808 | tf_op jit(solution)/shard_map/ppermute | solution.py:81
  28.0 0.7 %collective-permute-start.7 = (bf16[200,384]{1,0:T(8,128)(2,1)S(1)}, bf16[200,384]{1,0:T(8,128)(2,1)S(1)}, u32[]{:S(2)}, u32[]{:S(2)}) collective-permute-start(bf16[200,384]{1,0:T(8,128)(2,1)S(1)} %get-tuple-element.108), channel_id=1, source_target_pairs={{0,2},{1,3},{2,0},{3,1},{4,6},{5,7},{6,4},{7,5},{8,10},{9,11},{10,... | collective-permute-start | bytes 460808 | tf_op jit(solution)/shard_map/ppermute | solution.py:81
  28.7 0.8 %collective-permute-start.8 = (bf16[200,384]{1,0:T(8,128)(2,1)S(1)}, bf16[200,384]{1,0:T(8,128)(2,1)S(1)}, u32[]{:S(2)}, u32[]{:S(2)}) collective-permute-start(bf16[200,384]{1,0:T(8,128)(2,1)S(1)} %get-tuple-element.109), channel_id=1, source_target_pairs={{0,4},{1,5},{2,6},{3,7},{4,0},{5,1},{6,2},{7,3},{8,12},{9,13},{10,... | collective-permute-start | bytes 460808 | tf_op jit(solution)/shard_map/ppermute | solution.py:81
  29.5 2.2 %collective-permute-start.11 = (bf16[64,384]{1,0:T(8,128)(2,1)S(1)}, bf16[64,384]{1,0:T(8,128)(2,1)S(1)}, u32[]{:S(2)}, u32[]{:S(2)}) collective-permute-start(bf16[64,384]{1,0:T(8,128)(2,1)S(1)} %get-tuple-element.85), channel_id=1, source_target_pairs={{0,24},{1,25},{2,26},{3,27},{4,28},{5,29},{6,30},{7,31},{8,16},{9,... | collective-permute-start | bytes 147464 | tf_op jit(solution)/shard_map/ppermute | solution.py:81
  31.7 0.2 collective-permute-start.12
  31.9 1.9 %collective-permute-done.6 = bf16[200,384]{1,0:T(8,128)(2,1)S(1)} collective-permute-done((bf16[200,384]{1,0:T(8,128)(2,1)S(1)}, bf16[200,384]{1,0:T(8,128)(2,1)S(1)}, u32[]{:S(2)}, u32[]{:S(2)}) %collective-permute-start.6) | collective-permute-done | bytes 153632 | tf_op jit(solution)/shard_map/ppermute | solution.py:81
  33.8 0.9 %collective-permute-start.13 = (bf16[64,384]{1,0:T(8,128)(2,1)S(1)}, bf16[64,384]{1,0:T(8,128)(2,1)S(1)}, u32[]{:S(2)}, u32[]{:S(2)}) collective-permute-start(bf16[64,384]{1,0:T(8,128)(2,1)S(1)} %get-tuple-element.87), channel_id=1, source_target_pairs={{0,8},{1,9},{2,10},{3,11},{4,12},{5,13},{6,14},{7,15},{8,0},{9,1},... | collective-permute-start | bytes 147464 | tf_op jit(solution)/shard_map/ppermute | solution.py:81
  34.7 1.6 %collective-permute-done.7 = bf16[200,384]{1,0:T(8,128)(2,1)S(1)} collective-permute-done((bf16[200,384]{1,0:T(8,128)(2,1)S(1)}, bf16[200,384]{1,0:T(8,128)(2,1)S(1)}, u32[]{:S(2)}, u32[]{:S(2)}) %collective-permute-start.7) | collective-permute-done | bytes 153632 | tf_op jit(solution)/shard_map/ppermute | solution.py:81
  36.3 0.1 fusion.1
  36.4 0.6 collective-permute-done.12.refs_1_
  37.0 0.9 %collective-permute-done.13.refs_2_ = bf16[64,384]{1,0:T(8,128)(2,1)S(1)} collective-permute-done((bf16[64,384]{1,0:T(8,128)(2,1)S(1)}, bf16[64,384]{1,0:T(8,128)(2,1)S(1)}, u32[]{:S(2)}, u32[]{:S(2)}) %collective-permute-start.13) | collective-permute-done | bytes 49184 | tf_op jit(solution)/shard_map/ppermute | solution.py:81
  37.9 0.9 %collective-permute-start.9 = (bf16[104,384]{1,0:T(8,128)(2,1)S(1)}, bf16[104,384]{1,0:T(8,128)(2,1)S(1)}, u32[]{:S(2)}, u32[]{:S(2)}) collective-permute-start(bf16[104,384]{1,0:T(8,128)(2,1)S(1)} %pad_maximum_fusion.4), channel_id=1, source_target_pairs={{0,8},{1,9},{2,10},{3,11},{4,12},{5,13},{6,14},{7,15},{8,0},{9,1},... | collective-permute-start | bytes 239624 | tf_op jit(solution)/shard_map/ppermute | solution.py:81
  38.9 1.4 %collective-permute-start.15 = (bf16[128,384]{1,0:T(8,128)(2,1)S(1)}, bf16[128,384]{1,0:T(8,128)(2,1)S(1)}, u32[]{:S(2)}, u32[]{:S(2)}) collective-permute-start(bf16[128,384]{1,0:T(8,128)(2,1)S(1)} %pad_maximum_fusion.3), channel_id=1, source_target_pairs={{0,4},{1,5},{2,6},{3,7},{4,0},{5,1},{6,2},{7,3},{8,12},{9,13},{10,... | collective-permute-start | bytes 294920 | tf_op jit(solution)/shard_map/ppermute | solution.py:81
  40.3 2.1 %collective-permute-done.9 = bf16[104,384]{1,0:T(8,128)(2,1)S(1)} collective-permute-done((bf16[104,384]{1,0:T(8,128)(2,1)S(1)}, bf16[104,384]{1,0:T(8,128)(2,1)S(1)}, u32[]{:S(2)}, u32[]{:S(2)}) %collective-permute-start.9) | collective-permute-done | bytes 79904 | tf_op jit(solution)/shard_map/ppermute | solution.py:81
  42.5 2.0 %collective-permute-start.10 = (bf16[104,384]{1,0:T(8,128)(2,1)S(1)}, bf16[104,384]{1,0:T(8,128)(2,1)S(1)}, u32[]{:S(2)}, u32[]{:S(2)}) collective-permute-start(bf16[104,384]{1,0:T(8,128)(2,1)S(1)} %pad_maximum_fusion.5), channel_id=1, source_target_pairs={{0,16},{1,17},{2,18},{3,19},{4,20},{5,21},{6,22},{7,23},{8,24},{9,... | collective-permute-start | bytes 239624 | tf_op jit(solution)/shard_map/ppermute | solution.py:81
  44.5 1.0 %return_rows.1 = f32[256,384]{1,0:T(8,128)} custom-call(f32[256,384]{1,0:T(8,128)S(1)} %get-tuple-element.79.gf_ref, bf16[256,256]{1,0:T(8,128)(2,1)S(1)} %get-tuple-element.80.chosen_ref, bf16[128,384]{1,0:T(8,128)(2,1)S(1)} %collective-permute-done.14.halo_ref, bf16[64,384]{1,0:T(8,128)(2,1)S(1)} %get-tuple-element.90.own_ref, ...), custom_call_target="tpu_custom_call" | custom-call | bytes 1310720 | tf_op jit(solution)/shard_map/return_rows/pallas_call | solution.py:479
  45.5 3.2 %collective-permute-done.10 = bf16[104,384]{1,0:T(8,128)(2,1)S(1)} collective-permute-done((bf16[104,384]{1,0:T(8,128)(2,1)S(1)}, bf16[104,384]{1,0:T(8,128)(2,1)S(1)}, u32[]{:S(2)}, u32[]{:S(2)}) %collective-permute-start.10) | collective-permute-done | bytes 79904 | tf_op jit(solution)/shard_map/ppermute | solution.py:81
  48.7 0.2 collective-permute-start.16
  48.9 4.2 %collective-permute-done.16 = bf16[96,384]{1,0:T(8,128)(2,1)S(1)} collective-permute-done((bf16[96,384]{1,0:T(8,128)(2,1)S(1)}, bf16[96,384]{1,0:T(8,128)(2,1)S(1)}, u32[]{:S(2)}, u32[]{:S(2)}) %collective-permute-start.16) | collective-permute-done | bytes 73760 | tf_op jit(solution)/shard_map/ppermute | solution.py:81
  53.2 1.7 %collective-permute-start.19 = (bf16[192,384]{1,0:T(8,128)(2,1)S(1)}, bf16[192,384]{1,0:T(8,128)(2,1)S(1)}, u32[]{:S(2)}, u32[]{:S(2)}) collective-permute-start(bf16[192,384]{1,0:T(8,128)(2,1)S(1)} %constant_dynamic-update-slice_fusion.refs_0_), channel_id=1, source_target_pairs={{0,6},{1,7},{2,4},{3,5},{4,2},{5,3},{6,0},{7,1},{8,14},{9,15},{10,... | collective-permute-start | bytes 442376 | tf_op jit(solution)/shard_map/ppermute | solution.py:81
  54.9 1.1 %collective-permute-start.18 = (bf16[192,384]{1,0:T(8,128)(2,1)S(1)}, bf16[192,384]{1,0:T(8,128)(2,1)S(1)}, u32[]{:S(2)}, u32[]{:S(2)}) collective-permute-start(bf16[192,384]{1,0:T(8,128)(2,1)S(1)} %constant_dynamic-update-slice_fusion.refs_0_), channel_id=1, source_target_pairs={{0,2},{1,3},{2,0},{3,1},{4,6},{5,7},{6,4},{7,5},{8,10},{9,11},{10,... | collective-permute-start | bytes 442376 | tf_op jit(solution)/shard_map/ppermute | solution.py:81
  56.0 0.7 %collective-permute-start.17 = (bf16[192,384]{1,0:T(8,128)(2,1)S(1)}, bf16[192,384]{1,0:T(8,128)(2,1)S(1)}, u32[]{:S(2)}, u32[]{:S(2)}) collective-permute-start(bf16[192,384]{1,0:T(8,128)(2,1)S(1)} %constant_dynamic-update-slice_fusion.refs_0_), channel_id=1, source_target_pairs={{0,4},{1,5},{2,6},{3,7},{4,0},{5,1},{6,2},{7,3},{8,12},{9,13},{10,... | collective-permute-start | bytes 442376 | tf_op jit(solution)/shard_map/ppermute | solution.py:81
  56.7 2.6 %collective-permute-done.19.refs_3_ = bf16[192,384]{1,0:T(8,128)(2,1)S(1)} collective-permute-done((bf16[192,384]{1,0:T(8,128)(2,1)S(1)}, bf16[192,384]{1,0:T(8,128)(2,1)S(1)}, u32[]{:S(2)}, u32[]{:S(2)}) %collective-permute-start.19) | collective-permute-done | bytes 147488 | tf_op jit(solution)/shard_map/ppermute | solution.py:81
  59.4 1.5 %collective-permute-done.18.refs_2_ = bf16[192,384]{1,0:T(8,128)(2,1)S(1)} collective-permute-done((bf16[192,384]{1,0:T(8,128)(2,1)S(1)}, bf16[192,384]{1,0:T(8,128)(2,1)S(1)}, u32[]{:S(2)}, u32[]{:S(2)}) %collective-permute-start.18) | collective-permute-done | bytes 147488 | tf_op jit(solution)/shard_map/ppermute | solution.py:81
  60.9 0.3 collective-permute-done.17.refs_1_
  61.2 0.2 collective-permute-start.21
  61.4 0.6 convert_add_fusion.1
  62.0 0.3 collective-permute-done.22.refs_6_
  62.2 0.3 collective-permute-done.21.refs_5_
  62.5 1.6 %place_sums.1 = (f32[384,384]{1,0:T(8,128)}, f32[384,768]{1,0:T(8,128)}, f32[384,384]{1,0:T(8,128)}) custom-call(bf16[192,384]{1,0:T(8,128)(2,1)S(1)} %constant_dynamic-update-slice_fusion.refs_0_, bf16[192,384]{1,0:T(8,128)(2,1)S(1)} %collective-permute-done.17.refs_1_, bf16[192,384]{1,0:T(8,128)(2,1)S(1)} %collective-permute-done.18.refs_2_, ...), custom_call_target="tpu_custom_call" | custom-call | bytes 3538944 | tf_op jit(solution)/shard_map/place_sums/pallas_call | solution.py:479
  (33 shorter events, 0.3 us)
Async XLA Ops:
  1.9 5.9 %collective-permute-start = (bf16[128,384]{1,0:T(8,128)(2,1)S(1)}, bf16[128,384]{1,0:T(8,128)(2,1)S(1)}, u32[]{:S(2)}, u32[]{:S(2)}) collective-permute-start(bf16[128,384]{1,0:T(8,128)(2,1)S(1)} %get-tuple-element.56), channel_id=1, source_target_pairs={{0,4},{1,5},{2,6},{3,7},{4,0},{5,1},{6,2},{7,3},{8,12},{9,13},{10,... | collective-permute-start | bytes 294920 | tf_op jit(solution)/shard_map/ppermute | solution.py:81
  4.9 7.5 %collective-permute-start.4 = (bf16[128,384]{1,0:T(8,128)(2,1)S(1)}, bf16[128,384]{1,0:T(8,128)(2,1)S(1)}, u32[]{:S(2)}, u32[]{:S(2)}) collective-permute-start(bf16[128,384]{1,0:T(8,128)(2,1)S(1)} %get-tuple-element.61), channel_id=1, source_target_pairs={{3,0},{0,1},{1,2},{2,3},{7,4},{4,5},{5,6},{6,7},{11,8},{8,9},{9,10... | collective-permute-start | bytes 294920 | tf_op jit(solution)/shard_map/ppermute | solution.py:87
  7.8 6.1 %collective-permute-start.1 = (bf16[64,384]{1,0:T(8,128)(2,1)S(1)}, bf16[64,384]{1,0:T(8,128)(2,1)S(1)}, u32[]{:S(2)}, u32[]{:S(2)}) collective-permute-start(bf16[64,384]{1,0:T(8,128)(2,1)S(1)} %pad_maximum_fusion.6), channel_id=1, source_target_pairs={{0,24},{1,25},{2,26},{3,27},{4,28},{5,29},{6,30},{7,31},{8,16},{9,... | collective-permute-start | bytes 147464 | tf_op jit(solution)/shard_map/ppermute | solution.py:81
  11.7 5.5 %collective-permute-start.2 = (bf16[64,384]{1,0:T(8,128)(2,1)S(1)}, bf16[64,384]{1,0:T(8,128)(2,1)S(1)}, u32[]{:S(2)}, u32[]{:S(2)}) collective-permute-start(bf16[64,384]{1,0:T(8,128)(2,1)S(1)} %pad_maximum_fusion.7), channel_id=1, source_target_pairs={{0,16},{1,17},{2,18},{3,19},{4,20},{5,21},{6,22},{7,23},{8,24},{9,... | collective-permute-start | bytes 147464 | tf_op jit(solution)/shard_map/ppermute | solution.py:81
  11.7 5.5 %collective-permute-start.3 = (bf16[64,384]{1,0:T(8,128)(2,1)S(1)}, bf16[64,384]{1,0:T(8,128)(2,1)S(1)}, u32[]{:S(2)}, u32[]{:S(2)}) collective-permute-start(bf16[64,384]{1,0:T(8,128)(2,1)S(1)} %pad_maximum_fusion.8), channel_id=1, source_target_pairs={{0,8},{1,9},{2,10},{3,11},{4,12},{5,13},{6,14},{7,15},{8,0},{9,1},... | collective-permute-start | bytes 147464 | tf_op jit(solution)/shard_map/ppermute | solution.py:81
  23.6 2.1 %collective-permute-start.5 = (bf16[784,384]{1,0:T(8,128)(2,1)S(1)}, bf16[784,384]{1,0:T(8,128)(2,1)S(1)}, u32[]{:S(2)}, u32[]{:S(2)}) collective-permute-start(bf16[784,384]{1,0:T(8,128)(2,1)S(1)} %get-tuple-element.77), channel_id=1, source_target_pairs={{0,1},{1,0},{2,3},{3,2},{4,5},{5,4},{6,7},{7,6},{8,9},{9,8},{10,11... | collective-permute-start | bytes 1806344 | tf_op jit(solution)/shard_map/ppermute | solution.py:81
  26.0 7.8 %collective-permute-start.6 = (bf16[200,384]{1,0:T(8,128)(2,1)S(1)}, bf16[200,384]{1,0:T(8,128)(2,1)S(1)}, u32[]{:S(2)}, u32[]{:S(2)}) collective-permute-start(bf16[200,384]{1,0:T(8,128)(2,1)S(1)} %get-tuple-element.107), channel_id=1, source_target_pairs={{0,6},{1,7},{2,4},{3,5},{4,2},{5,3},{6,0},{7,1},{8,14},{9,15},{10,... | collective-permute-start | bytes 460808 | tf_op jit(solution)/shard_map/ppermute | solution.py:81
  28.0 8.3 %collective-permute-start.7 = (bf16[200,384]{1,0:T(8,128)(2,1)S(1)}, bf16[200,384]{1,0:T(8,128)(2,1)S(1)}, u32[]{:S(2)}, u32[]{:S(2)}) collective-permute-start(bf16[200,384]{1,0:T(8,128)(2,1)S(1)} %get-tuple-element.108), channel_id=1, source_target_pairs={{0,2},{1,3},{2,0},{3,1},{4,6},{5,7},{6,4},{7,5},{8,10},{9,11},{10,... | collective-permute-start | bytes 460808 | tf_op jit(solution)/shard_map/ppermute | solution.py:81
  28.7 7.6 %collective-permute-start.8 = (bf16[200,384]{1,0:T(8,128)(2,1)S(1)}, bf16[200,384]{1,0:T(8,128)(2,1)S(1)}, u32[]{:S(2)}, u32[]{:S(2)}) collective-permute-start(bf16[200,384]{1,0:T(8,128)(2,1)S(1)} %get-tuple-element.109), channel_id=1, source_target_pairs={{0,4},{1,5},{2,6},{3,7},{4,0},{5,1},{6,2},{7,3},{8,12},{9,13},{10,... | collective-permute-start | bytes 460808 | tf_op jit(solution)/shard_map/ppermute | solution.py:81
  29.5 6.8 %collective-permute-start.11 = (bf16[64,384]{1,0:T(8,128)(2,1)S(1)}, bf16[64,384]{1,0:T(8,128)(2,1)S(1)}, u32[]{:S(2)}, u32[]{:S(2)}) collective-permute-start(bf16[64,384]{1,0:T(8,128)(2,1)S(1)} %get-tuple-element.85), channel_id=1, source_target_pairs={{0,24},{1,25},{2,26},{3,27},{4,28},{5,29},{6,30},{7,31},{8,16},{9,... | collective-permute-start | bytes 147464 | tf_op jit(solution)/shard_map/ppermute | solution.py:81
  31.7 5.3 %collective-permute-start.12 = (bf16[64,384]{1,0:T(8,128)(2,1)S(1)}, bf16[64,384]{1,0:T(8,128)(2,1)S(1)}, u32[]{:S(2)}, u32[]{:S(2)}) collective-permute-start(bf16[64,384]{1,0:T(8,128)(2,1)S(1)} %get-tuple-element.86), channel_id=1, source_target_pairs={{0,16},{1,17},{2,18},{3,19},{4,20},{5,21},{6,22},{7,23},{8,24},{9,... | collective-permute-start | bytes 147464 | tf_op jit(solution)/shard_map/ppermute | solution.py:81
  33.8 4.1 %collective-permute-start.13 = (bf16[64,384]{1,0:T(8,128)(2,1)S(1)}, bf16[64,384]{1,0:T(8,128)(2,1)S(1)}, u32[]{:S(2)}, u32[]{:S(2)}) collective-permute-start(bf16[64,384]{1,0:T(8,128)(2,1)S(1)} %get-tuple-element.87), channel_id=1, source_target_pairs={{0,8},{1,9},{2,10},{3,11},{4,12},{5,13},{6,14},{7,15},{8,0},{9,1},... | collective-permute-start | bytes 147464 | tf_op jit(solution)/shard_map/ppermute | solution.py:81
  37.9 4.5 %collective-permute-start.9 = (bf16[104,384]{1,0:T(8,128)(2,1)S(1)}, bf16[104,384]{1,0:T(8,128)(2,1)S(1)}, u32[]{:S(2)}, u32[]{:S(2)}) collective-permute-start(bf16[104,384]{1,0:T(8,128)(2,1)S(1)} %pad_maximum_fusion.4), channel_id=1, source_target_pairs={{0,8},{1,9},{2,10},{3,11},{4,12},{5,13},{6,14},{7,15},{8,0},{9,1},... | collective-permute-start | bytes 239624 | tf_op jit(solution)/shard_map/ppermute | solution.py:81
  38.9 5.6 %collective-permute-start.15 = (bf16[128,384]{1,0:T(8,128)(2,1)S(1)}, bf16[128,384]{1,0:T(8,128)(2,1)S(1)}, u32[]{:S(2)}, u32[]{:S(2)}) collective-permute-start(bf16[128,384]{1,0:T(8,128)(2,1)S(1)} %pad_maximum_fusion.3), channel_id=1, source_target_pairs={{0,4},{1,5},{2,6},{3,7},{4,0},{5,1},{6,2},{7,3},{8,12},{9,13},{10,... | collective-permute-start | bytes 294920 | tf_op jit(solution)/shard_map/ppermute | solution.py:81
  40.3 4.1 %collective-permute-start.14 = (bf16[128,384]{1,0:T(8,128)(2,1)S(1)}, bf16[128,384]{1,0:T(8,128)(2,1)S(1)}, u32[]{:S(2)}, u32[]{:S(2)}) collective-permute-start(bf16[128,384]{1,0:T(8,128)(2,1)S(1)} %get-tuple-element.89), channel_id=1, source_target_pairs={{1,0},{2,1},{3,2},{0,3},{5,4},{6,5},{7,6},{4,7},{9,8},{10,9},{11,1... | collective-permute-start | bytes 294920 | tf_op jit(solution)/shard_map/ppermute | solution.py:87
  42.5 6.2 %collective-permute-start.10 = (bf16[104,384]{1,0:T(8,128)(2,1)S(1)}, bf16[104,384]{1,0:T(8,128)(2,1)S(1)}, u32[]{:S(2)}, u32[]{:S(2)}) collective-permute-start(bf16[104,384]{1,0:T(8,128)(2,1)S(1)} %pad_maximum_fusion.5), channel_id=1, source_target_pairs={{0,16},{1,17},{2,18},{3,19},{4,20},{5,21},{6,22},{7,23},{8,24},{9,... | collective-permute-start | bytes 239624 | tf_op jit(solution)/shard_map/ppermute | solution.py:81
  48.7 4.4 %collective-permute-start.16 = (bf16[96,384]{1,0:T(8,128)(2,1)S(1)}, bf16[96,384]{1,0:T(8,128)(2,1)S(1)}, u32[]{:S(2)}, u32[]{:S(2)}) collective-permute-start(bf16[96,384]{1,0:T(8,128)(2,1)S(1)} %add_convert_fusion), channel_id=1, source_target_pairs={{0,8},{1,9},{2,10},{3,11},{4,12},{5,13},{6,14},{7,15},{8,0},{9,1},... | collective-permute-start | bytes 221192 | tf_op jit(solution)/shard_map/ppermute | solution.py:81
  53.2 6.2 %collective-permute-start.19 = (bf16[192,384]{1,0:T(8,128)(2,1)S(1)}, bf16[192,384]{1,0:T(8,128)(2,1)S(1)}, u32[]{:S(2)}, u32[]{:S(2)}) collective-permute-start(bf16[192,384]{1,0:T(8,128)(2,1)S(1)} %constant_dynamic-update-slice_fusion.refs_0_), channel_id=1, source_target_pairs={{0,6},{1,7},{2,4},{3,5},{4,2},{5,3},{6,0},{7,1},{8,14},{9,15},{10,... | collective-permute-start | bytes 442376 | tf_op jit(solution)/shard_map/ppermute | solution.py:81
  54.9 6.0 %collective-permute-start.18 = (bf16[192,384]{1,0:T(8,128)(2,1)S(1)}, bf16[192,384]{1,0:T(8,128)(2,1)S(1)}, u32[]{:S(2)}, u32[]{:S(2)}) collective-permute-start(bf16[192,384]{1,0:T(8,128)(2,1)S(1)} %constant_dynamic-update-slice_fusion.refs_0_), channel_id=1, source_target_pairs={{0,2},{1,3},{2,0},{3,1},{4,6},{5,7},{6,4},{7,5},{8,10},{9,11},{10,... | collective-permute-start | bytes 442376 | tf_op jit(solution)/shard_map/ppermute | solution.py:81
  56.0 5.1 %collective-permute-start.17 = (bf16[192,384]{1,0:T(8,128)(2,1)S(1)}, bf16[192,384]{1,0:T(8,128)(2,1)S(1)}, u32[]{:S(2)}, u32[]{:S(2)}) collective-permute-start(bf16[192,384]{1,0:T(8,128)(2,1)S(1)} %constant_dynamic-update-slice_fusion.refs_0_), channel_id=1, source_target_pairs={{0,4},{1,5},{2,6},{3,7},{4,0},{5,1},{6,2},{7,3},{8,12},{9,13},{10,... | collective-permute-start | bytes 442376 | tf_op jit(solution)/shard_map/ppermute | solution.py:81
  56.7 5.2 %collective-permute-start.20 = (bf16[192,384]{1,0:T(8,128)(2,1)S(1)}, bf16[192,384]{1,0:T(8,128)(2,1)S(1)}, u32[]{:S(2)}, u32[]{:S(2)}) collective-permute-start(bf16[192,384]{1,0:T(8,128)(2,1)S(1)} %constant_dynamic-update-slice_fusion.refs_0_), channel_id=1, source_target_pairs={{0,1},{1,0},{2,3},{3,2},{4,5},{5,4},{6,7},{7,6},{8,9},{9,8},{10,11... | collective-permute-start | bytes 442376 | tf_op jit(solution)/shard_map/ppermute | solution.py:81
  59.4 2.6 %collective-permute-start.23 = (bf16[192,384]{1,0:T(8,128)(2,1)S(1)}, bf16[192,384]{1,0:T(8,128)(2,1)S(1)}, u32[]{:S(2)}, u32[]{:S(2)}) collective-permute-start(bf16[192,384]{1,0:T(8,128)(2,1)S(1)} %collective-permute-done.19.refs_3_), channel_id=1, source_target_pairs={{0,1},{1,0},{2,3},{3,2},{4,5},{5,4},{6,7},{7,6},{8,9},{9,8},{10,11... | collective-permute-start | bytes 442376 | tf_op jit(solution)/shard_map/ppermute | solution.py:81
  60.9 1.4 %collective-permute-start.22 = (bf16[192,384]{1,0:T(8,128)(2,1)S(1)}, bf16[192,384]{1,0:T(8,128)(2,1)S(1)}, u32[]{:S(2)}, u32[]{:S(2)}) collective-permute-start(bf16[192,384]{1,0:T(8,128)(2,1)S(1)} %collective-permute-done.18.refs_2_), channel_id=1, source_target_pairs={{0,1},{1,0},{2,3},{3,2},{4,5},{5,4},{6,7},{7,6},{8,9},{9,8},{10,11... | collective-permute-start | bytes 442376 | tf_op jit(solution)/shard_map/ppermute | solution.py:81
  61.2 1.4 %collective-permute-start.21 = (bf16[192,384]{1,0:T(8,128)(2,1)S(1)}, bf16[192,384]{1,0:T(8,128)(2,1)S(1)}, u32[]{:S(2)}, u32[]{:S(2)}) collective-permute-start(bf16[192,384]{1,0:T(8,128)(2,1)S(1)} %collective-permute-done.17.refs_1_), channel_id=1, source_target_pairs={{0,1},{1,0},{2,3},{3,2},{4,5},{5,4},{6,7},{7,6},{8,9},{9,8},{10,11... | collective-permute-start | bytes 442376 | tf_op jit(solution)/shard_map/ppermute | solution.py:81

commit v14 on v12

--- a/solution.py
+++ b/solution.py
@@ -288,24 +288,23 @@
     def tiles(of):
         return jnp.concatenate([of(t, slice(t * tile, (t + 1) * tile)) for t in range(tile_count)], 1)
 
-    for head in range(HEADS):
+    def bounds(head):
         low, high = head * head_dim, (head + 1) * head_dim
-        first = low // 128 * 128
-        last = min(-(-high // 128) * 128, width)
+        return low, high, low // LANES * LANES, min(-(-high // LANES) * LANES, width)
+
+    def products(head):
+        low, high, first, last = bounds(head)
         column = lax.broadcasted_iota(jnp.int32, (last - first, row_count), 0) + first
         of_head = (column >= low) & (column < high)
-        q_rows = jnp.where(of_head, qt_ref[first:last, :], 0)
-        d_rows = jnp.where(of_head, odt_ref[first:last, :], 0)
-
-        def products(operand, start, stop):
-            local = tiles(
-                lambda t, lanes: f32_dot(
-                    kv_ref[t * tile : (t + 2) * tile, start:stop], operand[:, lanes]
-                )
-            )
-            return local, f32_dot(kv_ref[near:, start:stop], operand)
-
-        s_local, s_far = products(q_rows, first, last)
+        out = []
+        for rows_ref, start in ((qt_ref, 0), (odt_ref, width)):
+            operand = jnp.where(of_head, rows_ref[first:last, :], 0)
+            every = f32_dot(kv_ref[:, start + first : start + last], operand)
+            out.append(tiles(lambda t, lanes: every[t * tile : (t + 2) * tile, lanes]))
+            out.append(every[near:])
+        return out
+
+    def weights(s_local, s_far, dp_local, dp_far):
         s_local += local_bias_ref[...]
         s_far += far_bias_ref[...]
         peak = jnp.maximum(
@@ -318,13 +317,15 @@
         inverse = 1.0 / total
         p_local = e_local * inverse
         p_far = e_far * inverse
-        dp_local, dp_far = products(d_rows, width + first, width + last)
         delta = jnp.sum(p_local * dp_local, axis=0, keepdims=True) + jnp.sum(
             p_far * dp_far, axis=0, keepdims=True
         )
-        pb_local, pb_far = rounded(p_local), rounded(p_far)
         ds_local = rounded(p_local * (dp_local - delta))
         ds_far = rounded(p_far * (dp_far - delta))
+        return rounded(p_local), rounded(p_far), ds_local, ds_far
+
+    def outputs(head, pb_local, pb_far, ds_local, ds_far):
+        low, high, _, _ = bounds(head)
 
         def to_queries(start, local, beyond):
             rows = slice(start + low, start + high)
@@ -332,9 +333,6 @@
                 lambda t, lanes: f32_dot(kvt_ref[rows, t * tile : (t + 2) * tile], local[:, lanes])
             )
             return near_part + f32_dot(kvt_ref[rows, near:], beyond)
-
-        ot_ref[low:high] = rounded(to_queries(width, pb_local, pb_far))
-        gqt_ref[low:high] = rounded(to_queries(0, ds_local, ds_far) * scale)
 
         def to_keys(start, operand, local, beyond, factor):
             rows = slice(start + low, start + high)
@@ -351,8 +349,21 @@
             gathered = jnp.concatenate(parts, axis=1)
             gkvt_ref[rows] = rounded(gathered if factor is None else gathered * factor)
 
+        ot_ref[low:high] = rounded(to_queries(width, pb_local, pb_far))
+        gqt_ref[low:high] = rounded(to_queries(0, ds_local, ds_far) * scale)
         to_keys(0, qt_ref[low:high], ds_local, ds_far, scale)
         to_keys(width, odt_ref[low:high], pb_local, pb_far, None)
+
+    coming = products(0)
+    done = None
+    for head in range(HEADS):
+        now = coming
+        if head + 1 < HEADS:
+            coming = products(head + 1)
+        if done is not None:
+            outputs(head - 1, *done)
+        done = weights(*now)
+    outputs(HEADS - 1, *done)
 
     rider_ref[...] = f32_dot(wkv_ref[...], gkvt_ref[:, virt_at:]).T * factor
     weight_sums(

time: 64.4 us -> 63.4 us (0.984)
  Pallas kernels: 15.1 us -> 14.1 us
    pallas_call x6, Pallas kernels: 15.1 us -> 14.1 us  [call(): pl.pallas_call(kernel, out_shape=outs, in_specs=[pl.BlockSpec(memory_spac...]
where the time goes in v14:
time: 63.4 us; the launch traced here: 63.2 us
  waiting for transfers between devices  25.8 us (41%)
  starting transfers between devices  21.3 us (34%)
  Pallas kernels  14.1 us (22%)
  other arithmetic  0.98 us (2%)
  between operations  0.85 us (1%)
    ppermute x22, waiting for transfers between devices, swapped(): return lax.ppermute(block, ('dom', 'rows'), route)  25.8 us
    ppermute x22, starting transfers between devices, swapped(): return lax.ppermute(block, ('dom', 'rows'), route)  21.2 us
    pallas_call x6, Pallas kernels, call(): pl.pallas_call(kernel, out_shape=outs, in_specs=[pl.BlockSpec(memory_spac...  14.1 us
  transfers between devices with their start and end apart: 24, of which 15 were waited for; matrix products, arithmetic and copies ran while one was open for 1% of the time, Pallas kernels for 8%

profile of v14, /device:TPU:0, one launch (start us, length us, event | category | flops | bytes accessed | tf_op | source)
XLA Modules:
  0.0 63.2 jit_solution(9718499237465444731)
XLA Ops:
  0.6 1.2 %pick_rows.1 = (bf16[128,384]{1,0:T(8,128)(2,1)S(1)}, bf16[256,256]{1,0:T(8,128)(2,1)S(1)}, bf16[128,384]{1,0:T(8,128)(2,1)S(1)}, bf16[32,384]{1,0:T(8,128)(2,1)...) custom-call(bf16[256,384]{1,0:T(8,128)(2,1)} %feat_hbm.3, ...), custom_call_target="tpu_custom_call" | custom-call | bytes 623616 | tf_op jit(solution)/shard_map/pick_rows/pallas_call | solution.py:473
  1.9 3.0 %collective-permute-start = (bf16[128,384]{1,0:T(8,128)(2,1)S(1)}, bf16[128,384]{1,0:T(8,128)(2,1)S(1)}, u32[]{:S(2)}, u32[]{:S(2)}) collective-permute-start(bf16[128,384]{1,0:T(8,128)(2,1)S(1)} %get-tuple-element.54), channel_id=1, source_target_pairs={{0,4},{1,5},{2,6},{3,7},{4,0},{5,1},{6,2},{7,3},{8,12},{9,13},{10,... | collective-permute-start | bytes 294920 | tf_op jit(solution)/shard_map/ppermute | solution.py:81
  4.9 2.9 %prepare.1 = (bf16[256,384]{1,0:T(8,128)(2,1)S(1)}, bf16[384,384]{1,0:T(8,128)(2,1)S(1)}, bf16[384,768]{1,0:T(8,128)(2,1)S(1)}, bf16[384,272]{1,0:T(8,128)(2,1)S...) custom-call(bf16[256,384]{1,0:T(8,128)(2,1)} %feat_hbm.3, ...), custom_call_target="tpu_custom_call" | custom-call | flops 377487360 | bytes 4656128 | tf_op jit(solution)/shard_map/prepare/pallas_call | solution.py:473
  7.8 3.9 %collective-permute-start.1 = (bf16[64,384]{1,0:T(8,128)(2,1)S(1)}, bf16[64,384]{1,0:T(8,128)(2,1)S(1)}, u32[]{:S(2)}, u32[]{:S(2)}) collective-permute-start(bf16[64,384]{1,0:T(8,128)(2,1)S(1)} %pad_maximum_fusion.6), channel_id=1, source_target_pairs={{0,24},{1,25},{2,26},{3,27},{4,28},{5,29},{6,30},{7,31},{8,16},{9,... | collective-permute-start | bytes 147464 | tf_op jit(solution)/shard_map/ppermute | solution.py:81
  11.7 0.1 collective-permute-start.4
  11.8 0.6 %collective-permute-start.3 = (bf16[64,384]{1,0:T(8,128)(2,1)S(1)}, bf16[64,384]{1,0:T(8,128)(2,1)S(1)}, u32[]{:S(2)}, u32[]{:S(2)}) collective-permute-start(bf16[64,384]{1,0:T(8,128)(2,1)S(1)} %pad_maximum_fusion.8), channel_id=1, source_target_pairs={{0,8},{1,9},{2,10},{3,11},{4,12},{5,13},{6,14},{7,15},{8,0},{9,1},... | collective-permute-start | bytes 147464 | tf_op jit(solution)/shard_map/ppermute | solution.py:81
  12.4 1.9 %collective-permute-done.1.refs_2_ = bf16[64,384]{1,0:T(8,128)(2,1)S(1)} collective-permute-done((bf16[64,384]{1,0:T(8,128)(2,1)S(1)}, bf16[64,384]{1,0:T(8,128)(2,1)S(1)}, u32[]{:S(2)}, u32[]{:S(2)}) %collective-permute-start.1) | collective-permute-done | bytes 49184 | tf_op jit(solution)/shard_map/ppermute | solution.py:81
  14.3 2.5 %collective-permute-done.2.refs_3_ = bf16[64,384]{1,0:T(8,128)(2,1)S(1)} collective-permute-done((bf16[64,384]{1,0:T(8,128)(2,1)S(1)}, bf16[64,384]{1,0:T(8,128)(2,1)S(1)}, u32[]{:S(2)}, u32[]{:S(2)}) %collective-permute-start.2) | collective-permute-done | bytes 49184 | tf_op jit(solution)/shard_map/ppermute | solution.py:81
  16.8 0.0 collective-permute-done.3.refs_4_
  16.8 0.0 collective-permute-done.4.refs_5_
  16.8 5.9 %attend.1 = (bf16[784,384]{1,0:T(8,128)(2,1)S(1)}, f32[16,384]{1,0:T(8,128)S(1)}, bf16[384,656]{1,0:T(8,128)(2,1)S(1)}, bf16[384,256]{1,0:T(8,128)(2,1)S(1)}, bf...) custom-call(bf16[32,384]{1,0:T(8,128)(2,1)S(1)} %get-tuple-element.53.refs_0_, ...), custom_call_target="tpu_custom_call" | custom-call | flops 2708471808 | bytes 5959680 | tf_op jit(solution)/shard_map/attend/pallas_call | solution.py:473
  22.7 0.1 collective-permute-start.5
  22.8 1.5 %finish.1 = (f32[256,384]{1,0:T(8,128)S(1)}, bf16[128,384]{1,0:T(8,128)(2,1)S(1)}, f32[768,384]{1,0:T(8,128)S(1)}, bf16[64,384]{1,0:T(8,128)(2,1)S(1)}, bf16[64,...) custom-call(bf16[256,384]{1,0:T(8,128)(2,1)S(1)} %get-tuple-element.50.refs_6_.og_ref, ...), custom_call_target="tpu_custom_call" | custom-call | flops 580386816 | bytes 4853760 | tf_op jit(solution)/shard_map/finish/pallas_call | solution.py:473
  24.2 0.5 collective-permute-done.5
  24.8 0.1 fusion.3
  25.1 2.4 %collective-permute-start.6 = (bf16[200,384]{1,0:T(8,128)(2,1)S(1)}, bf16[200,384]{1,0:T(8,128)(2,1)S(1)}, u32[]{:S(2)}, u32[]{:S(2)}) collective-permute-start(bf16[200,384]{1,0:T(8,128)(2,1)S(1)} %get-tuple-element.103), channel_id=1, source_target_pairs={{0,6},{1,7},{2,4},{3,5},{4,2},{5,3},{6,0},{7,1},{8,14},{9,15},{10,... | collective-permute-start | bytes 460808 | tf_op jit(solution)/shard_map/ppermute | solution.py:81
  27.5 0.6 collective-permute-start.7
  28.1 0.5 collective-permute-start.8
  28.6 1.7 %collective-permute-start.11 = (bf16[64,384]{1,0:T(8,128)(2,1)S(1)}, bf16[64,384]{1,0:T(8,128)(2,1)S(1)}, u32[]{:S(2)}, u32[]{:S(2)}) collective-permute-start(bf16[64,384]{1,0:T(8,128)(2,1)S(1)} %get-tuple-element.81), channel_id=1, source_target_pairs={{0,24},{1,25},{2,26},{3,27},{4,28},{5,29},{6,30},{7,31},{8,16},{9,... | collective-permute-start | bytes 147464 | tf_op jit(solution)/shard_map/ppermute | solution.py:81
  30.3 0.3 collective-permute-start.12
  30.6 2.2 %collective-permute-done.6 = bf16[200,384]{1,0:T(8,128)(2,1)S(1)} collective-permute-done((bf16[200,384]{1,0:T(8,128)(2,1)S(1)}, bf16[200,384]{1,0:T(8,128)(2,1)S(1)}, u32[]{:S(2)}, u32[]{:S(2)}) %collective-permute-start.6) | collective-permute-done | bytes 153632 | tf_op jit(solution)/shard_map/ppermute | solution.py:81
  32.9 0.2 collective-permute-start.13
  33.0 2.3 %collective-permute-done.7 = bf16[200,384]{1,0:T(8,128)(2,1)S(1)} collective-permute-done((bf16[200,384]{1,0:T(8,128)(2,1)S(1)}, bf16[200,384]{1,0:T(8,128)(2,1)S(1)}, u32[]{:S(2)}, u32[]{:S(2)}) %collective-permute-start.7) | collective-permute-done | bytes 153632 | tf_op jit(solution)/shard_map/ppermute | solution.py:81
  35.3 0.1 fusion.1
  35.4 0.0 collective-permute-done.11.refs_0_
  35.5 0.4 collective-permute-done.12.refs_1_
  35.9 1.1 %collective-permute-done.13.refs_2_ = bf16[64,384]{1,0:T(8,128)(2,1)S(1)} collective-permute-done((bf16[64,384]{1,0:T(8,128)(2,1)S(1)}, bf16[64,384]{1,0:T(8,128)(2,1)S(1)}, u32[]{:S(2)}, u32[]{:S(2)}) %collective-permute-start.13) | collective-permute-done | bytes 49184 | tf_op jit(solution)/shard_map/ppermute | solution.py:81
  37.0 0.2 collective-permute-start.9
  37.2 1.6 %collective-permute-start.15 = (bf16[128,384]{1,0:T(8,128)(2,1)S(1)}, bf16[128,384]{1,0:T(8,128)(2,1)S(1)}, u32[]{:S(2)}, u32[]{:S(2)}) collective-permute-start(bf16[128,384]{1,0:T(8,128)(2,1)S(1)} %pad_maximum_fusion.3), channel_id=1, source_target_pairs={{0,4},{1,5},{2,6},{3,7},{4,0},{5,1},{6,2},{7,3},{8,12},{9,13},{10,... | collective-permute-start | bytes 294920 | tf_op jit(solution)/shard_map/ppermute | solution.py:81
  38.8 0.0 collective-permute-start.14
  38.8 2.7 %collective-permute-done.9 = bf16[104,384]{1,0:T(8,128)(2,1)S(1)} collective-permute-done((bf16[104,384]{1,0:T(8,128)(2,1)S(1)}, bf16[104,384]{1,0:T(8,128)(2,1)S(1)}, u32[]{:S(2)}, u32[]{:S(2)}) %collective-permute-start.9) | collective-permute-done | bytes 79904 | tf_op jit(solution)/shard_map/ppermute | solution.py:81
  41.5 2.1 %collective-permute-start.10 = (bf16[104,384]{1,0:T(8,128)(2,1)S(1)}, bf16[104,384]{1,0:T(8,128)(2,1)S(1)}, u32[]{:S(2)}, u32[]{:S(2)}) collective-permute-start(bf16[104,384]{1,0:T(8,128)(2,1)S(1)} %pad_maximum_fusion.5), channel_id=1, source_target_pairs={{0,16},{1,17},{2,18},{3,19},{4,20},{5,21},{6,22},{7,23},{8,24},{9,... | collective-permute-start | bytes 239624 | tf_op jit(solution)/shard_map/ppermute | solution.py:81
  43.6 0.0 collective-permute-done.15.through_ref
  43.6 1.0 %return_rows.1 = f32[256,384]{1,0:T(8,128)} custom-call(f32[256,384]{1,0:T(8,128)S(1)} %get-tuple-element.75.gf_ref, bf16[256,256]{1,0:T(8,128)(2,1)S(1)} %get-tuple-element.76.chosen_ref, bf16[128,384]{1,0:T(8,128)(2,1)S(1)} %collective-permute-done.14.halo_ref, bf16[64,384]{1,0:T(8,128)(2,1)S(1)} %get-tuple-element.86.own_ref, ...), custom_call_target="tpu_custom_call" | custom-call | bytes 1310720 | tf_op jit(solution)/shard_map/return_rows/pallas_call | solution.py:473
  44.6 2.8 %collective-permute-done.10 = bf16[104,384]{1,0:T(8,128)(2,1)S(1)} collective-permute-done((bf16[104,384]{1,0:T(8,128)(2,1)S(1)}, bf16[104,384]{1,0:T(8,128)(2,1)S(1)}, u32[]{:S(2)}, u32[]{:S(2)}) %collective-permute-start.10) | collective-permute-done | bytes 79904 | tf_op jit(solution)/shard_map/ppermute | solution.py:81
  47.5 0.1 collective-permute-start.16
  47.5 4.3 %collective-permute-done.16 = bf16[96,384]{1,0:T(8,128)(2,1)S(1)} collective-permute-done((bf16[96,384]{1,0:T(8,128)(2,1)S(1)}, bf16[96,384]{1,0:T(8,128)(2,1)S(1)}, u32[]{:S(2)}, u32[]{:S(2)}) %collective-permute-start.16) | collective-permute-done | bytes 73760 | tf_op jit(solution)/shard_map/ppermute | solution.py:81
  51.9 2.9 %collective-permute-start.19 = (bf16[192,384]{1,0:T(8,128)(2,1)S(1)}, bf16[192,384]{1,0:T(8,128)(2,1)S(1)}, u32[]{:S(2)}, u32[]{:S(2)}) collective-permute-start(bf16[192,384]{1,0:T(8,128)(2,1)S(1)} %constant_dynamic-update-slice_fusion.refs_0_), channel_id=1, source_target_pairs={{0,6},{1,7},{2,4},{3,5},{4,2},{5,3},{6,0},{7,1},{8,14},{9,15},{10,... | collective-permute-start | bytes 442376 | tf_op jit(solution)/shard_map/ppermute | solution.py:81
  54.8 0.1 collective-permute-start.18
  54.9 0.6 collective-permute-start.17
  55.4 2.5 %collective-permute-done.19.refs_3_ = bf16[192,384]{1,0:T(8,128)(2,1)S(1)} collective-permute-done((bf16[192,384]{1,0:T(8,128)(2,1)S(1)}, bf16[192,384]{1,0:T(8,128)(2,1)S(1)}, u32[]{:S(2)}, u32[]{:S(2)}) %collective-permute-start.19) | collective-permute-done | bytes 147488 | tf_op jit(solution)/shard_map/ppermute | solution.py:81
  58.0 1.9 %collective-permute-done.18.refs_2_ = bf16[192,384]{1,0:T(8,128)(2,1)S(1)} collective-permute-done((bf16[192,384]{1,0:T(8,128)(2,1)S(1)}, bf16[192,384]{1,0:T(8,128)(2,1)S(1)}, u32[]{:S(2)}, u32[]{:S(2)}) %collective-permute-start.18) | collective-permute-done | bytes 147488 | tf_op jit(solution)/shard_map/ppermute | solution.py:81
  59.9 0.1 collective-permute-done.17.refs_1_
  60.0 0.4 collective-permute-start.21
  60.4 0.6 convert_add_fusion.1
  61.1 0.3 collective-permute-done.22.refs_6_
  61.3 0.2 collective-permute-done.21.refs_5_
  61.5 1.6 %place_sums.1 = (f32[384,384]{1,0:T(8,128)}, f32[384,768]{1,0:T(8,128)}, f32[384,384]{1,0:T(8,128)}) custom-call(bf16[192,384]{1,0:T(8,128)(2,1)S(1)} %constant_dynamic-update-slice_fusion.refs_0_, bf16[192,384]{1,0:T(8,128)(2,1)S(1)} %collective-permute-done.17.refs_1_, bf16[192,384]{1,0:T(8,128)(2,1)S(1)} %collective-permute-done.18.refs_2_, ...), custom_call_target="tpu_custom_call" | custom-call | bytes 3538944 | tf_op jit(solution)/shard_map/place_sums/pallas_call | solution.py:473
  (32 shorter events, 0.3 us)
Async XLA Ops:
  1.9 5.9 %collective-permute-start = (bf16[128,384]{1,0:T(8,128)(2,1)S(1)}, bf16[128,384]{1,0:T(8,128)(2,1)S(1)}, u32[]{:S(2)}, u32[]{:S(2)}) collective-permute-start(bf16[128,384]{1,0:T(8,128)(2,1)S(1)} %get-tuple-element.54), channel_id=1, source_target_pairs={{0,4},{1,5},{2,6},{3,7},{4,0},{5,1},{6,2},{7,3},{8,12},{9,13},{10,... | collective-permute-start | bytes 294920 | tf_op jit(solution)/shard_map/ppermute | solution.py:81
  7.8 6.5 %collective-permute-start.1 = (bf16[64,384]{1,0:T(8,128)(2,1)S(1)}, bf16[64,384]{1,0:T(8,128)(2,1)S(1)}, u32[]{:S(2)}, u32[]{:S(2)}) collective-permute-start(bf16[64,384]{1,0:T(8,128)(2,1)S(1)} %pad_maximum_fusion.6), channel_id=1, source_target_pairs={{0,24},{1,25},{2,26},{3,27},{4,28},{5,29},{6,30},{7,31},{8,16},{9,... | collective-permute-start | bytes 147464 | tf_op jit(solution)/shard_map/ppermute | solution.py:81
  11.7 5.1 %collective-permute-start.2 = (bf16[64,384]{1,0:T(8,128)(2,1)S(1)}, bf16[64,384]{1,0:T(8,128)(2,1)S(1)}, u32[]{:S(2)}, u32[]{:S(2)}) collective-permute-start(bf16[64,384]{1,0:T(8,128)(2,1)S(1)} %pad_maximum_fusion.7), channel_id=1, source_target_pairs={{0,16},{1,17},{2,18},{3,19},{4,20},{5,21},{6,22},{7,23},{8,24},{9,... | collective-permute-start | bytes 147464 | tf_op jit(solution)/shard_map/ppermute | solution.py:81
  11.7 5.1 %collective-permute-start.4 = (bf16[128,384]{1,0:T(8,128)(2,1)S(1)}, bf16[128,384]{1,0:T(8,128)(2,1)S(1)}, u32[]{:S(2)}, u32[]{:S(2)}) collective-permute-start(bf16[128,384]{1,0:T(8,128)(2,1)S(1)} %get-tuple-element.60), channel_id=1, source_target_pairs={{3,0},{0,1},{1,2},{2,3},{7,4},{4,5},{5,6},{6,7},{11,8},{8,9},{9,10... | collective-permute-start | bytes 294920 | tf_op jit(solution)/shard_map/ppermute | solution.py:87
  11.8 5.0 %collective-permute-start.3 = (bf16[64,384]{1,0:T(8,128)(2,1)S(1)}, bf16[64,384]{1,0:T(8,128)(2,1)S(1)}, u32[]{:S(2)}, u32[]{:S(2)}) collective-permute-start(bf16[64,384]{1,0:T(8,128)(2,1)S(1)} %pad_maximum_fusion.8), channel_id=1, source_target_pairs={{0,8},{1,9},{2,10},{3,11},{4,12},{5,13},{6,14},{7,15},{8,0},{9,1},... | collective-permute-start | bytes 147464 | tf_op jit(solution)/shard_map/ppermute | solution.py:81
  22.7 2.1 %collective-permute-start.5 = (bf16[784,384]{1,0:T(8,128)(2,1)S(1)}, bf16[784,384]{1,0:T(8,128)(2,1)S(1)}, u32[]{:S(2)}, u32[]{:S(2)}) collective-permute-start(bf16[784,384]{1,0:T(8,128)(2,1)S(1)} %get-tuple-element.73), channel_id=1, source_target_pairs={{0,1},{1,0},{2,3},{3,2},{4,5},{5,4},{6,7},{7,6},{8,9},{9,8},{10,11... | collective-permute-start | bytes 1806344 | tf_op jit(solution)/shard_map/ppermute | solution.py:81
  25.1 7.8 %collective-permute-start.6 = (bf16[200,384]{1,0:T(8,128)(2,1)S(1)}, bf16[200,384]{1,0:T(8,128)(2,1)S(1)}, u32[]{:S(2)}, u32[]{:S(2)}) collective-permute-start(bf16[200,384]{1,0:T(8,128)(2,1)S(1)} %get-tuple-element.103), channel_id=1, source_target_pairs={{0,6},{1,7},{2,4},{3,5},{4,2},{5,3},{6,0},{7,1},{8,14},{9,15},{10,... | collective-permute-start | bytes 460808 | tf_op jit(solution)/shard_map/ppermute | solution.py:81
  27.5 7.9 %collective-permute-start.7 = (bf16[200,384]{1,0:T(8,128)(2,1)S(1)}, bf16[200,384]{1,0:T(8,128)(2,1)S(1)}, u32[]{:S(2)}, u32[]{:S(2)}) collective-permute-start(bf16[200,384]{1,0:T(8,128)(2,1)S(1)} %get-tuple-element.104), channel_id=1, source_target_pairs={{0,2},{1,3},{2,0},{3,1},{4,6},{5,7},{6,4},{7,5},{8,10},{9,11},{10,... | collective-permute-start | bytes 460808 | tf_op jit(solution)/shard_map/ppermute | solution.py:81
  28.1 7.3 %collective-permute-start.8 = (bf16[200,384]{1,0:T(8,128)(2,1)S(1)}, bf16[200,384]{1,0:T(8,128)(2,1)S(1)}, u32[]{:S(2)}, u32[]{:S(2)}) collective-permute-start(bf16[200,384]{1,0:T(8,128)(2,1)S(1)} %get-tuple-element.105), channel_id=1, source_target_pairs={{0,4},{1,5},{2,6},{3,7},{4,0},{5,1},{6,2},{7,3},{8,12},{9,13},{10,... | collective-permute-start | bytes 460808 | tf_op jit(solution)/shard_map/ppermute | solution.py:81
  28.6 6.8 %collective-permute-start.11 = (bf16[64,384]{1,0:T(8,128)(2,1)S(1)}, bf16[64,384]{1,0:T(8,128)(2,1)S(1)}, u32[]{:S(2)}, u32[]{:S(2)}) collective-permute-start(bf16[64,384]{1,0:T(8,128)(2,1)S(1)} %get-tuple-element.81), channel_id=1, source_target_pairs={{0,24},{1,25},{2,26},{3,27},{4,28},{5,29},{6,30},{7,31},{8,16},{9,... | collective-permute-start | bytes 147464 | tf_op jit(solution)/shard_map/ppermute | solution.py:81
  30.3 5.5 %collective-permute-start.12 = (bf16[64,384]{1,0:T(8,128)(2,1)S(1)}, bf16[64,384]{1,0:T(8,128)(2,1)S(1)}, u32[]{:S(2)}, u32[]{:S(2)}) collective-permute-start(bf16[64,384]{1,0:T(8,128)(2,1)S(1)} %get-tuple-element.82), channel_id=1, source_target_pairs={{0,16},{1,17},{2,18},{3,19},{4,20},{5,21},{6,22},{7,23},{8,24},{9,... | collective-permute-start | bytes 147464 | tf_op jit(solution)/shard_map/ppermute | solution.py:81
  32.9 4.1 %collective-permute-start.13 = (bf16[64,384]{1,0:T(8,128)(2,1)S(1)}, bf16[64,384]{1,0:T(8,128)(2,1)S(1)}, u32[]{:S(2)}, u32[]{:S(2)}) collective-permute-start(bf16[64,384]{1,0:T(8,128)(2,1)S(1)} %get-tuple-element.83), channel_id=1, source_target_pairs={{0,8},{1,9},{2,10},{3,11},{4,12},{5,13},{6,14},{7,15},{8,0},{9,1},... | collective-permute-start | bytes 147464 | tf_op jit(solution)/shard_map/ppermute | solution.py:81
  37.0 4.5 %collective-permute-start.9 = (bf16[104,384]{1,0:T(8,128)(2,1)S(1)}, bf16[104,384]{1,0:T(8,128)(2,1)S(1)}, u32[]{:S(2)}, u32[]{:S(2)}) collective-permute-start(bf16[104,384]{1,0:T(8,128)(2,1)S(1)} %pad_maximum_fusion.4), channel_id=1, source_target_pairs={{0,8},{1,9},{2,10},{3,11},{4,12},{5,13},{6,14},{7,15},{8,0},{9,1},... | collective-permute-start | bytes 239624 | tf_op jit(solution)/shard_map/ppermute | solution.py:81
  37.2 6.4 %collective-permute-start.15 = (bf16[128,384]{1,0:T(8,128)(2,1)S(1)}, bf16[128,384]{1,0:T(8,128)(2,1)S(1)}, u32[]{:S(2)}, u32[]{:S(2)}) collective-permute-start(bf16[128,384]{1,0:T(8,128)(2,1)S(1)} %pad_maximum_fusion.3), channel_id=1, source_target_pairs={{0,4},{1,5},{2,6},{3,7},{4,0},{5,1},{6,2},{7,3},{8,12},{9,13},{10,... | collective-permute-start | bytes 294920 | tf_op jit(solution)/shard_map/ppermute | solution.py:81
  38.8 4.8 %collective-permute-start.14 = (bf16[128,384]{1,0:T(8,128)(2,1)S(1)}, bf16[128,384]{1,0:T(8,128)(2,1)S(1)}, u32[]{:S(2)}, u32[]{:S(2)}) collective-permute-start(bf16[128,384]{1,0:T(8,128)(2,1)S(1)} %get-tuple-element.85), channel_id=1, source_target_pairs={{1,0},{2,1},{3,2},{0,3},{5,4},{6,5},{7,6},{4,7},{9,8},{10,9},{11,1... | collective-permute-start | bytes 294920 | tf_op jit(solution)/shard_map/ppermute | solution.py:87
  41.5 5.9 %collective-permute-start.10 = (bf16[104,384]{1,0:T(8,128)(2,1)S(1)}, bf16[104,384]{1,0:T(8,128)(2,1)S(1)}, u32[]{:S(2)}, u32[]{:S(2)}) collective-permute-start(bf16[104,384]{1,0:T(8,128)(2,1)S(1)} %pad_maximum_fusion.5), channel_id=1, source_target_pairs={{0,16},{1,17},{2,18},{3,19},{4,20},{5,21},{6,22},{7,23},{8,24},{9,... | collective-permute-start | bytes 239624 | tf_op jit(solution)/shard_map/ppermute | solution.py:81
  47.5 4.4 %collective-permute-start.16 = (bf16[96,384]{1,0:T(8,128)(2,1)S(1)}, bf16[96,384]{1,0:T(8,128)(2,1)S(1)}, u32[]{:S(2)}, u32[]{:S(2)}) collective-permute-start(bf16[96,384]{1,0:T(8,128)(2,1)S(1)} %add_convert_fusion), channel_id=1, source_target_pairs={{0,8},{1,9},{2,10},{3,11},{4,12},{5,13},{6,14},{7,15},{8,0},{9,1},... | collective-permute-start | bytes 221192 | tf_op jit(solution)/shard_map/ppermute | solution.py:81
  51.9 6.1 %collective-permute-start.19 = (bf16[192,384]{1,0:T(8,128)(2,1)S(1)}, bf16[192,384]{1,0:T(8,128)(2,1)S(1)}, u32[]{:S(2)}, u32[]{:S(2)}) collective-permute-start(bf16[192,384]{1,0:T(8,128)(2,1)S(1)} %constant_dynamic-update-slice_fusion.refs_0_), channel_id=1, source_target_pairs={{0,6},{1,7},{2,4},{3,5},{4,2},{5,3},{6,0},{7,1},{8,14},{9,15},{10,... | collective-permute-start | bytes 442376 | tf_op jit(solution)/shard_map/ppermute | solution.py:81
  54.8 5.1 %collective-permute-start.18 = (bf16[192,384]{1,0:T(8,128)(2,1)S(1)}, bf16[192,384]{1,0:T(8,128)(2,1)S(1)}, u32[]{:S(2)}, u32[]{:S(2)}) collective-permute-start(bf16[192,384]{1,0:T(8,128)(2,1)S(1)} %constant_dynamic-update-slice_fusion.refs_0_), channel_id=1, source_target_pairs={{0,2},{1,3},{2,0},{3,1},{4,6},{5,7},{6,4},{7,5},{8,10},{9,11},{10,... | collective-permute-start | bytes 442376 | tf_op jit(solution)/shard_map/ppermute | solution.py:81
  54.9 5.1 %collective-permute-start.17 = (bf16[192,384]{1,0:T(8,128)(2,1)S(1)}, bf16[192,384]{1,0:T(8,128)(2,1)S(1)}, u32[]{:S(2)}, u32[]{:S(2)}) collective-permute-start(bf16[192,384]{1,0:T(8,128)(2,1)S(1)} %constant_dynamic-update-slice_fusion.refs_0_), channel_id=1, source_target_pairs={{0,4},{1,5},{2,6},{3,7},{4,0},{5,1},{6,2},{7,3},{8,12},{9,13},{10,... | collective-permute-start | bytes 442376 | tf_op jit(solution)/shard_map/ppermute | solution.py:81
  55.4 5.6 %collective-permute-start.20 = (bf16[192,384]{1,0:T(8,128)(2,1)S(1)}, bf16[192,384]{1,0:T(8,128)(2,1)S(1)}, u32[]{:S(2)}, u32[]{:S(2)}) collective-permute-start(bf16[192,384]{1,0:T(8,128)(2,1)S(1)} %constant_dynamic-update-slice_fusion.refs_0_), channel_id=1, source_target_pairs={{0,1},{1,0},{2,3},{3,2},{4,5},{5,4},{6,7},{7,6},{8,9},{9,8},{10,11... | collective-permute-start | bytes 442376 | tf_op jit(solution)/shard_map/ppermute | solution.py:81
  58.0 3.1 %collective-permute-start.23 = (bf16[192,384]{1,0:T(8,128)(2,1)S(1)}, bf16[192,384]{1,0:T(8,128)(2,1)S(1)}, u32[]{:S(2)}, u32[]{:S(2)}) collective-permute-start(bf16[192,384]{1,0:T(8,128)(2,1)S(1)} %collective-permute-done.19.refs_3_), channel_id=1, source_target_pairs={{0,1},{1,0},{2,3},{3,2},{4,5},{5,4},{6,7},{7,6},{8,9},{9,8},{10,11... | collective-permute-start | bytes 442376 | tf_op jit(solution)/shard_map/ppermute | solution.py:81
  59.9 1.4 %collective-permute-start.22 = (bf16[192,384]{1,0:T(8,128)(2,1)S(1)}, bf16[192,384]{1,0:T(8,128)(2,1)S(1)}, u32[]{:S(2)}, u32[]{:S(2)}) collective-permute-start(bf16[192,384]{1,0:T(8,128)(2,1)S(1)} %collective-permute-done.18.refs_2_), channel_id=1, source_target_pairs={{0,1},{1,0},{2,3},{3,2},{4,5},{5,4},{6,7},{7,6},{8,9},{9,8},{10,11... | collective-permute-start | bytes 442376 | tf_op jit(solution)/shard_map/ppermute | solution.py:81
  60.0 1.5 %collective-permute-start.21 = (bf16[192,384]{1,0:T(8,128)(2,1)S(1)}, bf16[192,384]{1,0:T(8,128)(2,1)S(1)}, u32[]{:S(2)}, u32[]{:S(2)}) collective-permute-start(bf16[192,384]{1,0:T(8,128)(2,1)S(1)} %collective-permute-done.17.refs_1_), channel_id=1, source_target_pairs={{0,1},{1,0},{2,3},{3,2},{4,5},{5,4},{6,7},{7,6},{8,9},{9,8},{10,11... | collective-permute-start | bytes 442376 | tf_op jit(solution)/shard_map/ppermute | solution.py:81

commit v15 on v14

--- a/solution.py
+++ b/solution.py
@@ -568,10 +568,11 @@
     pairs, _ = lax.optimization_barrier((pairs, keep))
     returned = [swapped(pairs[at], 2 * at, 0) for at in reversed(range(1, dom_size // 2))]
     keep, rider = scattered(keep, rider, square)
+    keep, *returned[:-1] = lax.optimization_barrier((keep, *returned[:-1]))
+    keep, rider = scattered(keep, rider, pair)
     (returned, halo_feat), _ = lax.optimization_barrier(((returned, halo_feat), keep))
     through = swapped(jnp.concatenate([x[per_peer:] for x in [pairs[0]] + returned[::-1]]), 1, 0)
     halo_back = shifted(halo_feat, "rows", -1)
-    keep, rider = scattered(keep, rider, pair)
     for mask in rest:
         message = swapped(with_rider(keep, rider), *mask)
         keep, rider = rounded(keep).astype(f32), rounded(rider).astype(f32)
@@ -583,8 +584,9 @@
         [own_feat, chosen, halo_back, pairs[0], through, *returned],
     )
 
-    held, grad_features = lax.optimization_barrier((rounded(keep), grad_features))
+    held = rounded(keep)
     held = jnp.concatenate([held, swapped(held, *pair[0])], axis=0)
+    held, grad_features = lax.optimization_barrier((held, grad_features))
     arrived = [swapped(held, *masks) for masks in partner_masks(square)[1:]]
     near = [held, *arrived]
     far = [swapped(part, *CORES) for part in near]

time: 63.4 us -> 63.2 us (level)
  waiting for transfers between devices: 25.8 us -> 23.4 us
  starting transfers between devices: 21.3 us -> 23.4 us
    ppermute x22, waiting for transfers between devices: 25.8 us -> 23.4 us  [swapped(): return lax.ppermute(block, ('dom', 'rows'), route)]
    ppermute x22, starting transfers between devices: 21.2 us -> 23.4 us  [swapped(): return lax.ppermute(block, ('dom', 'rows'), route)]
  transfers between devices with their start and end apart: 24 -> 24, of which waited for: 15 -> 16; matrix products, arithmetic and copies ran while one was open for 1% -> 1% of each run, Pallas kernels for 8% -> 9%
where the time goes in v15:
time: 63.2 us; the launch traced here: 62.9 us
  starting transfers between devices  23.4 us (37%)
  waiting for transfers between devices  23.4 us (37%)
  Pallas kernels  14.1 us (22%)
  other arithmetic  1 us (2%)
  between operations  0.83 us (1%)
    ppermute x22, waiting for transfers between devices, swapped(): return lax.ppermute(block, ('dom', 'rows'), route)  23.4 us
    ppermute x22, starting transfers between devices, swapped(): return lax.ppermute(block, ('dom', 'rows'), route)  23.4 us
    pallas_call x6, Pallas kernels, call(): pl.pallas_call(kernel, out_shape=outs, in_specs=[pl.BlockSpec(memory_spac...  14.1 us
  transfers between devices with their start and end apart: 24, of which 16 were waited for; matrix products, arithmetic and copies ran while one was open for 1% of the time, Pallas kernels for 9%

profile of v15, /device:TPU:0, one launch (start us, length us, event | category | flops | bytes accessed | tf_op | source)
XLA Modules:
  0.0 62.9 jit_solution(17640622272113545574)
XLA Ops:
  0.6 1.2 %pick_rows.1 = (bf16[128,384]{1,0:T(8,128)(2,1)S(1)}, bf16[256,256]{1,0:T(8,128)(2,1)S(1)}, bf16[128,384]{1,0:T(8,128)(2,1)S(1)}, bf16[32,384]{1,0:T(8,128)(2,1)...) custom-call(bf16[256,384]{1,0:T(8,128)(2,1)} %feat_hbm.3, ...), custom_call_target="tpu_custom_call" | custom-call | bytes 623616 | tf_op jit(solution)/shard_map/pick_rows/pallas_call | solution.py:473
  1.9 3.0 %collective-permute-start = (bf16[128,384]{1,0:T(8,128)(2,1)S(1)}, bf16[128,384]{1,0:T(8,128)(2,1)S(1)}, u32[]{:S(2)}, u32[]{:S(2)}) collective-permute-start(bf16[128,384]{1,0:T(8,128)(2,1)S(1)} %get-tuple-element.57), channel_id=1, source_target_pairs={{0,4},{1,5},{2,6},{3,7},{4,0},{5,1},{6,2},{7,3},{8,12},{9,13},{10,... | collective-permute-start | bytes 294920 | tf_op jit(solution)/shard_map/ppermute | solution.py:81
  4.9 2.9 %prepare.1 = (bf16[256,384]{1,0:T(8,128)(2,1)S(1)}, bf16[384,384]{1,0:T(8,128)(2,1)S(1)}, bf16[384,768]{1,0:T(8,128)(2,1)S(1)}, bf16[384,272]{1,0:T(8,128)(2,1)S...) custom-call(bf16[256,384]{1,0:T(8,128)(2,1)} %feat_hbm.3, ...), custom_call_target="tpu_custom_call" | custom-call | flops 377487360 | bytes 4656128 | tf_op jit(solution)/shard_map/prepare/pallas_call | solution.py:473
  7.8 3.9 %collective-permute-start.1 = (bf16[64,384]{1,0:T(8,128)(2,1)S(1)}, bf16[64,384]{1,0:T(8,128)(2,1)S(1)}, u32[]{:S(2)}, u32[]{:S(2)}) collective-permute-start(bf16[64,384]{1,0:T(8,128)(2,1)S(1)} %pad_maximum_fusion.7), channel_id=1, source_target_pairs={{0,24},{1,25},{2,26},{3,27},{4,28},{5,29},{6,30},{7,31},{8,16},{9,... | collective-permute-start | bytes 147464 | tf_op jit(solution)/shard_map/ppermute | solution.py:81
  11.7 0.1 collective-permute-start.4
  11.8 0.6 %collective-permute-start.3 = (bf16[64,384]{1,0:T(8,128)(2,1)S(1)}, bf16[64,384]{1,0:T(8,128)(2,1)S(1)}, u32[]{:S(2)}, u32[]{:S(2)}) collective-permute-start(bf16[64,384]{1,0:T(8,128)(2,1)S(1)} %pad_maximum_fusion.9), channel_id=1, source_target_pairs={{0,8},{1,9},{2,10},{3,11},{4,12},{5,13},{6,14},{7,15},{8,0},{9,1},... | collective-permute-start | bytes 147464 | tf_op jit(solution)/shard_map/ppermute | solution.py:81
  12.4 1.9 %collective-permute-done.1.refs_2_ = bf16[64,384]{1,0:T(8,128)(2,1)S(1)} collective-permute-done((bf16[64,384]{1,0:T(8,128)(2,1)S(1)}, bf16[64,384]{1,0:T(8,128)(2,1)S(1)}, u32[]{:S(2)}, u32[]{:S(2)}) %collective-permute-start.1) | collective-permute-done | bytes 49184 | tf_op jit(solution)/shard_map/ppermute | solution.py:81
  14.3 2.5 %collective-permute-done.2.refs_3_ = bf16[64,384]{1,0:T(8,128)(2,1)S(1)} collective-permute-done((bf16[64,384]{1,0:T(8,128)(2,1)S(1)}, bf16[64,384]{1,0:T(8,128)(2,1)S(1)}, u32[]{:S(2)}, u32[]{:S(2)}) %collective-permute-start.2) | collective-permute-done | bytes 49184 | tf_op jit(solution)/shard_map/ppermute | solution.py:81
  16.8 0.0 collective-permute-done.3.refs_4_
  16.8 0.0 collective-permute-done.4.refs_5_
  16.8 5.9 %attend.1 = (bf16[784,384]{1,0:T(8,128)(2,1)S(1)}, f32[16,384]{1,0:T(8,128)S(1)}, bf16[384,656]{1,0:T(8,128)(2,1)S(1)}, bf16[384,256]{1,0:T(8,128)(2,1)S(1)}, bf...) custom-call(bf16[32,384]{1,0:T(8,128)(2,1)S(1)} %get-tuple-element.56.refs_0_, ...), custom_call_target="tpu_custom_call" | custom-call | flops 2708471808 | bytes 5959680 | tf_op jit(solution)/shard_map/attend/pallas_call | solution.py:473
  22.7 0.1 collective-permute-start.5
  22.8 1.5 %finish.1 = (f32[256,384]{1,0:T(8,128)S(1)}, bf16[128,384]{1,0:T(8,128)(2,1)S(1)}, f32[768,384]{1,0:T(8,128)S(1)}, bf16[64,384]{1,0:T(8,128)(2,1)S(1)}, bf16[64,...) custom-call(bf16[256,384]{1,0:T(8,128)(2,1)S(1)} %get-tuple-element.53.refs_6_.og_ref, ...), custom_call_target="tpu_custom_call" | custom-call | flops 580386816 | bytes 4853760 | tf_op jit(solution)/shard_map/finish/pallas_call | solution.py:473
  24.2 0.5 collective-permute-done.5
  24.8 0.1 fusion.2
  25.1 2.4 %collective-permute-start.6 = (bf16[200,384]{1,0:T(8,128)(2,1)S(1)}, bf16[200,384]{1,0:T(8,128)(2,1)S(1)}, u32[]{:S(2)}, u32[]{:S(2)}) collective-permute-start(bf16[200,384]{1,0:T(8,128)(2,1)S(1)} %get-tuple-element.109), channel_id=1, source_target_pairs={{0,6},{1,7},{2,4},{3,5},{4,2},{5,3},{6,0},{7,1},{8,14},{9,15},{10,... | collective-permute-start | bytes 460808 | tf_op jit(solution)/shard_map/ppermute | solution.py:81
  27.5 0.6 collective-permute-start.7
  28.1 0.5 collective-permute-start.8
  28.6 1.7 %collective-permute-start.9 = (bf16[64,384]{1,0:T(8,128)(2,1)S(1)}, bf16[64,384]{1,0:T(8,128)(2,1)S(1)}, u32[]{:S(2)}, u32[]{:S(2)}) collective-permute-start(bf16[64,384]{1,0:T(8,128)(2,1)S(1)} %get-tuple-element.82), channel_id=1, source_target_pairs={{0,24},{1,25},{2,26},{3,27},{4,28},{5,29},{6,30},{7,31},{8,16},{9,... | collective-permute-start | bytes 147464 | tf_op jit(solution)/shard_map/ppermute | solution.py:81
  30.3 0.3 collective-permute-start.10
  30.6 2.2 %collective-permute-done.6 = bf16[200,384]{1,0:T(8,128)(2,1)S(1)} collective-permute-done((bf16[200,384]{1,0:T(8,128)(2,1)S(1)}, bf16[200,384]{1,0:T(8,128)(2,1)S(1)}, u32[]{:S(2)}, u32[]{:S(2)}) %collective-permute-start.6) | collective-permute-done | bytes 153632 | tf_op jit(solution)/shard_map/ppermute | solution.py:81
  32.9 2.5 %collective-permute-done.7 = bf16[200,384]{1,0:T(8,128)(2,1)S(1)} collective-permute-done((bf16[200,384]{1,0:T(8,128)(2,1)S(1)}, bf16[200,384]{1,0:T(8,128)(2,1)S(1)}, u32[]{:S(2)}, u32[]{:S(2)}) %collective-permute-start.7) | collective-permute-done | bytes 153632 | tf_op jit(solution)/shard_map/ppermute | solution.py:81
  35.3 0.0 collective-permute-done.8
  35.3 0.1 fusion.1
  35.4 0.0 collective-permute-done.9.refs_0_
  35.4 0.4 collective-permute-done.10.refs_1_
  35.9 0.5 collective-permute-start.11
  36.4 1.6 %collective-permute-start.14 = (bf16[64,384]{1,0:T(8,128)(2,1)S(1)}, bf16[64,384]{1,0:T(8,128)(2,1)S(1)}, u32[]{:S(2)}, u32[]{:S(2)}) collective-permute-start(bf16[64,384]{1,0:T(8,128)(2,1)S(1)} %get-tuple-element.89), channel_id=1, source_target_pairs={{0,8},{1,9},{2,10},{3,11},{4,12},{5,13},{6,14},{7,15},{8,0},{9,1},... | collective-permute-start | bytes 147464 | tf_op jit(solution)/shard_map/ppermute | solution.py:81
  38.0 2.4 %collective-permute-done.11 = bf16[104,384]{1,0:T(8,128)(2,1)S(1)} collective-permute-done((bf16[104,384]{1,0:T(8,128)(2,1)S(1)}, bf16[104,384]{1,0:T(8,128)(2,1)S(1)}, u32[]{:S(2)}, u32[]{:S(2)}) %collective-permute-start.11) | collective-permute-done | bytes 79904 | tf_op jit(solution)/shard_map/ppermute | solution.py:81
  40.4 0.5 collective-permute-done.14.refs_2_
  41.0 2.3 %collective-permute-start.12 = (bf16[104,384]{1,0:T(8,128)(2,1)S(1)}, bf16[104,384]{1,0:T(8,128)(2,1)S(1)}, u32[]{:S(2)}, u32[]{:S(2)}) collective-permute-start(bf16[104,384]{1,0:T(8,128)(2,1)S(1)} %pad_maximum_fusion.6), channel_id=1, source_target_pairs={{0,16},{1,17},{2,18},{3,19},{4,20},{5,21},{6,22},{7,23},{8,24},{9,... | collective-permute-start | bytes 239624 | tf_op jit(solution)/shard_map/ppermute | solution.py:81
  43.3 1.6 %collective-permute-start.16 = (bf16[128,384]{1,0:T(8,128)(2,1)S(1)}, bf16[128,384]{1,0:T(8,128)(2,1)S(1)}, u32[]{:S(2)}, u32[]{:S(2)}) collective-permute-start(bf16[128,384]{1,0:T(8,128)(2,1)S(1)} %pad_maximum_fusion.4), channel_id=1, source_target_pairs={{0,4},{1,5},{2,6},{3,7},{4,0},{5,1},{6,2},{7,3},{8,12},{9,13},{10,... | collective-permute-start | bytes 294920 | tf_op jit(solution)/shard_map/ppermute | solution.py:81
  44.8 2.4 %collective-permute-done.12 = bf16[104,384]{1,0:T(8,128)(2,1)S(1)} collective-permute-done((bf16[104,384]{1,0:T(8,128)(2,1)S(1)}, bf16[104,384]{1,0:T(8,128)(2,1)S(1)}, u32[]{:S(2)}, u32[]{:S(2)}) %collective-permute-start.12) | collective-permute-done | bytes 79904 | tf_op jit(solution)/shard_map/ppermute | solution.py:81
  47.3 0.5 collective-permute-start.13
  47.7 0.3 collective-permute-done.16.through_ref
  48.0 1.0 %return_rows.1 = f32[256,384]{1,0:T(8,128)} custom-call(f32[256,384]{1,0:T(8,128)S(1)} %get-tuple-element.85.gf_ref, bf16[256,256]{1,0:T(8,128)(2,1)S(1)} %get-tuple-element.86.chosen_ref, bf16[128,384]{1,0:T(8,128)(2,1)S(1)} %collective-permute-done.15.halo_ref, bf16[64,384]{1,0:T(8,128)(2,1)S(1)} %get-tuple-element.92.own_ref, ...), custom_call_target="tpu_custom_call" | custom-call | bytes 1310720 | tf_op jit(solution)/shard_map/return_rows/pallas_call | solution.py:473
  49.0 2.7 %collective-permute-done.13 = bf16[96,384]{1,0:T(8,128)(2,1)S(1)} collective-permute-done((bf16[96,384]{1,0:T(8,128)(2,1)S(1)}, bf16[96,384]{1,0:T(8,128)(2,1)S(1)}, u32[]{:S(2)}, u32[]{:S(2)}) %collective-permute-start.13) | collective-permute-done | bytes 73760 | tf_op jit(solution)/shard_map/ppermute | solution.py:81
  51.7 2.8 %collective-permute-start.19 = (bf16[192,384]{1,0:T(8,128)(2,1)S(1)}, bf16[192,384]{1,0:T(8,128)(2,1)S(1)}, u32[]{:S(2)}, u32[]{:S(2)}) collective-permute-start(bf16[192,384]{1,0:T(8,128)(2,1)S(1)} %pad_maximum_fusion.3.refs_0_), channel_id=1, source_target_pairs={{0,6},{1,7},{2,4},{3,5},{4,2},{5,3},{6,0},{7,1},{8,14},{9,15},{10,... | collective-permute-start | bytes 442376 | tf_op jit(solution)/shard_map/ppermute | solution.py:81
  54.5 0.3 collective-permute-start.18
  54.7 0.5 collective-permute-start.17
  55.3 2.5 %collective-permute-done.19.refs_3_ = bf16[192,384]{1,0:T(8,128)(2,1)S(1)} collective-permute-done((bf16[192,384]{1,0:T(8,128)(2,1)S(1)}, bf16[192,384]{1,0:T(8,128)(2,1)S(1)}, u32[]{:S(2)}, u32[]{:S(2)}) %collective-permute-start.19) | collective-permute-done | bytes 147488 | tf_op jit(solution)/shard_map/ppermute | solution.py:81
  57.8 1.8 %collective-permute-done.18.refs_2_ = bf16[192,384]{1,0:T(8,128)(2,1)S(1)} collective-permute-done((bf16[192,384]{1,0:T(8,128)(2,1)S(1)}, bf16[192,384]{1,0:T(8,128)(2,1)S(1)}, u32[]{:S(2)}, u32[]{:S(2)}) %collective-permute-start.18) | collective-permute-done | bytes 147488 | tf_op jit(solution)/shard_map/ppermute | solution.py:81
  59.6 0.3 collective-permute-done.17.refs_1_
  59.9 0.3 collective-permute-start.21
  60.1 0.6 convert_add_fusion.2
  60.7 0.3 collective-permute-done.22.refs_6_
  61.0 0.3 collective-permute-done.21.refs_5_
  61.2 1.6 %place_sums.1 = (f32[384,384]{1,0:T(8,128)}, f32[384,768]{1,0:T(8,128)}, f32[384,384]{1,0:T(8,128)}) custom-call(bf16[192,384]{1,0:T(8,128)(2,1)S(1)} %pad_maximum_fusion.3.refs_0_, bf16[192,384]{1,0:T(8,128)(2,1)S(1)} %collective-permute-done.17.refs_1_, bf16[192,384]{1,0:T(8,128)(2,1)S(1)} %collective-permute-done.18.refs_2_, ...), custom_call_target="tpu_custom_call" | custom-call | bytes 3538944 | tf_op jit(solution)/shard_map/place_sums/pallas_call | solution.py:473
  (31 shorter events, 0.3 us)
Async XLA Ops:
  1.9 5.9 %collective-permute-start = (bf16[128,384]{1,0:T(8,128)(2,1)S(1)}, bf16[128,384]{1,0:T(8,128)(2,1)S(1)}, u32[]{:S(2)}, u32[]{:S(2)}) collective-permute-start(bf16[128,384]{1,0:T(8,128)(2,1)S(1)} %get-tuple-element.57), channel_id=1, source_target_pairs={{0,4},{1,5},{2,6},{3,7},{4,0},{5,1},{6,2},{7,3},{8,12},{9,13},{10,... | collective-permute-start | bytes 294920 | tf_op jit(solution)/shard_map/ppermute | solution.py:81
  7.8 6.5 %collective-permute-start.1 = (bf16[64,384]{1,0:T(8,128)(2,1)S(1)}, bf16[64,384]{1,0:T(8,128)(2,1)S(1)}, u32[]{:S(2)}, u32[]{:S(2)}) collective-permute-start(bf16[64,384]{1,0:T(8,128)(2,1)S(1)} %pad_maximum_fusion.7), channel_id=1, source_target_pairs={{0,24},{1,25},{2,26},{3,27},{4,28},{5,29},{6,30},{7,31},{8,16},{9,... | collective-permute-start | bytes 147464 | tf_op jit(solution)/shard_map/ppermute | solution.py:81
  11.7 5.1 %collective-permute-start.2 = (bf16[64,384]{1,0:T(8,128)(2,1)S(1)}, bf16[64,384]{1,0:T(8,128)(2,1)S(1)}, u32[]{:S(2)}, u32[]{:S(2)}) collective-permute-start(bf16[64,384]{1,0:T(8,128)(2,1)S(1)} %pad_maximum_fusion.8), channel_id=1, source_target_pairs={{0,16},{1,17},{2,18},{3,19},{4,20},{5,21},{6,22},{7,23},{8,24},{9,... | collective-permute-start | bytes 147464 | tf_op jit(solution)/shard_map/ppermute | solution.py:81
  11.7 5.1 %collective-permute-start.4 = (bf16[128,384]{1,0:T(8,128)(2,1)S(1)}, bf16[128,384]{1,0:T(8,128)(2,1)S(1)}, u32[]{:S(2)}, u32[]{:S(2)}) collective-permute-start(bf16[128,384]{1,0:T(8,128)(2,1)S(1)} %get-tuple-element.63), channel_id=1, source_target_pairs={{3,0},{0,1},{1,2},{2,3},{7,4},{4,5},{5,6},{6,7},{11,8},{8,9},{9,10... | collective-permute-start | bytes 294920 | tf_op jit(solution)/shard_map/ppermute | solution.py:87
  11.8 5.0 %collective-permute-start.3 = (bf16[64,384]{1,0:T(8,128)(2,1)S(1)}, bf16[64,384]{1,0:T(8,128)(2,1)S(1)}, u32[]{:S(2)}, u32[]{:S(2)}) collective-permute-start(bf16[64,384]{1,0:T(8,128)(2,1)S(1)} %pad_maximum_fusion.9), channel_id=1, source_target_pairs={{0,8},{1,9},{2,10},{3,11},{4,12},{5,13},{6,14},{7,15},{8,0},{9,1},... | collective-permute-start | bytes 147464 | tf_op jit(solution)/shard_map/ppermute | solution.py:81
  22.7 2.1 %collective-permute-start.5 = (bf16[784,384]{1,0:T(8,128)(2,1)S(1)}, bf16[784,384]{1,0:T(8,128)(2,1)S(1)}, u32[]{:S(2)}, u32[]{:S(2)}) collective-permute-start(bf16[784,384]{1,0:T(8,128)(2,1)S(1)} %get-tuple-element.76), channel_id=1, source_target_pairs={{0,1},{1,0},{2,3},{3,2},{4,5},{5,4},{6,7},{7,6},{8,9},{9,8},{10,11... | collective-permute-start | bytes 1806344 | tf_op jit(solution)/shard_map/ppermute | solution.py:81
  25.1 7.8 %collective-permute-start.6 = (bf16[200,384]{1,0:T(8,128)(2,1)S(1)}, bf16[200,384]{1,0:T(8,128)(2,1)S(1)}, u32[]{:S(2)}, u32[]{:S(2)}) collective-permute-start(bf16[200,384]{1,0:T(8,128)(2,1)S(1)} %get-tuple-element.109), channel_id=1, source_target_pairs={{0,6},{1,7},{2,4},{3,5},{4,2},{5,3},{6,0},{7,1},{8,14},{9,15},{10,... | collective-permute-start | bytes 460808 | tf_op jit(solution)/shard_map/ppermute | solution.py:81
  27.5 7.9 %collective-permute-start.7 = (bf16[200,384]{1,0:T(8,128)(2,1)S(1)}, bf16[200,384]{1,0:T(8,128)(2,1)S(1)}, u32[]{:S(2)}, u32[]{:S(2)}) collective-permute-start(bf16[200,384]{1,0:T(8,128)(2,1)S(1)} %get-tuple-element.110), channel_id=1, source_target_pairs={{0,2},{1,3},{2,0},{3,1},{4,6},{5,7},{6,4},{7,5},{8,10},{9,11},{10,... | collective-permute-start | bytes 460808 | tf_op jit(solution)/shard_map/ppermute | solution.py:81
  28.1 7.3 %collective-permute-start.8 = (bf16[200,384]{1,0:T(8,128)(2,1)S(1)}, bf16[200,384]{1,0:T(8,128)(2,1)S(1)}, u32[]{:S(2)}, u32[]{:S(2)}) collective-permute-start(bf16[200,384]{1,0:T(8,128)(2,1)S(1)} %get-tuple-element.111), channel_id=1, source_target_pairs={{0,4},{1,5},{2,6},{3,7},{4,0},{5,1},{6,2},{7,3},{8,12},{9,13},{10,... | collective-permute-start | bytes 460808 | tf_op jit(solution)/shard_map/ppermute | solution.py:81
  28.6 6.8 %collective-permute-start.9 = (bf16[64,384]{1,0:T(8,128)(2,1)S(1)}, bf16[64,384]{1,0:T(8,128)(2,1)S(1)}, u32[]{:S(2)}, u32[]{:S(2)}) collective-permute-start(bf16[64,384]{1,0:T(8,128)(2,1)S(1)} %get-tuple-element.82), channel_id=1, source_target_pairs={{0,24},{1,25},{2,26},{3,27},{4,28},{5,29},{6,30},{7,31},{8,16},{9,... | collective-permute-start | bytes 147464 | tf_op jit(solution)/shard_map/ppermute | solution.py:81
  30.3 5.5 %collective-permute-start.10 = (bf16[64,384]{1,0:T(8,128)(2,1)S(1)}, bf16[64,384]{1,0:T(8,128)(2,1)S(1)}, u32[]{:S(2)}, u32[]{:S(2)}) collective-permute-start(bf16[64,384]{1,0:T(8,128)(2,1)S(1)} %get-tuple-element.83), channel_id=1, source_target_pairs={{0,16},{1,17},{2,18},{3,19},{4,20},{5,21},{6,22},{7,23},{8,24},{9,... | collective-permute-start | bytes 147464 | tf_op jit(solution)/shard_map/ppermute | solution.py:81
  35.9 4.5 %collective-permute-start.11 = (bf16[104,384]{1,0:T(8,128)(2,1)S(1)}, bf16[104,384]{1,0:T(8,128)(2,1)S(1)}, u32[]{:S(2)}, u32[]{:S(2)}) collective-permute-start(bf16[104,384]{1,0:T(8,128)(2,1)S(1)} %pad_maximum_fusion.5), channel_id=1, source_target_pairs={{0,8},{1,9},{2,10},{3,11},{4,12},{5,13},{6,14},{7,15},{8,0},{9,1},... | collective-permute-start | bytes 239624 | tf_op jit(solution)/shard_map/ppermute | solution.py:81
  36.4 4.5 %collective-permute-start.14 = (bf16[64,384]{1,0:T(8,128)(2,1)S(1)}, bf16[64,384]{1,0:T(8,128)(2,1)S(1)}, u32[]{:S(2)}, u32[]{:S(2)}) collective-permute-start(bf16[64,384]{1,0:T(8,128)(2,1)S(1)} %get-tuple-element.89), channel_id=1, source_target_pairs={{0,8},{1,9},{2,10},{3,11},{4,12},{5,13},{6,14},{7,15},{8,0},{9,1},... | collective-permute-start | bytes 147464 | tf_op jit(solution)/shard_map/ppermute | solution.py:81
  41.0 6.2 %collective-permute-start.12 = (bf16[104,384]{1,0:T(8,128)(2,1)S(1)}, bf16[104,384]{1,0:T(8,128)(2,1)S(1)}, u32[]{:S(2)}, u32[]{:S(2)}) collective-permute-start(bf16[104,384]{1,0:T(8,128)(2,1)S(1)} %pad_maximum_fusion.6), channel_id=1, source_target_pairs={{0,16},{1,17},{2,18},{3,19},{4,20},{5,21},{6,22},{7,23},{8,24},{9,... | collective-permute-start | bytes 239624 | tf_op jit(solution)/shard_map/ppermute | solution.py:81
  43.3 4.7 %collective-permute-start.16 = (bf16[128,384]{1,0:T(8,128)(2,1)S(1)}, bf16[128,384]{1,0:T(8,128)(2,1)S(1)}, u32[]{:S(2)}, u32[]{:S(2)}) collective-permute-start(bf16[128,384]{1,0:T(8,128)(2,1)S(1)} %pad_maximum_fusion.4), channel_id=1, source_target_pairs={{0,4},{1,5},{2,6},{3,7},{4,0},{5,1},{6,2},{7,3},{8,12},{9,13},{10,... | collective-permute-start | bytes 294920 | tf_op jit(solution)/shard_map/ppermute | solution.py:81
  44.8 3.1 %collective-permute-start.15 = (bf16[128,384]{1,0:T(8,128)(2,1)S(1)}, bf16[128,384]{1,0:T(8,128)(2,1)S(1)}, u32[]{:S(2)}, u32[]{:S(2)}) collective-permute-start(bf16[128,384]{1,0:T(8,128)(2,1)S(1)} %get-tuple-element.91), channel_id=1, source_target_pairs={{1,0},{2,1},{3,2},{0,3},{5,4},{6,5},{7,6},{4,7},{9,8},{10,9},{11,1... | collective-permute-start | bytes 294920 | tf_op jit(solution)/shard_map/ppermute | solution.py:87
  47.3 4.4 %collective-permute-start.13 = (bf16[96,384]{1,0:T(8,128)(2,1)S(1)}, bf16[96,384]{1,0:T(8,128)(2,1)S(1)}, u32[]{:S(2)}, u32[]{:S(2)}) collective-permute-start(bf16[96,384]{1,0:T(8,128)(2,1)S(1)} %add_convert_fusion), channel_id=1, source_target_pairs={{0,8},{1,9},{2,10},{3,11},{4,12},{5,13},{6,14},{7,15},{8,0},{9,1},... | collective-permute-start | bytes 221192 | tf_op jit(solution)/shard_map/ppermute | solution.py:81
  51.7 6.1 %collective-permute-start.19 = (bf16[192,384]{1,0:T(8,128)(2,1)S(1)}, bf16[192,384]{1,0:T(8,128)(2,1)S(1)}, u32[]{:S(2)}, u32[]{:S(2)}) collective-permute-start(bf16[192,384]{1,0:T(8,128)(2,1)S(1)} %pad_maximum_fusion.3.refs_0_), channel_id=1, source_target_pairs={{0,6},{1,7},{2,4},{3,5},{4,2},{5,3},{6,0},{7,1},{8,14},{9,15},{10,... | collective-permute-start | bytes 442376 | tf_op jit(solution)/shard_map/ppermute | solution.py:81
  54.5 5.1 %collective-permute-start.18 = (bf16[192,384]{1,0:T(8,128)(2,1)S(1)}, bf16[192,384]{1,0:T(8,128)(2,1)S(1)}, u32[]{:S(2)}, u32[]{:S(2)}) collective-permute-start(bf16[192,384]{1,0:T(8,128)(2,1)S(1)} %pad_maximum_fusion.3.refs_0_), channel_id=1, source_target_pairs={{0,2},{1,3},{2,0},{3,1},{4,6},{5,7},{6,4},{7,5},{8,10},{9,11},{10,... | collective-permute-start | bytes 442376 | tf_op jit(solution)/shard_map/ppermute | solution.py:81
  54.7 5.1 %collective-permute-start.17 = (bf16[192,384]{1,0:T(8,128)(2,1)S(1)}, bf16[192,384]{1,0:T(8,128)(2,1)S(1)}, u32[]{:S(2)}, u32[]{:S(2)}) collective-permute-start(bf16[192,384]{1,0:T(8,128)(2,1)S(1)} %pad_maximum_fusion.3.refs_0_), channel_id=1, source_target_pairs={{0,4},{1,5},{2,6},{3,7},{4,0},{5,1},{6,2},{7,3},{8,12},{9,13},{10,... | collective-permute-start | bytes 442376 | tf_op jit(solution)/shard_map/ppermute | solution.py:81
  55.2 5.5 %collective-permute-start.20 = (bf16[192,384]{1,0:T(8,128)(2,1)S(1)}, bf16[192,384]{1,0:T(8,128)(2,1)S(1)}, u32[]{:S(2)}, u32[]{:S(2)}) collective-permute-start(bf16[192,384]{1,0:T(8,128)(2,1)S(1)} %pad_maximum_fusion.3.refs_0_), channel_id=1, source_target_pairs={{0,1},{1,0},{2,3},{3,2},{4,5},{5,4},{6,7},{7,6},{8,9},{9,8},{10,11... | collective-permute-start | bytes 442376 | tf_op jit(solution)/shard_map/ppermute | solution.py:81
  57.8 2.9 %collective-permute-start.23 = (bf16[192,384]{1,0:T(8,128)(2,1)S(1)}, bf16[192,384]{1,0:T(8,128)(2,1)S(1)}, u32[]{:S(2)}, u32[]{:S(2)}) collective-permute-start(bf16[192,384]{1,0:T(8,128)(2,1)S(1)} %collective-permute-done.19.refs_3_), channel_id=1, source_target_pairs={{0,1},{1,0},{2,3},{3,2},{4,5},{5,4},{6,7},{7,6},{8,9},{9,8},{10,11... | collective-permute-start | bytes 442376 | tf_op jit(solution)/shard_map/ppermute | solution.py:81
  59.6 1.4 %collective-permute-start.22 = (bf16[192,384]{1,0:T(8,128)(2,1)S(1)}, bf16[192,384]{1,0:T(8,128)(2,1)S(1)}, u32[]{:S(2)}, u32[]{:S(2)}) collective-permute-start(bf16[192,384]{1,0:T(8,128)(2,1)S(1)} %collective-permute-done.18.refs_2_), channel_id=1, source_target_pairs={{0,1},{1,0},{2,3},{3,2},{4,5},{5,4},{6,7},{7,6},{8,9},{9,8},{10,11... | collective-permute-start | bytes 442376 | tf_op jit(solution)/shard_map/ppermute | solution.py:81
  59.9 1.4 %collective-permute-start.21 = (bf16[192,384]{1,0:T(8,128)(2,1)S(1)}, bf16[192,384]{1,0:T(8,128)(2,1)S(1)}, u32[]{:S(2)}, u32[]{:S(2)}) collective-permute-start(bf16[192,384]{1,0:T(8,128)(2,1)S(1)} %collective-permute-done.17.refs_1_), channel_id=1, source_target_pairs={{0,1},{1,0},{2,3},{3,2},{4,5},{5,4},{6,7},{7,6},{8,9},{9,8},{10,11... | collective-permute-start | bytes 442376 | tf_op jit(solution)/shard_map/ppermute | solution.py:81

commit v16 on v15

--- a/solution.py
+++ b/solution.py
@@ -45,9 +45,9 @@
 
 def exchange_plan():
     dom_size, rows_size = lax.axis_size("dom"), lax.axis_size("rows")
-    pair, square = [(2, 0)], [(1, 0), (0, 2)]
-    rest = [(bit, 0) for bit in bits_of(dom_size, 4)] + [(0, bit) for bit in bits_of(rows_size, 4)]
-    return pair, square, rest
+    square = [(1, 0), (0, 2)]
+    rest = [(bit, 0) for bit in bits_of(dom_size, 2)] + [(0, bit) for bit in bits_of(rows_size, 4)]
+    return square, rest
 
 
 def partner_masks(block):
@@ -63,9 +63,9 @@
 
 
 def own_digit():
-    pair, square, _ = exchange_plan()
+    square, _ = exchange_plan()
     digit = 0
-    for i, (dom_mask, rows_mask) in enumerate(pair + square):
+    for i, (dom_mask, rows_mask) in enumerate(square):
         own = (lax.axis_index("dom") & dom_mask) | (lax.axis_index("rows") & rows_mask)
         digit += jnp.where(own != 0, 1 << i, 0)
     return digit
@@ -375,8 +375,8 @@
 def weight_sums(core, out_ref, extt_ref, gqt_ref, gkvt_ref, ot_ref, og_ref, factor):
     width, row_count = gqt_ref.shape
     held = own_digit()
-    pair, square, _ = exchange_plan()
-    rows = 2 * width >> len(pair + square)
+    square, _ = exchange_plan()
+    rows = 2 * width >> len(square)
 
     def write(at, total):
         total = (total * factor).astype(out_ref.dtype)
@@ -419,8 +419,8 @@
 def place_kernel(*refs):
     part_refs, (gq_hbm, gkv_hbm, go_hbm, all_ref, out_ref, sems) = refs[:-6], refs[-6:]
     width = gq_hbm.shape[0]
-    pair, square, _ = exchange_plan()
-    half = 1 << len(pair + square)
+    square, _ = exchange_plan()
+    half = 1 << len(square)
     rows = 2 * width // half
     step = part_refs[0].shape[0]
     for at, part_ref in enumerate(part_refs):
@@ -490,7 +490,7 @@
     padded = ROW_PACK * -(-virt_rows // ROW_PACK)
     ext_rows = TILE + row_count + slots + padded
     nodes = row_count * lax.axis_size("dom") * lax.axis_size("rows")
-    pair, square, rest = exchange_plan()
+    square, rest = exchange_plan()
     bf16, f32 = jnp.bfloat16, jnp.float32
     shape = jax.ShapeDtypeStruct
 
@@ -569,14 +569,15 @@
     returned = [swapped(pairs[at], 2 * at, 0) for at in reversed(range(1, dom_size // 2))]
     keep, rider = scattered(keep, rider, square)
     keep, *returned[:-1] = lax.optimization_barrier((keep, *returned[:-1]))
-    keep, rider = scattered(keep, rider, pair)
-    (returned, halo_feat), _ = lax.optimization_barrier(((returned, halo_feat), keep))
-    through = swapped(jnp.concatenate([x[per_peer:] for x in [pairs[0]] + returned[::-1]]), 1, 0)
-    halo_back = shifted(halo_feat, "rows", -1)
-    for mask in rest:
+    for at, mask in enumerate(rest):
         message = swapped(with_rider(keep, rider), *mask)
         keep, rider = rounded(keep).astype(f32), rounded(rider).astype(f32)
         keep, rider = added(keep, rider, {1: message})
+        if at == 0:
+            (returned, halo_feat), _ = lax.optimization_barrier(((returned, halo_feat), keep))
+            odd = [block[per_peer:] for block in [pairs[0]] + returned[::-1]]
+            through = swapped(jnp.concatenate(odd, axis=0), 1, 0)
+            halo_back = shifted(halo_feat, "rows", -1)
     (grad_features,) = call(
         return_kernel,
         "return_rows",
@@ -585,7 +586,6 @@
     )
 
     held = rounded(keep)
-    held = jnp.concatenate([held, swapped(held, *pair[0])], axis=0)
     held, grad_features = lax.optimization_barrier((held, grad_features))
     arrived = [swapped(held, *masks) for masks in partner_masks(square)[1:]]
     near = [held, *arrived]
@@ -598,7 +598,7 @@
         [
             pltpu.VMEM((4 * width, width), bf16),
             pltpu.VMEM((4 * width, width), f32),
-            pltpu.SemaphoreType.DMA((2 << len(pair + square),)),
+            pltpu.SemaphoreType.DMA((2 << len(square),)),
         ],
         stored=True,
     )

time: 63.2 us -> 63.7 us (level)
  waiting for transfers between devices: 23.4 us -> 24.4 us
    ppermute x22 -> x21, waiting for transfers between devices: 23.4 us -> 24.4 us  [swapped(): return lax.ppermute(block, ('dom', 'rows'), route)]
    ppermute x22 -> x21, starting transfers between devices: 23.4 us -> 23 us  [swapped(): return lax.ppermute(block, ('dom', 'rows'), route)]
  transfers between devices with their start and end apart: 24 -> 23, of which waited for: 16 -> 13; matrix products, arithmetic and copies ran while one was open for 1% -> 1% of each run, Pallas kernels for 9% -> 8%
where the time goes in v16:
time: 63.7 us; the launch traced here: 63.4 us
  waiting for transfers between devices  24.4 us (38%)
  starting transfers between devices  23 us (36%)
  Pallas kernels  14 us (22%)
  other arithmetic  1.05 us (2%)
  between operations  0.83 us (1%)
    ppermute x21, waiting for transfers between devices, swapped(): return lax.ppermute(block, ('dom', 'rows'), route)  24.4 us
    ppermute x21, starting transfers between devices, swapped(): return lax.ppermute(block, ('dom', 'rows'), route)  23 us
    pallas_call x6, Pallas kernels, call(): pl.pallas_call(kernel, out_shape=outs, in_specs=[pl.BlockSpec(memory_spac...  14 us
  transfers between devices with their start and end apart: 23, of which 13 were waited for; matrix products, arithmetic and copies ran while one was open for 1% of the time, Pallas kernels for 8%

profile of v16, /device:TPU:0, one launch (start us, length us, event | category | flops | bytes accessed | tf_op | source)
XLA Modules:
  0.0 63.4 jit_solution(11548621482406383413)
XLA Ops:
  0.6 1.2 %pick_rows.1 = (bf16[128,384]{1,0:T(8,128)(2,1)S(1)}, bf16[256,256]{1,0:T(8,128)(2,1)S(1)}, bf16[128,384]{1,0:T(8,128)(2,1)S(1)}, bf16[32,384]{1,0:T(8,128)(2,1)...) custom-call(bf16[256,384]{1,0:T(8,128)(2,1)} %feat_hbm.3, ...), custom_call_target="tpu_custom_call" | custom-call | bytes 623616 | tf_op jit(solution)/shard_map/pick_rows/pallas_call | solution.py:473
  1.9 3.0 %collective-permute-start = (bf16[128,384]{1,0:T(8,128)(2,1)S(1)}, bf16[128,384]{1,0:T(8,128)(2,1)S(1)}, u32[]{:S(2)}, u32[]{:S(2)}) collective-permute-start(bf16[128,384]{1,0:T(8,128)(2,1)S(1)} %get-tuple-element.57), channel_id=1, source_target_pairs={{0,4},{1,5},{2,6},{3,7},{4,0},{5,1},{6,2},{7,3},{8,12},{9,13},{10,... | collective-permute-start | bytes 294920 | tf_op jit(solution)/shard_map/ppermute | solution.py:81
  4.9 2.9 %prepare.1 = (bf16[256,384]{1,0:T(8,128)(2,1)S(1)}, bf16[384,384]{1,0:T(8,128)(2,1)S(1)}, bf16[384,768]{1,0:T(8,128)(2,1)S(1)}, bf16[384,272]{1,0:T(8,128)(2,1)S...) custom-call(bf16[256,384]{1,0:T(8,128)(2,1)} %feat_hbm.3, ...), custom_call_target="tpu_custom_call" | custom-call | flops 377487360 | bytes 4656128 | tf_op jit(solution)/shard_map/prepare/pallas_call | solution.py:473
  7.7 0.0 collective-permute-done.refs_1_
  7.8 3.9 %collective-permute-start.1 = (bf16[64,384]{1,0:T(8,128)(2,1)S(1)}, bf16[64,384]{1,0:T(8,128)(2,1)S(1)}, u32[]{:S(2)}, u32[]{:S(2)}) collective-permute-start(bf16[64,384]{1,0:T(8,128)(2,1)S(1)} %pad_maximum_fusion.6), channel_id=1, source_target_pairs={{0,24},{1,25},{2,26},{3,27},{4,28},{5,29},{6,30},{7,31},{8,16},{9,... | collective-permute-start | bytes 147464 | tf_op jit(solution)/shard_map/ppermute | solution.py:81
  11.7 0.0 collective-permute-start.2
  11.7 0.1 collective-permute-start.4
  11.8 0.6 %collective-permute-start.3 = (bf16[64,384]{1,0:T(8,128)(2,1)S(1)}, bf16[64,384]{1,0:T(8,128)(2,1)S(1)}, u32[]{:S(2)}, u32[]{:S(2)}) collective-permute-start(bf16[64,384]{1,0:T(8,128)(2,1)S(1)} %pad_maximum_fusion.8), channel_id=1, source_target_pairs={{0,8},{1,9},{2,10},{3,11},{4,12},{5,13},{6,14},{7,15},{8,0},{9,1},... | collective-permute-start | bytes 147464 | tf_op jit(solution)/shard_map/ppermute | solution.py:81
  12.4 1.9 %collective-permute-done.1.refs_2_ = bf16[64,384]{1,0:T(8,128)(2,1)S(1)} collective-permute-done((bf16[64,384]{1,0:T(8,128)(2,1)S(1)}, bf16[64,384]{1,0:T(8,128)(2,1)S(1)}, u32[]{:S(2)}, u32[]{:S(2)}) %collective-permute-start.1) | collective-permute-done | bytes 49184 | tf_op jit(solution)/shard_map/ppermute | solution.py:81
  14.3 2.5 %collective-permute-done.2.refs_3_ = bf16[64,384]{1,0:T(8,128)(2,1)S(1)} collective-permute-done((bf16[64,384]{1,0:T(8,128)(2,1)S(1)}, bf16[64,384]{1,0:T(8,128)(2,1)S(1)}, u32[]{:S(2)}, u32[]{:S(2)}) %collective-permute-start.2) | collective-permute-done | bytes 49184 | tf_op jit(solution)/shard_map/ppermute | solution.py:81
  16.8 0.0 collective-permute-done.4.refs_5_
  16.8 5.9 %attend.1 = (bf16[784,384]{1,0:T(8,128)(2,1)S(1)}, f32[16,384]{1,0:T(8,128)S(1)}, bf16[384,656]{1,0:T(8,128)(2,1)S(1)}, bf16[384,256]{1,0:T(8,128)(2,1)S(1)}, bf...) custom-call(bf16[32,384]{1,0:T(8,128)(2,1)S(1)} %get-tuple-element.56.refs_0_, ...), custom_call_target="tpu_custom_call" | custom-call | flops 2708471808 | bytes 5959680 | tf_op jit(solution)/shard_map/attend/pallas_call | solution.py:473
  22.7 0.1 collective-permute-start.5
  22.8 1.5 %finish.1 = (f32[256,384]{1,0:T(8,128)S(1)}, bf16[128,384]{1,0:T(8,128)(2,1)S(1)}, f32[768,384]{1,0:T(8,128)S(1)}, bf16[64,384]{1,0:T(8,128)(2,1)S(1)}, bf16[64,...) custom-call(bf16[256,384]{1,0:T(8,128)(2,1)S(1)} %get-tuple-element.53.refs_6_.og_ref, ...), custom_call_target="tpu_custom_call" | custom-call | flops 580386816 | bytes 4853760 | tf_op jit(solution)/shard_map/finish/pallas_call | solution.py:473
  24.2 0.5 collective-permute-done.5
  24.8 0.1 fusion.3
  25.1 1.6 %collective-permute-start.8 = (bf16[200,384]{1,0:T(8,128)(2,1)S(1)}, bf16[200,384]{1,0:T(8,128)(2,1)S(1)}, u32[]{:S(2)}, u32[]{:S(2)}) collective-permute-start(bf16[200,384]{1,0:T(8,128)(2,1)S(1)} %get-tuple-element.109), channel_id=1, source_target_pairs={{0,4},{1,5},{2,6},{3,7},{4,0},{5,1},{6,2},{7,3},{8,12},{9,13},{10,... | collective-permute-start | bytes 460808 | tf_op jit(solution)/shard_map/ppermute | solution.py:81
  26.6 1.4 %collective-permute-start.7 = (bf16[200,384]{1,0:T(8,128)(2,1)S(1)}, bf16[200,384]{1,0:T(8,128)(2,1)S(1)}, u32[]{:S(2)}, u32[]{:S(2)}) collective-permute-start(bf16[200,384]{1,0:T(8,128)(2,1)S(1)} %get-tuple-element.110), channel_id=1, source_target_pairs={{0,2},{1,3},{2,0},{3,1},{4,6},{5,7},{6,4},{7,5},{8,10},{9,11},{10,... | collective-permute-start | bytes 460808 | tf_op jit(solution)/shard_map/ppermute | solution.py:81
  28.0 0.6 collective-permute-start.6
  28.6 1.7 %collective-permute-start.9 = (bf16[64,384]{1,0:T(8,128)(2,1)S(1)}, bf16[64,384]{1,0:T(8,128)(2,1)S(1)}, u32[]{:S(2)}, u32[]{:S(2)}) collective-permute-start(bf16[64,384]{1,0:T(8,128)(2,1)S(1)} %get-tuple-element.82), channel_id=1, source_target_pairs={{0,24},{1,25},{2,26},{3,27},{4,28},{5,29},{6,30},{7,31},{8,16},{9,... | collective-permute-start | bytes 147464 | tf_op jit(solution)/shard_map/ppermute | solution.py:81
  30.3 0.3 collective-permute-start.10
  30.6 1.3 %collective-permute-done.8 = bf16[200,384]{1,0:T(8,128)(2,1)S(1)} collective-permute-done((bf16[200,384]{1,0:T(8,128)(2,1)S(1)}, bf16[200,384]{1,0:T(8,128)(2,1)S(1)}, u32[]{:S(2)}, u32[]{:S(2)}) %collective-permute-start.8) | collective-permute-done | bytes 153632 | tf_op jit(solution)/shard_map/ppermute | solution.py:81
  32.0 3.7 %collective-permute-done.7 = bf16[200,384]{1,0:T(8,128)(2,1)S(1)} collective-permute-done((bf16[200,384]{1,0:T(8,128)(2,1)S(1)}, bf16[200,384]{1,0:T(8,128)(2,1)S(1)}, u32[]{:S(2)}, u32[]{:S(2)}) %collective-permute-start.7) | collective-permute-done | bytes 153632 | tf_op jit(solution)/shard_map/ppermute | solution.py:81
  35.7 0.0 collective-permute-done.6
  35.7 0.1 fusion.1
  35.7 0.0 collective-permute-done.9.refs_0_
  35.8 0.1 collective-permute-done.10.refs_1_
  35.9 0.5 collective-permute-start.11
  36.4 1.6 %collective-permute-start.13 = (bf16[64,384]{1,0:T(8,128)(2,1)S(1)}, bf16[64,384]{1,0:T(8,128)(2,1)S(1)}, u32[]{:S(2)}, u32[]{:S(2)}) collective-permute-start(bf16[64,384]{1,0:T(8,128)(2,1)S(1)} %get-tuple-element.89), channel_id=1, source_target_pairs={{0,8},{1,9},{2,10},{3,11},{4,12},{5,13},{6,14},{7,15},{8,0},{9,1},... | collective-permute-start | bytes 147464 | tf_op jit(solution)/shard_map/ppermute | solution.py:81
  38.0 4.0 %collective-permute-done.13.refs_2_ = bf16[64,384]{1,0:T(8,128)(2,1)S(1)} collective-permute-done((bf16[64,384]{1,0:T(8,128)(2,1)S(1)}, bf16[64,384]{1,0:T(8,128)(2,1)S(1)}, u32[]{:S(2)}, u32[]{:S(2)}) %collective-permute-start.13) | collective-permute-done | bytes 49184 | tf_op jit(solution)/shard_map/ppermute | solution.py:81
  42.0 0.0 collective-permute-done.11
  42.1 2.1 %collective-permute-start.12 = (bf16[200,384]{1,0:T(8,128)(2,1)S(1)}, bf16[200,384]{1,0:T(8,128)(2,1)S(1)}, u32[]{:S(2)}, u32[]{:S(2)}) collective-permute-start(bf16[200,384]{1,0:T(8,128)(2,1)S(1)} %pad_maximum_fusion.4), channel_id=1, source_target_pairs={{0,16},{1,17},{2,18},{3,19},{4,20},{5,21},{6,22},{7,23},{8,24},{9,... | collective-permute-start | bytes 460808 | tf_op jit(solution)/shard_map/ppermute | solution.py:81
  44.2 1.5 %collective-permute-start.15 = (bf16[128,384]{1,0:T(8,128)(2,1)S(1)}, bf16[128,384]{1,0:T(8,128)(2,1)S(1)}, u32[]{:S(2)}, u32[]{:S(2)}) collective-permute-start(bf16[128,384]{1,0:T(8,128)(2,1)S(1)} %pad_maximum_fusion.5), channel_id=1, source_target_pairs={{0,4},{1,5},{2,6},{3,7},{4,0},{5,1},{6,2},{7,3},{8,12},{9,13},{10,... | collective-permute-start | bytes 294920 | tf_op jit(solution)/shard_map/ppermute | solution.py:81
  45.7 0.0 collective-permute-start.14
  45.7 3.2 %collective-permute-done.15.through_ref = bf16[128,384]{1,0:T(8,128)(2,1)S(1)} collective-permute-done((bf16[128,384]{1,0:T(8,128)(2,1)S(1)}, bf16[128,384]{1,0:T(8,128)(2,1)S(1)}, u32[]{:S(2)}, u32[]{:S(2)}) %collective-permute-start.15) | collective-permute-done | bytes 98336 | tf_op jit(solution)/shard_map/ppermute | solution.py:81
  48.9 0.0 collective-permute-done.14.halo_ref
  48.9 1.0 %return_rows.1 = f32[256,384]{1,0:T(8,128)} custom-call(f32[256,384]{1,0:T(8,128)S(1)} %get-tuple-element.85.gf_ref, bf16[256,256]{1,0:T(8,128)(2,1)S(1)} %get-tuple-element.86.chosen_ref, bf16[128,384]{1,0:T(8,128)(2,1)S(1)} %collective-permute-done.14.halo_ref, bf16[64,384]{1,0:T(8,128)(2,1)S(1)} %get-tuple-element.92.own_ref, ...), custom_call_target="tpu_custom_call" | custom-call | bytes 1310720 | tf_op jit(solution)/shard_map/return_rows/pallas_call | solution.py:473
  49.9 0.5 collective-permute-done.12
  50.4 1.8 %collective-permute-start.18 = (bf16[192,384]{1,0:T(8,128)(2,1)S(1)}, bf16[192,384]{1,0:T(8,128)(2,1)S(1)}, u32[]{:S(2)}, u32[]{:S(2)}) collective-permute-start(bf16[192,384]{1,0:T(8,128)(2,1)S(1)} %add_convert_fusion.refs_0_), channel_id=1, source_target_pairs={{0,6},{1,7},{2,4},{3,5},{4,2},{5,3},{6,0},{7,1},{8,14},{9,15},{10,... | collective-permute-start | bytes 442376 | tf_op jit(solution)/shard_map/ppermute | solution.py:81
  52.2 1.2 %collective-permute-start.17 = (bf16[192,384]{1,0:T(8,128)(2,1)S(1)}, bf16[192,384]{1,0:T(8,128)(2,1)S(1)}, u32[]{:S(2)}, u32[]{:S(2)}) collective-permute-start(bf16[192,384]{1,0:T(8,128)(2,1)S(1)} %add_convert_fusion.refs_0_), channel_id=1, source_target_pairs={{0,2},{1,3},{2,0},{3,1},{4,6},{5,7},{6,4},{7,5},{8,10},{9,11},{10,... | collective-permute-start | bytes 442376 | tf_op jit(solution)/shard_map/ppermute | solution.py:81
  53.4 0.5 collective-permute-start.16
  54.0 4.1 %collective-permute-done.18.refs_3_ = bf16[192,384]{1,0:T(8,128)(2,1)S(1)} collective-permute-done((bf16[192,384]{1,0:T(8,128)(2,1)S(1)}, bf16[192,384]{1,0:T(8,128)(2,1)S(1)}, u32[]{:S(2)}, u32[]{:S(2)}) %collective-permute-start.18) | collective-permute-done | bytes 147488 | tf_op jit(solution)/shard_map/ppermute | solution.py:81
  58.1 2.1 %collective-permute-done.17.refs_2_ = bf16[192,384]{1,0:T(8,128)(2,1)S(1)} collective-permute-done((bf16[192,384]{1,0:T(8,128)(2,1)S(1)}, bf16[192,384]{1,0:T(8,128)(2,1)S(1)}, u32[]{:S(2)}, u32[]{:S(2)}) %collective-permute-start.17) | collective-permute-done | bytes 147488 | tf_op jit(solution)/shard_map/ppermute | solution.py:81
  60.2 0.5 collective-permute-start.20
  60.7 0.6 convert_add_fusion.2
  61.3 0.3 collective-permute-done.21.refs_6_
  61.6 0.2 collective-permute-done.20.refs_5_
  61.8 1.6 %place_sums.1 = (f32[384,384]{1,0:T(8,128)}, f32[384,768]{1,0:T(8,128)}, f32[384,384]{1,0:T(8,128)}) custom-call(bf16[192,384]{1,0:T(8,128)(2,1)S(1)} %add_convert_fusion.refs_0_, bf16[192,384]{1,0:T(8,128)(2,1)S(1)} %collective-permute-done.16.refs_1_, bf16[192,384]{1,0:T(8,128)(2,1)S(1)} %collective-permute-done.17.refs_2_, ...), custom_call_target="tpu_custom_call" | custom-call | bytes 3538944 | tf_op jit(solution)/shard_map/place_sums/pallas_call | solution.py:473
  (27 shorter events, 0.3 us)
Async XLA Ops:
  1.9 5.9 %collective-permute-start = (bf16[128,384]{1,0:T(8,128)(2,1)S(1)}, bf16[128,384]{1,0:T(8,128)(2,1)S(1)}, u32[]{:S(2)}, u32[]{:S(2)}) collective-permute-start(bf16[128,384]{1,0:T(8,128)(2,1)S(1)} %get-tuple-element.57), channel_id=1, source_target_pairs={{0,4},{1,5},{2,6},{3,7},{4,0},{5,1},{6,2},{7,3},{8,12},{9,13},{10,... | collective-permute-start | bytes 294920 | tf_op jit(solution)/shard_map/ppermute | solution.py:81
  7.8 6.5 %collective-permute-start.1 = (bf16[64,384]{1,0:T(8,128)(2,1)S(1)}, bf16[64,384]{1,0:T(8,128)(2,1)S(1)}, u32[]{:S(2)}, u32[]{:S(2)}) collective-permute-start(bf16[64,384]{1,0:T(8,128)(2,1)S(1)} %pad_maximum_fusion.6), channel_id=1, source_target_pairs={{0,24},{1,25},{2,26},{3,27},{4,28},{5,29},{6,30},{7,31},{8,16},{9,... | collective-permute-start | bytes 147464 | tf_op jit(solution)/shard_map/ppermute | solution.py:81
  11.7 5.1 %collective-permute-start.2 = (bf16[64,384]{1,0:T(8,128)(2,1)S(1)}, bf16[64,384]{1,0:T(8,128)(2,1)S(1)}, u32[]{:S(2)}, u32[]{:S(2)}) collective-permute-start(bf16[64,384]{1,0:T(8,128)(2,1)S(1)} %pad_maximum_fusion.7), channel_id=1, source_target_pairs={{0,16},{1,17},{2,18},{3,19},{4,20},{5,21},{6,22},{7,23},{8,24},{9,... | collective-permute-start | bytes 147464 | tf_op jit(solution)/shard_map/ppermute | solution.py:81
  11.7 5.1 %collective-permute-start.4 = (bf16[128,384]{1,0:T(8,128)(2,1)S(1)}, bf16[128,384]{1,0:T(8,128)(2,1)S(1)}, u32[]{:S(2)}, u32[]{:S(2)}) collective-permute-start(bf16[128,384]{1,0:T(8,128)(2,1)S(1)} %get-tuple-element.63), channel_id=1, source_target_pairs={{3,0},{0,1},{1,2},{2,3},{7,4},{4,5},{5,6},{6,7},{11,8},{8,9},{9,10... | collective-permute-start | bytes 294920 | tf_op jit(solution)/shard_map/ppermute | solution.py:87
  11.8 5.0 %collective-permute-start.3 = (bf16[64,384]{1,0:T(8,128)(2,1)S(1)}, bf16[64,384]{1,0:T(8,128)(2,1)S(1)}, u32[]{:S(2)}, u32[]{:S(2)}) collective-permute-start(bf16[64,384]{1,0:T(8,128)(2,1)S(1)} %pad_maximum_fusion.8), channel_id=1, source_target_pairs={{0,8},{1,9},{2,10},{3,11},{4,12},{5,13},{6,14},{7,15},{8,0},{9,1},... | collective-permute-start | bytes 147464 | tf_op jit(solution)/shard_map/ppermute | solution.py:81
  22.7 2.1 %collective-permute-start.5 = (bf16[784,384]{1,0:T(8,128)(2,1)S(1)}, bf16[784,384]{1,0:T(8,128)(2,1)S(1)}, u32[]{:S(2)}, u32[]{:S(2)}) collective-permute-start(bf16[784,384]{1,0:T(8,128)(2,1)S(1)} %get-tuple-element.76), channel_id=1, source_target_pairs={{0,1},{1,0},{2,3},{3,2},{4,5},{5,4},{6,7},{7,6},{8,9},{9,8},{10,11... | collective-permute-start | bytes 1806344 | tf_op jit(solution)/shard_map/ppermute | solution.py:81
  25.1 6.9 %collective-permute-start.8 = (bf16[200,384]{1,0:T(8,128)(2,1)S(1)}, bf16[200,384]{1,0:T(8,128)(2,1)S(1)}, u32[]{:S(2)}, u32[]{:S(2)}) collective-permute-start(bf16[200,384]{1,0:T(8,128)(2,1)S(1)} %get-tuple-element.109), channel_id=1, source_target_pairs={{0,4},{1,5},{2,6},{3,7},{4,0},{5,1},{6,2},{7,3},{8,12},{9,13},{10,... | collective-permute-start | bytes 460808 | tf_op jit(solution)/shard_map/ppermute | solution.py:81
  26.6 9.0 %collective-permute-start.7 = (bf16[200,384]{1,0:T(8,128)(2,1)S(1)}, bf16[200,384]{1,0:T(8,128)(2,1)S(1)}, u32[]{:S(2)}, u32[]{:S(2)}) collective-permute-start(bf16[200,384]{1,0:T(8,128)(2,1)S(1)} %get-tuple-element.110), channel_id=1, source_target_pairs={{0,2},{1,3},{2,0},{3,1},{4,6},{5,7},{6,4},{7,5},{8,10},{9,11},{10,... | collective-permute-start | bytes 460808 | tf_op jit(solution)/shard_map/ppermute | solution.py:81
  28.0 7.6 %collective-permute-start.6 = (bf16[200,384]{1,0:T(8,128)(2,1)S(1)}, bf16[200,384]{1,0:T(8,128)(2,1)S(1)}, u32[]{:S(2)}, u32[]{:S(2)}) collective-permute-start(bf16[200,384]{1,0:T(8,128)(2,1)S(1)} %get-tuple-element.111), channel_id=1, source_target_pairs={{0,6},{1,7},{2,4},{3,5},{4,2},{5,3},{6,0},{7,1},{8,14},{9,15},{10,... | collective-permute-start | bytes 460808 | tf_op jit(solution)/shard_map/ppermute | solution.py:81
  28.6 7.1 %collective-permute-start.9 = (bf16[64,384]{1,0:T(8,128)(2,1)S(1)}, bf16[64,384]{1,0:T(8,128)(2,1)S(1)}, u32[]{:S(2)}, u32[]{:S(2)}) collective-permute-start(bf16[64,384]{1,0:T(8,128)(2,1)S(1)} %get-tuple-element.82), channel_id=1, source_target_pairs={{0,24},{1,25},{2,26},{3,27},{4,28},{5,29},{6,30},{7,31},{8,16},{9,... | collective-permute-start | bytes 147464 | tf_op jit(solution)/shard_map/ppermute | solution.py:81
  30.3 5.5 %collective-permute-start.10 = (bf16[64,384]{1,0:T(8,128)(2,1)S(1)}, bf16[64,384]{1,0:T(8,128)(2,1)S(1)}, u32[]{:S(2)}, u32[]{:S(2)}) collective-permute-start(bf16[64,384]{1,0:T(8,128)(2,1)S(1)} %get-tuple-element.83), channel_id=1, source_target_pairs={{0,16},{1,17},{2,18},{3,19},{4,20},{5,21},{6,22},{7,23},{8,24},{9,... | collective-permute-start | bytes 147464 | tf_op jit(solution)/shard_map/ppermute | solution.py:81
  35.9 6.1 %collective-permute-start.11 = (bf16[200,384]{1,0:T(8,128)(2,1)S(1)}, bf16[200,384]{1,0:T(8,128)(2,1)S(1)}, u32[]{:S(2)}, u32[]{:S(2)}) collective-permute-start(bf16[200,384]{1,0:T(8,128)(2,1)S(1)} %pad_maximum_fusion.3), channel_id=1, source_target_pairs={{0,8},{1,9},{2,10},{3,11},{4,12},{5,13},{6,14},{7,15},{8,0},{9,1},... | collective-permute-start | bytes 460808 | tf_op jit(solution)/shard_map/ppermute | solution.py:81
  36.4 5.6 %collective-permute-start.13 = (bf16[64,384]{1,0:T(8,128)(2,1)S(1)}, bf16[64,384]{1,0:T(8,128)(2,1)S(1)}, u32[]{:S(2)}, u32[]{:S(2)}) collective-permute-start(bf16[64,384]{1,0:T(8,128)(2,1)S(1)} %get-tuple-element.89), channel_id=1, source_target_pairs={{0,8},{1,9},{2,10},{3,11},{4,12},{5,13},{6,14},{7,15},{8,0},{9,1},... | collective-permute-start | bytes 147464 | tf_op jit(solution)/shard_map/ppermute | solution.py:81
  42.1 8.3 %collective-permute-start.12 = (bf16[200,384]{1,0:T(8,128)(2,1)S(1)}, bf16[200,384]{1,0:T(8,128)(2,1)S(1)}, u32[]{:S(2)}, u32[]{:S(2)}) collective-permute-start(bf16[200,384]{1,0:T(8,128)(2,1)S(1)} %pad_maximum_fusion.4), channel_id=1, source_target_pairs={{0,16},{1,17},{2,18},{3,19},{4,20},{5,21},{6,22},{7,23},{8,24},{9,... | collective-permute-start | bytes 460808 | tf_op jit(solution)/shard_map/ppermute | solution.py:81
  44.2 4.7 %collective-permute-start.15 = (bf16[128,384]{1,0:T(8,128)(2,1)S(1)}, bf16[128,384]{1,0:T(8,128)(2,1)S(1)}, u32[]{:S(2)}, u32[]{:S(2)}) collective-permute-start(bf16[128,384]{1,0:T(8,128)(2,1)S(1)} %pad_maximum_fusion.5), channel_id=1, source_target_pairs={{0,4},{1,5},{2,6},{3,7},{4,0},{5,1},{6,2},{7,3},{8,12},{9,13},{10,... | collective-permute-start | bytes 294920 | tf_op jit(solution)/shard_map/ppermute | solution.py:81
  45.7 3.2 %collective-permute-start.14 = (bf16[128,384]{1,0:T(8,128)(2,1)S(1)}, bf16[128,384]{1,0:T(8,128)(2,1)S(1)}, u32[]{:S(2)}, u32[]{:S(2)}) collective-permute-start(bf16[128,384]{1,0:T(8,128)(2,1)S(1)} %get-tuple-element.91), channel_id=1, source_target_pairs={{1,0},{2,1},{3,2},{0,3},{5,4},{6,5},{7,6},{4,7},{9,8},{10,9},{11,1... | collective-permute-start | bytes 294920 | tf_op jit(solution)/shard_map/ppermute | solution.py:87
  50.4 7.7 %collective-permute-start.18 = (bf16[192,384]{1,0:T(8,128)(2,1)S(1)}, bf16[192,384]{1,0:T(8,128)(2,1)S(1)}, u32[]{:S(2)}, u32[]{:S(2)}) collective-permute-start(bf16[192,384]{1,0:T(8,128)(2,1)S(1)} %add_convert_fusion.refs_0_), channel_id=1, source_target_pairs={{0,6},{1,7},{2,4},{3,5},{4,2},{5,3},{6,0},{7,1},{8,14},{9,15},{10,... | collective-permute-start | bytes 442376 | tf_op jit(solution)/shard_map/ppermute | solution.py:81
  52.2 8.0 %collective-permute-start.17 = (bf16[192,384]{1,0:T(8,128)(2,1)S(1)}, bf16[192,384]{1,0:T(8,128)(2,1)S(1)}, u32[]{:S(2)}, u32[]{:S(2)}) collective-permute-start(bf16[192,384]{1,0:T(8,128)(2,1)S(1)} %add_convert_fusion.refs_0_), channel_id=1, source_target_pairs={{0,2},{1,3},{2,0},{3,1},{4,6},{5,7},{6,4},{7,5},{8,10},{9,11},{10,... | collective-permute-start | bytes 442376 | tf_op jit(solution)/shard_map/ppermute | solution.py:81
  53.4 6.8 %collective-permute-start.16 = (bf16[192,384]{1,0:T(8,128)(2,1)S(1)}, bf16[192,384]{1,0:T(8,128)(2,1)S(1)}, u32[]{:S(2)}, u32[]{:S(2)}) collective-permute-start(bf16[192,384]{1,0:T(8,128)(2,1)S(1)} %add_convert_fusion.refs_0_), channel_id=1, source_target_pairs={{0,4},{1,5},{2,6},{3,7},{4,0},{5,1},{6,2},{7,3},{8,12},{9,13},{10,... | collective-permute-start | bytes 442376 | tf_op jit(solution)/shard_map/ppermute | solution.py:81
  53.9 7.4 %collective-permute-start.19 = (bf16[192,384]{1,0:T(8,128)(2,1)S(1)}, bf16[192,384]{1,0:T(8,128)(2,1)S(1)}, u32[]{:S(2)}, u32[]{:S(2)}) collective-permute-start(bf16[192,384]{1,0:T(8,128)(2,1)S(1)} %add_convert_fusion.refs_0_), channel_id=1, source_target_pairs={{0,1},{1,0},{2,3},{3,2},{4,5},{5,4},{6,7},{7,6},{8,9},{9,8},{10,11... | collective-permute-start | bytes 442376 | tf_op jit(solution)/shard_map/ppermute | solution.py:81
  58.1 3.2 %collective-permute-start.22 = (bf16[192,384]{1,0:T(8,128)(2,1)S(1)}, bf16[192,384]{1,0:T(8,128)(2,1)S(1)}, u32[]{:S(2)}, u32[]{:S(2)}) collective-permute-start(bf16[192,384]{1,0:T(8,128)(2,1)S(1)} %collective-permute-done.18.refs_3_), channel_id=1, source_target_pairs={{0,1},{1,0},{2,3},{3,2},{4,5},{5,4},{6,7},{7,6},{8,9},{9,8},{10,11... | collective-permute-start | bytes 442376 | tf_op jit(solution)/shard_map/ppermute | solution.py:81
  60.2 1.4 %collective-permute-start.21 = (bf16[192,384]{1,0:T(8,128)(2,1)S(1)}, bf16[192,384]{1,0:T(8,128)(2,1)S(1)}, u32[]{:S(2)}, u32[]{:S(2)}) collective-permute-start(bf16[192,384]{1,0:T(8,128)(2,1)S(1)} %collective-permute-done.17.refs_2_), channel_id=1, source_target_pairs={{0,1},{1,0},{2,3},{3,2},{4,5},{5,4},{6,7},{7,6},{8,9},{9,8},{10,11... | collective-permute-start | bytes 442376 | tf_op jit(solution)/shard_map/ppermute | solution.py:81
  60.2 1.6 %collective-permute-start.20 = (bf16[192,384]{1,0:T(8,128)(2,1)S(1)}, bf16[192,384]{1,0:T(8,128)(2,1)S(1)}, u32[]{:S(2)}, u32[]{:S(2)}) collective-permute-start(bf16[192,384]{1,0:T(8,128)(2,1)S(1)} %collective-permute-done.16.refs_1_), channel_id=1, source_target_pairs={{0,1},{1,0},{2,3},{3,2},{4,5},{5,4},{6,7},{7,6},{8,9},{9,8},{10,11... | collective-permute-start | bytes 442376 | tf_op jit(solution)/shard_map/ppermute | solution.py:81

commit v17 on v15

--- a/solution.py
+++ b/solution.py
@@ -397,23 +397,23 @@
         write(1, f32_dot(ot_ref[...], og_ref[...]))
 
 
-def finish_kernel(factor, og_ref, wq_ref, wkv_ref, extt_ref, gqt_ref, gkvt_ref, ot_ref, *refs):
-    gf_ref, halo_feat_ref, keep_ref = refs[:3]
-    pair_refs = refs[3:]
-    width, row_count = gqt_ref.shape
+def keep_kernel(factor, og_ref, extt_ref, gqt_ref, gkvt_ref, ot_ref, keep_ref):
+    core = lax.axis_index("rows") % 2
+    weight_sums(core, keep_ref, extt_ref, gqt_ref, gkvt_ref, ot_ref, og_ref, factor)
+
+
+def finish_kernel(wq_ref, wkv_ref, gqt_ref, gkvt_ref, gf_ref, halo_feat_ref, *pair_refs):
+    row_count = gqt_ref.shape[1]
     near = TILE + row_count
     step = pair_refs[0].shape[0]
     slots = step * len(pair_refs)
-    weight_sums(
-        lax.axis_index("rows") % 2, keep_ref, extt_ref, gqt_ref, gkvt_ref, ot_ref, og_ref, factor
-    )
     by_feature = f32_dot(wkv_ref[...], gkvt_ref[:, : near + slots])
+    slot_feat = rounded(by_feature[:, near:].T)
+    for at, out_ref in enumerate(pair_refs):
+        out_ref[...] = slot_feat[at * step : (at + 1) * step]
     own = by_feature[:, TILE:near] + f32_dot(wq_ref[...], gqt_ref[...])
     gf_ref[...] = own.T
     halo_feat_ref[...] = rounded(by_feature[:, :TILE].T)
-    slot_feat = rounded(by_feature[:, near:].T)
-    for at, out_ref in enumerate(pair_refs):
-        out_ref[...] = slot_feat[at * step : (at + 1) * step]
 
 
 def place_kernel(*refs):
@@ -553,21 +553,35 @@
         ],
         flops=28 * ext_rows * width * width,
     )
-    message = swapped(message, *CORES)
-    own_feat, halo_feat, keep, *pairs = call(
-        functools.partial(finish_kernel, nodes**-0.5),
+    order = [*farthest_first(4), 0]
+    step = width // 2
+    parts = {at: message[at * step : (at + 1) * step + (padded if at == 3 else 0)] for at in order}
+    parts = {at: swapped(part, *CORES) for at, part in parts.items()}
+    (keep,) = call(
+        functools.partial(keep_kernel, nodes**-0.5),
+        "keep",
+        [shape((2 * width, width), f32)],
+        [prepared[0], *gradients],
+        flops=3 * ext_rows * width * width,
+    )
+    rider = rounded(rider).astype(f32) + parts[3][step:].astype(f32)
+    rider = rider[: -(-virt_rows // 8) * 8]
+    keep = {at: keep[at * step : (at + 1) * step] + parts[at][:step].astype(f32) for at in order}
+
+    masks = partner_masks(square)
+    messages = {at: with_rider(keep[at], rider) for at in order[:-1]}
+    gradients, _ = lax.optimization_barrier((gradients, list(messages.values())))
+    arrived = {at: swapped(message, *masks[at]) for at, message in messages.items()}
+    own_feat, halo_feat, *pairs = call(
+        finish_kernel,
         "finish",
-        [shape((row_count, width), f32), shape((TILE, width), bf16), shape((2 * width, width), f32)]
+        [shape((row_count, width), f32), shape((TILE, width), bf16)]
         + [shape((2 * per_peer, width), bf16)] * (dom_size // 2),
-        [*prepared[:3], *gradients],
-        flops=6 * ext_rows * width * width,
-    )
-
-    keep, rider = added(keep, rounded(rider).astype(f32), {1: message})
-    rider = rider[: -(-virt_rows // 8) * 8]
-    pairs, _ = lax.optimization_barrier((pairs, keep))
+        [*prepared[1:3], gradients[1], gradients[2]],
+        flops=3 * ext_rows * width * width,
+    )
     returned = [swapped(pairs[at], 2 * at, 0) for at in reversed(range(1, dom_size // 2))]
-    keep, rider = scattered(keep, rider, square)
+    keep, rider = added(keep[0], rounded(rider).astype(f32), arrived)
     keep, *returned[:-1] = lax.optimization_barrier((keep, *returned[:-1]))
     keep, rider = scattered(keep, rider, pair)
     (returned, halo_feat), _ = lax.optimization_barrier(((returned, halo_feat), keep))

time: 63.2 us -> 65.3 us (1.033)
  waiting for transfers between devices: 23.4 us -> 25.7 us
    ppermute x22 -> x25, waiting for transfers between devices: 23.4 us -> 25.7 us  [swapped(): return lax.ppermute(block, ('dom', 'rows'), route)]
    ppermute x22 -> x25, starting transfers between devices: 23.4 us -> 23.2 us  [swapped(): return lax.ppermute(block, ('dom', 'rows'), route)]
    pallas_call x6 -> x7, Pallas kernels: 14.1 us -> 14.2 us  [call(): pl.pallas_call(kernel, out_shape=outs, in_specs=[pl.BlockSpec(memory_spac...]
  transfers between devices with their start and end apart: 24 -> 27, of which waited for: 16 -> 18; matrix products, arithmetic and copies ran while one was open for 1% -> 1% of each run, Pallas kernels for 9% -> 8%
where the time goes in v17:
time: 65.3 us; the launch traced here: 65 us
  waiting for transfers between devices  25.7 us (39%)
  starting transfers between devices  23.2 us (36%)
  Pallas kernels  14.2 us (22%)
  other arithmetic  0.96 us (1%)
  between operations  0.86 us (1%)
    ppermute x25, waiting for transfers between devices, swapped(): return lax.ppermute(block, ('dom', 'rows'), route)  25.7 us
    ppermute x25, starting transfers between devices, swapped(): return lax.ppermute(block, ('dom', 'rows'), route)  23.2 us
    pallas_call x7, Pallas kernels, call(): pl.pallas_call(kernel, out_shape=outs, in_specs=[pl.BlockSpec(memory_spac...  14.2 us
  transfers between devices with their start and end apart: 27, of which 18 were waited for; matrix products, arithmetic and copies ran while one was open for 1% of the time, Pallas kernels for 8%

profile of v17, /device:TPU:0, one launch (start us, length us, event | category | flops | bytes accessed | tf_op | source)
XLA Modules:
  0.0 65.0 jit_solution(13235857052116852614)
XLA Ops:
  0.6 1.2 %pick_rows.1 = (bf16[128,384]{1,0:T(8,128)(2,1)S(1)}, bf16[256,256]{1,0:T(8,128)(2,1)S(1)}, bf16[128,384]{1,0:T(8,128)(2,1)S(1)}, bf16[32,384]{1,0:T(8,128)(2,1)...) custom-call(bf16[256,384]{1,0:T(8,128)(2,1)} %feat_hbm.3, ...), custom_call_target="tpu_custom_call" | custom-call | bytes 623616 | tf_op jit(solution)/shard_map/pick_rows/pallas_call | solution.py:473
  1.9 3.0 %collective-permute-start = (bf16[128,384]{1,0:T(8,128)(2,1)S(1)}, bf16[128,384]{1,0:T(8,128)(2,1)S(1)}, u32[]{:S(2)}, u32[]{:S(2)}) collective-permute-start(bf16[128,384]{1,0:T(8,128)(2,1)S(1)} %get-tuple-element.52), channel_id=1, source_target_pairs={{0,4},{1,5},{2,6},{3,7},{4,0},{5,1},{6,2},{7,3},{8,12},{9,13},{10,... | collective-permute-start | bytes 294920 | tf_op jit(solution)/shard_map/ppermute | solution.py:81
  4.9 2.9 %prepare.1 = (bf16[256,384]{1,0:T(8,128)(2,1)S(1)}, bf16[384,384]{1,0:T(8,128)(2,1)S(1)}, bf16[384,768]{1,0:T(8,128)(2,1)S(1)}, bf16[384,272]{1,0:T(8,128)(2,1)S...) custom-call(bf16[256,384]{1,0:T(8,128)(2,1)} %feat_hbm.3, ...), custom_call_target="tpu_custom_call" | custom-call | flops 377487360 | bytes 4656128 | tf_op jit(solution)/shard_map/prepare/pallas_call | solution.py:473
  7.8 3.9 %collective-permute-start.1 = (bf16[64,384]{1,0:T(8,128)(2,1)S(1)}, bf16[64,384]{1,0:T(8,128)(2,1)S(1)}, u32[]{:S(2)}, u32[]{:S(2)}) collective-permute-start(bf16[64,384]{1,0:T(8,128)(2,1)S(1)} %pad_maximum_fusion.7), channel_id=1, source_target_pairs={{0,24},{1,25},{2,26},{3,27},{4,28},{5,29},{6,30},{7,31},{8,16},{9,... | collective-permute-start | bytes 147464 | tf_op jit(solution)/shard_map/ppermute | solution.py:81
  11.7 0.1 collective-permute-start.4
  11.8 0.6 collective-permute-start.3
  12.4 1.9 %collective-permute-done.1.refs_2_ = bf16[64,384]{1,0:T(8,128)(2,1)S(1)} collective-permute-done((bf16[64,384]{1,0:T(8,128)(2,1)S(1)}, bf16[64,384]{1,0:T(8,128)(2,1)S(1)}, u32[]{:S(2)}, u32[]{:S(2)}) %collective-permute-start.1) | collective-permute-done | bytes 49184 | tf_op jit(solution)/shard_map/ppermute | solution.py:81
  14.3 2.5 %collective-permute-done.2.refs_3_ = bf16[64,384]{1,0:T(8,128)(2,1)S(1)} collective-permute-done((bf16[64,384]{1,0:T(8,128)(2,1)S(1)}, bf16[64,384]{1,0:T(8,128)(2,1)S(1)}, u32[]{:S(2)}, u32[]{:S(2)}) %collective-permute-start.2) | collective-permute-done | bytes 49184 | tf_op jit(solution)/shard_map/ppermute | solution.py:81
  16.8 5.9 %attend.1 = (bf16[784,384]{1,0:T(8,128)(2,1)S(1)}, f32[16,384]{1,0:T(8,128)S(1)}, bf16[384,656]{1,0:T(8,128)(2,1)S(1)}, bf16[384,256]{1,0:T(8,128)(2,1)S(1)}, bf...) custom-call(bf16[32,384]{1,0:T(8,128)(2,1)S(1)} %get-tuple-element.51.refs_0_, ...), custom_call_target="tpu_custom_call" | custom-call | flops 2708471808 | bytes 5959680 | tf_op jit(solution)/shard_map/attend/pallas_call | solution.py:473
  22.8 0.1 collective-permute-start.6
  22.9 0.6 collective-permute-start.8
  23.5 0.1 collective-permute-start.10
  23.5 0.6 keep.1
  24.1 0.1 collective-permute-done.6
  24.2 0.2 collective-permute-done.8
  24.5 0.4 collective-permute-done.10
  24.8 0.1 fusion.2
  25.0 2.4 %collective-permute-start.7 = (bf16[200,384]{1,0:T(8,128)(2,1)S(1)}, bf16[200,384]{1,0:T(8,128)(2,1)S(1)}, u32[]{:S(2)}, u32[]{:S(2)}) collective-permute-start(bf16[200,384]{1,0:T(8,128)(2,1)S(1)} %get-tuple-element.104), channel_id=1, source_target_pairs={{0,6},{1,7},{2,4},{3,5},{4,2},{5,3},{6,0},{7,1},{8,14},{9,15},{10,... | collective-permute-start | bytes 460808 | tf_op jit(solution)/shard_map/ppermute | solution.py:81
  27.4 0.6 collective-permute-start.9
  28.0 0.5 collective-permute-start.11
  28.5 0.9 %finish.1 = (f32[256,384]{1,0:T(8,128)S(1)}, bf16[128,384]{1,0:T(8,128)(2,1)S(1)}, bf16[64,384]{1,0:T(8,128)(2,1)S(1)}, bf16[64,384]{1,0:T(8,128)(2,1)S(1)}, bf1...) custom-call(bf16[384,384]{1,0:T(8,128)(2,1)S(1)} %get-tuple-element.59.refs_7_.wq_ref, ...), custom_call_target="tpu_custom_call" | custom-call | flops 290193408 | bytes 2777088 | tf_op jit(solution)/shard_map/finish/pallas_call | solution.py:473
  29.5 1.8 %collective-permute-start.12 = (bf16[64,384]{1,0:T(8,128)(2,1)S(1)}, bf16[64,384]{1,0:T(8,128)(2,1)S(1)}, u32[]{:S(2)}, u32[]{:S(2)}) collective-permute-start(bf16[64,384]{1,0:T(8,128)(2,1)S(1)} %get-tuple-element.76), channel_id=1, source_target_pairs={{0,24},{1,25},{2,26},{3,27},{4,28},{5,29},{6,30},{7,31},{8,16},{9,... | collective-permute-start | bytes 147464 | tf_op jit(solution)/shard_map/ppermute | solution.py:81
  31.3 0.7 %collective-permute-start.13 = (bf16[64,384]{1,0:T(8,128)(2,1)S(1)}, bf16[64,384]{1,0:T(8,128)(2,1)S(1)}, u32[]{:S(2)}, u32[]{:S(2)}) collective-permute-start(bf16[64,384]{1,0:T(8,128)(2,1)S(1)} %get-tuple-element.77), channel_id=1, source_target_pairs={{0,16},{1,17},{2,18},{3,19},{4,20},{5,21},{6,22},{7,23},{8,24},{9,... | collective-permute-start | bytes 147464 | tf_op jit(solution)/shard_map/ppermute | solution.py:81
  32.0 0.8 %collective-permute-done.7 = bf16[200,384]{1,0:T(8,128)(2,1)S(1)} collective-permute-done((bf16[200,384]{1,0:T(8,128)(2,1)S(1)}, bf16[200,384]{1,0:T(8,128)(2,1)S(1)}, u32[]{:S(2)}, u32[]{:S(2)}) %collective-permute-start.7) | collective-permute-done | bytes 153632 | tf_op jit(solution)/shard_map/ppermute | solution.py:81
  32.8 2.6 %collective-permute-done.9 = bf16[200,384]{1,0:T(8,128)(2,1)S(1)} collective-permute-done((bf16[200,384]{1,0:T(8,128)(2,1)S(1)}, bf16[200,384]{1,0:T(8,128)(2,1)S(1)}, u32[]{:S(2)}, u32[]{:S(2)}) %collective-permute-start.9) | collective-permute-done | bytes 153632 | tf_op jit(solution)/shard_map/ppermute | solution.py:81
  35.3 0.1 fusion.5
  35.4 0.4 collective-permute-done.12.refs_0_
  35.8 1.8 %collective-permute-done.13.refs_1_ = bf16[64,384]{1,0:T(8,128)(2,1)S(1)} collective-permute-done((bf16[64,384]{1,0:T(8,128)(2,1)S(1)}, bf16[64,384]{1,0:T(8,128)(2,1)S(1)}, u32[]{:S(2)}, u32[]{:S(2)}) %collective-permute-start.13) | collective-permute-done | bytes 49184 | tf_op jit(solution)/shard_map/ppermute | solution.py:81
  37.6 0.1 collective-permute-start.14
  37.7 2.0 %collective-permute-start.17 = (bf16[64,384]{1,0:T(8,128)(2,1)S(1)}, bf16[64,384]{1,0:T(8,128)(2,1)S(1)}, u32[]{:S(2)}, u32[]{:S(2)}) collective-permute-start(bf16[64,384]{1,0:T(8,128)(2,1)S(1)} %get-tuple-element.83), channel_id=1, source_target_pairs={{0,8},{1,9},{2,10},{3,11},{4,12},{5,13},{6,14},{7,15},{8,0},{9,1},... | collective-permute-start | bytes 147464 | tf_op jit(solution)/shard_map/ppermute | solution.py:81
  39.7 2.8 %collective-permute-done.14 = bf16[104,384]{1,0:T(8,128)(2,1)S(1)} collective-permute-done((bf16[104,384]{1,0:T(8,128)(2,1)S(1)}, bf16[104,384]{1,0:T(8,128)(2,1)S(1)}, u32[]{:S(2)}, u32[]{:S(2)}) %collective-permute-start.14) | collective-permute-done | bytes 79904 | tf_op jit(solution)/shard_map/ppermute | solution.py:81
  42.6 0.5 collective-permute-done.17.refs_2_
  43.1 1.5 %collective-permute-start.15 = (bf16[104,384]{1,0:T(8,128)(2,1)S(1)}, bf16[104,384]{1,0:T(8,128)(2,1)S(1)}, u32[]{:S(2)}, u32[]{:S(2)}) collective-permute-start(bf16[104,384]{1,0:T(8,128)(2,1)S(1)} %pad_maximum_fusion.6), channel_id=1, source_target_pairs={{0,16},{1,17},{2,18},{3,19},{4,20},{5,21},{6,22},{7,23},{8,24},{9,... | collective-permute-start | bytes 239624 | tf_op jit(solution)/shard_map/ppermute | solution.py:81
  44.7 1.6 %collective-permute-start.19 = (bf16[128,384]{1,0:T(8,128)(2,1)S(1)}, bf16[128,384]{1,0:T(8,128)(2,1)S(1)}, u32[]{:S(2)}, u32[]{:S(2)}) collective-permute-start(bf16[128,384]{1,0:T(8,128)(2,1)S(1)} %pad_maximum_fusion.4), channel_id=1, source_target_pairs={{0,4},{1,5},{2,6},{3,7},{4,0},{5,1},{6,2},{7,3},{8,12},{9,13},{10,... | collective-permute-start | bytes 294920 | tf_op jit(solution)/shard_map/ppermute | solution.py:81
  46.3 3.1 %collective-permute-done.15 = bf16[104,384]{1,0:T(8,128)(2,1)S(1)} collective-permute-done((bf16[104,384]{1,0:T(8,128)(2,1)S(1)}, bf16[104,384]{1,0:T(8,128)(2,1)S(1)}, u32[]{:S(2)}, u32[]{:S(2)}) %collective-permute-start.15) | collective-permute-done | bytes 79904 | tf_op jit(solution)/shard_map/ppermute | solution.py:81
  49.4 0.1 collective-permute-start.16
  49.5 1.0 %return_rows.1 = f32[256,384]{1,0:T(8,128)} custom-call(f32[256,384]{1,0:T(8,128)S(1)} %get-tuple-element.79.gf_ref, bf16[256,256]{1,0:T(8,128)(2,1)S(1)} %get-tuple-element.80.chosen_ref, bf16[128,384]{1,0:T(8,128)(2,1)S(1)} %collective-permute-done.18.halo_ref, bf16[64,384]{1,0:T(8,128)(2,1)S(1)} %get-tuple-element.86.own_ref, ...), custom_call_target="tpu_custom_call" | custom-call | bytes 1310720 | tf_op jit(solution)/shard_map/return_rows/pallas_call | solution.py:473
  50.5 3.3 %collective-permute-done.16 = bf16[96,384]{1,0:T(8,128)(2,1)S(1)} collective-permute-done((bf16[96,384]{1,0:T(8,128)(2,1)S(1)}, bf16[96,384]{1,0:T(8,128)(2,1)S(1)}, u32[]{:S(2)}, u32[]{:S(2)}) %collective-permute-start.16) | collective-permute-done | bytes 73760 | tf_op jit(solution)/shard_map/ppermute | solution.py:81
  53.9 2.4 %collective-permute-start.22 = (bf16[192,384]{1,0:T(8,128)(2,1)S(1)}, bf16[192,384]{1,0:T(8,128)(2,1)S(1)}, u32[]{:S(2)}, u32[]{:S(2)}) collective-permute-start(bf16[192,384]{1,0:T(8,128)(2,1)S(1)} %pad_maximum_fusion.3.refs_0_), channel_id=1, source_target_pairs={{0,6},{1,7},{2,4},{3,5},{4,2},{5,3},{6,0},{7,1},{8,14},{9,15},{10,... | collective-permute-start | bytes 442376 | tf_op jit(solution)/shard_map/ppermute | solution.py:81
  56.3 0.6 collective-permute-start.21
  56.9 0.5 collective-permute-start.20
  57.4 2.6 %collective-permute-done.22.refs_3_ = bf16[192,384]{1,0:T(8,128)(2,1)S(1)} collective-permute-done((bf16[192,384]{1,0:T(8,128)(2,1)S(1)}, bf16[192,384]{1,0:T(8,128)(2,1)S(1)}, u32[]{:S(2)}, u32[]{:S(2)}) %collective-permute-start.22) | collective-permute-done | bytes 147488 | tf_op jit(solution)/shard_map/ppermute | solution.py:81
  60.0 1.6 %collective-permute-done.21.refs_2_ = bf16[192,384]{1,0:T(8,128)(2,1)S(1)} collective-permute-done((bf16[192,384]{1,0:T(8,128)(2,1)S(1)}, bf16[192,384]{1,0:T(8,128)(2,1)S(1)}, u32[]{:S(2)}, u32[]{:S(2)}) %collective-permute-start.21) | collective-permute-done | bytes 147488 | tf_op jit(solution)/shard_map/ppermute | solution.py:81
  61.5 0.5 collective-permute-done.20.refs_1_
  62.1 0.6 convert_add_fusion.1
  62.7 0.3 collective-permute-done.25.refs_6_
  62.9 0.5 collective-permute-done.24.refs_5_
  63.4 1.6 %place_sums.1 = (f32[384,384]{1,0:T(8,128)}, f32[384,768]{1,0:T(8,128)}, f32[384,384]{1,0:T(8,128)}) custom-call(bf16[192,384]{1,0:T(8,128)(2,1)S(1)} %pad_maximum_fusion.3.refs_0_, bf16[192,384]{1,0:T(8,128)(2,1)S(1)} %collective-permute-done.20.refs_1_, bf16[192,384]{1,0:T(8,128)(2,1)S(1)} %collective-permute-done.21.refs_2_, ...), custom_call_target="tpu_custom_call" | custom-call | bytes 3538944 | tf_op jit(solution)/shard_map/place_sums/pallas_call | solution.py:473
  (39 shorter events, 0.4 us)
Async XLA Ops:
  1.9 5.9 %collective-permute-start = (bf16[128,384]{1,0:T(8,128)(2,1)S(1)}, bf16[128,384]{1,0:T(8,128)(2,1)S(1)}, u32[]{:S(2)}, u32[]{:S(2)}) collective-permute-start(bf16[128,384]{1,0:T(8,128)(2,1)S(1)} %get-tuple-element.52), channel_id=1, source_target_pairs={{0,4},{1,5},{2,6},{3,7},{4,0},{5,1},{6,2},{7,3},{8,12},{9,13},{10,... | collective-permute-start | bytes 294920 | tf_op jit(solution)/shard_map/ppermute | solution.py:81
  7.8 6.5 %collective-permute-start.1 = (bf16[64,384]{1,0:T(8,128)(2,1)S(1)}, bf16[64,384]{1,0:T(8,128)(2,1)S(1)}, u32[]{:S(2)}, u32[]{:S(2)}) collective-permute-start(bf16[64,384]{1,0:T(8,128)(2,1)S(1)} %pad_maximum_fusion.7), channel_id=1, source_target_pairs={{0,24},{1,25},{2,26},{3,27},{4,28},{5,29},{6,30},{7,31},{8,16},{9,... | collective-permute-start | bytes 147464 | tf_op jit(solution)/shard_map/ppermute | solution.py:81
  11.7 5.1 %collective-permute-start.2 = (bf16[64,384]{1,0:T(8,128)(2,1)S(1)}, bf16[64,384]{1,0:T(8,128)(2,1)S(1)}, u32[]{:S(2)}, u32[]{:S(2)}) collective-permute-start(bf16[64,384]{1,0:T(8,128)(2,1)S(1)} %pad_maximum_fusion.8), channel_id=1, source_target_pairs={{0,16},{1,17},{2,18},{3,19},{4,20},{5,21},{6,22},{7,23},{8,24},{9,... | collective-permute-start | bytes 147464 | tf_op jit(solution)/shard_map/ppermute | solution.py:81
  11.7 5.1 %collective-permute-start.4 = (bf16[128,384]{1,0:T(8,128)(2,1)S(1)}, bf16[128,384]{1,0:T(8,128)(2,1)S(1)}, u32[]{:S(2)}, u32[]{:S(2)}) collective-permute-start(bf16[128,384]{1,0:T(8,128)(2,1)S(1)} %get-tuple-element.58), channel_id=1, source_target_pairs={{3,0},{0,1},{1,2},{2,3},{7,4},{4,5},{5,6},{6,7},{11,8},{8,9},{9,10... | collective-permute-start | bytes 294920 | tf_op jit(solution)/shard_map/ppermute | solution.py:87
  11.8 5.0 %collective-permute-start.3 = (bf16[64,384]{1,0:T(8,128)(2,1)S(1)}, bf16[64,384]{1,0:T(8,128)(2,1)S(1)}, u32[]{:S(2)}, u32[]{:S(2)}) collective-permute-start(bf16[64,384]{1,0:T(8,128)(2,1)S(1)} %pad_maximum_fusion.9), channel_id=1, source_target_pairs={{0,8},{1,9},{2,10},{3,11},{4,12},{5,13},{6,14},{7,15},{8,0},{9,1},... | collective-permute-start | bytes 147464 | tf_op jit(solution)/shard_map/ppermute | solution.py:81
  22.8 1.5 %collective-permute-start.6 = (bf16[208,384]{1,0:T(8,128)(2,1)S(1)}, bf16[208,384]{1,0:T(8,128)(2,1)S(1)}, u32[]{:S(2)}, u32[]{:S(2)}) collective-permute-start(bf16[208,384]{1,0:T(8,128)(2,1)S(1)} %slice.101), channel_id=1, source_target_pairs={{0,1},{1,0},{2,3},{3,2},{4,5},{5,4},{6,7},{7,6},{8,9},{9,8},{10,11... | collective-permute-start | bytes 479240 | tf_op jit(solution)/shard_map/ppermute | solution.py:81
  22.9 1.6 %collective-permute-start.8 = (bf16[192,384]{1,0:T(8,128)(2,1)S(1)}, bf16[192,384]{1,0:T(8,128)(2,1)S(1)}, u32[]{:S(2)}, u32[]{:S(2)}) collective-permute-start(bf16[192,384]{1,0:T(8,128)(2,1)S(1)} %get-tuple-element.98), channel_id=1, source_target_pairs={{0,1},{1,0},{2,3},{3,2},{4,5},{5,4},{6,7},{7,6},{8,9},{9,8},{10,11... | collective-permute-start | bytes 442376 | tf_op jit(solution)/shard_map/ppermute | solution.py:81
  23.5 1.4 %collective-permute-start.10 = (bf16[192,384]{1,0:T(8,128)(2,1)S(1)}, bf16[192,384]{1,0:T(8,128)(2,1)S(1)}, u32[]{:S(2)}, u32[]{:S(2)}) collective-permute-start(bf16[192,384]{1,0:T(8,128)(2,1)S(1)} %get-tuple-element.99), channel_id=1, source_target_pairs={{0,1},{1,0},{2,3},{3,2},{4,5},{5,4},{6,7},{7,6},{8,9},{9,8},{10,11... | collective-permute-start | bytes 442376 | tf_op jit(solution)/shard_map/ppermute | solution.py:81
  25.0 7.8 %collective-permute-start.7 = (bf16[200,384]{1,0:T(8,128)(2,1)S(1)}, bf16[200,384]{1,0:T(8,128)(2,1)S(1)}, u32[]{:S(2)}, u32[]{:S(2)}) collective-permute-start(bf16[200,384]{1,0:T(8,128)(2,1)S(1)} %get-tuple-element.104), channel_id=1, source_target_pairs={{0,6},{1,7},{2,4},{3,5},{4,2},{5,3},{6,0},{7,1},{8,14},{9,15},{10,... | collective-permute-start | bytes 460808 | tf_op jit(solution)/shard_map/ppermute | solution.py:81
  27.4 8.0 %collective-permute-start.9 = (bf16[200,384]{1,0:T(8,128)(2,1)S(1)}, bf16[200,384]{1,0:T(8,128)(2,1)S(1)}, u32[]{:S(2)}, u32[]{:S(2)}) collective-permute-start(bf16[200,384]{1,0:T(8,128)(2,1)S(1)} %get-tuple-element.105), channel_id=1, source_target_pairs={{0,2},{1,3},{2,0},{3,1},{4,6},{5,7},{6,4},{7,5},{8,10},{9,11},{10,... | collective-permute-start | bytes 460808 | tf_op jit(solution)/shard_map/ppermute | solution.py:81
  28.0 7.3 %collective-permute-start.11 = (bf16[200,384]{1,0:T(8,128)(2,1)S(1)}, bf16[200,384]{1,0:T(8,128)(2,1)S(1)}, u32[]{:S(2)}, u32[]{:S(2)}) collective-permute-start(bf16[200,384]{1,0:T(8,128)(2,1)S(1)} %get-tuple-element.106), channel_id=1, source_target_pairs={{0,4},{1,5},{2,6},{3,7},{4,0},{5,1},{6,2},{7,3},{8,12},{9,13},{10,... | collective-permute-start | bytes 460808 | tf_op jit(solution)/shard_map/ppermute | solution.py:81
  28.5 2.8 %collective-permute-start.5 = (bf16[192,384]{1,0:T(8,128)(2,1)S(1)}, bf16[192,384]{1,0:T(8,128)(2,1)S(1)}, u32[]{:S(2)}, u32[]{:S(2)}) collective-permute-start(bf16[192,384]{1,0:T(8,128)(2,1)S(1)} %get-tuple-element.100), channel_id=1, source_target_pairs={{0,1},{1,0},{2,3},{3,2},{4,5},{5,4},{6,7},{7,6},{8,9},{9,8},{10,11... | collective-permute-start | bytes 442376 | tf_op jit(solution)/shard_map/ppermute | solution.py:81
  29.5 6.3 %collective-permute-start.12 = (bf16[64,384]{1,0:T(8,128)(2,1)S(1)}, bf16[64,384]{1,0:T(8,128)(2,1)S(1)}, u32[]{:S(2)}, u32[]{:S(2)}) collective-permute-start(bf16[64,384]{1,0:T(8,128)(2,1)S(1)} %get-tuple-element.76), channel_id=1, source_target_pairs={{0,24},{1,25},{2,26},{3,27},{4,28},{5,29},{6,30},{7,31},{8,16},{9,... | collective-permute-start | bytes 147464 | tf_op jit(solution)/shard_map/ppermute | solution.py:81
  31.3 6.3 %collective-permute-start.13 = (bf16[64,384]{1,0:T(8,128)(2,1)S(1)}, bf16[64,384]{1,0:T(8,128)(2,1)S(1)}, u32[]{:S(2)}, u32[]{:S(2)}) collective-permute-start(bf16[64,384]{1,0:T(8,128)(2,1)S(1)} %get-tuple-element.77), channel_id=1, source_target_pairs={{0,16},{1,17},{2,18},{3,19},{4,20},{5,21},{6,22},{7,23},{8,24},{9,... | collective-permute-start | bytes 147464 | tf_op jit(solution)/shard_map/ppermute | solution.py:81
  37.6 4.9 %collective-permute-start.14 = (bf16[104,384]{1,0:T(8,128)(2,1)S(1)}, bf16[104,384]{1,0:T(8,128)(2,1)S(1)}, u32[]{:S(2)}, u32[]{:S(2)}) collective-permute-start(bf16[104,384]{1,0:T(8,128)(2,1)S(1)} %pad_maximum_fusion.5), channel_id=1, source_target_pairs={{0,8},{1,9},{2,10},{3,11},{4,12},{5,13},{6,14},{7,15},{8,0},{9,1},... | collective-permute-start | bytes 239624 | tf_op jit(solution)/shard_map/ppermute | solution.py:81
  37.7 5.4 %collective-permute-start.17 = (bf16[64,384]{1,0:T(8,128)(2,1)S(1)}, bf16[64,384]{1,0:T(8,128)(2,1)S(1)}, u32[]{:S(2)}, u32[]{:S(2)}) collective-permute-start(bf16[64,384]{1,0:T(8,128)(2,1)S(1)} %get-tuple-element.83), channel_id=1, source_target_pairs={{0,8},{1,9},{2,10},{3,11},{4,12},{5,13},{6,14},{7,15},{8,0},{9,1},... | collective-permute-start | bytes 147464 | tf_op jit(solution)/shard_map/ppermute | solution.py:81
  43.1 6.2 %collective-permute-start.15 = (bf16[104,384]{1,0:T(8,128)(2,1)S(1)}, bf16[104,384]{1,0:T(8,128)(2,1)S(1)}, u32[]{:S(2)}, u32[]{:S(2)}) collective-permute-start(bf16[104,384]{1,0:T(8,128)(2,1)S(1)} %pad_maximum_fusion.6), channel_id=1, source_target_pairs={{0,16},{1,17},{2,18},{3,19},{4,20},{5,21},{6,22},{7,23},{8,24},{9,... | collective-permute-start | bytes 239624 | tf_op jit(solution)/shard_map/ppermute | solution.py:81
  44.7 4.8 %collective-permute-start.19 = (bf16[128,384]{1,0:T(8,128)(2,1)S(1)}, bf16[128,384]{1,0:T(8,128)(2,1)S(1)}, u32[]{:S(2)}, u32[]{:S(2)}) collective-permute-start(bf16[128,384]{1,0:T(8,128)(2,1)S(1)} %pad_maximum_fusion.4), channel_id=1, source_target_pairs={{0,4},{1,5},{2,6},{3,7},{4,0},{5,1},{6,2},{7,3},{8,12},{9,13},{10,... | collective-permute-start | bytes 294920 | tf_op jit(solution)/shard_map/ppermute | solution.py:81
  46.3 3.2 %collective-permute-start.18 = (bf16[128,384]{1,0:T(8,128)(2,1)S(1)}, bf16[128,384]{1,0:T(8,128)(2,1)S(1)}, u32[]{:S(2)}, u32[]{:S(2)}) collective-permute-start(bf16[128,384]{1,0:T(8,128)(2,1)S(1)} %get-tuple-element.85), channel_id=1, source_target_pairs={{1,0},{2,1},{3,2},{0,3},{5,4},{6,5},{7,6},{4,7},{9,8},{10,9},{11,1... | collective-permute-start | bytes 294920 | tf_op jit(solution)/shard_map/ppermute | solution.py:87
  49.4 4.4 %collective-permute-start.16 = (bf16[96,384]{1,0:T(8,128)(2,1)S(1)}, bf16[96,384]{1,0:T(8,128)(2,1)S(1)}, u32[]{:S(2)}, u32[]{:S(2)}) collective-permute-start(bf16[96,384]{1,0:T(8,128)(2,1)S(1)} %add_convert_fusion), channel_id=1, source_target_pairs={{0,8},{1,9},{2,10},{3,11},{4,12},{5,13},{6,14},{7,15},{8,0},{9,1},... | collective-permute-start | bytes 221192 | tf_op jit(solution)/shard_map/ppermute | solution.py:81
  53.9 6.1 %collective-permute-start.22 = (bf16[192,384]{1,0:T(8,128)(2,1)S(1)}, bf16[192,384]{1,0:T(8,128)(2,1)S(1)}, u32[]{:S(2)}, u32[]{:S(2)}) collective-permute-start(bf16[192,384]{1,0:T(8,128)(2,1)S(1)} %pad_maximum_fusion.3.refs_0_), channel_id=1, source_target_pairs={{0,6},{1,7},{2,4},{3,5},{4,2},{5,3},{6,0},{7,1},{8,14},{9,15},{10,... | collective-permute-start | bytes 442376 | tf_op jit(solution)/shard_map/ppermute | solution.py:81
  56.3 5.3 %collective-permute-start.21 = (bf16[192,384]{1,0:T(8,128)(2,1)S(1)}, bf16[192,384]{1,0:T(8,128)(2,1)S(1)}, u32[]{:S(2)}, u32[]{:S(2)}) collective-permute-start(bf16[192,384]{1,0:T(8,128)(2,1)S(1)} %pad_maximum_fusion.3.refs_0_), channel_id=1, source_target_pairs={{0,2},{1,3},{2,0},{3,1},{4,6},{5,7},{6,4},{7,5},{8,10},{9,11},{10,... | collective-permute-start | bytes 442376 | tf_op jit(solution)/shard_map/ppermute | solution.py:81
  56.9 5.1 %collective-permute-start.20 = (bf16[192,384]{1,0:T(8,128)(2,1)S(1)}, bf16[192,384]{1,0:T(8,128)(2,1)S(1)}, u32[]{:S(2)}, u32[]{:S(2)}) collective-permute-start(bf16[192,384]{1,0:T(8,128)(2,1)S(1)} %pad_maximum_fusion.3.refs_0_), channel_id=1, source_target_pairs={{0,4},{1,5},{2,6},{3,7},{4,0},{5,1},{6,2},{7,3},{8,12},{9,13},{10,... | collective-permute-start | bytes 442376 | tf_op jit(solution)/shard_map/ppermute | solution.py:81
  57.4 5.2 %collective-permute-start.23 = (bf16[192,384]{1,0:T(8,128)(2,1)S(1)}, bf16[192,384]{1,0:T(8,128)(2,1)S(1)}, u32[]{:S(2)}, u32[]{:S(2)}) collective-permute-start(bf16[192,384]{1,0:T(8,128)(2,1)S(1)} %pad_maximum_fusion.3.refs_0_), channel_id=1, source_target_pairs={{0,1},{1,0},{2,3},{3,2},{4,5},{5,4},{6,7},{7,6},{8,9},{9,8},{10,11... | collective-permute-start | bytes 442376 | tf_op jit(solution)/shard_map/ppermute | solution.py:81
  60.0 2.7 %collective-permute-start.26 = (bf16[192,384]{1,0:T(8,128)(2,1)S(1)}, bf16[192,384]{1,0:T(8,128)(2,1)S(1)}, u32[]{:S(2)}, u32[]{:S(2)}) collective-permute-start(bf16[192,384]{1,0:T(8,128)(2,1)S(1)} %collective-permute-done.22.refs_3_), channel_id=1, source_target_pairs={{0,1},{1,0},{2,3},{3,2},{4,5},{5,4},{6,7},{7,6},{8,9},{9,8},{10,11... | collective-permute-start | bytes 442376 | tf_op jit(solution)/shard_map/ppermute | solution.py:81
  61.5 1.4 %collective-permute-start.25 = (bf16[192,384]{1,0:T(8,128)(2,1)S(1)}, bf16[192,384]{1,0:T(8,128)(2,1)S(1)}, u32[]{:S(2)}, u32[]{:S(2)}) collective-permute-start(bf16[192,384]{1,0:T(8,128)(2,1)S(1)} %collective-permute-done.21.refs_2_), channel_id=1, source_target_pairs={{0,1},{1,0},{2,3},{3,2},{4,5},{5,4},{6,7},{7,6},{8,9},{9,8},{10,11... | collective-permute-start | bytes 442376 | tf_op jit(solution)/shard_map/ppermute | solution.py:81
  62.0 1.4 %collective-permute-start.24 = (bf16[192,384]{1,0:T(8,128)(2,1)S(1)}, bf16[192,384]{1,0:T(8,128)(2,1)S(1)}, u32[]{:S(2)}, u32[]{:S(2)}) collective-permute-start(bf16[192,384]{1,0:T(8,128)(2,1)S(1)} %collective-permute-done.20.refs_1_), channel_id=1, source_target_pairs={{0,1},{1,0},{2,3},{3,2},{4,5},{5,4},{6,7},{7,6},{8,9},{9,8},{10,11... | collective-permute-start | bytes 442376 | tf_op jit(solution)/shard_map/ppermute | solution.py:81

commit v18 on v15

--- a/solution.py
+++ b/solution.py
@@ -566,28 +566,32 @@
     keep, rider = added(keep, rounded(rider).astype(f32), {1: message})
     rider = rider[: -(-virt_rows // 8) * 8]
     pairs, _ = lax.optimization_barrier((pairs, keep))
-    returned = [swapped(pairs[at], 2 * at, 0) for at in reversed(range(1, dom_size // 2))]
+    returned = [swapped(pairs[at], 2 * at, 0) for at in reversed(range(2, dom_size // 2))]
     keep, rider = scattered(keep, rider, square)
-    keep, *returned[:-1] = lax.optimization_barrier((keep, *returned[:-1]))
+    keep, *returned = lax.optimization_barrier((keep, *returned))
     keep, rider = scattered(keep, rider, pair)
-    (returned, halo_feat), _ = lax.optimization_barrier(((returned, halo_feat), keep))
-    through = swapped(jnp.concatenate([x[per_peer:] for x in [pairs[0]] + returned[::-1]]), 1, 0)
+    (nearest, halo_feat), _ = lax.optimization_barrier(((pairs[1], halo_feat), keep))
+    returned.append(swapped(nearest, 2, 0))
     halo_back = shifted(halo_feat, "rows", -1)
     for mask in rest:
         message = swapped(with_rider(keep, rider), *mask)
         keep, rider = rounded(keep).astype(f32), rounded(rider).astype(f32)
         keep, rider = added(keep, rider, {1: message})
+
+    held = rounded(keep)
+    held, returned, halo_back = lax.optimization_barrier((held, returned, halo_back))
+    odd = [block[per_peer:] for block in [pairs[0]] + returned[::-1]]
+    through = swapped(jnp.concatenate(odd, axis=0), 1, 0)
+    held = jnp.concatenate([held, swapped(held, *pair[0])], axis=0)
+    held, through = lax.optimization_barrier((held, through))
     (grad_features,) = call(
         return_kernel,
         "return_rows",
         [shape((row_count, width), f32)],
         [own_feat, chosen, halo_back, pairs[0], through, *returned],
     )
-
-    held = rounded(keep)
-    held = jnp.concatenate([held, swapped(held, *pair[0])], axis=0)
-    held, grad_features = lax.optimization_barrier((held, grad_features))
     arrived = [swapped(held, *masks) for masks in partner_masks(square)[1:]]
+    arrived, _ = lax.optimization_barrier((arrived, grad_features))
     near = [held, *arrived]
     far = [swapped(part, *CORES) for part in near]
     grad_wq, grad_wkv, grad_wo = call(

time: 63.2 us -> 65.9 us (1.043)
  waiting for transfers between devices: 23.4 us -> 27.3 us
  starting transfers between devices: 23.4 us -> 22.2 us
    ppermute x22, waiting for transfers between devices: 23.4 us -> 27.3 us  [swapped(): return lax.ppermute(block, ('dom', 'rows'), route)]
    ppermute x22, starting transfers between devices: 23.4 us -> 22.2 us  [swapped(): return lax.ppermute(block, ('dom', 'rows'), route)]
  transfers between devices with their start and end apart: 24 -> 24, of which waited for: 16 -> 16; matrix products, arithmetic and copies ran while one was open for 1% -> 1% of each run, Pallas kernels for 9% -> 8%
where the time goes in v18:
time: 65.9 us; the launch traced here: 65.6 us
  waiting for transfers between devices  27.3 us (41%)
  starting transfers between devices  22.2 us (34%)
  Pallas kernels  14.1 us (21%)
  other arithmetic  0.99 us (2%)
  between operations  0.84 us (1%)
    ppermute x22, waiting for transfers between devices, swapped(): return lax.ppermute(block, ('dom', 'rows'), route)  27.3 us
    ppermute x22, starting transfers between devices, swapped(): return lax.ppermute(block, ('dom', 'rows'), route)  22.2 us
    pallas_call x6, Pallas kernels, call(): pl.pallas_call(kernel, out_shape=outs, in_specs=[pl.BlockSpec(memory_spac...  14.1 us
  transfers between devices with their start and end apart: 24, of which 16 were waited for; matrix products, arithmetic and copies ran while one was open for 1% of the time, Pallas kernels for 8%

profile of v18, /device:TPU:0, one launch (start us, length us, event | category | flops | bytes accessed | tf_op | source)
XLA Modules:
  0.0 65.6 jit_solution(13898701111633251386)
XLA Ops:
  0.6 1.2 %pick_rows.1 = (bf16[128,384]{1,0:T(8,128)(2,1)S(1)}, bf16[256,256]{1,0:T(8,128)(2,1)S(1)}, bf16[128,384]{1,0:T(8,128)(2,1)S(1)}, bf16[32,384]{1,0:T(8,128)(2,1)...) custom-call(bf16[256,384]{1,0:T(8,128)(2,1)} %feat_hbm.3, ...), custom_call_target="tpu_custom_call" | custom-call | bytes 623616 | tf_op jit(solution)/shard_map/pick_rows/pallas_call | solution.py:473
  1.9 3.0 %collective-permute-start = (bf16[128,384]{1,0:T(8,128)(2,1)S(1)}, bf16[128,384]{1,0:T(8,128)(2,1)S(1)}, u32[]{:S(2)}, u32[]{:S(2)}) collective-permute-start(bf16[128,384]{1,0:T(8,128)(2,1)S(1)} %get-tuple-element.63), channel_id=1, source_target_pairs={{0,4},{1,5},{2,6},{3,7},{4,0},{5,1},{6,2},{7,3},{8,12},{9,13},{10,... | collective-permute-start | bytes 294920 | tf_op jit(solution)/shard_map/ppermute | solution.py:81
  4.9 2.9 %prepare.1 = (bf16[256,384]{1,0:T(8,128)(2,1)S(1)}, bf16[384,384]{1,0:T(8,128)(2,1)S(1)}, bf16[384,768]{1,0:T(8,128)(2,1)S(1)}, bf16[384,272]{1,0:T(8,128)(2,1)S...) custom-call(bf16[256,384]{1,0:T(8,128)(2,1)} %feat_hbm.3, ...), custom_call_target="tpu_custom_call" | custom-call | flops 377487360 | bytes 4656128 | tf_op jit(solution)/shard_map/prepare/pallas_call | solution.py:473
  7.7 0.0 collective-permute-done.refs_1_
  7.8 3.9 %collective-permute-start.1 = (bf16[64,384]{1,0:T(8,128)(2,1)S(1)}, bf16[64,384]{1,0:T(8,128)(2,1)S(1)}, u32[]{:S(2)}, u32[]{:S(2)}) collective-permute-start(bf16[64,384]{1,0:T(8,128)(2,1)S(1)} %pad_maximum_fusion.7), channel_id=1, source_target_pairs={{0,24},{1,25},{2,26},{3,27},{4,28},{5,29},{6,30},{7,31},{8,16},{9,... | collective-permute-start | bytes 147464 | tf_op jit(solution)/shard_map/ppermute | solution.py:81
  11.7 0.0 collective-permute-start.2
  11.7 0.1 collective-permute-start.4
  11.8 0.6 collective-permute-start.3
  12.4 1.9 %collective-permute-done.1.refs_2_ = bf16[64,384]{1,0:T(8,128)(2,1)S(1)} collective-permute-done((bf16[64,384]{1,0:T(8,128)(2,1)S(1)}, bf16[64,384]{1,0:T(8,128)(2,1)S(1)}, u32[]{:S(2)}, u32[]{:S(2)}) %collective-permute-start.1) | collective-permute-done | bytes 49184 | tf_op jit(solution)/shard_map/ppermute | solution.py:81
  14.3 2.5 %collective-permute-done.2.refs_3_ = bf16[64,384]{1,0:T(8,128)(2,1)S(1)} collective-permute-done((bf16[64,384]{1,0:T(8,128)(2,1)S(1)}, bf16[64,384]{1,0:T(8,128)(2,1)S(1)}, u32[]{:S(2)}, u32[]{:S(2)}) %collective-permute-start.2) | collective-permute-done | bytes 49184 | tf_op jit(solution)/shard_map/ppermute | solution.py:81
  16.8 5.9 %attend.1 = (bf16[784,384]{1,0:T(8,128)(2,1)S(1)}, f32[16,384]{1,0:T(8,128)S(1)}, bf16[384,656]{1,0:T(8,128)(2,1)S(1)}, bf16[384,256]{1,0:T(8,128)(2,1)S(1)}, bf...) custom-call(bf16[32,384]{1,0:T(8,128)(2,1)S(1)} %get-tuple-element.62.refs_0_, ...), custom_call_target="tpu_custom_call" | custom-call | flops 2708471808 | bytes 5959680 | tf_op jit(solution)/shard_map/attend/pallas_call | solution.py:473
  22.7 0.1 collective-permute-start.5
  22.8 1.5 %finish.1 = (f32[256,384]{1,0:T(8,128)S(1)}, bf16[128,384]{1,0:T(8,128)(2,1)S(1)}, f32[768,384]{1,0:T(8,128)S(1)}, bf16[64,384]{1,0:T(8,128)(2,1)S(1)}, bf16[64,...) custom-call(bf16[256,384]{1,0:T(8,128)(2,1)S(1)} %get-tuple-element.59.refs_6_.og_ref, ...), custom_call_target="tpu_custom_call" | custom-call | flops 580386816 | bytes 4853760 | tf_op jit(solution)/shard_map/finish/pallas_call | solution.py:473
  24.2 0.5 collective-permute-done.5
  24.8 0.1 fusion.2
  25.1 2.4 %collective-permute-start.6 = (bf16[200,384]{1,0:T(8,128)(2,1)S(1)}, bf16[200,384]{1,0:T(8,128)(2,1)S(1)}, u32[]{:S(2)}, u32[]{:S(2)}) collective-permute-start(bf16[200,384]{1,0:T(8,128)(2,1)S(1)} %get-tuple-element.121), channel_id=1, source_target_pairs={{0,6},{1,7},{2,4},{3,5},{4,2},{5,3},{6,0},{7,1},{8,14},{9,15},{10,... | collective-permute-start | bytes 460808 | tf_op jit(solution)/shard_map/ppermute | solution.py:81
  27.5 0.6 collective-permute-start.7
  28.1 0.5 collective-permute-start.8
  28.6 1.7 %collective-permute-start.9 = (bf16[64,384]{1,0:T(8,128)(2,1)S(1)}, bf16[64,384]{1,0:T(8,128)(2,1)S(1)}, u32[]{:S(2)}, u32[]{:S(2)}) collective-permute-start(bf16[64,384]{1,0:T(8,128)(2,1)S(1)} %get-tuple-element.90), channel_id=1, source_target_pairs={{0,24},{1,25},{2,26},{3,27},{4,28},{5,29},{6,30},{7,31},{8,16},{9,... | collective-permute-start | bytes 147464 | tf_op jit(solution)/shard_map/ppermute | solution.py:81
  30.3 0.3 collective-permute-start.10
  30.6 2.2 %collective-permute-done.6 = bf16[200,384]{1,0:T(8,128)(2,1)S(1)} collective-permute-done((bf16[200,384]{1,0:T(8,128)(2,1)S(1)}, bf16[200,384]{1,0:T(8,128)(2,1)S(1)}, u32[]{:S(2)}, u32[]{:S(2)}) %collective-permute-start.6) | collective-permute-done | bytes 153632 | tf_op jit(solution)/shard_map/ppermute | solution.py:81
  32.9 2.5 %collective-permute-done.7 = bf16[200,384]{1,0:T(8,128)(2,1)S(1)} collective-permute-done((bf16[200,384]{1,0:T(8,128)(2,1)S(1)}, bf16[200,384]{1,0:T(8,128)(2,1)S(1)}, u32[]{:S(2)}, u32[]{:S(2)}) %collective-permute-start.7) | collective-permute-done | bytes 153632 | tf_op jit(solution)/shard_map/ppermute | solution.py:81
  35.3 0.0 collective-permute-done.8
  35.3 0.1 fusion.1
  35.4 0.4 collective-permute-done.10.refs_1_
  35.9 0.5 collective-permute-start.11
  36.4 4.0 %collective-permute-done.11 = bf16[104,384]{1,0:T(8,128)(2,1)S(1)} collective-permute-done((bf16[104,384]{1,0:T(8,128)(2,1)S(1)}, bf16[104,384]{1,0:T(8,128)(2,1)S(1)}, u32[]{:S(2)}, u32[]{:S(2)}) %collective-permute-start.11) | collective-permute-done | bytes 79904 | tf_op jit(solution)/shard_map/ppermute | solution.py:81
  40.4 1.9 %collective-permute-start.12 = (bf16[104,384]{1,0:T(8,128)(2,1)S(1)}, bf16[104,384]{1,0:T(8,128)(2,1)S(1)}, u32[]{:S(2)}, u32[]{:S(2)}) collective-permute-start(bf16[104,384]{1,0:T(8,128)(2,1)S(1)} %pad_maximum_fusion.6), channel_id=1, source_target_pairs={{0,16},{1,17},{2,18},{3,19},{4,20},{5,21},{6,22},{7,23},{8,24},{9,... | collective-permute-start | bytes 239624 | tf_op jit(solution)/shard_map/ppermute | solution.py:81
  42.3 0.8 %collective-permute-start.13 = (bf16[64,384]{1,0:T(8,128)(2,1)S(1)}, bf16[64,384]{1,0:T(8,128)(2,1)S(1)}, u32[]{:S(2)}, u32[]{:S(2)}) collective-permute-start(bf16[64,384]{1,0:T(8,128)(2,1)S(1)} %get-tuple-element.97), channel_id=1, source_target_pairs={{0,8},{1,9},{2,10},{3,11},{4,12},{5,13},{6,14},{7,15},{8,0},{9,1},... | collective-permute-start | bytes 147464 | tf_op jit(solution)/shard_map/ppermute | solution.py:81
  43.2 3.5 %collective-permute-done.12 = bf16[104,384]{1,0:T(8,128)(2,1)S(1)} collective-permute-done((bf16[104,384]{1,0:T(8,128)(2,1)S(1)}, bf16[104,384]{1,0:T(8,128)(2,1)S(1)}, u32[]{:S(2)}, u32[]{:S(2)}) %collective-permute-start.12) | collective-permute-done | bytes 79904 | tf_op jit(solution)/shard_map/ppermute | solution.py:81
  46.6 0.4 collective-permute-done.13.refs_2_
  47.1 0.3 collective-permute-start.15
  47.4 1.6 %collective-permute-start.16 = (bf16[128,384]{1,0:T(8,128)(2,1)S(1)}, bf16[128,384]{1,0:T(8,128)(2,1)S(1)}, u32[]{:S(2)}, u32[]{:S(2)}) collective-permute-start(bf16[128,384]{1,0:T(8,128)(2,1)S(1)} %pad_maximum_fusion.4), channel_id=1, source_target_pairs={{0,4},{1,5},{2,6},{3,7},{4,0},{5,1},{6,2},{7,3},{8,12},{9,13},{10,... | collective-permute-start | bytes 294920 | tf_op jit(solution)/shard_map/ppermute | solution.py:81
  48.9 2.6 %collective-permute-done.15 = bf16[96,384]{1,0:T(8,128)(2,1)S(1)} collective-permute-done((bf16[96,384]{1,0:T(8,128)(2,1)S(1)}, bf16[96,384]{1,0:T(8,128)(2,1)S(1)}, u32[]{:S(2)}, u32[]{:S(2)}) %collective-permute-start.15) | collective-permute-done | bytes 73760 | tf_op jit(solution)/shard_map/ppermute | solution.py:81
  51.5 1.2 %collective-permute-done.16.through_ref = bf16[128,384]{1,0:T(8,128)(2,1)S(1)} collective-permute-done((bf16[128,384]{1,0:T(8,128)(2,1)S(1)}, bf16[128,384]{1,0:T(8,128)(2,1)S(1)}, u32[]{:S(2)}, u32[]{:S(2)}) %collective-permute-start.16) | collective-permute-done | bytes 98336 | tf_op jit(solution)/shard_map/ppermute | solution.py:81
  52.7 1.7 %collective-permute-start.19 = (bf16[192,384]{1,0:T(8,128)(2,1)S(1)}, bf16[192,384]{1,0:T(8,128)(2,1)S(1)}, u32[]{:S(2)}, u32[]{:S(2)}) collective-permute-start(bf16[192,384]{1,0:T(8,128)(2,1)S(1)} %pad_maximum_fusion.3.refs_0_), channel_id=1, source_target_pairs={{0,6},{1,7},{2,4},{3,5},{4,2},{5,3},{6,0},{7,1},{8,14},{9,15},{10,... | collective-permute-start | bytes 442376 | tf_op jit(solution)/shard_map/ppermute | solution.py:81
  54.4 0.7 %collective-permute-start.18 = (bf16[192,384]{1,0:T(8,128)(2,1)S(1)}, bf16[192,384]{1,0:T(8,128)(2,1)S(1)}, u32[]{:S(2)}, u32[]{:S(2)}) collective-permute-start(bf16[192,384]{1,0:T(8,128)(2,1)S(1)} %pad_maximum_fusion.3.refs_0_), channel_id=1, source_target_pairs={{0,2},{1,3},{2,0},{3,1},{4,6},{5,7},{6,4},{7,5},{8,10},{9,11},{10,... | collective-permute-start | bytes 442376 | tf_op jit(solution)/shard_map/ppermute | solution.py:81
  55.1 1.1 %collective-permute-start.17 = (bf16[192,384]{1,0:T(8,128)(2,1)S(1)}, bf16[192,384]{1,0:T(8,128)(2,1)S(1)}, u32[]{:S(2)}, u32[]{:S(2)}) collective-permute-start(bf16[192,384]{1,0:T(8,128)(2,1)S(1)} %pad_maximum_fusion.3.refs_0_), channel_id=1, source_target_pairs={{0,4},{1,5},{2,6},{3,7},{4,0},{5,1},{6,2},{7,3},{8,12},{9,13},{10,... | collective-permute-start | bytes 442376 | tf_op jit(solution)/shard_map/ppermute | solution.py:81
  56.2 1.0 %return_rows.1 = f32[256,384]{1,0:T(8,128)} custom-call(f32[256,384]{1,0:T(8,128)S(1)} %get-tuple-element.81.gf_ref, bf16[256,256]{1,0:T(8,128)(2,1)S(1)} %get-tuple-element.82.chosen_ref, bf16[128,384]{1,0:T(8,128)(2,1)S(1)} %collective-permute-done.14.halo_ref, bf16[64,384]{1,0:T(8,128)(2,1)S(1)} %get-tuple-element.100.own_ref, ...), custom_call_target="tpu_custom_call" | custom-call | bytes 1310720 | tf_op jit(solution)/shard_map/return_rows/pallas_call | solution.py:473
  57.2 3.1 %collective-permute-done.19.refs_3_ = bf16[192,384]{1,0:T(8,128)(2,1)S(1)} collective-permute-done((bf16[192,384]{1,0:T(8,128)(2,1)S(1)}, bf16[192,384]{1,0:T(8,128)(2,1)S(1)}, u32[]{:S(2)}, u32[]{:S(2)}) %collective-permute-start.19) | collective-permute-done | bytes 147488 | tf_op jit(solution)/shard_map/ppermute | solution.py:81
  60.4 1.7 %collective-permute-done.18.refs_2_ = bf16[192,384]{1,0:T(8,128)(2,1)S(1)} collective-permute-done((bf16[192,384]{1,0:T(8,128)(2,1)S(1)}, bf16[192,384]{1,0:T(8,128)(2,1)S(1)}, u32[]{:S(2)}, u32[]{:S(2)}) %collective-permute-start.18) | collective-permute-done | bytes 147488 | tf_op jit(solution)/shard_map/ppermute | solution.py:81
  62.0 0.5 collective-permute-start.22
  62.6 0.0 collective-permute-start.23
  62.6 0.6 convert_add_fusion.2
  63.2 0.3 collective-permute-done.21.refs_5_
  63.4 0.2 collective-permute-done.22.refs_6_
  63.6 0.3 collective-permute-done.23.refs_7_
  63.9 1.6 %place_sums.1 = (f32[384,384]{1,0:T(8,128)}, f32[384,768]{1,0:T(8,128)}, f32[384,384]{1,0:T(8,128)}) custom-call(bf16[192,384]{1,0:T(8,128)(2,1)S(1)} %pad_maximum_fusion.3.refs_0_, bf16[192,384]{1,0:T(8,128)(2,1)S(1)} %collective-permute-done.17.refs_1_, bf16[192,384]{1,0:T(8,128)(2,1)S(1)} %collective-permute-done.18.refs_2_, ...), custom_call_target="tpu_custom_call" | custom-call | bytes 3538944 | tf_op jit(solution)/shard_map/place_sums/pallas_call | solution.py:473
  (31 shorter events, 0.3 us)
Async XLA Ops:
  1.9 5.9 %collective-permute-start = (bf16[128,384]{1,0:T(8,128)(2,1)S(1)}, bf16[128,384]{1,0:T(8,128)(2,1)S(1)}, u32[]{:S(2)}, u32[]{:S(2)}) collective-permute-start(bf16[128,384]{1,0:T(8,128)(2,1)S(1)} %get-tuple-element.63), channel_id=1, source_target_pairs={{0,4},{1,5},{2,6},{3,7},{4,0},{5,1},{6,2},{7,3},{8,12},{9,13},{10,... | collective-permute-start | bytes 294920 | tf_op jit(solution)/shard_map/ppermute | solution.py:81
  7.8 6.5 %collective-permute-start.1 = (bf16[64,384]{1,0:T(8,128)(2,1)S(1)}, bf16[64,384]{1,0:T(8,128)(2,1)S(1)}, u32[]{:S(2)}, u32[]{:S(2)}) collective-permute-start(bf16[64,384]{1,0:T(8,128)(2,1)S(1)} %pad_maximum_fusion.7), channel_id=1, source_target_pairs={{0,24},{1,25},{2,26},{3,27},{4,28},{5,29},{6,30},{7,31},{8,16},{9,... | collective-permute-start | bytes 147464 | tf_op jit(solution)/shard_map/ppermute | solution.py:81
  11.7 5.1 %collective-permute-start.2 = (bf16[64,384]{1,0:T(8,128)(2,1)S(1)}, bf16[64,384]{1,0:T(8,128)(2,1)S(1)}, u32[]{:S(2)}, u32[]{:S(2)}) collective-permute-start(bf16[64,384]{1,0:T(8,128)(2,1)S(1)} %pad_maximum_fusion.8), channel_id=1, source_target_pairs={{0,16},{1,17},{2,18},{3,19},{4,20},{5,21},{6,22},{7,23},{8,24},{9,... | collective-permute-start | bytes 147464 | tf_op jit(solution)/shard_map/ppermute | solution.py:81
  11.7 5.1 %collective-permute-start.4 = (bf16[128,384]{1,0:T(8,128)(2,1)S(1)}, bf16[128,384]{1,0:T(8,128)(2,1)S(1)}, u32[]{:S(2)}, u32[]{:S(2)}) collective-permute-start(bf16[128,384]{1,0:T(8,128)(2,1)S(1)} %get-tuple-element.69), channel_id=1, source_target_pairs={{3,0},{0,1},{1,2},{2,3},{7,4},{4,5},{5,6},{6,7},{11,8},{8,9},{9,10... | collective-permute-start | bytes 294920 | tf_op jit(solution)/shard_map/ppermute | solution.py:87
  11.8 5.0 %collective-permute-start.3 = (bf16[64,384]{1,0:T(8,128)(2,1)S(1)}, bf16[64,384]{1,0:T(8,128)(2,1)S(1)}, u32[]{:S(2)}, u32[]{:S(2)}) collective-permute-start(bf16[64,384]{1,0:T(8,128)(2,1)S(1)} %pad_maximum_fusion.9), channel_id=1, source_target_pairs={{0,8},{1,9},{2,10},{3,11},{4,12},{5,13},{6,14},{7,15},{8,0},{9,1},... | collective-permute-start | bytes 147464 | tf_op jit(solution)/shard_map/ppermute | solution.py:81
  22.7 2.1 %collective-permute-start.5 = (bf16[784,384]{1,0:T(8,128)(2,1)S(1)}, bf16[784,384]{1,0:T(8,128)(2,1)S(1)}, u32[]{:S(2)}, u32[]{:S(2)}) collective-permute-start(bf16[784,384]{1,0:T(8,128)(2,1)S(1)} %get-tuple-element.84), channel_id=1, source_target_pairs={{0,1},{1,0},{2,3},{3,2},{4,5},{5,4},{6,7},{7,6},{8,9},{9,8},{10,11... | collective-permute-start | bytes 1806344 | tf_op jit(solution)/shard_map/ppermute | solution.py:81
  25.1 7.8 %collective-permute-start.6 = (bf16[200,384]{1,0:T(8,128)(2,1)S(1)}, bf16[200,384]{1,0:T(8,128)(2,1)S(1)}, u32[]{:S(2)}, u32[]{:S(2)}) collective-permute-start(bf16[200,384]{1,0:T(8,128)(2,1)S(1)} %get-tuple-element.121), channel_id=1, source_target_pairs={{0,6},{1,7},{2,4},{3,5},{4,2},{5,3},{6,0},{7,1},{8,14},{9,15},{10,... | collective-permute-start | bytes 460808 | tf_op jit(solution)/shard_map/ppermute | solution.py:81
  27.5 7.9 %collective-permute-start.7 = (bf16[200,384]{1,0:T(8,128)(2,1)S(1)}, bf16[200,384]{1,0:T(8,128)(2,1)S(1)}, u32[]{:S(2)}, u32[]{:S(2)}) collective-permute-start(bf16[200,384]{1,0:T(8,128)(2,1)S(1)} %get-tuple-element.122), channel_id=1, source_target_pairs={{0,2},{1,3},{2,0},{3,1},{4,6},{5,7},{6,4},{7,5},{8,10},{9,11},{10,... | collective-permute-start | bytes 460808 | tf_op jit(solution)/shard_map/ppermute | solution.py:81
  28.1 7.3 %collective-permute-start.8 = (bf16[200,384]{1,0:T(8,128)(2,1)S(1)}, bf16[200,384]{1,0:T(8,128)(2,1)S(1)}, u32[]{:S(2)}, u32[]{:S(2)}) collective-permute-start(bf16[200,384]{1,0:T(8,128)(2,1)S(1)} %get-tuple-element.123), channel_id=1, source_target_pairs={{0,4},{1,5},{2,6},{3,7},{4,0},{5,1},{6,2},{7,3},{8,12},{9,13},{10,... | collective-permute-start | bytes 460808 | tf_op jit(solution)/shard_map/ppermute | solution.py:81
  28.6 6.8 %collective-permute-start.9 = (bf16[64,384]{1,0:T(8,128)(2,1)S(1)}, bf16[64,384]{1,0:T(8,128)(2,1)S(1)}, u32[]{:S(2)}, u32[]{:S(2)}) collective-permute-start(bf16[64,384]{1,0:T(8,128)(2,1)S(1)} %get-tuple-element.90), channel_id=1, source_target_pairs={{0,24},{1,25},{2,26},{3,27},{4,28},{5,29},{6,30},{7,31},{8,16},{9,... | collective-permute-start | bytes 147464 | tf_op jit(solution)/shard_map/ppermute | solution.py:81
  30.3 5.5 %collective-permute-start.10 = (bf16[64,384]{1,0:T(8,128)(2,1)S(1)}, bf16[64,384]{1,0:T(8,128)(2,1)S(1)}, u32[]{:S(2)}, u32[]{:S(2)}) collective-permute-start(bf16[64,384]{1,0:T(8,128)(2,1)S(1)} %get-tuple-element.91), channel_id=1, source_target_pairs={{0,16},{1,17},{2,18},{3,19},{4,20},{5,21},{6,22},{7,23},{8,24},{9,... | collective-permute-start | bytes 147464 | tf_op jit(solution)/shard_map/ppermute | solution.py:81
  35.9 4.5 %collective-permute-start.11 = (bf16[104,384]{1,0:T(8,128)(2,1)S(1)}, bf16[104,384]{1,0:T(8,128)(2,1)S(1)}, u32[]{:S(2)}, u32[]{:S(2)}) collective-permute-start(bf16[104,384]{1,0:T(8,128)(2,1)S(1)} %pad_maximum_fusion.5), channel_id=1, source_target_pairs={{0,8},{1,9},{2,10},{3,11},{4,12},{5,13},{6,14},{7,15},{8,0},{9,1},... | collective-permute-start | bytes 239624 | tf_op jit(solution)/shard_map/ppermute | solution.py:81
  40.4 6.2 %collective-permute-start.12 = (bf16[104,384]{1,0:T(8,128)(2,1)S(1)}, bf16[104,384]{1,0:T(8,128)(2,1)S(1)}, u32[]{:S(2)}, u32[]{:S(2)}) collective-permute-start(bf16[104,384]{1,0:T(8,128)(2,1)S(1)} %pad_maximum_fusion.6), channel_id=1, source_target_pairs={{0,16},{1,17},{2,18},{3,19},{4,20},{5,21},{6,22},{7,23},{8,24},{9,... | collective-permute-start | bytes 239624 | tf_op jit(solution)/shard_map/ppermute | solution.py:81
  42.3 4.8 %collective-permute-start.13 = (bf16[64,384]{1,0:T(8,128)(2,1)S(1)}, bf16[64,384]{1,0:T(8,128)(2,1)S(1)}, u32[]{:S(2)}, u32[]{:S(2)}) collective-permute-start(bf16[64,384]{1,0:T(8,128)(2,1)S(1)} %get-tuple-element.97), channel_id=1, source_target_pairs={{0,8},{1,9},{2,10},{3,11},{4,12},{5,13},{6,14},{7,15},{8,0},{9,1},... | collective-permute-start | bytes 147464 | tf_op jit(solution)/shard_map/ppermute | solution.py:81
  43.1 3.9 %collective-permute-start.14 = (bf16[128,384]{1,0:T(8,128)(2,1)S(1)}, bf16[128,384]{1,0:T(8,128)(2,1)S(1)}, u32[]{:S(2)}, u32[]{:S(2)}) collective-permute-start(bf16[128,384]{1,0:T(8,128)(2,1)S(1)} %get-tuple-element.98), channel_id=1, source_target_pairs={{1,0},{2,1},{3,2},{0,3},{5,4},{6,5},{7,6},{4,7},{9,8},{10,9},{11,1... | collective-permute-start | bytes 294920 | tf_op jit(solution)/shard_map/ppermute | solution.py:87
  47.1 4.4 %collective-permute-start.15 = (bf16[96,384]{1,0:T(8,128)(2,1)S(1)}, bf16[96,384]{1,0:T(8,128)(2,1)S(1)}, u32[]{:S(2)}, u32[]{:S(2)}) collective-permute-start(bf16[96,384]{1,0:T(8,128)(2,1)S(1)} %add_convert_fusion), channel_id=1, source_target_pairs={{0,8},{1,9},{2,10},{3,11},{4,12},{5,13},{6,14},{7,15},{8,0},{9,1},... | collective-permute-start | bytes 221192 | tf_op jit(solution)/shard_map/ppermute | solution.py:81
  47.4 5.4 %collective-permute-start.16 = (bf16[128,384]{1,0:T(8,128)(2,1)S(1)}, bf16[128,384]{1,0:T(8,128)(2,1)S(1)}, u32[]{:S(2)}, u32[]{:S(2)}) collective-permute-start(bf16[128,384]{1,0:T(8,128)(2,1)S(1)} %pad_maximum_fusion.4), channel_id=1, source_target_pairs={{0,4},{1,5},{2,6},{3,7},{4,0},{5,1},{6,2},{7,3},{8,12},{9,13},{10,... | collective-permute-start | bytes 294920 | tf_op jit(solution)/shard_map/ppermute | solution.py:81
  52.7 7.6 %collective-permute-start.19 = (bf16[192,384]{1,0:T(8,128)(2,1)S(1)}, bf16[192,384]{1,0:T(8,128)(2,1)S(1)}, u32[]{:S(2)}, u32[]{:S(2)}) collective-permute-start(bf16[192,384]{1,0:T(8,128)(2,1)S(1)} %pad_maximum_fusion.3.refs_0_), channel_id=1, source_target_pairs={{0,6},{1,7},{2,4},{3,5},{4,2},{5,3},{6,0},{7,1},{8,14},{9,15},{10,... | collective-permute-start | bytes 442376 | tf_op jit(solution)/shard_map/ppermute | solution.py:81
  54.4 7.6 %collective-permute-start.18 = (bf16[192,384]{1,0:T(8,128)(2,1)S(1)}, bf16[192,384]{1,0:T(8,128)(2,1)S(1)}, u32[]{:S(2)}, u32[]{:S(2)}) collective-permute-start(bf16[192,384]{1,0:T(8,128)(2,1)S(1)} %pad_maximum_fusion.3.refs_0_), channel_id=1, source_target_pairs={{0,2},{1,3},{2,0},{3,1},{4,6},{5,7},{6,4},{7,5},{8,10},{9,11},{10,... | collective-permute-start | bytes 442376 | tf_op jit(solution)/shard_map/ppermute | solution.py:81
  55.1 6.9 %collective-permute-start.17 = (bf16[192,384]{1,0:T(8,128)(2,1)S(1)}, bf16[192,384]{1,0:T(8,128)(2,1)S(1)}, u32[]{:S(2)}, u32[]{:S(2)}) collective-permute-start(bf16[192,384]{1,0:T(8,128)(2,1)S(1)} %pad_maximum_fusion.3.refs_0_), channel_id=1, source_target_pairs={{0,4},{1,5},{2,6},{3,7},{4,0},{5,1},{6,2},{7,3},{8,12},{9,13},{10,... | collective-permute-start | bytes 442376 | tf_op jit(solution)/shard_map/ppermute | solution.py:81
  56.2 6.9 %collective-permute-start.20 = (bf16[192,384]{1,0:T(8,128)(2,1)S(1)}, bf16[192,384]{1,0:T(8,128)(2,1)S(1)}, u32[]{:S(2)}, u32[]{:S(2)}) collective-permute-start(bf16[192,384]{1,0:T(8,128)(2,1)S(1)} %pad_maximum_fusion.3.refs_0_), channel_id=1, source_target_pairs={{0,1},{1,0},{2,3},{3,2},{4,5},{5,4},{6,7},{7,6},{8,9},{9,8},{10,11... | collective-permute-start | bytes 442376 | tf_op jit(solution)/shard_map/ppermute | solution.py:81
  62.0 1.4 %collective-permute-start.21 = (bf16[192,384]{1,0:T(8,128)(2,1)S(1)}, bf16[192,384]{1,0:T(8,128)(2,1)S(1)}, u32[]{:S(2)}, u32[]{:S(2)}) collective-permute-start(bf16[192,384]{1,0:T(8,128)(2,1)S(1)} %collective-permute-done.17.refs_1_), channel_id=1, source_target_pairs={{0,1},{1,0},{2,3},{3,2},{4,5},{5,4},{6,7},{7,6},{8,9},{9,8},{10,11... | collective-permute-start | bytes 442376 | tf_op jit(solution)/shard_map/ppermute | solution.py:81
  62.0 1.6 %collective-permute-start.22 = (bf16[192,384]{1,0:T(8,128)(2,1)S(1)}, bf16[192,384]{1,0:T(8,128)(2,1)S(1)}, u32[]{:S(2)}, u32[]{:S(2)}) collective-permute-start(bf16[192,384]{1,0:T(8,128)(2,1)S(1)} %collective-permute-done.18.refs_2_), channel_id=1, source_target_pairs={{0,1},{1,0},{2,3},{3,2},{4,5},{5,4},{6,7},{7,6},{8,9},{9,8},{10,11... | collective-permute-start | bytes 442376 | tf_op jit(solution)/shard_map/ppermute | solution.py:81
  62.6 1.4 %collective-permute-start.23 = (bf16[192,384]{1,0:T(8,128)(2,1)S(1)}, bf16[192,384]{1,0:T(8,128)(2,1)S(1)}, u32[]{:S(2)}, u32[]{:S(2)}) collective-permute-start(bf16[192,384]{1,0:T(8,128)(2,1)S(1)} %collective-permute-done.19.refs_3_), channel_id=1, source_target_pairs={{0,1},{1,0},{2,3},{3,2},{4,5},{5,4},{6,7},{7,6},{8,9},{9,8},{10,11... | collective-permute-start | bytes 442376 | tf_op jit(solution)/shard_map/ppermute | solution.py:81

commit v19 on v15

--- a/solution.py
+++ b/solution.py
@@ -292,78 +292,86 @@
         low, high = head * head_dim, (head + 1) * head_dim
         return low, high, low // LANES * LANES, min(-(-high // LANES) * LANES, width)
 
-    def products(head):
+    def product(head, rows_ref, start):
         low, high, first, last = bounds(head)
         column = lax.broadcasted_iota(jnp.int32, (last - first, row_count), 0) + first
         of_head = (column >= low) & (column < high)
-        out = []
-        for rows_ref, start in ((qt_ref, 0), (odt_ref, width)):
-            operand = jnp.where(of_head, rows_ref[first:last, :], 0)
-            every = f32_dot(kv_ref[:, start + first : start + last], operand)
-            out.append(tiles(lambda t, lanes: every[t * tile : (t + 2) * tile, lanes]))
-            out.append(every[near:])
-        return out
-
-    def weights(s_local, s_far, dp_local, dp_far):
-        s_local += local_bias_ref[...]
-        s_far += far_bias_ref[...]
-        peak = jnp.maximum(
-            jnp.max(s_local, axis=0, keepdims=True), jnp.max(s_far, axis=0, keepdims=True)
+        operand = jnp.where(of_head, rows_ref[first:last, :], 0)
+        every = f32_dot(kv_ref[:, start + first : start + last], operand)
+        return tiles(lambda t, lanes: every[t * tile : (t + 2) * tile, lanes]), every[near:]
+
+    def scores(head):
+        return product(head, qt_ref, 0)
+
+    def dprobs(head):
+        return product(head, odt_ref, width)
+
+    def to_queries(head, start, local, beyond):
+        low, high, _, _ = bounds(head)
+        rows = slice(start + low, start + high)
+        near_part = tiles(
+            lambda t, lanes: f32_dot(kvt_ref[rows, t * tile : (t + 2) * tile], local[:, lanes])
         )
-        exponent_scale = scale * math.log2(math.e)
-        e_local = jnp.exp2((s_local - peak) * exponent_scale)
-        e_far = jnp.exp2((s_far - peak) * exponent_scale)
-        total = jnp.sum(e_local, axis=0, keepdims=True) + jnp.sum(e_far, axis=0, keepdims=True)
-        inverse = 1.0 / total
-        p_local = e_local * inverse
-        p_far = e_far * inverse
-        delta = jnp.sum(p_local * dp_local, axis=0, keepdims=True) + jnp.sum(
-            p_far * dp_far, axis=0, keepdims=True
+        return near_part + f32_dot(kvt_ref[rows, near:], beyond)
+
+    def to_keys(head, start, rows_ref, local, beyond, factor):
+        low, high, _, _ = bounds(head)
+        operand = rows_ref[low:high]
+        parts = []
+        carried = None
+        for t in range(tile_count):
+            lanes = slice(t * tile, (t + 1) * tile)
+            window = times_transposed(operand[:, lanes], local[:, lanes])
+            previous = window[:, :tile]
+            parts.append(previous if carried is None else previous + carried)
+            carried = window[:, tile:]
+        parts.append(carried)
+        parts.append(times_transposed(operand, beyond))
+        gathered = jnp.concatenate(parts, axis=1)
+        gkvt_ref[start + low : start + high] = rounded(
+            gathered if factor is None else gathered * factor
         )
-        ds_local = rounded(p_local * (dp_local - delta))
-        ds_far = rounded(p_far * (dp_far - delta))
-        return rounded(p_local), rounded(p_far), ds_local, ds_far
-
-    def outputs(head, pb_local, pb_far, ds_local, ds_far):
-        low, high, _, _ = bounds(head)
-
-        def to_queries(start, local, beyond):
-            rows = slice(start + low, start + high)
-            near_part = tiles(
-                lambda t, lanes: f32_dot(kvt_ref[rows, t * tile : (t + 2) * tile], local[:, lanes])
+
+    def step(head, given, done):
+        if head < HEADS:
+            (s_local, s_far), (dp_local, dp_far) = given
+            s_local += local_bias_ref[...]
+            s_far += far_bias_ref[...]
+            peak = jnp.maximum(
+                jnp.max(s_local, axis=0, keepdims=True), jnp.max(s_far, axis=0, keepdims=True)
             )
-            return near_part + f32_dot(kvt_ref[rows, near:], beyond)
-
-        def to_keys(start, operand, local, beyond, factor):
-            rows = slice(start + low, start + high)
-            parts = []
-            carried = None
-            for t in range(tile_count):
-                lanes = slice(t * tile, (t + 1) * tile)
-                window = times_transposed(operand[:, lanes], local[:, lanes])
-                previous = window[:, :tile]
-                parts.append(previous if carried is None else previous + carried)
-                carried = window[:, tile:]
-            parts.append(carried)
-            parts.append(times_transposed(operand, beyond))
-            gathered = jnp.concatenate(parts, axis=1)
-            gkvt_ref[rows] = rounded(gathered if factor is None else gathered * factor)
-
-        ot_ref[low:high] = rounded(to_queries(width, pb_local, pb_far))
-        gqt_ref[low:high] = rounded(to_queries(0, ds_local, ds_far) * scale)
-        to_keys(0, qt_ref[low:high], ds_local, ds_far, scale)
-        to_keys(width, odt_ref[low:high], pb_local, pb_far, None)
-
-    coming = products(0)
-    done = None
-    for head in range(HEADS):
-        now = coming
-        if head + 1 < HEADS:
-            coming = products(head + 1)
-        if done is not None:
-            outputs(head - 1, *done)
-        done = weights(*now)
-    outputs(HEADS - 1, *done)
+        if done:
+            low, high, _, _ = bounds(head - 1)
+            pb_before, ds_before = done
+            ot_ref[low:high] = rounded(to_queries(head - 1, width, *pb_before))
+        if head < HEADS:
+            exponent_scale = scale * math.log2(math.e)
+            e_local = jnp.exp2((s_local - peak) * exponent_scale)
+            e_far = jnp.exp2((s_far - peak) * exponent_scale)
+            total = jnp.sum(e_local, axis=0, keepdims=True) + jnp.sum(e_far, axis=0, keepdims=True)
+            inverse = 1.0 / total
+        coming_scores = scores(head + 1) if head + 1 < HEADS else None
+        if done:
+            gqt_ref[low:high] = rounded(to_queries(head - 1, 0, *ds_before) * scale)
+        if head < HEADS:
+            p_local = e_local * inverse
+            p_far = e_far * inverse
+            delta = jnp.sum(p_local * dp_local, axis=0, keepdims=True) + jnp.sum(
+                p_far * dp_far, axis=0, keepdims=True
+            )
+            pb = rounded(p_local), rounded(p_far)
+        coming_dprobs = dprobs(head + 1) if head + 1 < HEADS else None
+        if done:
+            to_keys(head - 1, width, odt_ref, *pb_before, None)
+        if head < HEADS:
+            ds = rounded(p_local * (dp_local - delta)), rounded(p_far * (dp_far - delta))
+        if done:
+            to_keys(head - 1, 0, qt_ref, *ds_before, scale)
+        return (coming_scores, coming_dprobs), (pb, ds) if head < HEADS else None
+
+    given, done = (scores(0), dprobs(0)), None
+    for head in range(HEADS + 1):
+        given, done = step(head, given, done)
 
     rider_ref[...] = f32_dot(wkv_ref[...], gkvt_ref[:, virt_at:]).T * factor
     weight_sums(

time: 63.2 us -> 63.3 us (level)
  no operation moved by 1% of the time
where the time goes in v19:
time: 63.3 us; the launch traced here: 63 us
  starting transfers between devices  23.4 us (37%)
  waiting for transfers between devices  23.4 us (37%)
  Pallas kernels  14.2 us (22%)
  other arithmetic  1 us (2%)
  between operations  0.83 us (1%)
    ppermute x22, waiting for transfers between devices, swapped(): return lax.ppermute(block, ('dom', 'rows'), route)  23.4 us
    ppermute x22, starting transfers between devices, swapped(): return lax.ppermute(block, ('dom', 'rows'), route)  23.4 us
    pallas_call x6, Pallas kernels, call(): pl.pallas_call(kernel, out_shape=outs, in_specs=[pl.BlockSpec(memory_spac...  14.2 us
  transfers between devices with their start and end apart: 24, of which 16 were waited for; matrix products, arithmetic and copies ran while one was open for 1% of the time, Pallas kernels for 9%

profile of v19, /device:TPU:0, one launch (start us, length us, event | category | flops | bytes accessed | tf_op | source)
XLA Modules:
  0.0 63.0 jit_solution(11391995846430993855)
XLA Ops:
  0.6 1.2 %pick_rows.1 = (bf16[128,384]{1,0:T(8,128)(2,1)S(1)}, bf16[256,256]{1,0:T(8,128)(2,1)S(1)}, bf16[128,384]{1,0:T(8,128)(2,1)S(1)}, bf16[32,384]{1,0:T(8,128)(2,1)...) custom-call(bf16[256,384]{1,0:T(8,128)(2,1)} %feat_hbm.3, ...), custom_call_target="tpu_custom_call" | custom-call | bytes 623616 | tf_op jit(solution)/shard_map/pick_rows/pallas_call | solution.py:481
  1.9 3.0 %collective-permute-start = (bf16[128,384]{1,0:T(8,128)(2,1)S(1)}, bf16[128,384]{1,0:T(8,128)(2,1)S(1)}, u32[]{:S(2)}, u32[]{:S(2)}) collective-permute-start(bf16[128,384]{1,0:T(8,128)(2,1)S(1)} %get-tuple-element.57), channel_id=1, source_target_pairs={{0,4},{1,5},{2,6},{3,7},{4,0},{5,1},{6,2},{7,3},{8,12},{9,13},{10,... | collective-permute-start | bytes 294920 | tf_op jit(solution)/shard_map/ppermute | solution.py:81
  4.9 2.9 %prepare.1 = (bf16[256,384]{1,0:T(8,128)(2,1)S(1)}, bf16[384,384]{1,0:T(8,128)(2,1)S(1)}, bf16[384,768]{1,0:T(8,128)(2,1)S(1)}, bf16[384,272]{1,0:T(8,128)(2,1)S...) custom-call(bf16[256,384]{1,0:T(8,128)(2,1)} %feat_hbm.3, ...), custom_call_target="tpu_custom_call" | custom-call | flops 377487360 | bytes 4656128 | tf_op jit(solution)/shard_map/prepare/pallas_call | solution.py:481
  7.8 3.9 %collective-permute-start.1 = (bf16[64,384]{1,0:T(8,128)(2,1)S(1)}, bf16[64,384]{1,0:T(8,128)(2,1)S(1)}, u32[]{:S(2)}, u32[]{:S(2)}) collective-permute-start(bf16[64,384]{1,0:T(8,128)(2,1)S(1)} %pad_maximum_fusion.7), channel_id=1, source_target_pairs={{0,24},{1,25},{2,26},{3,27},{4,28},{5,29},{6,30},{7,31},{8,16},{9,... | collective-permute-start | bytes 147464 | tf_op jit(solution)/shard_map/ppermute | solution.py:81
  11.7 0.1 collective-permute-start.4
  11.8 0.6 %collective-permute-start.3 = (bf16[64,384]{1,0:T(8,128)(2,1)S(1)}, bf16[64,384]{1,0:T(8,128)(2,1)S(1)}, u32[]{:S(2)}, u32[]{:S(2)}) collective-permute-start(bf16[64,384]{1,0:T(8,128)(2,1)S(1)} %pad_maximum_fusion.9), channel_id=1, source_target_pairs={{0,8},{1,9},{2,10},{3,11},{4,12},{5,13},{6,14},{7,15},{8,0},{9,1},... | collective-permute-start | bytes 147464 | tf_op jit(solution)/shard_map/ppermute | solution.py:81
  12.4 1.9 %collective-permute-done.1.refs_2_ = bf16[64,384]{1,0:T(8,128)(2,1)S(1)} collective-permute-done((bf16[64,384]{1,0:T(8,128)(2,1)S(1)}, bf16[64,384]{1,0:T(8,128)(2,1)S(1)}, u32[]{:S(2)}, u32[]{:S(2)}) %collective-permute-start.1) | collective-permute-done | bytes 49184 | tf_op jit(solution)/shard_map/ppermute | solution.py:81
  14.3 2.5 %collective-permute-done.2.refs_3_ = bf16[64,384]{1,0:T(8,128)(2,1)S(1)} collective-permute-done((bf16[64,384]{1,0:T(8,128)(2,1)S(1)}, bf16[64,384]{1,0:T(8,128)(2,1)S(1)}, u32[]{:S(2)}, u32[]{:S(2)}) %collective-permute-start.2) | collective-permute-done | bytes 49184 | tf_op jit(solution)/shard_map/ppermute | solution.py:81
  16.8 0.0 collective-permute-done.3.refs_4_
  16.8 0.0 collective-permute-done.4.refs_5_
  16.8 6.0 %attend.1 = (bf16[784,384]{1,0:T(8,128)(2,1)S(1)}, f32[16,384]{1,0:T(8,128)S(1)}, bf16[384,656]{1,0:T(8,128)(2,1)S(1)}, bf16[384,256]{1,0:T(8,128)(2,1)S(1)}, bf...) custom-call(bf16[32,384]{1,0:T(8,128)(2,1)S(1)} %get-tuple-element.56.refs_0_, ...), custom_call_target="tpu_custom_call" | custom-call | flops 2708471808 | bytes 5959680 | tf_op jit(solution)/shard_map/attend/pallas_call | solution.py:481
  22.8 0.1 collective-permute-start.5
  22.9 1.5 %finish.1 = (f32[256,384]{1,0:T(8,128)S(1)}, bf16[128,384]{1,0:T(8,128)(2,1)S(1)}, f32[768,384]{1,0:T(8,128)S(1)}, bf16[64,384]{1,0:T(8,128)(2,1)S(1)}, bf16[64,...) custom-call(bf16[256,384]{1,0:T(8,128)(2,1)S(1)} %get-tuple-element.53.refs_6_.og_ref, ...), custom_call_target="tpu_custom_call" | custom-call | flops 580386816 | bytes 4853760 | tf_op jit(solution)/shard_map/finish/pallas_call | solution.py:481
  24.3 0.5 collective-permute-done.5
  24.9 0.1 fusion.2
  25.2 2.4 %collective-permute-start.6 = (bf16[200,384]{1,0:T(8,128)(2,1)S(1)}, bf16[200,384]{1,0:T(8,128)(2,1)S(1)}, u32[]{:S(2)}, u32[]{:S(2)}) collective-permute-start(bf16[200,384]{1,0:T(8,128)(2,1)S(1)} %get-tuple-element.109), channel_id=1, source_target_pairs={{0,6},{1,7},{2,4},{3,5},{4,2},{5,3},{6,0},{7,1},{8,14},{9,15},{10,... | collective-permute-start | bytes 460808 | tf_op jit(solution)/shard_map/ppermute | solution.py:81
  27.6 0.6 collective-permute-start.7
  28.2 0.5 collective-permute-start.8
  28.7 1.7 %collective-permute-start.9 = (bf16[64,384]{1,0:T(8,128)(2,1)S(1)}, bf16[64,384]{1,0:T(8,128)(2,1)S(1)}, u32[]{:S(2)}, u32[]{:S(2)}) collective-permute-start(bf16[64,384]{1,0:T(8,128)(2,1)S(1)} %get-tuple-element.82), channel_id=1, source_target_pairs={{0,24},{1,25},{2,26},{3,27},{4,28},{5,29},{6,30},{7,31},{8,16},{9,... | collective-permute-start | bytes 147464 | tf_op jit(solution)/shard_map/ppermute | solution.py:81
  30.4 0.3 collective-permute-start.10
  30.7 2.2 %collective-permute-done.6 = bf16[200,384]{1,0:T(8,128)(2,1)S(1)} collective-permute-done((bf16[200,384]{1,0:T(8,128)(2,1)S(1)}, bf16[200,384]{1,0:T(8,128)(2,1)S(1)}, u32[]{:S(2)}, u32[]{:S(2)}) %collective-permute-start.6) | collective-permute-done | bytes 153632 | tf_op jit(solution)/shard_map/ppermute | solution.py:81
  32.9 2.5 %collective-permute-done.7 = bf16[200,384]{1,0:T(8,128)(2,1)S(1)} collective-permute-done((bf16[200,384]{1,0:T(8,128)(2,1)S(1)}, bf16[200,384]{1,0:T(8,128)(2,1)S(1)}, u32[]{:S(2)}, u32[]{:S(2)}) %collective-permute-start.7) | collective-permute-done | bytes 153632 | tf_op jit(solution)/shard_map/ppermute | solution.py:81
  35.4 0.0 collective-permute-done.8
  35.4 0.1 fusion.1
  35.5 0.4 collective-permute-done.10.refs_1_
  36.0 0.5 collective-permute-start.11
  36.5 1.6 %collective-permute-start.14 = (bf16[64,384]{1,0:T(8,128)(2,1)S(1)}, bf16[64,384]{1,0:T(8,128)(2,1)S(1)}, u32[]{:S(2)}, u32[]{:S(2)}) collective-permute-start(bf16[64,384]{1,0:T(8,128)(2,1)S(1)} %get-tuple-element.89), channel_id=1, source_target_pairs={{0,8},{1,9},{2,10},{3,11},{4,12},{5,13},{6,14},{7,15},{8,0},{9,1},... | collective-permute-start | bytes 147464 | tf_op jit(solution)/shard_map/ppermute | solution.py:81
  38.1 2.4 %collective-permute-done.11 = bf16[104,384]{1,0:T(8,128)(2,1)S(1)} collective-permute-done((bf16[104,384]{1,0:T(8,128)(2,1)S(1)}, bf16[104,384]{1,0:T(8,128)(2,1)S(1)}, u32[]{:S(2)}, u32[]{:S(2)}) %collective-permute-start.11) | collective-permute-done | bytes 79904 | tf_op jit(solution)/shard_map/ppermute | solution.py:81
  40.5 0.5 collective-permute-done.14.refs_2_
  41.1 2.3 %collective-permute-start.12 = (bf16[104,384]{1,0:T(8,128)(2,1)S(1)}, bf16[104,384]{1,0:T(8,128)(2,1)S(1)}, u32[]{:S(2)}, u32[]{:S(2)}) collective-permute-start(bf16[104,384]{1,0:T(8,128)(2,1)S(1)} %pad_maximum_fusion.6), channel_id=1, source_target_pairs={{0,16},{1,17},{2,18},{3,19},{4,20},{5,21},{6,22},{7,23},{8,24},{9,... | collective-permute-start | bytes 239624 | tf_op jit(solution)/shard_map/ppermute | solution.py:81
  43.4 1.5 %collective-permute-start.16 = (bf16[128,384]{1,0:T(8,128)(2,1)S(1)}, bf16[128,384]{1,0:T(8,128)(2,1)S(1)}, u32[]{:S(2)}, u32[]{:S(2)}) collective-permute-start(bf16[128,384]{1,0:T(8,128)(2,1)S(1)} %pad_maximum_fusion.4), channel_id=1, source_target_pairs={{0,4},{1,5},{2,6},{3,7},{4,0},{5,1},{6,2},{7,3},{8,12},{9,13},{10,... | collective-permute-start | bytes 294920 | tf_op jit(solution)/shard_map/ppermute | solution.py:81
  44.9 2.4 %collective-permute-done.12 = bf16[104,384]{1,0:T(8,128)(2,1)S(1)} collective-permute-done((bf16[104,384]{1,0:T(8,128)(2,1)S(1)}, bf16[104,384]{1,0:T(8,128)(2,1)S(1)}, u32[]{:S(2)}, u32[]{:S(2)}) %collective-permute-start.12) | collective-permute-done | bytes 79904 | tf_op jit(solution)/shard_map/ppermute | solution.py:81
  47.3 0.5 collective-permute-start.13
  47.8 0.3 collective-permute-done.16.through_ref
  48.1 0.0 collective-permute-done.15.halo_ref
  48.1 1.0 %return_rows.1 = f32[256,384]{1,0:T(8,128)} custom-call(f32[256,384]{1,0:T(8,128)S(1)} %get-tuple-element.85.gf_ref, bf16[256,256]{1,0:T(8,128)(2,1)S(1)} %get-tuple-element.86.chosen_ref, bf16[128,384]{1,0:T(8,128)(2,1)S(1)} %collective-permute-done.15.halo_ref, bf16[64,384]{1,0:T(8,128)(2,1)S(1)} %get-tuple-element.92.own_ref, ...), custom_call_target="tpu_custom_call" | custom-call | bytes 1310720 | tf_op jit(solution)/shard_map/return_rows/pallas_call | solution.py:481
  49.1 2.7 %collective-permute-done.13 = bf16[96,384]{1,0:T(8,128)(2,1)S(1)} collective-permute-done((bf16[96,384]{1,0:T(8,128)(2,1)S(1)}, bf16[96,384]{1,0:T(8,128)(2,1)S(1)}, u32[]{:S(2)}, u32[]{:S(2)}) %collective-permute-start.13) | collective-permute-done | bytes 73760 | tf_op jit(solution)/shard_map/ppermute | solution.py:81
  51.8 2.8 %collective-permute-start.19 = (bf16[192,384]{1,0:T(8,128)(2,1)S(1)}, bf16[192,384]{1,0:T(8,128)(2,1)S(1)}, u32[]{:S(2)}, u32[]{:S(2)}) collective-permute-start(bf16[192,384]{1,0:T(8,128)(2,1)S(1)} %pad_maximum_fusion.3.refs_0_), channel_id=1, source_target_pairs={{0,6},{1,7},{2,4},{3,5},{4,2},{5,3},{6,0},{7,1},{8,14},{9,15},{10,... | collective-permute-start | bytes 442376 | tf_op jit(solution)/shard_map/ppermute | solution.py:81
  54.6 0.3 collective-permute-start.18
  54.8 0.5 collective-permute-start.17
  55.3 2.5 %collective-permute-done.19.refs_3_ = bf16[192,384]{1,0:T(8,128)(2,1)S(1)} collective-permute-done((bf16[192,384]{1,0:T(8,128)(2,1)S(1)}, bf16[192,384]{1,0:T(8,128)(2,1)S(1)}, u32[]{:S(2)}, u32[]{:S(2)}) %collective-permute-start.19) | collective-permute-done | bytes 147488 | tf_op jit(solution)/shard_map/ppermute | solution.py:81
  57.9 1.8 %collective-permute-done.18.refs_2_ = bf16[192,384]{1,0:T(8,128)(2,1)S(1)} collective-permute-done((bf16[192,384]{1,0:T(8,128)(2,1)S(1)}, bf16[192,384]{1,0:T(8,128)(2,1)S(1)}, u32[]{:S(2)}, u32[]{:S(2)}) %collective-permute-start.18) | collective-permute-done | bytes 147488 | tf_op jit(solution)/shard_map/ppermute | solution.py:81
  59.7 0.3 collective-permute-done.17.refs_1_
  60.0 0.2 collective-permute-start.21
  60.2 0.6 convert_add_fusion.2
  60.8 0.3 collective-permute-done.22.refs_6_
  61.1 0.3 collective-permute-done.21.refs_5_
  61.3 1.6 %place_sums.1 = (f32[384,384]{1,0:T(8,128)}, f32[384,768]{1,0:T(8,128)}, f32[384,384]{1,0:T(8,128)}) custom-call(bf16[192,384]{1,0:T(8,128)(2,1)S(1)} %pad_maximum_fusion.3.refs_0_, bf16[192,384]{1,0:T(8,128)(2,1)S(1)} %collective-permute-done.17.refs_1_, bf16[192,384]{1,0:T(8,128)(2,1)S(1)} %collective-permute-done.18.refs_2_, ...), custom_call_target="tpu_custom_call" | custom-call | bytes 3538944 | tf_op jit(solution)/shard_map/place_sums/pallas_call | solution.py:481
  (31 shorter events, 0.3 us)
Async XLA Ops:
  1.9 5.9 %collective-permute-start = (bf16[128,384]{1,0:T(8,128)(2,1)S(1)}, bf16[128,384]{1,0:T(8,128)(2,1)S(1)}, u32[]{:S(2)}, u32[]{:S(2)}) collective-permute-start(bf16[128,384]{1,0:T(8,128)(2,1)S(1)} %get-tuple-element.57), channel_id=1, source_target_pairs={{0,4},{1,5},{2,6},{3,7},{4,0},{5,1},{6,2},{7,3},{8,12},{9,13},{10,... | collective-permute-start | bytes 294920 | tf_op jit(solution)/shard_map/ppermute | solution.py:81
  7.8 6.5 %collective-permute-start.1 = (bf16[64,384]{1,0:T(8,128)(2,1)S(1)}, bf16[64,384]{1,0:T(8,128)(2,1)S(1)}, u32[]{:S(2)}, u32[]{:S(2)}) collective-permute-start(bf16[64,384]{1,0:T(8,128)(2,1)S(1)} %pad_maximum_fusion.7), channel_id=1, source_target_pairs={{0,24},{1,25},{2,26},{3,27},{4,28},{5,29},{6,30},{7,31},{8,16},{9,... | collective-permute-start | bytes 147464 | tf_op jit(solution)/shard_map/ppermute | solution.py:81
  11.7 5.1 %collective-permute-start.2 = (bf16[64,384]{1,0:T(8,128)(2,1)S(1)}, bf16[64,384]{1,0:T(8,128)(2,1)S(1)}, u32[]{:S(2)}, u32[]{:S(2)}) collective-permute-start(bf16[64,384]{1,0:T(8,128)(2,1)S(1)} %pad_maximum_fusion.8), channel_id=1, source_target_pairs={{0,16},{1,17},{2,18},{3,19},{4,20},{5,21},{6,22},{7,23},{8,24},{9,... | collective-permute-start | bytes 147464 | tf_op jit(solution)/shard_map/ppermute | solution.py:81
  11.7 5.1 %collective-permute-start.4 = (bf16[128,384]{1,0:T(8,128)(2,1)S(1)}, bf16[128,384]{1,0:T(8,128)(2,1)S(1)}, u32[]{:S(2)}, u32[]{:S(2)}) collective-permute-start(bf16[128,384]{1,0:T(8,128)(2,1)S(1)} %get-tuple-element.63), channel_id=1, source_target_pairs={{3,0},{0,1},{1,2},{2,3},{7,4},{4,5},{5,6},{6,7},{11,8},{8,9},{9,10... | collective-permute-start | bytes 294920 | tf_op jit(solution)/shard_map/ppermute | solution.py:87
  11.8 5.0 %collective-permute-start.3 = (bf16[64,384]{1,0:T(8,128)(2,1)S(1)}, bf16[64,384]{1,0:T(8,128)(2,1)S(1)}, u32[]{:S(2)}, u32[]{:S(2)}) collective-permute-start(bf16[64,384]{1,0:T(8,128)(2,1)S(1)} %pad_maximum_fusion.9), channel_id=1, source_target_pairs={{0,8},{1,9},{2,10},{3,11},{4,12},{5,13},{6,14},{7,15},{8,0},{9,1},... | collective-permute-start | bytes 147464 | tf_op jit(solution)/shard_map/ppermute | solution.py:81
  22.8 2.1 %collective-permute-start.5 = (bf16[784,384]{1,0:T(8,128)(2,1)S(1)}, bf16[784,384]{1,0:T(8,128)(2,1)S(1)}, u32[]{:S(2)}, u32[]{:S(2)}) collective-permute-start(bf16[784,384]{1,0:T(8,128)(2,1)S(1)} %get-tuple-element.76), channel_id=1, source_target_pairs={{0,1},{1,0},{2,3},{3,2},{4,5},{5,4},{6,7},{7,6},{8,9},{9,8},{10,11... | collective-permute-start | bytes 1806344 | tf_op jit(solution)/shard_map/ppermute | solution.py:81
  25.2 7.8 %collective-permute-start.6 = (bf16[200,384]{1,0:T(8,128)(2,1)S(1)}, bf16[200,384]{1,0:T(8,128)(2,1)S(1)}, u32[]{:S(2)}, u32[]{:S(2)}) collective-permute-start(bf16[200,384]{1,0:T(8,128)(2,1)S(1)} %get-tuple-element.109), channel_id=1, source_target_pairs={{0,6},{1,7},{2,4},{3,5},{4,2},{5,3},{6,0},{7,1},{8,14},{9,15},{10,... | collective-permute-start | bytes 460808 | tf_op jit(solution)/shard_map/ppermute | solution.py:81
  27.6 7.9 %collective-permute-start.7 = (bf16[200,384]{1,0:T(8,128)(2,1)S(1)}, bf16[200,384]{1,0:T(8,128)(2,1)S(1)}, u32[]{:S(2)}, u32[]{:S(2)}) collective-permute-start(bf16[200,384]{1,0:T(8,128)(2,1)S(1)} %get-tuple-element.110), channel_id=1, source_target_pairs={{0,2},{1,3},{2,0},{3,1},{4,6},{5,7},{6,4},{7,5},{8,10},{9,11},{10,... | collective-permute-start | bytes 460808 | tf_op jit(solution)/shard_map/ppermute | solution.py:81
  28.2 7.2 %collective-permute-start.8 = (bf16[200,384]{1,0:T(8,128)(2,1)S(1)}, bf16[200,384]{1,0:T(8,128)(2,1)S(1)}, u32[]{:S(2)}, u32[]{:S(2)}) collective-permute-start(bf16[200,384]{1,0:T(8,128)(2,1)S(1)} %get-tuple-element.111), channel_id=1, source_target_pairs={{0,4},{1,5},{2,6},{3,7},{4,0},{5,1},{6,2},{7,3},{8,12},{9,13},{10,... | collective-permute-start | bytes 460808 | tf_op jit(solution)/shard_map/ppermute | solution.py:81
  28.7 6.8 %collective-permute-start.9 = (bf16[64,384]{1,0:T(8,128)(2,1)S(1)}, bf16[64,384]{1,0:T(8,128)(2,1)S(1)}, u32[]{:S(2)}, u32[]{:S(2)}) collective-permute-start(bf16[64,384]{1,0:T(8,128)(2,1)S(1)} %get-tuple-element.82), channel_id=1, source_target_pairs={{0,24},{1,25},{2,26},{3,27},{4,28},{5,29},{6,30},{7,31},{8,16},{9,... | collective-permute-start | bytes 147464 | tf_op jit(solution)/shard_map/ppermute | solution.py:81
  30.4 5.5 %collective-permute-start.10 = (bf16[64,384]{1,0:T(8,128)(2,1)S(1)}, bf16[64,384]{1,0:T(8,128)(2,1)S(1)}, u32[]{:S(2)}, u32[]{:S(2)}) collective-permute-start(bf16[64,384]{1,0:T(8,128)(2,1)S(1)} %get-tuple-element.83), channel_id=1, source_target_pairs={{0,16},{1,17},{2,18},{3,19},{4,20},{5,21},{6,22},{7,23},{8,24},{9,... | collective-permute-start | bytes 147464 | tf_op jit(solution)/shard_map/ppermute | solution.py:81
  36.0 4.5 %collective-permute-start.11 = (bf16[104,384]{1,0:T(8,128)(2,1)S(1)}, bf16[104,384]{1,0:T(8,128)(2,1)S(1)}, u32[]{:S(2)}, u32[]{:S(2)}) collective-permute-start(bf16[104,384]{1,0:T(8,128)(2,1)S(1)} %pad_maximum_fusion.5), channel_id=1, source_target_pairs={{0,8},{1,9},{2,10},{3,11},{4,12},{5,13},{6,14},{7,15},{8,0},{9,1},... | collective-permute-start | bytes 239624 | tf_op jit(solution)/shard_map/ppermute | solution.py:81
  36.5 4.5 %collective-permute-start.14 = (bf16[64,384]{1,0:T(8,128)(2,1)S(1)}, bf16[64,384]{1,0:T(8,128)(2,1)S(1)}, u32[]{:S(2)}, u32[]{:S(2)}) collective-permute-start(bf16[64,384]{1,0:T(8,128)(2,1)S(1)} %get-tuple-element.89), channel_id=1, source_target_pairs={{0,8},{1,9},{2,10},{3,11},{4,12},{5,13},{6,14},{7,15},{8,0},{9,1},... | collective-permute-start | bytes 147464 | tf_op jit(solution)/shard_map/ppermute | solution.py:81
  41.1 6.2 %collective-permute-start.12 = (bf16[104,384]{1,0:T(8,128)(2,1)S(1)}, bf16[104,384]{1,0:T(8,128)(2,1)S(1)}, u32[]{:S(2)}, u32[]{:S(2)}) collective-permute-start(bf16[104,384]{1,0:T(8,128)(2,1)S(1)} %pad_maximum_fusion.6), channel_id=1, source_target_pairs={{0,16},{1,17},{2,18},{3,19},{4,20},{5,21},{6,22},{7,23},{8,24},{9,... | collective-permute-start | bytes 239624 | tf_op jit(solution)/shard_map/ppermute | solution.py:81
  43.4 4.7 %collective-permute-start.16 = (bf16[128,384]{1,0:T(8,128)(2,1)S(1)}, bf16[128,384]{1,0:T(8,128)(2,1)S(1)}, u32[]{:S(2)}, u32[]{:S(2)}) collective-permute-start(bf16[128,384]{1,0:T(8,128)(2,1)S(1)} %pad_maximum_fusion.4), channel_id=1, source_target_pairs={{0,4},{1,5},{2,6},{3,7},{4,0},{5,1},{6,2},{7,3},{8,12},{9,13},{10,... | collective-permute-start | bytes 294920 | tf_op jit(solution)/shard_map/ppermute | solution.py:81
  44.9 3.1 %collective-permute-start.15 = (bf16[128,384]{1,0:T(8,128)(2,1)S(1)}, bf16[128,384]{1,0:T(8,128)(2,1)S(1)}, u32[]{:S(2)}, u32[]{:S(2)}) collective-permute-start(bf16[128,384]{1,0:T(8,128)(2,1)S(1)} %get-tuple-element.91), channel_id=1, source_target_pairs={{1,0},{2,1},{3,2},{0,3},{5,4},{6,5},{7,6},{4,7},{9,8},{10,9},{11,1... | collective-permute-start | bytes 294920 | tf_op jit(solution)/shard_map/ppermute | solution.py:87
  47.3 4.4 %collective-permute-start.13 = (bf16[96,384]{1,0:T(8,128)(2,1)S(1)}, bf16[96,384]{1,0:T(8,128)(2,1)S(1)}, u32[]{:S(2)}, u32[]{:S(2)}) collective-permute-start(bf16[96,384]{1,0:T(8,128)(2,1)S(1)} %add_convert_fusion), channel_id=1, source_target_pairs={{0,8},{1,9},{2,10},{3,11},{4,12},{5,13},{6,14},{7,15},{8,0},{9,1},... | collective-permute-start | bytes 221192 | tf_op jit(solution)/shard_map/ppermute | solution.py:81
  51.8 6.1 %collective-permute-start.19 = (bf16[192,384]{1,0:T(8,128)(2,1)S(1)}, bf16[192,384]{1,0:T(8,128)(2,1)S(1)}, u32[]{:S(2)}, u32[]{:S(2)}) collective-permute-start(bf16[192,384]{1,0:T(8,128)(2,1)S(1)} %pad_maximum_fusion.3.refs_0_), channel_id=1, source_target_pairs={{0,6},{1,7},{2,4},{3,5},{4,2},{5,3},{6,0},{7,1},{8,14},{9,15},{10,... | collective-permute-start | bytes 442376 | tf_op jit(solution)/shard_map/ppermute | solution.py:81
  54.6 5.1 %collective-permute-start.18 = (bf16[192,384]{1,0:T(8,128)(2,1)S(1)}, bf16[192,384]{1,0:T(8,128)(2,1)S(1)}, u32[]{:S(2)}, u32[]{:S(2)}) collective-permute-start(bf16[192,384]{1,0:T(8,128)(2,1)S(1)} %pad_maximum_fusion.3.refs_0_), channel_id=1, source_target_pairs={{0,2},{1,3},{2,0},{3,1},{4,6},{5,7},{6,4},{7,5},{8,10},{9,11},{10,... | collective-permute-start | bytes 442376 | tf_op jit(solution)/shard_map/ppermute | solution.py:81
  54.8 5.1 %collective-permute-start.17 = (bf16[192,384]{1,0:T(8,128)(2,1)S(1)}, bf16[192,384]{1,0:T(8,128)(2,1)S(1)}, u32[]{:S(2)}, u32[]{:S(2)}) collective-permute-start(bf16[192,384]{1,0:T(8,128)(2,1)S(1)} %pad_maximum_fusion.3.refs_0_), channel_id=1, source_target_pairs={{0,4},{1,5},{2,6},{3,7},{4,0},{5,1},{6,2},{7,3},{8,12},{9,13},{10,... | collective-permute-start | bytes 442376 | tf_op jit(solution)/shard_map/ppermute | solution.py:81
  55.3 5.5 %collective-permute-start.20 = (bf16[192,384]{1,0:T(8,128)(2,1)S(1)}, bf16[192,384]{1,0:T(8,128)(2,1)S(1)}, u32[]{:S(2)}, u32[]{:S(2)}) collective-permute-start(bf16[192,384]{1,0:T(8,128)(2,1)S(1)} %pad_maximum_fusion.3.refs_0_), channel_id=1, source_target_pairs={{0,1},{1,0},{2,3},{3,2},{4,5},{5,4},{6,7},{7,6},{8,9},{9,8},{10,11... | collective-permute-start | bytes 442376 | tf_op jit(solution)/shard_map/ppermute | solution.py:81
  57.9 2.9 %collective-permute-start.23 = (bf16[192,384]{1,0:T(8,128)(2,1)S(1)}, bf16[192,384]{1,0:T(8,128)(2,1)S(1)}, u32[]{:S(2)}, u32[]{:S(2)}) collective-permute-start(bf16[192,384]{1,0:T(8,128)(2,1)S(1)} %collective-permute-done.19.refs_3_), channel_id=1, source_target_pairs={{0,1},{1,0},{2,3},{3,2},{4,5},{5,4},{6,7},{7,6},{8,9},{9,8},{10,11... | collective-permute-start | bytes 442376 | tf_op jit(solution)/shard_map/ppermute | solution.py:81
  59.7 1.4 %collective-permute-start.22 = (bf16[192,384]{1,0:T(8,128)(2,1)S(1)}, bf16[192,384]{1,0:T(8,128)(2,1)S(1)}, u32[]{:S(2)}, u32[]{:S(2)}) collective-permute-start(bf16[192,384]{1,0:T(8,128)(2,1)S(1)} %collective-permute-done.18.refs_2_), channel_id=1, source_target_pairs={{0,1},{1,0},{2,3},{3,2},{4,5},{5,4},{6,7},{7,6},{8,9},{9,8},{10,11... | collective-permute-start | bytes 442376 | tf_op jit(solution)/shard_map/ppermute | solution.py:81
  60.0 1.4 %collective-permute-start.21 = (bf16[192,384]{1,0:T(8,128)(2,1)S(1)}, bf16[192,384]{1,0:T(8,128)(2,1)S(1)}, u32[]{:S(2)}, u32[]{:S(2)}) collective-permute-start(bf16[192,384]{1,0:T(8,128)(2,1)S(1)} %collective-permute-done.17.refs_1_), channel_id=1, source_target_pairs={{0,1},{1,0},{2,3},{3,2},{4,5},{5,4},{6,7},{7,6},{8,9},{9,8},{10,11... | collective-permute-start | bytes 442376 | tf_op jit(solution)/shard_map/ppermute | solution.py:81

commit v20 on v15

--- a/solution.py
+++ b/solution.py
@@ -180,6 +180,8 @@
     featt_ref,
     qt_ref,
     odt_ref,
+    q_ref,
+    od_ref,
     kv_ref,
     kvt_ref,
     local_bias_ref,
@@ -248,6 +250,8 @@
     og_copy.wait()
     wo_copy.wait()
     odt_ref[...] = rounded(times_transposed(wo_ref[...], og_ref[...]))
+    q_ref[...] = qt_ref[...].T
+    od_ref[...] = odt_ref[...].T
 
 
 def attend_kernel(
@@ -258,9 +262,9 @@
 ):
     count = dom_size // 2 + 1
     piece_refs, halo_ref, refs = refs[:count], refs[count], refs[count + 1 :]
-    og_ref, wq_ref, wkv_ref, featt_ref, qt_ref, odt_ref, own_kv_ref, own_kvt_ref = refs[:8]
-    local_bias_ref, far_bias_ref, send_ref, rider_ref = refs[8:12]
-    extt_ref, gqt_ref, gkvt_ref, ot_ref, slot_ref, kv_ref, kvt_ref = refs[12:]
+    og_ref, wq_ref, wkv_ref, featt_ref, qt_ref, odt_ref, q_ref, od_ref = refs[:8]
+    own_kv_ref, own_kvt_ref, local_bias_ref, far_bias_ref, send_ref, rider_ref = refs[8:14]
+    extt_ref, gqt_ref, gkv_ref, ot_ref, slot_ref, kv_ref, kvt_ref, sum_ref = refs[14:]
     width, row_count = qt_ref.shape
     tile = halo_ref.shape[0]
     tile_count = row_count // tile
@@ -325,7 +329,7 @@
         return rounded(p_local), rounded(p_far), ds_local, ds_far
 
     def outputs(head, pb_local, pb_far, ds_local, ds_far):
-        low, high, _, _ = bounds(head)
+        low, high, first, last = bounds(head)
 
         def to_queries(start, local, beyond):
             rows = slice(start + low, start + high)
@@ -334,25 +338,22 @@
             )
             return near_part + f32_dot(kvt_ref[rows, near:], beyond)
 
-        def to_keys(start, operand, local, beyond, factor):
-            rows = slice(start + low, start + high)
-            parts = []
-            carried = None
+        def to_keys(start, rows_ref, local, beyond):
+            column = lax.broadcasted_iota(jnp.int32, (row_count, last - first), 1) + first
+            of_head = (column >= low) & (column < high)
+            operand = jnp.where(of_head, rows_ref[:, first:last], 0)
+            columns = slice(start + first, start + last)
             for t in range(tile_count):
                 lanes = slice(t * tile, (t + 1) * tile)
-                window = times_transposed(operand[:, lanes], local[:, lanes])
-                previous = window[:, :tile]
-                parts.append(previous if carried is None else previous + carried)
-                carried = window[:, tile:]
-            parts.append(carried)
-            parts.append(times_transposed(operand, beyond))
-            gathered = jnp.concatenate(parts, axis=1)
-            gkvt_ref[rows] = rounded(gathered if factor is None else gathered * factor)
+                sum_ref[t * tile : (t + 2) * tile, columns] += f32_dot(local[:, lanes], operand[lanes])
+            sum_ref[near:, columns] += f32_dot(beyond, operand)
 
         ot_ref[low:high] = rounded(to_queries(width, pb_local, pb_far))
         gqt_ref[low:high] = rounded(to_queries(0, ds_local, ds_far) * scale)
-        to_keys(0, qt_ref[low:high], ds_local, ds_far, scale)
-        to_keys(width, odt_ref[low:high], pb_local, pb_far, None)
+        to_keys(0, q_ref, ds_local, ds_far)
+        to_keys(width, od_ref, pb_local, pb_far)
+
+    sum_ref[...] = jnp.zeros_like(sum_ref)
 
     coming = products(0)
     done = None
@@ -365,14 +366,16 @@
         done = weights(*now)
     outputs(HEADS - 1, *done)
 
-    rider_ref[...] = f32_dot(wkv_ref[...], gkvt_ref[:, virt_at:]).T * factor
+    gkv_ref[:, :width] = rounded(sum_ref[:, :width] * scale)
+    gkv_ref[:, width:] = rounded(sum_ref[:, width:])
+    rider_ref[...] = times_transposed(gkv_ref[virt_at:], wkv_ref[...]) * factor
     weight_sums(
-        1 - lax.axis_index("rows") % 2, send_ref, extt_ref, gqt_ref, gkvt_ref, ot_ref, og_ref, factor
+        1 - lax.axis_index("rows") % 2, send_ref, extt_ref, gqt_ref, gkv_ref, ot_ref, og_ref, factor
     )
     send_ref[2 * width :] = rounded(rider_ref[...])
 
 
-def weight_sums(core, out_ref, extt_ref, gqt_ref, gkvt_ref, ot_ref, og_ref, factor):
+def weight_sums(core, out_ref, extt_ref, gqt_ref, gkv_ref, ot_ref, og_ref, factor):
     width, row_count = gqt_ref.shape
     held = own_digit()
     pair, square, _ = exchange_plan()
@@ -389,15 +392,15 @@
     def _():
         own = slice(TILE, TILE + row_count)
         write(0, times_transposed(extt_ref[:, own], gqt_ref[...]))
-        write(1, times_transposed(extt_ref[...], gkvt_ref[:width]))
+        write(1, f32_dot(extt_ref[...], gkv_ref[:, :width]))
 
     @pl.when(core == 1)
     def _():
-        write(0, times_transposed(extt_ref[...], gkvt_ref[width:]))
+        write(0, f32_dot(extt_ref[...], gkv_ref[:, width:]))
         write(1, f32_dot(ot_ref[...], og_ref[...]))
 
 
-def finish_kernel(factor, og_ref, wq_ref, wkv_ref, extt_ref, gqt_ref, gkvt_ref, ot_ref, *refs):
+def finish_kernel(factor, og_ref, wq_ref, wkv_ref, extt_ref, gqt_ref, gkv_ref, ot_ref, *refs):
     gf_ref, halo_feat_ref, keep_ref = refs[:3]
     pair_refs = refs[3:]
     width, row_count = gqt_ref.shape
@@ -405,15 +408,13 @@
     step = pair_refs[0].shape[0]
     slots = step * len(pair_refs)
     weight_sums(
-        lax.axis_index("rows") % 2, keep_ref, extt_ref, gqt_ref, gkvt_ref, ot_ref, og_ref, factor
-    )
-    by_feature = f32_dot(wkv_ref[...], gkvt_ref[:, : near + slots])
-    own = by_feature[:, TILE:near] + f32_dot(wq_ref[...], gqt_ref[...])
-    gf_ref[...] = own.T
-    halo_feat_ref[...] = rounded(by_feature[:, :TILE].T)
-    slot_feat = rounded(by_feature[:, near:].T)
+        lax.axis_index("rows") % 2, keep_ref, extt_ref, gqt_ref, gkv_ref, ot_ref, og_ref, factor
+    )
+    rows = times_transposed(gkv_ref[: near + slots], wkv_ref[...])
+    gf_ref[...] = rows[TILE:near] + times_transposed(gqt_ref[...].T, wq_ref[...])
+    halo_feat_ref[...] = rounded(rows[:TILE])
     for at, out_ref in enumerate(pair_refs):
-        out_ref[...] = slot_feat[at * step : (at + 1) * step]
+        out_ref[...] = rounded(rows[near + at * step : near + (at + 1) * step])
 
 
 def place_kernel(*refs):
@@ -515,6 +516,8 @@
             shape((width, row_count + padded), bf16),
             shape((width, row_count), bf16),
             shape((width, row_count), bf16),
+            shape((row_count, width), bf16),
+            shape((row_count, width), bf16),
             shape((row_count + padded, 2 * width), bf16),
             shape((2 * width, row_count + padded), bf16),
             shape((2 * TILE, row_count), f32),
@@ -542,7 +545,7 @@
             shape((padded, width), f32),
             shape((width, ext_rows), bf16),
             shape((width, row_count), bf16),
-            shape((2 * width, ext_rows), bf16),
+            shape((ext_rows, 2 * width), bf16),
             shape((width, row_count), bf16),
         ],
         [*arrived, halo, *prepared],
@@ -550,6 +553,7 @@
             pltpu.VMEM((slots, width), bf16),
             pltpu.VMEM((ext_rows, 2 * width), bf16),
             pltpu.VMEM((2 * width, ext_rows), bf16),
+            pltpu.VMEM((ext_rows, 2 * width), f32),
         ],
         flops=28 * ext_rows * width * width,
     )

time: 63.2 us -> 63.3 us (level)
  transfers between devices with their start and end apart: 24 -> 24, of which waited for: 16 -> 16; matrix products, arithmetic and copies ran while one was open for 1% -> 1% of each run, Pallas kernels for 9% -> 8%
where the time goes in v20:
time: 63.3 us; the launch traced here: 63 us
  starting transfers between devices  23.5 us (37%)
  waiting for transfers between devices  23.4 us (37%)
  Pallas kernels  14.2 us (22%)
  other arithmetic  1 us (2%)
  between operations  0.83 us (1%)
    ppermute x22, waiting for transfers between devices, swapped(): return lax.ppermute(block, ('dom', 'rows'), route)  23.4 us
    ppermute x22, starting transfers between devices, swapped(): return lax.ppermute(block, ('dom', 'rows'), route)  23.4 us
    pallas_call x6, Pallas kernels, call(): pl.pallas_call(kernel, out_shape=outs, in_specs=[pl.BlockSpec(memory_spac...  14.2 us
  transfers between devices with their start and end apart: 24, of which 16 were waited for; matrix products, arithmetic and copies ran while one was open for 1% of the time, Pallas kernels for 8%

profile of v20, /device:TPU:0, one launch (start us, length us, event | category | flops | bytes accessed | tf_op | source)
XLA Modules:
  0.0 63.0 jit_solution(6761921927820943357)
XLA Ops:
  0.6 1.2 %pick_rows.1 = (bf16[128,384]{1,0:T(8,128)(2,1)S(1)}, bf16[256,256]{1,0:T(8,128)(2,1)S(1)}, bf16[128,384]{1,0:T(8,128)(2,1)S(1)}, bf16[32,384]{1,0:T(8,128)(2,1)...) custom-call(bf16[256,384]{1,0:T(8,128)(2,1)} %feat_hbm.3, ...), custom_call_target="tpu_custom_call" | custom-call | bytes 623616 | tf_op jit(solution)/shard_map/pick_rows/pallas_call | solution.py:474
  1.9 3.0 %collective-permute-start = (bf16[128,384]{1,0:T(8,128)(2,1)S(1)}, bf16[128,384]{1,0:T(8,128)(2,1)S(1)}, u32[]{:S(2)}, u32[]{:S(2)}) collective-permute-start(bf16[128,384]{1,0:T(8,128)(2,1)S(1)} %get-tuple-element.59), channel_id=1, source_target_pairs={{0,4},{1,5},{2,6},{3,7},{4,0},{5,1},{6,2},{7,3},{8,12},{9,13},{10,... | collective-permute-start | bytes 294920 | tf_op jit(solution)/shard_map/ppermute | solution.py:81
  4.9 2.9 %prepare.1 = (bf16[256,384]{1,0:T(8,128)(2,1)S(1)}, bf16[384,384]{1,0:T(8,128)(2,1)S(1)}, bf16[384,768]{1,0:T(8,128)(2,1)S(1)}, bf16[384,272]{1,0:T(8,128)(2,1)S...) custom-call(bf16[256,384]{1,0:T(8,128)(2,1)} %feat_hbm.3, ...), custom_call_target="tpu_custom_call" | custom-call | flops 377487360 | bytes 5049344 | tf_op jit(solution)/shard_map/prepare/pallas_call | solution.py:474
  7.8 0.0 collective-permute-done.refs_1_
  7.9 3.8 %collective-permute-start.1 = (bf16[64,384]{1,0:T(8,128)(2,1)S(1)}, bf16[64,384]{1,0:T(8,128)(2,1)S(1)}, u32[]{:S(2)}, u32[]{:S(2)}) collective-permute-start(bf16[64,384]{1,0:T(8,128)(2,1)S(1)} %pad_maximum_fusion.7), channel_id=1, source_target_pairs={{0,24},{1,25},{2,26},{3,27},{4,28},{5,29},{6,30},{7,31},{8,16},{9,... | collective-permute-start | bytes 147464 | tf_op jit(solution)/shard_map/ppermute | solution.py:81
  11.7 0.0 collective-permute-start.2
  11.7 0.1 collective-permute-start.4
  11.8 0.6 %collective-permute-start.3 = (bf16[64,384]{1,0:T(8,128)(2,1)S(1)}, bf16[64,384]{1,0:T(8,128)(2,1)S(1)}, u32[]{:S(2)}, u32[]{:S(2)}) collective-permute-start(bf16[64,384]{1,0:T(8,128)(2,1)S(1)} %pad_maximum_fusion.9), channel_id=1, source_target_pairs={{0,8},{1,9},{2,10},{3,11},{4,12},{5,13},{6,14},{7,15},{8,0},{9,1},... | collective-permute-start | bytes 147464 | tf_op jit(solution)/shard_map/ppermute | solution.py:81
  12.4 1.9 %collective-permute-done.1.refs_2_ = bf16[64,384]{1,0:T(8,128)(2,1)S(1)} collective-permute-done((bf16[64,384]{1,0:T(8,128)(2,1)S(1)}, bf16[64,384]{1,0:T(8,128)(2,1)S(1)}, u32[]{:S(2)}, u32[]{:S(2)}) %collective-permute-start.1) | collective-permute-done | bytes 49184 | tf_op jit(solution)/shard_map/ppermute | solution.py:81
  14.3 2.5 %collective-permute-done.2.refs_3_ = bf16[64,384]{1,0:T(8,128)(2,1)S(1)} collective-permute-done((bf16[64,384]{1,0:T(8,128)(2,1)S(1)}, bf16[64,384]{1,0:T(8,128)(2,1)S(1)}, u32[]{:S(2)}, u32[]{:S(2)}) %collective-permute-start.2) | collective-permute-done | bytes 49184 | tf_op jit(solution)/shard_map/ppermute | solution.py:81
  16.8 6.0 %attend.1 = (bf16[784,384]{1,0:T(8,128)(2,1)S(1)}, f32[16,384]{1,0:T(8,128)S(1)}, bf16[384,656]{1,0:T(8,128)(2,1)S(1)}, bf16[384,256]{1,0:T(8,128)(2,1)S(1)}, bf...) custom-call(bf16[32,384]{1,0:T(8,128)(2,1)S(1)} %get-tuple-element.58.refs_0_, ...), custom_call_target="tpu_custom_call" | custom-call | flops 2708471808 | bytes 6352896 | tf_op jit(solution)/shard_map/attend/pallas_call | solution.py:474
  22.8 0.1 collective-permute-start.5
  22.9 1.4 %finish.1 = (f32[256,384]{1,0:T(8,128)S(1)}, bf16[128,384]{1,0:T(8,128)(2,1)S(1)}, f32[768,384]{1,0:T(8,128)S(1)}, bf16[64,384]{1,0:T(8,128)(2,1)S(1)}, bf16[64,...) custom-call(bf16[256,384]{1,0:T(8,128)(2,1)S(1)} %get-tuple-element.55.refs_6_.og_ref, ...), custom_call_target="tpu_custom_call" | custom-call | flops 580386816 | bytes 4853760 | tf_op jit(solution)/shard_map/finish/pallas_call | solution.py:474
  24.3 0.6 collective-permute-done.5
  24.9 0.1 fusion.2
  25.1 0.1 pad_maximum_fusion.2
  25.2 2.4 %collective-permute-start.6 = (bf16[200,384]{1,0:T(8,128)(2,1)S(1)}, bf16[200,384]{1,0:T(8,128)(2,1)S(1)}, u32[]{:S(2)}, u32[]{:S(2)}) collective-permute-start(bf16[200,384]{1,0:T(8,128)(2,1)S(1)} %get-tuple-element.113), channel_id=1, source_target_pairs={{0,6},{1,7},{2,4},{3,5},{4,2},{5,3},{6,0},{7,1},{8,14},{9,15},{10,... | collective-permute-start | bytes 460808 | tf_op jit(solution)/shard_map/ppermute | solution.py:81
  27.6 0.6 collective-permute-start.7
  28.2 0.5 collective-permute-start.8
  28.7 1.7 %collective-permute-start.9 = (bf16[64,384]{1,0:T(8,128)(2,1)S(1)}, bf16[64,384]{1,0:T(8,128)(2,1)S(1)}, u32[]{:S(2)}, u32[]{:S(2)}) collective-permute-start(bf16[64,384]{1,0:T(8,128)(2,1)S(1)} %get-tuple-element.86), channel_id=1, source_target_pairs={{0,24},{1,25},{2,26},{3,27},{4,28},{5,29},{6,30},{7,31},{8,16},{9,... | collective-permute-start | bytes 147464 | tf_op jit(solution)/shard_map/ppermute | solution.py:81
  30.4 0.3 collective-permute-start.10
  30.7 2.2 %collective-permute-done.6 = bf16[200,384]{1,0:T(8,128)(2,1)S(1)} collective-permute-done((bf16[200,384]{1,0:T(8,128)(2,1)S(1)}, bf16[200,384]{1,0:T(8,128)(2,1)S(1)}, u32[]{:S(2)}, u32[]{:S(2)}) %collective-permute-start.6) | collective-permute-done | bytes 153632 | tf_op jit(solution)/shard_map/ppermute | solution.py:81
  32.9 2.5 %collective-permute-done.7 = bf16[200,384]{1,0:T(8,128)(2,1)S(1)} collective-permute-done((bf16[200,384]{1,0:T(8,128)(2,1)S(1)}, bf16[200,384]{1,0:T(8,128)(2,1)S(1)}, u32[]{:S(2)}, u32[]{:S(2)}) %collective-permute-start.7) | collective-permute-done | bytes 153632 | tf_op jit(solution)/shard_map/ppermute | solution.py:81
  35.4 0.0 collective-permute-done.8
  35.4 0.1 fusion.1
  35.5 0.4 collective-permute-done.10.refs_1_
  36.0 0.5 collective-permute-start.11
  36.5 1.6 %collective-permute-start.14 = (bf16[64,384]{1,0:T(8,128)(2,1)S(1)}, bf16[64,384]{1,0:T(8,128)(2,1)S(1)}, u32[]{:S(2)}, u32[]{:S(2)}) collective-permute-start(bf16[64,384]{1,0:T(8,128)(2,1)S(1)} %get-tuple-element.93), channel_id=1, source_target_pairs={{0,8},{1,9},{2,10},{3,11},{4,12},{5,13},{6,14},{7,15},{8,0},{9,1},... | collective-permute-start | bytes 147464 | tf_op jit(solution)/shard_map/ppermute | solution.py:81
  38.1 2.4 %collective-permute-done.11 = bf16[104,384]{1,0:T(8,128)(2,1)S(1)} collective-permute-done((bf16[104,384]{1,0:T(8,128)(2,1)S(1)}, bf16[104,384]{1,0:T(8,128)(2,1)S(1)}, u32[]{:S(2)}, u32[]{:S(2)}) %collective-permute-start.11) | collective-permute-done | bytes 79904 | tf_op jit(solution)/shard_map/ppermute | solution.py:81
  40.5 0.5 collective-permute-done.14.refs_2_
  41.1 2.3 %collective-permute-start.12 = (bf16[104,384]{1,0:T(8,128)(2,1)S(1)}, bf16[104,384]{1,0:T(8,128)(2,1)S(1)}, u32[]{:S(2)}, u32[]{:S(2)}) collective-permute-start(bf16[104,384]{1,0:T(8,128)(2,1)S(1)} %pad_maximum_fusion.6), channel_id=1, source_target_pairs={{0,16},{1,17},{2,18},{3,19},{4,20},{5,21},{6,22},{7,23},{8,24},{9,... | collective-permute-start | bytes 239624 | tf_op jit(solution)/shard_map/ppermute | solution.py:81
  43.4 1.6 %collective-permute-start.16 = (bf16[128,384]{1,0:T(8,128)(2,1)S(1)}, bf16[128,384]{1,0:T(8,128)(2,1)S(1)}, u32[]{:S(2)}, u32[]{:S(2)}) collective-permute-start(bf16[128,384]{1,0:T(8,128)(2,1)S(1)} %pad_maximum_fusion.4), channel_id=1, source_target_pairs={{0,4},{1,5},{2,6},{3,7},{4,0},{5,1},{6,2},{7,3},{8,12},{9,13},{10,... | collective-permute-start | bytes 294920 | tf_op jit(solution)/shard_map/ppermute | solution.py:81
  45.0 2.4 %collective-permute-done.12 = bf16[104,384]{1,0:T(8,128)(2,1)S(1)} collective-permute-done((bf16[104,384]{1,0:T(8,128)(2,1)S(1)}, bf16[104,384]{1,0:T(8,128)(2,1)S(1)}, u32[]{:S(2)}, u32[]{:S(2)}) %collective-permute-start.12) | collective-permute-done | bytes 79904 | tf_op jit(solution)/shard_map/ppermute | solution.py:81
  47.3 0.5 collective-permute-start.13
  47.8 0.3 collective-permute-done.16.through_ref
  48.1 1.0 %return_rows.1 = f32[256,384]{1,0:T(8,128)} custom-call(f32[256,384]{1,0:T(8,128)S(1)} %get-tuple-element.89.gf_ref, bf16[256,256]{1,0:T(8,128)(2,1)S(1)} %get-tuple-element.90.chosen_ref, bf16[128,384]{1,0:T(8,128)(2,1)S(1)} %collective-permute-done.15.halo_ref, bf16[64,384]{1,0:T(8,128)(2,1)S(1)} %get-tuple-element.96.own_ref, ...), custom_call_target="tpu_custom_call" | custom-call | bytes 1310720 | tf_op jit(solution)/shard_map/return_rows/pallas_call | solution.py:474
  49.1 2.7 %collective-permute-done.13 = bf16[96,384]{1,0:T(8,128)(2,1)S(1)} collective-permute-done((bf16[96,384]{1,0:T(8,128)(2,1)S(1)}, bf16[96,384]{1,0:T(8,128)(2,1)S(1)}, u32[]{:S(2)}, u32[]{:S(2)}) %collective-permute-start.13) | collective-permute-done | bytes 73760 | tf_op jit(solution)/shard_map/ppermute | solution.py:81
  51.8 2.8 %collective-permute-start.19 = (bf16[192,384]{1,0:T(8,128)(2,1)S(1)}, bf16[192,384]{1,0:T(8,128)(2,1)S(1)}, u32[]{:S(2)}, u32[]{:S(2)}) collective-permute-start(bf16[192,384]{1,0:T(8,128)(2,1)S(1)} %pad_maximum_fusion.3.refs_0_), channel_id=1, source_target_pairs={{0,6},{1,7},{2,4},{3,5},{4,2},{5,3},{6,0},{7,1},{8,14},{9,15},{10,... | collective-permute-start | bytes 442376 | tf_op jit(solution)/shard_map/ppermute | solution.py:81
  54.6 0.3 collective-permute-start.18
  54.8 0.5 collective-permute-start.17
  55.3 2.5 %collective-permute-done.19.refs_3_ = bf16[192,384]{1,0:T(8,128)(2,1)S(1)} collective-permute-done((bf16[192,384]{1,0:T(8,128)(2,1)S(1)}, bf16[192,384]{1,0:T(8,128)(2,1)S(1)}, u32[]{:S(2)}, u32[]{:S(2)}) %collective-permute-start.19) | collective-permute-done | bytes 147488 | tf_op jit(solution)/shard_map/ppermute | solution.py:81
  57.9 1.8 %collective-permute-done.18.refs_2_ = bf16[192,384]{1,0:T(8,128)(2,1)S(1)} collective-permute-done((bf16[192,384]{1,0:T(8,128)(2,1)S(1)}, bf16[192,384]{1,0:T(8,128)(2,1)S(1)}, u32[]{:S(2)}, u32[]{:S(2)}) %collective-permute-start.18) | collective-permute-done | bytes 147488 | tf_op jit(solution)/shard_map/ppermute | solution.py:81
  59.7 0.3 collective-permute-done.17.refs_1_
  60.0 0.3 collective-permute-start.21
  60.2 0.6 convert_add_fusion.2
  60.8 0.3 collective-permute-done.22.refs_6_
  61.1 0.3 collective-permute-done.21.refs_5_
  61.3 1.6 %place_sums.1 = (f32[384,384]{1,0:T(8,128)}, f32[384,768]{1,0:T(8,128)}, f32[384,384]{1,0:T(8,128)}) custom-call(bf16[192,384]{1,0:T(8,128)(2,1)S(1)} %pad_maximum_fusion.3.refs_0_, bf16[192,384]{1,0:T(8,128)(2,1)S(1)} %collective-permute-done.17.refs_1_, bf16[192,384]{1,0:T(8,128)(2,1)S(1)} %collective-permute-done.18.refs_2_, ...), custom_call_target="tpu_custom_call" | custom-call | bytes 3538944 | tf_op jit(solution)/shard_map/place_sums/pallas_call | solution.py:474
  (31 shorter events, 0.2 us)
Async XLA Ops:
  1.9 6.0 %collective-permute-start = (bf16[128,384]{1,0:T(8,128)(2,1)S(1)}, bf16[128,384]{1,0:T(8,128)(2,1)S(1)}, u32[]{:S(2)}, u32[]{:S(2)}) collective-permute-start(bf16[128,384]{1,0:T(8,128)(2,1)S(1)} %get-tuple-element.59), channel_id=1, source_target_pairs={{0,4},{1,5},{2,6},{3,7},{4,0},{5,1},{6,2},{7,3},{8,12},{9,13},{10,... | collective-permute-start | bytes 294920 | tf_op jit(solution)/shard_map/ppermute | solution.py:81
  7.9 6.5 %collective-permute-start.1 = (bf16[64,384]{1,0:T(8,128)(2,1)S(1)}, bf16[64,384]{1,0:T(8,128)(2,1)S(1)}, u32[]{:S(2)}, u32[]{:S(2)}) collective-permute-start(bf16[64,384]{1,0:T(8,128)(2,1)S(1)} %pad_maximum_fusion.7), channel_id=1, source_target_pairs={{0,24},{1,25},{2,26},{3,27},{4,28},{5,29},{6,30},{7,31},{8,16},{9,... | collective-permute-start | bytes 147464 | tf_op jit(solution)/shard_map/ppermute | solution.py:81
  11.7 5.1 %collective-permute-start.2 = (bf16[64,384]{1,0:T(8,128)(2,1)S(1)}, bf16[64,384]{1,0:T(8,128)(2,1)S(1)}, u32[]{:S(2)}, u32[]{:S(2)}) collective-permute-start(bf16[64,384]{1,0:T(8,128)(2,1)S(1)} %pad_maximum_fusion.8), channel_id=1, source_target_pairs={{0,16},{1,17},{2,18},{3,19},{4,20},{5,21},{6,22},{7,23},{8,24},{9,... | collective-permute-start | bytes 147464 | tf_op jit(solution)/shard_map/ppermute | solution.py:81
  11.7 5.1 %collective-permute-start.4 = (bf16[128,384]{1,0:T(8,128)(2,1)S(1)}, bf16[128,384]{1,0:T(8,128)(2,1)S(1)}, u32[]{:S(2)}, u32[]{:S(2)}) collective-permute-start(bf16[128,384]{1,0:T(8,128)(2,1)S(1)} %get-tuple-element.65), channel_id=1, source_target_pairs={{3,0},{0,1},{1,2},{2,3},{7,4},{4,5},{5,6},{6,7},{11,8},{8,9},{9,10... | collective-permute-start | bytes 294920 | tf_op jit(solution)/shard_map/ppermute | solution.py:87
  11.8 5.0 %collective-permute-start.3 = (bf16[64,384]{1,0:T(8,128)(2,1)S(1)}, bf16[64,384]{1,0:T(8,128)(2,1)S(1)}, u32[]{:S(2)}, u32[]{:S(2)}) collective-permute-start(bf16[64,384]{1,0:T(8,128)(2,1)S(1)} %pad_maximum_fusion.9), channel_id=1, source_target_pairs={{0,8},{1,9},{2,10},{3,11},{4,12},{5,13},{6,14},{7,15},{8,0},{9,1},... | collective-permute-start | bytes 147464 | tf_op jit(solution)/shard_map/ppermute | solution.py:81
  22.8 2.1 %collective-permute-start.5 = (bf16[784,384]{1,0:T(8,128)(2,1)S(1)}, bf16[784,384]{1,0:T(8,128)(2,1)S(1)}, u32[]{:S(2)}, u32[]{:S(2)}) collective-permute-start(bf16[784,384]{1,0:T(8,128)(2,1)S(1)} %get-tuple-element.80), channel_id=1, source_target_pairs={{0,1},{1,0},{2,3},{3,2},{4,5},{5,4},{6,7},{7,6},{8,9},{9,8},{10,11... | collective-permute-start | bytes 1806344 | tf_op jit(solution)/shard_map/ppermute | solution.py:81
  25.2 7.8 %collective-permute-start.6 = (bf16[200,384]{1,0:T(8,128)(2,1)S(1)}, bf16[200,384]{1,0:T(8,128)(2,1)S(1)}, u32[]{:S(2)}, u32[]{:S(2)}) collective-permute-start(bf16[200,384]{1,0:T(8,128)(2,1)S(1)} %get-tuple-element.113), channel_id=1, source_target_pairs={{0,6},{1,7},{2,4},{3,5},{4,2},{5,3},{6,0},{7,1},{8,14},{9,15},{10,... | collective-permute-start | bytes 460808 | tf_op jit(solution)/shard_map/ppermute | solution.py:81
  27.6 7.9 %collective-permute-start.7 = (bf16[200,384]{1,0:T(8,128)(2,1)S(1)}, bf16[200,384]{1,0:T(8,128)(2,1)S(1)}, u32[]{:S(2)}, u32[]{:S(2)}) collective-permute-start(bf16[200,384]{1,0:T(8,128)(2,1)S(1)} %get-tuple-element.114), channel_id=1, source_target_pairs={{0,2},{1,3},{2,0},{3,1},{4,6},{5,7},{6,4},{7,5},{8,10},{9,11},{10,... | collective-permute-start | bytes 460808 | tf_op jit(solution)/shard_map/ppermute | solution.py:81
  28.2 7.3 %collective-permute-start.8 = (bf16[200,384]{1,0:T(8,128)(2,1)S(1)}, bf16[200,384]{1,0:T(8,128)(2,1)S(1)}, u32[]{:S(2)}, u32[]{:S(2)}) collective-permute-start(bf16[200,384]{1,0:T(8,128)(2,1)S(1)} %get-tuple-element.115), channel_id=1, source_target_pairs={{0,4},{1,5},{2,6},{3,7},{4,0},{5,1},{6,2},{7,3},{8,12},{9,13},{10,... | collective-permute-start | bytes 460808 | tf_op jit(solution)/shard_map/ppermute | solution.py:81
  28.7 6.8 %collective-permute-start.9 = (bf16[64,384]{1,0:T(8,128)(2,1)S(1)}, bf16[64,384]{1,0:T(8,128)(2,1)S(1)}, u32[]{:S(2)}, u32[]{:S(2)}) collective-permute-start(bf16[64,384]{1,0:T(8,128)(2,1)S(1)} %get-tuple-element.86), channel_id=1, source_target_pairs={{0,24},{1,25},{2,26},{3,27},{4,28},{5,29},{6,30},{7,31},{8,16},{9,... | collective-permute-start | bytes 147464 | tf_op jit(solution)/shard_map/ppermute | solution.py:81
  30.4 5.5 %collective-permute-start.10 = (bf16[64,384]{1,0:T(8,128)(2,1)S(1)}, bf16[64,384]{1,0:T(8,128)(2,1)S(1)}, u32[]{:S(2)}, u32[]{:S(2)}) collective-permute-start(bf16[64,384]{1,0:T(8,128)(2,1)S(1)} %get-tuple-element.87), channel_id=1, source_target_pairs={{0,16},{1,17},{2,18},{3,19},{4,20},{5,21},{6,22},{7,23},{8,24},{9,... | collective-permute-start | bytes 147464 | tf_op jit(solution)/shard_map/ppermute | solution.py:81
  36.0 4.5 %collective-permute-start.11 = (bf16[104,384]{1,0:T(8,128)(2,1)S(1)}, bf16[104,384]{1,0:T(8,128)(2,1)S(1)}, u32[]{:S(2)}, u32[]{:S(2)}) collective-permute-start(bf16[104,384]{1,0:T(8,128)(2,1)S(1)} %pad_maximum_fusion.5), channel_id=1, source_target_pairs={{0,8},{1,9},{2,10},{3,11},{4,12},{5,13},{6,14},{7,15},{8,0},{9,1},... | collective-permute-start | bytes 239624 | tf_op jit(solution)/shard_map/ppermute | solution.py:81
  36.5 4.5 %collective-permute-start.14 = (bf16[64,384]{1,0:T(8,128)(2,1)S(1)}, bf16[64,384]{1,0:T(8,128)(2,1)S(1)}, u32[]{:S(2)}, u32[]{:S(2)}) collective-permute-start(bf16[64,384]{1,0:T(8,128)(2,1)S(1)} %get-tuple-element.93), channel_id=1, source_target_pairs={{0,8},{1,9},{2,10},{3,11},{4,12},{5,13},{6,14},{7,15},{8,0},{9,1},... | collective-permute-start | bytes 147464 | tf_op jit(solution)/shard_map/ppermute | solution.py:81
  41.1 6.2 %collective-permute-start.12 = (bf16[104,384]{1,0:T(8,128)(2,1)S(1)}, bf16[104,384]{1,0:T(8,128)(2,1)S(1)}, u32[]{:S(2)}, u32[]{:S(2)}) collective-permute-start(bf16[104,384]{1,0:T(8,128)(2,1)S(1)} %pad_maximum_fusion.6), channel_id=1, source_target_pairs={{0,16},{1,17},{2,18},{3,19},{4,20},{5,21},{6,22},{7,23},{8,24},{9,... | collective-permute-start | bytes 239624 | tf_op jit(solution)/shard_map/ppermute | solution.py:81
  43.4 4.7 %collective-permute-start.16 = (bf16[128,384]{1,0:T(8,128)(2,1)S(1)}, bf16[128,384]{1,0:T(8,128)(2,1)S(1)}, u32[]{:S(2)}, u32[]{:S(2)}) collective-permute-start(bf16[128,384]{1,0:T(8,128)(2,1)S(1)} %pad_maximum_fusion.4), channel_id=1, source_target_pairs={{0,4},{1,5},{2,6},{3,7},{4,0},{5,1},{6,2},{7,3},{8,12},{9,13},{10,... | collective-permute-start | bytes 294920 | tf_op jit(solution)/shard_map/ppermute | solution.py:81
  44.9 3.1 %collective-permute-start.15 = (bf16[128,384]{1,0:T(8,128)(2,1)S(1)}, bf16[128,384]{1,0:T(8,128)(2,1)S(1)}, u32[]{:S(2)}, u32[]{:S(2)}) collective-permute-start(bf16[128,384]{1,0:T(8,128)(2,1)S(1)} %get-tuple-element.95), channel_id=1, source_target_pairs={{1,0},{2,1},{3,2},{0,3},{5,4},{6,5},{7,6},{4,7},{9,8},{10,9},{11,1... | collective-permute-start | bytes 294920 | tf_op jit(solution)/shard_map/ppermute | solution.py:87
  47.3 4.4 %collective-permute-start.13 = (bf16[96,384]{1,0:T(8,128)(2,1)S(1)}, bf16[96,384]{1,0:T(8,128)(2,1)S(1)}, u32[]{:S(2)}, u32[]{:S(2)}) collective-permute-start(bf16[96,384]{1,0:T(8,128)(2,1)S(1)} %add_convert_fusion), channel_id=1, source_target_pairs={{0,8},{1,9},{2,10},{3,11},{4,12},{5,13},{6,14},{7,15},{8,0},{9,1},... | collective-permute-start | bytes 221192 | tf_op jit(solution)/shard_map/ppermute | solution.py:81
  51.8 6.1 %collective-permute-start.19 = (bf16[192,384]{1,0:T(8,128)(2,1)S(1)}, bf16[192,384]{1,0:T(8,128)(2,1)S(1)}, u32[]{:S(2)}, u32[]{:S(2)}) collective-permute-start(bf16[192,384]{1,0:T(8,128)(2,1)S(1)} %pad_maximum_fusion.3.refs_0_), channel_id=1, source_target_pairs={{0,6},{1,7},{2,4},{3,5},{4,2},{5,3},{6,0},{7,1},{8,14},{9,15},{10,... | collective-permute-start | bytes 442376 | tf_op jit(solution)/shard_map/ppermute | solution.py:81
  54.6 5.1 %collective-permute-start.18 = (bf16[192,384]{1,0:T(8,128)(2,1)S(1)}, bf16[192,384]{1,0:T(8,128)(2,1)S(1)}, u32[]{:S(2)}, u32[]{:S(2)}) collective-permute-start(bf16[192,384]{1,0:T(8,128)(2,1)S(1)} %pad_maximum_fusion.3.refs_0_), channel_id=1, source_target_pairs={{0,2},{1,3},{2,0},{3,1},{4,6},{5,7},{6,4},{7,5},{8,10},{9,11},{10,... | collective-permute-start | bytes 442376 | tf_op jit(solution)/shard_map/ppermute | solution.py:81
  54.8 5.1 %collective-permute-start.17 = (bf16[192,384]{1,0:T(8,128)(2,1)S(1)}, bf16[192,384]{1,0:T(8,128)(2,1)S(1)}, u32[]{:S(2)}, u32[]{:S(2)}) collective-permute-start(bf16[192,384]{1,0:T(8,128)(2,1)S(1)} %pad_maximum_fusion.3.refs_0_), channel_id=1, source_target_pairs={{0,4},{1,5},{2,6},{3,7},{4,0},{5,1},{6,2},{7,3},{8,12},{9,13},{10,... | collective-permute-start | bytes 442376 | tf_op jit(solution)/shard_map/ppermute | solution.py:81
  55.3 5.5 %collective-permute-start.20 = (bf16[192,384]{1,0:T(8,128)(2,1)S(1)}, bf16[192,384]{1,0:T(8,128)(2,1)S(1)}, u32[]{:S(2)}, u32[]{:S(2)}) collective-permute-start(bf16[192,384]{1,0:T(8,128)(2,1)S(1)} %pad_maximum_fusion.3.refs_0_), channel_id=1, source_target_pairs={{0,1},{1,0},{2,3},{3,2},{4,5},{5,4},{6,7},{7,6},{8,9},{9,8},{10,11... | collective-permute-start | bytes 442376 | tf_op jit(solution)/shard_map/ppermute | solution.py:81
  57.9 2.9 %collective-permute-start.23 = (bf16[192,384]{1,0:T(8,128)(2,1)S(1)}, bf16[192,384]{1,0:T(8,128)(2,1)S(1)}, u32[]{:S(2)}, u32[]{:S(2)}) collective-permute-start(bf16[192,384]{1,0:T(8,128)(2,1)S(1)} %collective-permute-done.19.refs_3_), channel_id=1, source_target_pairs={{0,1},{1,0},{2,3},{3,2},{4,5},{5,4},{6,7},{7,6},{8,9},{9,8},{10,11... | collective-permute-start | bytes 442376 | tf_op jit(solution)/shard_map/ppermute | solution.py:81
  59.7 1.4 %collective-permute-start.22 = (bf16[192,384]{1,0:T(8,128)(2,1)S(1)}, bf16[192,384]{1,0:T(8,128)(2,1)S(1)}, u32[]{:S(2)}, u32[]{:S(2)}) collective-permute-start(bf16[192,384]{1,0:T(8,128)(2,1)S(1)} %collective-permute-done.18.refs_2_), channel_id=1, source_target_pairs={{0,1},{1,0},{2,3},{3,2},{4,5},{5,4},{6,7},{7,6},{8,9},{9,8},{10,11... | collective-permute-start | bytes 442376 | tf_op jit(solution)/shard_map/ppermute | solution.py:81
  60.0 1.4 %collective-permute-start.21 = (bf16[192,384]{1,0:T(8,128)(2,1)S(1)}, bf16[192,384]{1,0:T(8,128)(2,1)S(1)}, u32[]{:S(2)}, u32[]{:S(2)}) collective-permute-start(bf16[192,384]{1,0:T(8,128)(2,1)S(1)} %collective-permute-done.17.refs_1_), channel_id=1, source_target_pairs={{0,1},{1,0},{2,3},{3,2},{4,5},{5,4},{6,7},{7,6},{8,9},{9,8},{10,11... | collective-permute-start | bytes 442376 | tf_op jit(solution)/shard_map/ppermute | solution.py:81

commit v21 on v15

--- a/solution.py
+++ b/solution.py
@@ -315,11 +315,12 @@
         e_far = jnp.exp2((s_far - peak) * exponent_scale)
         total = jnp.sum(e_local, axis=0, keepdims=True) + jnp.sum(e_far, axis=0, keepdims=True)
         inverse = 1.0 / total
+        delta = inverse * (
+            jnp.sum(e_local * dp_local, axis=0, keepdims=True)
+            + jnp.sum(e_far * dp_far, axis=0, keepdims=True)
+        )
         p_local = e_local * inverse
         p_far = e_far * inverse
-        delta = jnp.sum(p_local * dp_local, axis=0, keepdims=True) + jnp.sum(
-            p_far * dp_far, axis=0, keepdims=True
-        )
         ds_local = rounded(p_local * (dp_local - delta))
         ds_far = rounded(p_far * (dp_far - delta))
         return rounded(p_local), rounded(p_far), ds_local, ds_far

time: 63.2 us -> 63.1 us (level)
  no operation moved by 1% of the time
where the time goes in v21:
time: 63.1 us; the launch traced here: 62.8 us
  starting transfers between devices  23.4 us (37%)
  waiting for transfers between devices  23.4 us (37%)
  Pallas kernels  14.1 us (22%)
  other arithmetic  1 us (2%)
  between operations  0.84 us (1%)
    ppermute x22, waiting for transfers between devices, swapped(): return lax.ppermute(block, ('dom', 'rows'), route)  23.4 us
    ppermute x22, starting transfers between devices, swapped(): return lax.ppermute(block, ('dom', 'rows'), route)  23.4 us
    pallas_call x6, Pallas kernels, call(): pl.pallas_call(kernel, out_shape=outs, in_specs=[pl.BlockSpec(memory_spac...  14.1 us
  transfers between devices with their start and end apart: 24, of which 16 were waited for; matrix products, arithmetic and copies ran while one was open for 1% of the time, Pallas kernels for 9%

profile of v21, /device:TPU:0, one launch (start us, length us, event | category | flops | bytes accessed | tf_op | source)
XLA Modules:
  0.0 62.8 jit_solution(15744137138163795509)
XLA Ops:
  0.6 1.2 %pick_rows.1 = (bf16[128,384]{1,0:T(8,128)(2,1)S(1)}, bf16[256,256]{1,0:T(8,128)(2,1)S(1)}, bf16[128,384]{1,0:T(8,128)(2,1)S(1)}, bf16[32,384]{1,0:T(8,128)(2,1)...) custom-call(bf16[256,384]{1,0:T(8,128)(2,1)} %feat_hbm.3, ...), custom_call_target="tpu_custom_call" | custom-call | bytes 623616 | tf_op jit(solution)/shard_map/pick_rows/pallas_call | solution.py:474
  1.9 3.0 %collective-permute-start = (bf16[128,384]{1,0:T(8,128)(2,1)S(1)}, bf16[128,384]{1,0:T(8,128)(2,1)S(1)}, u32[]{:S(2)}, u32[]{:S(2)}) collective-permute-start(bf16[128,384]{1,0:T(8,128)(2,1)S(1)} %get-tuple-element.57), channel_id=1, source_target_pairs={{0,4},{1,5},{2,6},{3,7},{4,0},{5,1},{6,2},{7,3},{8,12},{9,13},{10,... | collective-permute-start | bytes 294920 | tf_op jit(solution)/shard_map/ppermute | solution.py:81
  4.9 2.9 %prepare.1 = (bf16[256,384]{1,0:T(8,128)(2,1)S(1)}, bf16[384,384]{1,0:T(8,128)(2,1)S(1)}, bf16[384,768]{1,0:T(8,128)(2,1)S(1)}, bf16[384,272]{1,0:T(8,128)(2,1)S...) custom-call(bf16[256,384]{1,0:T(8,128)(2,1)} %feat_hbm.3, ...), custom_call_target="tpu_custom_call" | custom-call | flops 377487360 | bytes 4656128 | tf_op jit(solution)/shard_map/prepare/pallas_call | solution.py:474
  7.8 3.9 %collective-permute-start.1 = (bf16[64,384]{1,0:T(8,128)(2,1)S(1)}, bf16[64,384]{1,0:T(8,128)(2,1)S(1)}, u32[]{:S(2)}, u32[]{:S(2)}) collective-permute-start(bf16[64,384]{1,0:T(8,128)(2,1)S(1)} %pad_maximum_fusion.7), channel_id=1, source_target_pairs={{0,24},{1,25},{2,26},{3,27},{4,28},{5,29},{6,30},{7,31},{8,16},{9,... | collective-permute-start | bytes 147464 | tf_op jit(solution)/shard_map/ppermute | solution.py:81
  11.7 0.0 collective-permute-start.2
  11.7 0.1 collective-permute-start.4
  11.8 0.6 %collective-permute-start.3 = (bf16[64,384]{1,0:T(8,128)(2,1)S(1)}, bf16[64,384]{1,0:T(8,128)(2,1)S(1)}, u32[]{:S(2)}, u32[]{:S(2)}) collective-permute-start(bf16[64,384]{1,0:T(8,128)(2,1)S(1)} %pad_maximum_fusion.9), channel_id=1, source_target_pairs={{0,8},{1,9},{2,10},{3,11},{4,12},{5,13},{6,14},{7,15},{8,0},{9,1},... | collective-permute-start | bytes 147464 | tf_op jit(solution)/shard_map/ppermute | solution.py:81
  12.4 1.9 %collective-permute-done.1.refs_2_ = bf16[64,384]{1,0:T(8,128)(2,1)S(1)} collective-permute-done((bf16[64,384]{1,0:T(8,128)(2,1)S(1)}, bf16[64,384]{1,0:T(8,128)(2,1)S(1)}, u32[]{:S(2)}, u32[]{:S(2)}) %collective-permute-start.1) | collective-permute-done | bytes 49184 | tf_op jit(solution)/shard_map/ppermute | solution.py:81
  14.3 2.5 %collective-permute-done.2.refs_3_ = bf16[64,384]{1,0:T(8,128)(2,1)S(1)} collective-permute-done((bf16[64,384]{1,0:T(8,128)(2,1)S(1)}, bf16[64,384]{1,0:T(8,128)(2,1)S(1)}, u32[]{:S(2)}, u32[]{:S(2)}) %collective-permute-start.2) | collective-permute-done | bytes 49184 | tf_op jit(solution)/shard_map/ppermute | solution.py:81
  16.8 0.0 collective-permute-done.3.refs_4_
  16.8 0.0 collective-permute-done.4.refs_5_
  16.8 5.8 %attend.1 = (bf16[784,384]{1,0:T(8,128)(2,1)S(1)}, f32[16,384]{1,0:T(8,128)S(1)}, bf16[384,656]{1,0:T(8,128)(2,1)S(1)}, bf16[384,256]{1,0:T(8,128)(2,1)S(1)}, bf...) custom-call(bf16[32,384]{1,0:T(8,128)(2,1)S(1)} %get-tuple-element.56.refs_0_, ...), custom_call_target="tpu_custom_call" | custom-call | flops 2708471808 | bytes 5959680 | tf_op jit(solution)/shard_map/attend/pallas_call | solution.py:474
  22.6 0.1 collective-permute-start.5
  22.7 1.5 %finish.1 = (f32[256,384]{1,0:T(8,128)S(1)}, bf16[128,384]{1,0:T(8,128)(2,1)S(1)}, f32[768,384]{1,0:T(8,128)S(1)}, bf16[64,384]{1,0:T(8,128)(2,1)S(1)}, bf16[64,...) custom-call(bf16[256,384]{1,0:T(8,128)(2,1)S(1)} %get-tuple-element.53.refs_6_.og_ref, ...), custom_call_target="tpu_custom_call" | custom-call | flops 580386816 | bytes 4853760 | tf_op jit(solution)/shard_map/finish/pallas_call | solution.py:474
  24.2 0.5 collective-permute-done.5
  24.7 0.1 fusion.2
  25.0 2.4 %collective-permute-start.6 = (bf16[200,384]{1,0:T(8,128)(2,1)S(1)}, bf16[200,384]{1,0:T(8,128)(2,1)S(1)}, u32[]{:S(2)}, u32[]{:S(2)}) collective-permute-start(bf16[200,384]{1,0:T(8,128)(2,1)S(1)} %get-tuple-element.109), channel_id=1, source_target_pairs={{0,6},{1,7},{2,4},{3,5},{4,2},{5,3},{6,0},{7,1},{8,14},{9,15},{10,... | collective-permute-start | bytes 460808 | tf_op jit(solution)/shard_map/ppermute | solution.py:81
  27.4 0.6 collective-permute-start.7
  28.0 0.5 collective-permute-start.8
  28.6 1.7 %collective-permute-start.9 = (bf16[64,384]{1,0:T(8,128)(2,1)S(1)}, bf16[64,384]{1,0:T(8,128)(2,1)S(1)}, u32[]{:S(2)}, u32[]{:S(2)}) collective-permute-start(bf16[64,384]{1,0:T(8,128)(2,1)S(1)} %get-tuple-element.82), channel_id=1, source_target_pairs={{0,24},{1,25},{2,26},{3,27},{4,28},{5,29},{6,30},{7,31},{8,16},{9,... | collective-permute-start | bytes 147464 | tf_op jit(solution)/shard_map/ppermute | solution.py:81
  30.3 0.3 collective-permute-start.10
  30.6 2.2 %collective-permute-done.6 = bf16[200,384]{1,0:T(8,128)(2,1)S(1)} collective-permute-done((bf16[200,384]{1,0:T(8,128)(2,1)S(1)}, bf16[200,384]{1,0:T(8,128)(2,1)S(1)}, u32[]{:S(2)}, u32[]{:S(2)}) %collective-permute-start.6) | collective-permute-done | bytes 153632 | tf_op jit(solution)/shard_map/ppermute | solution.py:81
  32.8 2.5 %collective-permute-done.7 = bf16[200,384]{1,0:T(8,128)(2,1)S(1)} collective-permute-done((bf16[200,384]{1,0:T(8,128)(2,1)S(1)}, bf16[200,384]{1,0:T(8,128)(2,1)S(1)}, u32[]{:S(2)}, u32[]{:S(2)}) %collective-permute-start.7) | collective-permute-done | bytes 153632 | tf_op jit(solution)/shard_map/ppermute | solution.py:81
  35.3 0.0 collective-permute-done.8
  35.3 0.1 fusion.1
  35.4 0.4 collective-permute-done.10.refs_1_
  35.9 0.5 collective-permute-start.11
  36.4 1.6 %collective-permute-start.14 = (bf16[64,384]{1,0:T(8,128)(2,1)S(1)}, bf16[64,384]{1,0:T(8,128)(2,1)S(1)}, u32[]{:S(2)}, u32[]{:S(2)}) collective-permute-start(bf16[64,384]{1,0:T(8,128)(2,1)S(1)} %get-tuple-element.89), channel_id=1, source_target_pairs={{0,8},{1,9},{2,10},{3,11},{4,12},{5,13},{6,14},{7,15},{8,0},{9,1},... | collective-permute-start | bytes 147464 | tf_op jit(solution)/shard_map/ppermute | solution.py:81
  38.0 2.4 %collective-permute-done.11 = bf16[104,384]{1,0:T(8,128)(2,1)S(1)} collective-permute-done((bf16[104,384]{1,0:T(8,128)(2,1)S(1)}, bf16[104,384]{1,0:T(8,128)(2,1)S(1)}, u32[]{:S(2)}, u32[]{:S(2)}) %collective-permute-start.11) | collective-permute-done | bytes 79904 | tf_op jit(solution)/shard_map/ppermute | solution.py:81
  40.4 0.5 collective-permute-done.14.refs_2_
  40.9 2.3 %collective-permute-start.12 = (bf16[104,384]{1,0:T(8,128)(2,1)S(1)}, bf16[104,384]{1,0:T(8,128)(2,1)S(1)}, u32[]{:S(2)}, u32[]{:S(2)}) collective-permute-start(bf16[104,384]{1,0:T(8,128)(2,1)S(1)} %pad_maximum_fusion.6), channel_id=1, source_target_pairs={{0,16},{1,17},{2,18},{3,19},{4,20},{5,21},{6,22},{7,23},{8,24},{9,... | collective-permute-start | bytes 239624 | tf_op jit(solution)/shard_map/ppermute | solution.py:81
  43.2 1.6 %collective-permute-start.16 = (bf16[128,384]{1,0:T(8,128)(2,1)S(1)}, bf16[128,384]{1,0:T(8,128)(2,1)S(1)}, u32[]{:S(2)}, u32[]{:S(2)}) collective-permute-start(bf16[128,384]{1,0:T(8,128)(2,1)S(1)} %pad_maximum_fusion.4), channel_id=1, source_target_pairs={{0,4},{1,5},{2,6},{3,7},{4,0},{5,1},{6,2},{7,3},{8,12},{9,13},{10,... | collective-permute-start | bytes 294920 | tf_op jit(solution)/shard_map/ppermute | solution.py:81
  44.8 2.4 %collective-permute-done.12 = bf16[104,384]{1,0:T(8,128)(2,1)S(1)} collective-permute-done((bf16[104,384]{1,0:T(8,128)(2,1)S(1)}, bf16[104,384]{1,0:T(8,128)(2,1)S(1)}, u32[]{:S(2)}, u32[]{:S(2)}) %collective-permute-start.12) | collective-permute-done | bytes 79904 | tf_op jit(solution)/shard_map/ppermute | solution.py:81
  47.2 0.5 collective-permute-start.13
  47.7 0.2 collective-permute-done.16.through_ref
  47.9 1.0 %return_rows.1 = f32[256,384]{1,0:T(8,128)} custom-call(f32[256,384]{1,0:T(8,128)S(1)} %get-tuple-element.85.gf_ref, bf16[256,256]{1,0:T(8,128)(2,1)S(1)} %get-tuple-element.86.chosen_ref, bf16[128,384]{1,0:T(8,128)(2,1)S(1)} %collective-permute-done.15.halo_ref, bf16[64,384]{1,0:T(8,128)(2,1)S(1)} %get-tuple-element.92.own_ref, ...), custom_call_target="tpu_custom_call" | custom-call | bytes 1310720 | tf_op jit(solution)/shard_map/return_rows/pallas_call | solution.py:474
  48.9 2.7 %collective-permute-done.13 = bf16[96,384]{1,0:T(8,128)(2,1)S(1)} collective-permute-done((bf16[96,384]{1,0:T(8,128)(2,1)S(1)}, bf16[96,384]{1,0:T(8,128)(2,1)S(1)}, u32[]{:S(2)}, u32[]{:S(2)}) %collective-permute-start.13) | collective-permute-done | bytes 73760 | tf_op jit(solution)/shard_map/ppermute | solution.py:81
  51.6 2.8 %collective-permute-start.19 = (bf16[192,384]{1,0:T(8,128)(2,1)S(1)}, bf16[192,384]{1,0:T(8,128)(2,1)S(1)}, u32[]{:S(2)}, u32[]{:S(2)}) collective-permute-start(bf16[192,384]{1,0:T(8,128)(2,1)S(1)} %pad_maximum_fusion.3.refs_0_), channel_id=1, source_target_pairs={{0,6},{1,7},{2,4},{3,5},{4,2},{5,3},{6,0},{7,1},{8,14},{9,15},{10,... | collective-permute-start | bytes 442376 | tf_op jit(solution)/shard_map/ppermute | solution.py:81
  54.4 0.3 collective-permute-start.18
  54.7 0.5 collective-permute-start.17
  55.2 2.5 %collective-permute-done.19.refs_3_ = bf16[192,384]{1,0:T(8,128)(2,1)S(1)} collective-permute-done((bf16[192,384]{1,0:T(8,128)(2,1)S(1)}, bf16[192,384]{1,0:T(8,128)(2,1)S(1)}, u32[]{:S(2)}, u32[]{:S(2)}) %collective-permute-start.19) | collective-permute-done | bytes 147488 | tf_op jit(solution)/shard_map/ppermute | solution.py:81
  57.8 1.8 %collective-permute-done.18.refs_2_ = bf16[192,384]{1,0:T(8,128)(2,1)S(1)} collective-permute-done((bf16[192,384]{1,0:T(8,128)(2,1)S(1)}, bf16[192,384]{1,0:T(8,128)(2,1)S(1)}, u32[]{:S(2)}, u32[]{:S(2)}) %collective-permute-start.18) | collective-permute-done | bytes 147488 | tf_op jit(solution)/shard_map/ppermute | solution.py:81
  59.6 0.3 collective-permute-done.17.refs_1_
  59.8 0.3 collective-permute-start.21
  60.1 0.6 convert_add_fusion.2
  60.7 0.3 collective-permute-done.22.refs_6_
  60.9 0.3 collective-permute-done.21.refs_5_
  61.2 1.6 %place_sums.1 = (f32[384,384]{1,0:T(8,128)}, f32[384,768]{1,0:T(8,128)}, f32[384,384]{1,0:T(8,128)}) custom-call(bf16[192,384]{1,0:T(8,128)(2,1)S(1)} %pad_maximum_fusion.3.refs_0_, bf16[192,384]{1,0:T(8,128)(2,1)S(1)} %collective-permute-done.17.refs_1_, bf16[192,384]{1,0:T(8,128)(2,1)S(1)} %collective-permute-done.18.refs_2_, ...), custom_call_target="tpu_custom_call" | custom-call | bytes 3538944 | tf_op jit(solution)/shard_map/place_sums/pallas_call | solution.py:474
  (31 shorter events, 0.3 us)
Async XLA Ops:
  1.9 5.9 %collective-permute-start = (bf16[128,384]{1,0:T(8,128)(2,1)S(1)}, bf16[128,384]{1,0:T(8,128)(2,1)S(1)}, u32[]{:S(2)}, u32[]{:S(2)}) collective-permute-start(bf16[128,384]{1,0:T(8,128)(2,1)S(1)} %get-tuple-element.57), channel_id=1, source_target_pairs={{0,4},{1,5},{2,6},{3,7},{4,0},{5,1},{6,2},{7,3},{8,12},{9,13},{10,... | collective-permute-start | bytes 294920 | tf_op jit(solution)/shard_map/ppermute | solution.py:81
  7.8 6.5 %collective-permute-start.1 = (bf16[64,384]{1,0:T(8,128)(2,1)S(1)}, bf16[64,384]{1,0:T(8,128)(2,1)S(1)}, u32[]{:S(2)}, u32[]{:S(2)}) collective-permute-start(bf16[64,384]{1,0:T(8,128)(2,1)S(1)} %pad_maximum_fusion.7), channel_id=1, source_target_pairs={{0,24},{1,25},{2,26},{3,27},{4,28},{5,29},{6,30},{7,31},{8,16},{9,... | collective-permute-start | bytes 147464 | tf_op jit(solution)/shard_map/ppermute | solution.py:81
  11.7 5.1 %collective-permute-start.2 = (bf16[64,384]{1,0:T(8,128)(2,1)S(1)}, bf16[64,384]{1,0:T(8,128)(2,1)S(1)}, u32[]{:S(2)}, u32[]{:S(2)}) collective-permute-start(bf16[64,384]{1,0:T(8,128)(2,1)S(1)} %pad_maximum_fusion.8), channel_id=1, source_target_pairs={{0,16},{1,17},{2,18},{3,19},{4,20},{5,21},{6,22},{7,23},{8,24},{9,... | collective-permute-start | bytes 147464 | tf_op jit(solution)/shard_map/ppermute | solution.py:81
  11.7 5.1 %collective-permute-start.4 = (bf16[128,384]{1,0:T(8,128)(2,1)S(1)}, bf16[128,384]{1,0:T(8,128)(2,1)S(1)}, u32[]{:S(2)}, u32[]{:S(2)}) collective-permute-start(bf16[128,384]{1,0:T(8,128)(2,1)S(1)} %get-tuple-element.63), channel_id=1, source_target_pairs={{3,0},{0,1},{1,2},{2,3},{7,4},{4,5},{5,6},{6,7},{11,8},{8,9},{9,10... | collective-permute-start | bytes 294920 | tf_op jit(solution)/shard_map/ppermute | solution.py:87
  11.8 5.0 %collective-permute-start.3 = (bf16[64,384]{1,0:T(8,128)(2,1)S(1)}, bf16[64,384]{1,0:T(8,128)(2,1)S(1)}, u32[]{:S(2)}, u32[]{:S(2)}) collective-permute-start(bf16[64,384]{1,0:T(8,128)(2,1)S(1)} %pad_maximum_fusion.9), channel_id=1, source_target_pairs={{0,8},{1,9},{2,10},{3,11},{4,12},{5,13},{6,14},{7,15},{8,0},{9,1},... | collective-permute-start | bytes 147464 | tf_op jit(solution)/shard_map/ppermute | solution.py:81
  22.6 2.1 %collective-permute-start.5 = (bf16[784,384]{1,0:T(8,128)(2,1)S(1)}, bf16[784,384]{1,0:T(8,128)(2,1)S(1)}, u32[]{:S(2)}, u32[]{:S(2)}) collective-permute-start(bf16[784,384]{1,0:T(8,128)(2,1)S(1)} %get-tuple-element.76), channel_id=1, source_target_pairs={{0,1},{1,0},{2,3},{3,2},{4,5},{5,4},{6,7},{7,6},{8,9},{9,8},{10,11... | collective-permute-start | bytes 1806344 | tf_op jit(solution)/shard_map/ppermute | solution.py:81
  25.0 7.8 %collective-permute-start.6 = (bf16[200,384]{1,0:T(8,128)(2,1)S(1)}, bf16[200,384]{1,0:T(8,128)(2,1)S(1)}, u32[]{:S(2)}, u32[]{:S(2)}) collective-permute-start(bf16[200,384]{1,0:T(8,128)(2,1)S(1)} %get-tuple-element.109), channel_id=1, source_target_pairs={{0,6},{1,7},{2,4},{3,5},{4,2},{5,3},{6,0},{7,1},{8,14},{9,15},{10,... | collective-permute-start | bytes 460808 | tf_op jit(solution)/shard_map/ppermute | solution.py:81
  27.4 7.9 %collective-permute-start.7 = (bf16[200,384]{1,0:T(8,128)(2,1)S(1)}, bf16[200,384]{1,0:T(8,128)(2,1)S(1)}, u32[]{:S(2)}, u32[]{:S(2)}) collective-permute-start(bf16[200,384]{1,0:T(8,128)(2,1)S(1)} %get-tuple-element.110), channel_id=1, source_target_pairs={{0,2},{1,3},{2,0},{3,1},{4,6},{5,7},{6,4},{7,5},{8,10},{9,11},{10,... | collective-permute-start | bytes 460808 | tf_op jit(solution)/shard_map/ppermute | solution.py:81
  28.0 7.3 %collective-permute-start.8 = (bf16[200,384]{1,0:T(8,128)(2,1)S(1)}, bf16[200,384]{1,0:T(8,128)(2,1)S(1)}, u32[]{:S(2)}, u32[]{:S(2)}) collective-permute-start(bf16[200,384]{1,0:T(8,128)(2,1)S(1)} %get-tuple-element.111), channel_id=1, source_target_pairs={{0,4},{1,5},{2,6},{3,7},{4,0},{5,1},{6,2},{7,3},{8,12},{9,13},{10,... | collective-permute-start | bytes 460808 | tf_op jit(solution)/shard_map/ppermute | solution.py:81
  28.6 6.8 %collective-permute-start.9 = (bf16[64,384]{1,0:T(8,128)(2,1)S(1)}, bf16[64,384]{1,0:T(8,128)(2,1)S(1)}, u32[]{:S(2)}, u32[]{:S(2)}) collective-permute-start(bf16[64,384]{1,0:T(8,128)(2,1)S(1)} %get-tuple-element.82), channel_id=1, source_target_pairs={{0,24},{1,25},{2,26},{3,27},{4,28},{5,29},{6,30},{7,31},{8,16},{9,... | collective-permute-start | bytes 147464 | tf_op jit(solution)/shard_map/ppermute | solution.py:81
  30.3 5.5 %collective-permute-start.10 = (bf16[64,384]{1,0:T(8,128)(2,1)S(1)}, bf16[64,384]{1,0:T(8,128)(2,1)S(1)}, u32[]{:S(2)}, u32[]{:S(2)}) collective-permute-start(bf16[64,384]{1,0:T(8,128)(2,1)S(1)} %get-tuple-element.83), channel_id=1, source_target_pairs={{0,16},{1,17},{2,18},{3,19},{4,20},{5,21},{6,22},{7,23},{8,24},{9,... | collective-permute-start | bytes 147464 | tf_op jit(solution)/shard_map/ppermute | solution.py:81
  35.9 4.5 %collective-permute-start.11 = (bf16[104,384]{1,0:T(8,128)(2,1)S(1)}, bf16[104,384]{1,0:T(8,128)(2,1)S(1)}, u32[]{:S(2)}, u32[]{:S(2)}) collective-permute-start(bf16[104,384]{1,0:T(8,128)(2,1)S(1)} %pad_maximum_fusion.5), channel_id=1, source_target_pairs={{0,8},{1,9},{2,10},{3,11},{4,12},{5,13},{6,14},{7,15},{8,0},{9,1},... | collective-permute-start | bytes 239624 | tf_op jit(solution)/shard_map/ppermute | solution.py:81
  36.4 4.5 %collective-permute-start.14 = (bf16[64,384]{1,0:T(8,128)(2,1)S(1)}, bf16[64,384]{1,0:T(8,128)(2,1)S(1)}, u32[]{:S(2)}, u32[]{:S(2)}) collective-permute-start(bf16[64,384]{1,0:T(8,128)(2,1)S(1)} %get-tuple-element.89), channel_id=1, source_target_pairs={{0,8},{1,9},{2,10},{3,11},{4,12},{5,13},{6,14},{7,15},{8,0},{9,1},... | collective-permute-start | bytes 147464 | tf_op jit(solution)/shard_map/ppermute | solution.py:81
  40.9 6.2 %collective-permute-start.12 = (bf16[104,384]{1,0:T(8,128)(2,1)S(1)}, bf16[104,384]{1,0:T(8,128)(2,1)S(1)}, u32[]{:S(2)}, u32[]{:S(2)}) collective-permute-start(bf16[104,384]{1,0:T(8,128)(2,1)S(1)} %pad_maximum_fusion.6), channel_id=1, source_target_pairs={{0,16},{1,17},{2,18},{3,19},{4,20},{5,21},{6,22},{7,23},{8,24},{9,... | collective-permute-start | bytes 239624 | tf_op jit(solution)/shard_map/ppermute | solution.py:81
  43.2 4.7 %collective-permute-start.16 = (bf16[128,384]{1,0:T(8,128)(2,1)S(1)}, bf16[128,384]{1,0:T(8,128)(2,1)S(1)}, u32[]{:S(2)}, u32[]{:S(2)}) collective-permute-start(bf16[128,384]{1,0:T(8,128)(2,1)S(1)} %pad_maximum_fusion.4), channel_id=1, source_target_pairs={{0,4},{1,5},{2,6},{3,7},{4,0},{5,1},{6,2},{7,3},{8,12},{9,13},{10,... | collective-permute-start | bytes 294920 | tf_op jit(solution)/shard_map/ppermute | solution.py:81
  44.8 3.1 %collective-permute-start.15 = (bf16[128,384]{1,0:T(8,128)(2,1)S(1)}, bf16[128,384]{1,0:T(8,128)(2,1)S(1)}, u32[]{:S(2)}, u32[]{:S(2)}) collective-permute-start(bf16[128,384]{1,0:T(8,128)(2,1)S(1)} %get-tuple-element.91), channel_id=1, source_target_pairs={{1,0},{2,1},{3,2},{0,3},{5,4},{6,5},{7,6},{4,7},{9,8},{10,9},{11,1... | collective-permute-start | bytes 294920 | tf_op jit(solution)/shard_map/ppermute | solution.py:87
  47.2 4.4 %collective-permute-start.13 = (bf16[96,384]{1,0:T(8,128)(2,1)S(1)}, bf16[96,384]{1,0:T(8,128)(2,1)S(1)}, u32[]{:S(2)}, u32[]{:S(2)}) collective-permute-start(bf16[96,384]{1,0:T(8,128)(2,1)S(1)} %add_convert_fusion), channel_id=1, source_target_pairs={{0,8},{1,9},{2,10},{3,11},{4,12},{5,13},{6,14},{7,15},{8,0},{9,1},... | collective-permute-start | bytes 221192 | tf_op jit(solution)/shard_map/ppermute | solution.py:81
  51.6 6.1 %collective-permute-start.19 = (bf16[192,384]{1,0:T(8,128)(2,1)S(1)}, bf16[192,384]{1,0:T(8,128)(2,1)S(1)}, u32[]{:S(2)}, u32[]{:S(2)}) collective-permute-start(bf16[192,384]{1,0:T(8,128)(2,1)S(1)} %pad_maximum_fusion.3.refs_0_), channel_id=1, source_target_pairs={{0,6},{1,7},{2,4},{3,5},{4,2},{5,3},{6,0},{7,1},{8,14},{9,15},{10,... | collective-permute-start | bytes 442376 | tf_op jit(solution)/shard_map/ppermute | solution.py:81
  54.4 5.1 %collective-permute-start.18 = (bf16[192,384]{1,0:T(8,128)(2,1)S(1)}, bf16[192,384]{1,0:T(8,128)(2,1)S(1)}, u32[]{:S(2)}, u32[]{:S(2)}) collective-permute-start(bf16[192,384]{1,0:T(8,128)(2,1)S(1)} %pad_maximum_fusion.3.refs_0_), channel_id=1, source_target_pairs={{0,2},{1,3},{2,0},{3,1},{4,6},{5,7},{6,4},{7,5},{8,10},{9,11},{10,... | collective-permute-start | bytes 442376 | tf_op jit(solution)/shard_map/ppermute | solution.py:81
  54.7 5.1 %collective-permute-start.17 = (bf16[192,384]{1,0:T(8,128)(2,1)S(1)}, bf16[192,384]{1,0:T(8,128)(2,1)S(1)}, u32[]{:S(2)}, u32[]{:S(2)}) collective-permute-start(bf16[192,384]{1,0:T(8,128)(2,1)S(1)} %pad_maximum_fusion.3.refs_0_), channel_id=1, source_target_pairs={{0,4},{1,5},{2,6},{3,7},{4,0},{5,1},{6,2},{7,3},{8,12},{9,13},{10,... | collective-permute-start | bytes 442376 | tf_op jit(solution)/shard_map/ppermute | solution.py:81
  55.2 5.5 %collective-permute-start.20 = (bf16[192,384]{1,0:T(8,128)(2,1)S(1)}, bf16[192,384]{1,0:T(8,128)(2,1)S(1)}, u32[]{:S(2)}, u32[]{:S(2)}) collective-permute-start(bf16[192,384]{1,0:T(8,128)(2,1)S(1)} %pad_maximum_fusion.3.refs_0_), channel_id=1, source_target_pairs={{0,1},{1,0},{2,3},{3,2},{4,5},{5,4},{6,7},{7,6},{8,9},{9,8},{10,11... | collective-permute-start | bytes 442376 | tf_op jit(solution)/shard_map/ppermute | solution.py:81
  57.8 2.9 %collective-permute-start.23 = (bf16[192,384]{1,0:T(8,128)(2,1)S(1)}, bf16[192,384]{1,0:T(8,128)(2,1)S(1)}, u32[]{:S(2)}, u32[]{:S(2)}) collective-permute-start(bf16[192,384]{1,0:T(8,128)(2,1)S(1)} %collective-permute-done.19.refs_3_), channel_id=1, source_target_pairs={{0,1},{1,0},{2,3},{3,2},{4,5},{5,4},{6,7},{7,6},{8,9},{9,8},{10,11... | collective-permute-start | bytes 442376 | tf_op jit(solution)/shard_map/ppermute | solution.py:81
  59.6 1.4 %collective-permute-start.22 = (bf16[192,384]{1,0:T(8,128)(2,1)S(1)}, bf16[192,384]{1,0:T(8,128)(2,1)S(1)}, u32[]{:S(2)}, u32[]{:S(2)}) collective-permute-start(bf16[192,384]{1,0:T(8,128)(2,1)S(1)} %collective-permute-done.18.refs_2_), channel_id=1, source_target_pairs={{0,1},{1,0},{2,3},{3,2},{4,5},{5,4},{6,7},{7,6},{8,9},{9,8},{10,11... | collective-permute-start | bytes 442376 | tf_op jit(solution)/shard_map/ppermute | solution.py:81
  59.8 1.4 %collective-permute-start.21 = (bf16[192,384]{1,0:T(8,128)(2,1)S(1)}, bf16[192,384]{1,0:T(8,128)(2,1)S(1)}, u32[]{:S(2)}, u32[]{:S(2)}) collective-permute-start(bf16[192,384]{1,0:T(8,128)(2,1)S(1)} %collective-permute-done.17.refs_1_), channel_id=1, source_target_pairs={{0,1},{1,0},{2,3},{3,2},{4,5},{5,4},{6,7},{7,6},{8,9},{9,8},{10,11... | collective-permute-start | bytes 442376 | tf_op jit(solution)/shard_map/ppermute | solution.py:81

commit v22 on v15

--- a/solution.py
+++ b/solution.py
@@ -570,13 +570,17 @@
     keep, rider = scattered(keep, rider, square)
     keep, *returned[:-1] = lax.optimization_barrier((keep, *returned[:-1]))
     keep, rider = scattered(keep, rider, pair)
-    (returned, halo_feat), _ = lax.optimization_barrier(((returned, halo_feat), keep))
-    through = swapped(jnp.concatenate([x[per_peer:] for x in [pairs[0]] + returned[::-1]]), 1, 0)
-    halo_back = shifted(halo_feat, "rows", -1)
-    for mask in rest:
-        message = swapped(with_rider(keep, rider), *mask)
+    for at, mask in enumerate(rest):
+        message = with_rider(keep, rider)
+        if at == 0:
+            (last, halo_feat), _ = lax.optimization_barrier(((returned[-1], halo_feat), message))
+            halo_back = shifted(halo_feat, "rows", -1)
+        message = swapped(message, *mask)
         keep, rider = rounded(keep).astype(f32), rounded(rider).astype(f32)
         keep, rider = added(keep, rider, {1: message})
+    returned[-1] = last
+    odd = [block[per_peer:] for block in [pairs[0]] + returned[::-1]]
+    through = swapped(jnp.concatenate(odd, axis=0), 1, 0)
     (grad_features,) = call(
         return_kernel,
         "return_rows",

time: 63.2 us -> 62.6 us (level)
  transfers between devices with their start and end apart: 24 -> 24, of which waited for: 16 -> 15; matrix products, arithmetic and copies ran while one was open for 1% -> 1% of each run, Pallas kernels for 9% -> 9%
where the time goes in v22:
time: 62.6 us; the launch traced here: 62.4 us
  waiting for transfers between devices  23.4 us (37%)
  starting transfers between devices  23 us (37%)
  Pallas kernels  14.1 us (23%)
  other arithmetic  1 us (2%)
  between operations  0.83 us (1%)
    ppermute x22, waiting for transfers between devices, swapped(): return lax.ppermute(block, ('dom', 'rows'), route)  23.4 us
    ppermute x22, starting transfers between devices, swapped(): return lax.ppermute(block, ('dom', 'rows'), route)  22.9 us
    pallas_call x6, Pallas kernels, call(): pl.pallas_call(kernel, out_shape=outs, in_specs=[pl.BlockSpec(memory_spac...  14.1 us
  transfers between devices with their start and end apart: 24, of which 15 were waited for; matrix products, arithmetic and copies ran while one was open for 1% of the time, Pallas kernels for 9%

profile of v22, /device:TPU:0, one launch (start us, length us, event | category | flops | bytes accessed | tf_op | source)
XLA Modules:
  0.0 62.4 jit_solution(2972971193474279079)
XLA Ops:
  0.6 1.2 %pick_rows.1 = (bf16[128,384]{1,0:T(8,128)(2,1)S(1)}, bf16[256,256]{1,0:T(8,128)(2,1)S(1)}, bf16[128,384]{1,0:T(8,128)(2,1)S(1)}, bf16[32,384]{1,0:T(8,128)(2,1)...) custom-call(bf16[256,384]{1,0:T(8,128)(2,1)} %feat_hbm.3, ...), custom_call_target="tpu_custom_call" | custom-call | bytes 623616 | tf_op jit(solution)/shard_map/pick_rows/pallas_call | solution.py:473
  1.9 3.0 %collective-permute-start = (bf16[128,384]{1,0:T(8,128)(2,1)S(1)}, bf16[128,384]{1,0:T(8,128)(2,1)S(1)}, u32[]{:S(2)}, u32[]{:S(2)}) collective-permute-start(bf16[128,384]{1,0:T(8,128)(2,1)S(1)} %get-tuple-element.55), channel_id=1, source_target_pairs={{0,4},{1,5},{2,6},{3,7},{4,0},{5,1},{6,2},{7,3},{8,12},{9,13},{10,... | collective-permute-start | bytes 294920 | tf_op jit(solution)/shard_map/ppermute | solution.py:81
  4.9 2.9 %prepare.1 = (bf16[256,384]{1,0:T(8,128)(2,1)S(1)}, bf16[384,384]{1,0:T(8,128)(2,1)S(1)}, bf16[384,768]{1,0:T(8,128)(2,1)S(1)}, bf16[384,272]{1,0:T(8,128)(2,1)S...) custom-call(bf16[256,384]{1,0:T(8,128)(2,1)} %feat_hbm.3, ...), custom_call_target="tpu_custom_call" | custom-call | flops 377487360 | bytes 4656128 | tf_op jit(solution)/shard_map/prepare/pallas_call | solution.py:473
  7.7 0.0 collective-permute-done.refs_1_
  7.8 3.9 %collective-permute-start.1 = (bf16[64,384]{1,0:T(8,128)(2,1)S(1)}, bf16[64,384]{1,0:T(8,128)(2,1)S(1)}, u32[]{:S(2)}, u32[]{:S(2)}) collective-permute-start(bf16[64,384]{1,0:T(8,128)(2,1)S(1)} %pad_maximum_fusion.7), channel_id=1, source_target_pairs={{0,24},{1,25},{2,26},{3,27},{4,28},{5,29},{6,30},{7,31},{8,16},{9,... | collective-permute-start | bytes 147464 | tf_op jit(solution)/shard_map/ppermute | solution.py:81
  11.7 0.0 collective-permute-start.2
  11.7 0.1 collective-permute-start.4
  11.8 0.6 %collective-permute-start.3 = (bf16[64,384]{1,0:T(8,128)(2,1)S(1)}, bf16[64,384]{1,0:T(8,128)(2,1)S(1)}, u32[]{:S(2)}, u32[]{:S(2)}) collective-permute-start(bf16[64,384]{1,0:T(8,128)(2,1)S(1)} %pad_maximum_fusion.9), channel_id=1, source_target_pairs={{0,8},{1,9},{2,10},{3,11},{4,12},{5,13},{6,14},{7,15},{8,0},{9,1},... | collective-permute-start | bytes 147464 | tf_op jit(solution)/shard_map/ppermute | solution.py:81
  12.4 1.9 %collective-permute-done.1.refs_2_ = bf16[64,384]{1,0:T(8,128)(2,1)S(1)} collective-permute-done((bf16[64,384]{1,0:T(8,128)(2,1)S(1)}, bf16[64,384]{1,0:T(8,128)(2,1)S(1)}, u32[]{:S(2)}, u32[]{:S(2)}) %collective-permute-start.1) | collective-permute-done | bytes 49184 | tf_op jit(solution)/shard_map/ppermute | solution.py:81
  14.3 2.5 %collective-permute-done.2.refs_3_ = bf16[64,384]{1,0:T(8,128)(2,1)S(1)} collective-permute-done((bf16[64,384]{1,0:T(8,128)(2,1)S(1)}, bf16[64,384]{1,0:T(8,128)(2,1)S(1)}, u32[]{:S(2)}, u32[]{:S(2)}) %collective-permute-start.2) | collective-permute-done | bytes 49184 | tf_op jit(solution)/shard_map/ppermute | solution.py:81
  16.8 5.9 %attend.1 = (bf16[784,384]{1,0:T(8,128)(2,1)S(1)}, f32[16,384]{1,0:T(8,128)S(1)}, bf16[384,656]{1,0:T(8,128)(2,1)S(1)}, bf16[384,256]{1,0:T(8,128)(2,1)S(1)}, bf...) custom-call(bf16[32,384]{1,0:T(8,128)(2,1)S(1)} %get-tuple-element.54.refs_0_, ...), custom_call_target="tpu_custom_call" | custom-call | flops 2708471808 | bytes 5959680 | tf_op jit(solution)/shard_map/attend/pallas_call | solution.py:473
  22.7 0.1 collective-permute-start.5
  22.8 1.5 %finish.1 = (f32[256,384]{1,0:T(8,128)S(1)}, bf16[128,384]{1,0:T(8,128)(2,1)S(1)}, f32[768,384]{1,0:T(8,128)S(1)}, bf16[64,384]{1,0:T(8,128)(2,1)S(1)}, bf16[64,...) custom-call(bf16[256,384]{1,0:T(8,128)(2,1)S(1)} %get-tuple-element.51.refs_6_.og_ref, ...), custom_call_target="tpu_custom_call" | custom-call | flops 580386816 | bytes 4853760 | tf_op jit(solution)/shard_map/finish/pallas_call | solution.py:473
  24.2 0.5 collective-permute-done.5
  24.8 0.1 fusion.2
  25.1 2.4 %collective-permute-start.6 = (bf16[200,384]{1,0:T(8,128)(2,1)S(1)}, bf16[200,384]{1,0:T(8,128)(2,1)S(1)}, u32[]{:S(2)}, u32[]{:S(2)}) collective-permute-start(bf16[200,384]{1,0:T(8,128)(2,1)S(1)} %get-tuple-element.105), channel_id=1, source_target_pairs={{0,6},{1,7},{2,4},{3,5},{4,2},{5,3},{6,0},{7,1},{8,14},{9,15},{10,... | collective-permute-start | bytes 460808 | tf_op jit(solution)/shard_map/ppermute | solution.py:81
  27.5 0.6 collective-permute-start.7
  28.1 0.5 collective-permute-start.8
  28.6 1.7 %collective-permute-start.9 = (bf16[64,384]{1,0:T(8,128)(2,1)S(1)}, bf16[64,384]{1,0:T(8,128)(2,1)S(1)}, u32[]{:S(2)}, u32[]{:S(2)}) collective-permute-start(bf16[64,384]{1,0:T(8,128)(2,1)S(1)} %get-tuple-element.80), channel_id=1, source_target_pairs={{0,24},{1,25},{2,26},{3,27},{4,28},{5,29},{6,30},{7,31},{8,16},{9,... | collective-permute-start | bytes 147464 | tf_op jit(solution)/shard_map/ppermute | solution.py:81
  30.3 0.3 collective-permute-start.10
  30.6 2.2 %collective-permute-done.6 = bf16[200,384]{1,0:T(8,128)(2,1)S(1)} collective-permute-done((bf16[200,384]{1,0:T(8,128)(2,1)S(1)}, bf16[200,384]{1,0:T(8,128)(2,1)S(1)}, u32[]{:S(2)}, u32[]{:S(2)}) %collective-permute-start.6) | collective-permute-done | bytes 153632 | tf_op jit(solution)/shard_map/ppermute | solution.py:81
  32.9 2.5 %collective-permute-done.7 = bf16[200,384]{1,0:T(8,128)(2,1)S(1)} collective-permute-done((bf16[200,384]{1,0:T(8,128)(2,1)S(1)}, bf16[200,384]{1,0:T(8,128)(2,1)S(1)}, u32[]{:S(2)}, u32[]{:S(2)}) %collective-permute-start.7) | collective-permute-done | bytes 153632 | tf_op jit(solution)/shard_map/ppermute | solution.py:81
  35.3 0.0 collective-permute-done.8
  35.3 0.1 fusion.1
  35.4 0.4 collective-permute-done.10.refs_1_
  35.9 0.5 collective-permute-start.11
  36.4 1.6 %collective-permute-start.14 = (bf16[64,384]{1,0:T(8,128)(2,1)S(1)}, bf16[64,384]{1,0:T(8,128)(2,1)S(1)}, u32[]{:S(2)}, u32[]{:S(2)}) collective-permute-start(bf16[64,384]{1,0:T(8,128)(2,1)S(1)} %get-tuple-element.85), channel_id=1, source_target_pairs={{0,8},{1,9},{2,10},{3,11},{4,12},{5,13},{6,14},{7,15},{8,0},{9,1},... | collective-permute-start | bytes 147464 | tf_op jit(solution)/shard_map/ppermute | solution.py:81
  38.0 2.4 %collective-permute-done.11 = bf16[104,384]{1,0:T(8,128)(2,1)S(1)} collective-permute-done((bf16[104,384]{1,0:T(8,128)(2,1)S(1)}, bf16[104,384]{1,0:T(8,128)(2,1)S(1)}, u32[]{:S(2)}, u32[]{:S(2)}) %collective-permute-start.11) | collective-permute-done | bytes 79904 | tf_op jit(solution)/shard_map/ppermute | solution.py:81
  40.5 2.3 %collective-permute-start.12 = (bf16[104,384]{1,0:T(8,128)(2,1)S(1)}, bf16[104,384]{1,0:T(8,128)(2,1)S(1)}, u32[]{:S(2)}, u32[]{:S(2)}) collective-permute-start(bf16[104,384]{1,0:T(8,128)(2,1)S(1)} %pad_maximum_fusion.6), channel_id=1, source_target_pairs={{0,16},{1,17},{2,18},{3,19},{4,20},{5,21},{6,22},{7,23},{8,24},{9,... | collective-permute-start | bytes 239624 | tf_op jit(solution)/shard_map/ppermute | solution.py:81
  42.7 0.0 collective-permute-done.14.refs_2_
  42.8 1.6 %collective-permute-start.16 = (bf16[128,384]{1,0:T(8,128)(2,1)S(1)}, bf16[128,384]{1,0:T(8,128)(2,1)S(1)}, u32[]{:S(2)}, u32[]{:S(2)}) collective-permute-start(bf16[128,384]{1,0:T(8,128)(2,1)S(1)} %pad_maximum_fusion.4), channel_id=1, source_target_pairs={{0,4},{1,5},{2,6},{3,7},{4,0},{5,1},{6,2},{7,3},{8,12},{9,13},{10,... | collective-permute-start | bytes 294920 | tf_op jit(solution)/shard_map/ppermute | solution.py:81
  44.3 2.4 %collective-permute-done.12 = bf16[104,384]{1,0:T(8,128)(2,1)S(1)} collective-permute-done((bf16[104,384]{1,0:T(8,128)(2,1)S(1)}, bf16[104,384]{1,0:T(8,128)(2,1)S(1)}, u32[]{:S(2)}, u32[]{:S(2)}) %collective-permute-start.12) | collective-permute-done | bytes 79904 | tf_op jit(solution)/shard_map/ppermute | solution.py:81
  46.7 0.2 collective-permute-start.13
  46.9 0.5 collective-permute-done.16.through_ref
  47.5 1.0 %return_rows.1 = f32[256,384]{1,0:T(8,128)} custom-call(f32[256,384]{1,0:T(8,128)S(1)} %get-tuple-element.83.gf_ref, bf16[256,256]{1,0:T(8,128)(2,1)S(1)} %get-tuple-element.84.chosen_ref, bf16[128,384]{1,0:T(8,128)(2,1)S(1)} %collective-permute-done.15.halo_ref, bf16[64,384]{1,0:T(8,128)(2,1)S(1)} %get-tuple-element.88.own_ref, ...), custom_call_target="tpu_custom_call" | custom-call | bytes 1310720 | tf_op jit(solution)/shard_map/return_rows/pallas_call | solution.py:473
  48.5 2.7 %collective-permute-done.13 = bf16[96,384]{1,0:T(8,128)(2,1)S(1)} collective-permute-done((bf16[96,384]{1,0:T(8,128)(2,1)S(1)}, bf16[96,384]{1,0:T(8,128)(2,1)S(1)}, u32[]{:S(2)}, u32[]{:S(2)}) %collective-permute-start.13) | collective-permute-done | bytes 73760 | tf_op jit(solution)/shard_map/ppermute | solution.py:81
  51.2 2.5 %collective-permute-start.19 = (bf16[192,384]{1,0:T(8,128)(2,1)S(1)}, bf16[192,384]{1,0:T(8,128)(2,1)S(1)}, u32[]{:S(2)}, u32[]{:S(2)}) collective-permute-start(bf16[192,384]{1,0:T(8,128)(2,1)S(1)} %pad_maximum_fusion.3.refs_0_), channel_id=1, source_target_pairs={{0,6},{1,7},{2,4},{3,5},{4,2},{5,3},{6,0},{7,1},{8,14},{9,15},{10,... | collective-permute-start | bytes 442376 | tf_op jit(solution)/shard_map/ppermute | solution.py:81
  53.6 0.6 collective-permute-start.18
  54.2 0.5 collective-permute-start.17
  54.7 0.0 collective-permute-start.20
  54.7 2.6 %collective-permute-done.19.refs_3_ = bf16[192,384]{1,0:T(8,128)(2,1)S(1)} collective-permute-done((bf16[192,384]{1,0:T(8,128)(2,1)S(1)}, bf16[192,384]{1,0:T(8,128)(2,1)S(1)}, u32[]{:S(2)}, u32[]{:S(2)}) %collective-permute-start.19) | collective-permute-done | bytes 147488 | tf_op jit(solution)/shard_map/ppermute | solution.py:81
  57.3 1.6 %collective-permute-done.18.refs_2_ = bf16[192,384]{1,0:T(8,128)(2,1)S(1)} collective-permute-done((bf16[192,384]{1,0:T(8,128)(2,1)S(1)}, bf16[192,384]{1,0:T(8,128)(2,1)S(1)}, u32[]{:S(2)}, u32[]{:S(2)}) %collective-permute-start.18) | collective-permute-done | bytes 147488 | tf_op jit(solution)/shard_map/ppermute | solution.py:81
  58.9 0.5 collective-permute-done.17.refs_1_
  59.3 0.0 collective-permute-start.21
  59.4 0.6 convert_add_fusion.1
  60.0 0.3 collective-permute-done.22.refs_6_
  60.2 0.5 collective-permute-done.21.refs_5_
  60.7 1.6 %place_sums.1 = (f32[384,384]{1,0:T(8,128)}, f32[384,768]{1,0:T(8,128)}, f32[384,384]{1,0:T(8,128)}) custom-call(bf16[192,384]{1,0:T(8,128)(2,1)S(1)} %pad_maximum_fusion.3.refs_0_, bf16[192,384]{1,0:T(8,128)(2,1)S(1)} %collective-permute-done.17.refs_1_, bf16[192,384]{1,0:T(8,128)(2,1)S(1)} %collective-permute-done.18.refs_2_, ...), custom_call_target="tpu_custom_call" | custom-call | bytes 3538944 | tf_op jit(solution)/shard_map/place_sums/pallas_call | solution.py:473
  (31 shorter events, 0.3 us)
Async XLA Ops:
  1.9 5.9 %collective-permute-start = (bf16[128,384]{1,0:T(8,128)(2,1)S(1)}, bf16[128,384]{1,0:T(8,128)(2,1)S(1)}, u32[]{:S(2)}, u32[]{:S(2)}) collective-permute-start(bf16[128,384]{1,0:T(8,128)(2,1)S(1)} %get-tuple-element.55), channel_id=1, source_target_pairs={{0,4},{1,5},{2,6},{3,7},{4,0},{5,1},{6,2},{7,3},{8,12},{9,13},{10,... | collective-permute-start | bytes 294920 | tf_op jit(solution)/shard_map/ppermute | solution.py:81
  7.8 6.5 %collective-permute-start.1 = (bf16[64,384]{1,0:T(8,128)(2,1)S(1)}, bf16[64,384]{1,0:T(8,128)(2,1)S(1)}, u32[]{:S(2)}, u32[]{:S(2)}) collective-permute-start(bf16[64,384]{1,0:T(8,128)(2,1)S(1)} %pad_maximum_fusion.7), channel_id=1, source_target_pairs={{0,24},{1,25},{2,26},{3,27},{4,28},{5,29},{6,30},{7,31},{8,16},{9,... | collective-permute-start | bytes 147464 | tf_op jit(solution)/shard_map/ppermute | solution.py:81
  11.7 5.1 %collective-permute-start.2 = (bf16[64,384]{1,0:T(8,128)(2,1)S(1)}, bf16[64,384]{1,0:T(8,128)(2,1)S(1)}, u32[]{:S(2)}, u32[]{:S(2)}) collective-permute-start(bf16[64,384]{1,0:T(8,128)(2,1)S(1)} %pad_maximum_fusion.8), channel_id=1, source_target_pairs={{0,16},{1,17},{2,18},{3,19},{4,20},{5,21},{6,22},{7,23},{8,24},{9,... | collective-permute-start | bytes 147464 | tf_op jit(solution)/shard_map/ppermute | solution.py:81
  11.7 5.1 %collective-permute-start.4 = (bf16[128,384]{1,0:T(8,128)(2,1)S(1)}, bf16[128,384]{1,0:T(8,128)(2,1)S(1)}, u32[]{:S(2)}, u32[]{:S(2)}) collective-permute-start(bf16[128,384]{1,0:T(8,128)(2,1)S(1)} %get-tuple-element.61), channel_id=1, source_target_pairs={{3,0},{0,1},{1,2},{2,3},{7,4},{4,5},{5,6},{6,7},{11,8},{8,9},{9,10... | collective-permute-start | bytes 294920 | tf_op jit(solution)/shard_map/ppermute | solution.py:87
  11.8 5.0 %collective-permute-start.3 = (bf16[64,384]{1,0:T(8,128)(2,1)S(1)}, bf16[64,384]{1,0:T(8,128)(2,1)S(1)}, u32[]{:S(2)}, u32[]{:S(2)}) collective-permute-start(bf16[64,384]{1,0:T(8,128)(2,1)S(1)} %pad_maximum_fusion.9), channel_id=1, source_target_pairs={{0,8},{1,9},{2,10},{3,11},{4,12},{5,13},{6,14},{7,15},{8,0},{9,1},... | collective-permute-start | bytes 147464 | tf_op jit(solution)/shard_map/ppermute | solution.py:81
  22.7 2.1 %collective-permute-start.5 = (bf16[784,384]{1,0:T(8,128)(2,1)S(1)}, bf16[784,384]{1,0:T(8,128)(2,1)S(1)}, u32[]{:S(2)}, u32[]{:S(2)}) collective-permute-start(bf16[784,384]{1,0:T(8,128)(2,1)S(1)} %get-tuple-element.74), channel_id=1, source_target_pairs={{0,1},{1,0},{2,3},{3,2},{4,5},{5,4},{6,7},{7,6},{8,9},{9,8},{10,11... | collective-permute-start | bytes 1806344 | tf_op jit(solution)/shard_map/ppermute | solution.py:81
  25.1 7.8 %collective-permute-start.6 = (bf16[200,384]{1,0:T(8,128)(2,1)S(1)}, bf16[200,384]{1,0:T(8,128)(2,1)S(1)}, u32[]{:S(2)}, u32[]{:S(2)}) collective-permute-start(bf16[200,384]{1,0:T(8,128)(2,1)S(1)} %get-tuple-element.105), channel_id=1, source_target_pairs={{0,6},{1,7},{2,4},{3,5},{4,2},{5,3},{6,0},{7,1},{8,14},{9,15},{10,... | collective-permute-start | bytes 460808 | tf_op jit(solution)/shard_map/ppermute | solution.py:81
  27.5 7.9 %collective-permute-start.7 = (bf16[200,384]{1,0:T(8,128)(2,1)S(1)}, bf16[200,384]{1,0:T(8,128)(2,1)S(1)}, u32[]{:S(2)}, u32[]{:S(2)}) collective-permute-start(bf16[200,384]{1,0:T(8,128)(2,1)S(1)} %get-tuple-element.106), channel_id=1, source_target_pairs={{0,2},{1,3},{2,0},{3,1},{4,6},{5,7},{6,4},{7,5},{8,10},{9,11},{10,... | collective-permute-start | bytes 460808 | tf_op jit(solution)/shard_map/ppermute | solution.py:81
  28.1 7.3 %collective-permute-start.8 = (bf16[200,384]{1,0:T(8,128)(2,1)S(1)}, bf16[200,384]{1,0:T(8,128)(2,1)S(1)}, u32[]{:S(2)}, u32[]{:S(2)}) collective-permute-start(bf16[200,384]{1,0:T(8,128)(2,1)S(1)} %get-tuple-element.107), channel_id=1, source_target_pairs={{0,4},{1,5},{2,6},{3,7},{4,0},{5,1},{6,2},{7,3},{8,12},{9,13},{10,... | collective-permute-start | bytes 460808 | tf_op jit(solution)/shard_map/ppermute | solution.py:81
  28.6 6.8 %collective-permute-start.9 = (bf16[64,384]{1,0:T(8,128)(2,1)S(1)}, bf16[64,384]{1,0:T(8,128)(2,1)S(1)}, u32[]{:S(2)}, u32[]{:S(2)}) collective-permute-start(bf16[64,384]{1,0:T(8,128)(2,1)S(1)} %get-tuple-element.80), channel_id=1, source_target_pairs={{0,24},{1,25},{2,26},{3,27},{4,28},{5,29},{6,30},{7,31},{8,16},{9,... | collective-permute-start | bytes 147464 | tf_op jit(solution)/shard_map/ppermute | solution.py:81
  30.3 5.5 %collective-permute-start.10 = (bf16[64,384]{1,0:T(8,128)(2,1)S(1)}, bf16[64,384]{1,0:T(8,128)(2,1)S(1)}, u32[]{:S(2)}, u32[]{:S(2)}) collective-permute-start(bf16[64,384]{1,0:T(8,128)(2,1)S(1)} %get-tuple-element.81), channel_id=1, source_target_pairs={{0,16},{1,17},{2,18},{3,19},{4,20},{5,21},{6,22},{7,23},{8,24},{9,... | collective-permute-start | bytes 147464 | tf_op jit(solution)/shard_map/ppermute | solution.py:81
  35.9 4.5 %collective-permute-start.11 = (bf16[104,384]{1,0:T(8,128)(2,1)S(1)}, bf16[104,384]{1,0:T(8,128)(2,1)S(1)}, u32[]{:S(2)}, u32[]{:S(2)}) collective-permute-start(bf16[104,384]{1,0:T(8,128)(2,1)S(1)} %pad_maximum_fusion.5), channel_id=1, source_target_pairs={{0,8},{1,9},{2,10},{3,11},{4,12},{5,13},{6,14},{7,15},{8,0},{9,1},... | collective-permute-start | bytes 239624 | tf_op jit(solution)/shard_map/ppermute | solution.py:81
  36.4 6.4 %collective-permute-start.14 = (bf16[64,384]{1,0:T(8,128)(2,1)S(1)}, bf16[64,384]{1,0:T(8,128)(2,1)S(1)}, u32[]{:S(2)}, u32[]{:S(2)}) collective-permute-start(bf16[64,384]{1,0:T(8,128)(2,1)S(1)} %get-tuple-element.85), channel_id=1, source_target_pairs={{0,8},{1,9},{2,10},{3,11},{4,12},{5,13},{6,14},{7,15},{8,0},{9,1},... | collective-permute-start | bytes 147464 | tf_op jit(solution)/shard_map/ppermute | solution.py:81
  40.5 6.2 %collective-permute-start.12 = (bf16[104,384]{1,0:T(8,128)(2,1)S(1)}, bf16[104,384]{1,0:T(8,128)(2,1)S(1)}, u32[]{:S(2)}, u32[]{:S(2)}) collective-permute-start(bf16[104,384]{1,0:T(8,128)(2,1)S(1)} %pad_maximum_fusion.6), channel_id=1, source_target_pairs={{0,16},{1,17},{2,18},{3,19},{4,20},{5,21},{6,22},{7,23},{8,24},{9,... | collective-permute-start | bytes 239624 | tf_op jit(solution)/shard_map/ppermute | solution.py:81
  42.8 4.7 %collective-permute-start.16 = (bf16[128,384]{1,0:T(8,128)(2,1)S(1)}, bf16[128,384]{1,0:T(8,128)(2,1)S(1)}, u32[]{:S(2)}, u32[]{:S(2)}) collective-permute-start(bf16[128,384]{1,0:T(8,128)(2,1)S(1)} %pad_maximum_fusion.4), channel_id=1, source_target_pairs={{0,4},{1,5},{2,6},{3,7},{4,0},{5,1},{6,2},{7,3},{8,12},{9,13},{10,... | collective-permute-start | bytes 294920 | tf_op jit(solution)/shard_map/ppermute | solution.py:81
  44.3 3.1 %collective-permute-start.15 = (bf16[128,384]{1,0:T(8,128)(2,1)S(1)}, bf16[128,384]{1,0:T(8,128)(2,1)S(1)}, u32[]{:S(2)}, u32[]{:S(2)}) collective-permute-start(bf16[128,384]{1,0:T(8,128)(2,1)S(1)} %get-tuple-element.87), channel_id=1, source_target_pairs={{1,0},{2,1},{3,2},{0,3},{5,4},{6,5},{7,6},{4,7},{9,8},{10,9},{11,1... | collective-permute-start | bytes 294920 | tf_op jit(solution)/shard_map/ppermute | solution.py:87
  46.7 4.4 %collective-permute-start.13 = (bf16[96,384]{1,0:T(8,128)(2,1)S(1)}, bf16[96,384]{1,0:T(8,128)(2,1)S(1)}, u32[]{:S(2)}, u32[]{:S(2)}) collective-permute-start(bf16[96,384]{1,0:T(8,128)(2,1)S(1)} %add_convert_fusion), channel_id=1, source_target_pairs={{0,8},{1,9},{2,10},{3,11},{4,12},{5,13},{6,14},{7,15},{8,0},{9,1},... | collective-permute-start | bytes 221192 | tf_op jit(solution)/shard_map/ppermute | solution.py:81
  51.2 6.1 %collective-permute-start.19 = (bf16[192,384]{1,0:T(8,128)(2,1)S(1)}, bf16[192,384]{1,0:T(8,128)(2,1)S(1)}, u32[]{:S(2)}, u32[]{:S(2)}) collective-permute-start(bf16[192,384]{1,0:T(8,128)(2,1)S(1)} %pad_maximum_fusion.3.refs_0_), channel_id=1, source_target_pairs={{0,6},{1,7},{2,4},{3,5},{4,2},{5,3},{6,0},{7,1},{8,14},{9,15},{10,... | collective-permute-start | bytes 442376 | tf_op jit(solution)/shard_map/ppermute | solution.py:81
  53.6 5.2 %collective-permute-start.18 = (bf16[192,384]{1,0:T(8,128)(2,1)S(1)}, bf16[192,384]{1,0:T(8,128)(2,1)S(1)}, u32[]{:S(2)}, u32[]{:S(2)}) collective-permute-start(bf16[192,384]{1,0:T(8,128)(2,1)S(1)} %pad_maximum_fusion.3.refs_0_), channel_id=1, source_target_pairs={{0,2},{1,3},{2,0},{3,1},{4,6},{5,7},{6,4},{7,5},{8,10},{9,11},{10,... | collective-permute-start | bytes 442376 | tf_op jit(solution)/shard_map/ppermute | solution.py:81
  54.2 5.1 %collective-permute-start.17 = (bf16[192,384]{1,0:T(8,128)(2,1)S(1)}, bf16[192,384]{1,0:T(8,128)(2,1)S(1)}, u32[]{:S(2)}, u32[]{:S(2)}) collective-permute-start(bf16[192,384]{1,0:T(8,128)(2,1)S(1)} %pad_maximum_fusion.3.refs_0_), channel_id=1, source_target_pairs={{0,4},{1,5},{2,6},{3,7},{4,0},{5,1},{6,2},{7,3},{8,12},{9,13},{10,... | collective-permute-start | bytes 442376 | tf_op jit(solution)/shard_map/ppermute | solution.py:81
  54.7 5.2 %collective-permute-start.20 = (bf16[192,384]{1,0:T(8,128)(2,1)S(1)}, bf16[192,384]{1,0:T(8,128)(2,1)S(1)}, u32[]{:S(2)}, u32[]{:S(2)}) collective-permute-start(bf16[192,384]{1,0:T(8,128)(2,1)S(1)} %pad_maximum_fusion.3.refs_0_), channel_id=1, source_target_pairs={{0,1},{1,0},{2,3},{3,2},{4,5},{5,4},{6,7},{7,6},{8,9},{9,8},{10,11... | collective-permute-start | bytes 442376 | tf_op jit(solution)/shard_map/ppermute | solution.py:81
  57.3 2.7 %collective-permute-start.23 = (bf16[192,384]{1,0:T(8,128)(2,1)S(1)}, bf16[192,384]{1,0:T(8,128)(2,1)S(1)}, u32[]{:S(2)}, u32[]{:S(2)}) collective-permute-start(bf16[192,384]{1,0:T(8,128)(2,1)S(1)} %collective-permute-done.19.refs_3_), channel_id=1, source_target_pairs={{0,1},{1,0},{2,3},{3,2},{4,5},{5,4},{6,7},{7,6},{8,9},{9,8},{10,11... | collective-permute-start | bytes 442376 | tf_op jit(solution)/shard_map/ppermute | solution.py:81
  58.9 1.4 %collective-permute-start.22 = (bf16[192,384]{1,0:T(8,128)(2,1)S(1)}, bf16[192,384]{1,0:T(8,128)(2,1)S(1)}, u32[]{:S(2)}, u32[]{:S(2)}) collective-permute-start(bf16[192,384]{1,0:T(8,128)(2,1)S(1)} %collective-permute-done.18.refs_2_), channel_id=1, source_target_pairs={{0,1},{1,0},{2,3},{3,2},{4,5},{5,4},{6,7},{7,6},{8,9},{9,8},{10,11... | collective-permute-start | bytes 442376 | tf_op jit(solution)/shard_map/ppermute | solution.py:81
  59.3 1.4 %collective-permute-start.21 = (bf16[192,384]{1,0:T(8,128)(2,1)S(1)}, bf16[192,384]{1,0:T(8,128)(2,1)S(1)}, u32[]{:S(2)}, u32[]{:S(2)}) collective-permute-start(bf16[192,384]{1,0:T(8,128)(2,1)S(1)} %collective-permute-done.17.refs_1_), channel_id=1, source_target_pairs={{0,1},{1,0},{2,3},{3,2},{4,5},{5,4},{6,7},{7,6},{8,9},{9,8},{10,11... | collective-permute-start | bytes 442376 | tf_op jit(solution)/shard_map/ppermute | solution.py:81
